TPU v7x, 32 devices: a whole 2x2x4 slice. The times are simulated.
32 devices in a mesh: grp: 2 (over x), pipe: 2 (over core), patch: 8 (over z, y).
Axes of the slice: x: 2, y: 2, z: 4, core: 2. Of those that a mesh axis runs over, the one named last changes fastest.
Arguments:
- tokens: bfloat16 [2, 512, 1152], P(None, ('grp', 'patch')), parts along dimension 1, may hold values from -6 to 6
- stale_kv: bfloat16 [2, 2, 512, 1152], P('pipe', None, ('grp', 'patch')), parts along dimension 2, may hold values from -40 to 40
- w_qkv: bfloat16 [2, 1152, 1728], P('pipe'), may hold values from -0.1875 to 0.1875
- w_out: bfloat16 [2, 576, 1152], P('pipe'), may hold values from -0.25 to 0.25
- block_table: float32 [2, 3, 1152], P('pipe'), may hold values from -3 to 3
- time_table: float32 [100, 5, 1152], replicated, may hold values from -3 to 3
- t_index: int32 [2], P('grp'), parts along dimension 0, may hold values from 0 to 99
- w_final: bfloat16 [1152, 16], replicated, may hold values from -0.1875 to 0.1875
- w_in: bfloat16 [36, 512], replicated, may hold values from -1 to 1
- b_in: float32 [512], replicated, may hold values from -3 to 3
- w_up: bfloat16 [9, 512, 512], replicated, may hold values from -0.09375 to 0.09375
- b_up: float32 [512], replicated, may hold values from -3 to 3
Outputs:
- decoded: bfloat16 [16, 1024, 512], P(('grp', 'pipe'), 'patch'), parts along dimension 0
There are 2 independent parts, one for each index of `grp`. A program takes and returns all parts, laid end to end along the dimension named above; an argument that names none is the same for every part. Nothing has to cross between parts.
All inputs are finite; a program needn't handle non-finite values.
Results may differ from a plain program's by a relative error of at most 0.03.
Values may be sent and summed in bfloat16 or wider, within the bound.
No kernel may reach another device: no remote copies, remote signals or barrier semaphores. Data moves between devices by JAX's collectives and lax.ppermute only.
A program may use at most 128 MiB of HBM per device.

v0:
```python
import math

import jax
import jax.numpy as jnp
from jax import lax
from jax.sharding import PartitionSpec as P

D = 1152
DH = 72
HEADS = 8
CH = 512
LATC = 4
TC = 256
DA = 576


EPSILON = 1e-06


def passed_along(block, axis, distance):
    devices = range(lax.axis_size(axis))
    route = [((i - distance) % len(devices), i) for i in devices]
    return lax.ppermute(block, axis, route)


def with_halo(cells, sides, width):
    for axis, dim in sides:
        count = lax.axis_size(axis)
        ends = count - 1
        head = lax.slice_in_dim(cells, 0, width, axis=dim)
        tail = lax.slice_in_dim(cells, cells.shape[dim] - width, cells.shape[dim], axis=dim)
        cells = jnp.concatenate(
            [
                lax.ppermute(tail, axis, [(i, (i + 1) % count) for i in range(ends)]),
                cells,
                lax.ppermute(head, axis, [((i + 1) % count, i) for i in range(ends)]),
            ],
            axis=dim,
        )
    return cells


def layer_norm(values):
    widened = values.astype(jnp.float32)
    average = jnp.mean(widened, axis=-1, keepdims=True)
    centred = widened - average
    variance = jnp.mean(centred * centred, axis=-1, keepdims=True)
    return centred * lax.rsqrt(variance + EPSILON)


def split_heads(key_value):
    count = key_value.shape[0]
    key_heads = key_value[:, :DA].reshape(count, HEADS, DH)
    value_heads = key_value[:, DA:].reshape(count, HEADS, DH)
    return (key_heads, value_heads)


def attend_local(query, keys_early, keys_late):
    own_count = query.shape[0]
    key_heads, value_heads = split_heads(jnp.concatenate([keys_early, keys_late], axis=0))
    query_heads = query.reshape(own_count, HEADS, DH)
    scores = jnp.einsum(
        "qhd,khd->hqk", query_heads, key_heads, preferred_element_type=jnp.float32
    ) * (1.0 / math.sqrt(DH))
    row_top = jnp.max(scores, axis=2, keepdims=True)
    exponent = jnp.exp(scores - row_top)
    row_total = jnp.sum(exponent, axis=2)
    weights = exponent.astype(jnp.bfloat16)
    numerator = jnp.einsum("hqk,khd->qhd", weights, value_heads, preferred_element_type=jnp.float32)
    attended = numerator / row_total.T[:, :, None]
    return attended.reshape(own_count, DA).astype(jnp.bfloat16)


def convolve(padded, weights, out_rows, out_cols):
    total = jnp.zeros((out_rows, out_cols, weights.shape[-1]), jnp.float32)
    for offset_row in range(3):
        for offset_col in range(3):
            window = padded[offset_row : offset_row + out_rows, offset_col : offset_col + out_cols]
            total = total + jnp.dot(
                window, weights[offset_row * 3 + offset_col], preferred_element_type=jnp.float32
            )
    return total


def convolve_latent(latent_rim, w_in, b_in):
    out_rows = latent_rim.shape[0] - 2
    out_cols = latent_rim.shape[1] - 2
    activation = convolve(latent_rim, w_in.reshape(9, LATC, CH), out_rows, out_cols) + b_in
    return jax.nn.silu(activation).astype(jnp.bfloat16)


def local(
    tokens,
    stale_kv,
    w_qkv,
    w_out,
    block_table,
    time_table,
    t_index,
    w_final,
    w_in,
    b_in,
    w_up,
    b_up,
):
    section = lax.axis_index("pipe")
    micro_count = tokens.shape[0]
    own_rows = tokens.shape[1]
    time_row = lax.dynamic_index_in_dim(time_table, t_index[0], 0, keepdims=False)
    shift_vec = time_row[0] + block_table[0, 0]
    scale_vec = time_row[1] + block_table[0, 1]
    gate_vec = time_row[2] + block_table[0, 2]
    stale_own = stale_kv[0, 1]
    stale_all = lax.all_gather(stale_own, "patch", axis=0, tiled=True)
    fresh_prev = jnp.zeros_like(stale_all)
    received = jnp.zeros((own_rows, D), jnp.bfloat16)
    x_next = received
    tick_count = micro_count + lax.axis_size("pipe") - 1
    for moment in range(tick_count):
        position = moment - section
        micro_index = jnp.clip(position, 0, micro_count - 1)
        first_input = lax.dynamic_index_in_dim(tokens, micro_index, 0, keepdims=False)
        block_input = jnp.where(section == 0, first_input, received)
        modulated = (layer_norm(block_input) * (1.0 + scale_vec) + shift_vec).astype(jnp.bfloat16)
        projected = jnp.dot(modulated, w_qkv[0], preferred_element_type=jnp.float32)
        query = projected[:, :DA].astype(jnp.bfloat16)
        fresh_own = projected[:, DA:].astype(jnp.bfloat16)
        fresh_now = lax.all_gather(fresh_own, "patch", axis=0, tiled=True)
        keys_early = jnp.where(position == 0, fresh_now, fresh_prev)
        keys_late = jnp.where(position == 0, stale_all, fresh_now)
        attended = attend_local(query, keys_early, keys_late)
        fresh_prev = fresh_now
        branch = jnp.dot(attended, w_out[0], preferred_element_type=jnp.float32)
        x_next = (block_input.astype(jnp.float32) + gate_vec * branch).astype(jnp.bfloat16)
        if moment + 1 < tick_count:
            received = passed_along(x_next, "pipe", 1)
    final_state = jnp.where(section == 0, received, x_next)
    final_input = (layer_norm(final_state) * (1.0 + time_row[4]) + time_row[3]).astype(jnp.bfloat16)
    own_tokens = jnp.dot(final_input, w_final, preferred_element_type=jnp.float32).astype(
        jnp.bfloat16
    )
    gathered = lax.all_gather(own_tokens, "patch", axis=0, tiled=True)
    token_rows = gathered.shape[0] // TC
    tile_tokens = TC // lax.axis_size("patch")
    token_grid = gathered.reshape(token_rows, TC, 2, 2, LATC)
    tile_cols = lax.dynamic_slice_in_dim(
        token_grid, lax.axis_index("patch") * tile_tokens, tile_tokens, 1
    )
    latent_tile = tile_cols.transpose(0, 2, 1, 3, 4).reshape(2 * token_rows, 2 * tile_tokens, LATC)
    tile_rows = latent_tile.shape[0]
    tile_width = latent_tile.shape[1]
    latent_rim = with_halo(latent_tile, (("pipe", 0), ("patch", 1)), 2)
    features = convolve_latent(latent_rim, w_in, b_in)
    row_ids = section * tile_rows + jnp.arange(tile_rows + 2) - 1
    col_ids = lax.axis_index("patch") * tile_width + jnp.arange(tile_width + 2) - 1
    inside_rows = (row_ids >= 0) & (row_ids < tile_rows * lax.axis_size("pipe"))
    inside_cols = (col_ids >= 0) & (col_ids < tile_width * lax.axis_size("patch"))
    inside = inside_rows[:, None] & inside_cols[None, :]
    feature_rim = jnp.where(inside[:, :, None], features, jnp.zeros_like(features))
    upsampled = jnp.repeat(jnp.repeat(feature_rim, 2, axis=0), 2, axis=1)
    padded_up = upsampled[1:-1, 1:-1]
    decoded = convolve(padded_up, w_up, 2 * tile_rows, 2 * tile_width) + b_up
    return decoded.astype(jnp.bfloat16)


def solution(mesh):
    placed = (
        P(None, ("grp", "patch"), None),
        P("pipe", None, ("grp", "patch"), None),
        P("pipe", None, None),
        P("pipe", None, None),
        P("pipe", None, None),
        P(),
        P("grp"),
        P(),
        P(),
        P(),
        P(),
        P(),
    )
    return jax.shard_map(
        local,
        mesh=mesh,
        in_specs=placed,
        out_specs=P(("grp", "pipe"), "patch", None),
        check_vma=False,
    )
```

profile of v0, /device:TPU:0, one launch (start us, length us, event | category | flops | bytes accessed | tf_op | source)
XLA Modules:
  0.0 220.0 jit_solution(15561231215944642016)
XLA Ops:
  0.8 1.0 convert_reduce_fusion.2
  1.8 1.1 fusion.101
  3.8 3.4 %fusion.12 = bf16[32,1728]{1,0:T(8,128)(2,1)S(1)} fusion(bf16[1,1152,1728]{1,2,0:T(8,128)(2,1)} %param.14, f32[1152]{0:T(1024)S(1)} %get-tuple-element.6, f32[1152]{0:T(1024)S(1)} %get-tuple-element.7, f32[32]{0:T(128)S(1)} %add_rsqrt_fusion.3, f32[32]{0:T(128)S(1)} %broadcast_multiply_fusion.3, bf16[2,32,1152]{2,1,0:T(8,128)(2,1)} %param.12, s32[]{:T(128)S(6)} %min.11, ...), kind=kOutput, calls=%fused_computation.15 | convolution fusion | flops 127715328 | bytes 4175109 | tf_op jit(solution)/shard_map/dot_general | solution.py:125
  7.5 33.2 %all-gather = bf16[1,1,256,1152]{3,2,1,0:T(8,128)(2,1)S(1)} all-gather(bf16[1,1,32,1152]{3,2,1,0:T(8,128)(2,1)S(1)} %slice-done.2), channel_id=2, replica_groups=mesh['grp'=2,'pipe'=2,'patch'=8] {'patch'}, dimensions={2}, use_global_device_ids=true | all-gather | bytes 663552 | tf_op jit(solution)/shard_map/all_gather | solution.py:114
  40.7 31.3 %all_gather.15 = bf16[256,1152]{1,0:T(8,128)(2,1)S(1)} all-gather(bf16[32,1152]{1,0:T(8,128)(2,1)S(1)} %slice.272), channel_id=1, replica_groups=mesh['grp'=2,'pipe'=2,'patch'=8] {'patch'}, dimensions={0}, use_global_device_ids=true | all-gather | bytes 663552 | tf_op jit(solution)/shard_map/all_gather | solution.py:128
  72.1 1.2 pad_maximum_fusion.2
  73.3 2.1 copy.50
  75.4 1.0 copy.49
  76.5 1.4 fusion.167
  80.9 3.4 %fusion.15 = bf16[32,1728]{1,0:T(8,128)(2,1)S(1)} fusion(bf16[1,1152,1728]{1,2,0:T(8,128)(2,1)} %param.14, bf16[32,1152]{1,0:T(8,128)(2,1)S(1)} %get-tuple-element.13, f32[1152]{0:T(1024)S(1)} %get-tuple-element.6, f32[1152]{0:T(1024)S(1)} %get-tuple-element.7, f32[32]{0:T(128)S(1)} %add_rsqrt_fusion.2, f32[32]{0:T(128)S(1)} %broadcast_multiply_fusion.2), kind=kOutput, calls=%fused_computation.16 | convolution fusion | flops 127678464 | bytes 4175104 | tf_op jit(solution)/shard_map/dot_general | solution.py:125
  84.4 31.4 %all_gather.17 = bf16[256,1152]{1,0:T(8,128)(2,1)S(1)} all-gather(bf16[32,1152]{1,0:T(8,128)(2,1)S(1)} %slice.276), channel_id=1, replica_groups=mesh['grp'=2,'pipe'=2,'patch'=8] {'patch'}, dimensions={0}, use_global_device_ids=true | all-gather | bytes 663552 | tf_op jit(solution)/shard_map/all_gather | solution.py:128
  116.0 1.4 pad_maximum_fusion.1
  117.4 1.3 copy.54
  118.7 2.1 copy.53
  124.4 3.4 %fusion.18 = bf16[32,1728]{1,0:T(8,128)(2,1)S(1)} fusion(bf16[1,1152,1728]{1,2,0:T(8,128)(2,1)} %param.14, bf16[32,1152]{1,0:T(8,128)(2,1)S(1)} %get-tuple-element.11, f32[32]{0:T(128)S(1)} %add_rsqrt_fusion.1, f32[32]{0:T(128)S(1)} %broadcast_multiply_fusion.1, f32[1152]{0:T(1024)S(1)} %get-tuple-element.6, f32[1152]{0:T(1024)S(1)} %get-tuple-element.7), kind=kOutput, calls=%fused_computation.17 | convolution fusion | flops 127678464 | bytes 4175104 | tf_op jit(solution)/shard_map/dot_general | solution.py:125
  128.0 31.5 %all_gather.18 = bf16[256,1152]{1,0:T(8,128)(2,1)S(1)} all-gather(bf16[32,1152]{1,0:T(8,128)(2,1)S(1)} %slice.280), channel_id=1, replica_groups=mesh['grp'=2,'pipe'=2,'patch'=8] {'patch'}, dimensions={0}, use_global_device_ids=true | all-gather | bytes 663552 | tf_op jit(solution)/shard_map/all_gather | solution.py:128
  162.5 30.5 %all-gather.1 = bf16[8,32,16]{1,2,0:T(8,128)(2,1)S(1)} all-gather(bf16[1,32,16]{1,2,0:T(8,128)(2,1)S(1)} %fusion.42), channel_id=1, replica_groups=mesh['grp'=2,'pipe'=2,'patch'=8] {'patch'}, dimensions={0}, use_global_device_ids=true | all-gather | bytes 9216 | tf_op jit(solution)/shard_map/all_gather | solution.py:142
  193.4 1.3 collective-permute-start.3
  194.7 3.0 %collective-permute-start.2 = (bf16[2,64,4]{1,2,0:T(4,128)(2,1)S(1)}, bf16[2,64,4]{1,2,0:T(4,128)(2,1)S(1)}, u32[]{:S(2)}, u32[]{:S(2)}) collective-permute-start(bf16[2,64,4]{1,2,0:T(4,128)(2,1)S(1)} %copy.63), channel_id=1, source_target_pairs={{0,8},{1,9},{2,10},{3,11},{4,12},{5,13},{6,14},{7,15},{16,24},{17,... | collective-permute-start | bytes 3080 | tf_op jit(solution)/shard_map/ppermute | solution.py:34
  198.6 3.9 %collective-permute-start.4 = (bf16[6,2,4]{1,2,0:T(4,128)(2,1)S(1)}, bf16[6,2,4]{1,2,0:T(4,128)(2,1)S(1)}, u32[]{:S(2)}, u32[]{:S(2)}) collective-permute-start(bf16[6,2,4]{1,2,0:T(4,128)(2,1)S(1)} %get-tuple-element.35), channel_id=1, source_target_pairs={{0,1},{1,2},{2,3},{3,4},{4,5},{5,6},{6,7},{8,9},{9,10},{10,11},{11... | collective-permute-start | bytes 296 | tf_op jit(solution)/shard_map/ppermute | solution.py:34
  202.5 1.5 collective-permute-start.5
  204.0 4.0 %collective-permute-done.5 = bf16[6,2,4]{1,2,0:T(4,128)(2,1)S(1)} collective-permute-done((bf16[6,2,4]{1,2,0:T(4,128)(2,1)S(1)}, bf16[6,2,4]{1,2,0:T(4,128)(2,1)S(1)}, u32[]{:S(2)}, u32[]{:S(2)}) %collective-permute-start.5) | collective-permute-done | bytes 128 | tf_op jit(solution)/shard_map/ppermute | solution.py:36
  212.4 2.5 %fusion.165 = (bf16[4,128,512]{2,0,1:T(4,128)(2,1)S(1)}, bf16[4,128,512]{2,0,1:T(4,128)(2,1)S(1)}, bf16[4,128,512]{2,0,1:T(4,128)(2,1)S(1)}, bf16[4,128,512]{2,0...) fusion(bf16[8,132,512]{2,0,1:T(8,128)(2,1)S(1)} %bitcast.159), kind=kLoop, calls=%fused_computation.224 | loop fusion | bytes 9437184 | tf_op jit(solution)/shard_map/slice | solution.py:78
  218.7 1.2 fusion.27
  (113 shorter events, 20.3 us)
Async XLA Ops:
  0.0 78.7 %copy-start = (bf16[1,576,1152]{2,1,0:T(8,128)(2,1)S(1)}, bf16[1,576,1152]{2,1,0:T(8,128)(2,1)}, u32[]{:S(2)}) copy-start(bf16[1,576,1152]{2,1,0:T(8,128)(2,1)} %param.15) | copy-start | bytes 3981316
  3.8 3.7 %slice-start.2 = ((bf16[1,2,32,1152]{3,2,1,0:T(8,128)(2,1)}), bf16[1,1,32,1152]{3,2,1,0:T(8,128)(2,1)S(1)}, s32[]{:S(2)}) async-start(bf16[1,2,32,1152]{3,2,1,0:T(8,128)(2,1)} %param.13), calls=%async_computation.2 | async-start | bytes 147456 | tf_op jit(solution)/shard_map/slice | solution.py:113
  76.5 1.7 copy-start.2
  77.9 0.9 copy-start.1
  79.2 1.3 collective-permute-start
  120.9 1.1 copy-start.3
  122.8 1.3 collective-permute-start.1
  161.4 0.9 copy-start.7
  161.4 36.3 %copy-start.8 = (pred[4]{0:T(512)(128)(4,1)S(1)}, pred[4]{0:T(512)(128)(4,1)}, u32[]{:S(2)}) copy-start(pred[4]{0:T(512)(128)(4,1)} %compare_and_fusion.1) | copy-start | bytes 16
  161.4 36.3 %copy-start.9 = (pred[66]{0:T(512)(128)(4,1)S(1)}, pred[66]{0:T(512)(128)(4,1)}, u32[]{:S(2)}) copy-start(pred[66]{0:T(512)(128)(4,1)} %compare_and_fusion) | copy-start | bytes 202
  161.4 46.7 %copy-start.4 = (bf16[36,512]{1,0:T(8,128)(2,1)S(1)}, bf16[36,512]{1,0:T(8,128)(2,1)}, u32[]{:S(2)}) copy-start(bf16[36,512]{1,0:T(8,128)(2,1)} %param.20) | copy-start | bytes 110596
  193.4 4.4 %collective-permute-start.3 = (bf16[2,64,4]{1,2,0:T(4,128)(2,1)S(1)}, bf16[2,64,4]{1,2,0:T(4,128)(2,1)S(1)}, u32[]{:S(2)}, u32[]{:S(2)}) collective-permute-start(bf16[2,64,4]{1,2,0:T(4,128)(2,1)S(1)} %copy.63), channel_id=1, source_target_pairs={{8,0},{9,1},{10,2},{11,3},{12,4},{13,5},{14,6},{15,7},{24,16},{25,... | collective-permute-start | bytes 3080 | tf_op jit(solution)/shard_map/ppermute | solution.py:36
  194.7 3.8 %collective-permute-start.2 = (bf16[2,64,4]{1,2,0:T(4,128)(2,1)S(1)}, bf16[2,64,4]{1,2,0:T(4,128)(2,1)S(1)}, u32[]{:S(2)}, u32[]{:S(2)}) collective-permute-start(bf16[2,64,4]{1,2,0:T(4,128)(2,1)S(1)} %copy.63), channel_id=1, source_target_pairs={{0,8},{1,9},{2,10},{3,11},{4,12},{5,13},{6,14},{7,15},{16,24},{17,... | collective-permute-start | bytes 3080 | tf_op jit(solution)/shard_map/ppermute | solution.py:34
  198.6 5.4 %collective-permute-start.4 = (bf16[6,2,4]{1,2,0:T(4,128)(2,1)S(1)}, bf16[6,2,4]{1,2,0:T(4,128)(2,1)S(1)}, u32[]{:S(2)}, u32[]{:S(2)}) collective-permute-start(bf16[6,2,4]{1,2,0:T(4,128)(2,1)S(1)} %get-tuple-element.35), channel_id=1, source_target_pairs={{0,1},{1,2},{2,3},{3,4},{4,5},{5,6},{6,7},{8,9},{9,10},{10,11},{11... | collective-permute-start | bytes 296 | tf_op jit(solution)/shard_map/ppermute | solution.py:34
  202.5 5.5 %collective-permute-start.5 = (bf16[6,2,4]{1,2,0:T(4,128)(2,1)S(1)}, bf16[6,2,4]{1,2,0:T(4,128)(2,1)S(1)}, u32[]{:S(2)}, u32[]{:S(2)}) collective-permute-start(bf16[6,2,4]{1,2,0:T(4,128)(2,1)S(1)} %get-tuple-element.36), channel_id=1, source_target_pairs={{1,0},{2,1},{3,2},{4,3},{5,4},{6,5},{7,6},{9,8},{10,9},{11,10},{12... | collective-permute-start | bytes 296 | tf_op jit(solution)/shard_map/ppermute | solution.py:36
  209.6 1.4 copy-start.5
  212.3 2.6 %slice-start = ((s8[4718592]{0:T(1024)(128)(4,1)}), s8[4194304]{0:T(1024)(128)(4,1)S(1)}, s32[]{:S(2)}) async-start(s8[4718592]{0:T(1024)(128)(4,1)} %bitcast.160), calls=%async_computation | async-start | bytes 8388608
  212.4 2.5 %slice-start.1 = ((s8[4718592]{0:T(1024)(128)(4,1)}), s8[524288]{0:T(1024)(128)(4,1)S(1)}, s32[]{:S(2)}) async-start(s8[4718592]{0:T(1024)(128)(4,1)} %bitcast.160), calls=%async_computation.1 | async-start | bytes 1048576
  218.1 0.7 copy-start.6
where the time goes:
time: 221 us; the launch traced here: 220 us
  blocking collectives  158 us (71%)
  matrix products  22.7 us (10%)
  local copies, waits for them, and re-layouts  12.8 us (6%)
  starting transfers between devices  9.84 us (4%)
  other arithmetic  9.17 us (4%)
  waiting for transfers between devices  6.16 us (3%)
    all_gather x3, blocking collectives, local(): fresh_now = lax.all_gather(fresh_own, 'patch', axis=0, tiled=True)  94.2 us
    all_gather x1, blocking collectives, local(): stale_all = lax.all_gather(stale_own, 'patch', axis=0, tiled=True)  33.2 us
    all_gather x1, blocking collectives, local(): gathered = lax.all_gather(own_tokens, 'patch', axis=0, tiled=True)  30.5 us
    dot_general x3, matrix products, local(): projected = jnp.dot(modulated, w_qkv[0], preferred_element_type=jnp.float32)  10.1 us
    dot_general x18, matrix products, convolve(): jnp.dot(window, weights[offset_row * 3 + offset_col], preferred_element_t...  8.16 us
    ppermute x2, starting transfers between devices, with_halo(): lax.ppermute(tail, axis, [(i, (i + 1) % count) for i in range(ends)])  6.94 us
  transfers between devices with their start and end apart: 6, of which 4 were waited for; matrix products, arithmetic and copies ran while one was open for 1% of the time, Pallas kernels for 0%

commit v1 on v0

v1 whole, which is shorter than its diff:
```python
import math

import jax
import jax.numpy as jnp
import numpy as np
from jax import lax
from jax.sharding import PartitionSpec as P

D = 1152
DH = 72
HEADS = 8
CH = 512
LATC = 4
TC = 256
DA = 576

EPSILON = 1e-06


def layer_norm(values):
    widened = values.astype(jnp.float32)
    average = jnp.mean(widened, axis=-1, keepdims=True)
    centred = widened - average
    variance = jnp.mean(centred * centred, axis=-1, keepdims=True)
    return centred * lax.rsqrt(variance + EPSILON)


def modulate(values, scale, shift):
    return (layer_norm(values) * (1.0 + scale) + shift).astype(jnp.bfloat16)


def attend(query, first, second):
    count = query.shape[0]
    total_keys = first.shape[0] + second.shape[0]
    key_value = jnp.concatenate([first, second], axis=0)
    keys = key_value[:, :DA].reshape(total_keys, HEADS, DH).transpose(1, 0, 2)
    values = key_value[:, DA:].reshape(total_keys, HEADS, DH).transpose(1, 0, 2)
    queries = query.reshape(count, HEADS, DH).transpose(1, 0, 2)

    def one_head(args):
        q, k, v = args
        scores = jnp.dot(q, k.T, preferred_element_type=jnp.float32) * (1.0 / math.sqrt(DH))
        exponent = jnp.exp(scores - jnp.max(scores, axis=1, keepdims=True))
        total = jnp.sum(exponent, axis=1, keepdims=True)
        return jnp.dot(exponent.astype(jnp.bfloat16), v, preferred_element_type=jnp.float32) / total

    if count * total_keys <= 256 * 512:
        heads = jnp.stack([one_head((queries[h], keys[h], values[h])) for h in range(HEADS)])
    else:
        heads = lax.map(one_head, (queries, keys, values))
    return heads.transpose(1, 0, 2).reshape(count, DA).astype(jnp.bfloat16)


def convolve(padded, weights, out_rows, out_cols):
    total = jnp.zeros((out_rows, out_cols, weights.shape[-1]), jnp.float32)
    for offset_row in range(3):
        for offset_col in range(3):
            window = padded[offset_row : offset_row + out_rows, offset_col : offset_col + out_cols]
            total = total + jnp.dot(
                window, weights[offset_row * 3 + offset_col], preferred_element_type=jnp.float32
            )
    return total


def patch_selector():
    sel = np.zeros((3, 3, 2, 2, LATC, 2, 2, 9 * LATC), np.float32)
    for dr in range(3):
        for ds in range(3):
            for pp in range(2):
                for qq in range(2):
                    for p in range(2):
                        for q in range(2):
                            dy = 2 * (dr - 1) + pp - p
                            dx = 2 * (ds - 1) + qq - q
                            if abs(dy) <= 1 and abs(dx) <= 1:
                                tap = (dy + 1) * 3 + dx + 1
                                for c in range(LATC):
                                    sel[dr, ds, pp, qq, c, p, q, tap * LATC + c] = 1.0
    return sel.reshape(-1, 9 * LATC)


def local(
    tokens,
    stale_kv,
    w_qkv,
    w_out,
    block_table,
    time_table,
    t_index,
    w_final,
    w_in,
    b_in,
    w_up,
    b_up,
):
    section = lax.axis_index("pipe")
    tile = lax.axis_index("patch")
    n_tiles = lax.axis_size("patch")
    swap = [(0, 1), (1, 0)]
    first_core = section == 0

    time_row = lax.dynamic_index_in_dim(time_table, t_index[0], 0, keepdims=False)
    own_tokens = lax.dynamic_index_in_dim(tokens, section, 0, keepdims=False)
    gathered = lax.all_gather(
        jnp.stack([own_tokens, stale_kv[0, 1]]), "patch", axis=1, tiled=True
    )
    x, stale = gathered[0], gathered[1]
    w_qkv_other = lax.ppermute(w_qkv[0], "pipe", swap)
    w_out_other = lax.ppermute(w_out[0], "pipe", swap)
    table_other = lax.ppermute(block_table[0], "pipe", swap)

    def of_block(block, own, other):
        return jnp.where(section == block, own, other)

    count = x.shape[0]
    rows = count // TC
    cols = TC // n_tiles
    wanted = None
    for block in range(2):
        table = of_block(block, block_table[0], table_other)
        w_block = of_block(block, w_qkv[0], w_qkv_other)
        wo_block = of_block(block, w_out[0], w_out_other)
        shift, scale, gate = (time_row[i] + table[i] for i in range(3))
        modulated = modulate(x, scale, shift)
        fresh = jnp.dot(modulated, w_block[:, DA:], preferred_element_type=jnp.float32).astype(
            jnp.bfloat16
        )
        if block == 0:
            got = lax.ppermute(fresh, "pipe", [(0, 1)])
            second = jnp.where(first_core, stale, got)
            asking, asking_x = modulated, x
        else:
            second = lax.ppermute(jnp.where(first_core, fresh, stale), "pipe", swap)

            def tile_of(a):
                grid = jnp.pad(a.reshape(rows, TC, D), ((0, 0), (1, 1), (0, 0)))
                cut = lax.dynamic_slice_in_dim(grid, tile * cols, cols + 2, 1)
                return cut.reshape(rows * (cols + 2), D)

            asking, asking_x = tile_of(modulated), tile_of(x)
        query = jnp.dot(asking, w_block[:, :DA], preferred_element_type=jnp.float32).astype(
            jnp.bfloat16
        )
        attended = attend(query, fresh, second)
        branch = jnp.dot(attended, wo_block, preferred_element_type=jnp.float32)
        x = (asking_x.astype(jnp.float32) + gate * branch).astype(jnp.bfloat16)

    final_input = modulate(x, time_row[4], time_row[3])
    patches = jnp.dot(final_input, w_final, preferred_element_type=jnp.float32).astype(jnp.bfloat16)
    patches = patches.reshape(rows, cols + 2, 4 * LATC)
    col_ids = tile * cols + jnp.arange(cols + 2) - 1
    inside = (col_ids >= 0) & (col_ids < TC)
    patches = jnp.where(inside[None, :, None], patches, jnp.zeros_like(patches))
    edge = jnp.where(first_core, patches[rows - 1], patches[0])
    got = lax.ppermute(edge, "pipe", swap)
    nothing = jnp.zeros_like(got)
    rim = jnp.concatenate(
        [
            jnp.where(first_core, nothing, got)[None],
            patches,
            jnp.where(first_core, got, nothing)[None],
        ],
        axis=0,
    )

    w_patch = (
        jnp.dot(jnp.asarray(patch_selector(), jnp.bfloat16), w_in, preferred_element_type=jnp.float32)
        .astype(jnp.bfloat16)
        .reshape(9 * 4 * LATC, 4 * CH)
    )
    wide = jnp.pad(rim, ((1, 1), (1, 1), (0, 0)))
    around = jnp.concatenate(
        [wide[i : i + rows + 2, j : j + cols + 2] for i in range(3) for j in range(3)], axis=-1
    )
    activation = jnp.dot(
        around.reshape((rows + 2) * (cols + 2), 9 * 4 * LATC), w_patch, preferred_element_type=jnp.float32
    ).reshape(rows + 2, cols + 2, 2, 2, CH)
    features = jax.nn.silu(activation + b_in).astype(jnp.bfloat16)
    features = features.transpose(0, 2, 1, 3, 4).reshape(2 * rows + 4, 2 * cols + 4, CH)[1:-1, 1:-1]
    row_ids = section * 2 * rows + jnp.arange(2 * rows + 2) - 1
    pixel_ids = tile * 2 * cols + jnp.arange(2 * cols + 2) - 1
    inside_rows = (row_ids >= 0) & (row_ids < 4 * rows)
    inside_cols = (pixel_ids >= 0) & (pixel_ids < 2 * TC)
    features = jnp.where(
        (inside_rows[:, None] & inside_cols[None, :])[:, :, None], features, jnp.zeros_like(features)
    )
    upsampled = jnp.repeat(jnp.repeat(features, 2, axis=0), 2, axis=1)[1:-1, 1:-1]
    decoded = convolve(upsampled, w_up, 4 * rows, 4 * cols) + b_up
    return decoded.astype(jnp.bfloat16)


def solution(mesh):
    placed = (
        P(None, ("grp", "patch"), None),
        P("pipe", None, ("grp", "patch"), None),
        P("pipe", None, None),
        P("pipe", None, None),
        P("pipe", None, None),
        P(),
        P("grp"),
        P(),
        P(),
        P(),
        P(),
        P(),
    )
    return jax.shard_map(
        local,
        mesh=mesh,
        in_specs=placed,
        out_specs=P(("grp", "pipe"), "patch", None),
        check_vma=False,
    )
```

time: 221 us -> 132 us (0.60)
  blocking collectives: 158 us -> 0 us
  waiting for transfers between devices: 6.16 us -> 39.8 us
  other arithmetic: 9.17 us -> 25 us
  matrix products: 22.7 us -> 37.7 us
  between operations: 1.4 us -> 14.7 us
  starting transfers between devices: 9.84 us -> 2.48 us
    all_gather x5 -> x0, blocking collectives: 158 us -> none  [the longest x3 94.2 us: local(): fresh_now = lax.all_gather(fresh_own, 'patch', axis=0, tiled=True)]
    all_gather x0 -> x1, waiting for transfers between devices: none -> 38.2 us  [local(): lax.all_gather(jnp.stack([own_tokens, stale_kv[0, 1]]), 'patch', axis=1,...]
    dot_general x12 -> x40, matrix products: 14.3 us -> 32.7 us  [the longest x16 17.1 us: one_head(): jnp.dot(q, k.T, preferred_element_type=jnp.float32) * (1.0 / math.sqrt(DH))]
    reduce_sum x3 -> x16, other arithmetic: 0.67 us -> 9.08 us  [one_head(): total = jnp.sum(exponent, axis=1, keepdims=True)]
    ppermute x6, starting transfers between devices: 9.84 us -> 2.48 us  [the longest x1 1.51 us: local(): got = lax.ppermute(fresh, 'pipe', [(0, 1)])]
    select_n x3 -> x4, other arithmetic: 0.33 us -> 6.94 us  [the longest x2 6.73 us: of_block(): return jnp.where(section == block, own, other)]
    slice x15 -> x4, local copies, waits for them, and re-layouts: 7.46 us -> 1.77 us  [the longest x2 1.3 us: attend(): values = key_value[:, DA:].reshape(total_keys, HEADS, DH).transpose(1, 0, 2)]
    ppermute x6, waiting for transfers between devices: 6.16 us -> 1.58 us  [the longest x1 1.19 us: local(): second = lax.ppermute(jnp.where(first_core, fresh, stale), 'pipe', swap)]
  transfers between devices with their start and end apart: 6 -> 7, of which waited for: 4 -> 4; matrix products, arithmetic and copies ran while one was open for 1% -> 27% of each run, Pallas kernels for 0% -> 0%
where the time goes in v1:
time: 132 us; the launch traced here: 130 us
  waiting for transfers between devices  39.8 us (30%)
  matrix products  37.7 us (29%)
  other arithmetic  25 us (19%)
  between operations  14.7 us (11%)
  local copies, waits for them, and re-layouts  10.6 us (8%)
  starting transfers between devices  2.48 us (2%)
    all_gather x1, waiting for transfers between devices, local(): lax.all_gather(jnp.stack([own_tokens, stale_kv[0, 1]]), 'patch', axis=1,...  38.2 us
    dot_general x16, matrix products, one_head(): jnp.dot(q, k.T, preferred_element_type=jnp.float32) * (1.0 / math.sqrt(DH))  17.1 us
    reduce_sum x16, other arithmetic, one_head(): total = jnp.sum(exponent, axis=1, keepdims=True)  9.08 us
    dot_general x16, matrix products, one_head(): jnp.dot(exponent.astype(jnp.bfloat16), v, preferred_element_type=jnp.floa...  6.76 us
    select_n x2, other arithmetic, of_block(): return jnp.where(section == block, own, other)  6.73 us
    dot_general x9, matrix products, convolve(): jnp.dot(window, weights[offset_row * 3 + offset_col], preferred_element_t...  4.77 us
    unnamed x66, local copies, waits for them, and re-layouts  3.06 us
    dot_general x2, matrix products, local(): jnp.dot(modulated, w_block[:, DA:], preferred_element_type=jnp.float32)  3.06 us
  transfers between devices with their start and end apart: 7, of which 4 were waited for; matrix products, arithmetic and copies ran while one was open for 27% of the time, Pallas kernels for 0%

profile of v1, /device:TPU:0, one launch (start us, length us, event | category | flops | bytes accessed | tf_op | source)
XLA Modules:
  0.0 130.3 jit_solution(15510677185052243714)
XLA Ops:
  12.0 1.4 %fusion.205 = (f32[1152]{0:T(1024)}, f32[1152]{0:T(1024)}) fusion(f32[100,5,1152]{2,0,1:T(8,128)} %param.18, s32[]{:T(128)S(6)} %select_n.93, s32[]{:T(128)S(6)} %add.275, s32[]{:T(128)S(6)} %add.276), kind=kLoop, calls=%fused_computation.334 | loop fusion | flops 1152 | bytes 18444 | tf_op jit(solution)/shard_map/add | solution.py:29
  15.2 38.2 %all-gather.2.cloned.1.call-done = bf16[2,256,1152]{2,1,0:T(8,128)(2,1)} async-done(((bf16[2,32,1152]{2,1,0:T(8,128)(2,1)}), bf16[2,256,1152]{2,1,0:T(8,128)(2,1)}) %all-gather.2.cloned.1.call-update) | async-done | bytes 1179664 | tf_op jit(solution)/shard_map/all_gather | solution.py:104
  53.3 1.2 convert_reduce_fusion.1
  54.6 1.4 %fusion.36 = f32[256]{0:T(256)S(1)} fusion(f32[256]{0:T(256)S(1)} %broadcast_multiply_fusion.1, bf16[2,256,1152]{2,1,0:T(8,128)(2,1)} %all-gather.2.cloned.1.call-done), kind=kLoop, calls=%fused_computation.54 | loop fusion | flops 1179392 | bytes 591872 | tf_op jit(solution)/shard_map/reduce_sum | solution.py:24
  56.0 6.0 %broadcast_select_fusion = (bf16[1152,1728]{0,1:T(8,128)(2,1)}, bf16[1152,1728]{0,1:T(8,128)(2,1)S(1)}) fusion(bf16[1152,1728]{0,1:T(8,128)(2,1)} %collective-permute-done.1, pred[]{:T(512)S(6)} %eq.5, bf16[1,1152,1728]{1,2,0:T(8,128)(2,1)} %param.15, pred[]{:T(512)S(6)} %eq.4), kind=kLoop, calls=%fused_computation | loop fusion | flops 3981312 | bytes 15925250 | tf_op jit(solution)/shard_map/jit(_where)/select_n | solution.py:113
  62.0 1.1 fusion.4
  63.1 1.5 %collective-permute-start.2 = (bf16[256,1152]{1,0:T(8,128)(2,1)S(1)}, bf16[256,1152]{1,0:T(8,128)(2,1)S(1)}, u32[]{:S(2)}, u32[]{:S(2)}) collective-permute-start(bf16[256,1152]{1,0:T(8,128)(2,1)S(1)} %fusion.4), channel_id=1, source_target_pairs={{0,8},{1,9},{2,10},{3,11},{4,12},{5,13},{6,14},{7,15},{16,24},{17,... | collective-permute-start | bytes 1769480 | tf_op jit(solution)/shard_map/ppermute | solution.py:129
  65.2 1.1 convolution_convert_fusion
  77.0 1.4 %fusion.135 = f32[256]{0:T(256)S(1)} fusion(f32[256,512]{1,0:T(8,128)} %get-tuple-element.46, f32[256]{0:T(256)S(1)} %get-tuple-element.45), kind=kLoop, calls=%fused_computation.196 | loop fusion | flops 261888 | bytes 526336 | tf_op jit(solution)/shard_map/reduce_sum | solution.py:44
  84.3 2.0 %broadcast_select_fusion.2 = (bf16[256,1152]{1,0:T(8,128)(2,1)}, bf16[256,1152]{1,0:T(8,128)(2,1)S(1)}) fusion(pred[]{:T(512)S(6)} %eq.4, bf16[2,256,1152]{2,1,0:T(8,128)(2,1)S(1)} %copy-done.2, bf16[1152,1728]{0,1:T(8,128)(2,1)S(1)} %copy-done.1, bf16[256,1152]{1,0:T(8,128)(2,1)S(1)} %get-tuple-element.52, f32[1152]{0:T(1024)S(1)} %get-tuple-element.6, ...), kind=kOutput, calls=%fused_computation.148 | convolution fusion | flops 681836544 | bytes 5031937 | tf_op jit(solution)/shard_map/dot_general | solution.py:125
  87.3 1.2 collective-permute-done.4
  90.6 1.6 %fusion.239 = (f32[34]{0:T(128)S(1)}, f32[34,512]{1,0:T(8,128)}) fusion(bf16[8,512,72]{1,2,0:T(8,128)(2,1)S(1)} %bitcast.465, bf16[8,34,72]{2,1,0:T(8,128)(2,1)} %bitcast.490), kind=kOutput, calls=%fused_computation.383 | convolution fusion | flops 2541534 | bytes 153736 | tf_op jit(solution)/shard_map/dot_general | solution.py:42
  92.1 1.6 %fusion.238 = (f32[34]{0:T(128)S(1)}, f32[34,512]{1,0:T(8,128)}) fusion(bf16[8,512,72]{1,2,0:T(8,128)(2,1)S(1)} %bitcast.466, bf16[8,34,72]{2,1,0:T(8,128)(2,1)} %bitcast.491), kind=kOutput, calls=%fused_computation.382 | convolution fusion | flops 2541534 | bytes 153736 | tf_op jit(solution)/shard_map/dot_general | solution.py:42
  93.7 1.6 %fusion.237 = (f32[34]{0:T(128)S(1)}, f32[34,512]{1,0:T(8,128)}) fusion(bf16[8,512,72]{1,2,0:T(8,128)(2,1)S(1)} %bitcast.467, bf16[8,34,72]{2,1,0:T(8,128)(2,1)} %bitcast.492), kind=kOutput, calls=%fused_computation.381 | convolution fusion | flops 2541534 | bytes 153736 | tf_op jit(solution)/shard_map/dot_general | solution.py:42
  95.3 1.6 %fusion.236 = (f32[34]{0:T(128)S(1)}, f32[34,512]{1,0:T(8,128)}) fusion(bf16[8,512,72]{1,2,0:T(8,128)(2,1)S(1)} %bitcast.468, bf16[8,34,72]{2,1,0:T(8,128)(2,1)} %bitcast.493), kind=kOutput, calls=%fused_computation.380 | convolution fusion | flops 2541534 | bytes 153736 | tf_op jit(solution)/shard_map/dot_general | solution.py:42
  96.9 1.6 %fusion.235 = (f32[34]{0:T(128)S(1)}, f32[34,512]{1,0:T(8,128)}) fusion(bf16[8,512,72]{1,2,0:T(8,128)(2,1)S(1)} %bitcast.469, bf16[8,34,72]{2,1,0:T(8,128)(2,1)} %bitcast.494), kind=kOutput, calls=%fused_computation.379 | convolution fusion | flops 2541534 | bytes 153736 | tf_op jit(solution)/shard_map/dot_general | solution.py:42
  99.3 1.2 fusion.181
  101.6 1.1 fusion.177
  104.9 1.1 fusion.91
  106.0 1.1 fusion.89
  107.1 1.1 fusion.87
  109.6 1.9 %convert_reduce_fusion.2 = (f32[34]{0:T(128)S(1)}, bf16[34,1152]{1,0:T(8,128)(2,1)S(1)}) fusion(bf16[34,576]{1,0:T(8,128)(2,1)S(1)} %convert_element_type.157, bf16[576,1152]{1,0:T(8,128)(2,1)} %collective-permute-done.3, pred[]{:T(512)S(6)} %eq.5, bf16[1,576,1152]{2,1,0:T(8,128)(2,1)S(1)} %copy-done.12, f32[1152]{0:T(1024)S(1)} %get-tuple-element.7, ...), kind=kOutput, calls=%fused_computation.212 | convolution fusion | flops 46020064 | bytes 3366285 | tf_op jit(solution)/shard_map/dot_general | solution.py:145
  115.9 2.5 %fusion.226 = (bf16[4,128,512]{2,0,1:T(4,128)(2,1)S(1)}, bf16[4,128,512]{2,0,1:T(4,128)(2,1)S(1)}, bf16[4,128,512]{2,0,1:T(4,128)(2,1)S(1)}, bf16[4,128,512]{2,0...) fusion(bf16[8,132,512]{2,0,1:T(8,128)(2,1)S(1)} %bitcast.448), kind=kLoop, calls=%fused_computation.370 | loop fusion | bytes 9437184 | tf_op jit(solution)/shard_map/slice | solution.py:58
  122.2 1.2 fusion.28
  (171 shorter events, 39.9 us)
Async XLA Ops:
  6.5 46.8 %all-gather.2.cloned.1.call-start = ((), (), s32[]{:S(2)}) async-start(), calls=%async_computation | async-start | bytes 1327104 | tf_op jit(solution)/shard_map/all_gather | solution.py:104
  6.5 49.4 %collective-permute-start.1 = (bf16[1152,1728]{0,1:T(8,128)(2,1)}, bf16[1152,1728]{0,1:T(8,128)(2,1)}, u32[]{:S(2)}, u32[]{:S(2)}) collective-permute-start(bf16[1152,1728]{0,1:T(8,128)(2,1)} %bitcast.452), channel_id=1, source_target_pairs={{0,8},{8,0},{1,9},{9,1},{2,10},{10,2},{3,11},{11,3},{4,12},{12,4},... | collective-permute-start | bytes 11943944 | tf_op jit(solution)/shard_map/ppermute | solution.py:108
  9.8 3.8 %collective-permute-start = (f32[3,1152]{1,0:T(4,128)S(1)}, f32[3,1152]{1,0:T(4,128)S(1)}, u32[]{:S(2)}, u32[]{:S(2)}) collective-permute-start(f32[3,1152]{1,0:T(4,128)S(1)} %bitcast.504), channel_id=1, source_target_pairs={{0,8},{8,0},{1,9},{9,1},{2,10},{10,2},{3,11},{11,3},{4,12},{12,4},... | collective-permute-start | bytes 41480 | tf_op jit(solution)/shard_map/ppermute | solution.py:110
  10.2 71.8 %collective-permute-start.3 = (bf16[576,1152]{1,0:T(8,128)(2,1)}, bf16[576,1152]{1,0:T(8,128)(2,1)}, u32[]{:S(2)}, u32[]{:S(2)}) collective-permute-start(bf16[576,1152]{1,0:T(8,128)(2,1)} %bitcast.470), channel_id=1, source_target_pairs={{0,8},{8,0},{1,9},{9,1},{2,10},{10,2},{3,11},{11,3},{4,12},{12,4},... | collective-permute-start | bytes 3981320 | tf_op jit(solution)/shard_map/ppermute | solution.py:109
  55.9 6.0 %copy-start.2 = (bf16[2,256,1152]{2,1,0:T(8,128)(2,1)S(1)}, bf16[2,256,1152]{2,1,0:T(8,128)(2,1)}, u32[]{:S(2)}) copy-start(bf16[2,256,1152]{2,1,0:T(8,128)(2,1)} %all-gather.2.cloned.1.call-done) | copy-start | bytes 3538948
  62.0 3.2 %copy-start.17 = (bf16[576,36]{1,0:T(8,128)(2,1)S(1)}, bf16[576,36]{1,0:T(8,128)(2,1)}, u32[]{:S(2)}) copy-start(bf16[576,36]{1,0:T(8,128)(2,1)} %constant.76.clone) | copy-start | bytes 124420
  62.0 3.2 %copy-start.18 = (bf16[36,512]{1,0:T(8,128)(2,1)S(1)}, bf16[36,512]{1,0:T(8,128)(2,1)}, u32[]{:S(2)}) copy-start(bf16[36,512]{1,0:T(8,128)(2,1)} %param.21) | copy-start | bytes 110596
  63.1 3.9 %collective-permute-start.2 = (bf16[256,1152]{1,0:T(8,128)(2,1)S(1)}, bf16[256,1152]{1,0:T(8,128)(2,1)S(1)}, u32[]{:S(2)}, u32[]{:S(2)}) collective-permute-start(bf16[256,1152]{1,0:T(8,128)(2,1)S(1)} %fusion.4), channel_id=1, source_target_pairs={{0,8},{1,9},{2,10},{3,11},{4,12},{5,13},{6,14},{7,15},{16,24},{17,... | collective-permute-start | bytes 1769480 | tf_op jit(solution)/shard_map/ppermute | solution.py:129
  76.6 2.4 %copy-start.9 = (f32[256,512]{1,0:T(8,128)S(1)}, f32[256,512]{1,0:T(8,128)}, u32[]{:S(2)}) copy-start(f32[256,512]{1,0:T(8,128)} %get-tuple-element.38) | copy-start | bytes 1572868
  76.8 2.4 %copy-start.10 = (f32[256,512]{1,0:T(8,128)S(1)}, f32[256,512]{1,0:T(8,128)}, u32[]{:S(2)}) copy-start(f32[256,512]{1,0:T(8,128)} %get-tuple-element.36) | copy-start | bytes 1572868
  77.0 2.4 %copy-start.13 = (bf16[512,576]{0,1:T(8,128)(2,1)S(1)}, bf16[512,576]{0,1:T(8,128)(2,1)}, u32[]{:S(2)}) copy-start(bf16[512,576]{0,1:T(8,128)(2,1)} %copy.16) | copy-start | bytes 1769476
  86.3 2.2 %collective-permute-start.4 = (bf16[256,1152]{1,0:T(8,128)(2,1)}, bf16[256,1152]{1,0:T(8,128)(2,1)S(1)}, u32[]{:S(2)}, u32[]{:S(2)}) collective-permute-start(bf16[256,1152]{1,0:T(8,128)(2,1)} %get-tuple-element.53), channel_id=1, source_target_pairs={{0,8},{8,0},{1,9},{9,1},{2,10},{10,2},{3,11},{11,3},{4,12},{12,4},... | collective-permute-start | bytes 1769480 | tf_op jit(solution)/shard_map/ppermute | solution.py:133
  98.7 9.5 %copy-start.15 = (f32[34,512]{1,0:T(8,128)S(1)}, f32[34,512]{1,0:T(8,128)}, u32[]{:S(2)}) copy-start(f32[34,512]{1,0:T(8,128)} %get-tuple-element.62) | copy-start | bytes 208900
  98.7 9.7 %copy-start.14 = (f32[34,512]{1,0:T(8,128)S(1)}, f32[34,512]{1,0:T(8,128)}, u32[]{:S(2)}) copy-start(f32[34,512]{1,0:T(8,128)} %get-tuple-element.64) | copy-start | bytes 208900
  99.3 10.1 %copy-start.12 = (bf16[1,576,1152]{2,1,0:T(8,128)(2,1)S(1)}, bf16[1,576,1152]{2,1,0:T(8,128)(2,1)}, u32[]{:S(2)}) copy-start(bf16[1,576,1152]{2,1,0:T(8,128)(2,1)} %param.16) | copy-start | bytes 3981316
  109.5 2.2 %copy-start.19 = (f32[1152]{0:T(1024)S(1)}, f32[1152]{0:T(1024)}, u32[]{:S(2)}) copy-start(f32[1152]{0:T(1024)} %get-tuple-element.11) | copy-start | bytes 13828
  109.5 2.2 %copy-start.20 = (f32[1152]{0:T(1024)S(1)}, f32[1152]{0:T(1024)}, u32[]{:S(2)}) copy-start(f32[1152]{0:T(1024)} %get-tuple-element.12) | copy-start | bytes 13828
  109.5 2.2 %copy-start.22 = (bf16[1152,16]{0,1:T(8,128)(2,1)S(1)}, bf16[1152,16]{0,1:T(8,128)(2,1)}, u32[]{:S(2)}) copy-start(bf16[1152,16]{0,1:T(8,128)(2,1)} %param.20) | copy-start | bytes 110596
  109.5 2.5 %copy-start.24 = (pred[4]{0:T(512)(128)(4,1)S(1)}, pred[4]{0:T(512)(128)(4,1)}, u32[]{:S(2)}) copy-start(pred[4]{0:T(512)(128)(4,1)} %compare_and_fusion.2) | copy-start | bytes 16
  109.5 2.5 %copy-start.25 = (pred[66]{0:T(512)(128)(4,1)S(1)}, pred[66]{0:T(512)(128)(4,1)}, u32[]{:S(2)}) copy-start(pred[66]{0:T(512)(128)(4,1)} %compare_and_fusion.1) | copy-start | bytes 202
  109.5 2.5 %copy-start.3 = (bf16[576,512]{1,0:T(8,128)(2,1)S(1)}, bf16[576,512]{1,0:T(8,128)(2,1)}, u32[]{:S(2)}) copy-start(bf16[576,512]{1,0:T(8,128)(2,1)} %convolution_convert_fusion) | copy-start | bytes 1769476
  112.0 1.2 collective-permute-start.5
  115.7 2.6 %slice-start = ((s8[4718592]{0:T(1024)(128)(4,1)}), s8[4194304]{0:T(1024)(128)(4,1)S(1)}, s32[]{:S(2)}) async-start(s8[4718592]{0:T(1024)(128)(4,1)} %bitcast.450), calls=%async_computation.1 | async-start | bytes 8388608
  115.8 2.5 %slice-start.1 = ((s8[4718592]{0:T(1024)(128)(4,1)}), s8[524288]{0:T(1024)(128)(4,1)S(1)}, s32[]{:S(2)}) async-start(s8[4718592]{0:T(1024)(128)(4,1)} %bitcast.450), calls=%async_computation.2 | async-start | bytes 1048576
  (12 other events, 18.6 us)
Sparse Core Ops, SparseCore 0:
  9.6 43.7 all-gather.1

commit v2 on v1

--- a/solution.py
+++ b/solution.py
@@ -77,6 +77,31 @@
                                 for c in range(LATC):
                                     sel[dr, ds, pp, qq, c, p, q, tap * LATC + c] = 1.0
     return sel.reshape(-1, 9 * LATC)
+
+
+def in_order(pieces, first):
+    count = len(pieces)
+    twice = jnp.concatenate([jnp.stack(pieces)] * 2, axis=0)
+    return lax.dynamic_slice_in_dim(twice, (count - first) % count, count, 0)
+
+
+def gather_patch(own):
+    n = lax.axis_size("patch")
+    inner = 2 ** (int(math.log2(n)) // 2)
+    outer = n // inner
+    here = lax.axis_index("patch")
+
+    def shifted(block, k_outer, k_inner):
+        route = []
+        for i in range(n):
+            o, e = divmod(i, inner)
+            route.append(((o + k_outer) % outer * inner + (e + k_inner) % inner, i))
+        return lax.ppermute(block, "patch", route)
+
+    column = in_order([own] + [shifted(own, k, 0) for k in range(1, outer)], here // inner)
+    pieces = [column] + [shifted(column, 0, k) for k in range(1, inner)]
+    both = in_order(pieces, here % inner)
+    return both.transpose(1, 0, 2, 3).reshape(n * own.shape[0], own.shape[1])
 
 
 def local(
@@ -101,10 +126,8 @@
 
     time_row = lax.dynamic_index_in_dim(time_table, t_index[0], 0, keepdims=False)
     own_tokens = lax.dynamic_index_in_dim(tokens, section, 0, keepdims=False)
-    gathered = lax.all_gather(
-        jnp.stack([own_tokens, stale_kv[0, 1]]), "patch", axis=1, tiled=True
-    )
-    x, stale = gathered[0], gathered[1]
+    x = gather_patch(own_tokens)
+    stale = gather_patch(stale_kv[0, 1])
     w_qkv_other = lax.ppermute(w_qkv[0], "pipe", swap)
     w_out_other = lax.ppermute(w_out[0], "pipe", swap)
     table_other = lax.ppermute(block_table[0], "pipe", swap)

time: 132 us -> 90.8 us (0.69)
  waiting for transfers between devices: 39.8 us -> 14.9 us
  between operations: 14.7 us -> 1.54 us
  starting transfers between devices: 2.48 us -> 14.8 us
  other arithmetic: 25 us -> 17 us
  matrix products: 37.7 us -> 30.3 us
    all_gather x1 -> x0, waiting for transfers between devices: 38.2 us -> none  [local(): lax.all_gather(jnp.stack([own_tokens, stale_kv[0, 1]]), 'patch', axis=1,...]
    ppermute x0 -> x8, waiting for transfers between devices: none -> 13.6 us  [shifted(): return lax.ppermute(block, 'patch', route)]
    ppermute x0 -> x8, starting transfers between devices: none -> 12.3 us  [shifted(): return lax.ppermute(block, 'patch', route)]
    dot_general x16, matrix products: 17.1 us -> 9.77 us  [one_head(): jnp.dot(q, k.T, preferred_element_type=jnp.float32) * (1.0 / math.sqrt(DH))]
    reduce_sum x16, other arithmetic: 9.08 us -> 4.47 us  [one_head(): total = jnp.sum(exponent, axis=1, keepdims=True)]
    dot_general x2, matrix products: 2.78 us -> 4.61 us  [local(): branch = jnp.dot(attended, wo_block, preferred_element_type=jnp.float32)]
    squeeze x0 -> x2, local copies, waits for them, and re-layouts: none -> 1.84 us  [the longest x1 0.94 us: local(): stale = gather_patch(stale_kv[0, 1])]
    dot_general x16, matrix products: 6.76 us -> 5.01 us  [one_head(): jnp.dot(exponent.astype(jnp.bfloat16), v, preferred_element_type=jnp.floa...]
  transfers between devices with their start and end apart: 7 -> 14, of which waited for: 4 -> 6; matrix products, arithmetic and copies ran while one was open for 27% -> 38% of each run, Pallas kernels for 0% -> 0%
where the time goes in v2:
time: 90.8 us; the launch traced here: 90.2 us
  matrix products  30.3 us (33%)
  other arithmetic  17 us (19%)
  waiting for transfers between devices  14.9 us (16%)
  starting transfers between devices  14.8 us (16%)
  local copies, waits for them, and re-layouts  11.6 us (13%)
  between operations  1.54 us (2%)
    ppermute x8, waiting for transfers between devices, shifted(): return lax.ppermute(block, 'patch', route)  13.6 us
    ppermute x8, starting transfers between devices, shifted(): return lax.ppermute(block, 'patch', route)  12.3 us
    dot_general x16, matrix products, one_head(): jnp.dot(q, k.T, preferred_element_type=jnp.float32) * (1.0 / math.sqrt(DH))  9.77 us
    select_n x2, other arithmetic, of_block(): return jnp.where(section == block, own, other)  6.01 us
    dot_general x16, matrix products, one_head(): jnp.dot(exponent.astype(jnp.bfloat16), v, preferred_element_type=jnp.floa...  5.01 us
    dot_general x9, matrix products, convolve(): jnp.dot(window, weights[offset_row * 3 + offset_col], preferred_element_t...  4.76 us
    dot_general x2, matrix products, local(): branch = jnp.dot(attended, wo_block, preferred_element_type=jnp.float32)  4.61 us
    reduce_sum x16, other arithmetic, one_head(): total = jnp.sum(exponent, axis=1, keepdims=True)  4.47 us
  transfers between devices with their start and end apart: 14, of which 6 were waited for; matrix products, arithmetic and copies ran while one was open for 38% of the time, Pallas kernels for 0%

profile of v2, /device:TPU:0, one launch (start us, length us, event | category | flops | bytes accessed | tf_op | source)
XLA Modules:
  0.0 90.2 jit_solution(7336790830022229348)
XLA Ops:
  0.9 5.0 %collective-permute-start.6 = (bf16[32,1152]{1,0:T(8,128)(2,1)S(1)}, bf16[32,1152]{1,0:T(8,128)(2,1)S(1)}, u32[]{:S(2)}, u32[]{:S(2)}) collective-permute-start(bf16[32,1152]{1,0:T(8,128)(2,1)S(1)} %slice_bitcast_fusion.64), channel_id=1, source_target_pairs={{2,0},{3,1},{4,2},{5,3},{6,4},{7,5},{0,6},{1,7},{10,8},{11,9},{12,... | collective-permute-start | bytes 221192 | tf_op jit(solution)/shard_map/ppermute | solution.py:99
  7.9 2.9 %collective-permute-start = (bf16[32,1152]{1,0:T(8,128)(2,1)S(1)}, bf16[32,1152]{1,0:T(8,128)(2,1)S(1)}, u32[]{:S(2)}, u32[]{:S(2)}) collective-permute-start(bf16[32,1152]{1,0:T(8,128)(2,1)S(1)} %get-tuple-element.33), channel_id=1, source_target_pairs={{2,0},{3,1},{4,2},{5,3},{6,4},{7,5},{0,6},{1,7},{10,8},{11,9},{12,... | collective-permute-start | bytes 221192 | tf_op jit(solution)/shard_map/ppermute | solution.py:99
  12.4 2.0 %convolution_convert_fusion = bf16[576,512]{1,0:T(8,128)(2,1)} fusion(bf16[576,36]{1,0:T(8,128)(2,1)} %constant.118.clone, bf16[36,512]{1,0:T(8,128)(2,1)S(1)} %copy-done), kind=kOutput, calls=%fused_computation.33 | convolution fusion | flops 21528576 | bytes 668160 | tf_op jit(solution)/shard_map/dot_general | solution.py:190
  16.0 1.2 %collective-permute-start.1 = (bf16[32,1152]{1,0:T(8,128)(2,1)S(1)}, bf16[32,1152]{1,0:T(8,128)(2,1)S(1)}, u32[]{:S(2)}, u32[]{:S(2)}) collective-permute-start(bf16[32,1152]{1,0:T(8,128)(2,1)S(1)} %get-tuple-element.33), channel_id=1, source_target_pairs={{4,0},{5,1},{6,2},{7,3},{0,4},{1,5},{2,6},{3,7},{12,8},{13,9},{14,... | collective-permute-start | bytes 221192 | tf_op jit(solution)/shard_map/ppermute | solution.py:99
  18.2 4.1 %collective-permute-done.1 = bf16[32,1152]{1,0:T(8,128)(2,1)S(1)} collective-permute-done((bf16[32,1152]{1,0:T(8,128)(2,1)S(1)}, bf16[32,1152]{1,0:T(8,128)(2,1)S(1)}, u32[]{:S(2)}, u32[]{:S(2)}) %collective-permute-start.1) | collective-permute-done | bytes 73760 | tf_op jit(solution)/shard_map/ppermute | solution.py:99
  22.5 2.0 %collective-permute-done.2 = bf16[32,1152]{1,0:T(8,128)(2,1)S(1)} collective-permute-done((bf16[32,1152]{1,0:T(8,128)(2,1)S(1)}, bf16[32,1152]{1,0:T(8,128)(2,1)S(1)}, u32[]{:S(2)}, u32[]{:S(2)}) %collective-permute-start.2) | collective-permute-done | bytes 73760 | tf_op jit(solution)/shard_map/ppermute | solution.py:99
  24.6 1.6 %collective-permute-start.3 = (bf16[4,32,1152]{2,1,0:T(8,128)(2,1)S(1)}, bf16[4,32,1152]{2,1,0:T(8,128)(2,1)S(1)}, u32[]{:S(2)}, u32[]{:S(2)}) collective-permute-start(bf16[4,32,1152]{2,1,0:T(8,128)(2,1)S(1)} %constant_dynamic-slice_fusion.1), channel_id=1, source_target_pairs={{1,0},{0,1},{3,2},{2,3},{5,4},{4,5},{7,6},{6,7},{9,8},{8,9},{11,10... | collective-permute-start | bytes 884744 | tf_op jit(solution)/shard_map/ppermute | solution.py:99
  26.9 7.5 %collective-permute-done.3 = bf16[4,32,1152]{2,1,0:T(8,128)(2,1)S(1)} collective-permute-done((bf16[4,32,1152]{2,1,0:T(8,128)(2,1)S(1)}, bf16[4,32,1152]{2,1,0:T(8,128)(2,1)S(1)}, u32[]{:S(2)}, u32[]{:S(2)}) %collective-permute-start.3) | collective-permute-done | bytes 294944 | tf_op jit(solution)/shard_map/ppermute | solution.py:99
  36.0 6.0 %broadcast_select_fusion = (bf16[1152,1728]{0,1:T(8,128)(2,1)}, bf16[1152,1728]{0,1:T(8,128)(2,1)S(1)}) fusion(bf16[1152,1728]{0,1:T(8,128)(2,1)} %collective-permute-done.5, pred[]{:T(512)S(6)} %eq.19, bf16[1,1152,1728]{1,2,0:T(8,128)(2,1)} %param.15, pred[]{:T(512)S(6)} %eq.18), kind=kLoop, calls=%fused_computation | loop fusion | flops 3981312 | bytes 15925250 | tf_op jit(solution)/shard_map/jit(_where)/select_n | solution.py:136
  43.0 1.5 %collective-permute-start.10 = (bf16[256,1152]{1,0:T(8,128)(2,1)S(1)}, bf16[256,1152]{1,0:T(8,128)(2,1)S(1)}, u32[]{:S(2)}, u32[]{:S(2)}) collective-permute-start(bf16[256,1152]{1,0:T(8,128)(2,1)S(1)} %fusion.4), channel_id=1, source_target_pairs={{0,8},{1,9},{2,10},{3,11},{4,12},{5,13},{6,14},{7,15},{16,24},{17,... | collective-permute-start | bytes 1769480 | tf_op jit(solution)/shard_map/ppermute | solution.py:152
  46.8 1.1 %fusion.230 = (f32[256]{0:T(256)S(1)}, f32[256,512]{1,0:T(8,128)}) fusion(bf16[8,512,72]{1,2,0:T(8,128)(2,1)S(1)} %bitcast.480, bf16[8,256,72]{1,2,0:T(8,128)(2,1)S(1)} %bitcast.521), kind=kOutput, calls=%fused_computation.401 | convolution fusion | flops 19136256 | bytes 635904 | tf_op jit(solution)/shard_map/dot_general | solution.py:42
  47.8 1.1 %fusion.231 = (f32[256]{0:T(256)S(1)}, f32[256,512]{1,0:T(8,128)}) fusion(bf16[8,512,72]{1,2,0:T(8,128)(2,1)S(1)} %bitcast.481, bf16[8,256,72]{1,2,0:T(8,128)(2,1)S(1)} %bitcast.522), kind=kOutput, calls=%fused_computation.402 | convolution fusion | flops 19136256 | bytes 635904 | tf_op jit(solution)/shard_map/dot_general | solution.py:42
  48.9 1.1 %fusion.232 = (f32[256]{0:T(256)S(1)}, f32[256,512]{1,0:T(8,128)}) fusion(bf16[8,512,72]{1,2,0:T(8,128)(2,1)S(1)} %bitcast.482, bf16[8,256,72]{1,2,0:T(8,128)(2,1)S(1)} %bitcast.523), kind=kOutput, calls=%fused_computation.403 | convolution fusion | flops 19136256 | bytes 635904 | tf_op jit(solution)/shard_map/dot_general | solution.py:42
  52.1 1.1 %fusion.235 = (f32[256]{0:T(256)S(1)}, f32[256,512]{1,0:T(8,128)}) fusion(bf16[8,512,72]{1,2,0:T(8,128)(2,1)S(1)} %bitcast.485, bf16[8,256,72]{1,2,0:T(8,128)(2,1)S(1)} %bitcast.526), kind=kOutput, calls=%fused_computation.406 | convolution fusion | flops 19136256 | bytes 635904 | tf_op jit(solution)/shard_map/dot_general | solution.py:42
  53.2 1.1 %fusion.236 = (f32[256]{0:T(256)S(1)}, f32[256,512]{1,0:T(8,128)}) fusion(bf16[8,512,72]{1,2,0:T(8,128)(2,1)S(1)} %bitcast.486, bf16[8,256,72]{1,2,0:T(8,128)(2,1)S(1)} %bitcast.527), kind=kOutput, calls=%fused_computation.407 | convolution fusion | flops 19136256 | bytes 635904 | tf_op jit(solution)/shard_map/dot_general | solution.py:42
  54.6 1.1 %copy.44 = bf16[512,576]{0,1:T(8,128)(2,1)} copy(bf16[512,576]{1,0:T(8,128)(2,1)S(1)} %get-tuple-element.22) | data formatting | bytes 1179648 | tf_op jit(solution)/shard_map/slice | solution.py:37
  55.7 1.4 %fusion.129 = f32[256]{0:T(256)S(1)} fusion(f32[256,512]{1,0:T(8,128)} %get-tuple-element.40, f32[256]{0:T(256)S(1)} %get-tuple-element.39), kind=kLoop, calls=%fused_computation.199 | loop fusion | flops 261888 | bytes 526336 | tf_op jit(solution)/shard_map/reduce_sum | solution.py:44
  57.1 1.2 %fusion.63 = bf16[8,256,72]{1,2,0:T(8,128)(2,1)S(1)} fusion(f32[256,512]{1,0:T(8,128)S(1)} %copy-done.12, f32[256]{0:T(256)S(1)} %get-tuple-element.39, bf16[8,512,72]{1,2,0:T(8,128)(2,1)} %bitcast.497, f32[256]{0:T(256)S(1)} %fusion.129), kind=kOutput, calls=%fused_computation.109 | convolution fusion | flops 19173376 | bytes 636928 | tf_op jit(solution)/shard_map/dot_general | solution.py:45
  62.1 2.3 %convert_reduce_fusion = (f32[256]{0:T(256)S(1)}, bf16[256,1152]{1,0:T(8,128)(2,1)S(1)}) fusion(bf16[256,576]{0,1:T(8,128)(2,1)S(1)} %bitcast.535, bf16[576,1152]{1,0:T(8,128)(2,1)} %collective-permute-done.11, pred[]{:T(512)S(6)} %eq.18, bf16[1,576,1152]{2,1,0:T(8,128)(2,1)} %param.16, f32[1152]{0:T(1024)S(1)} %get-tuple-element.13, ...), kind=kOutput, calls=%fused_computation.9 | convolution fusion | flops 341876480 | bytes 4724225 | tf_op jit(solution)/shard_map/dot_general | solution.py:168
  64.8 1.1 %bitcast_select_fusion = (bf16[256,1152]{1,0:T(8,128)(2,1)S(1)}, bf16[256,1152]{1,0:T(8,128)(2,1)S(1)}) fusion(bf16[4,2,32,1152]{3,2,1,0:T(8,128)(2,1)S(1)} %copy-done.5, pred[]{:T(512)S(6)} %eq.18, bf16[1152,1728]{0,1:T(8,128)(2,1)S(1)} %copy-done.2, bf16[256,1152]{1,0:T(8,128)(2,1)S(1)} %get-tuple-element.56, f32[1152]{0:T(1024)S(1)} %get-tuple-element.6, ...), kind=kOutput, calls=%fused_computation.160 | convolution fusion | flops 681836544 | bytes 5031937 | tf_op jit(solution)/shard_map/dot_general | solution.py:148
  68.5 1.4 %fusion.89 = (bf16[512,576]{1,0:T(8,128)(2,1)S(1)}, bf16[512,576]{1,0:T(8,128)(2,1)S(1)}) fusion(bf16[256,1152]{1,0:T(8,128)(2,1)S(1)} %get-tuple-element.58, bf16[256,1152]{1,0:T(8,128)(2,1)} %collective-permute-done.12), kind=kLoop, calls=%fused_computation.145 | loop fusion | flops 2359296 | bytes 2359296 | tf_op jit(solution)/shard_map/concatenate | solution.py:35
  75.9 2.3 %convert_reduce_fusion.1 = (f32[34]{0:T(128)S(1)}, bf16[34,1152]{1,0:T(8,128)(2,1)S(1)}) fusion(bf16[34,576]{1,0:T(8,128)(2,1)S(1)} %convert_element_type.167, bf16[576,1152]{1,0:T(8,128)(2,1)} %collective-permute-done.11, pred[]{:T(512)S(6)} %eq.19, bf16[1,576,1152]{2,1,0:T(8,128)(2,1)} %param.16, f32[1152]{0:T(1024)S(1)} %get-tuple-element.7, ...), kind=kOutput, calls=%fused_computation.225 | convolution fusion | flops 46020064 | bytes 3366285 | tf_op jit(solution)/shard_map/dot_general | solution.py:168
  82.6 2.5 %fusion.229 = (bf16[4,128,512]{2,0,1:T(4,128)(2,1)S(1)}, bf16[4,128,512]{2,0,1:T(4,128)(2,1)S(1)}, bf16[4,128,512]{2,0,1:T(4,128)(2,1)S(1)}, bf16[4,128,512]{2,0...) fusion(bf16[8,132,512]{2,0,1:T(8,128)(2,1)S(1)} %bitcast.475), kind=kLoop, calls=%fused_computation.400 | loop fusion | bytes 9437184 | tf_op jit(solution)/shard_map/slice | solution.py:58
  88.9 1.2 %fusion.24 = bf16[4,128,512]{2,1,0:T(8,128)(2,1)} fusion(f32[4,128,512]{2,1,0:T(8,128)S(1)} %convolution_add_fusion.1, bf16[4,128,512]{2,0,1:T(4,128)(2,1)S(1)} %get-tuple-element.24, f32[512]{0:T(512)S(1)} %copy-done.17, bf16[9,512,512]{2,1,0:T(8,128)(2,1)S(1)} %bitcast.478), kind=kOutput, calls=%fused_computation.34 | convolution fusion | flops 269221888 | bytes 2623488 | tf_op jit(solution)/shard_map/dot_general | solution.py:59
  (197 shorter events, 35.0 us)
Async XLA Ops:
  0.0 12.4 %copy-start = (bf16[36,512]{1,0:T(8,128)(2,1)S(1)}, bf16[36,512]{1,0:T(8,128)(2,1)}, u32[]{:S(2)}) copy-start(bf16[36,512]{1,0:T(8,128)(2,1)} %param.21) | copy-start | bytes 110596
  0.0 24.4 %copy-start.15 = (bf16[2,32,1152]{2,1,0:T(8,128)(2,1)S(1)}, bf16[2,32,1152]{2,1,0:T(8,128)(2,1)}, u32[]{:S(2)}) copy-start(bf16[2,32,1152]{2,1,0:T(8,128)(2,1)} %param.13) | copy-start | bytes 442372
  0.0 17.2 %copy-start.16 = (f32[1,3,1152]{2,0,1:T(1,128)S(1)}, f32[1,3,1152]{2,0,1:T(1,128)}, u32[]{:S(2)}) copy-start(f32[1,3,1152]{2,0,1:T(1,128)} %param.17) | copy-start | bytes 41476
  0.9 23.6 %collective-permute-start.6 = (bf16[32,1152]{1,0:T(8,128)(2,1)S(1)}, bf16[32,1152]{1,0:T(8,128)(2,1)S(1)}, u32[]{:S(2)}, u32[]{:S(2)}) collective-permute-start(bf16[32,1152]{1,0:T(8,128)(2,1)S(1)} %slice_bitcast_fusion.64), channel_id=1, source_target_pairs={{2,0},{3,1},{4,2},{5,3},{6,4},{7,5},{0,6},{1,7},{10,8},{11,9},{12,... | collective-permute-start | bytes 221192 | tf_op jit(solution)/shard_map/ppermute | solution.py:99
  6.0 20.2 %collective-permute-start.7 = (bf16[32,1152]{1,0:T(8,128)(2,1)S(1)}, bf16[32,1152]{1,0:T(8,128)(2,1)S(1)}, u32[]{:S(2)}, u32[]{:S(2)}) collective-permute-start(bf16[32,1152]{1,0:T(8,128)(2,1)S(1)} %slice_bitcast_fusion.64), channel_id=1, source_target_pairs={{4,0},{5,1},{6,2},{7,3},{0,4},{1,5},{2,6},{3,7},{12,8},{13,9},{14,... | collective-permute-start | bytes 221192 | tf_op jit(solution)/shard_map/ppermute | solution.py:99
  6.0 20.2 %collective-permute-start.8 = (bf16[32,1152]{1,0:T(8,128)(2,1)S(1)}, bf16[32,1152]{1,0:T(8,128)(2,1)S(1)}, u32[]{:S(2)}, u32[]{:S(2)}) collective-permute-start(bf16[32,1152]{1,0:T(8,128)(2,1)S(1)} %slice_bitcast_fusion.64), channel_id=1, source_target_pairs={{6,0},{7,1},{0,2},{1,3},{2,4},{3,5},{4,6},{5,7},{14,8},{15,9},{8,1... | collective-permute-start | bytes 221192 | tf_op jit(solution)/shard_map/ppermute | solution.py:99
  7.9 10.2 %collective-permute-start = (bf16[32,1152]{1,0:T(8,128)(2,1)S(1)}, bf16[32,1152]{1,0:T(8,128)(2,1)S(1)}, u32[]{:S(2)}, u32[]{:S(2)}) collective-permute-start(bf16[32,1152]{1,0:T(8,128)(2,1)S(1)} %get-tuple-element.33), channel_id=1, source_target_pairs={{2,0},{3,1},{4,2},{5,3},{6,4},{7,5},{0,6},{1,7},{10,8},{11,9},{12,... | collective-permute-start | bytes 221192 | tf_op jit(solution)/shard_map/ppermute | solution.py:99
  11.5 4.5 %collective-permute-start.4 = (f32[3,1152]{1,0:T(4,128)S(1)}, f32[3,1152]{1,0:T(4,128)S(1)}, u32[]{:S(2)}, u32[]{:S(2)}) collective-permute-start(f32[3,1152]{1,0:T(4,128)S(1)} %bitcast.532), channel_id=1, source_target_pairs={{0,8},{8,0},{1,9},{9,1},{2,10},{10,2},{3,11},{11,3},{4,12},{12,4},... | collective-permute-start | bytes 41480 | tf_op jit(solution)/shard_map/ppermute | solution.py:133
  14.4 11.8 %copy-start.14 = (bf16[1,2,32,1152]{3,2,1,0:T(8,128)(2,1)S(1)}, bf16[1,2,32,1152]{3,2,1,0:T(8,128)(2,1)}, u32[]{:S(2)}) copy-start(bf16[1,2,32,1152]{3,2,1,0:T(8,128)(2,1)} %param.14) | copy-start | bytes 442372
  16.0 6.3 %collective-permute-start.1 = (bf16[32,1152]{1,0:T(8,128)(2,1)S(1)}, bf16[32,1152]{1,0:T(8,128)(2,1)S(1)}, u32[]{:S(2)}, u32[]{:S(2)}) collective-permute-start(bf16[32,1152]{1,0:T(8,128)(2,1)S(1)} %get-tuple-element.33), channel_id=1, source_target_pairs={{4,0},{5,1},{6,2},{7,3},{0,4},{1,5},{2,6},{3,7},{12,8},{13,9},{14,... | collective-permute-start | bytes 221192 | tf_op jit(solution)/shard_map/ppermute | solution.py:99
  18.2 6.2 %collective-permute-start.2 = (bf16[32,1152]{1,0:T(8,128)(2,1)S(1)}, bf16[32,1152]{1,0:T(8,128)(2,1)S(1)}, u32[]{:S(2)}, u32[]{:S(2)}) collective-permute-start(bf16[32,1152]{1,0:T(8,128)(2,1)S(1)} %get-tuple-element.33), channel_id=1, source_target_pairs={{6,0},{7,1},{0,2},{1,3},{2,4},{3,5},{4,6},{5,7},{14,8},{15,9},{8,1... | collective-permute-start | bytes 221192 | tf_op jit(solution)/shard_map/ppermute | solution.py:99
  22.4 13.6 %collective-permute-start.5 = (bf16[1152,1728]{0,1:T(8,128)(2,1)}, bf16[1152,1728]{0,1:T(8,128)(2,1)}, u32[]{:S(2)}, u32[]{:S(2)}) collective-permute-start(bf16[1152,1728]{0,1:T(8,128)(2,1)} %bitcast.479), channel_id=1, source_target_pairs={{0,8},{8,0},{1,9},{9,1},{2,10},{10,2},{3,11},{11,3},{4,12},{12,4},... | collective-permute-start | bytes 11943944 | tf_op jit(solution)/shard_map/ppermute | solution.py:131
  24.4 37.7 %collective-permute-start.11 = (bf16[576,1152]{1,0:T(8,128)(2,1)}, bf16[576,1152]{1,0:T(8,128)(2,1)}, u32[]{:S(2)}, u32[]{:S(2)}) collective-permute-start(bf16[576,1152]{1,0:T(8,128)(2,1)} %bitcast.65), channel_id=1, source_target_pairs={{0,8},{8,0},{1,9},{9,1},{2,10},{10,2},{3,11},{11,3},{4,12},{12,4},... | collective-permute-start | bytes 3981320 | tf_op jit(solution)/shard_map/ppermute | solution.py:132
  24.6 9.9 %collective-permute-start.3 = (bf16[4,32,1152]{2,1,0:T(8,128)(2,1)S(1)}, bf16[4,32,1152]{2,1,0:T(8,128)(2,1)S(1)}, u32[]{:S(2)}, u32[]{:S(2)}) collective-permute-start(bf16[4,32,1152]{2,1,0:T(8,128)(2,1)S(1)} %constant_dynamic-slice_fusion.1), channel_id=1, source_target_pairs={{1,0},{0,1},{3,2},{2,3},{5,4},{4,5},{7,6},{6,7},{9,8},{8,9},{11,10... | collective-permute-start | bytes 884744 | tf_op jit(solution)/shard_map/ppermute | solution.py:99
  26.3 18.2 %collective-permute-start.9 = (bf16[4,32,1152]{2,1,0:T(8,128)(2,1)S(1)}, bf16[4,32,1152]{2,1,0:T(8,128)(2,1)S(1)}, u32[]{:S(2)}, u32[]{:S(2)}) collective-permute-start(bf16[4,32,1152]{2,1,0:T(8,128)(2,1)S(1)} %constant_dynamic-slice_fusion), channel_id=1, source_target_pairs={{1,0},{0,1},{3,2},{2,3},{5,4},{4,5},{7,6},{6,7},{9,8},{8,9},{11,10... | collective-permute-start | bytes 884744 | tf_op jit(solution)/shard_map/ppermute | solution.py:99
  43.0 2.9 %collective-permute-start.10 = (bf16[256,1152]{1,0:T(8,128)(2,1)S(1)}, bf16[256,1152]{1,0:T(8,128)(2,1)S(1)}, u32[]{:S(2)}, u32[]{:S(2)}) collective-permute-start(bf16[256,1152]{1,0:T(8,128)(2,1)S(1)} %fusion.4), channel_id=1, source_target_pairs={{0,8},{1,9},{2,10},{3,11},{4,12},{5,13},{6,14},{7,15},{16,24},{17,... | collective-permute-start | bytes 1769480 | tf_op jit(solution)/shard_map/ppermute | solution.py:152
  54.6 3.6 %copy-start.11 = (f32[256,512]{1,0:T(8,128)S(1)}, f32[256,512]{1,0:T(8,128)}, u32[]{:S(2)}) copy-start(f32[256,512]{1,0:T(8,128)} %get-tuple-element.42) | copy-start | bytes 1572868
  55.7 2.8 %copy-start.13 = (bf16[512,576]{0,1:T(8,128)(2,1)S(1)}, bf16[512,576]{0,1:T(8,128)(2,1)}, u32[]{:S(2)}) copy-start(bf16[512,576]{0,1:T(8,128)(2,1)} %copy.44) | copy-start | bytes 1769476
  55.7 3.1 %copy-start.10 = (f32[256,512]{1,0:T(8,128)S(1)}, f32[256,512]{1,0:T(8,128)}, u32[]{:S(2)}) copy-start(f32[256,512]{1,0:T(8,128)} %get-tuple-element.44) | copy-start | bytes 1572868
  62.1 2.7 %copy-start.2 = (bf16[1152,1728]{0,1:T(8,128)(2,1)S(1)}, bf16[1152,1728]{0,1:T(8,128)(2,1)}, u32[]{:S(2)}) copy-start(bf16[1152,1728]{0,1:T(8,128)(2,1)} %get-tuple-element.18) | copy-start | bytes 11943940
  62.1 2.7 %copy-start.5 = (bf16[4,2,32,1152]{3,2,1,0:T(8,128)(2,1)S(1)}, bf16[4,2,32,1152]{3,2,1,0:T(8,128)(2,1)}, u32[]{:S(2)}) copy-start(bf16[4,2,32,1152]{3,2,1,0:T(8,128)(2,1)} %copy-done.4) | copy-start | bytes 1769476
  65.9 2.6 %collective-permute-start.12 = (bf16[256,1152]{1,0:T(8,128)(2,1)S(1)}, bf16[256,1152]{1,0:T(8,128)(2,1)}, u32[]{:S(2)}, u32[]{:S(2)}) collective-permute-start(bf16[256,1152]{1,0:T(8,128)(2,1)S(1)} %get-tuple-element.57), channel_id=1, source_target_pairs={{0,8},{8,0},{1,9},{9,1},{2,10},{10,2},{3,11},{11,3},{4,12},{12,4},... | collective-permute-start | bytes 1769480 | tf_op jit(solution)/shard_map/ppermute | solution.py:156
  75.9 2.9 %copy-start.3 = (bf16[576,512]{1,0:T(8,128)(2,1)S(1)}, bf16[576,512]{1,0:T(8,128)(2,1)}, u32[]{:S(2)}) copy-start(bf16[576,512]{1,0:T(8,128)(2,1)} %convolution_convert_fusion) | copy-start | bytes 1769476
  78.7 1.2 %collective-permute-start.13 = (bf16[34,16]{0,1:T(8,128)(2,1)S(1)}, bf16[34,16]{0,1:T(8,128)(2,1)S(1)}, u32[]{:S(2)}, u32[]{:S(2)}) collective-permute-start(bf16[34,16]{0,1:T(8,128)(2,1)S(1)} %fusion.88), channel_id=1, source_target_pairs={{0,8},{8,0},{1,9},{9,1},{2,10},{10,2},{3,11},{11,3},{4,12},{12,4},... | collective-permute-start | bytes 3272 | tf_op jit(solution)/shard_map/ppermute | solution.py:178
  (12 other events, 19.4 us)

commit v3 on v1

v3 whole, which is shorter than its diff:
```python
import functools
import math

import jax
import jax.numpy as jnp
import numpy as np
from jax import lax
from jax.experimental import pallas as pl
from jax.experimental.pallas import tpu as pltpu
from jax.sharding import PartitionSpec as P

D = 1152
DH = 72
HEADS = 8
CH = 512
LATC = 4
TC = 256
DA = 576
DP = 640
EPSILON = 1e-06
QUERY_SCALE = math.log2(math.e) / math.sqrt(DH)
BLOCK = 256
SMALL_BLOCK = 64
LANES = 128
VMEM_LIMIT = 56 * 1024 * 1024

F32 = jnp.float32
BF16 = jnp.bfloat16
VMEM = pl.BlockSpec(memory_space=pltpu.VMEM)
ANY = pl.BlockSpec(memory_space=pl.ANY)


def dot(a, b):
    return jnp.dot(a, b, preferred_element_type=F32)


def dot_t(a, b):
    return lax.dot_general(a, b, (((1,), (1,)), ((), ())), preferred_element_type=F32)


def normed(values, scale, shift):
    average = jnp.mean(values, axis=-1, keepdims=True)
    centred = values - average
    variance = jnp.mean(centred * centred, axis=-1, keepdims=True)
    return (centred * lax.rsqrt(variance + EPSILON) * scale + shift).astype(BF16)


def scaled_query(projected):
    return (projected * QUERY_SCALE).astype(BF16)


def window(head):
    first = head * DH // LANES * LANES
    last = -(-(head + 1) * DH // LANES) * LANES
    return first, last


def attend(query, k_ref, v_ref):
    count = query.shape[0]
    pieces = [None] * (DP // LANES)
    for head in range(HEADS):
        first, last = window(head)
        lane = lax.broadcasted_iota(jnp.int32, (count, last - first), 1) + first
        own = (lane >= head * DH) & (lane < (head + 1) * DH)
        q = jnp.where(own, query[:, first:last], jnp.zeros((), BF16))
        scores = dot_t(q, k_ref[:, first:last])
        exponent = jnp.exp2(scores - jnp.max(scores, axis=1, keepdims=True))
        total = jnp.sum(exponent, axis=1, keepdims=True)
        numerator = dot(exponent.astype(BF16), v_ref[:, first:last])
        out = jnp.where(own, numerator * (1.0 / total), 0.0)
        for i in range((last - first) // LANES):
            at = first // LANES + i
            part = out[:, i * LANES : (i + 1) * LANES]
            pieces[at] = part if pieces[at] is None else pieces[at] + part
    return jnp.concatenate(pieces, axis=1)


def each_block(count, body):
    if count <= BLOCK:
        body(0, count)
    else:

        @pl.loop(0, count // SMALL_BLOCK)
        def _(i):
            body(pl.multiple_of(i * SMALL_BLOCK, SMALL_BLOCK), SMALL_BLOCK)


def copy_of(block, own, other, target, sem):
    section = lax.axis_index("pipe")

    @pl.when(section == block)
    def _():
        pltpu.make_async_copy(own, target, sem).start()

    @pl.when(section != block)
    def _():
        pltpu.make_async_copy(other, target, sem).start()

    return pltpu.make_async_copy(own, target, sem)


QKV_CUTS = (0, 512, 1024, 1536, 3 * DA)


def project_kernel(n_pieces, *refs):
    piece_refs = refs[:n_pieces]
    vec_ref, own_ref, other_ref, x_ref, q_ref, kv_ref, w_ref, all_ref, sems = refs[n_pieces:]
    cuts = list(zip(QKV_CUTS[:-1], QKV_CUTS[1:]))
    copies = [
        copy_of(0, own_ref.at[0, :, a:b], other_ref.at[0, :, a:b], w_ref.at[:, a:b], sems.at[i])
        for i, (a, b) in enumerate(cuts)
    ]
    at = 0
    for ref in piece_refs:
        rows = ref.shape[0]
        x_ref[at : at + rows] = ref[...]
        at += rows
    waited = [False] * len(cuts)

    def body(start, size):
        values = x_ref[pl.ds(start, size)].astype(F32)
        modulated = normed(values, vec_ref[1:2], vec_ref[0:1])
        for i, (a, b) in enumerate(cuts):
            if not waited[i]:
                copies[i].wait()
            projected = dot(modulated, w_ref[:, a:b])
            if a < DA:
                lane = lax.broadcasted_iota(jnp.int32, projected.shape, 1) + a
                projected = projected * jnp.where(lane < DA, QUERY_SCALE, 1.0)
            all_ref[:, a:b] = projected.astype(BF16)
        rows = pl.ds(start, size)
        q_ref[rows, :DA] = all_ref[:, :DA]
        q_ref[rows, DA:] = jnp.zeros((size, DP - DA), BF16)
        kv_ref[0, rows] = all_ref[:, DA : 2 * DA]
        kv_ref[1, rows] = all_ref[:, 2 * DA :]

    if x_ref.shape[0] > BLOCK:
        for i, copy in enumerate(copies):
            copy.wait()
            waited[i] = True
    each_block(x_ref.shape[0], body)


def project(pieces, vecs, w_own, w_other):
    count = sum(piece.shape[0] for piece in pieces)
    return pl.pallas_call(
        functools.partial(project_kernel, len(pieces)),
        out_shape=(
            jax.ShapeDtypeStruct((count, D), BF16),
            jax.ShapeDtypeStruct((count, DP), BF16),
            jax.ShapeDtypeStruct((2, count, DA), BF16),
        ),
        in_specs=[VMEM] * (len(pieces) + 1) + [ANY] * 2,
        out_specs=(VMEM,) * 3,
        scratch_shapes=[
            pltpu.VMEM((D, 3 * DA), BF16),
            pltpu.VMEM((count if count <= BLOCK else SMALL_BLOCK, 3 * DA), BF16),
            pltpu.SemaphoreType.DMA((len(QKV_CUTS) - 1,)),
        ],
        compiler_params=pltpu.CompilerParams(vmem_limit_bytes=VMEM_LIMIT),
        name="layer_norm_and_projections",
    )(*pieces, vecs, w_own, w_other)


def fill(k_ref, v_ref, at, key, value):
    rows = pl.ds(at, key.shape[0])
    pad = jnp.zeros((key.shape[0], DP - DA), BF16)
    k_ref[rows, :DA] = key
    k_ref[rows, DA:] = pad
    v_ref[rows, :DA] = value
    v_ref[rows, DA:] = pad


def block_kernel(n_pieces, *refs):
    stale_refs = refs[:n_pieces]
    (
        x_ref, q_ref, kv_ref, got_ref, idx_ref, vec_ref, w_own, w_other, wo_own, wo_other,
        xt_ref, qt_ref, kv1_ref, w_ref, wo_ref, k_ref, v_ref, pick_ref, sems,
    ) = refs[n_pieces:]
    count = x_ref.shape[0]
    out_copy = copy_of(0, wo_own.at[0], wo_other.at[0], wo_ref, sems.at[0])
    in_copy = copy_of(1, w_own.at[0], w_other.at[0], w_ref, sems.at[1])
    first_core = lax.axis_index("pipe") == 0
    fill(k_ref, v_ref, 0, kv_ref[0], kv_ref[1])
    at = 0
    for ref in stale_refs:
        rows = ref.shape[0]
        stale = ref[...]
        key = jnp.where(first_core, stale[:, :DA], got_ref[0, at : at + rows])
        value = jnp.where(first_core, stale[:, DA:], got_ref[1, at : at + rows])
        fill(k_ref, v_ref, count + at, key, value)
        at += rows
    pick_ref[...] = jnp.zeros_like(pick_ref)
    tile_rows = idx_ref.shape[0]
    if count > BLOCK:
        out_copy.wait()
        in_copy.wait()

    def body(start, size):
        rows = pl.ds(start, size)
        attended = attend(q_ref[rows], k_ref, v_ref).astype(BF16)
        if count <= BLOCK:
            out_copy.wait()
        branch = dot(attended[:, :DA], wo_ref[...])
        x1 = (x_ref[rows].astype(F32) + vec_ref[2:3] * branch).astype(BF16)
        modulated = normed(x1.astype(F32), vec_ref[4:5], vec_ref[3:4])
        if count <= BLOCK:
            in_copy.wait()
        fresh = dot(modulated, w_ref[:, 512:])
        kv1_ref[0, rows] = fresh[:, DA - 512 : 2 * DA - 512].astype(BF16)
        kv1_ref[1, rows] = fresh[:, 2 * DA - 512 :].astype(BF16)
        lane = lax.broadcasted_iota(jnp.int32, (tile_rows, size), 1) + start
        chosen = (lane == idx_ref[:, :1]).astype(F32).astype(BF16)
        pick_ref[0] += dot(chosen, x1)
        pick_ref[1] += dot(chosen, modulated)

    each_block(count, body)
    xt_ref[...] = pick_ref[0].astype(BF16)
    projected = dot(pick_ref[1].astype(BF16), w_ref[:, :DP])
    query = scaled_query(projected)
    lane = lax.broadcasted_iota(jnp.int32, query.shape, 1)
    qt_ref[...] = jnp.where(lane < DA, query, jnp.zeros((), BF16))


def first_block(stale_pieces, x, q, kv, got, idx, vecs, w_own, w_other, wo_own, wo_other):
    count = x.shape[0]
    tile_rows = idx.shape[0]
    return pl.pallas_call(
        functools.partial(block_kernel, len(stale_pieces)),
        out_shape=(
            jax.ShapeDtypeStruct((tile_rows, D), BF16),
            jax.ShapeDtypeStruct((tile_rows, DP), BF16),
            jax.ShapeDtypeStruct((2, count, DA), BF16),
        ),
        in_specs=[VMEM] * (len(stale_pieces) + 6) + [ANY] * 4,
        out_specs=(VMEM,) * 3,
        scratch_shapes=[
            pltpu.VMEM((D, 3 * DA), BF16),
            pltpu.VMEM((DA, D), BF16),
            pltpu.VMEM((2 * count, DP), BF16),
            pltpu.VMEM((2 * count, DP), BF16),
            pltpu.VMEM((2, tile_rows, D), F32),
            pltpu.SemaphoreType.DMA((2,)),
        ],
        compiler_params=pltpu.CompilerParams(vmem_limit_bytes=VMEM_LIMIT),
        name="attention_and_next_keys",
    )(*stale_pieces, x, q, kv, got, idx, vecs, w_own, w_other, wo_own, wo_other)


def tile_kernel(
    x_ref, q_ref, kv_ref, got_ref, idx_ref, vec_ref, wf_ref, wo_own, wo_other, patch_ref, wo_ref, k_ref, v_ref, sems
):
    count = kv_ref.shape[1]
    out_copy = copy_of(1, wo_own.at[0], wo_other.at[0], wo_ref, sems.at[0])
    fill(k_ref, v_ref, 0, kv_ref[0], kv_ref[1])
    fill(k_ref, v_ref, count, got_ref[0], got_ref[1])
    attended = attend(q_ref[...], k_ref, v_ref).astype(BF16)
    out_copy.wait()
    branch = dot(attended[:, :DA], wo_ref[...])
    x2 = (x_ref[...].astype(F32) + vec_ref[5:6] * branch).astype(BF16)
    final = normed(x2.astype(F32), vec_ref[7:8], vec_ref[6:7])
    patches = dot(final, wf_ref[...]).astype(BF16).astype(F32)
    patch_ref[...] = jnp.where(idx_ref[:, :1] >= 0, patches, 0.0)


def tile_block(x, q, kv, got, idx, vecs, w_final, wo_own, wo_other):
    count = kv.shape[1]
    return pl.pallas_call(
        tile_kernel,
        out_shape=jax.ShapeDtypeStruct((x.shape[0], LANES), F32),
        in_specs=[VMEM] * 7 + [ANY] * 2,
        out_specs=VMEM,
        scratch_shapes=[
            pltpu.VMEM((DA, D), BF16),
            pltpu.VMEM((2 * count, DP), BF16),
            pltpu.VMEM((2 * count, DP), BF16),
            pltpu.SemaphoreType.DMA((1,)),
        ],
        compiler_params=pltpu.CompilerParams(vmem_limit_bytes=VMEM_LIMIT),
        name="tile_attention_and_patches",
    )(x, q, kv, got, idx, vecs, w_final, wo_own, wo_other)


def decode_kernel(
    rows, cols, pitch, patch_ref, got_ref, idx_ref, wp_ref, bin_ref, bup_ref, w_any, out_ref, w_ref, u_ref, ub_ref, sems
):
    copies = [pltpu.make_async_copy(w_any.at[t], w_ref.at[t], sems.at[t]) for t in range(9)]
    order = [3, 4, 5, 0, 1, 2, 6, 7, 8]
    for t in order:
        copies[t].start()
    first_core = lax.axis_index("pipe") == 0
    got = got_ref[...]
    above = jnp.where(first_core, 0.0, got)
    below = jnp.where(first_core, got, 0.0)
    rim = [above] + [patch_ref[r * pitch : (r + 1) * pitch] for r in range(rows)] + [below]
    column_in = idx_ref[:pitch, :1] >= 0
    shifted = [[pltpu.roll(p, (-ds) % pitch, 0) if ds else p for ds in (-1, 0, 1)] for p in rim]
    for r in range(rows + 2):
        low, high = None, None
        for dr in (-1, 0, 1):
            if not 0 <= r + dr < rows + 2:
                continue
            for ds in range(3):
                tap = (dr + 1) * 3 + ds
                piece = shifted[r + dr][ds]
                if tap == 8:
                    high = piece
                else:
                    piece = pltpu.roll(piece, 4 * LATC * tap, 1) if tap else piece
                    low = piece if low is None else low + piece
        high = jnp.zeros_like(low) if high is None else high
        around = jnp.concatenate([low, high], axis=1).astype(BF16)
        for p in range(2):
            y = 2 * (r - 1) + p + 1
            if not 0 <= y < 2 * rows + 2:
                continue
            for q in range(2):
                at = (2 * p + q) * CH
                act = dot(around, wp_ref[:, at : at + CH]) + bin_ref[...]
                feature = act / (1.0 + jnp.exp(-act))
                keep = column_in
                if y == 0:
                    keep = keep & jnp.logical_not(first_core)
                if y == 2 * rows + 1:
                    keep = keep & first_core
                feature = jnp.where(keep, feature, 0.0)
                for c in range(CH // LANES):
                    part = feature[:, c * LANES : (c + 1) * LANES]
                    u_ref[y, c, pl.ds(2 * q, pitch, stride=4), :] = part
                    u_ref[y, c, pl.ds(2 * q + 1, pitch, stride=4), :] = part
    wide = 4 * cols
    for y in range(2 * rows + 2):
        for dx in range(3):
            for c in range(CH // LANES):
                ub_ref[dx, y * wide : (y + 1) * wide, c * LANES : (c + 1) * LANES] = u_ref[
                    y, c, 3 + dx : 3 + dx + wide, :
                ].astype(BF16)

    def tap_row(dy, y_first, y_count):
        total = None
        for dx in range(3):
            copies[3 * dy + dx].wait()
            part = dot(ub_ref[dx, y_first * wide : (y_first + y_count) * wide], w_ref[3 * dy + dx])
            total = part if total is None else total + part
        return total

    def rows_of(total, y):
        return total[y * wide : (y + 1) * wide]

    middle = tap_row(1, 1, 2 * rows) + bup_ref[...]
    before = tap_row(0, 0, 2 * rows + 1)
    after = tap_row(2, 1, 2 * rows + 1)
    for y in range(2 * rows):
        own = rows_of(middle, y)
        out_ref[2 * y] = (own + rows_of(before, y) + rows_of(after, y)).astype(BF16)
        out_ref[2 * y + 1] = (own + rows_of(before, y + 1) + rows_of(after, y + 1)).astype(BF16)


def decode(rows, cols, pitch, patches, got, idx, w_patch, b_in, b_up, w_up):
    return pl.pallas_call(
        functools.partial(decode_kernel, rows, cols, pitch),
        out_shape=jax.ShapeDtypeStruct((4 * rows, 4 * cols, CH), BF16),
        in_specs=[VMEM] * 6 + [ANY],
        out_specs=VMEM,
        scratch_shapes=[
            pltpu.VMEM((9, CH, CH), BF16),
            pltpu.VMEM((2 * rows + 2, CH // LANES, 4 * pitch, LANES), F32),
            pltpu.VMEM((3, (2 * rows + 2) * 4 * cols, CH), BF16),
            pltpu.SemaphoreType.DMA((9,)),
        ],
        compiler_params=pltpu.CompilerParams(vmem_limit_bytes=VMEM_LIMIT),
        name="decoder_convolutions",
    )(patches, got, idx, w_patch, b_in, b_up, w_up)


def patch_selector():
    sel = np.zeros((3, 3, 2, 2, LATC, 2, 2, 9 * LATC), np.float32)
    for dr, ds, pp, qq, p, q in np.ndindex(3, 3, 2, 2, 2, 2):
        dy = 2 * (dr - 1) + pp - p
        dx = 2 * (ds - 1) + qq - q
        if abs(dy) <= 1 and abs(dx) <= 1:
            tap = (dy + 1) * 3 + dx + 1
            for c in range(LATC):
                sel[dr, ds, pp, qq, c, p, q, tap * LATC + c] = 1.0
    return sel.reshape(-1, 9 * LATC)


def split_of(n):
    inner = 2 ** (int(math.log2(n)) // 2)
    return n // inner, inner


def gather_patch(own):
    n = lax.axis_size("patch")
    outer, inner = split_of(n)

    def shifted(block, k_outer, k_inner):
        route = []
        for i in range(n):
            o, e = divmod(i, inner)
            route.append(((o + k_outer) % outer * inner + (e + k_inner) % inner, i))
        return lax.ppermute(block, "patch", route)

    column = jnp.concatenate([own] + [shifted(own, k, 0) for k in range(1, outer)], axis=0)
    return [column] + [shifted(column, 0, k) for k in range(1, inner)]


def local(
    tokens,
    stale_kv,
    w_qkv,
    w_out,
    block_table,
    time_table,
    t_index,
    w_final,
    w_in,
    b_in,
    w_up,
    b_up,
):
    section = lax.axis_index("pipe")
    tile = lax.axis_index("patch")
    n_tiles = lax.axis_size("patch")
    swap = [(0, 1), (1, 0)]
    first_core = section == 0
    own_count = tokens.shape[1]
    count = own_count * n_tiles
    rows = count // TC
    cols = TC // n_tiles
    pitch = -(-(cols + 3) // 8) * 8
    outer, inner = split_of(n_tiles)

    own_tokens = lax.dynamic_index_in_dim(tokens, section, 0, keepdims=False)
    x_pieces = gather_patch(own_tokens)
    stale_pieces = gather_patch(stale_kv[0, 1])
    w_qkv_other = lax.ppermute(w_qkv, "pipe", swap)
    w_out_other = lax.ppermute(w_out, "pipe", swap)
    table_other = lax.ppermute(block_table[0], "pipe", swap)

    time_row = lax.dynamic_index_in_dim(time_table, t_index[0], 0, keepdims=False)
    table = block_table[0]
    table_0 = jnp.where(first_core, table, table_other)
    table_1 = jnp.where(first_core, table_other, table)
    ones = jnp.asarray([[0.0], [1.0], [0.0]], F32)
    vecs = jnp.concatenate(
        [
            time_row[:3] + table_0 + ones,
            time_row[:3] + table_1 + ones,
            time_row[3:5] + ones[:2],
        ],
        axis=0,
    )

    padded_rows = -(-rows * pitch // 16) * 16
    place = jnp.arange(padded_rows)
    column = place % pitch - 1 + tile * cols
    inside = (place % pitch < cols + 2) & (place < rows * pitch) & (column >= 0) & (column < TC)
    token = place // pitch * TC + jnp.clip(column, 0, TC - 1)
    source = token // own_count
    k_outer = (source // inner - tile // inner) % outer
    k_inner = (source % inner - tile % inner) % inner
    spot = (k_inner * outer + k_outer) * own_count + token % own_count
    idx = jnp.broadcast_to(jnp.where(inside, spot, -1)[:, None], (padded_rows, LANES)).astype(jnp.int32)

    w_patch = (
        dot(jnp.asarray(patch_selector(), BF16), w_in).astype(BF16).reshape(9 * 4 * LATC, 4 * CH)
    )
    w_patch = jnp.pad(w_patch, ((0, 2 * LANES - 9 * 4 * LATC), (0, 0)))
    w_final = jnp.pad(w_final, ((0, 0), (0, LANES - 4 * LATC)))

    x, query, fresh = project(x_pieces, vecs, w_qkv, w_qkv_other)
    got = lax.ppermute(fresh, "pipe", [(0, 1)])
    x_tile, q_tile, fresh = first_block(
        stale_pieces, x, query, fresh, got, idx, vecs, w_qkv, w_qkv_other, w_out, w_out_other
    )
    stale = jnp.concatenate(stale_pieces, axis=0)
    stale = jnp.stack([stale[:, :DA], stale[:, DA:]])
    got = lax.ppermute(jnp.where(first_core, fresh, stale), "pipe", swap)
    patches = tile_block(x_tile, q_tile, fresh, got, idx, vecs, w_final, w_out, w_out_other)
    patches = patches[: rows * pitch]
    edge = jnp.where(first_core, patches[(rows - 1) * pitch :], patches[:pitch])
    got = lax.ppermute(edge, "pipe", swap)
    return decode(rows, cols, pitch, patches, got, idx, w_patch, b_in[None], b_up[None], w_up)


def solution(mesh):
    placed = (
        P(None, ("grp", "patch"), None),
        P("pipe", None, ("grp", "patch"), None),
        P("pipe", None, None),
        P("pipe", None, None),
        P("pipe", None, None),
        P(),
        P("grp"),
        P(),
        P(),
        P(),
        P(),
        P(),
    )
    return jax.shard_map(
        local,
        mesh=mesh,
        in_specs=placed,
        out_specs=P(("grp", "pipe"), "patch", None),
        check_vma=False,
    )
```

time: 132 us -> 84.2 us (0.64)
  matrix products: 37.7 us -> 1.11 us
  waiting for transfers between devices: 39.8 us -> 6.3 us
  local copies, waits for them, and re-layouts: 10.6 us -> 33.9 us
  Pallas kernels: 0 us -> 23.2 us
  other arithmetic: 25 us -> 2.03 us
  between operations: 14.7 us -> 1 us
  starting transfers between devices: 2.48 us -> 15.8 us
    all_gather x1 -> x0, waiting for transfers between devices: 38.2 us -> none  [local(): lax.all_gather(jnp.stack([own_tokens, stale_kv[0, 1]]), 'patch', axis=1,...]
    dot_general x50 -> x1, matrix products: 37.7 us -> 1.11 us  [dot(): return jnp.dot(a, b, preferred_element_type=F32)]
    pallas_call x0 -> x4, Pallas kernels: none -> 23.2 us  [the longest x1 7.32 us: first_block(): pl.pallas_call(functools.partial(block_kernel, len(stale_pieces)), out_sh...]
    ppermute x3 -> x11, starting transfers between devices: 0.52 us -> 13.1 us  [the longest x8 12.6 us: shifted(): return lax.ppermute(block, 'patch', route)]
    reduce_sum x20 -> x0, other arithmetic: 12.2 us -> none  [the longest x16 9.08 us: one_head(): total = jnp.sum(exponent, axis=1, keepdims=True)]
    ppermute x0 -> x3, local copies, waits for them, and re-layouts: none -> 9.71 us  [the longest x1 6.48 us: local(): w_qkv_other = lax.ppermute(w_qkv, 'pipe', swap)]
    unnamed x66 -> x31, local copies, waits for them, and re-layouts: 3.06 us -> 11.4 us
    select_n x4 -> x2, other arithmetic: 6.94 us -> 1.28 us  [the longest x1 1.24 us: local(): got = lax.ppermute(jnp.where(first_core, fresh, stale), 'pipe', swap)]
  transfers between devices with their start and end apart: 7 -> 14, of which waited for: 4 -> 3; matrix products, arithmetic and copies ran while one was open for 27% -> 38% of each run, Pallas kernels for 0% -> 7%
where the time goes in v3:
time: 84.2 us; the launch traced here: 83.4 us
  local copies, waits for them, and re-layouts  33.9 us (40%)
  Pallas kernels  23.2 us (28%)
  starting transfers between devices  15.8 us (19%)
  waiting for transfers between devices  6.3 us (7%)
  other arithmetic  2.03 us (2%)
  matrix products  1.11 us (1%)
  between operations  1 us (1%)
    ppermute x8, starting transfers between devices, shifted(): return lax.ppermute(block, 'patch', route)  12.6 us
    unnamed x31, local copies, waits for them, and re-layouts  11.4 us
    pallas_call x1, Pallas kernels, first_block(): pl.pallas_call(functools.partial(block_kernel, len(stale_pieces)), out_sh...  7.32 us
    ppermute x1, local copies, waits for them, and re-layouts, local(): w_qkv_other = lax.ppermute(w_qkv, 'pipe', swap)  6.48 us
    pallas_call x1, Pallas kernels, decode(): pl.pallas_call(functools.partial(decode_kernel, rows, cols, pitch), out_s...  5.77 us
    pallas_call x1, Pallas kernels, project(): pl.pallas_call(functools.partial(project_kernel, len(pieces)), out_shape=...  5.54 us
    ppermute x8, waiting for transfers between devices, shifted(): return lax.ppermute(block, 'patch', route)  5.08 us
    pallas_call x1, Pallas kernels, tile_block(): pl.pallas_call(tile_kernel, out_shape=jax.ShapeDtypeStruct((x.shape[0], L...  4.61 us
  transfers between devices with their start and end apart: 14, of which 3 were waited for; matrix products, arithmetic and copies ran while one was open for 38% of the time, Pallas kernels for 7%

profile of v3, /device:TPU:0, one launch (start us, length us, event | category | flops | bytes accessed | tf_op | source)
XLA Modules:
  0.0 83.4 jit_solution(4316168645848215820)
XLA Ops:
  0.5 1.1 %dynamic-slice_bitcast_fusion = bf16[32,1152]{1,0:T(8,128)(2,1)S(1)} fusion(bf16[2,32,1152]{2,1,0:T(8,128)(2,1)} %param.14, s32[]{:T(128)S(6)} %select_n.120), kind=kLoop, calls=%fused_computation.6 | loop fusion | bytes 147460 | tf_op jit(solution)/shard_map/jit(dynamic_index_in_dim)/squeeze | solution.py:434
  1.6 4.6 %collective-permute-start.4 = (bf16[32,1152]{1,0:T(8,128)(2,1)S(1)}, bf16[32,1152]{1,0:T(8,128)(2,1)S(1)}, u32[]{:S(2)}, u32[]{:S(2)}) collective-permute-start(bf16[32,1152]{1,0:T(8,128)(2,1)S(1)} %dynamic-slice_bitcast_fusion), channel_id=1, source_target_pairs={{2,0},{3,1},{4,2},{5,3},{6,4},{7,5},{0,6},{1,7},{10,8},{11,9},{12,... | collective-permute-start | bytes 221192 | tf_op jit(solution)/shard_map/ppermute | solution.py:402
  9.5 1.5 %constant_dynamic-update-slice_fusion.4 = bf16[256,1152]{1,0:T(8,128)(2,1)} fusion(bf16[1,2,32,1152]{3,2,1,0:T(8,128)(2,1)} %param.15), kind=kLoop, calls=%fused_computation.19 | loop fusion | bytes 147456
  11.1 6.4 %copy.21.refs_3_.refs_8_ = bf16[1,1152,1728]{2,1,0:T(8,128)(2,1)} copy(bf16[1,1152,1728]{1,2,0:T(8,128)(2,1)} %param.16) | data formatting | bytes 7962624 | tf_op args[2]
  17.5 2.8 %collective-permute-start = (bf16[32,1152]{1,0:T(8,128)(2,1)S(1)}, bf16[32,1152]{1,0:T(8,128)(2,1)S(1)}, u32[]{:S(2)}, u32[]{:S(2)}) collective-permute-start(bf16[32,1152]{1,0:T(8,128)(2,1)S(1)} %slice_bitcast_fusion.2), channel_id=1, source_target_pairs={{2,0},{3,1},{4,2},{5,3},{6,4},{7,5},{0,6},{1,7},{10,8},{11,9},{12,... | collective-permute-start | bytes 221192 | tf_op jit(solution)/shard_map/ppermute | solution.py:402
  21.1 1.1 %collective-permute-start.1 = (bf16[32,1152]{1,0:T(8,128)(2,1)S(1)}, bf16[32,1152]{1,0:T(8,128)(2,1)S(1)}, u32[]{:S(2)}, u32[]{:S(2)}) collective-permute-start(bf16[32,1152]{1,0:T(8,128)(2,1)S(1)} %slice_bitcast_fusion.2), channel_id=1, source_target_pairs={{4,0},{5,1},{6,2},{7,3},{0,4},{1,5},{2,6},{3,7},{12,8},{13,9},{14,... | collective-permute-start | bytes 221192 | tf_op jit(solution)/shard_map/ppermute | solution.py:402
  22.9 1.5 %collective-permute-start.7 = (bf16[128,1152]{1,0:T(8,128)(2,1)S(1)}, bf16[128,1152]{1,0:T(8,128)(2,1)}, u32[]{:S(2)}, u32[]{:S(2)}) collective-permute-start(bf16[128,1152]{1,0:T(8,128)(2,1)S(1)} %pad_maximum_fusion.1.refs_0_), channel_id=1, source_target_pairs={{1,0},{0,1},{3,2},{2,3},{5,4},{4,5},{7,6},{6,7},{9,8},{8,9},{11,10... | collective-permute-start | bytes 884744 | tf_op jit(solution)/shard_map/ppermute | solution.py:402
  24.5 4.4 %collective-permute-done.1 = bf16[32,1152]{1,0:T(8,128)(2,1)S(1)} collective-permute-done((bf16[32,1152]{1,0:T(8,128)(2,1)S(1)}, bf16[32,1152]{1,0:T(8,128)(2,1)S(1)}, u32[]{:S(2)}, u32[]{:S(2)}) %collective-permute-start.1) | collective-permute-done | bytes 73760 | tf_op jit(solution)/shard_map/ppermute | solution.py:402
  28.9 1.6 %collective-permute-start.3 = (bf16[128,1152]{1,0:T(8,128)(2,1)S(1)}, bf16[128,1152]{1,0:T(8,128)(2,1)S(1)}, u32[]{:S(2)}, u32[]{:S(2)}) collective-permute-start(bf16[128,1152]{1,0:T(8,128)(2,1)S(1)} %pad_maximum_fusion.refs_0_), channel_id=1, source_target_pairs={{1,0},{0,1},{3,2},{2,3},{5,4},{4,5},{7,6},{6,7},{9,8},{8,9},{11,10... | collective-permute-start | bytes 884744 | tf_op jit(solution)/shard_map/ppermute | solution.py:402
  31.8 6.5 %copy.22.refs_4_.refs_9_ = bf16[1,1152,1728]{2,1,0:T(8,128)(2,1)} copy(bf16[1,1152,1728]{1,2,0:T(8,128)(2,1)} %collective-permute-done.9) | data formatting | bytes 7962624 | tf_op jit(solution)/shard_map/ppermute | solution.py:437
  38.3 5.5 %layer_norm_and_projections.1 = (bf16[256,1152]{1,0:T(8,128)(2,1)}, bf16[256,640]{1,0:T(8,128)(2,1)}, bf16[2,256,576]{2,1,0:T(8,128)(2,1)}) custom-call(bf16[128,1152]{1,0:T(8,128)(2,1)} %copy-done.4, bf16[128,1152]{1,0:T(8,128)(2,1)} %collective-permute-done.7.refs_1_, f32[8,1152]{1,0:T(8,128)} %pad_maximum_fusion.2.refs_2_.refs_7_.vec_ref, ...), custom_call_target="tpu_custom_call" | custom-call | tf_op jit(solution)/shard_map/layer_norm_and_projections/pallas_call | solution.py:146
  43.9 2.1 %copy.23 = bf16[2,256,576]{1,2,0:T(8,128)(2,1)} copy(bf16[2,256,576]{2,1,0:T(8,128)(2,1)} %get-tuple-element.13.refs_4_) | data formatting | bytes 1179648 | tf_op jit(solution)/shard_map/layer_norm_and_projections/pallas_call | solution.py:146
  46.0 2.5 %collective-permute-start.10 = (bf16[2,256,576]{1,2,0:T(8,128)(2,1)}, bf16[2,256,576]{1,2,0:T(8,128)(2,1)}, u32[]{:S(2)}, u32[]{:S(2)}) collective-permute-start(bf16[2,256,576]{1,2,0:T(8,128)(2,1)} %copy.23), channel_id=1, source_target_pairs={{0,8},{1,9},{2,10},{3,11},{4,12},{5,13},{6,14},{7,15},{16,24},{17,... | collective-permute-start | bytes 1769480 | tf_op jit(solution)/shard_map/ppermute | solution.py:473
  49.9 2.0 %slice_bitcast_fusion.1 = (bf16[1,256,576]{2,1,0:T(8,128)(2,1)S(1)}, bf16[1,256,576]{2,1,0:T(8,128)(2,1)}) fusion(bf16[256,1152]{1,0:T(8,128)(2,1)} %constant_dynamic-update-slice_fusion), kind=kLoop, calls=%fused_computation.3 | loop fusion | bytes 1179648 | tf_op jit(solution)/shard_map/stack | solution.py:478
  51.8 2.1 %copy.24.refs_5_ = bf16[2,256,576]{2,1,0:T(8,128)(2,1)} copy(bf16[2,256,576]{1,2,0:T(8,128)(2,1)} %collective-permute-done.10) | data formatting | bytes 1179648 | tf_op jit(solution)/shard_map/ppermute | solution.py:473
  54.7 7.3 %attention_and_next_keys.1 = (bf16[48,1152]{1,0:T(8,128)(2,1)}, bf16[48,640]{1,0:T(8,128)(2,1)}, bf16[2,256,576]{2,1,0:T(8,128)(2,1)}) custom-call(bf16[128,1152]{1,0:T(8,128)(2,1)} %copy-done.2, bf16[128,1152]{1,0:T(8,128)(2,1)} %copy-done.3, bf16[256,1152]{1,0:T(8,128)(2,1)} %get-tuple-element.11.refs_2_, bf16[256,640]{1,0:T(8,128)(2,1)} %get-tuple-element.12.refs_3_, ...), custom_call_target="tpu_custom_call" | custom-call | tf_op jit(solution)/shard_map/attention_and_next_keys/pallas_call | solution.py:228
  62.0 1.2 %maximum_select_fusion = bf16[2,256,576]{2,1,0:T(8,128)(2,1)S(1)} fusion(bf16[2,256,576]{2,1,0:T(8,128)(2,1)} %get-tuple-element.16.kv_ref, bf16[1,256,576]{2,1,0:T(8,128)(2,1)S(1)} %copy-done.1, bf16[1,256,576]{2,1,0:T(8,128)(2,1)S(1)} %get-tuple-element.17, pred[]{:T(512)S(6)} %eq.12), kind=kLoop, calls=%fused_computation.1 | loop fusion | flops 589824 | bytes 1769473 | tf_op jit(solution)/shard_map/jit(_where)/select_n | solution.py:479
  65.3 1.2 %collective-permute-done.12 = bf16[2,256,576]{1,2,0:T(8,128)(2,1)S(1)} collective-permute-done((bf16[2,256,576]{1,2,0:T(8,128)(2,1)}, bf16[2,256,576]{1,2,0:T(8,128)(2,1)S(1)}, u32[]{:S(2)}, u32[]{:S(2)}) %collective-permute-start.12) | collective-permute-done | bytes 589856 | tf_op jit(solution)/shard_map/ppermute | solution.py:479
  66.6 1.1 %copy.29.got_ref = bf16[2,256,576]{2,1,0:T(8,128)(2,1)} copy(bf16[2,256,576]{1,2,0:T(8,128)(2,1)S(1)} %collective-permute-done.12) | data formatting | bytes 1179648 | tf_op jit(solution)/shard_map/ppermute | solution.py:479
  67.6 4.6 %tile_attention_and_patches.1 = f32[48,128]{1,0:T(8,128)} custom-call(bf16[48,1152]{1,0:T(8,128)(2,1)} %get-tuple-element.14.x_ref, bf16[48,640]{1,0:T(8,128)(2,1)} %get-tuple-element.15.q_ref, bf16[2,256,576]{2,1,0:T(8,128)(2,1)} %get-tuple-element.16.kv_ref, bf16[2,256,576]{2,1,0:T(8,128)(2,1)} %copy.29.got_ref, ...), custom_call_target="tpu_custom_call" | custom-call | tf_op jit(solution)/shard_map/tile_attention_and_patches/pallas_call | solution.py:268
  73.1 1.1 %convolution_convert_fusion = bf16[576,512]{1,0:T(8,128)(2,1)} fusion(bf16[576,36]{1,0:T(8,128)(2,1)S(1)} %copy-done.5, bf16[36,512]{1,0:T(8,128)(2,1)S(1)} %copy-done.8), kind=kOutput, calls=%fused_computation | convolution fusion | flops 21528576 | bytes 668160 | tf_op jit(solution)/shard_map/dot_general | solution.py:34
  74.3 1.4 %reshape.116 = bf16[144,2048]{1,0:T(8,128)(2,1)S(1)} reshape(bf16[576,512]{1,0:T(8,128)(2,1)} %convolution_convert_fusion) | data formatting | bytes 1179648 | tf_op jit(solution)/shard_map/reshape | solution.py:467
  75.7 1.1 %pad.9.wp_ref = bf16[256,2048]{1,0:T(8,128)(2,1)} pad(bf16[144,2048]{1,0:T(8,128)(2,1)S(1)} %reshape.116, bf16[]{:T(256)} %constant.129.clone.1), padding=0_112x0_0 | pad | bytes 1638402 | tf_op jit(solution)/shard_map/jit(_pad)/pad | solution.py:469
  77.4 5.8 %decoder_convolutions.1 = bf16[4,128,512]{2,1,0:T(8,128)(2,1)} custom-call(f32[40,128]{1,0:T(8,128)} %copy-done.6, f32[40,128]{1,0:T(8,128)} %copy-done.10, s32[48,128]{1,0:T(8,128)} %broadcast_in_dim.14.refs_6_.idx_ref, bf16[256,2048]{1,0:T(8,128)(2,1)} %pad.9.wp_ref, f32[1,512]{1,0:T(1,128)} %bitcast.40, f32[1,512]{1,0:T(1,128)} %bitcast.41, ...), custom_call_target="tpu_custom_call" | custom-call | tf_op jit(solution)/shard_map/decoder_convolutions/pallas_call | solution.py:360
  (63 shorter events, 11.6 us)
Async XLA Ops:
  0.0 8.5 %copy-start = (f32[100,5,1152]{2,0,1:T(8,128)S(1)}, f32[100,5,1152]{2,0,1:T(8,128)}, u32[]{:S(2)}) copy-start(f32[100,5,1152]{2,0,1:T(8,128)} %param.19) | copy-start | bytes 6912004
  0.0 31.8 %collective-permute-start.9 = (bf16[1,1152,1728]{1,2,0:T(8,128)(2,1)}, bf16[1,1152,1728]{1,2,0:T(8,128)(2,1)}, u32[]{:S(2)}, u32[]{:S(2)}) collective-permute-start(bf16[1,1152,1728]{1,2,0:T(8,128)(2,1)} %param.16), channel_id=1, source_target_pairs={{0,8},{8,0},{1,9},{9,1},{2,10},{10,2},{3,11},{11,3},{4,12},{12,4},... | collective-permute-start | bytes 11943944 | tf_op jit(solution)/shard_map/ppermute | solution.py:437
  1.6 19.5 %collective-permute-start.4 = (bf16[32,1152]{1,0:T(8,128)(2,1)S(1)}, bf16[32,1152]{1,0:T(8,128)(2,1)S(1)}, u32[]{:S(2)}, u32[]{:S(2)}) collective-permute-start(bf16[32,1152]{1,0:T(8,128)(2,1)S(1)} %dynamic-slice_bitcast_fusion), channel_id=1, source_target_pairs={{2,0},{3,1},{4,2},{5,3},{6,4},{7,5},{0,6},{1,7},{10,8},{11,9},{12,... | collective-permute-start | bytes 221192 | tf_op jit(solution)/shard_map/ppermute | solution.py:402
  6.1 16.0 %collective-permute-start.5 = (bf16[32,1152]{1,0:T(8,128)(2,1)S(1)}, bf16[32,1152]{1,0:T(8,128)(2,1)S(1)}, u32[]{:S(2)}, u32[]{:S(2)}) collective-permute-start(bf16[32,1152]{1,0:T(8,128)(2,1)S(1)} %dynamic-slice_bitcast_fusion), channel_id=1, source_target_pairs={{4,0},{5,1},{6,2},{7,3},{0,4},{1,5},{2,6},{3,7},{12,8},{13,9},{14,... | collective-permute-start | bytes 221192 | tf_op jit(solution)/shard_map/ppermute | solution.py:402
  6.1 16.0 %collective-permute-start.6 = (bf16[32,1152]{1,0:T(8,128)(2,1)S(1)}, bf16[32,1152]{1,0:T(8,128)(2,1)S(1)}, u32[]{:S(2)}, u32[]{:S(2)}) collective-permute-start(bf16[32,1152]{1,0:T(8,128)(2,1)S(1)} %dynamic-slice_bitcast_fusion), channel_id=1, source_target_pairs={{6,0},{7,1},{0,2},{1,3},{2,4},{3,5},{4,6},{5,7},{14,8},{15,9},{8,1... | collective-permute-start | bytes 221192 | tf_op jit(solution)/shard_map/ppermute | solution.py:402
  7.9 9.7 %collective-permute-start.8 = (f32[3,1152]{1,0:T(4,128)S(1)}, f32[3,1152]{1,0:T(4,128)S(1)}, u32[]{:S(2)}, u32[]{:S(2)}) collective-permute-start(f32[3,1152]{1,0:T(4,128)S(1)} %bitcast.39), channel_id=1, source_target_pairs={{0,8},{8,0},{1,9},{9,1},{2,10},{10,2},{3,11},{11,3},{4,12},{12,4},... | collective-permute-start | bytes 41480 | tf_op jit(solution)/shard_map/ppermute | solution.py:439
  11.1 9.3 %copy-start.7 = (f32[1,3,1152]{2,0,1:T(1,128)S(1)}, f32[1,3,1152]{2,0,1:T(1,128)}, u32[]{:S(2)}) copy-start(f32[1,3,1152]{2,0,1:T(1,128)} %param.18) | copy-start | bytes 41476
  11.1 9.3 %copy-start.11 = (f32[3]{0:T(128)S(1)}, f32[3]{0:T(128)}, u32[]{:S(2)}) copy-start(f32[3]{0:T(128)} %constant.141) | copy-start | bytes 40
  17.5 5.4 %collective-permute-start = (bf16[32,1152]{1,0:T(8,128)(2,1)S(1)}, bf16[32,1152]{1,0:T(8,128)(2,1)S(1)}, u32[]{:S(2)}, u32[]{:S(2)}) collective-permute-start(bf16[32,1152]{1,0:T(8,128)(2,1)S(1)} %slice_bitcast_fusion.2), channel_id=1, source_target_pairs={{2,0},{3,1},{4,2},{5,3},{6,4},{7,5},{0,6},{1,7},{10,8},{11,9},{12,... | collective-permute-start | bytes 221192 | tf_op jit(solution)/shard_map/ppermute | solution.py:402
  21.1 7.9 %collective-permute-start.1 = (bf16[32,1152]{1,0:T(8,128)(2,1)S(1)}, bf16[32,1152]{1,0:T(8,128)(2,1)S(1)}, u32[]{:S(2)}, u32[]{:S(2)}) collective-permute-start(bf16[32,1152]{1,0:T(8,128)(2,1)S(1)} %slice_bitcast_fusion.2), channel_id=1, source_target_pairs={{4,0},{5,1},{6,2},{7,3},{0,4},{1,5},{2,6},{3,7},{12,8},{13,9},{14,... | collective-permute-start | bytes 221192 | tf_op jit(solution)/shard_map/ppermute | solution.py:402
  22.2 6.7 %collective-permute-start.2 = (bf16[32,1152]{1,0:T(8,128)(2,1)S(1)}, bf16[32,1152]{1,0:T(8,128)(2,1)S(1)}, u32[]{:S(2)}, u32[]{:S(2)}) collective-permute-start(bf16[32,1152]{1,0:T(8,128)(2,1)S(1)} %slice_bitcast_fusion.2), channel_id=1, source_target_pairs={{6,0},{7,1},{0,2},{1,3},{2,4},{3,5},{4,6},{5,7},{14,8},{15,9},{8,1... | collective-permute-start | bytes 221192 | tf_op jit(solution)/shard_map/ppermute | solution.py:402
  22.2 31.8 %collective-permute-start.11 = (bf16[1,576,1152]{2,1,0:T(8,128)(2,1)}, bf16[1,576,1152]{2,1,0:T(8,128)(2,1)}, u32[]{:S(2)}, u32[]{:S(2)}) collective-permute-start(bf16[1,576,1152]{2,1,0:T(8,128)(2,1)} %wo_own.1), channel_id=1, source_target_pairs={{0,8},{8,0},{1,9},{9,1},{2,10},{10,2},{3,11},{11,3},{4,12},{12,4},... | collective-permute-start | bytes 3981320 | tf_op jit(solution)/shard_map/ppermute | solution.py:438
  22.3 16.0 %copy-start.4 = (bf16[128,1152]{1,0:T(8,128)(2,1)}, bf16[128,1152]{1,0:T(8,128)(2,1)S(1)}, u32[]{:S(2)}) copy-start(bf16[128,1152]{1,0:T(8,128)(2,1)S(1)} %pad_maximum_fusion.1.refs_0_) | copy-start | bytes 884740
  22.9 15.4 %collective-permute-start.7 = (bf16[128,1152]{1,0:T(8,128)(2,1)S(1)}, bf16[128,1152]{1,0:T(8,128)(2,1)}, u32[]{:S(2)}, u32[]{:S(2)}) collective-permute-start(bf16[128,1152]{1,0:T(8,128)(2,1)S(1)} %pad_maximum_fusion.1.refs_0_), channel_id=1, source_target_pairs={{1,0},{0,1},{3,2},{2,3},{5,4},{4,5},{7,6},{6,7},{9,8},{8,9},{11,10... | collective-permute-start | bytes 884744 | tf_op jit(solution)/shard_map/ppermute | solution.py:402
  28.9 9.4 %copy-start.2 = (bf16[128,1152]{1,0:T(8,128)(2,1)}, bf16[128,1152]{1,0:T(8,128)(2,1)S(1)}, u32[]{:S(2)}) copy-start(bf16[128,1152]{1,0:T(8,128)(2,1)S(1)} %pad_maximum_fusion.refs_0_) | copy-start | bytes 884740
  28.9 20.1 %collective-permute-start.3 = (bf16[128,1152]{1,0:T(8,128)(2,1)S(1)}, bf16[128,1152]{1,0:T(8,128)(2,1)S(1)}, u32[]{:S(2)}, u32[]{:S(2)}) collective-permute-start(bf16[128,1152]{1,0:T(8,128)(2,1)S(1)} %pad_maximum_fusion.refs_0_), channel_id=1, source_target_pairs={{1,0},{0,1},{3,2},{2,3},{5,4},{4,5},{7,6},{6,7},{9,8},{8,9},{11,10... | collective-permute-start | bytes 884744 | tf_op jit(solution)/shard_map/ppermute | solution.py:402
  46.0 5.9 %collective-permute-start.10 = (bf16[2,256,576]{1,2,0:T(8,128)(2,1)}, bf16[2,256,576]{1,2,0:T(8,128)(2,1)}, u32[]{:S(2)}, u32[]{:S(2)}) collective-permute-start(bf16[2,256,576]{1,2,0:T(8,128)(2,1)} %copy.23), channel_id=1, source_target_pairs={{0,8},{1,9},{2,10},{3,11},{4,12},{5,13},{6,14},{7,15},{16,24},{17,... | collective-permute-start | bytes 1769480 | tf_op jit(solution)/shard_map/ppermute | solution.py:473
  49.1 5.6 %copy-start.3 = (bf16[128,1152]{1,0:T(8,128)(2,1)}, bf16[128,1152]{1,0:T(8,128)(2,1)S(1)}, u32[]{:S(2)}) copy-start(bf16[128,1152]{1,0:T(8,128)(2,1)S(1)} %collective-permute-done.3.refs_1_) | copy-start | bytes 884740
  54.7 7.3 %copy-start.1 = (bf16[1,256,576]{2,1,0:T(8,128)(2,1)S(1)}, bf16[1,256,576]{2,1,0:T(8,128)(2,1)}, u32[]{:S(2)}) copy-start(bf16[1,256,576]{2,1,0:T(8,128)(2,1)} %get-tuple-element.18) | copy-start | bytes 884740
  64.3 2.2 %collective-permute-start.12 = (bf16[2,256,576]{1,2,0:T(8,128)(2,1)}, bf16[2,256,576]{1,2,0:T(8,128)(2,1)S(1)}, u32[]{:S(2)}, u32[]{:S(2)}) collective-permute-start(bf16[2,256,576]{1,2,0:T(8,128)(2,1)} %copy.27), channel_id=1, source_target_pairs={{0,8},{8,0},{1,9},{9,1},{2,10},{10,2},{3,11},{11,3},{4,12},{12,4},... | collective-permute-start | bytes 1769480 | tf_op jit(solution)/shard_map/ppermute | solution.py:479
  67.6 5.5 %copy-start.5 = (bf16[576,36]{1,0:T(8,128)(2,1)S(1)}, bf16[576,36]{1,0:T(8,128)(2,1)}, u32[]{:S(2)}) copy-start(bf16[576,36]{1,0:T(8,128)(2,1)} %constant.131.clone) | copy-start | bytes 124420
  67.6 5.5 %copy-start.8 = (bf16[36,512]{1,0:T(8,128)(2,1)S(1)}, bf16[36,512]{1,0:T(8,128)(2,1)}, u32[]{:S(2)}) copy-start(bf16[36,512]{1,0:T(8,128)(2,1)} %param.22) | copy-start | bytes 110596
  73.0 3.8 %copy-start.6 = (f32[40,128]{1,0:T(8,128)}, f32[40,128]{1,0:T(8,128)S(1)}, u32[]{:S(2)}) copy-start(f32[40,128]{1,0:T(8,128)S(1)} %slice.39.patch_ref) | copy-start | bytes 61444
  73.0 3.8 %collective-permute-start.13 = (f32[40,128]{1,0:T(8,128)S(1)}, f32[40,128]{1,0:T(8,128)S(1)}, u32[]{:S(2)}, u32[]{:S(2)}) collective-permute-start(f32[40,128]{1,0:T(8,128)S(1)} %slice.39.patch_ref), channel_id=1, source_target_pairs={{0,8},{8,0},{1,9},{9,1},{2,10},{10,2},{3,11},{11,3},{4,12},{12,4},... | collective-permute-start | bytes 61448 | tf_op jit(solution)/shard_map/ppermute | solution.py:483
  (2 other events, 2.9 us)

commit v4 on v3

v4 whole, which is shorter than its diff:
```python
import functools
import math

import jax
import jax.numpy as jnp
import numpy as np
from jax import lax
from jax.experimental import pallas as pl
from jax.experimental.pallas import tpu as pltpu
from jax.sharding import PartitionSpec as P

D = 1152
DH = 72
HEADS = 8
CH = 512
LATC = 4
TC = 256
DA = 576
DP = 640
SHIFT = 64
EPSILON = 1e-06
QUERY_SCALE = math.log2(math.e) / math.sqrt(DH)
BLOCK = 256
SMALL_BLOCK = 64
LANES = 128

F32 = jnp.float32
BF16 = jnp.bfloat16
VMEM = pl.BlockSpec(memory_space=pltpu.VMEM)
ANY = pl.BlockSpec(memory_space=pl.ANY)


def dot(a, b):
    return jnp.dot(a, b, preferred_element_type=F32)


def dot_t(a, b):
    return lax.dot_general(a, b, (((1,), (1,)), ((), ())), preferred_element_type=F32)


def normed(values, scale, shift):
    average = jnp.mean(values, axis=-1, keepdims=True)
    centred = values - average
    variance = jnp.mean(centred * centred, axis=-1, keepdims=True)
    return (centred * lax.rsqrt(variance + EPSILON) * scale + shift).astype(BF16)


def lane_window(start):
    return start // LANES * LANES, -(-(start + DH) // LANES) * LANES


def attend(query, kv_ref):
    count = query.shape[0]
    pieces = [None] * (DP // LANES)
    for head in range(HEADS):
        first, last = lane_window(head * DH)
        lane = lax.broadcasted_iota(jnp.int32, (count, last - first), 1) + first
        own = (lane >= head * DH) & (lane < (head + 1) * DH)
        q = jnp.where(own, query[:, first:last], jnp.zeros((), BF16))
        scores = dot_t(q, kv_ref[:, first:last])
        exponent = jnp.exp2(scores - jnp.max(scores, axis=1, keepdims=True))
        total = jnp.sum(exponent, axis=1, keepdims=True)
        start = DA + head * DH
        first, last = lane_window(start)
        numerator = dot(exponent.astype(BF16), kv_ref[:, first:last])
        lane = lax.broadcasted_iota(jnp.int32, (count, last - first), 1) + first
        own = (lane >= start) & (lane < start + DH)
        out = jnp.where(own, numerator * (1.0 / total), 0.0)
        for i in range((last - first) // LANES):
            at = (first - (DA - SHIFT)) // LANES + i
            part = out[:, i * LANES : (i + 1) * LANES]
            pieces[at] = part if pieces[at] is None else pieces[at] + part
    return jnp.concatenate(pieces, axis=1)


def each_block(count, body):
    if count <= BLOCK:
        body(0, count)
    else:

        @pl.loop(0, count // SMALL_BLOCK)
        def _(i):
            body(pl.multiple_of(i * SMALL_BLOCK, SMALL_BLOCK), SMALL_BLOCK)


def params(count):
    return pltpu.CompilerParams(vmem_limit_bytes=(24 if count <= BLOCK else 56) * 1024 * 1024)


def copy_of(block, own, other, target, sem):
    section = lax.axis_index("pipe")

    @pl.when(section == block)
    def _():
        pltpu.make_async_copy(own, target, sem).start()

    @pl.when(section != block)
    def _():
        pltpu.make_async_copy(other, target, sem).start()

    return pltpu.make_async_copy(own, target, sem)


def copy_qkv(block, own_ref, other_ref, w_ref, sems):
    return [
        copy_of(block, own_ref.at[0, a:b], other_ref.at[0, a:b], w_ref.at[a:b], sems.at[i])
        for i, (a, b) in enumerate(((0, DA), (DA, 3 * DA)))
    ]


def copy_out(block, own_ref, other_ref, wo_ref, sem):
    return copy_of(block, own_ref.at[0], other_ref.at[0], wo_ref.at[SHIFT:DP], sem)


def query_of(modulated, w_ref):
    projected = dot_t(modulated, w_ref[:DP]) * QUERY_SCALE
    lane = lax.broadcasted_iota(jnp.int32, projected.shape, 1)
    return jnp.where(lane < DA, projected, 0.0).astype(BF16)


def project_kernel(n_pieces, *refs):
    piece_refs = refs[:n_pieces]
    vec_ref, own_ref, other_ref, x_ref, q_ref, kv_ref, w_ref, sems = refs[n_pieces:]
    count = x_ref.shape[0]
    copies = copy_qkv(0, own_ref, other_ref, w_ref, sems)
    at = 0
    for ref in piece_refs:
        rows = ref.shape[0]
        x_ref[at : at + rows] = ref[...]
        at += rows
    if count > BLOCK:
        for copy in copies:
            copy.wait()

    def body(start, size):
        rows = pl.ds(start, size)
        modulated = normed(x_ref[rows].astype(F32), vec_ref[1:2], vec_ref[0:1])
        if count <= BLOCK:
            copies[0].wait()
            copies[1].wait()
        kv_ref[rows] = dot_t(modulated, w_ref[DA:]).astype(BF16)
        q_ref[rows] = query_of(modulated, w_ref)

    each_block(count, body)


def project(pieces, vecs, w_own, w_other):
    count = sum(piece.shape[0] for piece in pieces)
    return pl.pallas_call(
        functools.partial(project_kernel, len(pieces)),
        out_shape=(
            jax.ShapeDtypeStruct((count, D), BF16),
            jax.ShapeDtypeStruct((count, DP), BF16),
            jax.ShapeDtypeStruct((count, 2 * DA), BF16),
        ),
        in_specs=[VMEM] * (len(pieces) + 1) + [ANY] * 2,
        out_specs=(VMEM,) * 3,
        scratch_shapes=[
            pltpu.VMEM((3 * DA, D), BF16),
            pltpu.SemaphoreType.DMA((2,)),
        ],
        compiler_params=params(count),
        name="layer_norm_and_projections",
    )(*pieces, vecs, w_own, w_other)


def block_kernel(n_pieces, *refs):
    stale_refs = refs[:n_pieces]
    (
        x_ref, q_ref, kv_ref, got_ref, idx_ref, vec_ref, w_own, w_other, wo_own, wo_other,
        xt_ref, qt_ref, kv1_ref, send_ref, w_ref, wo_ref, all_ref, pick_ref, sems,
    ) = refs[n_pieces:]
    count = x_ref.shape[0]
    out_copy = copy_out(0, wo_own, wo_other, wo_ref, sems.at[2])
    in_copies = copy_qkv(1, w_own, w_other, w_ref, sems)
    first_core = lax.axis_index("pipe") == 0
    wo_ref[:SHIFT] = jnp.zeros((SHIFT, D), BF16)
    all_ref[:count] = kv_ref[...]
    at = 0
    for ref in stale_refs:
        rows = ref.shape[0]
        all_ref[count + at : count + at + rows] = jnp.where(first_core, ref[...], got_ref[at : at + rows])
        send_ref[at : at + rows] = ref[...]
        at += rows
    pick_ref[...] = jnp.zeros_like(pick_ref)
    tile_rows = idx_ref.shape[0]
    waits = [out_copy] + in_copies
    if count > BLOCK:
        for copy in waits:
            copy.wait()

    def body(start, size):
        rows = pl.ds(start, size)
        attended = attend(q_ref[rows], all_ref).astype(BF16)
        if count <= BLOCK:
            for copy in waits:
                copy.wait()
        branch = dot(attended, wo_ref[...])
        x1 = (x_ref[rows].astype(F32) + vec_ref[2:3] * branch).astype(BF16)
        modulated = normed(x1.astype(F32), vec_ref[4:5], vec_ref[3:4])
        fresh = dot_t(modulated, w_ref[DA:]).astype(BF16)
        kv1_ref[rows] = fresh

        @pl.when(first_core)
        def _():
            send_ref[rows] = fresh

        lane = lax.broadcasted_iota(jnp.int32, (tile_rows, size), 1) + start
        chosen = (lane == idx_ref[:, :1]).astype(F32).astype(BF16)
        pick_ref[0] += dot(chosen, x1)
        pick_ref[1] += dot(chosen, modulated)

    each_block(count, body)
    xt_ref[...] = pick_ref[0].astype(BF16)
    qt_ref[...] = query_of(pick_ref[1].astype(BF16), w_ref)


def first_block(stale_pieces, x, q, kv, got, idx, vecs, w_own, w_other, wo_own, wo_other):
    count = x.shape[0]
    tile_rows = idx.shape[0]
    return pl.pallas_call(
        functools.partial(block_kernel, len(stale_pieces)),
        out_shape=(
            jax.ShapeDtypeStruct((tile_rows, D), BF16),
            jax.ShapeDtypeStruct((tile_rows, DP), BF16),
            jax.ShapeDtypeStruct((count, 2 * DA), BF16),
            jax.ShapeDtypeStruct((count, 2 * DA), BF16),
        ),
        in_specs=[VMEM] * (len(stale_pieces) + 6) + [ANY] * 4,
        out_specs=(VMEM,) * 4,
        scratch_shapes=[
            pltpu.VMEM((3 * DA, D), BF16),
            pltpu.VMEM((DP, D), BF16),
            pltpu.VMEM((2 * count, 2 * DA), BF16),
            pltpu.VMEM((2, tile_rows, D), F32),
            pltpu.SemaphoreType.DMA((3,)),
        ],
        compiler_params=params(count),
        name="attention_and_next_keys",
    )(*stale_pieces, x, q, kv, got, idx, vecs, w_own, w_other, wo_own, wo_other)


def tile_kernel(
    x_ref, q_ref, kv_ref, got_ref, idx_ref, vec_ref, wf_ref, wo_own, wo_other, patch_ref, wo_ref, all_ref, sems
):
    count = kv_ref.shape[0]
    out_copy = copy_out(1, wo_own, wo_other, wo_ref, sems.at[0])
    wo_ref[:SHIFT] = jnp.zeros((SHIFT, D), BF16)
    all_ref[:count] = kv_ref[...]
    all_ref[count:] = got_ref[...]
    attended = attend(q_ref[...], all_ref).astype(BF16)
    out_copy.wait()
    branch = dot(attended, wo_ref[...])
    x2 = (x_ref[...].astype(F32) + vec_ref[5:6] * branch).astype(BF16)
    final = normed(x2.astype(F32), vec_ref[7:8], vec_ref[6:7])
    patches = dot_t(final, wf_ref[...]).astype(BF16).astype(F32)
    patch_ref[...] = jnp.zeros_like(patch_ref)
    patch_ref[:, : 4 * LATC] = jnp.where(idx_ref[:, :1] >= 0, patches, 0.0)


def tile_block(x, q, kv, got, idx, vecs, w_final, wo_own, wo_other):
    count = kv.shape[0]
    return pl.pallas_call(
        tile_kernel,
        out_shape=jax.ShapeDtypeStruct((x.shape[0], LANES), F32),
        in_specs=[VMEM] * 7 + [ANY] * 2,
        out_specs=VMEM,
        scratch_shapes=[
            pltpu.VMEM((DP, D), BF16),
            pltpu.VMEM((2 * count, 2 * DA), BF16),
            pltpu.SemaphoreType.DMA((1,)),
        ],
        compiler_params=params(count),
        name="tile_attention_and_patches",
    )(x, q, kv, got, idx, vecs, w_final, wo_own, wo_other)


def decode_kernel(
    rows, cols, pitch, patch_ref, got_ref, idx_ref, wp_ref, bin_ref, bup_ref, w_any, out_ref, w_ref, u_ref, ub_ref, sems
):
    copies = [pltpu.make_async_copy(w_any.at[t], w_ref.at[t], sems.at[t]) for t in range(9)]
    order = [3, 4, 5, 0, 1, 2, 6, 7, 8]
    for t in order:
        copies[t].start()
    first_core = lax.axis_index("pipe") == 0
    got = got_ref[:pitch]
    above = jnp.where(first_core, 0.0, got)
    below = jnp.where(first_core, got, 0.0)
    rim = [above] + [patch_ref[r * pitch : (r + 1) * pitch] for r in range(rows)] + [below]
    column_in = idx_ref[:pitch, :1] >= 0
    shifted = [[pltpu.roll(p, (-ds) % pitch, 0) if ds else p for ds in (-1, 0, 1)] for p in rim]
    for r in range(rows + 2):
        low, high = None, None
        for dr in (-1, 0, 1):
            if not 0 <= r + dr < rows + 2:
                continue
            for ds in range(3):
                tap = (dr + 1) * 3 + ds
                piece = shifted[r + dr][ds]
                if tap == 8:
                    high = piece
                else:
                    piece = pltpu.roll(piece, 4 * LATC * tap, 1) if tap else piece
                    low = piece if low is None else low + piece
        high = jnp.zeros_like(low) if high is None else high
        around = jnp.concatenate([low, high], axis=1).astype(BF16)
        for p in range(2):
            y = 2 * (r - 1) + p + 1
            if not 0 <= y < 2 * rows + 2:
                continue
            for q in range(2):
                at = (2 * p + q) * 2 * LANES
                act = dot(around, wp_ref[at : at + 2 * LANES]) + bin_ref[...]
                feature = act / (1.0 + jnp.exp(-act))
                keep = column_in
                if y == 0:
                    keep = keep & jnp.logical_not(first_core)
                if y == 2 * rows + 1:
                    keep = keep & first_core
                feature = jnp.where(keep, feature, 0.0)
                for c in range(CH // LANES):
                    part = feature[:, c * LANES : (c + 1) * LANES]
                    u_ref[y, c, pl.ds(2 * q, pitch, stride=4), :] = part
                    u_ref[y, c, pl.ds(2 * q + 1, pitch, stride=4), :] = part
    wide = 4 * cols
    for y in range(2 * rows + 2):
        for dx in range(3):
            for c in range(CH // LANES):
                ub_ref[dx, y * wide : (y + 1) * wide, c * LANES : (c + 1) * LANES] = u_ref[
                    y, c, 3 + dx : 3 + dx + wide, :
                ].astype(BF16)

    def tap_row(dy, y_first, y_count):
        total = None
        for dx in range(3):
            copies[3 * dy + dx].wait()
            part = dot(ub_ref[dx, y_first * wide : (y_first + y_count) * wide], w_ref[3 * dy + dx])
            total = part if total is None else total + part
        return total

    def rows_of(total, y):
        return total[y * wide : (y + 1) * wide]

    middle = tap_row(1, 1, 2 * rows) + bup_ref[...]
    before = tap_row(0, 0, 2 * rows + 1)
    after = tap_row(2, 1, 2 * rows + 1)
    for y in range(2 * rows):
        own = rows_of(middle, y)
        out_ref[2 * y] = (own + rows_of(before, y) + rows_of(after, y)).astype(BF16)
        out_ref[2 * y + 1] = (own + rows_of(before, y + 1) + rows_of(after, y + 1)).astype(BF16)


def decode(rows, cols, pitch, patches, got, idx, w_patch, b_in, b_up, w_up):
    return pl.pallas_call(
        functools.partial(decode_kernel, rows, cols, pitch),
        out_shape=jax.ShapeDtypeStruct((4 * rows, 4 * cols, CH), BF16),
        in_specs=[VMEM] * 6 + [ANY],
        out_specs=VMEM,
        scratch_shapes=[
            pltpu.VMEM((9, CH, CH), BF16),
            pltpu.VMEM((2 * rows + 2, CH // LANES, 4 * pitch, LANES), F32),
            pltpu.VMEM((3, (2 * rows + 2) * 4 * cols, CH), BF16),
            pltpu.SemaphoreType.DMA((9,)),
        ],
        compiler_params=params(0),
        name="decoder_convolutions",
    )(patches, got, idx, w_patch, b_in, b_up, w_up)


def patch_selector():
    sel = np.zeros((2, 2, 3, 3, 2, 2, LATC, 9 * LATC), np.float32)
    for p, q, dr, ds, pp, qq in np.ndindex(2, 2, 3, 3, 2, 2):
        dy = 2 * (dr - 1) + pp - p
        dx = 2 * (ds - 1) + qq - q
        if abs(dy) <= 1 and abs(dx) <= 1:
            tap = (dy + 1) * 3 + dx + 1
            for c in range(LATC):
                sel[p, q, dr, ds, pp, qq, c, tap * LATC + c] = 1.0
    sel = sel.reshape(4, 9 * 4 * LATC, 9 * LATC)
    return np.pad(sel, ((0, 0), (0, 2 * LANES - 9 * 4 * LATC), (0, 0))).reshape(-1, 9 * LATC)


def split_of(n):
    inner = 2 ** (int(math.log2(n)) // 2)
    return n // inner, inner


def shifted(block, k_outer, k_inner):
    n = lax.axis_size("patch")
    outer, inner = split_of(n)
    route = []
    for i in range(n):
        o, e = divmod(i, inner)
        route.append(((o + k_outer) % outer * inner + (e + k_inner) % inner, i))
    return lax.ppermute(block, "patch", route)


def gather_outer(own, outer):
    return jnp.concatenate([own] + [shifted(own, k, 0) for k in range(1, outer)], axis=0)


def gather_inner(column, inner):
    return [column] + [shifted(column, 0, k) for k in range(1, inner)]


def local(
    tokens,
    stale_kv,
    w_qkv,
    w_out,
    block_table,
    time_table,
    t_index,
    w_final,
    w_in,
    b_in,
    w_up,
    b_up,
):
    section = lax.axis_index("pipe")
    tile = lax.axis_index("patch")
    n_tiles = lax.axis_size("patch")
    swap = [(0, 1), (1, 0)]
    first_core = section == 0
    own_count = tokens.shape[1]
    count = own_count * n_tiles
    rows = count // TC
    cols = TC // n_tiles
    pitch = -(-(cols + 3) // 8) * 8
    outer, inner = split_of(n_tiles)

    own_tokens = lax.dynamic_index_in_dim(tokens, section, 0, keepdims=False)
    w_qkv = jnp.swapaxes(w_qkv, 1, 2)
    w_qkv_other = lax.ppermute(w_qkv, "pipe", swap)
    x_column = gather_outer(own_tokens, outer)
    x_column, own_stale = lax.optimization_barrier((x_column, stale_kv[0, 1]))
    x_pieces = gather_inner(x_column, inner)
    stale_pieces = gather_inner(gather_outer(own_stale, outer), inner)
    w_out_other = lax.ppermute(w_out, "pipe", swap)
    table_other = lax.ppermute(block_table[0], "pipe", swap)

    time_row = lax.dynamic_index_in_dim(time_table, t_index[0], 0, keepdims=False)
    table = block_table[0]
    table_0 = jnp.where(first_core, table, table_other)
    table_1 = jnp.where(first_core, table_other, table)
    ones = jnp.asarray([[0.0], [1.0], [0.0]], F32)
    vecs = jnp.concatenate(
        [
            time_row[:3] + table_0 + ones,
            time_row[:3] + table_1 + ones,
            time_row[3:5] + ones[:2],
        ],
        axis=0,
    )

    padded_rows = -(-rows * pitch // 16) * 16
    place = jnp.arange(padded_rows)
    column = place % pitch - 1 + tile * cols
    inside = (place % pitch < cols + 2) & (place < rows * pitch) & (column >= 0) & (column < TC)
    token = place // pitch * TC + jnp.clip(column, 0, TC - 1)
    source = token // own_count
    k_outer = (source // inner - tile // inner) % outer
    k_inner = (source % inner - tile % inner) % inner
    spot = (k_inner * outer + k_outer) * own_count + token % own_count
    idx = jnp.broadcast_to(jnp.where(inside, spot, -1)[:, None], (padded_rows, LANES)).astype(jnp.int32)

    w_patch = dot(jnp.asarray(patch_selector(), BF16), w_in).astype(BF16)
    x_pieces, w_patch, idx = lax.optimization_barrier((x_pieces, w_patch, idx))

    x, query, fresh = project(x_pieces, vecs, w_qkv, w_qkv_other)
    got = lax.ppermute(fresh, "pipe", [(0, 1)])
    x_tile, q_tile, fresh, send = first_block(
        stale_pieces, x, query, fresh, got, idx, vecs, w_qkv, w_qkv_other, w_out, w_out_other
    )
    got = lax.ppermute(send, "pipe", swap)
    patches = tile_block(x_tile, q_tile, fresh, got, idx, vecs, w_final.T, w_out, w_out_other)
    edge = patches
    if rows > 1:
        edge = jnp.where(first_core, patches[(rows - 1) * pitch : rows * pitch], patches[:pitch])
    got = lax.ppermute(edge, "pipe", swap)
    return decode(rows, cols, pitch, patches, got, idx, w_patch, b_in[None], b_up[None], w_up)


def solution(mesh):
    placed = (
        P(None, ("grp", "patch"), None),
        P("pipe", None, ("grp", "patch"), None),
        P("pipe", None, None),
        P("pipe", None, None),
        P("pipe", None, None),
        P(),
        P("grp"),
        P(),
        P(),
        P(),
        P(),
        P(),
    )
    return jax.shard_map(
        local,
        mesh=mesh,
        in_specs=placed,
        out_specs=P(("grp", "pipe"), "patch", None),
        check_vma=False,
    )
```

time: 84.2 us -> 59.7 us (0.71)
  local copies, waits for them, and re-layouts: 33.9 us -> 7.17 us
  Pallas kernels: 23.2 us -> 15.5 us
  waiting for transfers between devices: 6.3 us -> 13.9 us
  starting transfers between devices: 15.8 us -> 18.6 us
    ppermute x3 -> x0, local copies, waits for them, and re-layouts: 9.71 us -> none  [the longest x1 6.48 us: local(): w_qkv_other = lax.ppermute(w_qkv, 'pipe', swap)]
    unnamed x31 -> x22, local copies, waits for them, and re-layouts: 11.4 us -> 4.41 us
    ppermute x8, waiting for transfers between devices: 5.08 us -> 10.9 us  [shifted(): return lax.ppermute(block, 'patch', route)]
    pallas_call x1, Pallas kernels: 5.54 us -> 2.38 us  [project(): pl.pallas_call(functools.partial(project_kernel, len(pieces)), out_shape=...]
    ppermute x8, starting transfers between devices: 12.6 us -> 15.3 us  [shifted(): return lax.ppermute(block, 'patch', route)]
    pallas_call x1 -> x0, local copies, waits for them, and re-layouts: 2.13 us -> none  [project(): pl.pallas_call(functools.partial(project_kernel, len(pieces)), out_shape=...]
    another operation x1 -> x0, local copies, waits for them, and re-layouts: 1.95 us -> none  [local(): stale = jnp.stack([stale[:, :DA], stale[:, DA:]])]
    pad x2 -> x0, local copies, waits for them, and re-layouts: 1.89 us -> none  [the longest x1 1.11 us: local(): w_patch = jnp.pad(w_patch, ((0, 2 * LANES - 9 * 4 * LATC), (0, 0)))]
  transfers between devices with their start and end apart: 14 -> 14, of which waited for: 3 -> 5; matrix products, arithmetic and copies ran while one was open for 38% -> 14% of each run, Pallas kernels for 7% -> 4%
where the time goes in v4:
time: 59.7 us; the launch traced here: 59.3 us
  starting transfers between devices  18.6 us (31%)
  Pallas kernels  15.5 us (26%)
  waiting for transfers between devices  13.9 us (23%)
  local copies, waits for them, and re-layouts  7.17 us (12%)
  other arithmetic  1.87 us (3%)
  matrix products  1.36 us (2%)
  between operations  0.89 us (1%)
    ppermute x8, starting transfers between devices, shifted(): return lax.ppermute(block, 'patch', route)  15.3 us
    ppermute x8, waiting for transfers between devices, shifted(): return lax.ppermute(block, 'patch', route)  10.9 us
    pallas_call x1, Pallas kernels, first_block(): pl.pallas_call(functools.partial(block_kernel, len(stale_pieces)), out_sh...  5.48 us
    unnamed x22, local copies, waits for them, and re-layouts  4.41 us
    pallas_call x1, Pallas kernels, decode(): pl.pallas_call(functools.partial(decode_kernel, rows, cols, pitch), out_s...  4.32 us
    pallas_call x1, Pallas kernels, tile_block(): pl.pallas_call(tile_kernel, out_shape=jax.ShapeDtypeStruct((x.shape[0], L...  3.31 us
    pallas_call x1, Pallas kernels, project(): pl.pallas_call(functools.partial(project_kernel, len(pieces)), out_shape=...  2.38 us
    ppermute x1, waiting for transfers between devices, local(): got = lax.ppermute(send, 'pipe', swap)  1.99 us
  transfers between devices with their start and end apart: 14, of which 5 were waited for; matrix products, arithmetic and copies ran while one was open for 14% of the time, Pallas kernels for 4%

profile of v4, /device:TPU:0, one launch (start us, length us, event | category | flops | bytes accessed | tf_op | source)
XLA Modules:
  0.0 59.3 jit_solution(2185243532198155271)
XLA Ops:
  0.5 1.1 %dynamic-slice_bitcast_fusion = bf16[32,1152]{1,0:T(8,128)(2,1)S(1)} fusion(bf16[2,32,1152]{2,1,0:T(8,128)(2,1)} %param.14, s32[]{:T(128)S(6)} %select_n.108), kind=kLoop, calls=%fused_computation.3 | loop fusion | bytes 147460 | tf_op jit(solution)/shard_map/jit(dynamic_index_in_dim)/squeeze | solution.py:432
  1.6 2.5 %collective-permute-start.2 = (bf16[32,1152]{1,0:T(8,128)(2,1)S(1)}, bf16[32,1152]{1,0:T(8,128)(2,1)}, u32[]{:S(2)}, u32[]{:S(2)}) collective-permute-start(bf16[32,1152]{1,0:T(8,128)(2,1)S(1)} %dynamic-slice_bitcast_fusion), channel_id=1, source_target_pairs={{6,0},{7,1},{0,2},{1,3},{2,4},{3,5},{4,6},{5,7},{14,8},{15,9},{8,1... | collective-permute-start | bytes 221192 | tf_op jit(solution)/shard_map/ppermute | solution.py:395
  4.1 2.6 %collective-permute-start.1 = (bf16[32,1152]{1,0:T(8,128)(2,1)S(1)}, bf16[32,1152]{1,0:T(8,128)(2,1)}, u32[]{:S(2)}, u32[]{:S(2)}) collective-permute-start(bf16[32,1152]{1,0:T(8,128)(2,1)S(1)} %dynamic-slice_bitcast_fusion), channel_id=1, source_target_pairs={{4,0},{5,1},{6,2},{7,3},{0,4},{1,5},{2,6},{3,7},{12,8},{13,9},{14,... | collective-permute-start | bytes 221192 | tf_op jit(solution)/shard_map/ppermute | solution.py:395
  6.7 1.3 %collective-permute-start = (bf16[32,1152]{1,0:T(8,128)(2,1)S(1)}, bf16[32,1152]{1,0:T(8,128)(2,1)}, u32[]{:S(2)}, u32[]{:S(2)}) collective-permute-start(bf16[32,1152]{1,0:T(8,128)(2,1)S(1)} %dynamic-slice_bitcast_fusion), channel_id=1, source_target_pairs={{2,0},{3,1},{4,2},{5,3},{6,4},{7,5},{0,6},{1,7},{10,8},{11,9},{12,... | collective-permute-start | bytes 221192 | tf_op jit(solution)/shard_map/ppermute | solution.py:395
  8.0 1.3 %copy.37 = f32[1,3,1152]{2,1,0:T(4,128)} copy(f32[1,3,1152]{2,0,1:T(1,128)} %param.18) | data formatting | bytes 27648
  10.1 1.4 %convolution_convert_fusion.wp_ref = bf16[1024,512]{1,0:T(8,128)(2,1)S(1)} fusion(bf16[1024,36]{1,0:T(8,128)(2,1)} %constant.129.clone, bf16[36,512]{1,0:T(8,128)(2,1)} %param.22), kind=kOutput, calls=%fused_computation | convolution fusion | flops 38273024 | bytes 1159168 | tf_op jit(solution)/shard_map/dot_general | solution.py:34
  11.5 1.5 %slice_bitcast_fusion = bf16[32,1152]{1,0:T(8,128)(2,1)} fusion(bf16[1,2,32,1152]{3,2,1,0:T(8,128)(2,1)} %param.15), kind=kLoop, calls=%fused_computation.2 | loop fusion | bytes 147456 | tf_op jit(solution)/shard_map/squeeze | solution.py:436
  13.6 0.8 %fusion.2 = (f32[3,1152]{1,0:T(4,128)S(1)}, f32[3,1152]{1,0:T(4,128)S(1)}) fusion(f32[1,3,1152]{2,0,1:T(1,128)S(1)} %constant_dynamic-slice_fusion, f32[3,1152]{1,0:T(4,128)} %collective-permute-done.8, f32[3]{0:T(128)} %constant.135, pred[]{:T(512)S(6)} %eq.12, f32[1,3,1152]{2,0,1:T(1,128)} %param.18), kind=kLoop, calls=%fused_computation.8 | loop fusion | flops 20736 | bytes 69133 | tf_op jit(solution)/shard_map/add | solution.py:449
  14.5 1.0 %pad_maximum_fusion.refs_0_ = bf16[128,1152]{1,0:T(8,128)(2,1)S(1)} fusion(bf16[32,1152]{1,0:T(8,128)(2,1)} %collective-permute-done.2, bf16[32,1152]{1,0:T(8,128)(2,1)} %collective-permute-done.1, bf16[32,1152]{1,0:T(8,128)(2,1)} %collective-permute-done, bf16[32,1152]{1,0:T(8,128)(2,1)S(1)} %dynamic-slice_bitcast_fusion), kind=kLoop, calls=%fused_computation.1 | loop fusion | flops 1179648 | bytes 589824 | tf_op jit(solution)/shard_map/concatenate | solution.py:399
  16.2 3.1 %collective-permute-start.3 = (bf16[32,1152]{1,0:T(8,128)(2,1)}, bf16[32,1152]{1,0:T(8,128)(2,1)S(1)}, u32[]{:S(2)}, u32[]{:S(2)}) collective-permute-start(bf16[32,1152]{1,0:T(8,128)(2,1)} %slice_bitcast_fusion), channel_id=1, source_target_pairs={{2,0},{3,1},{4,2},{5,3},{6,4},{7,5},{0,6},{1,7},{10,8},{11,9},{12,... | collective-permute-start | bytes 221192 | tf_op jit(solution)/shard_map/ppermute | solution.py:395
  19.4 1.5 %collective-permute-start.7 = (bf16[128,1152]{1,0:T(8,128)(2,1)S(1)}, bf16[128,1152]{1,0:T(8,128)(2,1)S(1)}, u32[]{:S(2)}, u32[]{:S(2)}) collective-permute-start(bf16[128,1152]{1,0:T(8,128)(2,1)S(1)} %pad_maximum_fusion.refs_0_), channel_id=1, source_target_pairs={{1,0},{0,1},{3,2},{2,3},{5,4},{4,5},{7,6},{6,7},{9,8},{8,9},{11,10... | collective-permute-start | bytes 884744 | tf_op jit(solution)/shard_map/ppermute | solution.py:395
  20.9 0.9 %constant_dynamic-update-slice_fusion.3 = bf16[128,1152]{1,0:T(8,128)(2,1)S(1)} fusion(bf16[32,1152]{1,0:T(8,128)(2,1)} %slice_bitcast_fusion), kind=kLoop, calls=%fused_computation.14 | loop fusion | bytes 147456
  22.0 1.9 %collective-permute-start.4 = (bf16[32,1152]{1,0:T(8,128)(2,1)}, bf16[32,1152]{1,0:T(8,128)(2,1)S(1)}, u32[]{:S(2)}, u32[]{:S(2)}) collective-permute-start(bf16[32,1152]{1,0:T(8,128)(2,1)} %slice_bitcast_fusion), channel_id=1, source_target_pairs={{4,0},{5,1},{6,2},{7,3},{0,4},{1,5},{2,6},{3,7},{12,8},{13,9},{14,... | collective-permute-start | bytes 221192 | tf_op jit(solution)/shard_map/ppermute | solution.py:395
  23.9 3.8 %collective-permute-done.7.refs_1_ = bf16[128,1152]{1,0:T(8,128)(2,1)S(1)} collective-permute-done((bf16[128,1152]{1,0:T(8,128)(2,1)S(1)}, bf16[128,1152]{1,0:T(8,128)(2,1)S(1)}, u32[]{:S(2)}, u32[]{:S(2)}) %collective-permute-start.7) | collective-permute-done | bytes 294944 | tf_op jit(solution)/shard_map/ppermute | solution.py:395
  27.8 2.1 %copy-done.1 = bf16[1,1152,1728]{1,2,0:T(8,128)(2,1)S(1)} copy-done((bf16[1,1152,1728]{1,2,0:T(8,128)(2,1)S(1)}, bf16[1,1152,1728]{1,2,0:T(8,128)(2,1)}, u32[]{:S(2)}) %copy-start.1) | copy-done | bytes 3981336
  30.0 2.4 %layer_norm_and_projections.1 = (bf16[256,1152]{1,0:T(8,128)(2,1)S(1)}, bf16[256,640]{1,0:T(8,128)(2,1)S(1)}, bf16[256,1152]{1,0:T(8,128)(2,1)S(1)}) custom-call(bf16[128,1152]{1,0:T(8,128)(2,1)S(1)} %pad_maximum_fusion.refs_0_, bf16[128,1152]{1,0:T(8,128)(2,1)S(1)} %collective-permute-done.7.refs_1_, ...), custom_call_target="tpu_custom_call" | custom-call | tf_op jit(solution)/shard_map/layer_norm_and_projections/pallas_call | solution.py:149
  32.3 2.0 %collective-permute-start.10 = (bf16[256,1152]{1,0:T(8,128)(2,1)S(1)}, bf16[256,1152]{1,0:T(8,128)(2,1)S(1)}, u32[]{:S(2)}, u32[]{:S(2)}) collective-permute-start(bf16[256,1152]{1,0:T(8,128)(2,1)S(1)} %get-tuple-element.24.refs_4_), channel_id=1, source_target_pairs={{0,8},{1,9},{2,10},{3,11},{4,12},{5,13},{6,14},{7,15},{16,24},{17,... | collective-permute-start | bytes 1769480 | tf_op jit(solution)/shard_map/ppermute | solution.py:471
  34.4 1.6 %collective-permute-start.6 = (bf16[128,1152]{1,0:T(8,128)(2,1)S(1)}, bf16[128,1152]{1,0:T(8,128)(2,1)S(1)}, u32[]{:S(2)}, u32[]{:S(2)}) collective-permute-start(bf16[128,1152]{1,0:T(8,128)(2,1)S(1)} %constant_dynamic-update-slice_fusion.refs_0_), channel_id=1, source_target_pairs={{1,0},{0,1},{3,2},{2,3},{5,4},{4,5},{7,6},{6,7},{9,8},{8,9},{11,10... | collective-permute-start | bytes 884744 | tf_op jit(solution)/shard_map/ppermute | solution.py:395
  36.0 6.7 %collective-permute-done.6.refs_1_ = bf16[128,1152]{1,0:T(8,128)(2,1)S(1)} collective-permute-done((bf16[128,1152]{1,0:T(8,128)(2,1)S(1)}, bf16[128,1152]{1,0:T(8,128)(2,1)S(1)}, u32[]{:S(2)}, u32[]{:S(2)}) %collective-permute-start.6) | collective-permute-done | bytes 294944 | tf_op jit(solution)/shard_map/ppermute | solution.py:395
  42.8 5.5 %attention_and_next_keys.1 = (bf16[48,1152]{1,0:T(8,128)(2,1)S(1)}, bf16[48,640]{1,0:T(8,128)(2,1)S(1)}, bf16[256,1152]{1,0:T(8,128)(2,1)S(1)}, bf16[256,1152]{1,0:T(8,128)(2,1)S(1)}) custom-call(bf16[128,1152]{1,0:T(8,128)(2,1)S(1)} %constant_dynamic-update-slice_fusion.refs_0_, bf16[128,1152]{1,0:T(8,128)(2,1)S(1)} %collective-permute-done.6.refs_1_, ...), custom_call_target="tpu_custom_call" | custom-call | tf_op jit(solution)/shard_map/attention_and_next_keys/pallas_call | solution.py:221
  48.4 2.0 %collective-permute-done.12.got_ref = bf16[256,1152]{1,0:T(8,128)(2,1)S(1)} collective-permute-done((bf16[256,1152]{1,0:T(8,128)(2,1)S(1)}, bf16[256,1152]{1,0:T(8,128)(2,1)S(1)}, u32[]{:S(2)}, u32[]{:S(2)}) %collective-permute-start.12) | collective-permute-done | bytes 589856 | tf_op jit(solution)/shard_map/ppermute | solution.py:475
  50.4 3.3 %tile_attention_and_patches.1.patch_ref = f32[48,128]{1,0:T(8,128)S(1)} custom-call(bf16[48,1152]{1,0:T(8,128)(2,1)S(1)} %get-tuple-element.26.x_ref, bf16[48,640]{1,0:T(8,128)(2,1)S(1)} %get-tuple-element.27.q_ref, bf16[256,1152]{1,0:T(8,128)(2,1)S(1)} %get-tuple-element.28.kv_ref, bf16[256,1152]{1,0:T(8,128)(2,1)S(1)} %collective-permute-done.12.got_ref, ...), custom_call_target="tpu_custom_call" | custom-call | tf_op jit(solution)/shard_map/tile_attention_and_patches/pallas_call | solution.py:263
  53.9 1.1 %collective-permute-done.13.got_ref = f32[48,128]{1,0:T(8,128)S(1)} collective-permute-done((f32[48,128]{1,0:T(8,128)S(1)}, f32[48,128]{1,0:T(8,128)S(1)}, u32[]{:S(2)}, u32[]{:S(2)}) %collective-permute-start.13) | collective-permute-done | bytes 24608 | tf_op jit(solution)/shard_map/ppermute | solution.py:480
  55.0 4.3 %decoder_convolutions.1 = bf16[4,128,512]{2,1,0:T(8,128)(2,1)} custom-call(f32[48,128]{1,0:T(8,128)S(1)} %tile_attention_and_patches.1.patch_ref, f32[48,128]{1,0:T(8,128)S(1)} %collective-permute-done.13.got_ref, s32[48,128]{1,0:T(8,128)S(1)} %broadcast_in_dim.14.refs_6_.idx_ref, bf16[1024,512]{1,0:T(8,128)(2,1)S(1)} %convolution_convert_fusion.wp_ref, ...), custom_call_target="tpu_custom_call" | custom-call | tf_op jit(solution)/shard_map/decoder_convolutions/pallas_call | solution.py:354
  (43 shorter events, 2.6 us)
Async XLA Ops:
  0.0 10.0 %copy-start = (f32[100,5,1152]{2,0,1:T(8,128)S(1)}, f32[100,5,1152]{2,0,1:T(8,128)}, u32[]{:S(2)}) copy-start(f32[100,5,1152]{2,0,1:T(8,128)} %param.19) | copy-start | bytes 6912004
  0.0 27.8 %collective-permute-start.9 = (bf16[1,1728,1152]{2,1,0:T(8,128)(2,1)}, bf16[1,1728,1152]{2,1,0:T(8,128)(2,1)}, u32[]{:S(2)}, u32[]{:S(2)}) collective-permute-start(bf16[1,1728,1152]{2,1,0:T(8,128)(2,1)} %bitcast.35), channel_id=1, source_target_pairs={{0,8},{8,0},{1,9},{9,1},{2,10},{10,2},{3,11},{11,3},{4,12},{12,4},... | collective-permute-start | bytes 11943944 | tf_op jit(solution)/shard_map/ppermute | solution.py:434
  1.6 12.9 %collective-permute-start.2 = (bf16[32,1152]{1,0:T(8,128)(2,1)S(1)}, bf16[32,1152]{1,0:T(8,128)(2,1)}, u32[]{:S(2)}, u32[]{:S(2)}) collective-permute-start(bf16[32,1152]{1,0:T(8,128)(2,1)S(1)} %dynamic-slice_bitcast_fusion), channel_id=1, source_target_pairs={{6,0},{7,1},{0,2},{1,3},{2,4},{3,5},{4,6},{5,7},{14,8},{15,9},{8,1... | collective-permute-start | bytes 221192 | tf_op jit(solution)/shard_map/ppermute | solution.py:395
  4.1 10.4 %collective-permute-start.1 = (bf16[32,1152]{1,0:T(8,128)(2,1)S(1)}, bf16[32,1152]{1,0:T(8,128)(2,1)}, u32[]{:S(2)}, u32[]{:S(2)}) collective-permute-start(bf16[32,1152]{1,0:T(8,128)(2,1)S(1)} %dynamic-slice_bitcast_fusion), channel_id=1, source_target_pairs={{4,0},{5,1},{6,2},{7,3},{0,4},{1,5},{2,6},{3,7},{12,8},{13,9},{14,... | collective-permute-start | bytes 221192 | tf_op jit(solution)/shard_map/ppermute | solution.py:395
  6.7 7.8 %collective-permute-start = (bf16[32,1152]{1,0:T(8,128)(2,1)S(1)}, bf16[32,1152]{1,0:T(8,128)(2,1)}, u32[]{:S(2)}, u32[]{:S(2)}) collective-permute-start(bf16[32,1152]{1,0:T(8,128)(2,1)S(1)} %dynamic-slice_bitcast_fusion), channel_id=1, source_target_pairs={{2,0},{3,1},{4,2},{5,3},{6,4},{7,5},{0,6},{1,7},{10,8},{11,9},{12,... | collective-permute-start | bytes 221192 | tf_op jit(solution)/shard_map/ppermute | solution.py:395
  9.4 3.7 %collective-permute-start.8 = (f32[3,1152]{1,0:T(4,128)}, f32[3,1152]{1,0:T(4,128)}, u32[]{:S(2)}, u32[]{:S(2)}) collective-permute-start(f32[3,1152]{1,0:T(4,128)} %bitcast.31), channel_id=1, source_target_pairs={{0,8},{8,0},{1,9},{9,1},{2,10},{10,2},{3,11},{11,3},{4,12},{12,4},... | collective-permute-start | bytes 41480 | tf_op jit(solution)/shard_map/ppermute | solution.py:440
  13.1 29.7 %collective-permute-start.11 = (bf16[1,576,1152]{2,1,0:T(8,128)(2,1)}, bf16[1,576,1152]{2,1,0:T(8,128)(2,1)S(1)}, u32[]{:S(2)}, u32[]{:S(2)}) collective-permute-start(bf16[1,576,1152]{2,1,0:T(8,128)(2,1)} %wo_own.1), channel_id=1, source_target_pairs={{0,8},{8,0},{1,9},{9,1},{2,10},{10,2},{3,11},{11,3},{4,12},{12,4},... | collective-permute-start | bytes 3981320 | tf_op jit(solution)/shard_map/ppermute | solution.py:439
  15.5 18.9 %collective-permute-start.5 = (bf16[32,1152]{1,0:T(8,128)(2,1)}, bf16[32,1152]{1,0:T(8,128)(2,1)S(1)}, u32[]{:S(2)}, u32[]{:S(2)}) collective-permute-start(bf16[32,1152]{1,0:T(8,128)(2,1)} %slice_bitcast_fusion), channel_id=1, source_target_pairs={{6,0},{7,1},{0,2},{1,3},{2,4},{3,5},{4,6},{5,7},{14,8},{15,9},{8,1... | collective-permute-start | bytes 221192 | tf_op jit(solution)/shard_map/ppermute | solution.py:395
  16.2 5.8 %collective-permute-start.3 = (bf16[32,1152]{1,0:T(8,128)(2,1)}, bf16[32,1152]{1,0:T(8,128)(2,1)S(1)}, u32[]{:S(2)}, u32[]{:S(2)}) collective-permute-start(bf16[32,1152]{1,0:T(8,128)(2,1)} %slice_bitcast_fusion), channel_id=1, source_target_pairs={{2,0},{3,1},{4,2},{5,3},{6,4},{7,5},{0,6},{1,7},{10,8},{11,9},{12,... | collective-permute-start | bytes 221192 | tf_op jit(solution)/shard_map/ppermute | solution.py:395
  19.4 8.4 %collective-permute-start.7 = (bf16[128,1152]{1,0:T(8,128)(2,1)S(1)}, bf16[128,1152]{1,0:T(8,128)(2,1)S(1)}, u32[]{:S(2)}, u32[]{:S(2)}) collective-permute-start(bf16[128,1152]{1,0:T(8,128)(2,1)S(1)} %pad_maximum_fusion.refs_0_), channel_id=1, source_target_pairs={{1,0},{0,1},{3,2},{2,3},{5,4},{4,5},{7,6},{6,7},{9,8},{8,9},{11,10... | collective-permute-start | bytes 884744 | tf_op jit(solution)/shard_map/ppermute | solution.py:395
  22.0 12.3 %collective-permute-start.4 = (bf16[32,1152]{1,0:T(8,128)(2,1)}, bf16[32,1152]{1,0:T(8,128)(2,1)S(1)}, u32[]{:S(2)}, u32[]{:S(2)}) collective-permute-start(bf16[32,1152]{1,0:T(8,128)(2,1)} %slice_bitcast_fusion), channel_id=1, source_target_pairs={{4,0},{5,1},{6,2},{7,3},{0,4},{1,5},{2,6},{3,7},{12,8},{13,9},{14,... | collective-permute-start | bytes 221192 | tf_op jit(solution)/shard_map/ppermute | solution.py:395
  27.8 2.1 %copy-start.1 = (bf16[1,1152,1728]{1,2,0:T(8,128)(2,1)S(1)}, bf16[1,1152,1728]{1,2,0:T(8,128)(2,1)}, u32[]{:S(2)}) copy-start(bf16[1,1152,1728]{1,2,0:T(8,128)(2,1)} %param.16) | copy-start | bytes 11943940
  30.0 12.8 %copy-start.2 = (bf16[1,1152,1728]{1,2,0:T(8,128)(2,1)S(1)}, bf16[1,1152,1728]{1,2,0:T(8,128)(2,1)}, u32[]{:S(2)}) copy-start(bf16[1,1152,1728]{1,2,0:T(8,128)(2,1)} %param.16) | copy-start | bytes 11943940
  30.0 12.8 %copy-start.3 = (bf16[1,576,1152]{2,1,0:T(8,128)(2,1)S(1)}, bf16[1,576,1152]{2,1,0:T(8,128)(2,1)}, u32[]{:S(2)}) copy-start(bf16[1,576,1152]{2,1,0:T(8,128)(2,1)} %wo_own.1) | copy-start | bytes 3981316
  32.3 10.4 %collective-permute-start.10 = (bf16[256,1152]{1,0:T(8,128)(2,1)S(1)}, bf16[256,1152]{1,0:T(8,128)(2,1)S(1)}, u32[]{:S(2)}, u32[]{:S(2)}) collective-permute-start(bf16[256,1152]{1,0:T(8,128)(2,1)S(1)} %get-tuple-element.24.refs_4_), channel_id=1, source_target_pairs={{0,8},{1,9},{2,10},{3,11},{4,12},{5,13},{6,14},{7,15},{16,24},{17,... | collective-permute-start | bytes 1769480 | tf_op jit(solution)/shard_map/ppermute | solution.py:471
  34.4 8.3 %collective-permute-start.6 = (bf16[128,1152]{1,0:T(8,128)(2,1)S(1)}, bf16[128,1152]{1,0:T(8,128)(2,1)S(1)}, u32[]{:S(2)}, u32[]{:S(2)}) collective-permute-start(bf16[128,1152]{1,0:T(8,128)(2,1)S(1)} %constant_dynamic-update-slice_fusion.refs_0_), channel_id=1, source_target_pairs={{1,0},{0,1},{3,2},{2,3},{5,4},{4,5},{7,6},{6,7},{9,8},{8,9},{11,10... | collective-permute-start | bytes 884744 | tf_op jit(solution)/shard_map/ppermute | solution.py:395
  42.7 12.2 %slice-start = ((s8[4718592]{0:T(1024)(128)(4,1)}), s8[4194304]{0:T(1024)(128)(4,1)S(1)}, s32[]{:S(2)}) async-start(s8[4718592]{0:T(1024)(128)(4,1)} %bitcast.38), calls=%async_computation | async-start | bytes 8388608
  42.7 7.6 %copy-start.4 = (bf16[1152,16]{0,1:T(8,128)(2,1)S(1)}, bf16[1152,16]{0,1:T(8,128)(2,1)}, u32[]{:S(2)}) copy-start(bf16[1152,16]{0,1:T(8,128)(2,1)} %param.21) | copy-start | bytes 110596
  42.8 12.2 %slice-start.1 = ((s8[4718592]{0:T(1024)(128)(4,1)}), s8[524288]{0:T(1024)(128)(4,1)S(1)}, s32[]{:S(2)}) async-start(s8[4718592]{0:T(1024)(128)(4,1)} %bitcast.38), calls=%async_computation.1 | async-start | bytes 1048576
  48.3 6.7 %copy-start.5 = (f32[512]{0:T(512)S(1)}, f32[512]{0:T(512)}, u32[]{:S(2)}) copy-start(f32[512]{0:T(512)} %param.23) | copy-start | bytes 6148
  48.3 6.7 %copy-start.6 = (f32[512]{0:T(512)S(1)}, f32[512]{0:T(512)}, u32[]{:S(2)}) copy-start(f32[512]{0:T(512)} %param.25) | copy-start | bytes 6148
  48.3 2.1 %collective-permute-start.12 = (bf16[256,1152]{1,0:T(8,128)(2,1)S(1)}, bf16[256,1152]{1,0:T(8,128)(2,1)S(1)}, u32[]{:S(2)}, u32[]{:S(2)}) collective-permute-start(bf16[256,1152]{1,0:T(8,128)(2,1)S(1)} %get-tuple-element.29), channel_id=1, source_target_pairs={{0,8},{8,0},{1,9},{9,1},{2,10},{10,2},{3,11},{11,3},{4,12},{12,4},... | collective-permute-start | bytes 1769480 | tf_op jit(solution)/shard_map/ppermute | solution.py:475
  53.7 1.3 %collective-permute-start.13 = (f32[48,128]{1,0:T(8,128)S(1)}, f32[48,128]{1,0:T(8,128)S(1)}, u32[]{:S(2)}, u32[]{:S(2)}) collective-permute-start(f32[48,128]{1,0:T(8,128)S(1)} %tile_attention_and_patches.1.patch_ref), channel_id=1, source_target_pairs={{0,8},{8,0},{1,9},{9,1},{2,10},{10,2},{3,11},{11,3},{4,12},{12,4},... | collective-permute-start | bytes 73736 | tf_op jit(solution)/shard_map/ppermute | solution.py:480

commit v5 on v4

--- a/solution.py
+++ b/solution.py
@@ -164,24 +164,28 @@
     )(*pieces, vecs, w_own, w_other)
 
 
-def block_kernel(n_pieces, *refs):
-    stale_refs = refs[:n_pieces]
-    (
-        x_ref, q_ref, kv_ref, got_ref, idx_ref, vec_ref, w_own, w_other, wo_own, wo_other,
-        xt_ref, qt_ref, kv1_ref, send_ref, w_ref, wo_ref, all_ref, pick_ref, sems,
-    ) = refs[n_pieces:]
-    count = x_ref.shape[0]
-    out_copy = copy_out(0, wo_own, wo_other, wo_ref, sems.at[2])
-    in_copies = copy_qkv(1, w_own, w_other, w_ref, sems)
+def gather_keys(all_ref, kv_ref, stale_refs, got_ref):
+    count = kv_ref.shape[0]
     first_core = lax.axis_index("pipe") == 0
-    wo_ref[:SHIFT] = jnp.zeros((SHIFT, D), BF16)
     all_ref[:count] = kv_ref[...]
     at = 0
     for ref in stale_refs:
         rows = ref.shape[0]
         all_ref[count + at : count + at + rows] = jnp.where(first_core, ref[...], got_ref[at : at + rows])
-        send_ref[at : at + rows] = ref[...]
         at += rows
+
+
+def block_kernel(n_pieces, *refs):
+    stale_refs = refs[:n_pieces]
+    (
+        x_ref, q_ref, kv_ref, got_ref, idx_ref, vec_ref, w_own, w_other, wo_own, wo_other,
+        xt_ref, qt_ref, kv1_ref, w_ref, wo_ref, all_ref, pick_ref, sems,
+    ) = refs[n_pieces:]
+    count = x_ref.shape[0]
+    out_copy = copy_out(0, wo_own, wo_other, wo_ref, sems.at[2])
+    in_copies = copy_qkv(1, w_own, w_other, w_ref, sems)
+    wo_ref[:SHIFT] = jnp.zeros((SHIFT, D), BF16)
+    gather_keys(all_ref, kv_ref, stale_refs, got_ref)
     pick_ref[...] = jnp.zeros_like(pick_ref)
     tile_rows = idx_ref.shape[0]
     waits = [out_copy] + in_copies
@@ -200,11 +204,6 @@
         modulated = normed(x1.astype(F32), vec_ref[4:5], vec_ref[3:4])
         fresh = dot_t(modulated, w_ref[DA:]).astype(BF16)
         kv1_ref[rows] = fresh
-
-        @pl.when(first_core)
-        def _():
-            send_ref[rows] = fresh
-
         lane = lax.broadcasted_iota(jnp.int32, (tile_rows, size), 1) + start
         chosen = (lane == idx_ref[:, :1]).astype(F32).astype(BF16)
         pick_ref[0] += dot(chosen, x1)
@@ -224,10 +223,9 @@
             jax.ShapeDtypeStruct((tile_rows, D), BF16),
             jax.ShapeDtypeStruct((tile_rows, DP), BF16),
             jax.ShapeDtypeStruct((count, 2 * DA), BF16),
-            jax.ShapeDtypeStruct((count, 2 * DA), BF16),
         ),
         in_specs=[VMEM] * (len(stale_pieces) + 6) + [ANY] * 4,
-        out_specs=(VMEM,) * 4,
+        out_specs=(VMEM,) * 3,
         scratch_shapes=[
             pltpu.VMEM((3 * DA, D), BF16),
             pltpu.VMEM((DP, D), BF16),
@@ -240,14 +238,15 @@
     )(*stale_pieces, x, q, kv, got, idx, vecs, w_own, w_other, wo_own, wo_other)
 
 
-def tile_kernel(
-    x_ref, q_ref, kv_ref, got_ref, idx_ref, vec_ref, wf_ref, wo_own, wo_other, patch_ref, wo_ref, all_ref, sems
-):
-    count = kv_ref.shape[0]
+def tile_kernel(n_pieces, *refs):
+    stale_refs = refs[:n_pieces]
+    (
+        x_ref, q_ref, kv_ref, got_ref, idx_ref, vec_ref, wf_ref, wo_own, wo_other,
+        patch_ref, wo_ref, all_ref, sems,
+    ) = refs[n_pieces:]
     out_copy = copy_out(1, wo_own, wo_other, wo_ref, sems.at[0])
     wo_ref[:SHIFT] = jnp.zeros((SHIFT, D), BF16)
-    all_ref[:count] = kv_ref[...]
-    all_ref[count:] = got_ref[...]
+    gather_keys(all_ref, kv_ref, stale_refs, got_ref)
     attended = attend(q_ref[...], all_ref).astype(BF16)
     out_copy.wait()
     branch = dot(attended, wo_ref[...])
@@ -258,12 +257,12 @@
     patch_ref[:, : 4 * LATC] = jnp.where(idx_ref[:, :1] >= 0, patches, 0.0)
 
 
-def tile_block(x, q, kv, got, idx, vecs, w_final, wo_own, wo_other):
+def tile_block(stale_pieces, x, q, kv, got, idx, vecs, w_final, wo_own, wo_other):
     count = kv.shape[0]
     return pl.pallas_call(
-        tile_kernel,
+        functools.partial(tile_kernel, len(stale_pieces)),
         out_shape=jax.ShapeDtypeStruct((x.shape[0], LANES), F32),
-        in_specs=[VMEM] * 7 + [ANY] * 2,
+        in_specs=[VMEM] * (len(stale_pieces) + 7) + [ANY] * 2,
         out_specs=VMEM,
         scratch_shapes=[
             pltpu.VMEM((DP, D), BF16),
@@ -272,7 +271,7 @@
         ],
         compiler_params=params(count),
         name="tile_attention_and_patches",
-    )(x, q, kv, got, idx, vecs, w_final, wo_own, wo_other)
+    )(*stale_pieces, x, q, kv, got, idx, vecs, w_final, wo_own, wo_other)
 
 
 def decode_kernel(
@@ -395,12 +394,18 @@
     return lax.ppermute(block, "patch", route)
 
 
-def gather_outer(own, outer):
-    return jnp.concatenate([own] + [shifted(own, k, 0) for k in range(1, outer)], axis=0)
-
-
-def gather_inner(column, inner):
-    return [column] + [shifted(column, 0, k) for k in range(1, inner)]
+def doubled(column, bit):
+    route = [(i ^ bit, i) for i in range(lax.axis_size("patch"))]
+    return [column, lax.ppermute(column, ("pipe", "patch"), route)]
+
+
+def stale_column(own):
+    n = lax.axis_size("patch")
+    outer, inner = split_of(n)
+    bits = [inner << i for i in range(int(math.log2(outer)))] + [1 << i for i in range(1, int(math.log2(inner)))]
+    for bit in bits:
+        own = jnp.concatenate(doubled(own, bit), axis=0)
+    return own
 
 
 def local(
@@ -432,10 +437,16 @@
     own_tokens = lax.dynamic_index_in_dim(tokens, section, 0, keepdims=False)
     w_qkv = jnp.swapaxes(w_qkv, 1, 2)
     w_qkv_other = lax.ppermute(w_qkv, "pipe", swap)
-    x_column = gather_outer(own_tokens, outer)
-    x_column, own_stale = lax.optimization_barrier((x_column, stale_kv[0, 1]))
-    x_pieces = gather_inner(x_column, inner)
-    stale_pieces = gather_inner(gather_outer(own_stale, outer), inner)
+    x_column = [shifted(own_tokens, k, 0) for k in range(1, outer)]
+    x_own_inner = [shifted(own_tokens, 0, k) for k in range(1, inner)]
+    x_own_inner[0], own_stale = lax.optimization_barrier((x_own_inner[0], stale_kv[0, 1]))
+    x_others = jnp.concatenate(x_column, axis=0)
+    x_others, w_in = lax.optimization_barrier((x_others, w_in))
+    x_pieces = [own_tokens, x_others]
+    for k in range(1, inner):
+        x_pieces += [x_own_inner[k - 1], shifted(x_others, 0, k)]
+    later_stale = lax.ppermute(own_stale, "pipe", [(1, 0)])
+    stale = stale_column(own_stale)
     w_out_other = lax.ppermute(w_out, "pipe", swap)
     table_other = lax.ppermute(block_table[0], "pipe", swap)
 
@@ -465,15 +476,18 @@
     idx = jnp.broadcast_to(jnp.where(inside, spot, -1)[:, None], (padded_rows, LANES)).astype(jnp.int32)
 
     w_patch = dot(jnp.asarray(patch_selector(), BF16), w_in).astype(BF16)
-    x_pieces, w_patch, idx = lax.optimization_barrier((x_pieces, w_patch, idx))
+    x_pieces, w_patch, idx, stale = lax.optimization_barrier((x_pieces, w_patch, idx, stale))
+    stale_pieces = doubled(stale, 1)
 
     x, query, fresh = project(x_pieces, vecs, w_qkv, w_qkv_other)
     got = lax.ppermute(fresh, "pipe", [(0, 1)])
-    x_tile, q_tile, fresh, send = first_block(
+    later_stale, x = lax.optimization_barrier((later_stale, x))
+    later_pieces = doubled(stale_column(later_stale), 1)
+    x_tile, q_tile, fresh = first_block(
         stale_pieces, x, query, fresh, got, idx, vecs, w_qkv, w_qkv_other, w_out, w_out_other
     )
-    got = lax.ppermute(send, "pipe", swap)
-    patches = tile_block(x_tile, q_tile, fresh, got, idx, vecs, w_final.T, w_out, w_out_other)
+    got = lax.ppermute(fresh, "pipe", [(0, 1)])
+    patches = tile_block(later_pieces, x_tile, q_tile, fresh, got, idx, vecs, w_final.T, w_out, w_out_other)
     edge = patches
     if rows > 1:
         edge = jnp.where(first_core, patches[(rows - 1) * pitch : rows * pitch], patches[:pitch])

time: 59.7 us -> 72.1 us (1.21)
  starting transfers between devices: 18.6 us -> 31.6 us
  waiting for transfers between devices: 13.9 us -> 16.5 us
  local copies, waits for them, and re-layouts: 7.17 us -> 5.05 us
  other arithmetic: 1.87 us -> 0.94 us
    ppermute x1 -> x7, starting transfers between devices: 0.07 us -> 20.4 us  [the longest x6 19.1 us: doubled(): return [column, lax.ppermute(column, ('pipe', 'patch'), route)]]
    ppermute x1 -> x7, waiting for transfers between devices: 1.99 us -> 15.3 us  [the longest x6 15.3 us: doubled(): return [column, lax.ppermute(column, ('pipe', 'patch'), route)]]
    ppermute x8 -> x5, waiting for transfers between devices: 10.9 us -> 0.01 us  [shifted(): return lax.ppermute(block, 'patch', route)]
    ppermute x8 -> x5, starting transfers between devices: 15.3 us -> 7.72 us  [shifted(): return lax.ppermute(block, 'patch', route)]
    unnamed x22 -> x21, local copies, waits for them, and re-layouts: 4.41 us -> 2.91 us
    concatenate x1 -> x4, other arithmetic: 0.98 us -> 0.07 us  [the longest x3 0.05 us: stale_column(): own = jnp.concatenate(doubled(own, bit), axis=0)]
    ppermute x1 -> x2, starting transfers between devices: 1.97 us -> 2.65 us  [local(): got = lax.ppermute(fresh, 'pipe', [(0, 1)])]
  transfers between devices with their start and end apart: 14 -> 18, of which waited for: 5 -> 6; matrix products, arithmetic and copies ran while one was open for 14% -> 7% of each run, Pallas kernels for 4% -> 10%
where the time goes in v5:
time: 72.1 us; the launch traced here: 71.5 us
  starting transfers between devices  31.6 us (44%)
  waiting for transfers between devices  16.5 us (23%)
  Pallas kernels  15 us (21%)
  local copies, waits for them, and re-layouts  5.05 us (7%)
  matrix products  1.38 us (2%)
  between operations  1 us (1%)
  other arithmetic  0.94 us (1%)
    ppermute x6, starting transfers between devices, doubled(): return [column, lax.ppermute(column, ('pipe', 'patch'), route)]  19.1 us
    ppermute x6, waiting for transfers between devices, doubled(): return [column, lax.ppermute(column, ('pipe', 'patch'), route)]  15.3 us
    ppermute x5, starting transfers between devices, shifted(): return lax.ppermute(block, 'patch', route)  7.72 us
    pallas_call x1, Pallas kernels, first_block(): pl.pallas_call(functools.partial(block_kernel, len(stale_pieces)), out_sh...  5.03 us
    pallas_call x1, Pallas kernels, decode(): pl.pallas_call(functools.partial(decode_kernel, rows, cols, pitch), out_s...  4.31 us
    pallas_call x1, Pallas kernels, tile_block(): pl.pallas_call(functools.partial(tile_kernel, len(stale_pieces)), out_sha...  3.31 us
    unnamed x21, local copies, waits for them, and re-layouts  2.91 us
    ppermute x2, starting transfers between devices, local(): got = lax.ppermute(fresh, 'pipe', [(0, 1)])  2.65 us
  transfers between devices with their start and end apart: 18, of which 6 were waited for; matrix products, arithmetic and copies ran while one was open for 7% of the time, Pallas kernels for 10%

profile of v5, /device:TPU:0, one launch (start us, length us, event | category | flops | bytes accessed | tf_op | source)
XLA Modules:
  0.0 71.5 jit_solution(18287387916189807784)
XLA Ops:
  0.5 1.1 %dynamic-slice_bitcast_fusion.refs_0_ = bf16[32,1152]{1,0:T(8,128)(2,1)S(1)} fusion(bf16[2,32,1152]{2,1,0:T(8,128)(2,1)} %param.14, s32[]{:T(128)S(6)} %select_n.108), kind=kLoop, calls=%fused_computation.7 | loop fusion | bytes 147460 | tf_op jit(solution)/shard_map/jit(dynamic_index_in_dim)/squeeze | solution.py:437
  1.6 2.5 %collective-permute-start = (bf16[32,1152]{1,0:T(8,128)(2,1)S(1)}, bf16[32,1152]{1,0:T(8,128)(2,1)S(1)}, u32[]{:S(2)}, u32[]{:S(2)}) collective-permute-start(bf16[32,1152]{1,0:T(8,128)(2,1)S(1)} %dynamic-slice_bitcast_fusion.refs_0_), channel_id=1, source_target_pairs={{1,0},{0,1},{3,2},{2,3},{5,4},{4,5},{7,6},{6,7},{9,8},{8,9},{11,10... | collective-permute-start | bytes 221192 | tf_op jit(solution)/shard_map/ppermute | solution.py:394
  4.1 3.6 %collective-permute-start.2 = (bf16[32,1152]{1,0:T(8,128)(2,1)S(1)}, bf16[32,1152]{1,0:T(8,128)(2,1)S(1)}, u32[]{:S(2)}, u32[]{:S(2)}) collective-permute-start(bf16[32,1152]{1,0:T(8,128)(2,1)S(1)} %dynamic-slice_bitcast_fusion.refs_0_), channel_id=1, source_target_pairs={{2,0},{3,1},{4,2},{5,3},{6,4},{7,5},{0,6},{1,7},{10,8},{11,9},{12,... | collective-permute-start | bytes 221192 | tf_op jit(solution)/shard_map/ppermute | solution.py:394
  10.1 1.1 %collective-permute-start.4 = (bf16[32,1152]{1,0:T(8,128)(2,1)S(1)}, bf16[32,1152]{1,0:T(8,128)(2,1)S(1)}, u32[]{:S(2)}, u32[]{:S(2)}) collective-permute-start(bf16[32,1152]{1,0:T(8,128)(2,1)S(1)} %dynamic-slice_bitcast_fusion.refs_0_), channel_id=1, source_target_pairs={{6,0},{7,1},{0,2},{1,3},{2,4},{3,5},{4,6},{5,7},{14,8},{15,9},{8,1... | collective-permute-start | bytes 221192 | tf_op jit(solution)/shard_map/ppermute | solution.py:394
  12.3 4.4 %collective-permute-start.6 = (bf16[32,1152]{1,0:T(8,128)(2,1)S(1)}, bf16[32,1152]{1,0:T(8,128)(2,1)S(1)}, u32[]{:S(2)}, u32[]{:S(2)}) collective-permute-start(bf16[32,1152]{1,0:T(8,128)(2,1)S(1)} %slice_bitcast_fusion), channel_id=1, source_target_pairs={{2,0},{3,1},{0,2},{1,3},{6,4},{7,5},{4,6},{5,7},{18,16},{19,17},{1... | collective-permute-start | bytes 221192 | tf_op jit(solution)/shard_map/ppermute | solution.py:399
  17.3 1.7 %collective-permute-done.6 = bf16[32,1152]{1,0:T(8,128)(2,1)S(1)} collective-permute-done((bf16[32,1152]{1,0:T(8,128)(2,1)S(1)}, bf16[32,1152]{1,0:T(8,128)(2,1)S(1)}, u32[]{:S(2)}, u32[]{:S(2)}) %collective-permute-start.6) | collective-permute-done | bytes 73760 | tf_op jit(solution)/shard_map/ppermute | solution.py:399
  19.0 3.7 %collective-permute-start.7 = (bf16[64,1152]{1,0:T(8,128)(2,1)S(1)}, bf16[64,1152]{1,0:T(8,128)(2,1)S(1)}, u32[]{:S(2)}, u32[]{:S(2)}) collective-permute-start(bf16[64,1152]{1,0:T(8,128)(2,1)S(1)} %pad_maximum_fusion.2), channel_id=1, source_target_pairs={{4,0},{5,1},{6,2},{7,3},{0,4},{1,5},{2,6},{3,7},{20,16},{21,17},{2... | collective-permute-start | bytes 442376 | tf_op jit(solution)/shard_map/ppermute | solution.py:399
  22.6 1.4 %fusion.wp_ref = bf16[1024,512]{1,0:T(8,128)(2,1)S(1)} fusion(bf16[36,512]{1,0:T(8,128)(2,1)} %param.22, bf16[1024,36]{1,0:T(8,128)(2,1)} %constant.129.clone), kind=kOutput, calls=%fused_computation.1 | convolution fusion | flops 38273024 | bytes 1159168 | tf_op jit(solution)/shard_map/dot_general | solution.py:34
  24.0 4.5 %collective-permute-done.7 = bf16[64,1152]{1,0:T(8,128)(2,1)S(1)} collective-permute-done((bf16[64,1152]{1,0:T(8,128)(2,1)S(1)}, bf16[64,1152]{1,0:T(8,128)(2,1)S(1)}, u32[]{:S(2)}, u32[]{:S(2)}) %collective-permute-start.7) | collective-permute-done | bytes 147488 | tf_op jit(solution)/shard_map/ppermute | solution.py:399
  28.6 2.1 %copy-done.1 = bf16[1,1152,1728]{1,2,0:T(8,128)(2,1)S(1)} copy-done((bf16[1,1152,1728]{1,2,0:T(8,128)(2,1)S(1)}, bf16[1,1152,1728]{1,2,0:T(8,128)(2,1)}, u32[]{:S(2)}) %copy-start.1) | copy-done | bytes 3981336
  30.7 2.4 %layer_norm_and_projections.1 = (bf16[256,1152]{1,0:T(8,128)(2,1)S(1)}, bf16[256,640]{1,0:T(8,128)(2,1)S(1)}, bf16[256,1152]{1,0:T(8,128)(2,1)S(1)}) custom-call(bf16[32,1152]{1,0:T(8,128)(2,1)S(1)} %dynamic-slice_bitcast_fusion.refs_0_, bf16[96,1152]{1,0:T(8,128)(2,1)S(1)} %pad_maximum_fusion.1.refs_1_, bf16[32,1152]{1,0:T(8,128)(2,1)S(1)} %collective-permute-done.refs_2_, ...), custom_call_target="tpu_custom_call" | custom-call | tf_op jit(solution)/shard_map/layer_norm_and_projections/pallas_call | solution.py:149
  33.1 1.3 %collective-permute-start.14 = (bf16[256,1152]{1,0:T(8,128)(2,1)S(1)}, bf16[256,1152]{1,0:T(8,128)(2,1)S(1)}, u32[]{:S(2)}, u32[]{:S(2)}) collective-permute-start(bf16[256,1152]{1,0:T(8,128)(2,1)S(1)} %get-tuple-element.37.refs_4_), channel_id=1, source_target_pairs={{0,8},{1,9},{2,10},{3,11},{4,12},{5,13},{6,14},{7,15},{16,24},{17,... | collective-permute-start | bytes 1769480 | tf_op jit(solution)/shard_map/ppermute | solution.py:483
  34.5 1.3 %collective-permute-start.1 = (bf16[32,1152]{1,0:T(8,128)(2,1)S(1)}, bf16[32,1152]{1,0:T(8,128)(2,1)S(1)}, u32[]{:S(2)}, u32[]{:S(2)}) collective-permute-start(bf16[32,1152]{1,0:T(8,128)(2,1)S(1)} %slice_bitcast_fusion), channel_id=1, source_target_pairs={{8,0},{9,1},{10,2},{11,3},{12,4},{13,5},{14,6},{15,7},{24,16},{25,... | collective-permute-start | bytes 221192 | tf_op jit(solution)/shard_map/ppermute | solution.py:448
  35.8 2.4 %collective-permute-start.13 = (bf16[128,1152]{1,0:T(8,128)(2,1)S(1)}, bf16[128,1152]{1,0:T(8,128)(2,1)S(1)}, u32[]{:S(2)}, u32[]{:S(2)}) collective-permute-start(bf16[128,1152]{1,0:T(8,128)(2,1)S(1)} %pad_maximum_fusion.refs_0_), channel_id=1, source_target_pairs={{1,0},{0,1},{3,2},{2,3},{5,4},{4,5},{7,6},{6,7},{17,16},{16,17},{1... | collective-permute-start | bytes 884744 | tf_op jit(solution)/shard_map/ppermute | solution.py:399
  38.2 2.4 %collective-permute-start.10 = (bf16[32,1152]{1,0:T(8,128)(2,1)S(1)}, bf16[32,1152]{1,0:T(8,128)(2,1)S(1)}, u32[]{:S(2)}, u32[]{:S(2)}) collective-permute-start(bf16[32,1152]{1,0:T(8,128)(2,1)S(1)} %collective-permute-done.1), channel_id=1, source_target_pairs={{2,0},{3,1},{0,2},{1,3},{6,4},{7,5},{4,6},{5,7},{18,16},{19,17},{1... | collective-permute-start | bytes 221192 | tf_op jit(solution)/shard_map/ppermute | solution.py:399
  40.7 3.8 %collective-permute-done.10 = bf16[32,1152]{1,0:T(8,128)(2,1)S(1)} collective-permute-done((bf16[32,1152]{1,0:T(8,128)(2,1)S(1)}, bf16[32,1152]{1,0:T(8,128)(2,1)S(1)}, u32[]{:S(2)}, u32[]{:S(2)}) %collective-permute-start.10) | collective-permute-done | bytes 73760 | tf_op jit(solution)/shard_map/ppermute | solution.py:399
  44.5 2.8 %collective-permute-start.11 = (bf16[64,1152]{1,0:T(8,128)(2,1)S(1)}, bf16[64,1152]{1,0:T(8,128)(2,1)S(1)}, u32[]{:S(2)}, u32[]{:S(2)}) collective-permute-start(bf16[64,1152]{1,0:T(8,128)(2,1)S(1)} %pad_maximum_fusion.3), channel_id=1, source_target_pairs={{4,0},{5,1},{6,2},{7,3},{0,4},{1,5},{2,6},{3,7},{20,16},{21,17},{2... | collective-permute-start | bytes 442376 | tf_op jit(solution)/shard_map/ppermute | solution.py:399
  47.4 5.0 %attention_and_next_keys.1 = (bf16[48,1152]{1,0:T(8,128)(2,1)S(1)}, bf16[48,640]{1,0:T(8,128)(2,1)S(1)}, bf16[256,1152]{1,0:T(8,128)(2,1)S(1)}) custom-call(bf16[128,1152]{1,0:T(8,128)(2,1)S(1)} %pad_maximum_fusion.refs_0_, bf16[128,1152]{1,0:T(8,128)(2,1)S(1)} %collective-permute-done.13.refs_1_, bf16[256,1152]{1,0:T(8,128)(2,1)S(1)} %get-tuple-element.35.refs_2_, ...), custom_call_target="tpu_custom_call" | custom-call | tf_op jit(solution)/shard_map/attention_and_next_keys/pallas_call | solution.py:220
  52.4 1.3 %collective-permute-start.16 = (bf16[256,1152]{1,0:T(8,128)(2,1)S(1)}, bf16[256,1152]{1,0:T(8,128)(2,1)S(1)}, u32[]{:S(2)}, u32[]{:S(2)}) collective-permute-start(bf16[256,1152]{1,0:T(8,128)(2,1)S(1)} %get-tuple-element.41.refs_4_), channel_id=1, source_target_pairs={{0,8},{1,9},{2,10},{3,11},{4,12},{5,13},{6,14},{7,15},{16,24},{17,... | collective-permute-start | bytes 1769480 | tf_op jit(solution)/shard_map/ppermute | solution.py:489
  54.0 3.4 %collective-permute-start.12 = (bf16[128,1152]{1,0:T(8,128)(2,1)S(1)}, bf16[128,1152]{1,0:T(8,128)(2,1)S(1)}, u32[]{:S(2)}, u32[]{:S(2)}) collective-permute-start(bf16[128,1152]{1,0:T(8,128)(2,1)S(1)} %constant_dynamic-update-slice_fusion.refs_0_), channel_id=1, source_target_pairs={{1,0},{0,1},{3,2},{2,3},{5,4},{4,5},{7,6},{6,7},{17,16},{16,17},{1... | collective-permute-start | bytes 884744 | tf_op jit(solution)/shard_map/ppermute | solution.py:399
  57.4 5.2 %collective-permute-done.12.refs_1_ = bf16[128,1152]{1,0:T(8,128)(2,1)S(1)} collective-permute-done((bf16[128,1152]{1,0:T(8,128)(2,1)S(1)}, bf16[128,1152]{1,0:T(8,128)(2,1)S(1)}, u32[]{:S(2)}, u32[]{:S(2)}) %collective-permute-start.12) | collective-permute-done | bytes 294944 | tf_op jit(solution)/shard_map/ppermute | solution.py:399
  62.6 3.3 %tile_attention_and_patches.1.patch_ref = f32[48,128]{1,0:T(8,128)S(1)} custom-call(bf16[128,1152]{1,0:T(8,128)(2,1)S(1)} %constant_dynamic-update-slice_fusion.refs_0_, bf16[128,1152]{1,0:T(8,128)(2,1)S(1)} %collective-permute-done.12.refs_1_, bf16[48,1152]{1,0:T(8,128)(2,1)S(1)} %get-tuple-element.39.refs_2_, ...), custom_call_target="tpu_custom_call" | custom-call | tf_op jit(solution)/shard_map/tile_attention_and_patches/pallas_call | solution.py:262
  66.0 1.2 %collective-permute-done.17.got_ref = f32[48,128]{1,0:T(8,128)S(1)} collective-permute-done((f32[48,128]{1,0:T(8,128)S(1)}, f32[48,128]{1,0:T(8,128)S(1)}, u32[]{:S(2)}, u32[]{:S(2)}) %collective-permute-start.17) | collective-permute-done | bytes 24608 | tf_op jit(solution)/shard_map/ppermute | solution.py:494
  67.2 4.3 %decoder_convolutions.1 = bf16[4,128,512]{2,1,0:T(8,128)(2,1)} custom-call(f32[48,128]{1,0:T(8,128)S(1)} %tile_attention_and_patches.1.patch_ref, f32[48,128]{1,0:T(8,128)S(1)} %collective-permute-done.17.got_ref, s32[48,128]{1,0:T(8,128)S(1)} %broadcast_in_dim.14.refs_6_.idx_ref, bf16[1024,512]{1,0:T(8,128)(2,1)S(1)} %fusion.wp_ref, f32[1,512]{1,0:T(1,128)S(1)} %bitcast.43, ...), custom_call_target="tpu_custom_call" | custom-call | tf_op jit(solution)/shard_map/decoder_convolutions/pallas_call | solution.py:353
  (53 shorter events, 4.4 us)
Async XLA Ops:
  0.0 28.6 %collective-permute-start.9 = (bf16[1,1728,1152]{2,1,0:T(8,128)(2,1)}, bf16[1,1728,1152]{2,1,0:T(8,128)(2,1)}, u32[]{:S(2)}, u32[]{:S(2)}) collective-permute-start(bf16[1,1728,1152]{2,1,0:T(8,128)(2,1)} %bitcast.37), channel_id=1, source_target_pairs={{0,8},{8,0},{1,9},{9,1},{2,10},{10,2},{3,11},{11,3},{4,12},{12,4},... | collective-permute-start | bytes 11943944 | tf_op jit(solution)/shard_map/ppermute | solution.py:439
  1.6 10.4 %collective-permute-start = (bf16[32,1152]{1,0:T(8,128)(2,1)S(1)}, bf16[32,1152]{1,0:T(8,128)(2,1)S(1)}, u32[]{:S(2)}, u32[]{:S(2)}) collective-permute-start(bf16[32,1152]{1,0:T(8,128)(2,1)S(1)} %dynamic-slice_bitcast_fusion.refs_0_), channel_id=1, source_target_pairs={{1,0},{0,1},{3,2},{2,3},{5,4},{4,5},{7,6},{6,7},{9,8},{8,9},{11,10... | collective-permute-start | bytes 221192 | tf_op jit(solution)/shard_map/ppermute | solution.py:394
  4.1 8.2 %collective-permute-start.2 = (bf16[32,1152]{1,0:T(8,128)(2,1)S(1)}, bf16[32,1152]{1,0:T(8,128)(2,1)S(1)}, u32[]{:S(2)}, u32[]{:S(2)}) collective-permute-start(bf16[32,1152]{1,0:T(8,128)(2,1)S(1)} %dynamic-slice_bitcast_fusion.refs_0_), channel_id=1, source_target_pairs={{2,0},{3,1},{4,2},{5,3},{6,4},{7,5},{0,6},{1,7},{10,8},{11,9},{12,... | collective-permute-start | bytes 221192 | tf_op jit(solution)/shard_map/ppermute | solution.py:394
  7.7 9.0 %collective-permute-start.3 = (bf16[32,1152]{1,0:T(8,128)(2,1)S(1)}, bf16[32,1152]{1,0:T(8,128)(2,1)S(1)}, u32[]{:S(2)}, u32[]{:S(2)}) collective-permute-start(bf16[32,1152]{1,0:T(8,128)(2,1)S(1)} %dynamic-slice_bitcast_fusion.refs_0_), channel_id=1, source_target_pairs={{4,0},{5,1},{6,2},{7,3},{0,4},{1,5},{2,6},{3,7},{12,8},{13,9},{14,... | collective-permute-start | bytes 221192 | tf_op jit(solution)/shard_map/ppermute | solution.py:394
  8.4 1.7 %collective-permute-start.8 = (f32[3,1152]{1,0:T(4,128)S(1)}, f32[3,1152]{1,0:T(4,128)S(1)}, u32[]{:S(2)}, u32[]{:S(2)}) collective-permute-start(f32[3,1152]{1,0:T(4,128)S(1)} %bitcast.45), channel_id=1, source_target_pairs={{0,8},{8,0},{1,9},{9,1},{2,10},{10,2},{3,11},{11,3},{4,12},{12,4},... | collective-permute-start | bytes 41480 | tf_op jit(solution)/shard_map/ppermute | solution.py:451
  10.1 6.6 %collective-permute-start.4 = (bf16[32,1152]{1,0:T(8,128)(2,1)S(1)}, bf16[32,1152]{1,0:T(8,128)(2,1)S(1)}, u32[]{:S(2)}, u32[]{:S(2)}) collective-permute-start(bf16[32,1152]{1,0:T(8,128)(2,1)S(1)} %dynamic-slice_bitcast_fusion.refs_0_), channel_id=1, source_target_pairs={{6,0},{7,1},{0,2},{1,3},{2,4},{3,5},{4,6},{5,7},{14,8},{15,9},{8,1... | collective-permute-start | bytes 221192 | tf_op jit(solution)/shard_map/ppermute | solution.py:394
  12.0 35.3 %collective-permute-start.15 = (bf16[1,576,1152]{2,1,0:T(8,128)(2,1)}, bf16[1,576,1152]{2,1,0:T(8,128)(2,1)S(1)}, u32[]{:S(2)}, u32[]{:S(2)}) collective-permute-start(bf16[1,576,1152]{2,1,0:T(8,128)(2,1)} %refs_9_.1), channel_id=1, source_target_pairs={{0,8},{8,0},{1,9},{9,1},{2,10},{10,2},{3,11},{11,3},{4,12},{12,4},... | collective-permute-start | bytes 3981320 | tf_op jit(solution)/shard_map/ppermute | solution.py:450
  12.3 6.7 %collective-permute-start.6 = (bf16[32,1152]{1,0:T(8,128)(2,1)S(1)}, bf16[32,1152]{1,0:T(8,128)(2,1)S(1)}, u32[]{:S(2)}, u32[]{:S(2)}) collective-permute-start(bf16[32,1152]{1,0:T(8,128)(2,1)S(1)} %slice_bitcast_fusion), channel_id=1, source_target_pairs={{2,0},{3,1},{0,2},{1,3},{6,4},{7,5},{4,6},{5,7},{18,16},{19,17},{1... | collective-permute-start | bytes 221192 | tf_op jit(solution)/shard_map/ppermute | solution.py:399
  16.7 11.8 %collective-permute-start.5 = (bf16[96,1152]{1,0:T(8,128)(2,1)S(1)}, bf16[96,1152]{1,0:T(8,128)(2,1)S(1)}, u32[]{:S(2)}, u32[]{:S(2)}) collective-permute-start(bf16[96,1152]{1,0:T(8,128)(2,1)S(1)} %pad_maximum_fusion.1.refs_1_), channel_id=1, source_target_pairs={{1,0},{0,1},{3,2},{2,3},{5,4},{4,5},{7,6},{6,7},{9,8},{8,9},{11,10... | collective-permute-start | bytes 663560 | tf_op jit(solution)/shard_map/ppermute | solution.py:394
  19.0 9.5 %collective-permute-start.7 = (bf16[64,1152]{1,0:T(8,128)(2,1)S(1)}, bf16[64,1152]{1,0:T(8,128)(2,1)S(1)}, u32[]{:S(2)}, u32[]{:S(2)}) collective-permute-start(bf16[64,1152]{1,0:T(8,128)(2,1)S(1)} %pad_maximum_fusion.2), channel_id=1, source_target_pairs={{4,0},{5,1},{6,2},{7,3},{0,4},{1,5},{2,6},{3,7},{20,16},{21,17},{2... | collective-permute-start | bytes 442376 | tf_op jit(solution)/shard_map/ppermute | solution.py:399
  30.7 16.6 %copy-start.2 = (bf16[1,1152,1728]{1,2,0:T(8,128)(2,1)S(1)}, bf16[1,1152,1728]{1,2,0:T(8,128)(2,1)}, u32[]{:S(2)}) copy-start(bf16[1,1152,1728]{1,2,0:T(8,128)(2,1)} %param.16) | copy-start | bytes 11943940
  30.7 16.6 %copy-start.3 = (bf16[1,576,1152]{2,1,0:T(8,128)(2,1)S(1)}, bf16[1,576,1152]{2,1,0:T(8,128)(2,1)}, u32[]{:S(2)}) copy-start(bf16[1,576,1152]{2,1,0:T(8,128)(2,1)} %refs_9_.1) | copy-start | bytes 3981316
  33.1 14.2 %collective-permute-start.14 = (bf16[256,1152]{1,0:T(8,128)(2,1)S(1)}, bf16[256,1152]{1,0:T(8,128)(2,1)S(1)}, u32[]{:S(2)}, u32[]{:S(2)}) collective-permute-start(bf16[256,1152]{1,0:T(8,128)(2,1)S(1)} %get-tuple-element.37.refs_4_), channel_id=1, source_target_pairs={{0,8},{1,9},{2,10},{3,11},{4,12},{5,13},{6,14},{7,15},{16,24},{17,... | collective-permute-start | bytes 1769480 | tf_op jit(solution)/shard_map/ppermute | solution.py:483
  34.5 3.7 %collective-permute-start.1 = (bf16[32,1152]{1,0:T(8,128)(2,1)S(1)}, bf16[32,1152]{1,0:T(8,128)(2,1)S(1)}, u32[]{:S(2)}, u32[]{:S(2)}) collective-permute-start(bf16[32,1152]{1,0:T(8,128)(2,1)S(1)} %slice_bitcast_fusion), channel_id=1, source_target_pairs={{8,0},{9,1},{10,2},{11,3},{12,4},{13,5},{14,6},{15,7},{24,16},{25,... | collective-permute-start | bytes 221192 | tf_op jit(solution)/shard_map/ppermute | solution.py:448
  35.8 11.5 %collective-permute-start.13 = (bf16[128,1152]{1,0:T(8,128)(2,1)S(1)}, bf16[128,1152]{1,0:T(8,128)(2,1)S(1)}, u32[]{:S(2)}, u32[]{:S(2)}) collective-permute-start(bf16[128,1152]{1,0:T(8,128)(2,1)S(1)} %pad_maximum_fusion.refs_0_), channel_id=1, source_target_pairs={{1,0},{0,1},{3,2},{2,3},{5,4},{4,5},{7,6},{6,7},{17,16},{16,17},{1... | collective-permute-start | bytes 884744 | tf_op jit(solution)/shard_map/ppermute | solution.py:399
  38.2 6.2 %collective-permute-start.10 = (bf16[32,1152]{1,0:T(8,128)(2,1)S(1)}, bf16[32,1152]{1,0:T(8,128)(2,1)S(1)}, u32[]{:S(2)}, u32[]{:S(2)}) collective-permute-start(bf16[32,1152]{1,0:T(8,128)(2,1)S(1)} %collective-permute-done.1), channel_id=1, source_target_pairs={{2,0},{3,1},{0,2},{1,3},{6,4},{7,5},{4,6},{5,7},{18,16},{19,17},{1... | collective-permute-start | bytes 221192 | tf_op jit(solution)/shard_map/ppermute | solution.py:399
  44.5 9.5 %collective-permute-start.11 = (bf16[64,1152]{1,0:T(8,128)(2,1)S(1)}, bf16[64,1152]{1,0:T(8,128)(2,1)S(1)}, u32[]{:S(2)}, u32[]{:S(2)}) collective-permute-start(bf16[64,1152]{1,0:T(8,128)(2,1)S(1)} %pad_maximum_fusion.3), channel_id=1, source_target_pairs={{4,0},{5,1},{6,2},{7,3},{0,4},{1,5},{2,6},{3,7},{20,16},{21,17},{2... | collective-permute-start | bytes 442376 | tf_op jit(solution)/shard_map/ppermute | solution.py:399
  47.3 19.9 %slice-start = ((s8[4718592]{0:T(1024)(128)(4,1)}), s8[4194304]{0:T(1024)(128)(4,1)S(1)}, s32[]{:S(2)}) async-start(s8[4718592]{0:T(1024)(128)(4,1)} %bitcast.40), calls=%async_computation | async-start | bytes 8388608
  47.3 15.3 %copy-start.4 = (bf16[1152,16]{0,1:T(8,128)(2,1)S(1)}, bf16[1152,16]{0,1:T(8,128)(2,1)}, u32[]{:S(2)}) copy-start(bf16[1152,16]{0,1:T(8,128)(2,1)} %param.21) | copy-start | bytes 110596
  47.4 19.8 %slice-start.1 = ((s8[4718592]{0:T(1024)(128)(4,1)}), s8[524288]{0:T(1024)(128)(4,1)S(1)}, s32[]{:S(2)}) async-start(s8[4718592]{0:T(1024)(128)(4,1)} %bitcast.40), calls=%async_computation.1 | async-start | bytes 1048576
  52.4 10.2 %collective-permute-start.16 = (bf16[256,1152]{1,0:T(8,128)(2,1)S(1)}, bf16[256,1152]{1,0:T(8,128)(2,1)S(1)}, u32[]{:S(2)}, u32[]{:S(2)}) collective-permute-start(bf16[256,1152]{1,0:T(8,128)(2,1)S(1)} %get-tuple-element.41.refs_4_), channel_id=1, source_target_pairs={{0,8},{1,9},{2,10},{3,11},{4,12},{5,13},{6,14},{7,15},{16,24},{17,... | collective-permute-start | bytes 1769480 | tf_op jit(solution)/shard_map/ppermute | solution.py:489
  54.0 13.2 %copy-start.5 = (f32[512]{0:T(512)S(1)}, f32[512]{0:T(512)}, u32[]{:S(2)}) copy-start(f32[512]{0:T(512)} %param.23) | copy-start | bytes 6148
  54.0 8.6 %collective-permute-start.12 = (bf16[128,1152]{1,0:T(8,128)(2,1)S(1)}, bf16[128,1152]{1,0:T(8,128)(2,1)S(1)}, u32[]{:S(2)}, u32[]{:S(2)}) collective-permute-start(bf16[128,1152]{1,0:T(8,128)(2,1)S(1)} %constant_dynamic-update-slice_fusion.refs_0_), channel_id=1, source_target_pairs={{1,0},{0,1},{3,2},{2,3},{5,4},{4,5},{7,6},{6,7},{17,16},{16,17},{1... | collective-permute-start | bytes 884744 | tf_op jit(solution)/shard_map/ppermute | solution.py:399
  65.9 1.3 %collective-permute-start.17 = (f32[48,128]{1,0:T(8,128)S(1)}, f32[48,128]{1,0:T(8,128)S(1)}, u32[]{:S(2)}, u32[]{:S(2)}) collective-permute-start(f32[48,128]{1,0:T(8,128)S(1)} %tile_attention_and_patches.1.patch_ref), channel_id=1, source_target_pairs={{0,8},{8,0},{1,9},{9,1},{2,10},{10,2},{3,11},{11,3},{4,12},{12,4},... | collective-permute-start | bytes 73736 | tf_op jit(solution)/shard_map/ppermute | solution.py:494
  (3 other events, 24.4 us)

commit v6 on v4

--- a/solution.py
+++ b/solution.py
@@ -380,27 +380,10 @@
     return np.pad(sel, ((0, 0), (0, 2 * LANES - 9 * 4 * LATC), (0, 0))).reshape(-1, 9 * LATC)
 
 
-def split_of(n):
-    inner = 2 ** (int(math.log2(n)) // 2)
-    return n // inner, inner
-
-
-def shifted(block, k_outer, k_inner):
+def gather_patch(own):
     n = lax.axis_size("patch")
-    outer, inner = split_of(n)
-    route = []
-    for i in range(n):
-        o, e = divmod(i, inner)
-        route.append(((o + k_outer) % outer * inner + (e + k_inner) % inner, i))
-    return lax.ppermute(block, "patch", route)
-
-
-def gather_outer(own, outer):
-    return jnp.concatenate([own] + [shifted(own, k, 0) for k in range(1, outer)], axis=0)
-
-
-def gather_inner(column, inner):
-    return [column] + [shifted(column, 0, k) for k in range(1, inner)]
+    pieces = lax.all_to_all(jnp.broadcast_to(own[None], (n,) + own.shape), "patch", 0, 0, tiled=True)
+    return [pieces.reshape(n * own.shape[0], own.shape[1])]
 
 
 def local(
@@ -427,15 +410,12 @@
     rows = count // TC
     cols = TC // n_tiles
     pitch = -(-(cols + 3) // 8) * 8
-    outer, inner = split_of(n_tiles)
 
     own_tokens = lax.dynamic_index_in_dim(tokens, section, 0, keepdims=False)
     w_qkv = jnp.swapaxes(w_qkv, 1, 2)
     w_qkv_other = lax.ppermute(w_qkv, "pipe", swap)
-    x_column = gather_outer(own_tokens, outer)
-    x_column, own_stale = lax.optimization_barrier((x_column, stale_kv[0, 1]))
-    x_pieces = gather_inner(x_column, inner)
-    stale_pieces = gather_inner(gather_outer(own_stale, outer), inner)
+    x_pieces = gather_patch(own_tokens)
+    stale_pieces = gather_patch(stale_kv[0, 1])
     w_out_other = lax.ppermute(w_out, "pipe", swap)
     table_other = lax.ppermute(block_table[0], "pipe", swap)
 
@@ -458,11 +438,7 @@
     column = place % pitch - 1 + tile * cols
     inside = (place % pitch < cols + 2) & (place < rows * pitch) & (column >= 0) & (column < TC)
     token = place // pitch * TC + jnp.clip(column, 0, TC - 1)
-    source = token // own_count
-    k_outer = (source // inner - tile // inner) % outer
-    k_inner = (source % inner - tile % inner) % inner
-    spot = (k_inner * outer + k_outer) * own_count + token % own_count
-    idx = jnp.broadcast_to(jnp.where(inside, spot, -1)[:, None], (padded_rows, LANES)).astype(jnp.int32)
+    idx = jnp.broadcast_to(jnp.where(inside, token, -1)[:, None], (padded_rows, LANES)).astype(jnp.int32)
 
     w_patch = dot(jnp.asarray(patch_selector(), BF16), w_in).astype(BF16)
     x_pieces, w_patch, idx = lax.optimization_barrier((x_pieces, w_patch, idx))

time: 59.7 us -> 73 us (1.22)
  waiting for transfers between devices: 13.9 us -> 21.9 us
  local copies, waits for them, and re-layouts: 7.17 us -> 14.3 us
  starting transfers between devices: 18.6 us -> 14.6 us
  Pallas kernels: 15.5 us -> 18 us
  other arithmetic: 1.87 us -> 0.12 us
  matrix products: 1.36 us -> 2.37 us
    all_to_all x0 -> x2, waiting for transfers between devices: none -> 18.8 us  [gather_patch(): lax.all_to_all(jnp.broadcast_to(own[None], (n,) + own.shape), 'patch', 0,...]
    ppermute x8 -> x0, starting transfers between devices: 15.3 us -> none  [shifted(): return lax.ppermute(block, 'patch', route)]
    all_to_all x0 -> x2, starting transfers between devices: none -> 11.5 us  [gather_patch(): lax.all_to_all(jnp.broadcast_to(own[None], (n,) + own.shape), 'patch', 0,...]
    ppermute x8 -> x0, waiting for transfers between devices: 10.9 us -> none  [shifted(): return lax.ppermute(block, 'patch', route)]
    unnamed x22 -> x37, local copies, waits for them, and re-layouts: 4.41 us -> 10.9 us
    broadcast_in_dim x1 -> x5, local copies, waits for them, and re-layouts: 0.07 us -> 3.37 us  [the longest x4 2.69 us: gather_patch(): jnp.broadcast_to(own[None], (n,) + own.shape)]
    squeeze x2 -> x0, local copies, waits for them, and re-layouts: 2.64 us -> none  [the longest x1 1.53 us: local(): x_column, own_stale = lax.optimization_barrier((x_column, stale_kv[0, 1]))]
    pallas_call x1, Pallas kernels: 5.48 us -> 6.83 us  [first_block(): pl.pallas_call(functools.partial(block_kernel, len(stale_pieces)), out_sh...]
  transfers between devices with their start and end apart: 14 -> 8, of which waited for: 5 -> 4; matrix products, arithmetic and copies ran while one was open for 14% -> 9% of each run, Pallas kernels for 4% -> 4%
where the time goes in v6:
time: 73 us; the launch traced here: 72.3 us
  waiting for transfers between devices  21.9 us (30%)
  Pallas kernels  18 us (25%)
  starting transfers between devices  14.6 us (20%)
  local copies, waits for them, and re-layouts  14.3 us (20%)
  matrix products  2.37 us (3%)
  between operations  0.88 us (1%)
    all_to_all x2, waiting for transfers between devices, gather_patch(): lax.all_to_all(jnp.broadcast_to(own[None], (n,) + own.shape), 'patch', 0,...  18.8 us
    all_to_all x2, starting transfers between devices, gather_patch(): lax.all_to_all(jnp.broadcast_to(own[None], (n,) + own.shape), 'patch', 0,...  11.5 us
    unnamed x37, local copies, waits for them, and re-layouts  10.9 us
    pallas_call x1, Pallas kernels, first_block(): pl.pallas_call(functools.partial(block_kernel, len(stale_pieces)), out_sh...  6.83 us
    pallas_call x1, Pallas kernels, decode(): pl.pallas_call(functools.partial(decode_kernel, rows, cols, pitch), out_s...  4.32 us
    pallas_call x1, Pallas kernels, tile_block(): pl.pallas_call(tile_kernel, out_shape=jax.ShapeDtypeStruct((x.shape[0], L...  4.09 us
    pallas_call x1, Pallas kernels, project(): pl.pallas_call(functools.partial(project_kernel, len(pieces)), out_shape=...  2.78 us
    broadcast_in_dim x4, local copies, waits for them, and re-layouts, gather_patch(): jnp.broadcast_to(own[None], (n,) + own.shape)  2.69 us
  transfers between devices with their start and end apart: 8, of which 4 were waited for; matrix products, arithmetic and copies ran while one was open for 9% of the time, Pallas kernels for 4%

profile of v6, /device:TPU:0, one launch (start us, length us, event | category | flops | bytes accessed | tf_op | source)
XLA Modules:
  0.0 72.3 jit_solution(2174809098086566664)
XLA Ops:
  0.5 0.9 %copy.37 = f32[1,3,1152]{2,1,0:T(4,128)S(1)} copy(f32[1,3,1152]{2,0,1:T(1,128)} %param.18) | data formatting | bytes 27648
  1.4 0.9 %dynamic-slice_bitcast_fusion = bf16[32,1152]{1,0:T(8,128)(2,1)S(1)} fusion(bf16[2,32,1152]{2,1,0:T(8,128)(2,1)} %param.14, s32[]{:T(128)S(6)} %select_n.52), kind=kLoop, calls=%fused_computation.1 | loop fusion | bytes 147460 | tf_op jit(solution)/shard_map/broadcast_in_dim | solution.py:385
  2.3 0.9 %broadcast_in_dim.32 = bf16[8,32,1152]{2,1,0:T(8,128)(2,1)} broadcast(bf16[32,1152]{1,0:T(8,128)(2,1)S(1)} %dynamic-slice_bitcast_fusion), dimensions={1,2} | broadcast | bytes 663552 | tf_op jit(solution)/shard_map/broadcast_in_dim | solution.py:385
  3.2 7.3 %all-to-all-start.1 = ((bf16[8,32,1152]{2,1,0:T(8,128)(2,1)}), bf16[8,32,1152]{2,1,0:T(8,128)(2,1)S(1)}, u32[]{:S(2)}, u32[]{:S(2)}) async-start(bf16[8,32,1152]{2,1,0:T(8,128)(2,1)} %broadcast_in_dim.32), calls=%async_computation.1 | async-start | bytes 1179648 | tf_op jit(solution)/shard_map/all_to_all | solution.py:385
  11.2 2.4 %convolution_convert_fusion.wp_ref = bf16[1024,512]{1,0:T(8,128)(2,1)} fusion(bf16[1024,36]{1,0:T(8,128)(2,1)} %constant.61.clone, bf16[36,512]{1,0:T(8,128)(2,1)} %param.22), kind=kOutput, calls=%fused_computation | convolution fusion | flops 38273024 | bytes 1159168 | tf_op jit(solution)/shard_map/dot_general | solution.py:34
  13.7 13.0 %all-to-all-done.1 = bf16[8,32,1152]{2,1,0:T(8,128)(2,1)S(1)} async-done(((bf16[8,32,1152]{2,1,0:T(8,128)(2,1)}), bf16[8,32,1152]{2,1,0:T(8,128)(2,1)S(1)}, u32[]{:S(2)}, u32[]{:S(2)}) %all-to-all-start.1) | async-done | bytes 589856 | tf_op jit(solution)/shard_map/all_to_all | solution.py:385
  26.6 0.9 %broadcast_in_dim.30 = bf16[8,32,1152]{2,1,0:T(8,128)(2,1)} broadcast(bf16[32,1152]{1,0:T(8,128)(2,1)S(1)} %slice_bitcast_fusion), dimensions={1,2} | broadcast | bytes 663552 | tf_op jit(solution)/shard_map/broadcast_in_dim | solution.py:385
  27.6 4.2 %all-to-all-start = ((bf16[8,32,1152]{2,1,0:T(8,128)(2,1)}), bf16[8,32,1152]{2,1,0:T(8,128)(2,1)}, u32[]{:S(2)}, u32[]{:S(2)}) async-start(bf16[8,32,1152]{2,1,0:T(8,128)(2,1)} %broadcast_in_dim.30), calls=%async_computation | async-start | bytes 1179648 | tf_op jit(solution)/shard_map/all_to_all | solution.py:385
  32.6 2.1 %copy-done.1 = bf16[1,1152,1728]{1,2,0:T(8,128)(2,1)S(1)} copy-done((bf16[1,1152,1728]{1,2,0:T(8,128)(2,1)S(1)}, bf16[1,1152,1728]{1,2,0:T(8,128)(2,1)}, u32[]{:S(2)}) %copy-start.1) | copy-done | bytes 3981336
  34.7 2.8 %layer_norm_and_projections.1 = (bf16[256,1152]{1,0:T(8,128)(2,1)S(1)}, bf16[256,640]{1,0:T(8,128)(2,1)S(1)}, bf16[256,1152]{1,0:T(8,128)(2,1)}) custom-call(bf16[256,1152]{1,0:T(8,128)(2,1)S(1)} %bitcast.42, f32[8,1152]{1,0:T(8,128)S(1)} %pad_maximum_fusion.refs_1_.refs_6_.vec_ref, bf16[1,1728,1152]{2,1,0:T(8,128)(2,1)S(1)} %bitcast.38, ...), custom_call_target="tpu_custom_call" | custom-call | tf_op jit(solution)/shard_map/layer_norm_and_projections/pallas_call | solution.py:149
  37.5 0.9 %copy-done.5 = bf16[256,1152]{1,0:T(8,128)(2,1)} copy-done((bf16[256,1152]{1,0:T(8,128)(2,1)}, bf16[256,1152]{1,0:T(8,128)(2,1)S(1)}, u32[]{:S(2)}) %copy-start.5) | copy-done | bytes 589848
  38.4 0.7 copy-done.8
  39.1 2.5 %collective-permute-start.2 = (bf16[256,1152]{1,0:T(8,128)(2,1)}, bf16[256,1152]{1,0:T(8,128)(2,1)S(1)}, u32[]{:S(2)}, u32[]{:S(2)}) collective-permute-start(bf16[256,1152]{1,0:T(8,128)(2,1)} %get-tuple-element.18.refs_3_), channel_id=1, source_target_pairs={{0,8},{1,9},{2,10},{3,11},{4,12},{5,13},{6,14},{7,15},{16,24},{17,... | collective-permute-start | bytes 1769480 | tf_op jit(solution)/shard_map/ppermute | solution.py:447
  41.6 5.8 %all-to-all-done = bf16[8,32,1152]{2,1,0:T(8,128)(2,1)} async-done(((bf16[8,32,1152]{2,1,0:T(8,128)(2,1)}), bf16[8,32,1152]{2,1,0:T(8,128)(2,1)}, u32[]{:S(2)}, u32[]{:S(2)}) %all-to-all-start) | async-done | bytes 589856 | tf_op jit(solution)/shard_map/all_to_all | solution.py:385
  47.4 2.1 %copy-done.2 = bf16[1,1152,1728]{1,2,0:T(8,128)(2,1)S(1)} copy-done((bf16[1,1152,1728]{1,2,0:T(8,128)(2,1)S(1)}, bf16[1,1152,1728]{1,2,0:T(8,128)(2,1)}, u32[]{:S(2)}) %copy-start.2) | copy-done | bytes 3981336
  49.5 1.3 %copy-done.3 = bf16[1,576,1152]{2,1,0:T(8,128)(2,1)S(1)} copy-done((bf16[1,576,1152]{2,1,0:T(8,128)(2,1)S(1)}, bf16[1,576,1152]{2,1,0:T(8,128)(2,1)}, u32[]{:S(2)}) %copy-start.3) | copy-done | bytes 1327128
  50.9 1.1 %copy-done.6 = bf16[256,1152]{1,0:T(8,128)(2,1)S(1)} copy-done((bf16[256,1152]{1,0:T(8,128)(2,1)S(1)}, bf16[256,1152]{1,0:T(8,128)(2,1)}, u32[]{:S(2)}) %copy-start.6) | copy-done | bytes 589848
  51.9 0.7 %copy-done.7 = s32[48,128]{1,0:T(8,128)S(1)} copy-done((s32[48,128]{1,0:T(8,128)S(1)}, s32[48,128]{1,0:T(8,128)}, u32[]{:S(2)}) %copy-start.7) | copy-done | bytes 24600
  52.7 1.0 %copy-done.9 = bf16[256,640]{1,0:T(8,128)(2,1)S(1)} copy-done((bf16[256,640]{1,0:T(8,128)(2,1)S(1)}, bf16[256,640]{1,0:T(8,128)(2,1)}, u32[]{:S(2)}) %copy-start.9) | copy-done | bytes 327704
  53.6 6.8 %attention_and_next_keys.1 = (bf16[48,1152]{1,0:T(8,128)(2,1)S(1)}, bf16[48,640]{1,0:T(8,128)(2,1)S(1)}, bf16[256,1152]{1,0:T(8,128)(2,1)S(1)}, bf16[256,1152]{1,0:T(8,128)(2,1)S(1)}) custom-call(bf16[256,1152]{1,0:T(8,128)(2,1)} %bitcast.1.refs_0_, bf16[256,1152]{1,0:T(8,128)(2,1)S(1)} %copy-done.6, bf16[256,640]{1,0:T(8,128)(2,1)S(1)} %copy-done.9, ...), custom_call_target="tpu_custom_call" | custom-call | tf_op jit(solution)/shard_map/attention_and_next_keys/pallas_call | solution.py:221
  60.6 2.0 %collective-permute-done.4.got_ref = bf16[256,1152]{1,0:T(8,128)(2,1)S(1)} collective-permute-done((bf16[256,1152]{1,0:T(8,128)(2,1)S(1)}, bf16[256,1152]{1,0:T(8,128)(2,1)S(1)}, u32[]{:S(2)}, u32[]{:S(2)}) %collective-permute-start.4) | collective-permute-done | bytes 589856 | tf_op jit(solution)/shard_map/ppermute | solution.py:451
  62.6 4.1 %tile_attention_and_patches.1.patch_ref = f32[48,128]{1,0:T(8,128)S(1)} custom-call(bf16[48,1152]{1,0:T(8,128)(2,1)S(1)} %get-tuple-element.20.x_ref, bf16[48,640]{1,0:T(8,128)(2,1)S(1)} %get-tuple-element.21.q_ref, bf16[256,1152]{1,0:T(8,128)(2,1)S(1)} %get-tuple-element.22.kv_ref, bf16[256,1152]{1,0:T(8,128)(2,1)S(1)} %collective-permute-done.4.got_ref, ...), custom_call_target="tpu_custom_call" | custom-call | tf_op jit(solution)/shard_map/tile_attention_and_patches/pallas_call | solution.py:263
  66.8 1.2 %collective-permute-done.5.got_ref = f32[48,128]{1,0:T(8,128)S(1)} collective-permute-done((f32[48,128]{1,0:T(8,128)S(1)}, f32[48,128]{1,0:T(8,128)S(1)}, u32[]{:S(2)}, u32[]{:S(2)}) %collective-permute-start.5) | collective-permute-done | bytes 24608 | tf_op jit(solution)/shard_map/ppermute | solution.py:456
  68.0 4.3 %decoder_convolutions.1 = bf16[4,128,512]{2,1,0:T(8,128)(2,1)} custom-call(f32[48,128]{1,0:T(8,128)S(1)} %tile_attention_and_patches.1.patch_ref, f32[48,128]{1,0:T(8,128)S(1)} %collective-permute-done.5.got_ref, s32[48,128]{1,0:T(8,128)S(1)} %copy-done.7, bf16[1024,512]{1,0:T(8,128)(2,1)S(1)} %copy-done.4, f32[1,512]{1,0:T(1,128)S(1)} %bitcast.44, ...), custom_call_target="tpu_custom_call" | custom-call | tf_op jit(solution)/shard_map/decoder_convolutions/pallas_call | solution.py:354
  (46 shorter events, 1.5 us)
Async XLA Ops:
  0.0 11.2 %copy-start = (f32[100,5,1152]{2,0,1:T(8,128)S(1)}, f32[100,5,1152]{2,0,1:T(8,128)}, u32[]{:S(2)}) copy-start(f32[100,5,1152]{2,0,1:T(8,128)} %param.19) | copy-start | bytes 6912004
  0.0 13.6 %copy-start.14 = (bf16[1,2,32,1152]{3,2,1,0:T(8,128)(2,1)S(1)}, bf16[1,2,32,1152]{3,2,1,0:T(8,128)(2,1)}, u32[]{:S(2)}) copy-start(bf16[1,2,32,1152]{3,2,1,0:T(8,128)(2,1)} %param.15) | copy-start | bytes 442372
  0.0 32.6 %collective-permute-start.1 = (bf16[1,1728,1152]{2,1,0:T(8,128)(2,1)}, bf16[1,1728,1152]{2,1,0:T(8,128)(2,1)}, u32[]{:S(2)}, u32[]{:S(2)}) collective-permute-start(bf16[1,1728,1152]{2,1,0:T(8,128)(2,1)} %bitcast.37), channel_id=1, source_target_pairs={{0,8},{8,0},{1,9},{9,1},{2,10},{10,2},{3,11},{11,3},{4,12},{12,4},... | collective-permute-start | bytes 11943944 | tf_op jit(solution)/shard_map/ppermute | solution.py:416
  1.4 30.4 %collective-permute-start = (f32[3,1152]{1,0:T(4,128)S(1)}, f32[3,1152]{1,0:T(4,128)S(1)}, u32[]{:S(2)}, u32[]{:S(2)}) collective-permute-start(f32[3,1152]{1,0:T(4,128)S(1)} %bitcast.46), channel_id=1, source_target_pairs={{0,8},{8,0},{1,9},{9,1},{2,10},{10,2},{3,11},{11,3},{4,12},{12,4},... | collective-permute-start | bytes 41480 | tf_op jit(solution)/shard_map/ppermute | solution.py:420
  3.2 28.6 %copy-start.13 = (f32[1,3,1152]{2,0,1:T(1,128)S(1)}, f32[1,3,1152]{2,0,1:T(1,128)}, u32[]{:S(2)}) copy-start(f32[1,3,1152]{2,0,1:T(1,128)} %param.18) | copy-start | bytes 41476
  3.2 28.6 %copy-start.15 = (f32[3]{0:T(128)S(1)}, f32[3]{0:T(128)}, u32[]{:S(2)}) copy-start(f32[3]{0:T(128)} %constant.67) | copy-start | bytes 40
  3.2 23.5 %all-to-all-start.1 = ((bf16[8,32,1152]{2,1,0:T(8,128)(2,1)}), bf16[8,32,1152]{2,1,0:T(8,128)(2,1)S(1)}, u32[]{:S(2)}, u32[]{:S(2)}) async-start(bf16[8,32,1152]{2,1,0:T(8,128)(2,1)} %broadcast_in_dim.32), calls=%async_computation.1 | async-start | bytes 1179648 | tf_op jit(solution)/shard_map/all_to_all | solution.py:385
  10.5 36.9 %collective-permute-start.3 = (bf16[1,576,1152]{2,1,0:T(8,128)(2,1)}, bf16[1,576,1152]{2,1,0:T(8,128)(2,1)}, u32[]{:S(2)}, u32[]{:S(2)}) collective-permute-start(bf16[1,576,1152]{2,1,0:T(8,128)(2,1)} %wo_own.1), channel_id=1, source_target_pairs={{0,8},{8,0},{1,9},{9,1},{2,10},{10,2},{3,11},{11,3},{4,12},{12,4},... | collective-permute-start | bytes 3981320 | tf_op jit(solution)/shard_map/ppermute | solution.py:419
  27.6 19.8 %all-to-all-start = ((bf16[8,32,1152]{2,1,0:T(8,128)(2,1)}), bf16[8,32,1152]{2,1,0:T(8,128)(2,1)}, u32[]{:S(2)}, u32[]{:S(2)}) async-start(bf16[8,32,1152]{2,1,0:T(8,128)(2,1)} %broadcast_in_dim.30), calls=%async_computation | async-start | bytes 1179648 | tf_op jit(solution)/shard_map/all_to_all | solution.py:385
  32.6 2.1 %copy-start.1 = (bf16[1,1152,1728]{1,2,0:T(8,128)(2,1)S(1)}, bf16[1,1152,1728]{1,2,0:T(8,128)(2,1)}, u32[]{:S(2)}) copy-start(bf16[1,1152,1728]{1,2,0:T(8,128)(2,1)} %param.16) | copy-start | bytes 11943940
  34.7 33.2 %slice-start = ((s8[4718592]{0:T(1024)(128)(4,1)}), s8[524288]{0:T(1024)(128)(4,1)S(1)}, s32[]{:S(2)}) async-start(s8[4718592]{0:T(1024)(128)(4,1)} %bitcast.40), calls=%async_computation.2 | async-start | bytes 1048576
  37.5 0.9 %copy-start.5 = (bf16[256,1152]{1,0:T(8,128)(2,1)}, bf16[256,1152]{1,0:T(8,128)(2,1)S(1)}, u32[]{:S(2)}) copy-start(bf16[256,1152]{1,0:T(8,128)(2,1)S(1)} %get-tuple-element.16.refs_1_) | copy-start | bytes 1769476
  39.1 8.3 %collective-permute-start.2 = (bf16[256,1152]{1,0:T(8,128)(2,1)}, bf16[256,1152]{1,0:T(8,128)(2,1)S(1)}, u32[]{:S(2)}, u32[]{:S(2)}) collective-permute-start(bf16[256,1152]{1,0:T(8,128)(2,1)} %get-tuple-element.18.refs_3_), channel_id=1, source_target_pairs={{0,8},{1,9},{2,10},{3,11},{4,12},{5,13},{6,14},{7,15},{16,24},{17,... | collective-permute-start | bytes 1769480 | tf_op jit(solution)/shard_map/ppermute | solution.py:447
  47.4 2.1 %copy-start.2 = (bf16[1,1152,1728]{1,2,0:T(8,128)(2,1)S(1)}, bf16[1,1152,1728]{1,2,0:T(8,128)(2,1)}, u32[]{:S(2)}) copy-start(bf16[1,1152,1728]{1,2,0:T(8,128)(2,1)} %param.16) | copy-start | bytes 11943940
  49.5 1.3 %copy-start.3 = (bf16[1,576,1152]{2,1,0:T(8,128)(2,1)S(1)}, bf16[1,576,1152]{2,1,0:T(8,128)(2,1)}, u32[]{:S(2)}) copy-start(bf16[1,576,1152]{2,1,0:T(8,128)(2,1)} %wo_own.1) | copy-start | bytes 3981316
  50.9 1.1 %copy-start.6 = (bf16[256,1152]{1,0:T(8,128)(2,1)S(1)}, bf16[256,1152]{1,0:T(8,128)(2,1)}, u32[]{:S(2)}) copy-start(bf16[256,1152]{1,0:T(8,128)(2,1)} %copy-done.5) | copy-start | bytes 1769476
  52.7 1.0 %copy-start.9 = (bf16[256,640]{1,0:T(8,128)(2,1)S(1)}, bf16[256,640]{1,0:T(8,128)(2,1)}, u32[]{:S(2)}) copy-start(bf16[256,640]{1,0:T(8,128)(2,1)} %copy-done.8) | copy-start | bytes 983044
  53.6 8.9 %copy-start.10 = (bf16[1152,16]{0,1:T(8,128)(2,1)S(1)}, bf16[1152,16]{0,1:T(8,128)(2,1)}, u32[]{:S(2)}) copy-start(bf16[1152,16]{0,1:T(8,128)(2,1)} %param.21) | copy-start | bytes 110596
  53.6 14.3 %slice-start.1 = ((s8[4718592]{0:T(1024)(128)(4,1)}), s8[4194304]{0:T(1024)(128)(4,1)S(1)}, s32[]{:S(2)}) async-start(s8[4718592]{0:T(1024)(128)(4,1)} %bitcast.40), calls=%async_computation.3 | async-start | bytes 8388608
  60.5 7.5 %copy-start.4 = (bf16[1024,512]{1,0:T(8,128)(2,1)S(1)}, bf16[1024,512]{1,0:T(8,128)(2,1)}, u32[]{:S(2)}) copy-start(bf16[1024,512]{1,0:T(8,128)(2,1)} %convolution_convert_fusion.wp_ref) | copy-start | bytes 3145732
  60.5 7.5 %copy-start.11 = (f32[512]{0:T(512)S(1)}, f32[512]{0:T(512)}, u32[]{:S(2)}) copy-start(f32[512]{0:T(512)} %param.23) | copy-start | bytes 6148
  60.5 7.5 %copy-start.12 = (f32[512]{0:T(512)S(1)}, f32[512]{0:T(512)}, u32[]{:S(2)}) copy-start(f32[512]{0:T(512)} %param.25) | copy-start | bytes 6148
  60.5 2.1 %collective-permute-start.4 = (bf16[256,1152]{1,0:T(8,128)(2,1)S(1)}, bf16[256,1152]{1,0:T(8,128)(2,1)S(1)}, u32[]{:S(2)}, u32[]{:S(2)}) collective-permute-start(bf16[256,1152]{1,0:T(8,128)(2,1)S(1)} %get-tuple-element.23), channel_id=1, source_target_pairs={{0,8},{8,0},{1,9},{9,1},{2,10},{10,2},{3,11},{11,3},{4,12},{12,4},... | collective-permute-start | bytes 1769480 | tf_op jit(solution)/shard_map/ppermute | solution.py:451
  66.7 1.3 %collective-permute-start.5 = (f32[48,128]{1,0:T(8,128)S(1)}, f32[48,128]{1,0:T(8,128)S(1)}, u32[]{:S(2)}, u32[]{:S(2)}) collective-permute-start(f32[48,128]{1,0:T(8,128)S(1)} %tile_attention_and_patches.1.patch_ref), channel_id=1, source_target_pairs={{0,8},{8,0},{1,9},{9,1},{2,10},{10,2},{3,11},{11,3},{4,12},{12,4},... | collective-permute-start | bytes 73736 | tf_op jit(solution)/shard_map/ppermute | solution.py:456
  (2 other events, 1.5 us)

commit v7 on v4

--- a/solution.py
+++ b/solution.py
@@ -27,7 +27,7 @@
 F32 = jnp.float32
 BF16 = jnp.bfloat16
 VMEM = pl.BlockSpec(memory_space=pltpu.VMEM)
-ANY = pl.BlockSpec(memory_space=pl.ANY)
+HBM = pl.BlockSpec(memory_space=pltpu.HBM)
 
 
 def dot(a, b):
@@ -153,7 +153,7 @@
             jax.ShapeDtypeStruct((count, DP), BF16),
             jax.ShapeDtypeStruct((count, 2 * DA), BF16),
         ),
-        in_specs=[VMEM] * (len(pieces) + 1) + [ANY] * 2,
+        in_specs=[VMEM] * (len(pieces) + 1) + [HBM] * 2,
         out_specs=(VMEM,) * 3,
         scratch_shapes=[
             pltpu.VMEM((3 * DA, D), BF16),
@@ -226,7 +226,7 @@
             jax.ShapeDtypeStruct((count, 2 * DA), BF16),
             jax.ShapeDtypeStruct((count, 2 * DA), BF16),
         ),
-        in_specs=[VMEM] * (len(stale_pieces) + 6) + [ANY] * 4,
+        in_specs=[VMEM] * (len(stale_pieces) + 6) + [HBM] * 4,
         out_specs=(VMEM,) * 4,
         scratch_shapes=[
             pltpu.VMEM((3 * DA, D), BF16),
@@ -263,7 +263,7 @@
     return pl.pallas_call(
         tile_kernel,
         out_shape=jax.ShapeDtypeStruct((x.shape[0], LANES), F32),
-        in_specs=[VMEM] * 7 + [ANY] * 2,
+        in_specs=[VMEM] * 7 + [HBM] * 2,
         out_specs=VMEM,
         scratch_shapes=[
             pltpu.VMEM((DP, D), BF16),
@@ -354,7 +354,7 @@
     return pl.pallas_call(
         functools.partial(decode_kernel, rows, cols, pitch),
         out_shape=jax.ShapeDtypeStruct((4 * rows, 4 * cols, CH), BF16),
-        in_specs=[VMEM] * 6 + [ANY],
+        in_specs=[VMEM] * 6 + [HBM],
         out_specs=VMEM,
         scratch_shapes=[
             pltpu.VMEM((9, CH, CH), BF16),
@@ -393,14 +393,6 @@
         o, e = divmod(i, inner)
         route.append(((o + k_outer) % outer * inner + (e + k_inner) % inner, i))
     return lax.ppermute(block, "patch", route)
-
-
-def gather_outer(own, outer):
-    return jnp.concatenate([own] + [shifted(own, k, 0) for k in range(1, outer)], axis=0)
-
-
-def gather_inner(column, inner):
-    return [column] + [shifted(column, 0, k) for k in range(1, inner)]
 
 
 def local(
@@ -432,22 +424,24 @@
     own_tokens = lax.dynamic_index_in_dim(tokens, section, 0, keepdims=False)
     w_qkv = jnp.swapaxes(w_qkv, 1, 2)
     w_qkv_other = lax.ppermute(w_qkv, "pipe", swap)
-    x_column = gather_outer(own_tokens, outer)
-    x_column, own_stale = lax.optimization_barrier((x_column, stale_kv[0, 1]))
-    x_pieces = gather_inner(x_column, inner)
-    stale_pieces = gather_inner(gather_outer(own_stale, outer), inner)
-    w_out_other = lax.ppermute(w_out, "pipe", swap)
-    table_other = lax.ppermute(block_table[0], "pipe", swap)
+    tables = lax.all_gather(block_table[0], "pipe")
+    x_column = [shifted(own_tokens, k, 0) for k in range(1, outer)]
+    x_own_inner = [shifted(own_tokens, 0, k) for k in range(1, inner)]
+    own_stale = stale_kv[0, 1]
+    x_column, x_own_inner, w_qkv_other, own_stale, w_in = lax.optimization_barrier(
+        (x_column, x_own_inner, w_qkv_other, own_stale, w_in)
+    )
+    x_pieces = [own_tokens] + x_column
+    for k in range(1, inner):
+        x_pieces += [x_own_inner[k - 1]] + [shifted(piece, 0, k) for piece in x_column]
+    stale_column = [own_stale] + [shifted(own_stale, k, 0) for k in range(1, outer)]
 
     time_row = lax.dynamic_index_in_dim(time_table, t_index[0], 0, keepdims=False)
-    table = block_table[0]
-    table_0 = jnp.where(first_core, table, table_other)
-    table_1 = jnp.where(first_core, table_other, table)
     ones = jnp.asarray([[0.0], [1.0], [0.0]], F32)
     vecs = jnp.concatenate(
         [
-            time_row[:3] + table_0 + ones,
-            time_row[:3] + table_1 + ones,
+            time_row[:3] + tables[0] + ones,
+            time_row[:3] + tables[1] + ones,
             time_row[3:5] + ones[:2],
         ],
         axis=0,
@@ -465,7 +459,11 @@
     idx = jnp.broadcast_to(jnp.where(inside, spot, -1)[:, None], (padded_rows, LANES)).astype(jnp.int32)
 
     w_patch = dot(jnp.asarray(patch_selector(), BF16), w_in).astype(BF16)
-    x_pieces, w_patch, idx = lax.optimization_barrier((x_pieces, w_patch, idx))
+    x_pieces, w_patch, idx, stale_column, w_out = lax.optimization_barrier(
+        (x_pieces, w_patch, idx, stale_column, w_out)
+    )
+    w_out_other = lax.ppermute(w_out, "pipe", swap)
+    stale_pieces = stale_column + [shifted(piece, 0, k) for k in range(1, inner) for piece in stale_column]
 
     x, query, fresh = project(x_pieces, vecs, w_qkv, w_qkv_other)
     got = lax.ppermute(fresh, "pipe", [(0, 1)])

time: 59.7 us -> 64 us (1.072)
  starting transfers between devices: 18.6 us -> 22.8 us
  blocking collectives: 0 us -> 2.32 us
  local copies, waits for them, and re-layouts: 7.17 us -> 5 us
  Pallas kernels: 15.5 us -> 16.6 us
  other arithmetic: 1.87 us -> 0.8 us
    ppermute x8 -> x14, starting transfers between devices: 15.3 us -> 18.5 us  [shifted(): return lax.ppermute(block, 'patch', route)]
    all_gather x0 -> x1, blocking collectives: none -> 2.32 us  [local(): tables = lax.all_gather(block_table[0], 'pipe')]
    ppermute x1, starting transfers between devices: 1.97 us -> 3.57 us  [local(): got = lax.ppermute(fresh, 'pipe', [(0, 1)])]
    unnamed x22 -> x19, local copies, waits for them, and re-layouts: 4.41 us -> 2.88 us
    pallas_call x1, Pallas kernels: 5.48 us -> 6.62 us  [first_block(): pl.pallas_call(functools.partial(block_kernel, len(stale_pieces)), out_sh...]
    concatenate x2 -> x1, other arithmetic: 1 us -> 0.02 us  [local(): jnp.concatenate([time_row[:3] + tables[0] + ones, time_row[:3] + tables[1...]
    ppermute x8 -> x14, waiting for transfers between devices: 10.9 us -> 10.8 us  [shifted(): return lax.ppermute(block, 'patch', route)]
  transfers between devices with their start and end apart: 14 -> 19, of which waited for: 5 -> 10; matrix products, arithmetic and copies ran while one was open for 14% -> 8% of each run, Pallas kernels for 4% -> 4%
where the time goes in v7:
time: 64 us; the launch traced here: 63.7 us
  starting transfers between devices  22.8 us (36%)
  Pallas kernels  16.6 us (26%)
  waiting for transfers between devices  13.9 us (22%)
  local copies, waits for them, and re-layouts  5 us (8%)
  blocking collectives  2.32 us (4%)
  matrix products  1.37 us (2%)
  between operations  0.88 us (1%)
  other arithmetic  0.8 us (1%)
    ppermute x14, starting transfers between devices, shifted(): return lax.ppermute(block, 'patch', route)  18.5 us
    ppermute x14, waiting for transfers between devices, shifted(): return lax.ppermute(block, 'patch', route)  10.8 us
    pallas_call x1, Pallas kernels, first_block(): pl.pallas_call(functools.partial(block_kernel, len(stale_pieces)), out_sh...  6.62 us
    pallas_call x1, Pallas kernels, decode(): pl.pallas_call(functools.partial(decode_kernel, rows, cols, pitch), out_s...  4.32 us
    ppermute x1, starting transfers between devices, local(): got = lax.ppermute(fresh, 'pipe', [(0, 1)])  3.57 us
    pallas_call x1, Pallas kernels, tile_block(): pl.pallas_call(tile_kernel, out_shape=jax.ShapeDtypeStruct((x.shape[0], L...  3.31 us
    unnamed x19, local copies, waits for them, and re-layouts  2.88 us
    pallas_call x1, Pallas kernels, project(): pl.pallas_call(functools.partial(project_kernel, len(pieces)), out_shape=...  2.39 us
  transfers between devices with their start and end apart: 19, of which 10 were waited for; matrix products, arithmetic and copies ran while one was open for 8% of the time, Pallas kernels for 4%

profile of v7, /device:TPU:0, one launch (start us, length us, event | category | flops | bytes accessed | tf_op | source)
XLA Modules:
  0.0 63.7 jit_solution(13881675360064899419)
XLA Ops:
  0.5 1.1 %dynamic-slice_bitcast_fusion.refs_0_ = bf16[32,1152]{1,0:T(8,128)(2,1)S(1)} fusion(bf16[2,32,1152]{2,1,0:T(8,128)(2,1)} %param.14, s32[]{:T(128)S(6)} %select_n.96), kind=kLoop, calls=%fused_computation.3 | loop fusion | bytes 147460 | tf_op jit(solution)/shard_map/jit(dynamic_index_in_dim)/squeeze | solution.py:424
  1.6 2.5 %collective-permute-start.3 = (bf16[32,1152]{1,0:T(8,128)(2,1)S(1)}, bf16[32,1152]{1,0:T(8,128)(2,1)S(1)}, u32[]{:S(2)}, u32[]{:S(2)}) collective-permute-start(bf16[32,1152]{1,0:T(8,128)(2,1)S(1)} %dynamic-slice_bitcast_fusion.refs_0_), channel_id=1, source_target_pairs={{1,0},{0,1},{3,2},{2,3},{5,4},{4,5},{7,6},{6,7},{9,8},{8,9},{11,10... | collective-permute-start | bytes 221192 | tf_op jit(solution)/shard_map/ppermute | solution.py:395
  4.1 1.6 %collective-permute-start.2 = (bf16[32,1152]{1,0:T(8,128)(2,1)S(1)}, bf16[32,1152]{1,0:T(8,128)(2,1)S(1)}, u32[]{:S(2)}, u32[]{:S(2)}) collective-permute-start(bf16[32,1152]{1,0:T(8,128)(2,1)S(1)} %dynamic-slice_bitcast_fusion.refs_0_), channel_id=1, source_target_pairs={{6,0},{7,1},{0,2},{1,3},{2,4},{3,5},{4,6},{5,7},{14,8},{15,9},{8,1... | collective-permute-start | bytes 221192 | tf_op jit(solution)/shard_map/ppermute | solution.py:395
  5.6 2.6 %collective-permute-start.1 = (bf16[32,1152]{1,0:T(8,128)(2,1)S(1)}, bf16[32,1152]{1,0:T(8,128)(2,1)S(1)}, u32[]{:S(2)}, u32[]{:S(2)}) collective-permute-start(bf16[32,1152]{1,0:T(8,128)(2,1)S(1)} %dynamic-slice_bitcast_fusion.refs_0_), channel_id=1, source_target_pairs={{4,0},{5,1},{6,2},{7,3},{0,4},{1,5},{2,6},{3,7},{12,8},{13,9},{14,... | collective-permute-start | bytes 221192 | tf_op jit(solution)/shard_map/ppermute | solution.py:395
  8.2 1.3 %collective-permute-start = (bf16[32,1152]{1,0:T(8,128)(2,1)S(1)}, bf16[32,1152]{1,0:T(8,128)(2,1)S(1)}, u32[]{:S(2)}, u32[]{:S(2)}) collective-permute-start(bf16[32,1152]{1,0:T(8,128)(2,1)S(1)} %dynamic-slice_bitcast_fusion.refs_0_), channel_id=1, source_target_pairs={{2,0},{3,1},{4,2},{5,3},{6,4},{7,5},{0,6},{1,7},{10,8},{11,9},{12,... | collective-permute-start | bytes 221192 | tf_op jit(solution)/shard_map/ppermute | solution.py:395
  11.2 2.2 %collective-permute-done.1.refs_2_ = bf16[32,1152]{1,0:T(8,128)(2,1)S(1)} collective-permute-done((bf16[32,1152]{1,0:T(8,128)(2,1)S(1)}, bf16[32,1152]{1,0:T(8,128)(2,1)S(1)}, u32[]{:S(2)}, u32[]{:S(2)}) %collective-permute-start.1) | collective-permute-done | bytes 73760 | tf_op jit(solution)/shard_map/ppermute | solution.py:395
  14.2 1.9 %collective-permute-start.10 = (bf16[32,1152]{1,0:T(8,128)(2,1)S(1)}, bf16[32,1152]{1,0:T(8,128)(2,1)S(1)}, u32[]{:S(2)}, u32[]{:S(2)}) collective-permute-start(bf16[32,1152]{1,0:T(8,128)(2,1)S(1)} %slice_bitcast_fusion.refs_0_), channel_id=1, source_target_pairs={{6,0},{7,1},{0,2},{1,3},{2,4},{3,5},{4,6},{5,7},{14,8},{15,9},{8,1... | collective-permute-start | bytes 221192 | tf_op jit(solution)/shard_map/ppermute | solution.py:395
  16.1 1.7 %collective-permute-start.9 = (bf16[32,1152]{1,0:T(8,128)(2,1)S(1)}, bf16[32,1152]{1,0:T(8,128)(2,1)S(1)}, u32[]{:S(2)}, u32[]{:S(2)}) collective-permute-start(bf16[32,1152]{1,0:T(8,128)(2,1)S(1)} %slice_bitcast_fusion.refs_0_), channel_id=1, source_target_pairs={{4,0},{5,1},{6,2},{7,3},{0,4},{1,5},{2,6},{3,7},{12,8},{13,9},{14,... | collective-permute-start | bytes 221192 | tf_op jit(solution)/shard_map/ppermute | solution.py:395
  18.5 1.5 %collective-permute-start.6 = (bf16[32,1152]{1,0:T(8,128)(2,1)S(1)}, bf16[32,1152]{1,0:T(8,128)(2,1)S(1)}, u32[]{:S(2)}, u32[]{:S(2)}) collective-permute-start(bf16[32,1152]{1,0:T(8,128)(2,1)S(1)} %collective-permute-done.1.refs_2_), channel_id=1, source_target_pairs={{1,0},{0,1},{3,2},{2,3},{5,4},{4,5},{7,6},{6,7},{9,8},{8,9},{11,10... | collective-permute-start | bytes 221192 | tf_op jit(solution)/shard_map/ppermute | solution.py:395
  20.5 1.4 %fusion.wp_ref = bf16[1024,512]{1,0:T(8,128)(2,1)S(1)} fusion(bf16[36,512]{1,0:T(8,128)(2,1)} %param.22, bf16[1024,36]{1,0:T(8,128)(2,1)} %constant.129.clone), kind=kOutput, calls=%fused_computation.1 | convolution fusion | flops 38273024 | bytes 1159168 | tf_op jit(solution)/shard_map/dot_general | solution.py:34
  21.9 1.2 %collective-permute-done.6.refs_6_ = bf16[32,1152]{1,0:T(8,128)(2,1)S(1)} collective-permute-done((bf16[32,1152]{1,0:T(8,128)(2,1)S(1)}, bf16[32,1152]{1,0:T(8,128)(2,1)S(1)}, u32[]{:S(2)}, u32[]{:S(2)}) %collective-permute-start.6) | collective-permute-done | bytes 73760 | tf_op jit(solution)/shard_map/ppermute | solution.py:395
  23.1 1.3 %collective-permute-done.7.refs_7_ = bf16[32,1152]{1,0:T(8,128)(2,1)S(1)} collective-permute-done((bf16[32,1152]{1,0:T(8,128)(2,1)S(1)}, bf16[32,1152]{1,0:T(8,128)(2,1)S(1)}, u32[]{:S(2)}, u32[]{:S(2)}) %collective-permute-start.7) | collective-permute-done | bytes 73760 | tf_op jit(solution)/shard_map/ppermute | solution.py:395
  25.3 2.3 %all_gather.3 = f32[2,3,1152]{2,1,0:T(4,128)S(1)} all-gather(f32[1,3,1152]{2,1,0:T(4,128)S(1)} %copy.20), channel_id=1, replica_groups=mesh['grp'=2,'pipe'=2,'patch'=8] {'pipe'}, dimensions={0}, use_global_device_ids=true | all-gather | bytes 41472 | tf_op jit(solution)/shard_map/all_gather | solution.py:427
  28.3 2.1 %copy-done.1 = bf16[1,1152,1728]{1,2,0:T(8,128)(2,1)S(1)} copy-done((bf16[1,1152,1728]{1,2,0:T(8,128)(2,1)S(1)}, bf16[1,1152,1728]{1,2,0:T(8,128)(2,1)}, u32[]{:S(2)}) %copy-start.1) | copy-done | bytes 3981336
  30.5 2.4 %layer_norm_and_projections.1 = (bf16[256,1152]{1,0:T(8,128)(2,1)S(1)}, bf16[256,640]{1,0:T(8,128)(2,1)S(1)}, bf16[256,1152]{1,0:T(8,128)(2,1)S(1)}) custom-call(bf16[32,1152]{1,0:T(8,128)(2,1)S(1)} %dynamic-slice_bitcast_fusion.refs_0_, bf16[32,1152]{1,0:T(8,128)(2,1)S(1)} %collective-permute-done.refs_1_, ...), custom_call_target="tpu_custom_call" | custom-call | tf_op jit(solution)/shard_map/layer_norm_and_projections/pallas_call | solution.py:149
  32.9 3.6 %collective-permute-start.15 = (bf16[256,1152]{1,0:T(8,128)(2,1)S(1)}, bf16[256,1152]{1,0:T(8,128)(2,1)S(1)}, u32[]{:S(2)}, u32[]{:S(2)}) collective-permute-start(bf16[256,1152]{1,0:T(8,128)(2,1)S(1)} %get-tuple-element.55.refs_10_), channel_id=1, source_target_pairs={{0,8},{1,9},{2,10},{3,11},{4,12},{5,13},{6,14},{7,15},{16,24},{17,... | collective-permute-start | bytes 1769480 | tf_op jit(solution)/shard_map/ppermute | solution.py:469
  37.3 1.2 %collective-permute-start.12 = (bf16[32,1152]{1,0:T(8,128)(2,1)S(1)}, bf16[32,1152]{1,0:T(8,128)(2,1)S(1)}, u32[]{:S(2)}, u32[]{:S(2)}) collective-permute-start(bf16[32,1152]{1,0:T(8,128)(2,1)S(1)} %collective-permute-done.8.refs_1_), channel_id=1, source_target_pairs={{1,0},{0,1},{3,2},{2,3},{5,4},{4,5},{7,6},{6,7},{9,8},{8,9},{11,10... | collective-permute-start | bytes 221192 | tf_op jit(solution)/shard_map/ppermute | solution.py:395
  39.3 2.3 %collective-permute-done.11.refs_4_ = bf16[32,1152]{1,0:T(8,128)(2,1)S(1)} collective-permute-done((bf16[32,1152]{1,0:T(8,128)(2,1)S(1)}, bf16[32,1152]{1,0:T(8,128)(2,1)S(1)}, u32[]{:S(2)}, u32[]{:S(2)}) %collective-permute-start.11) | collective-permute-done | bytes 73760 | tf_op jit(solution)/shard_map/ppermute | solution.py:395
  44.0 2.0 %collective-permute-done.14.refs_7_ = bf16[32,1152]{1,0:T(8,128)(2,1)S(1)} collective-permute-done((bf16[32,1152]{1,0:T(8,128)(2,1)S(1)}, bf16[32,1152]{1,0:T(8,128)(2,1)S(1)}, u32[]{:S(2)}, u32[]{:S(2)}) %collective-permute-start.14) | collective-permute-done | bytes 73760 | tf_op jit(solution)/shard_map/ppermute | solution.py:395
  46.0 6.6 %attention_and_next_keys.1 = (bf16[48,1152]{1,0:T(8,128)(2,1)S(1)}, bf16[48,640]{1,0:T(8,128)(2,1)S(1)}, bf16[256,1152]{1,0:T(8,128)(2,1)S(1)}, bf16[256,1152]{1,0:T(8,128)(2,1)S(1)}) custom-call(bf16[32,1152]{1,0:T(8,128)(2,1)S(1)} %slice_bitcast_fusion.refs_0_, bf16[32,1152]{1,0:T(8,128)(2,1)S(1)} %collective-permute-done.8.refs_1_, ...), custom_call_target="tpu_custom_call" | custom-call | tf_op jit(solution)/shard_map/attention_and_next_keys/pallas_call | solution.py:221
  52.7 2.0 %collective-permute-done.17.got_ref = bf16[256,1152]{1,0:T(8,128)(2,1)S(1)} collective-permute-done((bf16[256,1152]{1,0:T(8,128)(2,1)S(1)}, bf16[256,1152]{1,0:T(8,128)(2,1)S(1)}, u32[]{:S(2)}, u32[]{:S(2)}) %collective-permute-start.17) | collective-permute-done | bytes 589856 | tf_op jit(solution)/shard_map/ppermute | solution.py:473
  54.7 3.3 %tile_attention_and_patches.1.patch_ref = f32[48,128]{1,0:T(8,128)S(1)} custom-call(bf16[48,1152]{1,0:T(8,128)(2,1)S(1)} %get-tuple-element.58.x_ref, bf16[48,640]{1,0:T(8,128)(2,1)S(1)} %get-tuple-element.59.q_ref, bf16[256,1152]{1,0:T(8,128)(2,1)S(1)} %get-tuple-element.60.kv_ref, bf16[256,1152]{1,0:T(8,128)(2,1)S(1)} %collective-permute-done.17.got_ref, ...), custom_call_target="tpu_custom_call" | custom-call | tf_op jit(solution)/shard_map/tile_attention_and_patches/pallas_call | solution.py:263
  58.3 1.1 %collective-permute-done.18.got_ref = f32[48,128]{1,0:T(8,128)S(1)} collective-permute-done((f32[48,128]{1,0:T(8,128)S(1)}, f32[48,128]{1,0:T(8,128)S(1)}, u32[]{:S(2)}, u32[]{:S(2)}) %collective-permute-start.18) | collective-permute-done | bytes 24608 | tf_op jit(solution)/shard_map/ppermute | solution.py:478
  59.3 4.3 %decoder_convolutions.1 = bf16[4,128,512]{2,1,0:T(8,128)(2,1)} custom-call(f32[48,128]{1,0:T(8,128)S(1)} %tile_attention_and_patches.1.patch_ref, f32[48,128]{1,0:T(8,128)S(1)} %collective-permute-done.18.got_ref, s32[48,128]{1,0:T(8,128)S(1)} %broadcast_in_dim.14.refs_12_.idx_ref, bf16[1024,512]{1,0:T(8,128)(2,1)S(1)} %fusion.wp_ref, ...), custom_call_target="tpu_custom_call" | custom-call | tf_op jit(solution)/shard_map/decoder_convolutions/pallas_call | solution.py:354
  (49 shorter events, 9.3 us)
Async XLA Ops:
  0.0 10.2 %copy-start = (f32[100,5,1152]{2,0,1:T(8,128)S(1)}, f32[100,5,1152]{2,0,1:T(8,128)}, u32[]{:S(2)}) copy-start(f32[100,5,1152]{2,0,1:T(8,128)} %param.19) | copy-start | bytes 6912004
  0.0 13.7 %collective-permute-start.4 = (bf16[1,1728,1152]{2,1,0:T(8,128)(2,1)}, bf16[1,1728,1152]{2,1,0:T(8,128)(2,1)}, u32[]{:S(2)}, u32[]{:S(2)}) collective-permute-start(bf16[1,1728,1152]{2,1,0:T(8,128)(2,1)} %bitcast.28), channel_id=1, source_target_pairs={{0,8},{8,0},{1,9},{9,1},{2,10},{10,2},{3,11},{11,3},{4,12},{12,4},... | collective-permute-start | bytes 11943944 | tf_op jit(solution)/shard_map/ppermute | solution.py:426
  1.6 9.6 %collective-permute-start.3 = (bf16[32,1152]{1,0:T(8,128)(2,1)S(1)}, bf16[32,1152]{1,0:T(8,128)(2,1)S(1)}, u32[]{:S(2)}, u32[]{:S(2)}) collective-permute-start(bf16[32,1152]{1,0:T(8,128)(2,1)S(1)} %dynamic-slice_bitcast_fusion.refs_0_), channel_id=1, source_target_pairs={{1,0},{0,1},{3,2},{2,3},{5,4},{4,5},{7,6},{6,7},{9,8},{8,9},{11,10... | collective-permute-start | bytes 221192 | tf_op jit(solution)/shard_map/ppermute | solution.py:395
  4.1 7.1 %collective-permute-start.2 = (bf16[32,1152]{1,0:T(8,128)(2,1)S(1)}, bf16[32,1152]{1,0:T(8,128)(2,1)S(1)}, u32[]{:S(2)}, u32[]{:S(2)}) collective-permute-start(bf16[32,1152]{1,0:T(8,128)(2,1)S(1)} %dynamic-slice_bitcast_fusion.refs_0_), channel_id=1, source_target_pairs={{6,0},{7,1},{0,2},{1,3},{2,4},{3,5},{4,6},{5,7},{14,8},{15,9},{8,1... | collective-permute-start | bytes 221192 | tf_op jit(solution)/shard_map/ppermute | solution.py:395
  5.6 7.8 %collective-permute-start.1 = (bf16[32,1152]{1,0:T(8,128)(2,1)S(1)}, bf16[32,1152]{1,0:T(8,128)(2,1)S(1)}, u32[]{:S(2)}, u32[]{:S(2)}) collective-permute-start(bf16[32,1152]{1,0:T(8,128)(2,1)S(1)} %dynamic-slice_bitcast_fusion.refs_0_), channel_id=1, source_target_pairs={{4,0},{5,1},{6,2},{7,3},{0,4},{1,5},{2,6},{3,7},{12,8},{13,9},{14,... | collective-permute-start | bytes 221192 | tf_op jit(solution)/shard_map/ppermute | solution.py:395
  8.2 5.4 %collective-permute-start = (bf16[32,1152]{1,0:T(8,128)(2,1)S(1)}, bf16[32,1152]{1,0:T(8,128)(2,1)S(1)}, u32[]{:S(2)}, u32[]{:S(2)}) collective-permute-start(bf16[32,1152]{1,0:T(8,128)(2,1)S(1)} %dynamic-slice_bitcast_fusion.refs_0_), channel_id=1, source_target_pairs={{2,0},{3,1},{4,2},{5,3},{6,4},{7,5},{0,6},{1,7},{10,8},{11,9},{12,... | collective-permute-start | bytes 221192 | tf_op jit(solution)/shard_map/ppermute | solution.py:395
  13.7 6.4 %collective-permute-start.5 = (bf16[32,1152]{1,0:T(8,128)(2,1)S(1)}, bf16[32,1152]{1,0:T(8,128)(2,1)S(1)}, u32[]{:S(2)}, u32[]{:S(2)}) collective-permute-start(bf16[32,1152]{1,0:T(8,128)(2,1)S(1)} %collective-permute-done.refs_1_), channel_id=1, source_target_pairs={{1,0},{0,1},{3,2},{2,3},{5,4},{4,5},{7,6},{6,7},{9,8},{8,9},{11,10... | collective-permute-start | bytes 221192 | tf_op jit(solution)/shard_map/ppermute | solution.py:395
  14.2 10.2 %collective-permute-start.10 = (bf16[32,1152]{1,0:T(8,128)(2,1)S(1)}, bf16[32,1152]{1,0:T(8,128)(2,1)S(1)}, u32[]{:S(2)}, u32[]{:S(2)}) collective-permute-start(bf16[32,1152]{1,0:T(8,128)(2,1)S(1)} %slice_bitcast_fusion.refs_0_), channel_id=1, source_target_pairs={{6,0},{7,1},{0,2},{1,3},{2,4},{3,5},{4,6},{5,7},{14,8},{15,9},{8,1... | collective-permute-start | bytes 221192 | tf_op jit(solution)/shard_map/ppermute | solution.py:395
  16.1 8.3 %collective-permute-start.9 = (bf16[32,1152]{1,0:T(8,128)(2,1)S(1)}, bf16[32,1152]{1,0:T(8,128)(2,1)S(1)}, u32[]{:S(2)}, u32[]{:S(2)}) collective-permute-start(bf16[32,1152]{1,0:T(8,128)(2,1)S(1)} %slice_bitcast_fusion.refs_0_), channel_id=1, source_target_pairs={{4,0},{5,1},{6,2},{7,3},{0,4},{1,5},{2,6},{3,7},{12,8},{13,9},{14,... | collective-permute-start | bytes 221192 | tf_op jit(solution)/shard_map/ppermute | solution.py:395
  17.8 6.6 %collective-permute-start.8 = (bf16[32,1152]{1,0:T(8,128)(2,1)S(1)}, bf16[32,1152]{1,0:T(8,128)(2,1)S(1)}, u32[]{:S(2)}, u32[]{:S(2)}) collective-permute-start(bf16[32,1152]{1,0:T(8,128)(2,1)S(1)} %slice_bitcast_fusion.refs_0_), channel_id=1, source_target_pairs={{2,0},{3,1},{4,2},{5,3},{6,4},{7,5},{0,6},{1,7},{10,8},{11,9},{12,... | collective-permute-start | bytes 221192 | tf_op jit(solution)/shard_map/ppermute | solution.py:395
  18.5 4.6 %collective-permute-start.6 = (bf16[32,1152]{1,0:T(8,128)(2,1)S(1)}, bf16[32,1152]{1,0:T(8,128)(2,1)S(1)}, u32[]{:S(2)}, u32[]{:S(2)}) collective-permute-start(bf16[32,1152]{1,0:T(8,128)(2,1)S(1)} %collective-permute-done.1.refs_2_), channel_id=1, source_target_pairs={{1,0},{0,1},{3,2},{2,3},{5,4},{4,5},{7,6},{6,7},{9,8},{8,9},{11,10... | collective-permute-start | bytes 221192 | tf_op jit(solution)/shard_map/ppermute | solution.py:395
  20.0 4.4 %collective-permute-start.7 = (bf16[32,1152]{1,0:T(8,128)(2,1)S(1)}, bf16[32,1152]{1,0:T(8,128)(2,1)S(1)}, u32[]{:S(2)}, u32[]{:S(2)}) collective-permute-start(bf16[32,1152]{1,0:T(8,128)(2,1)S(1)} %collective-permute-done.2.refs_3_), channel_id=1, source_target_pairs={{1,0},{0,1},{3,2},{2,3},{5,4},{4,5},{7,6},{6,7},{9,8},{8,9},{11,10... | collective-permute-start | bytes 221192 | tf_op jit(solution)/shard_map/ppermute | solution.py:395
  24.5 21.5 %collective-permute-start.16 = (bf16[1,576,1152]{2,1,0:T(8,128)(2,1)}, bf16[1,576,1152]{2,1,0:T(8,128)(2,1)S(1)}, u32[]{:S(2)}, u32[]{:S(2)}) collective-permute-start(bf16[1,576,1152]{2,1,0:T(8,128)(2,1)} %wo_own), channel_id=1, source_target_pairs={{0,8},{8,0},{1,9},{9,1},{2,10},{10,2},{3,11},{11,3},{4,12},{12,4},... | collective-permute-start | bytes 3981320 | tf_op jit(solution)/shard_map/ppermute | solution.py:465
  30.5 15.5 %copy-start.2 = (bf16[1,1152,1728]{1,2,0:T(8,128)(2,1)S(1)}, bf16[1,1152,1728]{1,2,0:T(8,128)(2,1)}, u32[]{:S(2)}) copy-start(bf16[1,1152,1728]{1,2,0:T(8,128)(2,1)} %param.16) | copy-start | bytes 11943940
  30.5 15.5 %copy-start.3 = (bf16[1,576,1152]{2,1,0:T(8,128)(2,1)S(1)}, bf16[1,576,1152]{2,1,0:T(8,128)(2,1)}, u32[]{:S(2)}) copy-start(bf16[1,576,1152]{2,1,0:T(8,128)(2,1)} %wo_own) | copy-start | bytes 3981316
  32.9 13.1 %collective-permute-start.15 = (bf16[256,1152]{1,0:T(8,128)(2,1)S(1)}, bf16[256,1152]{1,0:T(8,128)(2,1)S(1)}, u32[]{:S(2)}, u32[]{:S(2)}) collective-permute-start(bf16[256,1152]{1,0:T(8,128)(2,1)S(1)} %get-tuple-element.55.refs_10_), channel_id=1, source_target_pairs={{0,8},{1,9},{2,10},{3,11},{4,12},{5,13},{6,14},{7,15},{16,24},{17,... | collective-permute-start | bytes 1769480 | tf_op jit(solution)/shard_map/ppermute | solution.py:469
  36.4 5.2 %collective-permute-start.11 = (bf16[32,1152]{1,0:T(8,128)(2,1)S(1)}, bf16[32,1152]{1,0:T(8,128)(2,1)S(1)}, u32[]{:S(2)}, u32[]{:S(2)}) collective-permute-start(bf16[32,1152]{1,0:T(8,128)(2,1)S(1)} %slice_bitcast_fusion.refs_0_), channel_id=1, source_target_pairs={{1,0},{0,1},{3,2},{2,3},{5,4},{4,5},{7,6},{6,7},{9,8},{8,9},{11,10... | collective-permute-start | bytes 221192 | tf_op jit(solution)/shard_map/ppermute | solution.py:395
  37.3 5.8 %collective-permute-start.12 = (bf16[32,1152]{1,0:T(8,128)(2,1)S(1)}, bf16[32,1152]{1,0:T(8,128)(2,1)S(1)}, u32[]{:S(2)}, u32[]{:S(2)}) collective-permute-start(bf16[32,1152]{1,0:T(8,128)(2,1)S(1)} %collective-permute-done.8.refs_1_), channel_id=1, source_target_pairs={{1,0},{0,1},{3,2},{2,3},{5,4},{4,5},{7,6},{6,7},{9,8},{8,9},{11,10... | collective-permute-start | bytes 221192 | tf_op jit(solution)/shard_map/ppermute | solution.py:395
  38.5 5.4 %collective-permute-start.13 = (bf16[32,1152]{1,0:T(8,128)(2,1)S(1)}, bf16[32,1152]{1,0:T(8,128)(2,1)S(1)}, u32[]{:S(2)}, u32[]{:S(2)}) collective-permute-start(bf16[32,1152]{1,0:T(8,128)(2,1)S(1)} %collective-permute-done.9.refs_2_), channel_id=1, source_target_pairs={{1,0},{0,1},{3,2},{2,3},{5,4},{4,5},{7,6},{6,7},{9,8},{8,9},{11,10... | collective-permute-start | bytes 221192 | tf_op jit(solution)/shard_map/ppermute | solution.py:395
  41.6 4.4 %collective-permute-start.14 = (bf16[32,1152]{1,0:T(8,128)(2,1)S(1)}, bf16[32,1152]{1,0:T(8,128)(2,1)S(1)}, u32[]{:S(2)}, u32[]{:S(2)}) collective-permute-start(bf16[32,1152]{1,0:T(8,128)(2,1)S(1)} %collective-permute-done.10.refs_3_), channel_id=1, source_target_pairs={{1,0},{0,1},{3,2},{2,3},{5,4},{4,5},{7,6},{6,7},{9,8},{8,9},{11,10... | collective-permute-start | bytes 221192 | tf_op jit(solution)/shard_map/ppermute | solution.py:395
  46.0 13.4 %slice-start = ((s8[4718592]{0:T(1024)(128)(4,1)}), s8[4194304]{0:T(1024)(128)(4,1)S(1)}, s32[]{:S(2)}) async-start(s8[4718592]{0:T(1024)(128)(4,1)} %bitcast.31), calls=%async_computation | async-start | bytes 8388608
  46.0 13.3 %slice-start.1 = ((s8[4718592]{0:T(1024)(128)(4,1)}), s8[524288]{0:T(1024)(128)(4,1)S(1)}, s32[]{:S(2)}) async-start(s8[4718592]{0:T(1024)(128)(4,1)} %bitcast.31), calls=%async_computation.1 | async-start | bytes 1048576
  52.7 2.1 %collective-permute-start.17 = (bf16[256,1152]{1,0:T(8,128)(2,1)S(1)}, bf16[256,1152]{1,0:T(8,128)(2,1)S(1)}, u32[]{:S(2)}, u32[]{:S(2)}) collective-permute-start(bf16[256,1152]{1,0:T(8,128)(2,1)S(1)} %get-tuple-element.61), channel_id=1, source_target_pairs={{0,8},{8,0},{1,9},{9,1},{2,10},{10,2},{3,11},{11,3},{4,12},{12,4},... | collective-permute-start | bytes 1769480 | tf_op jit(solution)/shard_map/ppermute | solution.py:473
  58.0 1.3 %collective-permute-start.18 = (f32[48,128]{1,0:T(8,128)S(1)}, f32[48,128]{1,0:T(8,128)S(1)}, u32[]{:S(2)}, u32[]{:S(2)}) collective-permute-start(f32[48,128]{1,0:T(8,128)S(1)} %tile_attention_and_patches.1.patch_ref), channel_id=1, source_target_pairs={{0,8},{8,0},{1,9},{9,1},{2,10},{10,2},{3,11},{11,3},{4,12},{12,4},... | collective-permute-start | bytes 73736 | tf_op jit(solution)/shard_map/ppermute | solution.py:478
  (4 other events, 24.2 us)

commit v8 on v4

--- a/solution.py
+++ b/solution.py
@@ -118,16 +118,33 @@
     return jnp.where(lane < DA, projected, 0.0).astype(BF16)
 
 
-def project_kernel(n_pieces, *refs):
+def join(refs, target):
+    at = 0
+    for ref in refs:
+        rows = ref.shape[0]
+        target[at : at + rows] = ref[...]
+        at += rows
+
+
+def chunks(first, last, step=256):
+    return [(at, min(at + step, last)) for at in range(first, last, step)]
+
+
+KV_CUTS = chunks(DA, 3 * DA)
+QUERY_CUTS = chunks(0, DA)
+
+
+def project_kernel(n_pieces, n_stale, *refs):
     piece_refs = refs[:n_pieces]
-    vec_ref, own_ref, other_ref, x_ref, q_ref, kv_ref, w_ref, sems = refs[n_pieces:]
+    stale_refs = refs[n_pieces : n_pieces + n_stale]
+    vec_ref, own_ref, other_ref, x_ref, q_ref, kv_ref, stale_ref, w_ref, sems = refs[n_pieces + n_stale :]
     count = x_ref.shape[0]
-    copies = copy_qkv(0, own_ref, other_ref, w_ref, sems)
-    at = 0
-    for ref in piece_refs:
-        rows = ref.shape[0]
-        x_ref[at : at + rows] = ref[...]
-        at += rows
+    copies = [
+        copy_of(0, own_ref.at[0, a:b], other_ref.at[0, a:b], w_ref.at[a:b], sems.at[i])
+        for i, (a, b) in enumerate(KV_CUTS + QUERY_CUTS)
+    ]
+    join(piece_refs, x_ref)
+    join(stale_refs, stale_ref)
     if count > BLOCK:
         for copy in copies:
             copy.wait()
@@ -135,33 +152,42 @@
     def body(start, size):
         rows = pl.ds(start, size)
         modulated = normed(x_ref[rows].astype(F32), vec_ref[1:2], vec_ref[0:1])
+        for i, (a, b) in enumerate(KV_CUTS):
+            if count <= BLOCK:
+                copies[i].wait()
+            kv_ref[rows, a - DA : b - DA] = dot_t(modulated, w_ref[a:b]).astype(BF16)
         if count <= BLOCK:
-            copies[0].wait()
-            copies[1].wait()
-        kv_ref[rows] = dot_t(modulated, w_ref[DA:]).astype(BF16)
+            for copy in copies[len(KV_CUTS) :]:
+                copy.wait()
         q_ref[rows] = query_of(modulated, w_ref)
 
     each_block(count, body)
 
 
-def project(pieces, vecs, w_own, w_other):
+def project(pieces, stale_pieces, vecs, w_own, w_other):
     count = sum(piece.shape[0] for piece in pieces)
+    stale_count = sum(piece.shape[0] for piece in stale_pieces)
     return pl.pallas_call(
-        functools.partial(project_kernel, len(pieces)),
+        functools.partial(project_kernel, len(pieces), len(stale_pieces)),
         out_shape=(
             jax.ShapeDtypeStruct((count, D), BF16),
             jax.ShapeDtypeStruct((count, DP), BF16),
             jax.ShapeDtypeStruct((count, 2 * DA), BF16),
+            jax.ShapeDtypeStruct((stale_count, 2 * DA), BF16),
         ),
-        in_specs=[VMEM] * (len(pieces) + 1) + [ANY] * 2,
-        out_specs=(VMEM,) * 3,
+        in_specs=[VMEM] * (len(pieces) + len(stale_pieces) + 1) + [ANY] * 2,
+        out_specs=(VMEM,) * 4,
         scratch_shapes=[
             pltpu.VMEM((3 * DA, D), BF16),
-            pltpu.SemaphoreType.DMA((2,)),
+            pltpu.SemaphoreType.DMA((len(KV_CUTS) + len(QUERY_CUTS),)),
         ],
         compiler_params=params(count),
         name="layer_norm_and_projections",
-    )(*pieces, vecs, w_own, w_other)
+    )(*pieces, *stale_pieces, vecs, in_hbm(w_own), w_other)
+
+
+def in_hbm(array):
+    return pltpu.with_memory_space_constraint(array, pltpu.HBM)
 
 
 def block_kernel(n_pieces, *refs):
@@ -237,7 +263,9 @@
         ],
         compiler_params=params(count),
         name="attention_and_next_keys",
-    )(*stale_pieces, x, q, kv, got, idx, vecs, w_own, w_other, wo_own, wo_other)
+    )(
+        *stale_pieces, x, q, kv, got, idx, vecs, in_hbm(w_own), w_other, in_hbm(wo_own), wo_other
+    )
 
 
 def tile_kernel(
@@ -272,7 +300,7 @@
         ],
         compiler_params=params(count),
         name="tile_attention_and_patches",
-    )(x, q, kv, got, idx, vecs, w_final, wo_own, wo_other)
+    )(x, q, kv, got, idx, vecs, w_final, in_hbm(wo_own), wo_other)
 
 
 def decode_kernel(
@@ -395,14 +423,6 @@
     return lax.ppermute(block, "patch", route)
 
 
-def gather_outer(own, outer):
-    return jnp.concatenate([own] + [shifted(own, k, 0) for k in range(1, outer)], axis=0)
-
-
-def gather_inner(column, inner):
-    return [column] + [shifted(column, 0, k) for k in range(1, inner)]
-
-
 def local(
     tokens,
     stale_kv,
@@ -432,22 +452,16 @@
     own_tokens = lax.dynamic_index_in_dim(tokens, section, 0, keepdims=False)
     w_qkv = jnp.swapaxes(w_qkv, 1, 2)
     w_qkv_other = lax.ppermute(w_qkv, "pipe", swap)
-    x_column = gather_outer(own_tokens, outer)
-    x_column, own_stale = lax.optimization_barrier((x_column, stale_kv[0, 1]))
-    x_pieces = gather_inner(x_column, inner)
-    stale_pieces = gather_inner(gather_outer(own_stale, outer), inner)
     w_out_other = lax.ppermute(w_out, "pipe", swap)
-    table_other = lax.ppermute(block_table[0], "pipe", swap)
+    tables = lax.all_gather(block_table[0], "pipe")
+    x_column = [shifted(own_tokens, k, 0) for k in range(1, outer)]
 
     time_row = lax.dynamic_index_in_dim(time_table, t_index[0], 0, keepdims=False)
-    table = block_table[0]
-    table_0 = jnp.where(first_core, table, table_other)
-    table_1 = jnp.where(first_core, table_other, table)
     ones = jnp.asarray([[0.0], [1.0], [0.0]], F32)
     vecs = jnp.concatenate(
         [
-            time_row[:3] + table_0 + ones,
-            time_row[:3] + table_1 + ones,
+            time_row[:3] + tables[0] + ones,
+            time_row[:3] + tables[1] + ones,
             time_row[3:5] + ones[:2],
         ],
         axis=0,
@@ -465,10 +479,16 @@
     idx = jnp.broadcast_to(jnp.where(inside, spot, -1)[:, None], (padded_rows, LANES)).astype(jnp.int32)
 
     w_patch = dot(jnp.asarray(patch_selector(), BF16), w_in).astype(BF16)
-    x_pieces, w_patch, idx = lax.optimization_barrier((x_pieces, w_patch, idx))
-
-    x, query, fresh = project(x_pieces, vecs, w_qkv, w_qkv_other)
+
+    x_column, w_qkv_other, w_out_other, vecs, w_patch, idx, own_stale = lax.optimization_barrier(
+        (x_column, w_qkv_other, w_out_other, vecs, w_patch, idx, stale_kv[0, 1])
+    )
+    x_column = jnp.concatenate([own_tokens] + x_column, axis=0)
+    x_pieces = [x_column] + [shifted(x_column, 0, k) for k in range(1, inner)]
+    stale_column = [own_stale] + [shifted(own_stale, k, 0) for k in range(1, outer)]
+    x, query, fresh, stale_column = project(x_pieces, stale_column, vecs, w_qkv, w_qkv_other)
     got = lax.ppermute(fresh, "pipe", [(0, 1)])
+    stale_pieces = [stale_column] + [shifted(stale_column, 0, k) for k in range(1, inner)]
     x_tile, q_tile, fresh, send = first_block(
         stale_pieces, x, query, fresh, got, idx, vecs, w_qkv, w_qkv_other, w_out, w_out_other
     )

time: 59.7 us -> 58.2 us (0.975)
  Pallas kernels: 15.5 us -> 20.2 us
  local copies, waits for them, and re-layouts: 7.17 us -> 2.86 us
  starting transfers between devices: 18.6 us -> 15 us
  blocking collectives: 0 us -> 1.99 us
  other arithmetic: 1.87 us -> 0.83 us
  waiting for transfers between devices: 13.9 us -> 14.8 us
    unnamed x22 -> x13, local copies, waits for them, and re-layouts: 4.41 us -> 0.75 us
    ppermute x8, starting transfers between devices: 15.3 us -> 13 us  [shifted(): return lax.ppermute(block, 'patch', route)]
    pallas_call x1, Pallas kernels: 2.38 us -> 4.54 us  [project(): pl.pallas_call(functools.partial(project_kernel, len(pieces), len(stale_p...]
    all_gather x0 -> x1, blocking collectives: none -> 1.99 us  [local(): tables = lax.all_gather(block_table[0], 'pipe')]
    pallas_call x1, Pallas kernels: 5.48 us -> 7.25 us  [first_block(): pl.pallas_call(functools.partial(block_kernel, len(stale_pieces)), out_sh...]
    concatenate x2, other arithmetic: 1 us -> 0.04 us  [the longest x1 0.02 us: local(): x_column = jnp.concatenate([own_tokens] + x_column, axis=0)]
    ppermute x8, waiting for transfers between devices: 10.9 us -> 11.8 us  [shifted(): return lax.ppermute(block, 'patch', route)]
    pallas_call x1, Pallas kernels: 3.31 us -> 4.1 us  [tile_block(): pl.pallas_call(tile_kernel, out_shape=jax.ShapeDtypeStruct((x.shape[0], L...]
  transfers between devices with their start and end apart: 14 -> 13, of which waited for: 5 -> 5; matrix products, arithmetic and copies ran while one was open for 14% -> 9% of each run, Pallas kernels for 4% -> 0%
where the time goes in v8:
time: 58.2 us; the launch traced here: 57.9 us
  Pallas kernels  20.2 us (35%)
  starting transfers between devices  15 us (26%)
  waiting for transfers between devices  14.8 us (25%)
  local copies, waits for them, and re-layouts  2.86 us (5%)
  blocking collectives  1.99 us (3%)
  matrix products  1.36 us (2%)
  other arithmetic  0.83 us (1%)
  between operations  0.82 us (1%)
    ppermute x8, starting transfers between devices, shifted(): return lax.ppermute(block, 'patch', route)  13 us
    ppermute x8, waiting for transfers between devices, shifted(): return lax.ppermute(block, 'patch', route)  11.8 us
    pallas_call x1, Pallas kernels, first_block(): pl.pallas_call(functools.partial(block_kernel, len(stale_pieces)), out_sh...  7.25 us
    pallas_call x1, Pallas kernels, project(): pl.pallas_call(functools.partial(project_kernel, len(pieces), len(stale_p...  4.54 us
    pallas_call x1, Pallas kernels, decode(): pl.pallas_call(functools.partial(decode_kernel, rows, cols, pitch), out_s...  4.32 us
    pallas_call x1, Pallas kernels, tile_block(): pl.pallas_call(tile_kernel, out_shape=jax.ShapeDtypeStruct((x.shape[0], L...  4.1 us
    ppermute x1, waiting for transfers between devices, local(): got = lax.ppermute(send, 'pipe', swap)  1.99 us
    all_gather x1, blocking collectives, local(): tables = lax.all_gather(block_table[0], 'pipe')  1.99 us
  transfers between devices with their start and end apart: 13, of which 5 were waited for; matrix products, arithmetic and copies ran while one was open for 9% of the time, Pallas kernels for 0%

profile of v8, /device:TPU:0, one launch (start us, length us, event | category | flops | bytes accessed | tf_op | source)
XLA Modules:
  0.0 57.9 jit_solution(11584268476286716861)
XLA Ops:
  0.5 1.1 %dynamic-slice_bitcast_fusion = bf16[32,1152]{1,0:T(8,128)(2,1)S(1)} fusion(bf16[2,32,1152]{2,1,0:T(8,128)(2,1)} %param.14, s32[]{:T(128)S(6)} %select_n.96), kind=kLoop, calls=%fused_computation.3 | loop fusion | bytes 147460 | tf_op jit(solution)/shard_map/jit(dynamic_index_in_dim)/squeeze | solution.py:452
  1.6 2.5 %collective-permute-start.2 = (bf16[32,1152]{1,0:T(8,128)(2,1)S(1)}, bf16[32,1152]{1,0:T(8,128)(2,1)S(1)}, u32[]{:S(2)}, u32[]{:S(2)}) collective-permute-start(bf16[32,1152]{1,0:T(8,128)(2,1)S(1)} %dynamic-slice_bitcast_fusion), channel_id=1, source_target_pairs={{6,0},{7,1},{0,2},{1,3},{2,4},{3,5},{4,6},{5,7},{14,8},{15,9},{8,1... | collective-permute-start | bytes 221192 | tf_op jit(solution)/shard_map/ppermute | solution.py:423
  4.1 2.6 %collective-permute-start.1 = (bf16[32,1152]{1,0:T(8,128)(2,1)S(1)}, bf16[32,1152]{1,0:T(8,128)(2,1)S(1)}, u32[]{:S(2)}, u32[]{:S(2)}) collective-permute-start(bf16[32,1152]{1,0:T(8,128)(2,1)S(1)} %dynamic-slice_bitcast_fusion), channel_id=1, source_target_pairs={{4,0},{5,1},{6,2},{7,3},{0,4},{1,5},{2,6},{3,7},{12,8},{13,9},{14,... | collective-permute-start | bytes 221192 | tf_op jit(solution)/shard_map/ppermute | solution.py:423
  6.7 1.3 %collective-permute-start = (bf16[32,1152]{1,0:T(8,128)(2,1)S(1)}, bf16[32,1152]{1,0:T(8,128)(2,1)S(1)}, u32[]{:S(2)}, u32[]{:S(2)}) collective-permute-start(bf16[32,1152]{1,0:T(8,128)(2,1)S(1)} %dynamic-slice_bitcast_fusion), channel_id=1, source_target_pairs={{2,0},{3,1},{4,2},{5,3},{6,4},{7,5},{0,6},{1,7},{10,8},{11,9},{12,... | collective-permute-start | bytes 221192 | tf_op jit(solution)/shard_map/ppermute | solution.py:423
  8.7 0.7 %copy.18 = f32[1,3,1152]{2,1,0:T(4,128)S(1)} copy(f32[1,3,1152]{2,0,1:T(1,128)} %param.18) | data formatting | bytes 27648 | tf_op args[4]
  9.4 2.0 %all_gather.3 = f32[2,3,1152]{2,1,0:T(4,128)S(1)} all-gather(f32[1,3,1152]{2,1,0:T(4,128)S(1)} %copy.18), channel_id=1, replica_groups=mesh['grp'=2,'pipe'=2,'patch'=8] {'pipe'}, dimensions={0}, use_global_device_ids=true | all-gather | bytes 41472 | tf_op jit(solution)/shard_map/all_gather | solution.py:456
  11.5 0.7 %fusion.1 = (f32[3,1152]{1,0:T(4,128)S(1)}, f32[3,1152]{1,0:T(4,128)S(1)}) fusion(f32[1,3,1152]{2,0,1:T(1,128)S(1)} %constant_dynamic-slice_fusion, f32[2,3,1152]{2,1,0:T(4,128)S(1)} %all_gather.3, f32[3]{0:T(128)} %constant.135), kind=kLoop, calls=%fused_computation.8 | loop fusion | flops 13824 | bytes 69132 | tf_op jit(solution)/shard_map/add | solution.py:463
  12.2 1.4 %convolution_convert_fusion.wp_ref = bf16[1024,512]{1,0:T(8,128)(2,1)S(1)} fusion(bf16[1024,36]{1,0:T(8,128)(2,1)} %constant.129.clone, bf16[36,512]{1,0:T(8,128)(2,1)} %param.22), kind=kOutput, calls=%fused_computation | convolution fusion | flops 38273024 | bytes 1159168 | tf_op jit(solution)/shard_map/dot_general | solution.py:34
  13.6 0.9 %slice_bitcast_fusion.refs_2_ = bf16[32,1152]{1,0:T(8,128)(2,1)S(1)} fusion(bf16[1,2,32,1152]{3,2,1,0:T(8,128)(2,1)} %param.15), kind=kLoop, calls=%fused_computation.2 | loop fusion | bytes 147456 | tf_op jit(solution)/shard_map/squeeze | solution.py:484
  14.7 1.6 %collective-permute-start.5 = (bf16[128,1152]{1,0:T(8,128)(2,1)S(1)}, bf16[128,1152]{1,0:T(8,128)(2,1)S(1)}, u32[]{:S(2)}, u32[]{:S(2)}) collective-permute-start(bf16[128,1152]{1,0:T(8,128)(2,1)S(1)} %pad_maximum_fusion.refs_0_), channel_id=1, source_target_pairs={{1,0},{0,1},{3,2},{2,3},{5,4},{4,5},{7,6},{6,7},{9,8},{8,9},{11,10... | collective-permute-start | bytes 884744 | tf_op jit(solution)/shard_map/ppermute | solution.py:423
  16.3 0.7 %collective-permute-start.8 = (bf16[32,1152]{1,0:T(8,128)(2,1)S(1)}, bf16[32,1152]{1,0:T(8,128)(2,1)S(1)}, u32[]{:S(2)}, u32[]{:S(2)}) collective-permute-start(bf16[32,1152]{1,0:T(8,128)(2,1)S(1)} %slice_bitcast_fusion.refs_2_), channel_id=1, source_target_pairs={{6,0},{7,1},{0,2},{1,3},{2,4},{3,5},{4,6},{5,7},{14,8},{15,9},{8,1... | collective-permute-start | bytes 221192 | tf_op jit(solution)/shard_map/ppermute | solution.py:423
  17.0 2.0 %collective-permute-start.7 = (bf16[32,1152]{1,0:T(8,128)(2,1)S(1)}, bf16[32,1152]{1,0:T(8,128)(2,1)S(1)}, u32[]{:S(2)}, u32[]{:S(2)}) collective-permute-start(bf16[32,1152]{1,0:T(8,128)(2,1)S(1)} %slice_bitcast_fusion.refs_2_), channel_id=1, source_target_pairs={{4,0},{5,1},{6,2},{7,3},{0,4},{1,5},{2,6},{3,7},{12,8},{13,9},{14,... | collective-permute-start | bytes 221192 | tf_op jit(solution)/shard_map/ppermute | solution.py:423
  18.9 1.7 %collective-permute-start.6 = (bf16[32,1152]{1,0:T(8,128)(2,1)S(1)}, bf16[32,1152]{1,0:T(8,128)(2,1)S(1)}, u32[]{:S(2)}, u32[]{:S(2)}) collective-permute-start(bf16[32,1152]{1,0:T(8,128)(2,1)S(1)} %slice_bitcast_fusion.refs_2_), channel_id=1, source_target_pairs={{2,0},{3,1},{4,2},{5,3},{6,4},{7,5},{0,6},{1,7},{10,8},{11,9},{12,... | collective-permute-start | bytes 221192 | tf_op jit(solution)/shard_map/ppermute | solution.py:423
  20.6 2.7 %collective-permute-done.8.refs_5_ = bf16[32,1152]{1,0:T(8,128)(2,1)S(1)} collective-permute-done((bf16[32,1152]{1,0:T(8,128)(2,1)S(1)}, bf16[32,1152]{1,0:T(8,128)(2,1)S(1)}, u32[]{:S(2)}, u32[]{:S(2)}) %collective-permute-start.8) | collective-permute-done | bytes 73760 | tf_op jit(solution)/shard_map/ppermute | solution.py:423
  23.3 2.3 %collective-permute-done.7.refs_4_ = bf16[32,1152]{1,0:T(8,128)(2,1)S(1)} collective-permute-done((bf16[32,1152]{1,0:T(8,128)(2,1)S(1)}, bf16[32,1152]{1,0:T(8,128)(2,1)S(1)}, u32[]{:S(2)}, u32[]{:S(2)}) %collective-permute-start.7) | collective-permute-done | bytes 73760 | tf_op jit(solution)/shard_map/ppermute | solution.py:423
  25.6 4.5 %layer_norm_and_projections.1 = (bf16[256,1152]{1,0:T(8,128)(2,1)S(1)}, bf16[256,640]{1,0:T(8,128)(2,1)S(1)}, bf16[256,1152]{1,0:T(8,128)(2,1)S(1)}, bf16[128,1152]{1,0:T(8,128)(2,1)S(1)}) custom-call(bf16[128,1152]{1,0:T(8,128)(2,1)S(1)} %pad_maximum_fusion.refs_0_, bf16[128,1152]{1,0:T(8,128)(2,1)S(1)} %collective-permute-done.5.refs_1_, ...), custom_call_target="tpu_custom_call" | custom-call | tf_op jit(solution)/shard_map/layer_norm_and_projections/pallas_call | solution.py:170
  30.1 1.3 %collective-permute-start.10 = (bf16[256,1152]{1,0:T(8,128)(2,1)S(1)}, bf16[256,1152]{1,0:T(8,128)(2,1)S(1)}, u32[]{:S(2)}, u32[]{:S(2)}) collective-permute-start(bf16[256,1152]{1,0:T(8,128)(2,1)S(1)} %get-tuple-element.31.refs_4_), channel_id=1, source_target_pairs={{0,8},{1,9},{2,10},{3,11},{4,12},{5,13},{6,14},{7,15},{16,24},{17,... | collective-permute-start | bytes 1769480 | tf_op jit(solution)/shard_map/ppermute | solution.py:490
  31.5 0.6 collective-permute-start.9
  32.0 6.8 %collective-permute-done.9.refs_1_ = bf16[128,1152]{1,0:T(8,128)(2,1)S(1)} collective-permute-done((bf16[128,1152]{1,0:T(8,128)(2,1)S(1)}, bf16[128,1152]{1,0:T(8,128)(2,1)S(1)}, u32[]{:S(2)}, u32[]{:S(2)}) %collective-permute-start.9) | collective-permute-done | bytes 294944 | tf_op jit(solution)/shard_map/ppermute | solution.py:423
  38.8 7.3 %attention_and_next_keys.1 = (bf16[48,1152]{1,0:T(8,128)(2,1)S(1)}, bf16[48,640]{1,0:T(8,128)(2,1)S(1)}, bf16[256,1152]{1,0:T(8,128)(2,1)S(1)}, bf16[256,1152]{1,0:T(8,128)(2,1)S(1)}) custom-call(bf16[128,1152]{1,0:T(8,128)(2,1)S(1)} %get-tuple-element.28.refs_0_, bf16[128,1152]{1,0:T(8,128)(2,1)S(1)} %collective-permute-done.9.refs_1_, ...), custom_call_target="tpu_custom_call" | custom-call | tf_op jit(solution)/shard_map/attention_and_next_keys/pallas_call | solution.py:247
  46.2 2.0 %collective-permute-done.11.got_ref = bf16[256,1152]{1,0:T(8,128)(2,1)S(1)} collective-permute-done((bf16[256,1152]{1,0:T(8,128)(2,1)S(1)}, bf16[256,1152]{1,0:T(8,128)(2,1)S(1)}, u32[]{:S(2)}, u32[]{:S(2)}) %collective-permute-start.11) | collective-permute-done | bytes 589856 | tf_op jit(solution)/shard_map/ppermute | solution.py:495
  48.2 4.1 %tile_attention_and_patches.1.patch_ref = f32[48,128]{1,0:T(8,128)S(1)} custom-call(bf16[48,1152]{1,0:T(8,128)(2,1)S(1)} %get-tuple-element.34.x_ref, bf16[48,640]{1,0:T(8,128)(2,1)S(1)} %get-tuple-element.35.q_ref, bf16[256,1152]{1,0:T(8,128)(2,1)S(1)} %get-tuple-element.36.kv_ref, bf16[256,1152]{1,0:T(8,128)(2,1)S(1)} %collective-permute-done.11.got_ref, ...), custom_call_target="tpu_custom_call" | custom-call | tf_op jit(solution)/shard_map/tile_attention_and_patches/pallas_call | solution.py:291
  52.5 1.1 %collective-permute-done.12.got_ref = f32[48,128]{1,0:T(8,128)S(1)} collective-permute-done((f32[48,128]{1,0:T(8,128)S(1)}, f32[48,128]{1,0:T(8,128)S(1)}, u32[]{:S(2)}, u32[]{:S(2)}) %collective-permute-start.12) | collective-permute-done | bytes 24608 | tf_op jit(solution)/shard_map/ppermute | solution.py:500
  53.6 4.3 %decoder_convolutions.1 = bf16[4,128,512]{2,1,0:T(8,128)(2,1)} custom-call(f32[48,128]{1,0:T(8,128)S(1)} %tile_attention_and_patches.1.patch_ref, f32[48,128]{1,0:T(8,128)S(1)} %collective-permute-done.12.got_ref, s32[48,128]{1,0:T(8,128)S(1)} %broadcast_in_dim.14.refs_6_.idx_ref, bf16[1024,512]{1,0:T(8,128)(2,1)S(1)} %convolution_convert_fusion.wp_ref, ...), custom_call_target="tpu_custom_call" | custom-call | tf_op jit(solution)/shard_map/decoder_convolutions/pallas_call | solution.py:382
  (32 shorter events, 1.0 us)
Async XLA Ops:
  0.0 11.4 %copy-start = (f32[100,5,1152]{2,0,1:T(8,128)S(1)}, f32[100,5,1152]{2,0,1:T(8,128)}, u32[]{:S(2)}) copy-start(f32[100,5,1152]{2,0,1:T(8,128)} %param.19) | copy-start | bytes 6912004
  0.0 14.6 %collective-permute-start.3 = (bf16[1,1728,1152]{2,1,0:T(8,128)(2,1)}, bf16[1,1728,1152]{2,1,0:T(8,128)(2,1)}, u32[]{:S(2)}, u32[]{:S(2)}) collective-permute-start(bf16[1,1728,1152]{2,1,0:T(8,128)(2,1)} %bitcast.31), channel_id=1, source_target_pairs={{0,8},{8,0},{1,9},{9,1},{2,10},{10,2},{3,11},{11,3},{4,12},{12,4},... | collective-permute-start | bytes 11943944 | tf_op jit(solution)/shard_map/ppermute | solution.py:454
  1.6 13.0 %collective-permute-start.2 = (bf16[32,1152]{1,0:T(8,128)(2,1)S(1)}, bf16[32,1152]{1,0:T(8,128)(2,1)S(1)}, u32[]{:S(2)}, u32[]{:S(2)}) collective-permute-start(bf16[32,1152]{1,0:T(8,128)(2,1)S(1)} %dynamic-slice_bitcast_fusion), channel_id=1, source_target_pairs={{6,0},{7,1},{0,2},{1,3},{2,4},{3,5},{4,6},{5,7},{14,8},{15,9},{8,1... | collective-permute-start | bytes 221192 | tf_op jit(solution)/shard_map/ppermute | solution.py:423
  4.1 10.4 %collective-permute-start.1 = (bf16[32,1152]{1,0:T(8,128)(2,1)S(1)}, bf16[32,1152]{1,0:T(8,128)(2,1)S(1)}, u32[]{:S(2)}, u32[]{:S(2)}) collective-permute-start(bf16[32,1152]{1,0:T(8,128)(2,1)S(1)} %dynamic-slice_bitcast_fusion), channel_id=1, source_target_pairs={{4,0},{5,1},{6,2},{7,3},{0,4},{1,5},{2,6},{3,7},{12,8},{13,9},{14,... | collective-permute-start | bytes 221192 | tf_op jit(solution)/shard_map/ppermute | solution.py:423
  6.7 7.9 %collective-permute-start = (bf16[32,1152]{1,0:T(8,128)(2,1)S(1)}, bf16[32,1152]{1,0:T(8,128)(2,1)S(1)}, u32[]{:S(2)}, u32[]{:S(2)}) collective-permute-start(bf16[32,1152]{1,0:T(8,128)(2,1)S(1)} %dynamic-slice_bitcast_fusion), channel_id=1, source_target_pairs={{2,0},{3,1},{4,2},{5,3},{6,4},{7,5},{0,6},{1,7},{10,8},{11,9},{12,... | collective-permute-start | bytes 221192 | tf_op jit(solution)/shard_map/ppermute | solution.py:423
  8.0 6.5 %collective-permute-start.4 = (bf16[1,576,1152]{2,1,0:T(8,128)(2,1)}, bf16[1,576,1152]{2,1,0:T(8,128)(2,1)}, u32[]{:S(2)}, u32[]{:S(2)}) collective-permute-start(bf16[1,576,1152]{2,1,0:T(8,128)(2,1)} %wo_own.1), channel_id=1, source_target_pairs={{0,8},{8,0},{1,9},{9,1},{2,10},{10,2},{3,11},{11,3},{4,12},{12,4},... | collective-permute-start | bytes 3981320 | tf_op jit(solution)/shard_map/ppermute | solution.py:455
  14.7 10.9 %collective-permute-start.5 = (bf16[128,1152]{1,0:T(8,128)(2,1)S(1)}, bf16[128,1152]{1,0:T(8,128)(2,1)S(1)}, u32[]{:S(2)}, u32[]{:S(2)}) collective-permute-start(bf16[128,1152]{1,0:T(8,128)(2,1)S(1)} %pad_maximum_fusion.refs_0_), channel_id=1, source_target_pairs={{1,0},{0,1},{3,2},{2,3},{5,4},{4,5},{7,6},{6,7},{9,8},{8,9},{11,10... | collective-permute-start | bytes 884744 | tf_op jit(solution)/shard_map/ppermute | solution.py:423
  16.3 7.0 %collective-permute-start.8 = (bf16[32,1152]{1,0:T(8,128)(2,1)S(1)}, bf16[32,1152]{1,0:T(8,128)(2,1)S(1)}, u32[]{:S(2)}, u32[]{:S(2)}) collective-permute-start(bf16[32,1152]{1,0:T(8,128)(2,1)S(1)} %slice_bitcast_fusion.refs_2_), channel_id=1, source_target_pairs={{6,0},{7,1},{0,2},{1,3},{2,4},{3,5},{4,6},{5,7},{14,8},{15,9},{8,1... | collective-permute-start | bytes 221192 | tf_op jit(solution)/shard_map/ppermute | solution.py:423
  17.0 8.6 %collective-permute-start.7 = (bf16[32,1152]{1,0:T(8,128)(2,1)S(1)}, bf16[32,1152]{1,0:T(8,128)(2,1)S(1)}, u32[]{:S(2)}, u32[]{:S(2)}) collective-permute-start(bf16[32,1152]{1,0:T(8,128)(2,1)S(1)} %slice_bitcast_fusion.refs_2_), channel_id=1, source_target_pairs={{4,0},{5,1},{6,2},{7,3},{0,4},{1,5},{2,6},{3,7},{12,8},{13,9},{14,... | collective-permute-start | bytes 221192 | tf_op jit(solution)/shard_map/ppermute | solution.py:423
  18.9 6.7 %collective-permute-start.6 = (bf16[32,1152]{1,0:T(8,128)(2,1)S(1)}, bf16[32,1152]{1,0:T(8,128)(2,1)S(1)}, u32[]{:S(2)}, u32[]{:S(2)}) collective-permute-start(bf16[32,1152]{1,0:T(8,128)(2,1)S(1)} %slice_bitcast_fusion.refs_2_), channel_id=1, source_target_pairs={{2,0},{3,1},{4,2},{5,3},{6,4},{7,5},{0,6},{1,7},{10,8},{11,9},{12,... | collective-permute-start | bytes 221192 | tf_op jit(solution)/shard_map/ppermute | solution.py:423
  30.1 8.7 %collective-permute-start.10 = (bf16[256,1152]{1,0:T(8,128)(2,1)S(1)}, bf16[256,1152]{1,0:T(8,128)(2,1)S(1)}, u32[]{:S(2)}, u32[]{:S(2)}) collective-permute-start(bf16[256,1152]{1,0:T(8,128)(2,1)S(1)} %get-tuple-element.31.refs_4_), channel_id=1, source_target_pairs={{0,8},{1,9},{2,10},{3,11},{4,12},{5,13},{6,14},{7,15},{16,24},{17,... | collective-permute-start | bytes 1769480 | tf_op jit(solution)/shard_map/ppermute | solution.py:490
  31.5 7.3 %collective-permute-start.9 = (bf16[128,1152]{1,0:T(8,128)(2,1)S(1)}, bf16[128,1152]{1,0:T(8,128)(2,1)S(1)}, u32[]{:S(2)}, u32[]{:S(2)}) collective-permute-start(bf16[128,1152]{1,0:T(8,128)(2,1)S(1)} %get-tuple-element.28.refs_0_), channel_id=1, source_target_pairs={{1,0},{0,1},{3,2},{2,3},{5,4},{4,5},{7,6},{6,7},{9,8},{8,9},{11,10... | collective-permute-start | bytes 884744 | tf_op jit(solution)/shard_map/ppermute | solution.py:423
  38.8 14.7 %slice-start = ((s8[4718592]{0:T(1024)(128)(4,1)}), s8[4194304]{0:T(1024)(128)(4,1)S(1)}, s32[]{:S(2)}) async-start(s8[4718592]{0:T(1024)(128)(4,1)} %bitcast.26), calls=%async_computation | async-start | bytes 8388608
  38.8 9.4 %copy-start.1 = (bf16[1152,16]{0,1:T(8,128)(2,1)S(1)}, bf16[1152,16]{0,1:T(8,128)(2,1)}, u32[]{:S(2)}) copy-start(bf16[1152,16]{0,1:T(8,128)(2,1)} %param.21) | copy-start | bytes 110596
  38.8 14.7 %slice-start.1 = ((s8[4718592]{0:T(1024)(128)(4,1)}), s8[524288]{0:T(1024)(128)(4,1)S(1)}, s32[]{:S(2)}) async-start(s8[4718592]{0:T(1024)(128)(4,1)} %bitcast.26), calls=%async_computation.1 | async-start | bytes 1048576
  46.1 7.5 %copy-start.2 = (f32[512]{0:T(512)S(1)}, f32[512]{0:T(512)}, u32[]{:S(2)}) copy-start(f32[512]{0:T(512)} %param.23) | copy-start | bytes 6148
  46.1 7.5 %copy-start.3 = (f32[512]{0:T(512)S(1)}, f32[512]{0:T(512)}, u32[]{:S(2)}) copy-start(f32[512]{0:T(512)} %param.25) | copy-start | bytes 6148
  46.1 2.1 %collective-permute-start.11 = (bf16[256,1152]{1,0:T(8,128)(2,1)S(1)}, bf16[256,1152]{1,0:T(8,128)(2,1)S(1)}, u32[]{:S(2)}, u32[]{:S(2)}) collective-permute-start(bf16[256,1152]{1,0:T(8,128)(2,1)S(1)} %get-tuple-element.37), channel_id=1, source_target_pairs={{0,8},{8,0},{1,9},{9,1},{2,10},{10,2},{3,11},{11,3},{4,12},{12,4},... | collective-permute-start | bytes 1769480 | tf_op jit(solution)/shard_map/ppermute | solution.py:495
  52.3 1.3 %collective-permute-start.12 = (f32[48,128]{1,0:T(8,128)S(1)}, f32[48,128]{1,0:T(8,128)S(1)}, u32[]{:S(2)}, u32[]{:S(2)}) collective-permute-start(f32[48,128]{1,0:T(8,128)S(1)} %tile_attention_and_patches.1.patch_ref), channel_id=1, source_target_pairs={{0,8},{8,0},{1,9},{9,1},{2,10},{10,2},{3,11},{11,3},{4,12},{12,4},... | collective-permute-start | bytes 73736 | tf_op jit(solution)/shard_map/ppermute | solution.py:500

commit v9 on v8

--- a/solution.py
+++ b/solution.py
@@ -87,29 +87,43 @@
     return pltpu.CompilerParams(vmem_limit_bytes=(24 if count <= BLOCK else 56) * 1024 * 1024)
 
 
-def copy_of(block, own, other, target, sem):
-    section = lax.axis_index("pipe")
-
-    @pl.when(section == block)
-    def _():
-        pltpu.make_async_copy(own, target, sem).start()
-
-    @pl.when(section != block)
-    def _():
-        pltpu.make_async_copy(other, target, sem).start()
-
-    return pltpu.make_async_copy(own, target, sem)
-
-
-def copy_qkv(block, own_ref, other_ref, w_ref, sems):
-    return [
-        copy_of(block, own_ref.at[0, a:b], other_ref.at[0, a:b], w_ref.at[a:b], sems.at[i])
-        for i, (a, b) in enumerate(((0, DA), (DA, 3 * DA)))
-    ]
-
-
-def copy_out(block, own_ref, other_ref, wo_ref, sem):
-    return copy_of(block, own_ref.at[0], other_ref.at[0], wo_ref.at[SHIFT:DP], sem)
+def weights_kernel(own_ref, other_ref, wo_own, wo_other, w0_ref, w1_ref, wo0_ref, wo1_ref, sems):
+    first = lax.axis_index("pipe") == 0
+    pad = jnp.zeros((SHIFT, D), BF16)
+    wo0_ref[:SHIFT] = pad
+    wo1_ref[:SHIFT] = pad
+    outs = (wo0_ref.at[SHIFT:], wo1_ref.at[SHIFT:])
+    copies = []
+    for i, (in_place, arrived, targets) in enumerate(
+        ((own_ref.at[0], other_ref.at[0], (w0_ref, w1_ref)), (wo_own.at[0], wo_other.at[0], outs))
+    ):
+        for block in range(2):
+            own = (first if block == 0 else jnp.logical_not(first))
+            sem = sems.at[2 * i + block]
+            copies.append(pltpu.make_async_copy(in_place, targets[block], sem))
+
+            @pl.when(own)
+            def _():
+                pltpu.make_async_copy(in_place, targets[block], sem).start()
+
+            @pl.when(jnp.logical_not(own))
+            def _():
+                pltpu.make_async_copy(arrived, targets[block], sem).start()
+
+    for copy in copies:
+        copy.wait()
+
+
+def weights_in_vmem(w_own, w_other, wo_own, wo_other):
+    return pl.pallas_call(
+        weights_kernel,
+        out_shape=(jax.ShapeDtypeStruct((3 * DA, D), BF16),) * 2 + (jax.ShapeDtypeStruct((DP, D), BF16),) * 2,
+        in_specs=[ANY] * 4,
+        out_specs=(VMEM,) * 4,
+        scratch_shapes=[pltpu.SemaphoreType.DMA((4,))],
+        compiler_params=params(0),
+        name="weights_by_block",
+    )(in_hbm(w_own), w_other, in_hbm(wo_own), wo_other)
 
 
 def query_of(modulated, w_ref):
@@ -126,105 +140,78 @@
         at += rows
 
 
-def chunks(first, last, step=256):
-    return [(at, min(at + step, last)) for at in range(first, last, step)]
-
-
-KV_CUTS = chunks(DA, 3 * DA)
-QUERY_CUTS = chunks(0, DA)
-
-
-def project_kernel(n_pieces, n_stale, *refs):
+def project_kernel(n_pieces, *refs):
     piece_refs = refs[:n_pieces]
-    stale_refs = refs[n_pieces : n_pieces + n_stale]
-    vec_ref, own_ref, other_ref, x_ref, q_ref, kv_ref, stale_ref, w_ref, sems = refs[n_pieces + n_stale :]
-    count = x_ref.shape[0]
-    copies = [
-        copy_of(0, own_ref.at[0, a:b], other_ref.at[0, a:b], w_ref.at[a:b], sems.at[i])
-        for i, (a, b) in enumerate(KV_CUTS + QUERY_CUTS)
-    ]
+    vec_ref, w_ref, x_ref, q_ref, kv_ref = refs[n_pieces:]
     join(piece_refs, x_ref)
-    join(stale_refs, stale_ref)
-    if count > BLOCK:
-        for copy in copies:
-            copy.wait()
 
     def body(start, size):
         rows = pl.ds(start, size)
         modulated = normed(x_ref[rows].astype(F32), vec_ref[1:2], vec_ref[0:1])
-        for i, (a, b) in enumerate(KV_CUTS):
-            if count <= BLOCK:
-                copies[i].wait()
-            kv_ref[rows, a - DA : b - DA] = dot_t(modulated, w_ref[a:b]).astype(BF16)
-        if count <= BLOCK:
-            for copy in copies[len(KV_CUTS) :]:
-                copy.wait()
+        kv_ref[rows] = dot_t(modulated, w_ref[DA:]).astype(BF16)
         q_ref[rows] = query_of(modulated, w_ref)
 
-    each_block(count, body)
-
-
-def project(pieces, stale_pieces, vecs, w_own, w_other):
+    each_block(x_ref.shape[0], body)
+
+
+def project(pieces, vecs, weights):
     count = sum(piece.shape[0] for piece in pieces)
-    stale_count = sum(piece.shape[0] for piece in stale_pieces)
     return pl.pallas_call(
-        functools.partial(project_kernel, len(pieces), len(stale_pieces)),
+        functools.partial(project_kernel, len(pieces)),
         out_shape=(
             jax.ShapeDtypeStruct((count, D), BF16),
             jax.ShapeDtypeStruct((count, DP), BF16),
             jax.ShapeDtypeStruct((count, 2 * DA), BF16),
-            jax.ShapeDtypeStruct((stale_count, 2 * DA), BF16),
         ),
-        in_specs=[VMEM] * (len(pieces) + len(stale_pieces) + 1) + [ANY] * 2,
-        out_specs=(VMEM,) * 4,
-        scratch_shapes=[
-            pltpu.VMEM((3 * DA, D), BF16),
-            pltpu.SemaphoreType.DMA((len(KV_CUTS) + len(QUERY_CUTS),)),
-        ],
+        in_specs=[VMEM] * (len(pieces) + 2),
+        out_specs=(VMEM,) * 3,
         compiler_params=params(count),
         name="layer_norm_and_projections",
-    )(*pieces, *stale_pieces, vecs, in_hbm(w_own), w_other)
+    )(*pieces, vecs, weights)
 
 
 def in_hbm(array):
     return pltpu.with_memory_space_constraint(array, pltpu.HBM)
 
 
-def block_kernel(n_pieces, *refs):
+def block_kernel(n_pieces, n_got, *refs):
     stale_refs = refs[:n_pieces]
+    got_refs = refs[n_pieces : n_pieces + n_got]
     (
-        x_ref, q_ref, kv_ref, got_ref, idx_ref, vec_ref, w_own, w_other, wo_own, wo_other,
-        xt_ref, qt_ref, kv1_ref, send_ref, w_ref, wo_ref, all_ref, pick_ref, sems,
-    ) = refs[n_pieces:]
+        x_ref, q_ref, kv_ref, idx_ref, vec_ref, w0_ref, w1_ref, wo_ref,
+        xt_ref, qt_ref, kv1_ref, send_ref, all_ref, pick_ref,
+    ) = refs[n_pieces + n_got :]
     count = x_ref.shape[0]
-    out_copy = copy_out(0, wo_own, wo_other, wo_ref, sems.at[2])
-    in_copies = copy_qkv(1, w_own, w_other, w_ref, sems)
     first_core = lax.axis_index("pipe") == 0
-    wo_ref[:SHIFT] = jnp.zeros((SHIFT, D), BF16)
     all_ref[:count] = kv_ref[...]
-    at = 0
-    for ref in stale_refs:
-        rows = ref.shape[0]
-        all_ref[count + at : count + at + rows] = jnp.where(first_core, ref[...], got_ref[at : at + rows])
-        send_ref[at : at + rows] = ref[...]
-        at += rows
+    join(stale_refs, send_ref)
+
+    @pl.when(first_core)
+    def _():
+        join(stale_refs, all_ref.at[count:])
+
+    @pl.when(jnp.logical_not(first_core))
+    def _():
+        at = count
+        for ref in got_refs:
+
+            def body(start, size):
+                modulated = normed(ref[pl.ds(start, size)].astype(F32), vec_ref[1:2], vec_ref[0:1])
+                all_ref[pl.ds(at + start, size)] = dot_t(modulated, w0_ref[DA:]).astype(BF16)
+
+            each_block(ref.shape[0], body)
+            at += ref.shape[0]
+
     pick_ref[...] = jnp.zeros_like(pick_ref)
     tile_rows = idx_ref.shape[0]
-    waits = [out_copy] + in_copies
-    if count > BLOCK:
-        for copy in waits:
-            copy.wait()
 
     def body(start, size):
         rows = pl.ds(start, size)
         attended = attend(q_ref[rows], all_ref).astype(BF16)
-        if count <= BLOCK:
-            for copy in waits:
-                copy.wait()
         branch = dot(attended, wo_ref[...])
         x1 = (x_ref[rows].astype(F32) + vec_ref[2:3] * branch).astype(BF16)
         modulated = normed(x1.astype(F32), vec_ref[4:5], vec_ref[3:4])
-        fresh = dot_t(modulated, w_ref[DA:]).astype(BF16)
+        fresh = dot_t(modulated, w1_ref[DA:]).astype(BF16)
         kv1_ref[rows] = fresh
 
         @pl.when(first_core)
@@ -238,46 +225,36 @@
 
     each_block(count, body)
     xt_ref[...] = pick_ref[0].astype(BF16)
-    qt_ref[...] = query_of(pick_ref[1].astype(BF16), w_ref)
-
-
-def first_block(stale_pieces, x, q, kv, got, idx, vecs, w_own, w_other, wo_own, wo_other):
+    qt_ref[...] = query_of(pick_ref[1].astype(BF16), w1_ref)
+
+
+def first_block(stale_pieces, got_pieces, x, q, kv, idx, vecs, w_block, w_next, wo_block):
     count = x.shape[0]
     tile_rows = idx.shape[0]
     return pl.pallas_call(
-        functools.partial(block_kernel, len(stale_pieces)),
+        functools.partial(block_kernel, len(stale_pieces), len(got_pieces)),
         out_shape=(
             jax.ShapeDtypeStruct((tile_rows, D), BF16),
             jax.ShapeDtypeStruct((tile_rows, DP), BF16),
             jax.ShapeDtypeStruct((count, 2 * DA), BF16),
             jax.ShapeDtypeStruct((count, 2 * DA), BF16),
         ),
-        in_specs=[VMEM] * (len(stale_pieces) + 6) + [ANY] * 4,
+        in_specs=[VMEM] * (len(stale_pieces) + len(got_pieces) + 8),
         out_specs=(VMEM,) * 4,
         scratch_shapes=[
-            pltpu.VMEM((3 * DA, D), BF16),
-            pltpu.VMEM((DP, D), BF16),
             pltpu.VMEM((2 * count, 2 * DA), BF16),
             pltpu.VMEM((2, tile_rows, D), F32),
-            pltpu.SemaphoreType.DMA((3,)),
         ],
         compiler_params=params(count),
         name="attention_and_next_keys",
-    )(
-        *stale_pieces, x, q, kv, got, idx, vecs, in_hbm(w_own), w_other, in_hbm(wo_own), wo_other
-    )
-
-
-def tile_kernel(
-    x_ref, q_ref, kv_ref, got_ref, idx_ref, vec_ref, wf_ref, wo_own, wo_other, patch_ref, wo_ref, all_ref, sems
-):
+    )(*stale_pieces, *got_pieces, x, q, kv, idx, vecs, w_block, w_next, wo_block)
+
+
+def tile_kernel(x_ref, q_ref, kv_ref, got_ref, idx_ref, vec_ref, wf_ref, wo_ref, patch_ref, all_ref):
     count = kv_ref.shape[0]
-    out_copy = copy_out(1, wo_own, wo_other, wo_ref, sems.at[0])
-    wo_ref[:SHIFT] = jnp.zeros((SHIFT, D), BF16)
     all_ref[:count] = kv_ref[...]
     all_ref[count:] = got_ref[...]
     attended = attend(q_ref[...], all_ref).astype(BF16)
-    out_copy.wait()
     branch = dot(attended, wo_ref[...])
     x2 = (x_ref[...].astype(F32) + vec_ref[5:6] * branch).astype(BF16)
     final = normed(x2.astype(F32), vec_ref[7:8], vec_ref[6:7])
@@ -286,30 +263,22 @@
     patch_ref[:, : 4 * LATC] = jnp.where(idx_ref[:, :1] >= 0, patches, 0.0)
 
 
-def tile_block(x, q, kv, got, idx, vecs, w_final, wo_own, wo_other):
+def tile_block(x, q, kv, got, idx, vecs, w_final, wo_block):
     count = kv.shape[0]
     return pl.pallas_call(
         tile_kernel,
         out_shape=jax.ShapeDtypeStruct((x.shape[0], LANES), F32),
-        in_specs=[VMEM] * 7 + [ANY] * 2,
+        in_specs=[VMEM] * 8,
         out_specs=VMEM,
-        scratch_shapes=[
-            pltpu.VMEM((DP, D), BF16),
-            pltpu.VMEM((2 * count, 2 * DA), BF16),
-            pltpu.SemaphoreType.DMA((1,)),
-        ],
+        scratch_shapes=[pltpu.VMEM((2 * count, 2 * DA), BF16)],
         compiler_params=params(count),
         name="tile_attention_and_patches",
-    )(x, q, kv, got, idx, vecs, w_final, in_hbm(wo_own), wo_other)
+    )(x, q, kv, got, idx, vecs, w_final, wo_block)
 
 
 def decode_kernel(
-    rows, cols, pitch, patch_ref, got_ref, idx_ref, wp_ref, bin_ref, bup_ref, w_any, out_ref, w_ref, u_ref, ub_ref, sems
+    rows, cols, pitch, patch_ref, got_ref, idx_ref, wp_ref, bin_ref, bup_ref, w_ref, out_ref, u_ref, ub_ref
 ):
-    copies = [pltpu.make_async_copy(w_any.at[t], w_ref.at[t], sems.at[t]) for t in range(9)]
-    order = [3, 4, 5, 0, 1, 2, 6, 7, 8]
-    for t in order:
-        copies[t].start()
     first_core = lax.axis_index("pipe") == 0
     got = got_ref[:pitch]
     above = jnp.where(first_core, 0.0, got)
@@ -361,7 +330,6 @@
     def tap_row(dy, y_first, y_count):
         total = None
         for dx in range(3):
-            copies[3 * dy + dx].wait()
             part = dot(ub_ref[dx, y_first * wide : (y_first + y_count) * wide], w_ref[3 * dy + dx])
             total = part if total is None else total + part
         return total
@@ -382,13 +350,11 @@
     return pl.pallas_call(
         functools.partial(decode_kernel, rows, cols, pitch),
         out_shape=jax.ShapeDtypeStruct((4 * rows, 4 * cols, CH), BF16),
-        in_specs=[VMEM] * 6 + [ANY],
+        in_specs=[VMEM] * 7,
         out_specs=VMEM,
         scratch_shapes=[
-            pltpu.VMEM((9, CH, CH), BF16),
             pltpu.VMEM((2 * rows + 2, CH // LANES, 4 * pitch, LANES), F32),
             pltpu.VMEM((3, (2 * rows + 2) * 4 * cols, CH), BF16),
-            pltpu.SemaphoreType.DMA((9,)),
         ],
         compiler_params=params(0),
         name="decoder_convolutions",
@@ -452,7 +418,6 @@
     own_tokens = lax.dynamic_index_in_dim(tokens, section, 0, keepdims=False)
     w_qkv = jnp.swapaxes(w_qkv, 1, 2)
     w_qkv_other = lax.ppermute(w_qkv, "pipe", swap)
-    w_out_other = lax.ppermute(w_out, "pipe", swap)
     tables = lax.all_gather(block_table[0], "pipe")
     x_column = [shifted(own_tokens, k, 0) for k in range(1, outer)]
 
@@ -478,22 +443,27 @@
     spot = (k_inner * outer + k_outer) * own_count + token % own_count
     idx = jnp.broadcast_to(jnp.where(inside, spot, -1)[:, None], (padded_rows, LANES)).astype(jnp.int32)
 
+    x_column, w_qkv_other, vecs, idx, own_stale, w_in, w_out = lax.optimization_barrier(
+        (x_column, w_qkv_other, vecs, idx, stale_kv[0, 1], w_in, w_out)
+    )
     w_patch = dot(jnp.asarray(patch_selector(), BF16), w_in).astype(BF16)
-
-    x_column, w_qkv_other, w_out_other, vecs, w_patch, idx, own_stale = lax.optimization_barrier(
-        (x_column, w_qkv_other, w_out_other, vecs, w_patch, idx, stale_kv[0, 1])
-    )
     x_column = jnp.concatenate([own_tokens] + x_column, axis=0)
+    x_column, own_stale, w_out = lax.optimization_barrier((x_column, own_stale, w_out))
     x_pieces = [x_column] + [shifted(x_column, 0, k) for k in range(1, inner)]
     stale_column = [own_stale] + [shifted(own_stale, k, 0) for k in range(1, outer)]
-    x, query, fresh, stale_column = project(x_pieces, stale_column, vecs, w_qkv, w_qkv_other)
-    got = lax.ppermute(fresh, "pipe", [(0, 1)])
+    w_out_other = lax.ppermute(w_out, "pipe", swap)
+    w_0, w_1, wo_0, wo_1 = weights_in_vmem(w_qkv, w_qkv_other, w_out, w_out_other)
+    x_pieces, stale_column, w_patch, w_0 = lax.optimization_barrier((x_pieces, stale_column, w_patch, w_0))
+    stale_column = jnp.concatenate(stale_column, axis=0)
+    x_pieces, stale_column, w_patch = lax.optimization_barrier((x_pieces, stale_column, w_patch))
+    got_pieces = [lax.ppermute(piece, "pipe", [(0, 1)]) for piece in x_pieces]
+    x, query, fresh = project(x_pieces, vecs, w_0)
     stale_pieces = [stale_column] + [shifted(stale_column, 0, k) for k in range(1, inner)]
     x_tile, q_tile, fresh, send = first_block(
-        stale_pieces, x, query, fresh, got, idx, vecs, w_qkv, w_qkv_other, w_out, w_out_other
+        stale_pieces, got_pieces, x, query, fresh, idx, vecs, w_0, w_1, wo_0
     )
     got = lax.ppermute(send, "pipe", swap)
-    patches = tile_block(x_tile, q_tile, fresh, got, idx, vecs, w_final.T, w_out, w_out_other)
+    patches = tile_block(x_tile, q_tile, fresh, got, idx, vecs, w_final.T, wo_1)
     edge = patches
     if rows > 1:
         edge = jnp.where(first_core, patches[(rows - 1) * pitch : rows * pitch], patches[:pitch])

time: 58.2 us -> 51.4 us (0.88)
  waiting for transfers between devices: 14.8 us -> 11.1 us
  Pallas kernels: 20.2 us -> 16.7 us
    ppermute x8, waiting for transfers between devices: 11.8 us -> 8.47 us  [shifted(): return lax.ppermute(block, 'patch', route)]
    ppermute x8, starting transfers between devices: 13 us -> 11.5 us  [shifted(): return lax.ppermute(block, 'patch', route)]
    ppermute x1 -> x2, starting transfers between devices: 1.33 us -> 2.77 us  [local(): got_pieces = [lax.ppermute(piece, 'pipe', [(0, 1)]) for piece in x_pieces]]
    pallas_call x2 -> x3, Pallas kernels: 11.8 us -> 10.5 us  [the longest x1 4.93 us: first_block(): pl.pallas_call(functools.partial(block_kernel, len(stale_pieces), len(got...]
    pallas_call x1, Pallas kernels: 4.32 us -> 3.14 us  [decode(): pl.pallas_call(functools.partial(decode_kernel, rows, cols, pitch), out_s...]
    pallas_call x1, Pallas kernels: 4.1 us -> 3.05 us  [tile_block(): pl.pallas_call(tile_kernel, out_shape=jax.ShapeDtypeStruct((x.shape[0], L...]
  transfers between devices with their start and end apart: 13 -> 14, of which waited for: 5 -> 5; matrix products, arithmetic and copies ran while one was open for 9% -> 10% of each run, Pallas kernels for 0% -> 11%
where the time goes in v9:
time: 51.4 us; the launch traced here: 51.1 us
  Pallas kernels  16.7 us (32%)
  starting transfers between devices  15.5 us (30%)
  waiting for transfers between devices  11.1 us (22%)
  local copies, waits for them, and re-layouts  2.86 us (6%)
  blocking collectives  1.82 us (4%)
  matrix products  1.37 us (3%)
  other arithmetic  0.86 us (2%)
  between operations  0.84 us (2%)
    ppermute x8, starting transfers between devices, shifted(): return lax.ppermute(block, 'patch', route)  11.5 us
    ppermute x8, waiting for transfers between devices, shifted(): return lax.ppermute(block, 'patch', route)  8.47 us
    pallas_call x1, Pallas kernels, first_block(): pl.pallas_call(functools.partial(block_kernel, len(stale_pieces), len(got...  4.93 us
    pallas_call x1, Pallas kernels, weights_in_vmem(): pl.pallas_call(weights_kernel, out_shape=(jax.ShapeDtypeStruct((3 * DA, D...  3.71 us
    pallas_call x1, Pallas kernels, decode(): pl.pallas_call(functools.partial(decode_kernel, rows, cols, pitch), out_s...  3.14 us
    pallas_call x1, Pallas kernels, tile_block(): pl.pallas_call(tile_kernel, out_shape=jax.ShapeDtypeStruct((x.shape[0], L...  3.05 us
    ppermute x2, starting transfers between devices, local(): got_pieces = [lax.ppermute(piece, 'pipe', [(0, 1)]) for piece in x_pieces]  2.77 us
    pallas_call x1, Pallas kernels, project(): pl.pallas_call(functools.partial(project_kernel, len(pieces)), out_shape=...  1.87 us
  transfers between devices with their start and end apart: 14, of which 5 were waited for; matrix products, arithmetic and copies ran while one was open for 10% of the time, Pallas kernels for 11%

profile of v9, /device:TPU:0, one launch (start us, length us, event | category | flops | bytes accessed | tf_op | source)
XLA Modules:
  0.0 51.1 jit_solution(2115385601281384265)
XLA Ops:
  0.5 1.1 %dynamic-slice_bitcast_fusion = bf16[32,1152]{1,0:T(8,128)(2,1)S(1)} fusion(bf16[2,32,1152]{2,1,0:T(8,128)(2,1)} %param.14, s32[]{:T(128)S(6)} %select_n.96), kind=kLoop, calls=%fused_computation.5 | loop fusion | bytes 147460 | tf_op jit(solution)/shard_map/jit(dynamic_index_in_dim)/squeeze | solution.py:418
  1.6 4.6 %collective-permute-start = (bf16[32,1152]{1,0:T(8,128)(2,1)S(1)}, bf16[32,1152]{1,0:T(8,128)(2,1)S(1)}, u32[]{:S(2)}, u32[]{:S(2)}) collective-permute-start(bf16[32,1152]{1,0:T(8,128)(2,1)S(1)} %dynamic-slice_bitcast_fusion), channel_id=1, source_target_pairs={{2,0},{3,1},{4,2},{5,3},{6,4},{7,5},{0,6},{1,7},{10,8},{11,9},{12,... | collective-permute-start | bytes 221192 | tf_op jit(solution)/shard_map/ppermute | solution.py:389
  6.1 1.0 %collective-permute-start.2 = (bf16[32,1152]{1,0:T(8,128)(2,1)S(1)}, bf16[32,1152]{1,0:T(8,128)(2,1)S(1)}, u32[]{:S(2)}, u32[]{:S(2)}) collective-permute-start(bf16[32,1152]{1,0:T(8,128)(2,1)S(1)} %dynamic-slice_bitcast_fusion), channel_id=1, source_target_pairs={{6,0},{7,1},{0,2},{1,3},{2,4},{3,5},{4,6},{5,7},{14,8},{15,9},{8,1... | collective-permute-start | bytes 221192 | tf_op jit(solution)/shard_map/ppermute | solution.py:389
  7.8 0.7 %copy.19 = f32[1,3,1152]{2,1,0:T(4,128)S(1)} copy(f32[1,3,1152]{2,0,1:T(1,128)} %param.18) | data formatting | bytes 27648 | tf_op args[4]
  8.5 1.8 %all_gather.3 = f32[2,3,1152]{2,1,0:T(4,128)S(1)} all-gather(f32[1,3,1152]{2,1,0:T(4,128)S(1)} %copy.19), channel_id=1, replica_groups=mesh['grp'=2,'pipe'=2,'patch'=8] {'pipe'}, dimensions={0}, use_global_device_ids=true | all-gather | bytes 41472 | tf_op jit(solution)/shard_map/all_gather | solution.py:421
  10.4 0.7 %fusion.2 = (f32[3,1152]{1,0:T(4,128)S(1)}, f32[3,1152]{1,0:T(4,128)S(1)}) fusion(f32[1,3,1152]{2,0,1:T(1,128)S(1)} %constant_dynamic-slice_fusion, f32[2,3,1152]{2,1,0:T(4,128)S(1)} %all_gather.3, f32[3]{0:T(128)} %constant.135), kind=kLoop, calls=%fused_computation.10 | loop fusion | flops 13824 | bytes 69132 | tf_op jit(solution)/shard_map/add | solution.py:428
  11.2 0.9 %slice_bitcast_fusion = bf16[32,1152]{1,0:T(8,128)(2,1)S(1)} fusion(bf16[1,2,32,1152]{3,2,1,0:T(8,128)(2,1)} %param.15), kind=kLoop, calls=%fused_computation.4 | loop fusion | bytes 147456 | tf_op jit(solution)/shard_map/squeeze | solution.py:447
  12.1 1.7 %collective-permute-done.1 = bf16[32,1152]{1,0:T(8,128)(2,1)S(1)} collective-permute-done((bf16[32,1152]{1,0:T(8,128)(2,1)S(1)}, bf16[32,1152]{1,0:T(8,128)(2,1)S(1)}, u32[]{:S(2)}, u32[]{:S(2)}) %collective-permute-start.1) | collective-permute-done | bytes 73760 | tf_op jit(solution)/shard_map/ppermute | solution.py:389
  14.0 1.6 %collective-permute-start.4 = (bf16[128,1152]{1,0:T(8,128)(2,1)S(1)}, bf16[128,1152]{1,0:T(8,128)(2,1)S(1)}, u32[]{:S(2)}, u32[]{:S(2)}) collective-permute-start(bf16[128,1152]{1,0:T(8,128)(2,1)S(1)} %pad_maximum_fusion.refs_0_), channel_id=1, source_target_pairs={{1,0},{0,1},{3,2},{2,3},{5,4},{4,5},{7,6},{6,7},{9,8},{8,9},{11,10... | collective-permute-start | bytes 884744 | tf_op jit(solution)/shard_map/ppermute | solution.py:389
  15.6 1.8 %collective-permute-start.5 = (bf16[32,1152]{1,0:T(8,128)(2,1)S(1)}, bf16[32,1152]{1,0:T(8,128)(2,1)S(1)}, u32[]{:S(2)}, u32[]{:S(2)}) collective-permute-start(bf16[32,1152]{1,0:T(8,128)(2,1)S(1)} %slice_bitcast_fusion), channel_id=1, source_target_pairs={{2,0},{3,1},{4,2},{5,3},{6,4},{7,5},{0,6},{1,7},{10,8},{11,9},{12,... | collective-permute-start | bytes 221192 | tf_op jit(solution)/shard_map/ppermute | solution.py:389
  17.9 1.4 %collective-permute-start.7 = (bf16[32,1152]{1,0:T(8,128)(2,1)S(1)}, bf16[32,1152]{1,0:T(8,128)(2,1)S(1)}, u32[]{:S(2)}, u32[]{:S(2)}) collective-permute-start(bf16[32,1152]{1,0:T(8,128)(2,1)S(1)} %slice_bitcast_fusion), channel_id=1, source_target_pairs={{6,0},{7,1},{0,2},{1,3},{2,4},{3,5},{4,6},{5,7},{14,8},{15,9},{8,1... | collective-permute-start | bytes 221192 | tf_op jit(solution)/shard_map/ppermute | solution.py:389
  19.4 1.4 %fusion.wp_ref = bf16[1024,512]{1,0:T(8,128)(2,1)S(1)} fusion(bf16[36,512]{1,0:T(8,128)(2,1)} %param.22, bf16[1024,36]{1,0:T(8,128)(2,1)} %constant.129.clone), kind=kOutput, calls=%fused_computation.1 | convolution fusion | flops 38273024 | bytes 1159168 | tf_op jit(solution)/shard_map/dot_general | solution.py:34
  20.8 3.7 %weights_by_block.1 = (bf16[1728,1152]{1,0:T(8,128)(2,1)S(1)}, bf16[1728,1152]{1,0:T(8,128)(2,1)S(1)}, bf16[640,1152]{1,0:T(8,128)(2,1)S(1)}, bf16[640,1152]{1,0:T(8,128)(2,1)S(1)}) custom-call(bf16[1,1728,1152]{2,1,0:T(8,128)(2,1)} %bitcast.34, bf16[1,1728,1152]{2,1,0:T(8,128)(2,1)} %collective-permute-done.3.other_ref, bf16[1,576,1152]{2,1,0:T(8,128)(2,1)} %wo_own, ...), custom_call_target="tpu_custom_call" | custom-call | tf_op jit(solution)/shard_map/weights_by_block/pallas_call | solution.py:118
  24.5 0.9 %collective-permute-done.6 = bf16[32,1152]{1,0:T(8,128)(2,1)S(1)} collective-permute-done((bf16[32,1152]{1,0:T(8,128)(2,1)S(1)}, bf16[32,1152]{1,0:T(8,128)(2,1)S(1)}, u32[]{:S(2)}, u32[]{:S(2)}) %collective-permute-start.6) | collective-permute-done | bytes 73760 | tf_op jit(solution)/shard_map/ppermute | solution.py:389
  25.4 1.5 %collective-permute-start.10 = (bf16[128,1152]{1,0:T(8,128)(2,1)S(1)}, bf16[128,1152]{1,0:T(8,128)(2,1)S(1)}, u32[]{:S(2)}, u32[]{:S(2)}) collective-permute-start(bf16[128,1152]{1,0:T(8,128)(2,1)S(1)} %pad_maximum_fusion.refs_0_), channel_id=1, source_target_pairs={{0,8},{1,9},{2,10},{3,11},{4,12},{5,13},{6,14},{7,15},{16,24},{17,... | collective-permute-start | bytes 884744 | tf_op jit(solution)/shard_map/ppermute | solution.py:459
  26.9 1.3 %collective-permute-start.11 = (bf16[128,1152]{1,0:T(8,128)(2,1)S(1)}, bf16[128,1152]{1,0:T(8,128)(2,1)S(1)}, u32[]{:S(2)}, u32[]{:S(2)}) collective-permute-start(bf16[128,1152]{1,0:T(8,128)(2,1)S(1)} %collective-permute-done.4.refs_1_), channel_id=1, source_target_pairs={{0,8},{1,9},{2,10},{3,11},{4,12},{5,13},{6,14},{7,15},{16,24},{17,... | collective-permute-start | bytes 884744 | tf_op jit(solution)/shard_map/ppermute | solution.py:459
  28.2 0.6 %collective-permute-start.9 = (bf16[128,1152]{1,0:T(8,128)(2,1)S(1)}, bf16[128,1152]{1,0:T(8,128)(2,1)S(1)}, u32[]{:S(2)}, u32[]{:S(2)}) collective-permute-start(bf16[128,1152]{1,0:T(8,128)(2,1)S(1)} %pad_maximum_fusion.1.refs_0_), channel_id=1, source_target_pairs={{1,0},{0,1},{3,2},{2,3},{5,4},{4,5},{7,6},{6,7},{9,8},{8,9},{11,10... | collective-permute-start | bytes 884744 | tf_op jit(solution)/shard_map/ppermute | solution.py:389
  28.8 1.9 %layer_norm_and_projections.1 = (bf16[256,1152]{1,0:T(8,128)(2,1)S(1)}, bf16[256,640]{1,0:T(8,128)(2,1)S(1)}, bf16[256,1152]{1,0:T(8,128)(2,1)S(1)}) custom-call(bf16[128,1152]{1,0:T(8,128)(2,1)S(1)} %pad_maximum_fusion.refs_0_, bf16[128,1152]{1,0:T(8,128)(2,1)S(1)} %collective-permute-done.4.refs_1_, ...), custom_call_target="tpu_custom_call" | custom-call | tf_op jit(solution)/shard_map/layer_norm_and_projections/pallas_call | solution.py:159
  30.7 5.9 %collective-permute-done.9.refs_1_ = bf16[128,1152]{1,0:T(8,128)(2,1)S(1)} collective-permute-done((bf16[128,1152]{1,0:T(8,128)(2,1)S(1)}, bf16[128,1152]{1,0:T(8,128)(2,1)S(1)}, u32[]{:S(2)}, u32[]{:S(2)}) %collective-permute-start.9) | collective-permute-done | bytes 294944 | tf_op jit(solution)/shard_map/ppermute | solution.py:389
  36.5 4.9 %attention_and_next_keys.1 = (bf16[48,1152]{1,0:T(8,128)(2,1)S(1)}, bf16[48,640]{1,0:T(8,128)(2,1)S(1)}, bf16[256,1152]{1,0:T(8,128)(2,1)S(1)}, bf16[256,1152]{1,0:T(8,128)(2,1)S(1)}) custom-call(bf16[128,1152]{1,0:T(8,128)(2,1)S(1)} %pad_maximum_fusion.1.refs_0_, bf16[128,1152]{1,0:T(8,128)(2,1)S(1)} %collective-permute-done.9.refs_1_, ...), custom_call_target="tpu_custom_call" | custom-call | tf_op jit(solution)/shard_map/attention_and_next_keys/pallas_call | solution.py:234
  41.8 1.7 %collective-permute-done.12.got_ref = bf16[256,1152]{1,0:T(8,128)(2,1)S(1)} collective-permute-done((bf16[256,1152]{1,0:T(8,128)(2,1)S(1)}, bf16[256,1152]{1,0:T(8,128)(2,1)S(1)}, u32[]{:S(2)}, u32[]{:S(2)}) %collective-permute-start.12) | collective-permute-done | bytes 589856 | tf_op jit(solution)/shard_map/ppermute | solution.py:465
  43.6 3.1 %tile_attention_and_patches.1.patch_ref = f32[48,128]{1,0:T(8,128)S(1)} custom-call(bf16[48,1152]{1,0:T(8,128)(2,1)S(1)} %get-tuple-element.69.x_ref, bf16[48,640]{1,0:T(8,128)(2,1)S(1)} %get-tuple-element.70.q_ref, bf16[256,1152]{1,0:T(8,128)(2,1)S(1)} %get-tuple-element.71.kv_ref, bf16[256,1152]{1,0:T(8,128)(2,1)S(1)} %collective-permute-done.12.got_ref, ...), custom_call_target="tpu_custom_call" | custom-call | tf_op jit(solution)/shard_map/tile_attention_and_patches/pallas_call | solution.py:268
  47.0 0.9 %collective-permute-done.13.got_ref = f32[48,128]{1,0:T(8,128)S(1)} collective-permute-done((f32[48,128]{1,0:T(8,128)S(1)}, f32[48,128]{1,0:T(8,128)S(1)}, u32[]{:S(2)}, u32[]{:S(2)}) %collective-permute-start.13) | collective-permute-done | bytes 24608 | tf_op jit(solution)/shard_map/ppermute | solution.py:470
  47.9 3.1 %decoder_convolutions.1 = bf16[4,128,512]{2,1,0:T(8,128)(2,1)} custom-call(f32[48,128]{1,0:T(8,128)S(1)} %tile_attention_and_patches.1.patch_ref, f32[48,128]{1,0:T(8,128)S(1)} %collective-permute-done.13.got_ref, s32[48,128]{1,0:T(8,128)S(1)} %broadcast_in_dim.14.refs_7_.idx_ref, bf16[1024,512]{1,0:T(8,128)(2,1)S(1)} %fusion.wp_ref, f32[1,512]{1,0:T(1,128)S(1)} %bitcast.31, ...), custom_call_target="tpu_custom_call" | custom-call | tf_op jit(solution)/shard_map/decoder_convolutions/pallas_call | solution.py:350
  (36 shorter events, 2.0 us)
Async XLA Ops:
  0.0 10.3 %copy-start = (f32[100,5,1152]{2,0,1:T(8,128)S(1)}, f32[100,5,1152]{2,0,1:T(8,128)}, u32[]{:S(2)}) copy-start(f32[100,5,1152]{2,0,1:T(8,128)} %param.19) | copy-start | bytes 6912004
  0.0 13.8 %collective-permute-start.3 = (bf16[1,1728,1152]{2,1,0:T(8,128)(2,1)}, bf16[1,1728,1152]{2,1,0:T(8,128)(2,1)}, u32[]{:S(2)}, u32[]{:S(2)}) collective-permute-start(bf16[1,1728,1152]{2,1,0:T(8,128)(2,1)} %bitcast.33), channel_id=1, source_target_pairs={{0,8},{8,0},{1,9},{9,1},{2,10},{10,2},{3,11},{11,3},{4,12},{12,4},... | collective-permute-start | bytes 11943944 | tf_op jit(solution)/shard_map/ppermute | solution.py:420
  1.6 10.5 %collective-permute-start = (bf16[32,1152]{1,0:T(8,128)(2,1)S(1)}, bf16[32,1152]{1,0:T(8,128)(2,1)S(1)}, u32[]{:S(2)}, u32[]{:S(2)}) collective-permute-start(bf16[32,1152]{1,0:T(8,128)(2,1)S(1)} %dynamic-slice_bitcast_fusion), channel_id=1, source_target_pairs={{2,0},{3,1},{4,2},{5,3},{6,4},{7,5},{0,6},{1,7},{10,8},{11,9},{12,... | collective-permute-start | bytes 221192 | tf_op jit(solution)/shard_map/ppermute | solution.py:389
  6.1 7.7 %collective-permute-start.1 = (bf16[32,1152]{1,0:T(8,128)(2,1)S(1)}, bf16[32,1152]{1,0:T(8,128)(2,1)S(1)}, u32[]{:S(2)}, u32[]{:S(2)}) collective-permute-start(bf16[32,1152]{1,0:T(8,128)(2,1)S(1)} %dynamic-slice_bitcast_fusion), channel_id=1, source_target_pairs={{4,0},{5,1},{6,2},{7,3},{0,4},{1,5},{2,6},{3,7},{12,8},{13,9},{14,... | collective-permute-start | bytes 221192 | tf_op jit(solution)/shard_map/ppermute | solution.py:389
  6.1 7.7 %collective-permute-start.2 = (bf16[32,1152]{1,0:T(8,128)(2,1)S(1)}, bf16[32,1152]{1,0:T(8,128)(2,1)S(1)}, u32[]{:S(2)}, u32[]{:S(2)}) collective-permute-start(bf16[32,1152]{1,0:T(8,128)(2,1)S(1)} %dynamic-slice_bitcast_fusion), channel_id=1, source_target_pairs={{6,0},{7,1},{0,2},{1,3},{2,4},{3,5},{4,6},{5,7},{14,8},{15,9},{8,1... | collective-permute-start | bytes 221192 | tf_op jit(solution)/shard_map/ppermute | solution.py:389
  13.9 6.8 %collective-permute-start.8 = (bf16[1,576,1152]{2,1,0:T(8,128)(2,1)}, bf16[1,576,1152]{2,1,0:T(8,128)(2,1)S(1)}, u32[]{:S(2)}, u32[]{:S(2)}) collective-permute-start(bf16[1,576,1152]{2,1,0:T(8,128)(2,1)} %wo_own), channel_id=1, source_target_pairs={{0,8},{8,0},{1,9},{9,1},{2,10},{10,2},{3,11},{11,3},{4,12},{12,4},... | collective-permute-start | bytes 3981320 | tf_op jit(solution)/shard_map/ppermute | solution.py:454
  14.0 11.3 %collective-permute-start.4 = (bf16[128,1152]{1,0:T(8,128)(2,1)S(1)}, bf16[128,1152]{1,0:T(8,128)(2,1)S(1)}, u32[]{:S(2)}, u32[]{:S(2)}) collective-permute-start(bf16[128,1152]{1,0:T(8,128)(2,1)S(1)} %pad_maximum_fusion.refs_0_), channel_id=1, source_target_pairs={{1,0},{0,1},{3,2},{2,3},{5,4},{4,5},{7,6},{6,7},{9,8},{8,9},{11,10... | collective-permute-start | bytes 884744 | tf_op jit(solution)/shard_map/ppermute | solution.py:389
  15.6 8.9 %collective-permute-start.5 = (bf16[32,1152]{1,0:T(8,128)(2,1)S(1)}, bf16[32,1152]{1,0:T(8,128)(2,1)S(1)}, u32[]{:S(2)}, u32[]{:S(2)}) collective-permute-start(bf16[32,1152]{1,0:T(8,128)(2,1)S(1)} %slice_bitcast_fusion), channel_id=1, source_target_pairs={{2,0},{3,1},{4,2},{5,3},{6,4},{7,5},{0,6},{1,7},{10,8},{11,9},{12,... | collective-permute-start | bytes 221192 | tf_op jit(solution)/shard_map/ppermute | solution.py:389
  17.4 7.9 %collective-permute-start.6 = (bf16[32,1152]{1,0:T(8,128)(2,1)S(1)}, bf16[32,1152]{1,0:T(8,128)(2,1)S(1)}, u32[]{:S(2)}, u32[]{:S(2)}) collective-permute-start(bf16[32,1152]{1,0:T(8,128)(2,1)S(1)} %slice_bitcast_fusion), channel_id=1, source_target_pairs={{4,0},{5,1},{6,2},{7,3},{0,4},{1,5},{2,6},{3,7},{12,8},{13,9},{14,... | collective-permute-start | bytes 221192 | tf_op jit(solution)/shard_map/ppermute | solution.py:389
  17.9 7.4 %collective-permute-start.7 = (bf16[32,1152]{1,0:T(8,128)(2,1)S(1)}, bf16[32,1152]{1,0:T(8,128)(2,1)S(1)}, u32[]{:S(2)}, u32[]{:S(2)}) collective-permute-start(bf16[32,1152]{1,0:T(8,128)(2,1)S(1)} %slice_bitcast_fusion), channel_id=1, source_target_pairs={{6,0},{7,1},{0,2},{1,3},{2,4},{3,5},{4,6},{5,7},{14,8},{15,9},{8,1... | collective-permute-start | bytes 221192 | tf_op jit(solution)/shard_map/ppermute | solution.py:389
  25.4 5.2 %collective-permute-start.10 = (bf16[128,1152]{1,0:T(8,128)(2,1)S(1)}, bf16[128,1152]{1,0:T(8,128)(2,1)S(1)}, u32[]{:S(2)}, u32[]{:S(2)}) collective-permute-start(bf16[128,1152]{1,0:T(8,128)(2,1)S(1)} %pad_maximum_fusion.refs_0_), channel_id=1, source_target_pairs={{0,8},{1,9},{2,10},{3,11},{4,12},{5,13},{6,14},{7,15},{16,24},{17,... | collective-permute-start | bytes 884744 | tf_op jit(solution)/shard_map/ppermute | solution.py:459
  26.9 3.8 %collective-permute-start.11 = (bf16[128,1152]{1,0:T(8,128)(2,1)S(1)}, bf16[128,1152]{1,0:T(8,128)(2,1)S(1)}, u32[]{:S(2)}, u32[]{:S(2)}) collective-permute-start(bf16[128,1152]{1,0:T(8,128)(2,1)S(1)} %collective-permute-done.4.refs_1_), channel_id=1, source_target_pairs={{0,8},{1,9},{2,10},{3,11},{4,12},{5,13},{6,14},{7,15},{16,24},{17,... | collective-permute-start | bytes 884744 | tf_op jit(solution)/shard_map/ppermute | solution.py:459
  28.2 8.3 %collective-permute-start.9 = (bf16[128,1152]{1,0:T(8,128)(2,1)S(1)}, bf16[128,1152]{1,0:T(8,128)(2,1)S(1)}, u32[]{:S(2)}, u32[]{:S(2)}) collective-permute-start(bf16[128,1152]{1,0:T(8,128)(2,1)S(1)} %pad_maximum_fusion.1.refs_0_), channel_id=1, source_target_pairs={{1,0},{0,1},{3,2},{2,3},{5,4},{4,5},{7,6},{6,7},{9,8},{8,9},{11,10... | collective-permute-start | bytes 884744 | tf_op jit(solution)/shard_map/ppermute | solution.py:389
  36.5 11.4 %slice-start = ((s8[4718592]{0:T(1024)(128)(4,1)}), s8[4194304]{0:T(1024)(128)(4,1)S(1)}, s32[]{:S(2)}) async-start(s8[4718592]{0:T(1024)(128)(4,1)} %bitcast.28), calls=%async_computation | async-start | bytes 8388608
  36.5 7.0 %copy-start.1 = (bf16[1152,16]{0,1:T(8,128)(2,1)S(1)}, bf16[1152,16]{0,1:T(8,128)(2,1)}, u32[]{:S(2)}) copy-start(bf16[1152,16]{0,1:T(8,128)(2,1)} %param.21) | copy-start | bytes 110596
  36.5 11.4 %slice-start.1 = ((s8[4718592]{0:T(1024)(128)(4,1)}), s8[524288]{0:T(1024)(128)(4,1)S(1)}, s32[]{:S(2)}) async-start(s8[4718592]{0:T(1024)(128)(4,1)} %bitcast.28), calls=%async_computation.1 | async-start | bytes 1048576
  41.5 6.4 %copy-start.2 = (f32[512]{0:T(512)S(1)}, f32[512]{0:T(512)}, u32[]{:S(2)}) copy-start(f32[512]{0:T(512)} %param.23) | copy-start | bytes 6148
  41.5 6.4 %copy-start.3 = (f32[512]{0:T(512)S(1)}, f32[512]{0:T(512)}, u32[]{:S(2)}) copy-start(f32[512]{0:T(512)} %param.25) | copy-start | bytes 6148
  41.5 2.1 %collective-permute-start.12 = (bf16[256,1152]{1,0:T(8,128)(2,1)S(1)}, bf16[256,1152]{1,0:T(8,128)(2,1)S(1)}, u32[]{:S(2)}, u32[]{:S(2)}) collective-permute-start(bf16[256,1152]{1,0:T(8,128)(2,1)S(1)} %get-tuple-element.72), channel_id=1, source_target_pairs={{0,8},{8,0},{1,9},{9,1},{2,10},{10,2},{3,11},{11,3},{4,12},{12,4},... | collective-permute-start | bytes 1769480 | tf_op jit(solution)/shard_map/ppermute | solution.py:465
  46.6 1.3 %collective-permute-start.13 = (f32[48,128]{1,0:T(8,128)S(1)}, f32[48,128]{1,0:T(8,128)S(1)}, u32[]{:S(2)}, u32[]{:S(2)}) collective-permute-start(f32[48,128]{1,0:T(8,128)S(1)} %tile_attention_and_patches.1.patch_ref), channel_id=1, source_target_pairs={{0,8},{8,0},{1,9},{9,1},{2,10},{10,2},{3,11},{11,3},{4,12},{12,4},... | collective-permute-start | bytes 73736 | tf_op jit(solution)/shard_map/ppermute | solution.py:470

commit v10 on v9

--- a/solution.py
+++ b/solution.py
@@ -87,43 +87,52 @@
     return pltpu.CompilerParams(vmem_limit_bytes=(24 if count <= BLOCK else 56) * 1024 * 1024)
 
 
-def weights_kernel(own_ref, other_ref, wo_own, wo_other, w0_ref, w1_ref, wo0_ref, wo1_ref, sems):
+def weights_kernel(own_ref, other_ref, wo_own, w0_ref, w1_ref, wo_ref, sems):
     first = lax.axis_index("pipe") == 0
-    pad = jnp.zeros((SHIFT, D), BF16)
-    wo0_ref[:SHIFT] = pad
-    wo1_ref[:SHIFT] = pad
-    outs = (wo0_ref.at[SHIFT:], wo1_ref.at[SHIFT:])
-    copies = []
-    for i, (in_place, arrived, targets) in enumerate(
-        ((own_ref.at[0], other_ref.at[0], (w0_ref, w1_ref)), (wo_own.at[0], wo_other.at[0], outs))
-    ):
-        for block in range(2):
-            own = (first if block == 0 else jnp.logical_not(first))
-            sem = sems.at[2 * i + block]
-            copies.append(pltpu.make_async_copy(in_place, targets[block], sem))
-
-            @pl.when(own)
-            def _():
-                pltpu.make_async_copy(in_place, targets[block], sem).start()
-
-            @pl.when(jnp.logical_not(own))
-            def _():
-                pltpu.make_async_copy(arrived, targets[block], sem).start()
+    copies = [
+        pltpu.make_async_copy(own_ref.at[0], w0_ref, sems.at[0]),
+        pltpu.make_async_copy(own_ref.at[0], w1_ref, sems.at[1]),
+        pltpu.make_async_copy(wo_own.at[0], wo_ref, sems.at[2]),
+    ]
+    copies[2].start()
+
+    @pl.when(first)
+    def _():
+        copies[0].start()
+        pltpu.make_async_copy(other_ref.at[0], w1_ref, sems.at[1]).start()
+
+    @pl.when(jnp.logical_not(first))
+    def _():
+        copies[1].start()
+        pltpu.make_async_copy(other_ref.at[0], w0_ref, sems.at[0]).start()
 
     for copy in copies:
         copy.wait()
 
 
-def weights_in_vmem(w_own, w_other, wo_own, wo_other):
+def weights_in_vmem(w_own, w_other, wo_own):
     return pl.pallas_call(
         weights_kernel,
-        out_shape=(jax.ShapeDtypeStruct((3 * DA, D), BF16),) * 2 + (jax.ShapeDtypeStruct((DP, D), BF16),) * 2,
-        in_specs=[ANY] * 4,
-        out_specs=(VMEM,) * 4,
-        scratch_shapes=[pltpu.SemaphoreType.DMA((4,))],
+        out_shape=(jax.ShapeDtypeStruct((3 * DA, D), BF16),) * 2 + (jax.ShapeDtypeStruct((DA, D), BF16),),
+        in_specs=[ANY] * 3,
+        out_specs=(VMEM,) * 3,
+        scratch_shapes=[pltpu.SemaphoreType.DMA((3,))],
         compiler_params=params(0),
         name="weights_by_block",
-    )(in_hbm(w_own), w_other, in_hbm(wo_own), wo_other)
+    )(in_hbm(w_own), w_other, in_hbm(wo_own))
+
+
+def choose_out(block, own_ref, other_ref, wo_ref):
+    mine = lax.axis_index("pipe") == block
+    wo_ref[:SHIFT] = jnp.zeros((SHIFT, D), BF16)
+
+    @pl.when(mine)
+    def _():
+        wo_ref[SHIFT:] = own_ref[...]
+
+    @pl.when(jnp.logical_not(mine))
+    def _():
+        wo_ref[SHIFT:] = other_ref[0]
 
 
 def query_of(modulated, w_ref):
@@ -140,11 +149,7 @@
         at += rows
 
 
-def project_kernel(n_pieces, *refs):
-    piece_refs = refs[:n_pieces]
-    vec_ref, w_ref, x_ref, q_ref, kv_ref = refs[n_pieces:]
-    join(piece_refs, x_ref)
-
+def project_kernel(x_ref, vec_ref, w_ref, q_ref, kv_ref):
     def body(start, size):
         rows = pl.ds(start, size)
         modulated = normed(x_ref[rows].astype(F32), vec_ref[1:2], vec_ref[0:1])
@@ -154,37 +159,35 @@
     each_block(x_ref.shape[0], body)
 
 
-def project(pieces, vecs, weights):
-    count = sum(piece.shape[0] for piece in pieces)
+def project(x, vecs, weights):
+    count = x.shape[0]
     return pl.pallas_call(
-        functools.partial(project_kernel, len(pieces)),
+        project_kernel,
         out_shape=(
-            jax.ShapeDtypeStruct((count, D), BF16),
             jax.ShapeDtypeStruct((count, DP), BF16),
             jax.ShapeDtypeStruct((count, 2 * DA), BF16),
         ),
-        in_specs=[VMEM] * (len(pieces) + 2),
-        out_specs=(VMEM,) * 3,
+        in_specs=[VMEM] * 3,
+        out_specs=(VMEM,) * 2,
         compiler_params=params(count),
         name="layer_norm_and_projections",
-    )(*pieces, vecs, weights)
+    )(x, vecs, weights)
 
 
 def in_hbm(array):
     return pltpu.with_memory_space_constraint(array, pltpu.HBM)
 
 
-def block_kernel(n_pieces, n_got, *refs):
+def block_kernel(n_pieces, *refs):
     stale_refs = refs[:n_pieces]
-    got_refs = refs[n_pieces : n_pieces + n_got]
     (
-        x_ref, q_ref, kv_ref, idx_ref, vec_ref, w0_ref, w1_ref, wo_ref,
-        xt_ref, qt_ref, kv1_ref, send_ref, all_ref, pick_ref,
-    ) = refs[n_pieces + n_got :]
+        got_ref, x_ref, q_ref, kv_ref, idx_ref, vec_ref, w0_ref, w1_ref, wo_own, wo_other,
+        xt_ref, qt_ref, kv1_ref, all_ref, pick_ref, wo_ref,
+    ) = refs[n_pieces:]
     count = x_ref.shape[0]
     first_core = lax.axis_index("pipe") == 0
     all_ref[:count] = kv_ref[...]
-    join(stale_refs, send_ref)
+    choose_out(0, wo_own, wo_other, wo_ref)
 
     @pl.when(first_core)
     def _():
@@ -192,15 +195,11 @@
 
     @pl.when(jnp.logical_not(first_core))
     def _():
-        at = count
-        for ref in got_refs:
-
-            def body(start, size):
-                modulated = normed(ref[pl.ds(start, size)].astype(F32), vec_ref[1:2], vec_ref[0:1])
-                all_ref[pl.ds(at + start, size)] = dot_t(modulated, w0_ref[DA:]).astype(BF16)
-
-            each_block(ref.shape[0], body)
-            at += ref.shape[0]
+        def body(start, size):
+            modulated = normed(got_ref[pl.ds(start, size)].astype(F32), vec_ref[1:2], vec_ref[0:1])
+            all_ref[pl.ds(count + start, size)] = dot_t(modulated, w0_ref[DA:]).astype(BF16)
+
+        each_block(count, body)
 
     pick_ref[...] = jnp.zeros_like(pick_ref)
     tile_rows = idx_ref.shape[0]
@@ -213,11 +212,6 @@
         modulated = normed(x1.astype(F32), vec_ref[4:5], vec_ref[3:4])
         fresh = dot_t(modulated, w1_ref[DA:]).astype(BF16)
         kv1_ref[rows] = fresh
-
-        @pl.when(first_core)
-        def _():
-            send_ref[rows] = fresh
-
         lane = lax.broadcasted_iota(jnp.int32, (tile_rows, size), 1) + start
         chosen = (lane == idx_ref[:, :1]).astype(F32).astype(BF16)
         pick_ref[0] += dot(chosen, x1)
@@ -228,33 +222,54 @@
     qt_ref[...] = query_of(pick_ref[1].astype(BF16), w1_ref)
 
 
-def first_block(stale_pieces, got_pieces, x, q, kv, idx, vecs, w_block, w_next, wo_block):
+def first_block(stale_pieces, got_x, x, q, kv, idx, vecs, w_block, w_next, wo_own, wo_other):
     count = x.shape[0]
     tile_rows = idx.shape[0]
     return pl.pallas_call(
-        functools.partial(block_kernel, len(stale_pieces), len(got_pieces)),
+        functools.partial(block_kernel, len(stale_pieces)),
         out_shape=(
             jax.ShapeDtypeStruct((tile_rows, D), BF16),
             jax.ShapeDtypeStruct((tile_rows, DP), BF16),
             jax.ShapeDtypeStruct((count, 2 * DA), BF16),
-            jax.ShapeDtypeStruct((count, 2 * DA), BF16),
         ),
-        in_specs=[VMEM] * (len(stale_pieces) + len(got_pieces) + 8),
-        out_specs=(VMEM,) * 4,
+        in_specs=[VMEM] * (len(stale_pieces) + 10),
+        out_specs=(VMEM,) * 3,
         scratch_shapes=[
             pltpu.VMEM((2 * count, 2 * DA), BF16),
             pltpu.VMEM((2, tile_rows, D), F32),
+            pltpu.VMEM((DP, D), BF16),
         ],
         compiler_params=params(count),
         name="attention_and_next_keys",
-    )(*stale_pieces, *got_pieces, x, q, kv, idx, vecs, w_block, w_next, wo_block)
-
-
-def tile_kernel(x_ref, q_ref, kv_ref, got_ref, idx_ref, vec_ref, wf_ref, wo_ref, patch_ref, all_ref):
+    )(*stale_pieces, got_x, x, q, kv, idx, vecs, w_block, w_next, wo_own, wo_other)
+
+
+def attend_at_once(query, kv_ref):
+    count = query.shape[0]
+    lane = lax.broadcasted_iota(jnp.int32, (count, DP), 1)
+    masked = [
+        jnp.where((lane >= h * DH) & (lane < (h + 1) * DH), query, jnp.zeros((), BF16)) for h in range(HEADS)
+    ]
+    scores = dot_t(jnp.concatenate(masked, axis=0), kv_ref[:, :DP])
+    exponent = jnp.exp2(scores - jnp.max(scores, axis=1, keepdims=True))
+    total = jnp.sum(exponent, axis=1, keepdims=True)
+    numerator = dot(exponent.astype(BF16), kv_ref[:, DA - SHIFT :]) * (1.0 / total)
+    out = None
+    for h in range(HEADS):
+        own = (lane >= SHIFT + h * DH) & (lane < SHIFT + (h + 1) * DH)
+        part = jnp.where(own, numerator[h * count : (h + 1) * count], 0.0)
+        out = part if out is None else out + part
+    return out
+
+
+def tile_kernel(
+    x_ref, q_ref, kv_ref, got_ref, idx_ref, vec_ref, wf_ref, wo_own, wo_other, patch_ref, all_ref, wo_ref
+):
     count = kv_ref.shape[0]
     all_ref[:count] = kv_ref[...]
     all_ref[count:] = got_ref[...]
-    attended = attend(q_ref[...], all_ref).astype(BF16)
+    choose_out(1, wo_own, wo_other, wo_ref)
+    attended = (attend_at_once if count <= BLOCK else attend)(q_ref[...], all_ref).astype(BF16)
     branch = dot(attended, wo_ref[...])
     x2 = (x_ref[...].astype(F32) + vec_ref[5:6] * branch).astype(BF16)
     final = normed(x2.astype(F32), vec_ref[7:8], vec_ref[6:7])
@@ -263,17 +278,17 @@
     patch_ref[:, : 4 * LATC] = jnp.where(idx_ref[:, :1] >= 0, patches, 0.0)
 
 
-def tile_block(x, q, kv, got, idx, vecs, w_final, wo_block):
+def tile_block(x, q, kv, got, idx, vecs, w_final, wo_own, wo_other):
     count = kv.shape[0]
     return pl.pallas_call(
         tile_kernel,
         out_shape=jax.ShapeDtypeStruct((x.shape[0], LANES), F32),
-        in_specs=[VMEM] * 8,
+        in_specs=[VMEM] * 9,
         out_specs=VMEM,
-        scratch_shapes=[pltpu.VMEM((2 * count, 2 * DA), BF16)],
+        scratch_shapes=[pltpu.VMEM((2 * count, 2 * DA), BF16), pltpu.VMEM((DP, D), BF16)],
         compiler_params=params(count),
         name="tile_attention_and_patches",
-    )(x, q, kv, got, idx, vecs, w_final, wo_block)
+    )(x, q, kv, got, idx, vecs, w_final, wo_own, wo_other)
 
 
 def decode_kernel(
@@ -379,14 +394,16 @@
     return n // inner, inner
 
 
-def shifted(block, k_outer, k_inner):
+def shifted(block, k_outer, k_inner, cores=(0, 1)):
     n = lax.axis_size("patch")
     outer, inner = split_of(n)
     route = []
-    for i in range(n):
-        o, e = divmod(i, inner)
-        route.append(((o + k_outer) % outer * inner + (e + k_inner) % inner, i))
-    return lax.ppermute(block, "patch", route)
+    for core in cores:
+        for i in range(n):
+            o, e = divmod(i, inner)
+            source = (o + k_outer) % outer * inner + (e + k_inner) % inner
+            route.append((core * n + source, core * n + i))
+    return lax.ppermute(block, ("pipe", "patch"), route)
 
 
 def local(
@@ -419,7 +436,9 @@
     w_qkv = jnp.swapaxes(w_qkv, 1, 2)
     w_qkv_other = lax.ppermute(w_qkv, "pipe", swap)
     tables = lax.all_gather(block_table[0], "pipe")
-    x_column = [shifted(own_tokens, k, 0) for k in range(1, outer)]
+    w_out_other = lax.ppermute(w_out, "pipe", swap)
+    x_others = jnp.concatenate([shifted(own_tokens, k, 0) for k in range(1, outer)], axis=0)
+    x_own_inner = [shifted(own_tokens, 0, k) for k in range(1, inner)]
 
     time_row = lax.dynamic_index_in_dim(time_table, t_index[0], 0, keepdims=False)
     ones = jnp.asarray([[0.0], [1.0], [0.0]], F32)
@@ -443,27 +462,33 @@
     spot = (k_inner * outer + k_outer) * own_count + token % own_count
     idx = jnp.broadcast_to(jnp.where(inside, spot, -1)[:, None], (padded_rows, LANES)).astype(jnp.int32)
 
-    x_column, w_qkv_other, vecs, idx, own_stale, w_in, w_out = lax.optimization_barrier(
-        (x_column, w_qkv_other, vecs, idx, stale_kv[0, 1], w_in, w_out)
+    x_others, x_own_inner, w_qkv_other, w_out_other, vecs, idx, own_stale = lax.optimization_barrier(
+        (x_others, x_own_inner, w_qkv_other, w_out_other, vecs, idx, stale_kv[0, 1])
     )
+    x_late = [shifted(x_others, 0, k) for k in range(1, inner)]
+    stale_column = [own_stale] + [shifted(own_stale, k, 0) for k in range(1, outer)]
+    w_0, w_1, w_out_own = weights_in_vmem(w_qkv, w_qkv_other, w_out)
+    x_late, stale_column, w_0 = lax.optimization_barrier((x_late, stale_column, w_0))
+    stale_column = jnp.concatenate(stale_column, axis=0)
+    x_pieces = [own_tokens, x_others]
+    for k in range(1, inner):
+        x_pieces += [x_own_inner[k - 1], x_late[k - 1]]
+    x = jnp.concatenate(x_pieces, axis=0)
+    x, stale_column = lax.optimization_barrier((x, stale_column))
+    got_x = lax.ppermute(x, "pipe", [(0, 1)])
+    stale_pieces = [stale_column] + [shifted(stale_column, 0, k, (0,)) for k in range(1, inner)]
+    query, fresh = project(x, vecs, w_0)
+    fresh, own_column = lax.optimization_barrier((fresh, stale_column))
+    next_pieces = [own_column] + [shifted(own_column, 0, k, (1,)) for k in range(1, inner)]
+    x_tile, q_tile, fresh = first_block(
+        stale_pieces, got_x, x, query, fresh, idx, vecs, w_0, w_1, w_out_own, w_out_other
+    )
+    send = jnp.where(first_core, fresh, jnp.concatenate(next_pieces, axis=0))
+    send, w_in = lax.optimization_barrier((send, w_in))
+    got = lax.ppermute(send, "pipe", swap)
     w_patch = dot(jnp.asarray(patch_selector(), BF16), w_in).astype(BF16)
-    x_column = jnp.concatenate([own_tokens] + x_column, axis=0)
-    x_column, own_stale, w_out = lax.optimization_barrier((x_column, own_stale, w_out))
-    x_pieces = [x_column] + [shifted(x_column, 0, k) for k in range(1, inner)]
-    stale_column = [own_stale] + [shifted(own_stale, k, 0) for k in range(1, outer)]
-    w_out_other = lax.ppermute(w_out, "pipe", swap)
-    w_0, w_1, wo_0, wo_1 = weights_in_vmem(w_qkv, w_qkv_other, w_out, w_out_other)
-    x_pieces, stale_column, w_patch, w_0 = lax.optimization_barrier((x_pieces, stale_column, w_patch, w_0))
-    stale_column = jnp.concatenate(stale_column, axis=0)
-    x_pieces, stale_column, w_patch = lax.optimization_barrier((x_pieces, stale_column, w_patch))
-    got_pieces = [lax.ppermute(piece, "pipe", [(0, 1)]) for piece in x_pieces]
-    x, query, fresh = project(x_pieces, vecs, w_0)
-    stale_pieces = [stale_column] + [shifted(stale_column, 0, k) for k in range(1, inner)]
-    x_tile, q_tile, fresh, send = first_block(
-        stale_pieces, got_pieces, x, query, fresh, idx, vecs, w_0, w_1, wo_0
-    )
-    got = lax.ppermute(send, "pipe", swap)
-    patches = tile_block(x_tile, q_tile, fresh, got, idx, vecs, w_final.T, wo_1)
+    got, w_patch = lax.optimization_barrier((got, w_patch))
+    patches = tile_block(x_tile, q_tile, fresh, got, idx, vecs, w_final.T, w_out_own, w_out_other)
     edge = patches
     if rows > 1:
         edge = jnp.where(first_core, patches[(rows - 1) * pitch : rows * pitch], patches[:pitch])

time: 51.4 us -> 69.7 us (1.36)
  local copies, waits for them, and re-layouts: 2.86 us -> 16.2 us
  starting transfers between devices: 15.5 us -> 19.5 us
  waiting for transfers between devices: 11.1 us -> 9.5 us
  Pallas kernels: 16.7 us -> 18.2 us
  other arithmetic: 0.86 us -> 2.07 us
  matrix products: 1.37 us -> 0.4 us
    unnamed x13 -> x35, local copies, waits for them, and re-layouts: 0.75 us -> 14.1 us
    ppermute x10 -> x11, starting transfers between devices: 14.3 us -> 18.8 us  [the longest x10 16.6 us: shifted(): return lax.ppermute(block, ('pipe', 'patch'), route)]
    ppermute x10 -> x11, waiting for transfers between devices: 8.48 us -> 6.87 us  [the longest x10 6.87 us: shifted(): return lax.ppermute(block, ('pipe', 'patch'), route)]
    pallas_call x2, Pallas kernels: 6.8 us -> 8.03 us  [the longest x1 6.18 us: first_block(): pl.pallas_call(functools.partial(block_kernel, len(stale_pieces)), out_sh...]
    select_n x0 -> x1, other arithmetic: none -> 1.16 us  [local(): send = jnp.where(first_core, fresh, jnp.concatenate(next_pieces, axis=0))]
    dot_general x1, matrix products: 1.37 us -> 0.4 us  [dot(): return jnp.dot(a, b, preferred_element_type=F32)]
  transfers between devices with their start and end apart: 14 -> 15, of which waited for: 5 -> 5; matrix products, arithmetic and copies ran while one was open for 10% -> 6% of each run, Pallas kernels for 11% -> 17%
where the time goes in v10:
time: 69.7 us; the launch traced here: 68.7 us
  starting transfers between devices  19.5 us (28%)
  Pallas kernels  18.2 us (26%)
  local copies, waits for them, and re-layouts  16.2 us (23%)
  waiting for transfers between devices  9.5 us (14%)
  other arithmetic  2.07 us (3%)
  blocking collectives  1.99 us (3%)
  between operations  0.87 us (1%)
    ppermute x10, starting transfers between devices, shifted(): return lax.ppermute(block, ('pipe', 'patch'), route)  16.6 us
    unnamed x35, local copies, waits for them, and re-layouts  14.1 us
    ppermute x10, waiting for transfers between devices, shifted(): return lax.ppermute(block, ('pipe', 'patch'), route)  6.87 us
    pallas_call x1, Pallas kernels, first_block(): pl.pallas_call(functools.partial(block_kernel, len(stale_pieces)), out_sh...  6.18 us
    pallas_call x1, Pallas kernels, weights_in_vmem(): pl.pallas_call(weights_kernel, out_shape=(jax.ShapeDtypeStruct((3 * DA, D...  3.75 us
    pallas_call x1, Pallas kernels, tile_block(): pl.pallas_call(tile_kernel, out_shape=jax.ShapeDtypeStruct((x.shape[0], L...  3.26 us
    pallas_call x1, Pallas kernels, decode(): pl.pallas_call(functools.partial(decode_kernel, rows, cols, pitch), out_s...  3.13 us
    ppermute x1, starting transfers between devices, local(): got_x = lax.ppermute(x, 'pipe', [(0, 1)])  2.11 us
  transfers between devices with their start and end apart: 15, of which 5 were waited for; matrix products, arithmetic and copies ran while one was open for 6% of the time, Pallas kernels for 17%

profile of v10, /device:TPU:0, one launch (start us, length us, event | category | flops | bytes accessed | tf_op | source)
XLA Modules:
  0.0 68.7 jit_solution(11934408864624577499)
XLA Ops:
  0.5 1.1 %dynamic-slice_bitcast_fusion = bf16[32,1152]{1,0:T(8,128)(2,1)S(1)} fusion(bf16[2,32,1152]{2,1,0:T(8,128)(2,1)} %param.14, s32[]{:T(128)S(6)} %select_n.104), kind=kLoop, calls=%fused_computation.7 | loop fusion | bytes 147460 | tf_op jit(solution)/shard_map/jit(dynamic_index_in_dim)/squeeze | solution.py:435
  1.6 4.6 %collective-permute-start = (bf16[32,1152]{1,0:T(8,128)(2,1)S(1)}, bf16[32,1152]{1,0:T(8,128)(2,1)S(1)}, u32[]{:S(2)}, u32[]{:S(2)}) collective-permute-start(bf16[32,1152]{1,0:T(8,128)(2,1)S(1)} %dynamic-slice_bitcast_fusion), channel_id=1, source_target_pairs={{2,0},{3,1},{4,2},{5,3},{6,4},{7,5},{0,6},{1,7},{10,8},{11,9},{12,... | collective-permute-start | bytes 221192 | tf_op jit(solution)/shard_map/ppermute | solution.py:406
  8.5 2.0 %all_gather.3 = f32[2,3,1152]{2,1,0:T(4,128)S(1)} all-gather(f32[1,3,1152]{2,1,0:T(4,128)S(1)} %copy.19), channel_id=1, replica_groups=mesh['grp'=2,'pipe'=2,'patch'=8] {'pipe'}, dimensions={0}, use_global_device_ids=true | all-gather | bytes 41472 | tf_op jit(solution)/shard_map/all_gather | solution.py:438
  12.3 1.6 %collective-permute-start.3 = (bf16[32,1152]{1,0:T(8,128)(2,1)S(1)}, bf16[32,1152]{1,0:T(8,128)(2,1)S(1)}, u32[]{:S(2)}, u32[]{:S(2)}) collective-permute-start(bf16[32,1152]{1,0:T(8,128)(2,1)S(1)} %dynamic-slice_bitcast_fusion), channel_id=1, source_target_pairs={{1,0},{0,1},{3,2},{2,3},{5,4},{4,5},{7,6},{6,7},{9,8},{8,9},{11,10... | collective-permute-start | bytes 221192 | tf_op jit(solution)/shard_map/ppermute | solution.py:406
  13.9 3.0 %collective-permute-done.3 = bf16[32,1152]{1,0:T(8,128)(2,1)S(1)} collective-permute-done((bf16[32,1152]{1,0:T(8,128)(2,1)S(1)}, bf16[32,1152]{1,0:T(8,128)(2,1)S(1)}, u32[]{:S(2)}, u32[]{:S(2)}) %collective-permute-start.3) | collective-permute-done | bytes 73760 | tf_op jit(solution)/shard_map/ppermute | solution.py:406
  16.9 1.5 %collective-permute-start.6 = (bf16[96,1152]{1,0:T(8,128)(2,1)S(1)}, bf16[96,1152]{1,0:T(8,128)(2,1)S(1)}, u32[]{:S(2)}, u32[]{:S(2)}) collective-permute-start(bf16[96,1152]{1,0:T(8,128)(2,1)S(1)} %pad_maximum_fusion.2), channel_id=1, source_target_pairs={{1,0},{0,1},{3,2},{2,3},{5,4},{4,5},{7,6},{6,7},{9,8},{8,9},{11,10... | collective-permute-start | bytes 663560 | tf_op jit(solution)/shard_map/ppermute | solution.py:406
  18.5 3.2 %collective-permute-start.7 = (bf16[32,1152]{1,0:T(8,128)(2,1)S(1)}, bf16[32,1152]{1,0:T(8,128)(2,1)S(1)}, u32[]{:S(2)}, u32[]{:S(2)}) collective-permute-start(bf16[32,1152]{1,0:T(8,128)(2,1)S(1)} %slice_bitcast_fusion), channel_id=1, source_target_pairs={{2,0},{3,1},{4,2},{5,3},{6,4},{7,5},{0,6},{1,7},{10,8},{11,9},{12,... | collective-permute-start | bytes 221192 | tf_op jit(solution)/shard_map/ppermute | solution.py:406
  22.6 3.7 %weights_by_block.1 = (bf16[1728,1152]{1,0:T(8,128)(2,1)S(1)}, bf16[1728,1152]{1,0:T(8,128)(2,1)S(1)}, bf16[576,1152]{1,0:T(8,128)(2,1)S(1)}) custom-call(bf16[1,1728,1152]{2,1,0:T(8,128)(2,1)} %bitcast.32, bf16[1,1728,1152]{2,1,0:T(8,128)(2,1)} %collective-permute-done.4.other_ref, bf16[1,576,1152]{2,1,0:T(8,128)(2,1)} %wo_own.1), custom_call_target="tpu_custom_call" | custom-call | tf_op jit(solution)/shard_map/weights_by_block/pallas_call | solution.py:114
  26.4 1.9 %copy-done.6 = bf16[1728,1152]{1,0:T(8,128)(2,1)} copy-done((bf16[1728,1152]{1,0:T(8,128)(2,1)}, bf16[1728,1152]{1,0:T(8,128)(2,1)S(1)}, u32[]{:S(2)}) %copy-start.6) | copy-done | bytes 3981336
  28.8 2.1 %collective-permute-start.11 = (bf16[256,1152]{1,0:T(8,128)(2,1)S(1)}, bf16[256,1152]{1,0:T(8,128)(2,1)}, u32[]{:S(2)}, u32[]{:S(2)}) collective-permute-start(bf16[256,1152]{1,0:T(8,128)(2,1)S(1)} %pad_maximum_fusion.x_ref.refs_3_), channel_id=1, source_target_pairs={{0,8},{1,9},{2,10},{3,11},{4,12},{5,13},{6,14},{7,15},{16,24},{17,... | collective-permute-start | bytes 1769480 | tf_op jit(solution)/shard_map/ppermute | solution.py:478
  30.9 2.4 %collective-permute-start.10 = (bf16[128,1152]{1,0:T(8,128)(2,1)S(1)}, bf16[128,1152]{1,0:T(8,128)(2,1)}, u32[]{:S(2)}, u32[]{:S(2)}) collective-permute-start(bf16[128,1152]{1,0:T(8,128)(2,1)S(1)} %pad_maximum_fusion.1.refs_0_), channel_id=1, source_target_pairs={{1,0},{0,1},{3,2},{2,3},{5,4},{4,5},{7,6},{6,7},{17,16},{16,17},{1... | collective-permute-start | bytes 884744 | tf_op jit(solution)/shard_map/ppermute | solution.py:406
  33.3 1.9 %layer_norm_and_projections.1 = (bf16[256,640]{1,0:T(8,128)(2,1)S(1)}, bf16[256,1152]{1,0:T(8,128)(2,1)S(1)}) custom-call(bf16[256,1152]{1,0:T(8,128)(2,1)S(1)} %pad_maximum_fusion.x_ref.refs_3_, f32[8,1152]{1,0:T(8,128)S(1)} %pad_maximum_fusion.3.vec_ref.refs_7_, bf16[1728,1152]{1,0:T(8,128)(2,1)S(1)} %get-tuple-element.47.w_ref.refs_8_), custom_call_target="tpu_custom_call" | custom-call | tf_op jit(solution)/shard_map/layer_norm_and_projections/pallas_call | solution.py:164
  36.7 1.4 %collective-permute-start.12 = (bf16[128,1152]{1,0:T(8,128)(2,1)S(1)}, bf16[128,1152]{1,0:T(8,128)(2,1)}, u32[]{:S(2)}, u32[]{:S(2)}) collective-permute-start(bf16[128,1152]{1,0:T(8,128)(2,1)S(1)} %pad_maximum_fusion.1.refs_0_), channel_id=1, source_target_pairs={{9,8},{8,9},{11,10},{10,11},{13,12},{12,13},{15,14},{14,15},{25,24... | collective-permute-start | bytes 884744 | tf_op jit(solution)/shard_map/ppermute | solution.py:406
  38.1 3.5 %collective-permute-done.10.refs_1_ = bf16[128,1152]{1,0:T(8,128)(2,1)} collective-permute-done((bf16[128,1152]{1,0:T(8,128)(2,1)S(1)}, bf16[128,1152]{1,0:T(8,128)(2,1)}, u32[]{:S(2)}, u32[]{:S(2)}) %collective-permute-start.10) | collective-permute-done | bytes 294944 | tf_op jit(solution)/shard_map/ppermute | solution.py:406
  41.6 2.1 %copy-done.2 = bf16[1728,1152]{1,0:T(8,128)(2,1)S(1)} copy-done((bf16[1728,1152]{1,0:T(8,128)(2,1)S(1)}, bf16[1728,1152]{1,0:T(8,128)(2,1)}, u32[]{:S(2)}) %copy-start.2) | copy-done | bytes 3981336
  43.7 1.3 %copy-done.4 = bf16[576,1152]{1,0:T(8,128)(2,1)S(1)} copy-done((bf16[576,1152]{1,0:T(8,128)(2,1)S(1)}, bf16[576,1152]{1,0:T(8,128)(2,1)}, u32[]{:S(2)}) %copy-start.4) | copy-done | bytes 1327128
  45.1 2.1 %copy-done.7 = bf16[1728,1152]{1,0:T(8,128)(2,1)S(1)} copy-done((bf16[1728,1152]{1,0:T(8,128)(2,1)S(1)}, bf16[1728,1152]{1,0:T(8,128)(2,1)}, u32[]{:S(2)}) %copy-start.7) | copy-done | bytes 3981336
  47.2 1.1 %copy-done.9 = bf16[256,1152]{1,0:T(8,128)(2,1)S(1)} copy-done((bf16[256,1152]{1,0:T(8,128)(2,1)S(1)}, bf16[256,1152]{1,0:T(8,128)(2,1)}, u32[]{:S(2)}) %copy-start.9) | copy-done | bytes 589848
  49.2 6.2 %attention_and_next_keys.1 = (bf16[48,1152]{1,0:T(8,128)(2,1)S(1)}, bf16[48,640]{1,0:T(8,128)(2,1)S(1)}, bf16[256,1152]{1,0:T(8,128)(2,1)S(1)}) custom-call(bf16[128,1152]{1,0:T(8,128)(2,1)S(1)} %pad_maximum_fusion.1.refs_0_, bf16[128,1152]{1,0:T(8,128)(2,1)} %collective-permute-done.10.refs_1_, bf16[256,1152]{1,0:T(8,128)(2,1)} %collective-permute-done.11.refs_2_, ...), custom_call_target="tpu_custom_call" | custom-call | tf_op jit(solution)/shard_map/attention_and_next_keys/pallas_call | solution.py:228
  55.4 1.2 %maximum_select_fusion = bf16[256,1152]{1,0:T(8,128)(2,1)S(1)} fusion(bf16[256,1152]{1,0:T(8,128)(2,1)S(1)} %get-tuple-element.57.kv_ref, bf16[128,1152]{1,0:T(8,128)(2,1)} %collective-permute-done.12, bf16[128,1152]{1,0:T(8,128)(2,1)S(1)} %pad_maximum_fusion.1.refs_0_, pred[]{:T(512)S(6)} %eq.12), kind=kLoop, calls=%fused_computation.3 | loop fusion | flops 1474560 | bytes 1769473 | tf_op jit(solution)/shard_map/jit(_where)/select_n | solution.py:486
  57.1 1.6 %collective-permute-done.13.got_ref = bf16[256,1152]{1,0:T(8,128)(2,1)S(1)} collective-permute-done((bf16[256,1152]{1,0:T(8,128)(2,1)S(1)}, bf16[256,1152]{1,0:T(8,128)(2,1)S(1)}, u32[]{:S(2)}, u32[]{:S(2)}) %collective-permute-start.13) | collective-permute-done | bytes 589856 | tf_op jit(solution)/shard_map/ppermute | solution.py:488
  58.7 3.3 %tile_attention_and_patches.1.patch_ref = f32[48,128]{1,0:T(8,128)S(1)} custom-call(bf16[48,1152]{1,0:T(8,128)(2,1)S(1)} %get-tuple-element.55.x_ref, bf16[48,640]{1,0:T(8,128)(2,1)S(1)} %get-tuple-element.56.q_ref, bf16[256,1152]{1,0:T(8,128)(2,1)S(1)} %get-tuple-element.57.kv_ref, bf16[256,1152]{1,0:T(8,128)(2,1)S(1)} %collective-permute-done.13.got_ref, ...), custom_call_target="tpu_custom_call" | custom-call | tf_op jit(solution)/shard_map/tile_attention_and_patches/pallas_call | solution.py:283
  63.2 2.3 %copy-done.5 = bf16[9,512,512]{2,1,0:T(8,128)(2,1)S(1)} copy-done((bf16[9,512,512]{2,1,0:T(8,128)(2,1)S(1)}, bf16[9,512,512]{2,1,0:T(8,128)(2,1)}, u32[]{:S(2)}) %copy-start.5) | copy-done | bytes 4718616
  65.6 3.1 %decoder_convolutions.1 = bf16[4,128,512]{2,1,0:T(8,128)(2,1)} custom-call(f32[48,128]{1,0:T(8,128)S(1)} %tile_attention_and_patches.1.patch_ref, f32[48,128]{1,0:T(8,128)S(1)} %collective-permute-done.14.got_ref, s32[48,128]{1,0:T(8,128)S(1)} %broadcast_in_dim.14.refs_6_.idx_ref, bf16[1024,512]{1,0:T(8,128)(2,1)S(1)} %fusion.wp_ref, f32[1,512]{1,0:T(1,128)S(1)} %bitcast.29, ...), custom_call_target="tpu_custom_call" | custom-call | tf_op jit(solution)/shard_map/decoder_convolutions/pallas_call | solution.py:365
  (61 shorter events, 9.8 us)
Async XLA Ops:
  0.0 10.5 %copy-start = (f32[100,5,1152]{2,0,1:T(8,128)S(1)}, f32[100,5,1152]{2,0,1:T(8,128)}, u32[]{:S(2)}) copy-start(f32[100,5,1152]{2,0,1:T(8,128)} %param.19) | copy-start | bytes 6912004
  0.0 16.9 %collective-permute-start.4 = (bf16[1,1728,1152]{2,1,0:T(8,128)(2,1)}, bf16[1,1728,1152]{2,1,0:T(8,128)(2,1)}, u32[]{:S(2)}, u32[]{:S(2)}) collective-permute-start(bf16[1,1728,1152]{2,1,0:T(8,128)(2,1)} %bitcast.31), channel_id=1, source_target_pairs={{0,8},{8,0},{1,9},{9,1},{2,10},{10,2},{3,11},{11,3},{4,12},{12,4},... | collective-permute-start | bytes 11943944 | tf_op jit(solution)/shard_map/ppermute | solution.py:437
  1.6 10.7 %collective-permute-start = (bf16[32,1152]{1,0:T(8,128)(2,1)S(1)}, bf16[32,1152]{1,0:T(8,128)(2,1)S(1)}, u32[]{:S(2)}, u32[]{:S(2)}) collective-permute-start(bf16[32,1152]{1,0:T(8,128)(2,1)S(1)} %dynamic-slice_bitcast_fusion), channel_id=1, source_target_pairs={{2,0},{3,1},{4,2},{5,3},{6,4},{7,5},{0,6},{1,7},{10,8},{11,9},{12,... | collective-permute-start | bytes 221192 | tf_op jit(solution)/shard_map/ppermute | solution.py:406
  6.1 7.7 %collective-permute-start.1 = (bf16[32,1152]{1,0:T(8,128)(2,1)S(1)}, bf16[32,1152]{1,0:T(8,128)(2,1)S(1)}, u32[]{:S(2)}, u32[]{:S(2)}) collective-permute-start(bf16[32,1152]{1,0:T(8,128)(2,1)S(1)} %dynamic-slice_bitcast_fusion), channel_id=1, source_target_pairs={{4,0},{5,1},{6,2},{7,3},{0,4},{1,5},{2,6},{3,7},{12,8},{13,9},{14,... | collective-permute-start | bytes 221192 | tf_op jit(solution)/shard_map/ppermute | solution.py:406
  6.1 7.7 %collective-permute-start.2 = (bf16[32,1152]{1,0:T(8,128)(2,1)S(1)}, bf16[32,1152]{1,0:T(8,128)(2,1)S(1)}, u32[]{:S(2)}, u32[]{:S(2)}) collective-permute-start(bf16[32,1152]{1,0:T(8,128)(2,1)S(1)} %dynamic-slice_bitcast_fusion), channel_id=1, source_target_pairs={{6,0},{7,1},{0,2},{1,3},{2,4},{3,5},{4,6},{5,7},{14,8},{15,9},{8,1... | collective-permute-start | bytes 221192 | tf_op jit(solution)/shard_map/ppermute | solution.py:406
  7.1 9.7 %collective-permute-start.5 = (bf16[1,576,1152]{2,1,0:T(8,128)(2,1)}, bf16[1,576,1152]{2,1,0:T(8,128)(2,1)}, u32[]{:S(2)}, u32[]{:S(2)}) collective-permute-start(bf16[1,576,1152]{2,1,0:T(8,128)(2,1)} %wo_own.1), channel_id=1, source_target_pairs={{0,8},{8,0},{1,9},{9,1},{2,10},{10,2},{3,11},{11,3},{4,12},{12,4},... | collective-permute-start | bytes 3981320 | tf_op jit(solution)/shard_map/ppermute | solution.py:439
  12.3 4.6 %collective-permute-start.3 = (bf16[32,1152]{1,0:T(8,128)(2,1)S(1)}, bf16[32,1152]{1,0:T(8,128)(2,1)S(1)}, u32[]{:S(2)}, u32[]{:S(2)}) collective-permute-start(bf16[32,1152]{1,0:T(8,128)(2,1)S(1)} %dynamic-slice_bitcast_fusion), channel_id=1, source_target_pairs={{1,0},{0,1},{3,2},{2,3},{5,4},{4,5},{7,6},{6,7},{9,8},{8,9},{11,10... | collective-permute-start | bytes 221192 | tf_op jit(solution)/shard_map/ppermute | solution.py:406
  16.9 11.7 %collective-permute-start.6 = (bf16[96,1152]{1,0:T(8,128)(2,1)S(1)}, bf16[96,1152]{1,0:T(8,128)(2,1)S(1)}, u32[]{:S(2)}, u32[]{:S(2)}) collective-permute-start(bf16[96,1152]{1,0:T(8,128)(2,1)S(1)} %pad_maximum_fusion.2), channel_id=1, source_target_pairs={{1,0},{0,1},{3,2},{2,3},{5,4},{4,5},{7,6},{6,7},{9,8},{8,9},{11,10... | collective-permute-start | bytes 663560 | tf_op jit(solution)/shard_map/ppermute | solution.py:406
  18.5 9.8 %collective-permute-start.7 = (bf16[32,1152]{1,0:T(8,128)(2,1)S(1)}, bf16[32,1152]{1,0:T(8,128)(2,1)S(1)}, u32[]{:S(2)}, u32[]{:S(2)}) collective-permute-start(bf16[32,1152]{1,0:T(8,128)(2,1)S(1)} %slice_bitcast_fusion), channel_id=1, source_target_pairs={{2,0},{3,1},{4,2},{5,3},{6,4},{7,5},{0,6},{1,7},{10,8},{11,9},{12,... | collective-permute-start | bytes 221192 | tf_op jit(solution)/shard_map/ppermute | solution.py:406
  21.6 7.0 %collective-permute-start.8 = (bf16[32,1152]{1,0:T(8,128)(2,1)S(1)}, bf16[32,1152]{1,0:T(8,128)(2,1)S(1)}, u32[]{:S(2)}, u32[]{:S(2)}) collective-permute-start(bf16[32,1152]{1,0:T(8,128)(2,1)S(1)} %slice_bitcast_fusion), channel_id=1, source_target_pairs={{4,0},{5,1},{6,2},{7,3},{0,4},{1,5},{2,6},{3,7},{12,8},{13,9},{14,... | collective-permute-start | bytes 221192 | tf_op jit(solution)/shard_map/ppermute | solution.py:406
  22.4 6.3 %collective-permute-start.9 = (bf16[32,1152]{1,0:T(8,128)(2,1)S(1)}, bf16[32,1152]{1,0:T(8,128)(2,1)S(1)}, u32[]{:S(2)}, u32[]{:S(2)}) collective-permute-start(bf16[32,1152]{1,0:T(8,128)(2,1)S(1)} %slice_bitcast_fusion), channel_id=1, source_target_pairs={{6,0},{7,1},{0,2},{1,3},{2,4},{3,5},{4,6},{5,7},{14,8},{15,9},{8,1... | collective-permute-start | bytes 221192 | tf_op jit(solution)/shard_map/ppermute | solution.py:406
  28.3 6.9 %copy-start.1 = (bf16[1728,1152]{1,0:T(8,128)(2,1)}, bf16[1728,1152]{1,0:T(8,128)(2,1)S(1)}, u32[]{:S(2)}) copy-start(bf16[1728,1152]{1,0:T(8,128)(2,1)S(1)} %get-tuple-element.47.w_ref.refs_8_) | copy-start | bytes 11943940
  28.3 6.9 %copy-start.3 = (bf16[576,1152]{1,0:T(8,128)(2,1)}, bf16[576,1152]{1,0:T(8,128)(2,1)S(1)}, u32[]{:S(2)}) copy-start(bf16[576,1152]{1,0:T(8,128)(2,1)S(1)} %get-tuple-element.53.refs_10_.wo_own) | copy-start | bytes 3981316
  28.8 12.8 %collective-permute-start.11 = (bf16[256,1152]{1,0:T(8,128)(2,1)S(1)}, bf16[256,1152]{1,0:T(8,128)(2,1)}, u32[]{:S(2)}, u32[]{:S(2)}) collective-permute-start(bf16[256,1152]{1,0:T(8,128)(2,1)S(1)} %pad_maximum_fusion.x_ref.refs_3_), channel_id=1, source_target_pairs={{0,8},{1,9},{2,10},{3,11},{4,12},{5,13},{6,14},{7,15},{16,24},{17,... | collective-permute-start | bytes 1769480 | tf_op jit(solution)/shard_map/ppermute | solution.py:478
  30.9 10.7 %collective-permute-start.10 = (bf16[128,1152]{1,0:T(8,128)(2,1)S(1)}, bf16[128,1152]{1,0:T(8,128)(2,1)}, u32[]{:S(2)}, u32[]{:S(2)}) collective-permute-start(bf16[128,1152]{1,0:T(8,128)(2,1)S(1)} %pad_maximum_fusion.1.refs_0_), channel_id=1, source_target_pairs={{1,0},{0,1},{3,2},{2,3},{5,4},{4,5},{7,6},{6,7},{17,16},{16,17},{1... | collective-permute-start | bytes 884744 | tf_op jit(solution)/shard_map/ppermute | solution.py:406
  36.7 18.7 %collective-permute-start.12 = (bf16[128,1152]{1,0:T(8,128)(2,1)S(1)}, bf16[128,1152]{1,0:T(8,128)(2,1)}, u32[]{:S(2)}, u32[]{:S(2)}) collective-permute-start(bf16[128,1152]{1,0:T(8,128)(2,1)S(1)} %pad_maximum_fusion.1.refs_0_), channel_id=1, source_target_pairs={{9,8},{8,9},{11,10},{10,11},{13,12},{12,13},{15,14},{14,15},{25,24... | collective-permute-start | bytes 884744 | tf_op jit(solution)/shard_map/ppermute | solution.py:406
  41.6 2.1 %copy-start.2 = (bf16[1728,1152]{1,0:T(8,128)(2,1)S(1)}, bf16[1728,1152]{1,0:T(8,128)(2,1)}, u32[]{:S(2)}) copy-start(bf16[1728,1152]{1,0:T(8,128)(2,1)} %copy-done.1) | copy-start | bytes 11943940
  45.0 2.1 %copy-start.7 = (bf16[1728,1152]{1,0:T(8,128)(2,1)S(1)}, bf16[1728,1152]{1,0:T(8,128)(2,1)}, u32[]{:S(2)}) copy-start(bf16[1728,1152]{1,0:T(8,128)(2,1)} %copy-done.6) | copy-start | bytes 11943940
  55.4 3.3 %copy-start.12 = (bf16[1152,16]{0,1:T(8,128)(2,1)S(1)}, bf16[1152,16]{0,1:T(8,128)(2,1)}, u32[]{:S(2)}) copy-start(bf16[1152,16]{0,1:T(8,128)(2,1)} %param.21) | copy-start | bytes 110596
  56.6 2.1 %collective-permute-start.13 = (bf16[256,1152]{1,0:T(8,128)(2,1)S(1)}, bf16[256,1152]{1,0:T(8,128)(2,1)S(1)}, u32[]{:S(2)}, u32[]{:S(2)}) collective-permute-start(bf16[256,1152]{1,0:T(8,128)(2,1)S(1)} %maximum_select_fusion), channel_id=1, source_target_pairs={{0,8},{8,0},{1,9},{9,1},{2,10},{10,2},{3,11},{11,3},{4,12},{12,4},... | collective-permute-start | bytes 1769480 | tf_op jit(solution)/shard_map/ppermute | solution.py:488
  58.7 4.5 %copy-start.13 = (f32[512]{0:T(512)S(1)}, f32[512]{0:T(512)}, u32[]{:S(2)}) copy-start(f32[512]{0:T(512)} %param.23) | copy-start | bytes 6148
  58.7 4.5 %copy-start.14 = (f32[512]{0:T(512)S(1)}, f32[512]{0:T(512)}, u32[]{:S(2)}) copy-start(f32[512]{0:T(512)} %param.25) | copy-start | bytes 6148
  62.0 1.3 %collective-permute-start.14 = (f32[48,128]{1,0:T(8,128)S(1)}, f32[48,128]{1,0:T(8,128)S(1)}, u32[]{:S(2)}, u32[]{:S(2)}) collective-permute-start(f32[48,128]{1,0:T(8,128)S(1)} %tile_attention_and_patches.1.patch_ref), channel_id=1, source_target_pairs={{0,8},{8,0},{1,9},{9,1},{2,10},{10,2},{3,11},{11,3},{4,12},{12,4},... | collective-permute-start | bytes 73736 | tf_op jit(solution)/shard_map/ppermute | solution.py:495
  63.2 2.3 %copy-start.5 = (bf16[9,512,512]{2,1,0:T(8,128)(2,1)S(1)}, bf16[9,512,512]{2,1,0:T(8,128)(2,1)}, u32[]{:S(2)}) copy-start(bf16[9,512,512]{2,1,0:T(8,128)(2,1)} %w_ref.1) | copy-start | bytes 14155780
  (8 other events, 9.4 us)

commit v11 on v9

--- a/solution.py
+++ b/solution.py
@@ -174,17 +174,10 @@
     return pltpu.with_memory_space_constraint(array, pltpu.HBM)
 
 
-def block_kernel(n_pieces, n_got, *refs):
-    stale_refs = refs[:n_pieces]
-    got_refs = refs[n_pieces : n_pieces + n_got]
-    (
-        x_ref, q_ref, kv_ref, idx_ref, vec_ref, w0_ref, w1_ref, wo_ref,
-        xt_ref, qt_ref, kv1_ref, send_ref, all_ref, pick_ref,
-    ) = refs[n_pieces + n_got :]
-    count = x_ref.shape[0]
+def gather_keys(all_ref, kv_ref, stale_refs, got_ref):
+    count = kv_ref.shape[0]
     first_core = lax.axis_index("pipe") == 0
     all_ref[:count] = kv_ref[...]
-    join(stale_refs, send_ref)
 
     @pl.when(first_core)
     def _():
@@ -192,16 +185,17 @@
 
     @pl.when(jnp.logical_not(first_core))
     def _():
-        at = count
-        for ref in got_refs:
-
-            def body(start, size):
-                modulated = normed(ref[pl.ds(start, size)].astype(F32), vec_ref[1:2], vec_ref[0:1])
-                all_ref[pl.ds(at + start, size)] = dot_t(modulated, w0_ref[DA:]).astype(BF16)
-
-            each_block(ref.shape[0], body)
-            at += ref.shape[0]
-
+        all_ref[count:] = got_ref[...]
+
+
+def block_kernel(n_pieces, *refs):
+    stale_refs = refs[:n_pieces]
+    (
+        got_ref, x_ref, q_ref, kv_ref, idx_ref, vec_ref, w1_ref, wo_ref,
+        xt_ref, qt_ref, kv1_ref, all_ref, pick_ref,
+    ) = refs[n_pieces:]
+    count = x_ref.shape[0]
+    gather_keys(all_ref, kv_ref, stale_refs, got_ref)
     pick_ref[...] = jnp.zeros_like(pick_ref)
     tile_rows = idx_ref.shape[0]
 
@@ -213,11 +207,6 @@
         modulated = normed(x1.astype(F32), vec_ref[4:5], vec_ref[3:4])
         fresh = dot_t(modulated, w1_ref[DA:]).astype(BF16)
         kv1_ref[rows] = fresh
-
-        @pl.when(first_core)
-        def _():
-            send_ref[rows] = fresh
-
         lane = lax.broadcasted_iota(jnp.int32, (tile_rows, size), 1) + start
         chosen = (lane == idx_ref[:, :1]).astype(F32).astype(BF16)
         pick_ref[0] += dot(chosen, x1)
@@ -228,32 +217,31 @@
     qt_ref[...] = query_of(pick_ref[1].astype(BF16), w1_ref)
 
 
-def first_block(stale_pieces, got_pieces, x, q, kv, idx, vecs, w_block, w_next, wo_block):
+def first_block(stale_pieces, got, x, q, kv, idx, vecs, w_next, wo_block):
     count = x.shape[0]
     tile_rows = idx.shape[0]
     return pl.pallas_call(
-        functools.partial(block_kernel, len(stale_pieces), len(got_pieces)),
+        functools.partial(block_kernel, len(stale_pieces)),
         out_shape=(
             jax.ShapeDtypeStruct((tile_rows, D), BF16),
             jax.ShapeDtypeStruct((tile_rows, DP), BF16),
             jax.ShapeDtypeStruct((count, 2 * DA), BF16),
-            jax.ShapeDtypeStruct((count, 2 * DA), BF16),
         ),
-        in_specs=[VMEM] * (len(stale_pieces) + len(got_pieces) + 8),
-        out_specs=(VMEM,) * 4,
+        in_specs=[VMEM] * (len(stale_pieces) + 8),
+        out_specs=(VMEM,) * 3,
         scratch_shapes=[
             pltpu.VMEM((2 * count, 2 * DA), BF16),
             pltpu.VMEM((2, tile_rows, D), F32),
         ],
         compiler_params=params(count),
         name="attention_and_next_keys",
-    )(*stale_pieces, *got_pieces, x, q, kv, idx, vecs, w_block, w_next, wo_block)
-
-
-def tile_kernel(x_ref, q_ref, kv_ref, got_ref, idx_ref, vec_ref, wf_ref, wo_ref, patch_ref, all_ref):
-    count = kv_ref.shape[0]
-    all_ref[:count] = kv_ref[...]
-    all_ref[count:] = got_ref[...]
+    )(*stale_pieces, got, x, q, kv, idx, vecs, w_next, wo_block)
+
+
+def tile_kernel(n_pieces, *refs):
+    stale_refs = refs[:n_pieces]
+    x_ref, q_ref, kv_ref, got_ref, idx_ref, vec_ref, wf_ref, wo_ref, patch_ref, all_ref = refs[n_pieces:]
+    gather_keys(all_ref, kv_ref, stale_refs, got_ref)
     attended = attend(q_ref[...], all_ref).astype(BF16)
     branch = dot(attended, wo_ref[...])
     x2 = (x_ref[...].astype(F32) + vec_ref[5:6] * branch).astype(BF16)
@@ -263,17 +251,17 @@
     patch_ref[:, : 4 * LATC] = jnp.where(idx_ref[:, :1] >= 0, patches, 0.0)
 
 
-def tile_block(x, q, kv, got, idx, vecs, w_final, wo_block):
+def tile_block(stale_pieces, x, q, kv, got, idx, vecs, w_final, wo_block):
     count = kv.shape[0]
     return pl.pallas_call(
-        tile_kernel,
+        functools.partial(tile_kernel, len(stale_pieces)),
         out_shape=jax.ShapeDtypeStruct((x.shape[0], LANES), F32),
-        in_specs=[VMEM] * 8,
+        in_specs=[VMEM] * (len(stale_pieces) + 8),
         out_specs=VMEM,
         scratch_shapes=[pltpu.VMEM((2 * count, 2 * DA), BF16)],
         compiler_params=params(count),
         name="tile_attention_and_patches",
-    )(x, q, kv, got, idx, vecs, w_final, wo_block)
+    )(*stale_pieces, x, q, kv, got, idx, vecs, w_final, wo_block)
 
 
 def decode_kernel(
@@ -379,14 +367,16 @@
     return n // inner, inner
 
 
-def shifted(block, k_outer, k_inner):
+def shifted(block, k_outer, k_inner, cores=(0, 1)):
     n = lax.axis_size("patch")
     outer, inner = split_of(n)
     route = []
-    for i in range(n):
-        o, e = divmod(i, inner)
-        route.append(((o + k_outer) % outer * inner + (e + k_inner) % inner, i))
-    return lax.ppermute(block, "patch", route)
+    for core in cores:
+        for i in range(n):
+            o, e = divmod(i, inner)
+            source = (o + k_outer) % outer * inner + (e + k_inner) % inner
+            route.append((core * n + source, core * n + i))
+    return lax.ppermute(block, ("pipe", "patch"), route)
 
 
 def local(
@@ -420,6 +410,9 @@
     w_qkv_other = lax.ppermute(w_qkv, "pipe", swap)
     tables = lax.all_gather(block_table[0], "pipe")
     x_column = [shifted(own_tokens, k, 0) for k in range(1, outer)]
+    own_stale = stale_kv[0, 1]
+    both_stale = jnp.concatenate([own_stale, lax.ppermute(own_stale, "pipe", [(1, 0)])], axis=0)
+    lines = [both_stale] + [shifted(both_stale, 0, k, (0,)) for k in range(1, inner)]
 
     time_row = lax.dynamic_index_in_dim(time_table, t_index[0], 0, keepdims=False)
     ones = jnp.asarray([[0.0], [1.0], [0.0]], F32)
@@ -443,27 +436,28 @@
     spot = (k_inner * outer + k_outer) * own_count + token % own_count
     idx = jnp.broadcast_to(jnp.where(inside, spot, -1)[:, None], (padded_rows, LANES)).astype(jnp.int32)
 
-    x_column, w_qkv_other, vecs, idx, own_stale, w_in, w_out = lax.optimization_barrier(
-        (x_column, w_qkv_other, vecs, idx, stale_kv[0, 1], w_in, w_out)
+    x_column, lines, w_qkv_other, vecs, idx, w_out = lax.optimization_barrier(
+        (x_column, lines, w_qkv_other, vecs, idx, w_out)
     )
-    w_patch = dot(jnp.asarray(patch_selector(), BF16), w_in).astype(BF16)
     x_column = jnp.concatenate([own_tokens] + x_column, axis=0)
-    x_column, own_stale, w_out = lax.optimization_barrier((x_column, own_stale, w_out))
+    stale_line = jnp.concatenate([line[:own_count] for line in lines], axis=0)
+    next_line = jnp.concatenate([line[own_count:] for line in lines], axis=0)
+    x_column, stale_line, next_line, w_out = lax.optimization_barrier((x_column, stale_line, next_line, w_out))
     x_pieces = [x_column] + [shifted(x_column, 0, k) for k in range(1, inner)]
-    stale_column = [own_stale] + [shifted(own_stale, k, 0) for k in range(1, outer)]
+    stale_pieces = [stale_line] + [shifted(stale_line, k, 0, (0,)) for k in range(1, outer)]
     w_out_other = lax.ppermute(w_out, "pipe", swap)
     w_0, w_1, wo_0, wo_1 = weights_in_vmem(w_qkv, w_qkv_other, w_out, w_out_other)
-    x_pieces, stale_column, w_patch, w_0 = lax.optimization_barrier((x_pieces, stale_column, w_patch, w_0))
-    stale_column = jnp.concatenate(stale_column, axis=0)
-    x_pieces, stale_column, w_patch = lax.optimization_barrier((x_pieces, stale_column, w_patch))
-    got_pieces = [lax.ppermute(piece, "pipe", [(0, 1)]) for piece in x_pieces]
+    x_pieces, stale_pieces, w_0 = lax.optimization_barrier((x_pieces, stale_pieces, w_0))
     x, query, fresh = project(x_pieces, vecs, w_0)
-    stale_pieces = [stale_column] + [shifted(stale_column, 0, k) for k in range(1, inner)]
-    x_tile, q_tile, fresh, send = first_block(
-        stale_pieces, got_pieces, x, query, fresh, idx, vecs, w_0, w_1, wo_0
-    )
-    got = lax.ppermute(send, "pipe", swap)
-    patches = tile_block(x_tile, q_tile, fresh, got, idx, vecs, w_final.T, wo_1)
+    got = lax.ppermute(fresh, "pipe", [(0, 1)])
+    fresh, next_line = lax.optimization_barrier((fresh, next_line))
+    next_pieces = [next_line] + [shifted(next_line, k, 0, (0,)) for k in range(1, outer)]
+    x_tile, q_tile, fresh = first_block(stale_pieces, got, x, query, fresh, idx, vecs, w_1, wo_0)
+    fresh, next_pieces, w_in = lax.optimization_barrier((fresh, next_pieces, w_in))
+    got = lax.ppermute(fresh, "pipe", [(0, 1)])
+    w_patch = dot(jnp.asarray(patch_selector(), BF16), w_in).astype(BF16)
+    got, w_patch = lax.optimization_barrier((got, w_patch))
+    patches = tile_block(next_pieces, x_tile, q_tile, fresh, got, idx, vecs, w_final.T, wo_1)
     edge = patches
     if rows > 1:
         edge = jnp.where(first_core, patches[(rows - 1) * pitch : rows * pitch], patches[:pitch])

time: 51.4 us -> 67.6 us (1.32)
  starting transfers between devices: 15.5 us -> 33 us
  waiting for transfers between devices: 11.1 us -> 10 us
  matrix products: 1.37 us -> 0.4 us
  blocking collectives: 1.82 us -> 2.61 us
    ppermute x11 -> x14, starting transfers between devices: 14.6 us -> 32.1 us  [the longest x11 28 us: shifted(): return lax.ppermute(block, ('pipe', 'patch'), route)]
    ppermute x11 -> x14, waiting for transfers between devices: 10.2 us -> 9.15 us  [the longest x11 8 us: shifted(): return lax.ppermute(block, ('pipe', 'patch'), route)]
    dot_general x1, matrix products: 1.37 us -> 0.4 us  [dot(): return jnp.dot(a, b, preferred_element_type=F32)]
    all_gather x1, blocking collectives: 1.82 us -> 2.61 us  [local(): tables = lax.all_gather(block_table[0], 'pipe')]
  transfers between devices with their start and end apart: 14 -> 17, of which waited for: 5 -> 5; matrix products, arithmetic and copies ran while one was open for 10% -> 6% of each run, Pallas kernels for 11% -> 12%
where the time goes in v11:
time: 67.6 us; the launch traced here: 67.1 us
  starting transfers between devices  33 us (49%)
  Pallas kernels  16.3 us (24%)
  waiting for transfers between devices  10 us (15%)
  local copies, waits for them, and re-layouts  2.91 us (4%)
  blocking collectives  2.61 us (4%)
  between operations  1 us (1%)
  other arithmetic  0.88 us (1%)
    ppermute x11, starting transfers between devices, shifted(): return lax.ppermute(block, ('pipe', 'patch'), route)  28 us
    ppermute x11, waiting for transfers between devices, shifted(): return lax.ppermute(block, ('pipe', 'patch'), route)  8 us
    pallas_call x1, Pallas kernels, first_block(): pl.pallas_call(functools.partial(block_kernel, len(stale_pieces)), out_sh...  4.47 us
    pallas_call x1, Pallas kernels, weights_in_vmem(): pl.pallas_call(weights_kernel, out_shape=(jax.ShapeDtypeStruct((3 * DA, D...  3.71 us
    pallas_call x1, Pallas kernels, decode(): pl.pallas_call(functools.partial(decode_kernel, rows, cols, pitch), out_s...  3.13 us
    pallas_call x1, Pallas kernels, tile_block(): pl.pallas_call(functools.partial(tile_kernel, len(stale_pieces)), out_sha...  3.1 us
    ppermute x2, starting transfers between devices, local(): got = lax.ppermute(fresh, 'pipe', [(0, 1)])  2.78 us
    all_gather x1, blocking collectives, local(): tables = lax.all_gather(block_table[0], 'pipe')  2.61 us
  transfers between devices with their start and end apart: 17, of which 5 were waited for; matrix products, arithmetic and copies ran while one was open for 6% of the time, Pallas kernels for 12%

profile of v11, /device:TPU:0, one launch (start us, length us, event | category | flops | bytes accessed | tf_op | source)
XLA Modules:
  0.0 67.1 jit_solution(8896485927568518364)
XLA Ops:
  0.5 1.1 %dynamic-slice_bitcast_fusion = bf16[32,1152]{1,0:T(8,128)(2,1)S(1)} fusion(bf16[2,32,1152]{2,1,0:T(8,128)(2,1)} %param.14, s32[]{:T(128)S(6)} %select_n.96), kind=kLoop, calls=%fused_computation.7 | loop fusion | bytes 147460 | tf_op jit(solution)/shard_map/jit(dynamic_index_in_dim)/squeeze | solution.py:408
  1.6 4.6 %collective-permute-start = (bf16[32,1152]{1,0:T(8,128)(2,1)S(1)}, bf16[32,1152]{1,0:T(8,128)(2,1)S(1)}, u32[]{:S(2)}, u32[]{:S(2)}) collective-permute-start(bf16[32,1152]{1,0:T(8,128)(2,1)S(1)} %dynamic-slice_bitcast_fusion), channel_id=1, source_target_pairs={{2,0},{3,1},{4,2},{5,3},{6,4},{7,5},{0,6},{1,7},{10,8},{11,9},{12,... | collective-permute-start | bytes 221192 | tf_op jit(solution)/shard_map/ppermute | solution.py:379
  6.1 1.0 %collective-permute-start.2 = (bf16[32,1152]{1,0:T(8,128)(2,1)S(1)}, bf16[32,1152]{1,0:T(8,128)(2,1)S(1)}, u32[]{:S(2)}, u32[]{:S(2)}) collective-permute-start(bf16[32,1152]{1,0:T(8,128)(2,1)S(1)} %dynamic-slice_bitcast_fusion), channel_id=1, source_target_pairs={{6,0},{7,1},{0,2},{1,3},{2,4},{3,5},{4,6},{5,7},{14,8},{15,9},{8,1... | collective-permute-start | bytes 221192 | tf_op jit(solution)/shard_map/ppermute | solution.py:379
  8.0 1.3 %collective-permute-start.3 = (bf16[32,1152]{1,0:T(8,128)(2,1)S(1)}, bf16[32,1152]{1,0:T(8,128)(2,1)S(1)}, u32[]{:S(2)}, u32[]{:S(2)}) collective-permute-start(bf16[32,1152]{1,0:T(8,128)(2,1)S(1)} %slice_bitcast_fusion), channel_id=1, source_target_pairs={{8,0},{9,1},{10,2},{11,3},{12,4},{13,5},{14,6},{15,7},{24,16},{25,... | collective-permute-start | bytes 221192 | tf_op jit(solution)/shard_map/ppermute | solution.py:414
  10.7 2.6 %all_gather.3 = f32[2,3,1152]{2,1,0:T(4,128)S(1)} all-gather(f32[1,3,1152]{2,1,0:T(4,128)S(1)} %copy.19), channel_id=1, replica_groups=mesh['grp'=2,'pipe'=2,'patch'=8] {'pipe'}, dimensions={0}, use_global_device_ids=true | all-gather | bytes 41472 | tf_op jit(solution)/shard_map/all_gather | solution.py:411
  14.1 3.4 %collective-permute-start.4 = (bf16[64,1152]{1,0:T(8,128)(2,1)S(1)}, bf16[64,1152]{1,0:T(8,128)(2,1)S(1)}, u32[]{:S(2)}, u32[]{:S(2)}) collective-permute-start(bf16[64,1152]{1,0:T(8,128)(2,1)S(1)} %pad_maximum_fusion.1), channel_id=1, source_target_pairs={{1,0},{0,1},{3,2},{2,3},{5,4},{4,5},{7,6},{6,7},{17,16},{16,17},{1... | collective-permute-start | bytes 442376 | tf_op jit(solution)/shard_map/ppermute | solution.py:379
  17.7 3.5 %collective-permute-done.4 = bf16[64,1152]{1,0:T(8,128)(2,1)S(1)} collective-permute-done((bf16[64,1152]{1,0:T(8,128)(2,1)S(1)}, bf16[64,1152]{1,0:T(8,128)(2,1)S(1)}, u32[]{:S(2)}, u32[]{:S(2)}) %collective-permute-start.4) | collective-permute-done | bytes 147488 | tf_op jit(solution)/shard_map/ppermute | solution.py:379
  21.4 1.6 %collective-permute-start.6 = (bf16[128,1152]{1,0:T(8,128)(2,1)S(1)}, bf16[128,1152]{1,0:T(8,128)(2,1)S(1)}, u32[]{:S(2)}, u32[]{:S(2)}) collective-permute-start(bf16[128,1152]{1,0:T(8,128)(2,1)S(1)} %pad_maximum_fusion.refs_0_), channel_id=1, source_target_pairs={{1,0},{0,1},{3,2},{2,3},{5,4},{4,5},{7,6},{6,7},{9,8},{8,9},{11,10... | collective-permute-start | bytes 884744 | tf_op jit(solution)/shard_map/ppermute | solution.py:379
  23.0 4.7 %collective-permute-start.7 = (bf16[64,1152]{1,0:T(8,128)(2,1)S(1)}, bf16[64,1152]{1,0:T(8,128)(2,1)S(1)}, u32[]{:S(2)}, u32[]{:S(2)}) collective-permute-start(bf16[64,1152]{1,0:T(8,128)(2,1)S(1)} %pad_maximum_fusion.2.refs_0_), channel_id=1, source_target_pairs={{2,0},{3,1},{4,2},{5,3},{6,4},{7,5},{0,6},{1,7},{18,16},{19,17},{2... | collective-permute-start | bytes 442376 | tf_op jit(solution)/shard_map/ppermute | solution.py:379
  27.7 3.0 %collective-permute-start.8 = (bf16[64,1152]{1,0:T(8,128)(2,1)S(1)}, bf16[64,1152]{1,0:T(8,128)(2,1)S(1)}, u32[]{:S(2)}, u32[]{:S(2)}) collective-permute-start(bf16[64,1152]{1,0:T(8,128)(2,1)S(1)} %pad_maximum_fusion.2.refs_0_), channel_id=1, source_target_pairs={{4,0},{5,1},{6,2},{7,3},{0,4},{1,5},{2,6},{3,7},{20,16},{21,17},{2... | collective-permute-start | bytes 442376 | tf_op jit(solution)/shard_map/ppermute | solution.py:379
  30.8 1.9 %collective-permute-start.9 = (bf16[64,1152]{1,0:T(8,128)(2,1)S(1)}, bf16[64,1152]{1,0:T(8,128)(2,1)S(1)}, u32[]{:S(2)}, u32[]{:S(2)}) collective-permute-start(bf16[64,1152]{1,0:T(8,128)(2,1)S(1)} %pad_maximum_fusion.2.refs_0_), channel_id=1, source_target_pairs={{6,0},{7,1},{0,2},{1,3},{2,4},{3,5},{4,6},{5,7},{22,16},{23,17},{1... | collective-permute-start | bytes 442376 | tf_op jit(solution)/shard_map/ppermute | solution.py:379
  32.7 3.7 %weights_by_block.1 = (bf16[1728,1152]{1,0:T(8,128)(2,1)S(1)}, bf16[1728,1152]{1,0:T(8,128)(2,1)S(1)}, bf16[640,1152]{1,0:T(8,128)(2,1)S(1)}, bf16[640,1152]{1,0:T(8,128)(2,1)S(1)}) custom-call(bf16[1,1728,1152]{2,1,0:T(8,128)(2,1)} %bitcast.34, bf16[1,1728,1152]{2,1,0:T(8,128)(2,1)} %collective-permute-done.5.other_ref, bf16[1,576,1152]{2,1,0:T(8,128)(2,1)} %wo_own, ...), custom_call_target="tpu_custom_call" | custom-call | tf_op jit(solution)/shard_map/weights_by_block/pallas_call | solution.py:118
  36.5 3.2 %collective-permute-done.9.refs_3_ = bf16[64,1152]{1,0:T(8,128)(2,1)S(1)} collective-permute-done((bf16[64,1152]{1,0:T(8,128)(2,1)S(1)}, bf16[64,1152]{1,0:T(8,128)(2,1)S(1)}, u32[]{:S(2)}, u32[]{:S(2)}) %collective-permute-start.9) | collective-permute-done | bytes 147488 | tf_op jit(solution)/shard_map/ppermute | solution.py:379
  39.6 1.9 %layer_norm_and_projections.1 = (bf16[256,1152]{1,0:T(8,128)(2,1)S(1)}, bf16[256,640]{1,0:T(8,128)(2,1)S(1)}, bf16[256,1152]{1,0:T(8,128)(2,1)S(1)}) custom-call(bf16[128,1152]{1,0:T(8,128)(2,1)S(1)} %pad_maximum_fusion.refs_0_, bf16[128,1152]{1,0:T(8,128)(2,1)S(1)} %collective-permute-done.6.refs_1_, f32[8,1152]{1,0:T(8,128)S(1)} %pad_maximum_fusion.4.refs_2_.refs_9_, ...), custom_call_target="tpu_custom_call" | custom-call | tf_op jit(solution)/shard_map/layer_norm_and_projections/pallas_call | solution.py:159
  41.5 1.3 %collective-permute-start.11 = (bf16[256,1152]{1,0:T(8,128)(2,1)S(1)}, bf16[256,1152]{1,0:T(8,128)(2,1)S(1)}, u32[]{:S(2)}, u32[]{:S(2)}) collective-permute-start(bf16[256,1152]{1,0:T(8,128)(2,1)S(1)} %get-tuple-element.68.refs_7_), channel_id=1, source_target_pairs={{0,8},{1,9},{2,10},{3,11},{4,12},{5,13},{6,14},{7,15},{16,24},{17,... | collective-permute-start | bytes 1769480 | tf_op jit(solution)/shard_map/ppermute | solution.py:452
  42.8 2.6 %collective-permute-start.12 = (bf16[64,1152]{1,0:T(8,128)(2,1)S(1)}, bf16[64,1152]{1,0:T(8,128)(2,1)S(1)}, u32[]{:S(2)}, u32[]{:S(2)}) collective-permute-start(bf16[64,1152]{1,0:T(8,128)(2,1)S(1)} %pad_maximum_fusion.3.refs_0_), channel_id=1, source_target_pairs={{2,0},{3,1},{4,2},{5,3},{6,4},{7,5},{0,6},{1,7},{18,16},{19,17},{2... | collective-permute-start | bytes 442376 | tf_op jit(solution)/shard_map/ppermute | solution.py:379
  45.4 1.9 %collective-permute-start.13 = (bf16[64,1152]{1,0:T(8,128)(2,1)S(1)}, bf16[64,1152]{1,0:T(8,128)(2,1)S(1)}, u32[]{:S(2)}, u32[]{:S(2)}) collective-permute-start(bf16[64,1152]{1,0:T(8,128)(2,1)S(1)} %pad_maximum_fusion.3.refs_0_), channel_id=1, source_target_pairs={{4,0},{5,1},{6,2},{7,3},{0,4},{1,5},{2,6},{3,7},{20,16},{21,17},{2... | collective-permute-start | bytes 442376 | tf_op jit(solution)/shard_map/ppermute | solution.py:379
  47.3 3.3 %collective-permute-start.14 = (bf16[64,1152]{1,0:T(8,128)(2,1)S(1)}, bf16[64,1152]{1,0:T(8,128)(2,1)S(1)}, u32[]{:S(2)}, u32[]{:S(2)}) collective-permute-start(bf16[64,1152]{1,0:T(8,128)(2,1)S(1)} %pad_maximum_fusion.3.refs_0_), channel_id=1, source_target_pairs={{6,0},{7,1},{0,2},{1,3},{2,4},{3,5},{4,6},{5,7},{22,16},{23,17},{1... | collective-permute-start | bytes 442376 | tf_op jit(solution)/shard_map/ppermute | solution.py:379
  50.7 4.5 %attention_and_next_keys.1 = (bf16[48,1152]{1,0:T(8,128)(2,1)S(1)}, bf16[48,640]{1,0:T(8,128)(2,1)S(1)}, bf16[256,1152]{1,0:T(8,128)(2,1)S(1)}) custom-call(bf16[64,1152]{1,0:T(8,128)(2,1)S(1)} %pad_maximum_fusion.2.refs_0_, bf16[64,1152]{1,0:T(8,128)(2,1)S(1)} %collective-permute-done.7.refs_1_, bf16[64,1152]{1,0:T(8,128)(2,1)S(1)} %collective-permute-done.8.refs_2_, ...), custom_call_target="tpu_custom_call" | custom-call | tf_op jit(solution)/shard_map/attention_and_next_keys/pallas_call | solution.py:223
  55.2 1.3 %collective-permute-done.13.refs_2_ = bf16[64,1152]{1,0:T(8,128)(2,1)S(1)} collective-permute-done((bf16[64,1152]{1,0:T(8,128)(2,1)S(1)}, bf16[64,1152]{1,0:T(8,128)(2,1)S(1)}, u32[]{:S(2)}, u32[]{:S(2)}) %collective-permute-start.13) | collective-permute-done | bytes 147488 | tf_op jit(solution)/shard_map/ppermute | solution.py:379
  56.5 1.5 %collective-permute-start.15 = (bf16[256,1152]{1,0:T(8,128)(2,1)S(1)}, bf16[256,1152]{1,0:T(8,128)(2,1)S(1)}, u32[]{:S(2)}, u32[]{:S(2)}) collective-permute-start(bf16[256,1152]{1,0:T(8,128)(2,1)S(1)} %get-tuple-element.80.refs_6_), channel_id=1, source_target_pairs={{0,8},{1,9},{2,10},{3,11},{4,12},{5,13},{6,14},{7,15},{16,24},{17,... | collective-permute-start | bytes 1769480 | tf_op jit(solution)/shard_map/ppermute | solution.py:457
  58.4 1.1 %collective-permute-done.15.refs_7_ = bf16[256,1152]{1,0:T(8,128)(2,1)S(1)} collective-permute-done((bf16[256,1152]{1,0:T(8,128)(2,1)S(1)}, bf16[256,1152]{1,0:T(8,128)(2,1)S(1)}, u32[]{:S(2)}, u32[]{:S(2)}) %collective-permute-start.15) | collective-permute-done | bytes 589856 | tf_op jit(solution)/shard_map/ppermute | solution.py:457
  59.6 3.1 %tile_attention_and_patches.1.patch_ref = f32[48,128]{1,0:T(8,128)S(1)} custom-call(bf16[64,1152]{1,0:T(8,128)(2,1)S(1)} %pad_maximum_fusion.3.refs_0_, bf16[64,1152]{1,0:T(8,128)(2,1)S(1)} %collective-permute-done.12.refs_1_, bf16[64,1152]{1,0:T(8,128)(2,1)S(1)} %collective-permute-done.13.refs_2_, bf16[64,1152]{1,0:T(8,128)(2,1)S(1)} %collective-permute-done.14.refs_3_, ...), custom_call_target="tpu_custom_call" | custom-call | tf_op jit(solution)/shard_map/tile_attention_and_patches/pallas_call | solution.py:256
  64.0 3.1 %decoder_convolutions.1 = bf16[4,128,512]{2,1,0:T(8,128)(2,1)} custom-call(f32[48,128]{1,0:T(8,128)S(1)} %tile_attention_and_patches.1.patch_ref, f32[48,128]{1,0:T(8,128)S(1)} %collective-permute-done.16.got_ref, s32[48,128]{1,0:T(8,128)S(1)} %broadcast_in_dim.14.refs_8_.idx_ref, bf16[1024,512]{1,0:T(8,128)(2,1)S(1)} %fusion.wp_ref, f32[1,512]{1,0:T(1,128)S(1)} %bitcast.31, ...), custom_call_target="tpu_custom_call" | custom-call | tf_op jit(solution)/shard_map/decoder_convolutions/pallas_call | solution.py:338
  (49 shorter events, 4.9 us)
Async XLA Ops:
  0.0 13.3 %copy-start = (f32[100,5,1152]{2,0,1:T(8,128)S(1)}, f32[100,5,1152]{2,0,1:T(8,128)}, u32[]{:S(2)}) copy-start(f32[100,5,1152]{2,0,1:T(8,128)} %param.19) | copy-start | bytes 6912004
  0.0 21.2 %collective-permute-start.5 = (bf16[1,1728,1152]{2,1,0:T(8,128)(2,1)}, bf16[1,1728,1152]{2,1,0:T(8,128)(2,1)}, u32[]{:S(2)}, u32[]{:S(2)}) collective-permute-start(bf16[1,1728,1152]{2,1,0:T(8,128)(2,1)} %bitcast.33), channel_id=1, source_target_pairs={{0,8},{8,0},{1,9},{9,1},{2,10},{10,2},{3,11},{11,3},{4,12},{12,4},... | collective-permute-start | bytes 11943944 | tf_op jit(solution)/shard_map/ppermute | solution.py:410
  1.6 16.1 %collective-permute-start = (bf16[32,1152]{1,0:T(8,128)(2,1)S(1)}, bf16[32,1152]{1,0:T(8,128)(2,1)S(1)}, u32[]{:S(2)}, u32[]{:S(2)}) collective-permute-start(bf16[32,1152]{1,0:T(8,128)(2,1)S(1)} %dynamic-slice_bitcast_fusion), channel_id=1, source_target_pairs={{2,0},{3,1},{4,2},{5,3},{6,4},{7,5},{0,6},{1,7},{10,8},{11,9},{12,... | collective-permute-start | bytes 221192 | tf_op jit(solution)/shard_map/ppermute | solution.py:379
  6.1 11.5 %collective-permute-start.1 = (bf16[32,1152]{1,0:T(8,128)(2,1)S(1)}, bf16[32,1152]{1,0:T(8,128)(2,1)S(1)}, u32[]{:S(2)}, u32[]{:S(2)}) collective-permute-start(bf16[32,1152]{1,0:T(8,128)(2,1)S(1)} %dynamic-slice_bitcast_fusion), channel_id=1, source_target_pairs={{4,0},{5,1},{6,2},{7,3},{0,4},{1,5},{2,6},{3,7},{12,8},{13,9},{14,... | collective-permute-start | bytes 221192 | tf_op jit(solution)/shard_map/ppermute | solution.py:379
  6.1 11.5 %collective-permute-start.2 = (bf16[32,1152]{1,0:T(8,128)(2,1)S(1)}, bf16[32,1152]{1,0:T(8,128)(2,1)S(1)}, u32[]{:S(2)}, u32[]{:S(2)}) collective-permute-start(bf16[32,1152]{1,0:T(8,128)(2,1)S(1)} %dynamic-slice_bitcast_fusion), channel_id=1, source_target_pairs={{6,0},{7,1},{0,2},{1,3},{2,4},{3,5},{4,6},{5,7},{14,8},{15,9},{8,1... | collective-permute-start | bytes 221192 | tf_op jit(solution)/shard_map/ppermute | solution.py:379
  8.0 6.1 %collective-permute-start.3 = (bf16[32,1152]{1,0:T(8,128)(2,1)S(1)}, bf16[32,1152]{1,0:T(8,128)(2,1)S(1)}, u32[]{:S(2)}, u32[]{:S(2)}) collective-permute-start(bf16[32,1152]{1,0:T(8,128)(2,1)S(1)} %slice_bitcast_fusion), channel_id=1, source_target_pairs={{8,0},{9,1},{10,2},{11,3},{12,4},{13,5},{14,6},{15,7},{24,16},{25,... | collective-permute-start | bytes 221192 | tf_op jit(solution)/shard_map/ppermute | solution.py:414
  14.1 7.0 %collective-permute-start.4 = (bf16[64,1152]{1,0:T(8,128)(2,1)S(1)}, bf16[64,1152]{1,0:T(8,128)(2,1)S(1)}, u32[]{:S(2)}, u32[]{:S(2)}) collective-permute-start(bf16[64,1152]{1,0:T(8,128)(2,1)S(1)} %pad_maximum_fusion.1), channel_id=1, source_target_pairs={{1,0},{0,1},{3,2},{2,3},{5,4},{4,5},{7,6},{6,7},{17,16},{16,17},{1... | collective-permute-start | bytes 442376 | tf_op jit(solution)/shard_map/ppermute | solution.py:379
  21.4 11.4 %collective-permute-start.10 = (bf16[1,576,1152]{2,1,0:T(8,128)(2,1)}, bf16[1,576,1152]{2,1,0:T(8,128)(2,1)S(1)}, u32[]{:S(2)}, u32[]{:S(2)}) collective-permute-start(bf16[1,576,1152]{2,1,0:T(8,128)(2,1)} %wo_own), channel_id=1, source_target_pairs={{0,8},{8,0},{1,9},{9,1},{2,10},{10,2},{3,11},{11,3},{4,12},{12,4},... | collective-permute-start | bytes 3981320 | tf_op jit(solution)/shard_map/ppermute | solution.py:448
  21.4 18.2 %collective-permute-start.6 = (bf16[128,1152]{1,0:T(8,128)(2,1)S(1)}, bf16[128,1152]{1,0:T(8,128)(2,1)S(1)}, u32[]{:S(2)}, u32[]{:S(2)}) collective-permute-start(bf16[128,1152]{1,0:T(8,128)(2,1)S(1)} %pad_maximum_fusion.refs_0_), channel_id=1, source_target_pairs={{1,0},{0,1},{3,2},{2,3},{5,4},{4,5},{7,6},{6,7},{9,8},{8,9},{11,10... | collective-permute-start | bytes 884744 | tf_op jit(solution)/shard_map/ppermute | solution.py:379
  23.0 13.4 %collective-permute-start.7 = (bf16[64,1152]{1,0:T(8,128)(2,1)S(1)}, bf16[64,1152]{1,0:T(8,128)(2,1)S(1)}, u32[]{:S(2)}, u32[]{:S(2)}) collective-permute-start(bf16[64,1152]{1,0:T(8,128)(2,1)S(1)} %pad_maximum_fusion.2.refs_0_), channel_id=1, source_target_pairs={{2,0},{3,1},{4,2},{5,3},{6,4},{7,5},{0,6},{1,7},{18,16},{19,17},{2... | collective-permute-start | bytes 442376 | tf_op jit(solution)/shard_map/ppermute | solution.py:379
  27.7 8.7 %collective-permute-start.8 = (bf16[64,1152]{1,0:T(8,128)(2,1)S(1)}, bf16[64,1152]{1,0:T(8,128)(2,1)S(1)}, u32[]{:S(2)}, u32[]{:S(2)}) collective-permute-start(bf16[64,1152]{1,0:T(8,128)(2,1)S(1)} %pad_maximum_fusion.2.refs_0_), channel_id=1, source_target_pairs={{4,0},{5,1},{6,2},{7,3},{0,4},{1,5},{2,6},{3,7},{20,16},{21,17},{2... | collective-permute-start | bytes 442376 | tf_op jit(solution)/shard_map/ppermute | solution.py:379
  30.8 8.8 %collective-permute-start.9 = (bf16[64,1152]{1,0:T(8,128)(2,1)S(1)}, bf16[64,1152]{1,0:T(8,128)(2,1)S(1)}, u32[]{:S(2)}, u32[]{:S(2)}) collective-permute-start(bf16[64,1152]{1,0:T(8,128)(2,1)S(1)} %pad_maximum_fusion.2.refs_0_), channel_id=1, source_target_pairs={{6,0},{7,1},{0,2},{1,3},{2,4},{3,5},{4,6},{5,7},{22,16},{23,17},{1... | collective-permute-start | bytes 442376 | tf_op jit(solution)/shard_map/ppermute | solution.py:379
  41.5 9.1 %collective-permute-start.11 = (bf16[256,1152]{1,0:T(8,128)(2,1)S(1)}, bf16[256,1152]{1,0:T(8,128)(2,1)S(1)}, u32[]{:S(2)}, u32[]{:S(2)}) collective-permute-start(bf16[256,1152]{1,0:T(8,128)(2,1)S(1)} %get-tuple-element.68.refs_7_), channel_id=1, source_target_pairs={{0,8},{1,9},{2,10},{3,11},{4,12},{5,13},{6,14},{7,15},{16,24},{17,... | collective-permute-start | bytes 1769480 | tf_op jit(solution)/shard_map/ppermute | solution.py:452
  42.8 12.3 %collective-permute-start.12 = (bf16[64,1152]{1,0:T(8,128)(2,1)S(1)}, bf16[64,1152]{1,0:T(8,128)(2,1)S(1)}, u32[]{:S(2)}, u32[]{:S(2)}) collective-permute-start(bf16[64,1152]{1,0:T(8,128)(2,1)S(1)} %pad_maximum_fusion.3.refs_0_), channel_id=1, source_target_pairs={{2,0},{3,1},{4,2},{5,3},{6,4},{7,5},{0,6},{1,7},{18,16},{19,17},{2... | collective-permute-start | bytes 442376 | tf_op jit(solution)/shard_map/ppermute | solution.py:379
  45.4 11.1 %collective-permute-start.13 = (bf16[64,1152]{1,0:T(8,128)(2,1)S(1)}, bf16[64,1152]{1,0:T(8,128)(2,1)S(1)}, u32[]{:S(2)}, u32[]{:S(2)}) collective-permute-start(bf16[64,1152]{1,0:T(8,128)(2,1)S(1)} %pad_maximum_fusion.3.refs_0_), channel_id=1, source_target_pairs={{4,0},{5,1},{6,2},{7,3},{0,4},{1,5},{2,6},{3,7},{20,16},{21,17},{2... | collective-permute-start | bytes 442376 | tf_op jit(solution)/shard_map/ppermute | solution.py:379
  47.3 9.2 %collective-permute-start.14 = (bf16[64,1152]{1,0:T(8,128)(2,1)S(1)}, bf16[64,1152]{1,0:T(8,128)(2,1)S(1)}, u32[]{:S(2)}, u32[]{:S(2)}) collective-permute-start(bf16[64,1152]{1,0:T(8,128)(2,1)S(1)} %pad_maximum_fusion.3.refs_0_), channel_id=1, source_target_pairs={{6,0},{7,1},{0,2},{1,3},{2,4},{3,5},{4,6},{5,7},{22,16},{23,17},{1... | collective-permute-start | bytes 442376 | tf_op jit(solution)/shard_map/ppermute | solution.py:379
  50.6 13.3 %slice-start = ((s8[4718592]{0:T(1024)(128)(4,1)}), s8[4194304]{0:T(1024)(128)(4,1)S(1)}, s32[]{:S(2)}) async-start(s8[4718592]{0:T(1024)(128)(4,1)} %bitcast.28), calls=%async_computation | async-start | bytes 8388608
  50.6 7.3 %copy-start.4 = (bf16[1024,36]{1,0:T(8,128)(2,1)S(1)}, bf16[1024,36]{1,0:T(8,128)(2,1)}, u32[]{:S(2)}) copy-start(bf16[1024,36]{1,0:T(8,128)(2,1)} %constant.129.clone) | copy-start | bytes 221188
  50.7 8.9 %copy-start.1 = (bf16[1152,16]{0,1:T(8,128)(2,1)S(1)}, bf16[1152,16]{0,1:T(8,128)(2,1)}, u32[]{:S(2)}) copy-start(bf16[1152,16]{0,1:T(8,128)(2,1)} %param.21) | copy-start | bytes 110596
  50.7 13.3 %slice-start.1 = ((s8[4718592]{0:T(1024)(128)(4,1)}), s8[524288]{0:T(1024)(128)(4,1)S(1)}, s32[]{:S(2)}) async-start(s8[4718592]{0:T(1024)(128)(4,1)} %bitcast.28), calls=%async_computation.1 | async-start | bytes 1048576
  56.5 7.5 %copy-start.2 = (f32[512]{0:T(512)S(1)}, f32[512]{0:T(512)}, u32[]{:S(2)}) copy-start(f32[512]{0:T(512)} %param.23) | copy-start | bytes 6148
  56.5 7.5 %copy-start.3 = (f32[512]{0:T(512)S(1)}, f32[512]{0:T(512)}, u32[]{:S(2)}) copy-start(f32[512]{0:T(512)} %param.25) | copy-start | bytes 6148
  56.5 3.0 %collective-permute-start.15 = (bf16[256,1152]{1,0:T(8,128)(2,1)S(1)}, bf16[256,1152]{1,0:T(8,128)(2,1)S(1)}, u32[]{:S(2)}, u32[]{:S(2)}) collective-permute-start(bf16[256,1152]{1,0:T(8,128)(2,1)S(1)} %get-tuple-element.80.refs_6_), channel_id=1, source_target_pairs={{0,8},{1,9},{2,10},{3,11},{4,12},{5,13},{6,14},{7,15},{16,24},{17,... | collective-permute-start | bytes 1769480 | tf_op jit(solution)/shard_map/ppermute | solution.py:457
  62.7 1.3 %collective-permute-start.16 = (f32[48,128]{1,0:T(8,128)S(1)}, f32[48,128]{1,0:T(8,128)S(1)}, u32[]{:S(2)}, u32[]{:S(2)}) collective-permute-start(f32[48,128]{1,0:T(8,128)S(1)} %tile_attention_and_patches.1.patch_ref), channel_id=1, source_target_pairs={{0,8},{8,0},{1,9},{9,1},{2,10},{10,2},{3,11},{11,3},{4,12},{12,4},... | collective-permute-start | bytes 73736 | tf_op jit(solution)/shard_map/ppermute | solution.py:464
  (1 other events, 7.3 us)

commit v12 on v9

--- a/solution.py
+++ b/solution.py
@@ -142,7 +142,8 @@
 
 def project_kernel(n_pieces, *refs):
     piece_refs = refs[:n_pieces]
-    vec_ref, w_ref, x_ref, q_ref, kv_ref = refs[n_pieces:]
+    vec_ref, w_ref, x_ref, q_ref, kv_ref = refs[n_pieces : n_pieces + 5]
+    part_refs = refs[n_pieces + 5 :]
     join(piece_refs, x_ref)
 
     def body(start, size):
@@ -152,19 +153,27 @@
         q_ref[rows] = query_of(modulated, w_ref)
 
     each_block(x_ref.shape[0], body)
+    at = 0
+    for ref in part_refs:
+        rows = ref.shape[0]
+        ref[...] = kv_ref[at : at + rows]
+        at += rows
 
 
 def project(pieces, vecs, weights):
     count = sum(piece.shape[0] for piece in pieces)
+    step = 3 * count // 8
+    parts = (step, step, count - 2 * step)
     return pl.pallas_call(
         functools.partial(project_kernel, len(pieces)),
         out_shape=(
             jax.ShapeDtypeStruct((count, D), BF16),
             jax.ShapeDtypeStruct((count, DP), BF16),
             jax.ShapeDtypeStruct((count, 2 * DA), BF16),
-        ),
+        )
+        + tuple(jax.ShapeDtypeStruct((part, 2 * DA), BF16) for part in parts),
         in_specs=[VMEM] * (len(pieces) + 2),
-        out_specs=(VMEM,) * 3,
+        out_specs=(VMEM,) * 6,
         compiler_params=params(count),
         name="layer_norm_and_projections",
     )(*pieces, vecs, weights)
@@ -172,36 +181,33 @@
 
 def in_hbm(array):
     return pltpu.with_memory_space_constraint(array, pltpu.HBM)
+
+
+def gather_keys(all_ref, kv_ref, stale_refs, got_refs):
+    count = kv_ref.shape[0]
+    first_core = lax.axis_index("pipe") == 0
+    all_ref[:count] = kv_ref[...]
+
+    @pl.when(first_core)
+    def _():
+        join(stale_refs, all_ref.at[count:])
+
+    @pl.when(jnp.logical_not(first_core))
+    def _():
+        join(got_refs, all_ref.at[count:])
 
 
 def block_kernel(n_pieces, n_got, *refs):
     stale_refs = refs[:n_pieces]
     got_refs = refs[n_pieces : n_pieces + n_got]
     (
-        x_ref, q_ref, kv_ref, idx_ref, vec_ref, w0_ref, w1_ref, wo_ref,
+        x_ref, q_ref, kv_ref, idx_ref, vec_ref, w1_ref, wo_ref,
         xt_ref, qt_ref, kv1_ref, send_ref, all_ref, pick_ref,
     ) = refs[n_pieces + n_got :]
     count = x_ref.shape[0]
     first_core = lax.axis_index("pipe") == 0
-    all_ref[:count] = kv_ref[...]
+    gather_keys(all_ref, kv_ref, stale_refs, got_refs)
     join(stale_refs, send_ref)
-
-    @pl.when(first_core)
-    def _():
-        join(stale_refs, all_ref.at[count:])
-
-    @pl.when(jnp.logical_not(first_core))
-    def _():
-        at = count
-        for ref in got_refs:
-
-            def body(start, size):
-                modulated = normed(ref[pl.ds(start, size)].astype(F32), vec_ref[1:2], vec_ref[0:1])
-                all_ref[pl.ds(at + start, size)] = dot_t(modulated, w0_ref[DA:]).astype(BF16)
-
-            each_block(ref.shape[0], body)
-            at += ref.shape[0]
-
     pick_ref[...] = jnp.zeros_like(pick_ref)
     tile_rows = idx_ref.shape[0]
 
@@ -228,7 +234,7 @@
     qt_ref[...] = query_of(pick_ref[1].astype(BF16), w1_ref)
 
 
-def first_block(stale_pieces, got_pieces, x, q, kv, idx, vecs, w_block, w_next, wo_block):
+def first_block(stale_pieces, got_pieces, x, q, kv, idx, vecs, w_next, wo_block):
     count = x.shape[0]
     tile_rows = idx.shape[0]
     return pl.pallas_call(
@@ -239,7 +245,7 @@
             jax.ShapeDtypeStruct((count, 2 * DA), BF16),
             jax.ShapeDtypeStruct((count, 2 * DA), BF16),
         ),
-        in_specs=[VMEM] * (len(stale_pieces) + len(got_pieces) + 8),
+        in_specs=[VMEM] * (len(stale_pieces) + len(got_pieces) + 7),
         out_specs=(VMEM,) * 4,
         scratch_shapes=[
             pltpu.VMEM((2 * count, 2 * DA), BF16),
@@ -247,7 +253,7 @@
         ],
         compiler_params=params(count),
         name="attention_and_next_keys",
-    )(*stale_pieces, *got_pieces, x, q, kv, idx, vecs, w_block, w_next, wo_block)
+    )(*stale_pieces, *got_pieces, x, q, kv, idx, vecs, w_next, wo_block)
 
 
 def tile_kernel(x_ref, q_ref, kv_ref, got_ref, idx_ref, vec_ref, wf_ref, wo_ref, patch_ref, all_ref):
@@ -379,14 +385,16 @@
     return n // inner, inner
 
 
-def shifted(block, k_outer, k_inner):
+def shifted(block, k_outer, k_inner, cores=(0, 1)):
     n = lax.axis_size("patch")
     outer, inner = split_of(n)
     route = []
-    for i in range(n):
-        o, e = divmod(i, inner)
-        route.append(((o + k_outer) % outer * inner + (e + k_inner) % inner, i))
-    return lax.ppermute(block, "patch", route)
+    for core in cores:
+        for i in range(n):
+            o, e = divmod(i, inner)
+            source = (o + k_outer) % outer * inner + (e + k_inner) % inner
+            route.append((core * n + source, core * n + i))
+    return lax.ppermute(block, ("pipe", "patch"), route)
 
 
 def local(
@@ -443,26 +451,28 @@
     spot = (k_inner * outer + k_outer) * own_count + token % own_count
     idx = jnp.broadcast_to(jnp.where(inside, spot, -1)[:, None], (padded_rows, LANES)).astype(jnp.int32)
 
-    x_column, w_qkv_other, vecs, idx, own_stale, w_in, w_out = lax.optimization_barrier(
-        (x_column, w_qkv_other, vecs, idx, stale_kv[0, 1], w_in, w_out)
+    x_column, w_qkv_other, vecs, idx, own_stale, w_out = lax.optimization_barrier(
+        (x_column, w_qkv_other, vecs, idx, stale_kv[0, 1], w_out)
     )
-    w_patch = dot(jnp.asarray(patch_selector(), BF16), w_in).astype(BF16)
     x_column = jnp.concatenate([own_tokens] + x_column, axis=0)
     x_column, own_stale, w_out = lax.optimization_barrier((x_column, own_stale, w_out))
     x_pieces = [x_column] + [shifted(x_column, 0, k) for k in range(1, inner)]
     stale_column = [own_stale] + [shifted(own_stale, k, 0) for k in range(1, outer)]
     w_out_other = lax.ppermute(w_out, "pipe", swap)
     w_0, w_1, wo_0, wo_1 = weights_in_vmem(w_qkv, w_qkv_other, w_out, w_out_other)
-    x_pieces, stale_column, w_patch, w_0 = lax.optimization_barrier((x_pieces, stale_column, w_patch, w_0))
+    x_pieces, stale_column, w_0 = lax.optimization_barrier((x_pieces, stale_column, w_0))
     stale_column = jnp.concatenate(stale_column, axis=0)
-    x_pieces, stale_column, w_patch = lax.optimization_barrier((x_pieces, stale_column, w_patch))
-    got_pieces = [lax.ppermute(piece, "pipe", [(0, 1)]) for piece in x_pieces]
-    x, query, fresh = project(x_pieces, vecs, w_0)
+    x_pieces, stale_column = lax.optimization_barrier((x_pieces, stale_column))
     stale_pieces = [stale_column] + [shifted(stale_column, 0, k) for k in range(1, inner)]
+    x, query, fresh, *parts = project(x_pieces, vecs, w_0)
+    got_pieces = [lax.ppermute(part, "pipe", [(0, 1)]) for part in parts]
     x_tile, q_tile, fresh, send = first_block(
-        stale_pieces, got_pieces, x, query, fresh, idx, vecs, w_0, w_1, wo_0
+        stale_pieces, got_pieces, x, query, fresh, idx, vecs, w_1, wo_0
     )
+    send, w_in = lax.optimization_barrier((send, w_in))
     got = lax.ppermute(send, "pipe", swap)
+    w_patch = dot(jnp.asarray(patch_selector(), BF16), w_in).astype(BF16)
+    got, w_patch = lax.optimization_barrier((got, w_patch))
     patches = tile_block(x_tile, q_tile, fresh, got, idx, vecs, w_final.T, wo_1)
     edge = patches
     if rows > 1:

time: 51.4 us -> 48.8 us (0.949)
  waiting for transfers between devices: 11.1 us -> 8.75 us
  matrix products: 1.37 us -> 0.4 us
  starting transfers between devices: 15.5 us -> 16.2 us
    ppermute x10 -> x11, waiting for transfers between devices: 8.48 us -> 6.11 us  [the longest x8 5.13 us: shifted(): return lax.ppermute(block, ('pipe', 'patch'), route)]
    ppermute x10 -> x11, starting transfers between devices: 14.3 us -> 15.4 us  [the longest x8 11.5 us: shifted(): return lax.ppermute(block, ('pipe', 'patch'), route)]
    dot_general x1, matrix products: 1.37 us -> 0.4 us  [dot(): return jnp.dot(a, b, preferred_element_type=F32)]
  transfers between devices with their start and end apart: 14 -> 15, of which waited for: 5 -> 6; matrix products, arithmetic and copies ran while one was open for 10% -> 8% of each run, Pallas kernels for 11% -> 12%
where the time goes in v12:
time: 48.8 us; the launch traced here: 48.5 us
  Pallas kernels  16.7 us (34%)
  starting transfers between devices  16.2 us (33%)
  waiting for transfers between devices  8.75 us (18%)
  local copies, waits for them, and re-layouts  2.87 us (6%)
  blocking collectives  1.82 us (4%)
  other arithmetic  0.86 us (2%)
  between operations  0.86 us (2%)
    ppermute x8, starting transfers between devices, shifted(): return lax.ppermute(block, ('pipe', 'patch'), route)  11.5 us
    ppermute x8, waiting for transfers between devices, shifted(): return lax.ppermute(block, ('pipe', 'patch'), route)  5.13 us
    pallas_call x1, Pallas kernels, first_block(): pl.pallas_call(functools.partial(block_kernel, len(stale_pieces), len(got...  4.96 us
    ppermute x3, starting transfers between devices, local(): got_pieces = [lax.ppermute(part, 'pipe', [(0, 1)]) for part in parts]  3.9 us
    pallas_call x1, Pallas kernels, weights_in_vmem(): pl.pallas_call(weights_kernel, out_shape=(jax.ShapeDtypeStruct((3 * DA, D...  3.7 us
    pallas_call x1, Pallas kernels, decode(): pl.pallas_call(functools.partial(decode_kernel, rows, cols, pitch), out_s...  3.14 us
    pallas_call x1, Pallas kernels, tile_block(): pl.pallas_call(tile_kernel, out_shape=jax.ShapeDtypeStruct((x.shape[0], L...  3.05 us
    pallas_call x1, Pallas kernels, project(): pl.pallas_call(functools.partial(project_kernel, len(pieces)), out_shape=...  1.89 us
  transfers between devices with their start and end apart: 15, of which 6 were waited for; matrix products, arithmetic and copies ran while one was open for 8% of the time, Pallas kernels for 12%

profile of v12, /device:TPU:0, one launch (start us, length us, event | category | flops | bytes accessed | tf_op | source)
XLA Modules:
  0.0 48.5 jit_solution(16367748792963175680)
XLA Ops:
  0.5 1.1 %dynamic-slice_bitcast_fusion = bf16[32,1152]{1,0:T(8,128)(2,1)S(1)} fusion(bf16[2,32,1152]{2,1,0:T(8,128)(2,1)} %param.14, s32[]{:T(128)S(6)} %select_n.96), kind=kLoop, calls=%fused_computation.5 | loop fusion | bytes 147460 | tf_op jit(solution)/shard_map/jit(dynamic_index_in_dim)/squeeze | solution.py:426
  1.6 4.6 %collective-permute-start = (bf16[32,1152]{1,0:T(8,128)(2,1)S(1)}, bf16[32,1152]{1,0:T(8,128)(2,1)S(1)}, u32[]{:S(2)}, u32[]{:S(2)}) collective-permute-start(bf16[32,1152]{1,0:T(8,128)(2,1)S(1)} %dynamic-slice_bitcast_fusion), channel_id=1, source_target_pairs={{2,0},{3,1},{4,2},{5,3},{6,4},{7,5},{0,6},{1,7},{10,8},{11,9},{12,... | collective-permute-start | bytes 221192 | tf_op jit(solution)/shard_map/ppermute | solution.py:397
  6.1 1.0 %collective-permute-start.2 = (bf16[32,1152]{1,0:T(8,128)(2,1)S(1)}, bf16[32,1152]{1,0:T(8,128)(2,1)S(1)}, u32[]{:S(2)}, u32[]{:S(2)}) collective-permute-start(bf16[32,1152]{1,0:T(8,128)(2,1)S(1)} %dynamic-slice_bitcast_fusion), channel_id=1, source_target_pairs={{6,0},{7,1},{0,2},{1,3},{2,4},{3,5},{4,6},{5,7},{14,8},{15,9},{8,1... | collective-permute-start | bytes 221192 | tf_op jit(solution)/shard_map/ppermute | solution.py:397
  7.8 0.7 %copy.19 = f32[1,3,1152]{2,1,0:T(4,128)S(1)} copy(f32[1,3,1152]{2,0,1:T(1,128)} %param.18) | data formatting | bytes 27648 | tf_op args[4]
  8.5 1.8 %all_gather.3 = f32[2,3,1152]{2,1,0:T(4,128)S(1)} all-gather(f32[1,3,1152]{2,1,0:T(4,128)S(1)} %copy.19), channel_id=1, replica_groups=mesh['grp'=2,'pipe'=2,'patch'=8] {'pipe'}, dimensions={0}, use_global_device_ids=true | all-gather | bytes 41472 | tf_op jit(solution)/shard_map/all_gather | solution.py:429
  10.4 0.7 %fusion.2 = (f32[3,1152]{1,0:T(4,128)S(1)}, f32[3,1152]{1,0:T(4,128)S(1)}) fusion(f32[1,3,1152]{2,0,1:T(1,128)S(1)} %constant_dynamic-slice_fusion, f32[2,3,1152]{2,1,0:T(4,128)S(1)} %all_gather.3, f32[3]{0:T(128)} %constant.135), kind=kLoop, calls=%fused_computation.10 | loop fusion | flops 13824 | bytes 69132 | tf_op jit(solution)/shard_map/add | solution.py:436
  11.2 0.9 %slice_bitcast_fusion = bf16[32,1152]{1,0:T(8,128)(2,1)S(1)} fusion(bf16[1,2,32,1152]{3,2,1,0:T(8,128)(2,1)} %param.15), kind=kLoop, calls=%fused_computation.4 | loop fusion | bytes 147456 | tf_op jit(solution)/shard_map/squeeze | solution.py:455
  12.1 1.7 %collective-permute-done.1 = bf16[32,1152]{1,0:T(8,128)(2,1)S(1)} collective-permute-done((bf16[32,1152]{1,0:T(8,128)(2,1)S(1)}, bf16[32,1152]{1,0:T(8,128)(2,1)S(1)}, u32[]{:S(2)}, u32[]{:S(2)}) %collective-permute-start.1) | collective-permute-done | bytes 73760 | tf_op jit(solution)/shard_map/ppermute | solution.py:397
  14.0 1.6 %collective-permute-start.4 = (bf16[128,1152]{1,0:T(8,128)(2,1)S(1)}, bf16[128,1152]{1,0:T(8,128)(2,1)S(1)}, u32[]{:S(2)}, u32[]{:S(2)}) collective-permute-start(bf16[128,1152]{1,0:T(8,128)(2,1)S(1)} %pad_maximum_fusion.refs_0_), channel_id=1, source_target_pairs={{1,0},{0,1},{3,2},{2,3},{5,4},{4,5},{7,6},{6,7},{9,8},{8,9},{11,10... | collective-permute-start | bytes 884744 | tf_op jit(solution)/shard_map/ppermute | solution.py:397
  15.6 1.8 %collective-permute-start.5 = (bf16[32,1152]{1,0:T(8,128)(2,1)S(1)}, bf16[32,1152]{1,0:T(8,128)(2,1)S(1)}, u32[]{:S(2)}, u32[]{:S(2)}) collective-permute-start(bf16[32,1152]{1,0:T(8,128)(2,1)S(1)} %slice_bitcast_fusion), channel_id=1, source_target_pairs={{2,0},{3,1},{4,2},{5,3},{6,4},{7,5},{0,6},{1,7},{10,8},{11,9},{12,... | collective-permute-start | bytes 221192 | tf_op jit(solution)/shard_map/ppermute | solution.py:397
  17.9 1.4 %collective-permute-start.7 = (bf16[32,1152]{1,0:T(8,128)(2,1)S(1)}, bf16[32,1152]{1,0:T(8,128)(2,1)S(1)}, u32[]{:S(2)}, u32[]{:S(2)}) collective-permute-start(bf16[32,1152]{1,0:T(8,128)(2,1)S(1)} %slice_bitcast_fusion), channel_id=1, source_target_pairs={{6,0},{7,1},{0,2},{1,3},{2,4},{3,5},{4,6},{5,7},{14,8},{15,9},{8,1... | collective-permute-start | bytes 221192 | tf_op jit(solution)/shard_map/ppermute | solution.py:397
  19.4 3.7 %weights_by_block.1 = (bf16[1728,1152]{1,0:T(8,128)(2,1)S(1)}, bf16[1728,1152]{1,0:T(8,128)(2,1)S(1)}, bf16[640,1152]{1,0:T(8,128)(2,1)S(1)}, bf16[640,1152]{1,0:T(8,128)(2,1)S(1)}) custom-call(bf16[1,1728,1152]{2,1,0:T(8,128)(2,1)} %bitcast.34, bf16[1,1728,1152]{2,1,0:T(8,128)(2,1)} %collective-permute-done.3.other_ref, bf16[1,576,1152]{2,1,0:T(8,128)(2,1)} %wo_own, ...), custom_call_target="tpu_custom_call" | custom-call | tf_op jit(solution)/shard_map/weights_by_block/pallas_call | solution.py:118
  23.1 2.3 %collective-permute-done.6 = bf16[32,1152]{1,0:T(8,128)(2,1)S(1)} collective-permute-done((bf16[32,1152]{1,0:T(8,128)(2,1)S(1)}, bf16[32,1152]{1,0:T(8,128)(2,1)S(1)}, u32[]{:S(2)}, u32[]{:S(2)}) %collective-permute-start.6) | collective-permute-done | bytes 73760 | tf_op jit(solution)/shard_map/ppermute | solution.py:397
  26.0 1.9 %layer_norm_and_projections.1 = (bf16[256,1152]{1,0:T(8,128)(2,1)S(1)}, bf16[256,640]{1,0:T(8,128)(2,1)S(1)}, bf16[256,1152]{1,0:T(8,128)(2,1)S(1)}, bf16[96,115...) custom-call(bf16[128,1152]{1,0:T(8,128)(2,1)S(1)} %pad_maximum_fusion.refs_0_, ...), custom_call_target="tpu_custom_call" | custom-call | tf_op jit(solution)/shard_map/layer_norm_and_projections/pallas_call | solution.py:167
  27.9 1.3 %collective-permute-start.10 = (bf16[96,1152]{1,0:T(8,128)(2,1)S(1)}, bf16[96,1152]{1,0:T(8,128)(2,1)S(1)}, u32[]{:S(2)}, u32[]{:S(2)}) collective-permute-start(bf16[96,1152]{1,0:T(8,128)(2,1)S(1)} %get-tuple-element.65), channel_id=1, source_target_pairs={{0,8},{1,9},{2,10},{3,11},{4,12},{5,13},{6,14},{7,15},{16,24},{17,... | collective-permute-start | bytes 663560 | tf_op jit(solution)/shard_map/ppermute | solution.py:468
  29.2 1.3 %collective-permute-start.11 = (bf16[96,1152]{1,0:T(8,128)(2,1)S(1)}, bf16[96,1152]{1,0:T(8,128)(2,1)S(1)}, u32[]{:S(2)}, u32[]{:S(2)}) collective-permute-start(bf16[96,1152]{1,0:T(8,128)(2,1)S(1)} %get-tuple-element.66), channel_id=1, source_target_pairs={{0,8},{1,9},{2,10},{3,11},{4,12},{5,13},{6,14},{7,15},{16,24},{17,... | collective-permute-start | bytes 663560 | tf_op jit(solution)/shard_map/ppermute | solution.py:468
  30.5 1.3 %collective-permute-start.12 = (bf16[64,1152]{1,0:T(8,128)(2,1)S(1)}, bf16[64,1152]{1,0:T(8,128)(2,1)S(1)}, u32[]{:S(2)}, u32[]{:S(2)}) collective-permute-start(bf16[64,1152]{1,0:T(8,128)(2,1)S(1)} %get-tuple-element.67), channel_id=1, source_target_pairs={{0,8},{1,9},{2,10},{3,11},{4,12},{5,13},{6,14},{7,15},{16,24},{17,... | collective-permute-start | bytes 442376 | tf_op jit(solution)/shard_map/ppermute | solution.py:468
  31.8 1.0 %collective-permute-done.12.refs_4_ = bf16[64,1152]{1,0:T(8,128)(2,1)S(1)} collective-permute-done((bf16[64,1152]{1,0:T(8,128)(2,1)S(1)}, bf16[64,1152]{1,0:T(8,128)(2,1)S(1)}, u32[]{:S(2)}, u32[]{:S(2)}) %collective-permute-start.12) | collective-permute-done | bytes 147488 | tf_op jit(solution)/shard_map/ppermute | solution.py:468
  32.8 1.1 %collective-permute-done.9.refs_1_ = bf16[128,1152]{1,0:T(8,128)(2,1)S(1)} collective-permute-done((bf16[128,1152]{1,0:T(8,128)(2,1)S(1)}, bf16[128,1152]{1,0:T(8,128)(2,1)S(1)}, u32[]{:S(2)}, u32[]{:S(2)}) %collective-permute-start.9) | collective-permute-done | bytes 294944 | tf_op jit(solution)/shard_map/ppermute | solution.py:397
  33.9 5.0 %attention_and_next_keys.1 = (bf16[48,1152]{1,0:T(8,128)(2,1)S(1)}, bf16[48,640]{1,0:T(8,128)(2,1)S(1)}, bf16[256,1152]{1,0:T(8,128)(2,1)S(1)}, bf16[256,1152]{1,0:T(8,128)(2,1)S(1)}) custom-call(bf16[128,1152]{1,0:T(8,128)(2,1)S(1)} %pad_maximum_fusion.1.refs_0_, bf16[128,1152]{1,0:T(8,128)(2,1)S(1)} %collective-permute-done.9.refs_1_, ...), custom_call_target="tpu_custom_call" | custom-call | tf_op jit(solution)/shard_map/attention_and_next_keys/pallas_call | solution.py:240
  39.4 1.6 %collective-permute-done.13.got_ref = bf16[256,1152]{1,0:T(8,128)(2,1)S(1)} collective-permute-done((bf16[256,1152]{1,0:T(8,128)(2,1)S(1)}, bf16[256,1152]{1,0:T(8,128)(2,1)S(1)}, u32[]{:S(2)}, u32[]{:S(2)}) %collective-permute-start.13) | collective-permute-done | bytes 589856 | tf_op jit(solution)/shard_map/ppermute | solution.py:473
  41.0 3.1 %tile_attention_and_patches.1.patch_ref = f32[48,128]{1,0:T(8,128)S(1)} custom-call(bf16[48,1152]{1,0:T(8,128)(2,1)S(1)} %get-tuple-element.74.x_ref, bf16[48,640]{1,0:T(8,128)(2,1)S(1)} %get-tuple-element.75.q_ref, bf16[256,1152]{1,0:T(8,128)(2,1)S(1)} %get-tuple-element.76.kv_ref, bf16[256,1152]{1,0:T(8,128)(2,1)S(1)} %collective-permute-done.13.got_ref, ...), custom_call_target="tpu_custom_call" | custom-call | tf_op jit(solution)/shard_map/tile_attention_and_patches/pallas_call | solution.py:274
  44.3 1.1 %collective-permute-done.14.got_ref = f32[48,128]{1,0:T(8,128)S(1)} collective-permute-done((f32[48,128]{1,0:T(8,128)S(1)}, f32[48,128]{1,0:T(8,128)S(1)}, u32[]{:S(2)}, u32[]{:S(2)}) %collective-permute-start.14) | collective-permute-done | bytes 24608 | tf_op jit(solution)/shard_map/ppermute | solution.py:480
  45.4 3.1 %decoder_convolutions.1 = bf16[4,128,512]{2,1,0:T(8,128)(2,1)} custom-call(f32[48,128]{1,0:T(8,128)S(1)} %tile_attention_and_patches.1.patch_ref, f32[48,128]{1,0:T(8,128)S(1)} %collective-permute-done.14.got_ref, s32[48,128]{1,0:T(8,128)S(1)} %broadcast_in_dim.14.refs_8_.idx_ref, bf16[1024,512]{1,0:T(8,128)(2,1)S(1)} %fusion.wp_ref, f32[1,512]{1,0:T(1,128)S(1)} %bitcast.31, ...), custom_call_target="tpu_custom_call" | custom-call | tf_op jit(solution)/shard_map/decoder_convolutions/pallas_call | solution.py:356
  (42 shorter events, 2.6 us)
Async XLA Ops:
  0.0 10.3 %copy-start = (f32[100,5,1152]{2,0,1:T(8,128)S(1)}, f32[100,5,1152]{2,0,1:T(8,128)}, u32[]{:S(2)}) copy-start(f32[100,5,1152]{2,0,1:T(8,128)} %param.19) | copy-start | bytes 6912004
  0.0 13.8 %collective-permute-start.3 = (bf16[1,1728,1152]{2,1,0:T(8,128)(2,1)}, bf16[1,1728,1152]{2,1,0:T(8,128)(2,1)}, u32[]{:S(2)}, u32[]{:S(2)}) collective-permute-start(bf16[1,1728,1152]{2,1,0:T(8,128)(2,1)} %bitcast.33), channel_id=1, source_target_pairs={{0,8},{8,0},{1,9},{9,1},{2,10},{10,2},{3,11},{11,3},{4,12},{12,4},... | collective-permute-start | bytes 11943944 | tf_op jit(solution)/shard_map/ppermute | solution.py:428
  1.6 10.5 %collective-permute-start = (bf16[32,1152]{1,0:T(8,128)(2,1)S(1)}, bf16[32,1152]{1,0:T(8,128)(2,1)S(1)}, u32[]{:S(2)}, u32[]{:S(2)}) collective-permute-start(bf16[32,1152]{1,0:T(8,128)(2,1)S(1)} %dynamic-slice_bitcast_fusion), channel_id=1, source_target_pairs={{2,0},{3,1},{4,2},{5,3},{6,4},{7,5},{0,6},{1,7},{10,8},{11,9},{12,... | collective-permute-start | bytes 221192 | tf_op jit(solution)/shard_map/ppermute | solution.py:397
  6.1 7.7 %collective-permute-start.1 = (bf16[32,1152]{1,0:T(8,128)(2,1)S(1)}, bf16[32,1152]{1,0:T(8,128)(2,1)S(1)}, u32[]{:S(2)}, u32[]{:S(2)}) collective-permute-start(bf16[32,1152]{1,0:T(8,128)(2,1)S(1)} %dynamic-slice_bitcast_fusion), channel_id=1, source_target_pairs={{4,0},{5,1},{6,2},{7,3},{0,4},{1,5},{2,6},{3,7},{12,8},{13,9},{14,... | collective-permute-start | bytes 221192 | tf_op jit(solution)/shard_map/ppermute | solution.py:397
  6.1 7.7 %collective-permute-start.2 = (bf16[32,1152]{1,0:T(8,128)(2,1)S(1)}, bf16[32,1152]{1,0:T(8,128)(2,1)S(1)}, u32[]{:S(2)}, u32[]{:S(2)}) collective-permute-start(bf16[32,1152]{1,0:T(8,128)(2,1)S(1)} %dynamic-slice_bitcast_fusion), channel_id=1, source_target_pairs={{6,0},{7,1},{0,2},{1,3},{2,4},{3,5},{4,6},{5,7},{14,8},{15,9},{8,1... | collective-permute-start | bytes 221192 | tf_op jit(solution)/shard_map/ppermute | solution.py:397
  13.9 5.4 %collective-permute-start.8 = (bf16[1,576,1152]{2,1,0:T(8,128)(2,1)}, bf16[1,576,1152]{2,1,0:T(8,128)(2,1)S(1)}, u32[]{:S(2)}, u32[]{:S(2)}) collective-permute-start(bf16[1,576,1152]{2,1,0:T(8,128)(2,1)} %wo_own), channel_id=1, source_target_pairs={{0,8},{8,0},{1,9},{9,1},{2,10},{10,2},{3,11},{11,3},{4,12},{12,4},... | collective-permute-start | bytes 3981320 | tf_op jit(solution)/shard_map/ppermute | solution.py:461
  14.0 11.3 %collective-permute-start.4 = (bf16[128,1152]{1,0:T(8,128)(2,1)S(1)}, bf16[128,1152]{1,0:T(8,128)(2,1)S(1)}, u32[]{:S(2)}, u32[]{:S(2)}) collective-permute-start(bf16[128,1152]{1,0:T(8,128)(2,1)S(1)} %pad_maximum_fusion.refs_0_), channel_id=1, source_target_pairs={{1,0},{0,1},{3,2},{2,3},{5,4},{4,5},{7,6},{6,7},{9,8},{8,9},{11,10... | collective-permute-start | bytes 884744 | tf_op jit(solution)/shard_map/ppermute | solution.py:397
  15.6 7.5 %collective-permute-start.5 = (bf16[32,1152]{1,0:T(8,128)(2,1)S(1)}, bf16[32,1152]{1,0:T(8,128)(2,1)S(1)}, u32[]{:S(2)}, u32[]{:S(2)}) collective-permute-start(bf16[32,1152]{1,0:T(8,128)(2,1)S(1)} %slice_bitcast_fusion), channel_id=1, source_target_pairs={{2,0},{3,1},{4,2},{5,3},{6,4},{7,5},{0,6},{1,7},{10,8},{11,9},{12,... | collective-permute-start | bytes 221192 | tf_op jit(solution)/shard_map/ppermute | solution.py:397
  17.4 7.9 %collective-permute-start.6 = (bf16[32,1152]{1,0:T(8,128)(2,1)S(1)}, bf16[32,1152]{1,0:T(8,128)(2,1)S(1)}, u32[]{:S(2)}, u32[]{:S(2)}) collective-permute-start(bf16[32,1152]{1,0:T(8,128)(2,1)S(1)} %slice_bitcast_fusion), channel_id=1, source_target_pairs={{4,0},{5,1},{6,2},{7,3},{0,4},{1,5},{2,6},{3,7},{12,8},{13,9},{14,... | collective-permute-start | bytes 221192 | tf_op jit(solution)/shard_map/ppermute | solution.py:397
  17.9 7.4 %collective-permute-start.7 = (bf16[32,1152]{1,0:T(8,128)(2,1)S(1)}, bf16[32,1152]{1,0:T(8,128)(2,1)S(1)}, u32[]{:S(2)}, u32[]{:S(2)}) collective-permute-start(bf16[32,1152]{1,0:T(8,128)(2,1)S(1)} %slice_bitcast_fusion), channel_id=1, source_target_pairs={{6,0},{7,1},{0,2},{1,3},{2,4},{3,5},{4,6},{5,7},{14,8},{15,9},{8,1... | collective-permute-start | bytes 221192 | tf_op jit(solution)/shard_map/ppermute | solution.py:397
  25.4 8.5 %collective-permute-start.9 = (bf16[128,1152]{1,0:T(8,128)(2,1)S(1)}, bf16[128,1152]{1,0:T(8,128)(2,1)S(1)}, u32[]{:S(2)}, u32[]{:S(2)}) collective-permute-start(bf16[128,1152]{1,0:T(8,128)(2,1)S(1)} %pad_maximum_fusion.1.refs_0_), channel_id=1, source_target_pairs={{1,0},{0,1},{3,2},{2,3},{5,4},{4,5},{7,6},{6,7},{9,8},{8,9},{11,10... | collective-permute-start | bytes 884744 | tf_op jit(solution)/shard_map/ppermute | solution.py:397
  27.9 4.9 %collective-permute-start.10 = (bf16[96,1152]{1,0:T(8,128)(2,1)S(1)}, bf16[96,1152]{1,0:T(8,128)(2,1)S(1)}, u32[]{:S(2)}, u32[]{:S(2)}) collective-permute-start(bf16[96,1152]{1,0:T(8,128)(2,1)S(1)} %get-tuple-element.65), channel_id=1, source_target_pairs={{0,8},{1,9},{2,10},{3,11},{4,12},{5,13},{6,14},{7,15},{16,24},{17,... | collective-permute-start | bytes 663560 | tf_op jit(solution)/shard_map/ppermute | solution.py:468
  29.2 3.6 %collective-permute-start.11 = (bf16[96,1152]{1,0:T(8,128)(2,1)S(1)}, bf16[96,1152]{1,0:T(8,128)(2,1)S(1)}, u32[]{:S(2)}, u32[]{:S(2)}) collective-permute-start(bf16[96,1152]{1,0:T(8,128)(2,1)S(1)} %get-tuple-element.66), channel_id=1, source_target_pairs={{0,8},{1,9},{2,10},{3,11},{4,12},{5,13},{6,14},{7,15},{16,24},{17,... | collective-permute-start | bytes 663560 | tf_op jit(solution)/shard_map/ppermute | solution.py:468
  30.5 2.3 %collective-permute-start.12 = (bf16[64,1152]{1,0:T(8,128)(2,1)S(1)}, bf16[64,1152]{1,0:T(8,128)(2,1)S(1)}, u32[]{:S(2)}, u32[]{:S(2)}) collective-permute-start(bf16[64,1152]{1,0:T(8,128)(2,1)S(1)} %get-tuple-element.67), channel_id=1, source_target_pairs={{0,8},{1,9},{2,10},{3,11},{4,12},{5,13},{6,14},{7,15},{16,24},{17,... | collective-permute-start | bytes 442376 | tf_op jit(solution)/shard_map/ppermute | solution.py:468
  33.9 11.4 %slice-start = ((s8[4718592]{0:T(1024)(128)(4,1)}), s8[4194304]{0:T(1024)(128)(4,1)S(1)}, s32[]{:S(2)}) async-start(s8[4718592]{0:T(1024)(128)(4,1)} %bitcast.28), calls=%async_computation | async-start | bytes 8388608
  33.9 5.1 %copy-start.4 = (bf16[1024,36]{1,0:T(8,128)(2,1)S(1)}, bf16[1024,36]{1,0:T(8,128)(2,1)}, u32[]{:S(2)}) copy-start(bf16[1024,36]{1,0:T(8,128)(2,1)} %constant.129.clone) | copy-start | bytes 221188
  33.9 5.1 %copy-start.5 = (bf16[36,512]{1,0:T(8,128)(2,1)S(1)}, bf16[36,512]{1,0:T(8,128)(2,1)}, u32[]{:S(2)}) copy-start(bf16[36,512]{1,0:T(8,128)(2,1)} %param.22) | copy-start | bytes 110596
  33.9 7.1 %copy-start.1 = (bf16[1152,16]{0,1:T(8,128)(2,1)S(1)}, bf16[1152,16]{0,1:T(8,128)(2,1)}, u32[]{:S(2)}) copy-start(bf16[1152,16]{0,1:T(8,128)(2,1)} %param.21) | copy-start | bytes 110596
  33.9 11.4 %slice-start.1 = ((s8[4718592]{0:T(1024)(128)(4,1)}), s8[524288]{0:T(1024)(128)(4,1)S(1)}, s32[]{:S(2)}) async-start(s8[4718592]{0:T(1024)(128)(4,1)} %bitcast.28), calls=%async_computation.1 | async-start | bytes 1048576
  38.9 6.4 %copy-start.2 = (f32[512]{0:T(512)S(1)}, f32[512]{0:T(512)}, u32[]{:S(2)}) copy-start(f32[512]{0:T(512)} %param.23) | copy-start | bytes 6148
  38.9 6.4 %copy-start.3 = (f32[512]{0:T(512)S(1)}, f32[512]{0:T(512)}, u32[]{:S(2)}) copy-start(f32[512]{0:T(512)} %param.25) | copy-start | bytes 6148
  38.9 2.1 %collective-permute-start.13 = (bf16[256,1152]{1,0:T(8,128)(2,1)S(1)}, bf16[256,1152]{1,0:T(8,128)(2,1)S(1)}, u32[]{:S(2)}, u32[]{:S(2)}) collective-permute-start(bf16[256,1152]{1,0:T(8,128)(2,1)S(1)} %get-tuple-element.78), channel_id=1, source_target_pairs={{0,8},{8,0},{1,9},{9,1},{2,10},{10,2},{3,11},{11,3},{4,12},{12,4},... | collective-permute-start | bytes 1769480 | tf_op jit(solution)/shard_map/ppermute | solution.py:473
  44.1 1.3 %collective-permute-start.14 = (f32[48,128]{1,0:T(8,128)S(1)}, f32[48,128]{1,0:T(8,128)S(1)}, u32[]{:S(2)}, u32[]{:S(2)}) collective-permute-start(f32[48,128]{1,0:T(8,128)S(1)} %tile_attention_and_patches.1.patch_ref), channel_id=1, source_target_pairs={{0,8},{8,0},{1,9},{9,1},{2,10},{10,2},{3,11},{11,3},{4,12},{12,4},... | collective-permute-start | bytes 73736 | tf_op jit(solution)/shard_map/ppermute | solution.py:480

commit v13 on v12

--- a/solution.py
+++ b/solution.py
@@ -385,16 +385,10 @@
     return n // inner, inner
 
 
-def shifted(block, k_outer, k_inner, cores=(0, 1)):
+def swapped(block, k_outer, k_inner):
     n = lax.axis_size("patch")
-    outer, inner = split_of(n)
-    route = []
-    for core in cores:
-        for i in range(n):
-            o, e = divmod(i, inner)
-            source = (o + k_outer) % outer * inner + (e + k_inner) % inner
-            route.append((core * n + source, core * n + i))
-    return lax.ppermute(block, ("pipe", "patch"), route)
+    _, inner = split_of(n)
+    return lax.ppermute(block, "patch", [(i ^ (k_outer * inner + k_inner), i) for i in range(n)])
 
 
 def local(
@@ -427,7 +421,7 @@
     w_qkv = jnp.swapaxes(w_qkv, 1, 2)
     w_qkv_other = lax.ppermute(w_qkv, "pipe", swap)
     tables = lax.all_gather(block_table[0], "pipe")
-    x_column = [shifted(own_tokens, k, 0) for k in range(1, outer)]
+    x_column = [swapped(own_tokens, k, 0) for k in range(1, outer)]
 
     time_row = lax.dynamic_index_in_dim(time_table, t_index[0], 0, keepdims=False)
     ones = jnp.asarray([[0.0], [1.0], [0.0]], F32)
@@ -446,8 +440,8 @@
     inside = (place % pitch < cols + 2) & (place < rows * pitch) & (column >= 0) & (column < TC)
     token = place // pitch * TC + jnp.clip(column, 0, TC - 1)
     source = token // own_count
-    k_outer = (source // inner - tile // inner) % outer
-    k_inner = (source % inner - tile % inner) % inner
+    k_outer = (source // inner) ^ (tile // inner)
+    k_inner = (source % inner) ^ (tile % inner)
     spot = (k_inner * outer + k_outer) * own_count + token % own_count
     idx = jnp.broadcast_to(jnp.where(inside, spot, -1)[:, None], (padded_rows, LANES)).astype(jnp.int32)
 
@@ -456,16 +450,16 @@
     )
     x_column = jnp.concatenate([own_tokens] + x_column, axis=0)
     x_column, own_stale, w_out = lax.optimization_barrier((x_column, own_stale, w_out))
-    x_pieces = [x_column] + [shifted(x_column, 0, k) for k in range(1, inner)]
-    stale_column = [own_stale] + [shifted(own_stale, k, 0) for k in range(1, outer)]
+    x_pieces = [x_column] + [swapped(x_column, 0, k) for k in range(1, inner)]
+    stale_column = [own_stale] + [swapped(own_stale, k, 0) for k in range(1, outer)]
     w_out_other = lax.ppermute(w_out, "pipe", swap)
     w_0, w_1, wo_0, wo_1 = weights_in_vmem(w_qkv, w_qkv_other, w_out, w_out_other)
     x_pieces, stale_column, w_0 = lax.optimization_barrier((x_pieces, stale_column, w_0))
     stale_column = jnp.concatenate(stale_column, axis=0)
     x_pieces, stale_column = lax.optimization_barrier((x_pieces, stale_column))
-    stale_pieces = [stale_column] + [shifted(stale_column, 0, k) for k in range(1, inner)]
+    stale_pieces = [stale_column] + [swapped(stale_column, 0, k) for k in range(1, inner)]
     x, query, fresh, *parts = project(x_pieces, vecs, w_0)
-    got_pieces = [lax.ppermute(part, "pipe", [(0, 1)]) for part in parts]
+    got_pieces = [lax.ppermute(part, "pipe", swap) for part in parts]
     x_tile, q_tile, fresh, send = first_block(
         stale_pieces, got_pieces, x, query, fresh, idx, vecs, w_1, wo_0
     )

time: 48.8 us -> 47.5 us (0.973)
  starting transfers between devices: 16.2 us -> 13.1 us
  waiting for transfers between devices: 8.75 us -> 10.6 us
    ppermute x11, starting transfers between devices: 15.4 us -> 12.3 us  [the longest x8 11.7 us: swapped(): lax.ppermute(block, 'patch', [(i ^ k_outer * inner + k_inner, i) for i in...]
    ppermute x11, waiting for transfers between devices: 6.11 us -> 7.97 us  [the longest x8 6.55 us: swapped(): lax.ppermute(block, 'patch', [(i ^ k_outer * inner + k_inner, i) for i in...]
where the time goes in v13:
time: 47.5 us; the launch traced here: 47.2 us
  Pallas kernels  16.7 us (35%)
  starting transfers between devices  13.1 us (28%)
  waiting for transfers between devices  10.6 us (22%)
  local copies, waits for them, and re-layouts  2.87 us (6%)
  blocking collectives  1.82 us (4%)
  other arithmetic  0.85 us (2%)
  between operations  0.85 us (2%)
    ppermute x8, starting transfers between devices, swapped(): lax.ppermute(block, 'patch', [(i ^ k_outer * inner + k_inner, i) for i in...  11.7 us
    ppermute x8, waiting for transfers between devices, swapped(): lax.ppermute(block, 'patch', [(i ^ k_outer * inner + k_inner, i) for i in...  6.55 us
    pallas_call x1, Pallas kernels, first_block(): pl.pallas_call(functools.partial(block_kernel, len(stale_pieces), len(got...  4.96 us
    pallas_call x1, Pallas kernels, weights_in_vmem(): pl.pallas_call(weights_kernel, out_shape=(jax.ShapeDtypeStruct((3 * DA, D...  3.7 us
    pallas_call x1, Pallas kernels, decode(): pl.pallas_call(functools.partial(decode_kernel, rows, cols, pitch), out_s...  3.14 us
    pallas_call x1, Pallas kernels, tile_block(): pl.pallas_call(tile_kernel, out_shape=jax.ShapeDtypeStruct((x.shape[0], L...  3.05 us
    pallas_call x1, Pallas kernels, project(): pl.pallas_call(functools.partial(project_kernel, len(pieces)), out_shape=...  1.89 us
    all_gather x1, blocking collectives, local(): tables = lax.all_gather(block_table[0], 'pipe')  1.82 us
  transfers between devices with their start and end apart: 15, of which 6 were waited for; matrix products, arithmetic and copies ran while one was open for 8% of the time, Pallas kernels for 12%

profile of v13, /device:TPU:0, one launch (start us, length us, event | category | flops | bytes accessed | tf_op | source)
XLA Modules:
  0.0 47.2 jit_solution(17330688793820227014)
XLA Ops:
  0.5 1.1 %dynamic-slice_bitcast_fusion = bf16[32,1152]{1,0:T(8,128)(2,1)S(1)} fusion(bf16[2,32,1152]{2,1,0:T(8,128)(2,1)} %param.14, s32[]{:T(128)S(6)} %select_n.80), kind=kLoop, calls=%fused_computation.5 | loop fusion | bytes 147460 | tf_op jit(solution)/shard_map/jit(dynamic_index_in_dim)/squeeze | solution.py:420
  1.6 2.5 %collective-permute-start = (bf16[32,1152]{1,0:T(8,128)(2,1)S(1)}, bf16[32,1152]{1,0:T(8,128)(2,1)S(1)}, u32[]{:S(2)}, u32[]{:S(2)}) collective-permute-start(bf16[32,1152]{1,0:T(8,128)(2,1)S(1)} %dynamic-slice_bitcast_fusion), channel_id=1, source_target_pairs={{2,0},{3,1},{0,2},{1,3},{6,4},{7,5},{4,6},{5,7},{10,8},{11,9},{8,1... | collective-permute-start | bytes 221192 | tf_op jit(solution)/shard_map/ppermute | solution.py:391
  4.1 2.6 %collective-permute-start.1 = (bf16[32,1152]{1,0:T(8,128)(2,1)S(1)}, bf16[32,1152]{1,0:T(8,128)(2,1)S(1)}, u32[]{:S(2)}, u32[]{:S(2)}) collective-permute-start(bf16[32,1152]{1,0:T(8,128)(2,1)S(1)} %dynamic-slice_bitcast_fusion), channel_id=1, source_target_pairs={{4,0},{5,1},{6,2},{7,3},{0,4},{1,5},{2,6},{3,7},{12,8},{13,9},{14,... | collective-permute-start | bytes 221192 | tf_op jit(solution)/shard_map/ppermute | solution.py:391
  7.4 0.7 %copy.19 = f32[1,3,1152]{2,1,0:T(4,128)S(1)} copy(f32[1,3,1152]{2,0,1:T(1,128)} %param.18) | data formatting | bytes 27648 | tf_op args[4]
  8.1 1.8 %all_gather.3 = f32[2,3,1152]{2,1,0:T(4,128)S(1)} all-gather(f32[1,3,1152]{2,1,0:T(4,128)S(1)} %copy.19), channel_id=1, replica_groups=mesh['grp'=2,'pipe'=2,'patch'=8] {'pipe'}, dimensions={0}, use_global_device_ids=true | all-gather | bytes 41472 | tf_op jit(solution)/shard_map/all_gather | solution.py:423
  10.0 0.7 %fusion.2 = (f32[3,1152]{1,0:T(4,128)S(1)}, f32[3,1152]{1,0:T(4,128)S(1)}) fusion(f32[1,3,1152]{2,0,1:T(1,128)S(1)} %constant_dynamic-slice_fusion, f32[2,3,1152]{2,1,0:T(4,128)S(1)} %all_gather.3, f32[3]{0:T(128)} %constant.120), kind=kLoop, calls=%fused_computation.10 | loop fusion | flops 13824 | bytes 69132 | tf_op jit(solution)/shard_map/add | solution.py:430
  10.7 0.9 %slice_bitcast_fusion = bf16[32,1152]{1,0:T(8,128)(2,1)S(1)} fusion(bf16[1,2,32,1152]{3,2,1,0:T(8,128)(2,1)} %param.15), kind=kLoop, calls=%fused_computation.4 | loop fusion | bytes 147456 | tf_op jit(solution)/shard_map/squeeze | solution.py:449
  11.7 1.4 %collective-permute-done.1 = bf16[32,1152]{1,0:T(8,128)(2,1)S(1)} collective-permute-done((bf16[32,1152]{1,0:T(8,128)(2,1)S(1)}, bf16[32,1152]{1,0:T(8,128)(2,1)S(1)}, u32[]{:S(2)}, u32[]{:S(2)}) %collective-permute-start.1) | collective-permute-done | bytes 73760 | tf_op jit(solution)/shard_map/ppermute | solution.py:391
  13.3 1.6 %collective-permute-start.4 = (bf16[128,1152]{1,0:T(8,128)(2,1)S(1)}, bf16[128,1152]{1,0:T(8,128)(2,1)S(1)}, u32[]{:S(2)}, u32[]{:S(2)}) collective-permute-start(bf16[128,1152]{1,0:T(8,128)(2,1)S(1)} %pad_maximum_fusion.refs_0_), channel_id=1, source_target_pairs={{1,0},{0,1},{3,2},{2,3},{5,4},{4,5},{7,6},{6,7},{9,8},{8,9},{11,10... | collective-permute-start | bytes 884744 | tf_op jit(solution)/shard_map/ppermute | solution.py:391
  14.9 1.6 %collective-permute-start.5 = (bf16[32,1152]{1,0:T(8,128)(2,1)S(1)}, bf16[32,1152]{1,0:T(8,128)(2,1)S(1)}, u32[]{:S(2)}, u32[]{:S(2)}) collective-permute-start(bf16[32,1152]{1,0:T(8,128)(2,1)S(1)} %slice_bitcast_fusion), channel_id=1, source_target_pairs={{2,0},{3,1},{0,2},{1,3},{6,4},{7,5},{4,6},{5,7},{10,8},{11,9},{8,1... | collective-permute-start | bytes 221192 | tf_op jit(solution)/shard_map/ppermute | solution.py:391
  16.4 1.6 %collective-permute-start.6 = (bf16[32,1152]{1,0:T(8,128)(2,1)S(1)}, bf16[32,1152]{1,0:T(8,128)(2,1)S(1)}, u32[]{:S(2)}, u32[]{:S(2)}) collective-permute-start(bf16[32,1152]{1,0:T(8,128)(2,1)S(1)} %slice_bitcast_fusion), channel_id=1, source_target_pairs={{4,0},{5,1},{6,2},{7,3},{0,4},{1,5},{2,6},{3,7},{12,8},{13,9},{14,... | collective-permute-start | bytes 221192 | tf_op jit(solution)/shard_map/ppermute | solution.py:391
  18.0 1.2 %collective-permute-start.7 = (bf16[32,1152]{1,0:T(8,128)(2,1)S(1)}, bf16[32,1152]{1,0:T(8,128)(2,1)S(1)}, u32[]{:S(2)}, u32[]{:S(2)}) collective-permute-start(bf16[32,1152]{1,0:T(8,128)(2,1)S(1)} %slice_bitcast_fusion), channel_id=1, source_target_pairs={{6,0},{7,1},{4,2},{5,3},{2,4},{3,5},{0,6},{1,7},{14,8},{15,9},{12,... | collective-permute-start | bytes 221192 | tf_op jit(solution)/shard_map/ppermute | solution.py:391
  19.3 3.7 %weights_by_block.1 = (bf16[1728,1152]{1,0:T(8,128)(2,1)S(1)}, bf16[1728,1152]{1,0:T(8,128)(2,1)S(1)}, bf16[640,1152]{1,0:T(8,128)(2,1)S(1)}, bf16[640,1152]{1,0:T(8,128)(2,1)S(1)}) custom-call(bf16[1,1728,1152]{2,1,0:T(8,128)(2,1)} %bitcast.34, bf16[1,1728,1152]{2,1,0:T(8,128)(2,1)} %collective-permute-done.3.other_ref, bf16[1,576,1152]{2,1,0:T(8,128)(2,1)} %wo_own, ...), custom_call_target="tpu_custom_call" | custom-call | tf_op jit(solution)/shard_map/weights_by_block/pallas_call | solution.py:118
  23.0 2.3 %collective-permute-done.6 = bf16[32,1152]{1,0:T(8,128)(2,1)S(1)} collective-permute-done((bf16[32,1152]{1,0:T(8,128)(2,1)S(1)}, bf16[32,1152]{1,0:T(8,128)(2,1)S(1)}, u32[]{:S(2)}, u32[]{:S(2)}) %collective-permute-start.6) | collective-permute-done | bytes 73760 | tf_op jit(solution)/shard_map/ppermute | solution.py:391
  25.3 0.6 %collective-permute-start.9 = (bf16[128,1152]{1,0:T(8,128)(2,1)S(1)}, bf16[128,1152]{1,0:T(8,128)(2,1)S(1)}, u32[]{:S(2)}, u32[]{:S(2)}) collective-permute-start(bf16[128,1152]{1,0:T(8,128)(2,1)S(1)} %pad_maximum_fusion.1.refs_0_), channel_id=1, source_target_pairs={{1,0},{0,1},{3,2},{2,3},{5,4},{4,5},{7,6},{6,7},{9,8},{8,9},{11,10... | collective-permute-start | bytes 884744 | tf_op jit(solution)/shard_map/ppermute | solution.py:391
  25.9 1.9 %layer_norm_and_projections.1 = (bf16[256,1152]{1,0:T(8,128)(2,1)S(1)}, bf16[256,640]{1,0:T(8,128)(2,1)S(1)}, bf16[256,1152]{1,0:T(8,128)(2,1)S(1)}, bf16[96,115...) custom-call(bf16[128,1152]{1,0:T(8,128)(2,1)S(1)} %pad_maximum_fusion.refs_0_, ...), custom_call_target="tpu_custom_call" | custom-call | tf_op jit(solution)/shard_map/layer_norm_and_projections/pallas_call | solution.py:167
  27.9 0.5 %collective-permute-start.11 = (bf16[96,1152]{1,0:T(8,128)(2,1)S(1)}, bf16[96,1152]{1,0:T(8,128)(2,1)S(1)}, u32[]{:S(2)}, u32[]{:S(2)}) collective-permute-start(bf16[96,1152]{1,0:T(8,128)(2,1)S(1)} %get-tuple-element.66), channel_id=1, source_target_pairs={{0,8},{8,0},{1,9},{9,1},{2,10},{10,2},{3,11},{11,3},{4,12},{12,4},... | collective-permute-start | bytes 663560 | tf_op jit(solution)/shard_map/ppermute | solution.py:462
  28.5 1.4 %collective-permute-done.12.refs_4_ = bf16[64,1152]{1,0:T(8,128)(2,1)S(1)} collective-permute-done((bf16[64,1152]{1,0:T(8,128)(2,1)S(1)}, bf16[64,1152]{1,0:T(8,128)(2,1)S(1)}, u32[]{:S(2)}, u32[]{:S(2)}) %collective-permute-start.12) | collective-permute-done | bytes 147488 | tf_op jit(solution)/shard_map/ppermute | solution.py:462
  29.9 2.8 %collective-permute-done.9.refs_1_ = bf16[128,1152]{1,0:T(8,128)(2,1)S(1)} collective-permute-done((bf16[128,1152]{1,0:T(8,128)(2,1)S(1)}, bf16[128,1152]{1,0:T(8,128)(2,1)S(1)}, u32[]{:S(2)}, u32[]{:S(2)}) %collective-permute-start.9) | collective-permute-done | bytes 294944 | tf_op jit(solution)/shard_map/ppermute | solution.py:391
  32.7 5.0 %attention_and_next_keys.1 = (bf16[48,1152]{1,0:T(8,128)(2,1)S(1)}, bf16[48,640]{1,0:T(8,128)(2,1)S(1)}, bf16[256,1152]{1,0:T(8,128)(2,1)S(1)}, bf16[256,1152]{1,0:T(8,128)(2,1)S(1)}) custom-call(bf16[128,1152]{1,0:T(8,128)(2,1)S(1)} %pad_maximum_fusion.1.refs_0_, bf16[128,1152]{1,0:T(8,128)(2,1)S(1)} %collective-permute-done.9.refs_1_, ...), custom_call_target="tpu_custom_call" | custom-call | tf_op jit(solution)/shard_map/attention_and_next_keys/pallas_call | solution.py:240
  38.2 1.6 %collective-permute-done.13.got_ref = bf16[256,1152]{1,0:T(8,128)(2,1)S(1)} collective-permute-done((bf16[256,1152]{1,0:T(8,128)(2,1)S(1)}, bf16[256,1152]{1,0:T(8,128)(2,1)S(1)}, u32[]{:S(2)}, u32[]{:S(2)}) %collective-permute-start.13) | collective-permute-done | bytes 589856 | tf_op jit(solution)/shard_map/ppermute | solution.py:467
  39.8 3.0 %tile_attention_and_patches.1.patch_ref = f32[48,128]{1,0:T(8,128)S(1)} custom-call(bf16[48,1152]{1,0:T(8,128)(2,1)S(1)} %get-tuple-element.74.x_ref, bf16[48,640]{1,0:T(8,128)(2,1)S(1)} %get-tuple-element.75.q_ref, bf16[256,1152]{1,0:T(8,128)(2,1)S(1)} %get-tuple-element.76.kv_ref, bf16[256,1152]{1,0:T(8,128)(2,1)S(1)} %collective-permute-done.13.got_ref, ...), custom_call_target="tpu_custom_call" | custom-call | tf_op jit(solution)/shard_map/tile_attention_and_patches/pallas_call | solution.py:274
  43.0 1.1 %collective-permute-done.14.got_ref = f32[48,128]{1,0:T(8,128)S(1)} collective-permute-done((f32[48,128]{1,0:T(8,128)S(1)}, f32[48,128]{1,0:T(8,128)S(1)}, u32[]{:S(2)}, u32[]{:S(2)}) %collective-permute-start.14) | collective-permute-done | bytes 24608 | tf_op jit(solution)/shard_map/ppermute | solution.py:474
  44.1 3.1 %decoder_convolutions.1 = bf16[4,128,512]{2,1,0:T(8,128)(2,1)} custom-call(f32[48,128]{1,0:T(8,128)S(1)} %tile_attention_and_patches.1.patch_ref, f32[48,128]{1,0:T(8,128)S(1)} %collective-permute-done.14.got_ref, s32[48,128]{1,0:T(8,128)S(1)} %broadcast_in_dim.14.refs_8_.idx_ref, bf16[1024,512]{1,0:T(8,128)(2,1)S(1)} %fusion.wp_ref, f32[1,512]{1,0:T(1,128)S(1)} %bitcast.31, ...), custom_call_target="tpu_custom_call" | custom-call | tf_op jit(solution)/shard_map/decoder_convolutions/pallas_call | solution.py:356
  (42 shorter events, 1.6 us)
Async XLA Ops:
  0.0 9.9 %copy-start = (f32[100,5,1152]{2,0,1:T(8,128)S(1)}, f32[100,5,1152]{2,0,1:T(8,128)}, u32[]{:S(2)}) copy-start(f32[100,5,1152]{2,0,1:T(8,128)} %param.19) | copy-start | bytes 6912004
  0.0 13.1 %collective-permute-start.3 = (bf16[1,1728,1152]{2,1,0:T(8,128)(2,1)}, bf16[1,1728,1152]{2,1,0:T(8,128)(2,1)}, u32[]{:S(2)}, u32[]{:S(2)}) collective-permute-start(bf16[1,1728,1152]{2,1,0:T(8,128)(2,1)} %bitcast.33), channel_id=1, source_target_pairs={{0,8},{8,0},{1,9},{9,1},{2,10},{10,2},{3,11},{11,3},{4,12},{12,4},... | collective-permute-start | bytes 11943944 | tf_op jit(solution)/shard_map/ppermute | solution.py:422
  1.6 10.1 %collective-permute-start = (bf16[32,1152]{1,0:T(8,128)(2,1)S(1)}, bf16[32,1152]{1,0:T(8,128)(2,1)S(1)}, u32[]{:S(2)}, u32[]{:S(2)}) collective-permute-start(bf16[32,1152]{1,0:T(8,128)(2,1)S(1)} %dynamic-slice_bitcast_fusion), channel_id=1, source_target_pairs={{2,0},{3,1},{0,2},{1,3},{6,4},{7,5},{4,6},{5,7},{10,8},{11,9},{8,1... | collective-permute-start | bytes 221192 | tf_op jit(solution)/shard_map/ppermute | solution.py:391
  4.1 9.0 %collective-permute-start.1 = (bf16[32,1152]{1,0:T(8,128)(2,1)S(1)}, bf16[32,1152]{1,0:T(8,128)(2,1)S(1)}, u32[]{:S(2)}, u32[]{:S(2)}) collective-permute-start(bf16[32,1152]{1,0:T(8,128)(2,1)S(1)} %dynamic-slice_bitcast_fusion), channel_id=1, source_target_pairs={{4,0},{5,1},{6,2},{7,3},{0,4},{1,5},{2,6},{3,7},{12,8},{13,9},{14,... | collective-permute-start | bytes 221192 | tf_op jit(solution)/shard_map/ppermute | solution.py:391
  6.7 6.4 %collective-permute-start.2 = (bf16[32,1152]{1,0:T(8,128)(2,1)S(1)}, bf16[32,1152]{1,0:T(8,128)(2,1)S(1)}, u32[]{:S(2)}, u32[]{:S(2)}) collective-permute-start(bf16[32,1152]{1,0:T(8,128)(2,1)S(1)} %dynamic-slice_bitcast_fusion), channel_id=1, source_target_pairs={{6,0},{7,1},{4,2},{5,3},{2,4},{3,5},{0,6},{1,7},{14,8},{15,9},{12,... | collective-permute-start | bytes 221192 | tf_op jit(solution)/shard_map/ppermute | solution.py:391
  13.2 6.1 %collective-permute-start.8 = (bf16[1,576,1152]{2,1,0:T(8,128)(2,1)}, bf16[1,576,1152]{2,1,0:T(8,128)(2,1)S(1)}, u32[]{:S(2)}, u32[]{:S(2)}) collective-permute-start(bf16[1,576,1152]{2,1,0:T(8,128)(2,1)} %wo_own), channel_id=1, source_target_pairs={{0,8},{8,0},{1,9},{9,1},{2,10},{10,2},{3,11},{11,3},{4,12},{12,4},... | collective-permute-start | bytes 3981320 | tf_op jit(solution)/shard_map/ppermute | solution.py:455
  13.3 12.0 %collective-permute-start.4 = (bf16[128,1152]{1,0:T(8,128)(2,1)S(1)}, bf16[128,1152]{1,0:T(8,128)(2,1)S(1)}, u32[]{:S(2)}, u32[]{:S(2)}) collective-permute-start(bf16[128,1152]{1,0:T(8,128)(2,1)S(1)} %pad_maximum_fusion.refs_0_), channel_id=1, source_target_pairs={{1,0},{0,1},{3,2},{2,3},{5,4},{4,5},{7,6},{6,7},{9,8},{8,9},{11,10... | collective-permute-start | bytes 884744 | tf_op jit(solution)/shard_map/ppermute | solution.py:391
  14.9 8.1 %collective-permute-start.5 = (bf16[32,1152]{1,0:T(8,128)(2,1)S(1)}, bf16[32,1152]{1,0:T(8,128)(2,1)S(1)}, u32[]{:S(2)}, u32[]{:S(2)}) collective-permute-start(bf16[32,1152]{1,0:T(8,128)(2,1)S(1)} %slice_bitcast_fusion), channel_id=1, source_target_pairs={{2,0},{3,1},{0,2},{1,3},{6,4},{7,5},{4,6},{5,7},{10,8},{11,9},{8,1... | collective-permute-start | bytes 221192 | tf_op jit(solution)/shard_map/ppermute | solution.py:391
  16.4 8.9 %collective-permute-start.6 = (bf16[32,1152]{1,0:T(8,128)(2,1)S(1)}, bf16[32,1152]{1,0:T(8,128)(2,1)S(1)}, u32[]{:S(2)}, u32[]{:S(2)}) collective-permute-start(bf16[32,1152]{1,0:T(8,128)(2,1)S(1)} %slice_bitcast_fusion), channel_id=1, source_target_pairs={{4,0},{5,1},{6,2},{7,3},{0,4},{1,5},{2,6},{3,7},{12,8},{13,9},{14,... | collective-permute-start | bytes 221192 | tf_op jit(solution)/shard_map/ppermute | solution.py:391
  18.0 7.3 %collective-permute-start.7 = (bf16[32,1152]{1,0:T(8,128)(2,1)S(1)}, bf16[32,1152]{1,0:T(8,128)(2,1)S(1)}, u32[]{:S(2)}, u32[]{:S(2)}) collective-permute-start(bf16[32,1152]{1,0:T(8,128)(2,1)S(1)} %slice_bitcast_fusion), channel_id=1, source_target_pairs={{6,0},{7,1},{4,2},{5,3},{2,4},{3,5},{0,6},{1,7},{14,8},{15,9},{12,... | collective-permute-start | bytes 221192 | tf_op jit(solution)/shard_map/ppermute | solution.py:391
  25.3 7.3 %collective-permute-start.9 = (bf16[128,1152]{1,0:T(8,128)(2,1)S(1)}, bf16[128,1152]{1,0:T(8,128)(2,1)S(1)}, u32[]{:S(2)}, u32[]{:S(2)}) collective-permute-start(bf16[128,1152]{1,0:T(8,128)(2,1)S(1)} %pad_maximum_fusion.1.refs_0_), channel_id=1, source_target_pairs={{1,0},{0,1},{3,2},{2,3},{5,4},{4,5},{7,6},{6,7},{9,8},{8,9},{11,10... | collective-permute-start | bytes 884744 | tf_op jit(solution)/shard_map/ppermute | solution.py:391
  27.8 2.1 %collective-permute-start.10 = (bf16[96,1152]{1,0:T(8,128)(2,1)S(1)}, bf16[96,1152]{1,0:T(8,128)(2,1)S(1)}, u32[]{:S(2)}, u32[]{:S(2)}) collective-permute-start(bf16[96,1152]{1,0:T(8,128)(2,1)S(1)} %get-tuple-element.65), channel_id=1, source_target_pairs={{0,8},{8,0},{1,9},{9,1},{2,10},{10,2},{3,11},{11,3},{4,12},{12,4},... | collective-permute-start | bytes 663560 | tf_op jit(solution)/shard_map/ppermute | solution.py:462
  27.9 2.0 %collective-permute-start.11 = (bf16[96,1152]{1,0:T(8,128)(2,1)S(1)}, bf16[96,1152]{1,0:T(8,128)(2,1)S(1)}, u32[]{:S(2)}, u32[]{:S(2)}) collective-permute-start(bf16[96,1152]{1,0:T(8,128)(2,1)S(1)} %get-tuple-element.66), channel_id=1, source_target_pairs={{0,8},{8,0},{1,9},{9,1},{2,10},{10,2},{3,11},{11,3},{4,12},{12,4},... | collective-permute-start | bytes 663560 | tf_op jit(solution)/shard_map/ppermute | solution.py:462
  28.4 1.5 %collective-permute-start.12 = (bf16[64,1152]{1,0:T(8,128)(2,1)S(1)}, bf16[64,1152]{1,0:T(8,128)(2,1)S(1)}, u32[]{:S(2)}, u32[]{:S(2)}) collective-permute-start(bf16[64,1152]{1,0:T(8,128)(2,1)S(1)} %get-tuple-element.67), channel_id=1, source_target_pairs={{0,8},{8,0},{1,9},{9,1},{2,10},{10,2},{3,11},{11,3},{4,12},{12,4},... | collective-permute-start | bytes 442376 | tf_op jit(solution)/shard_map/ppermute | solution.py:462
  32.7 11.4 %slice-start = ((s8[4718592]{0:T(1024)(128)(4,1)}), s8[4194304]{0:T(1024)(128)(4,1)S(1)}, s32[]{:S(2)}) async-start(s8[4718592]{0:T(1024)(128)(4,1)} %bitcast.28), calls=%async_computation | async-start | bytes 8388608
  32.7 5.1 %copy-start.4 = (bf16[1024,36]{1,0:T(8,128)(2,1)S(1)}, bf16[1024,36]{1,0:T(8,128)(2,1)}, u32[]{:S(2)}) copy-start(bf16[1024,36]{1,0:T(8,128)(2,1)} %constant.114.clone) | copy-start | bytes 221188
  32.7 5.1 %copy-start.5 = (bf16[36,512]{1,0:T(8,128)(2,1)S(1)}, bf16[36,512]{1,0:T(8,128)(2,1)}, u32[]{:S(2)}) copy-start(bf16[36,512]{1,0:T(8,128)(2,1)} %param.22) | copy-start | bytes 110596
  32.7 7.1 %copy-start.1 = (bf16[1152,16]{0,1:T(8,128)(2,1)S(1)}, bf16[1152,16]{0,1:T(8,128)(2,1)}, u32[]{:S(2)}) copy-start(bf16[1152,16]{0,1:T(8,128)(2,1)} %param.21) | copy-start | bytes 110596
  32.7 11.4 %slice-start.1 = ((s8[4718592]{0:T(1024)(128)(4,1)}), s8[524288]{0:T(1024)(128)(4,1)S(1)}, s32[]{:S(2)}) async-start(s8[4718592]{0:T(1024)(128)(4,1)} %bitcast.28), calls=%async_computation.1 | async-start | bytes 1048576
  37.7 6.4 %copy-start.2 = (f32[512]{0:T(512)S(1)}, f32[512]{0:T(512)}, u32[]{:S(2)}) copy-start(f32[512]{0:T(512)} %param.23) | copy-start | bytes 6148
  37.7 6.4 %copy-start.3 = (f32[512]{0:T(512)S(1)}, f32[512]{0:T(512)}, u32[]{:S(2)}) copy-start(f32[512]{0:T(512)} %param.25) | copy-start | bytes 6148
  37.7 2.1 %collective-permute-start.13 = (bf16[256,1152]{1,0:T(8,128)(2,1)S(1)}, bf16[256,1152]{1,0:T(8,128)(2,1)S(1)}, u32[]{:S(2)}, u32[]{:S(2)}) collective-permute-start(bf16[256,1152]{1,0:T(8,128)(2,1)S(1)} %get-tuple-element.78), channel_id=1, source_target_pairs={{0,8},{8,0},{1,9},{9,1},{2,10},{10,2},{3,11},{11,3},{4,12},{12,4},... | collective-permute-start | bytes 1769480 | tf_op jit(solution)/shard_map/ppermute | solution.py:467
  42.8 1.3 %collective-permute-start.14 = (f32[48,128]{1,0:T(8,128)S(1)}, f32[48,128]{1,0:T(8,128)S(1)}, u32[]{:S(2)}, u32[]{:S(2)}) collective-permute-start(f32[48,128]{1,0:T(8,128)S(1)} %tile_attention_and_patches.1.patch_ref), channel_id=1, source_target_pairs={{0,8},{8,0},{1,9},{9,1},{2,10},{10,2},{3,11},{11,3},{4,12},{12,4},... | collective-permute-start | bytes 73736 | tf_op jit(solution)/shard_map/ppermute | solution.py:474

commit v14 on v13

--- a/solution.py
+++ b/solution.py
@@ -49,28 +49,73 @@
     return start // LANES * LANES, -(-(start + DH) // LANES) * LANES
 
 
-def attend(query, kv_ref):
-    count = query.shape[0]
+def head_scores(query, kv_ref, head):
+    first, last = lane_window(head * DH)
+    lane = lax.broadcasted_iota(jnp.int32, (query.shape[0], last - first), 1) + first
+    own = (lane >= head * DH) & (lane < (head + 1) * DH)
+    return dot_t(jnp.where(own, query[:, first:last], jnp.zeros((), BF16)), kv_ref[:, first:last])
+
+
+def value_window(head):
+    return lane_window(DA + head * DH)
+
+
+def weigh(exponent, kv_ref, head):
+    first, last = value_window(head)
+    return dot(exponent.astype(BF16), kv_ref[:, first:last])
+
+
+def spread(outs):
     pieces = [None] * (DP // LANES)
-    for head in range(HEADS):
-        first, last = lane_window(head * DH)
-        lane = lax.broadcasted_iota(jnp.int32, (count, last - first), 1) + first
-        own = (lane >= head * DH) & (lane < (head + 1) * DH)
-        q = jnp.where(own, query[:, first:last], jnp.zeros((), BF16))
-        scores = dot_t(q, kv_ref[:, first:last])
-        exponent = jnp.exp2(scores - jnp.max(scores, axis=1, keepdims=True))
-        total = jnp.sum(exponent, axis=1, keepdims=True)
+    for head, out in enumerate(outs):
+        first, last = value_window(head)
         start = DA + head * DH
-        first, last = lane_window(start)
-        numerator = dot(exponent.astype(BF16), kv_ref[:, first:last])
-        lane = lax.broadcasted_iota(jnp.int32, (count, last - first), 1) + first
-        own = (lane >= start) & (lane < start + DH)
-        out = jnp.where(own, numerator * (1.0 / total), 0.0)
+        lane = lax.broadcasted_iota(jnp.int32, out.shape, 1) + first
+        out = jnp.where((lane >= start) & (lane < start + DH), out, 0.0)
         for i in range((last - first) // LANES):
             at = (first - (DA - SHIFT)) // LANES + i
             part = out[:, i * LANES : (i + 1) * LANES]
             pieces[at] = part if pieces[at] is None else pieces[at] + part
     return jnp.concatenate(pieces, axis=1)
+
+
+def attend(query, kv_ref):
+    outs = []
+    for head in range(HEADS):
+        scores = head_scores(query, kv_ref, head)
+        exponent = jnp.exp2(scores - jnp.max(scores, axis=1, keepdims=True))
+        total = jnp.sum(exponent, axis=1, keepdims=True)
+        outs.append(weigh(exponent, kv_ref, head) * (1.0 / total))
+    return spread(outs)
+
+
+def attend_begin(query, kv_ref):
+    outs = []
+    lane = lax.broadcasted_iota(jnp.int32, (query.shape[0], LANES), 1)
+    state = jnp.zeros((query.shape[0], LANES), F32)
+    for head in range(HEADS):
+        scores = head_scores(query, kv_ref, head)
+        top = jnp.max(scores, axis=1, keepdims=True)
+        exponent = jnp.exp2(scores - top)
+        total = jnp.sum(exponent, axis=1, keepdims=True)
+        outs.append(weigh(exponent, kv_ref, head))
+        state = jnp.where(lane == head, top, jnp.where(lane == HEADS + head, total, state))
+    return spread(outs), state
+
+
+def attend_end(query, kv_ref, sums, state):
+    outs = []
+    for head in range(HEADS):
+        scores = head_scores(query, kv_ref, head)
+        before, total = state[:, head : head + 1], state[:, HEADS + head : HEADS + head + 1]
+        top = jnp.maximum(before, jnp.max(scores, axis=1, keepdims=True))
+        exponent = jnp.exp2(scores - top)
+        keep = jnp.exp2(before - top)
+        total = keep * total + jnp.sum(exponent, axis=1, keepdims=True)
+        first, last = value_window(head)
+        earlier = sums[:, first - (DA - SHIFT) : last - (DA - SHIFT)]
+        outs.append((keep * earlier + weigh(exponent, kv_ref, head)) * (1.0 / total))
+    return spread(outs)
 
 
 def each_block(count, body):
@@ -162,8 +207,7 @@
 
 def project(pieces, vecs, weights):
     count = sum(piece.shape[0] for piece in pieces)
-    step = 3 * count // 8
-    parts = (step, step, count - 2 * step)
+    parts = (count // 4,) * 4
     return pl.pallas_call(
         functools.partial(project_kernel, len(pieces)),
         out_shape=(
@@ -173,7 +217,7 @@
         )
         + tuple(jax.ShapeDtypeStruct((part, 2 * DA), BF16) for part in parts),
         in_specs=[VMEM] * (len(pieces) + 2),
-        out_specs=(VMEM,) * 6,
+        out_specs=(VMEM,) * 7,
         compiler_params=params(count),
         name="layer_norm_and_projections",
     )(*pieces, vecs, weights)
@@ -183,37 +227,53 @@
     return pltpu.with_memory_space_constraint(array, pltpu.HBM)
 
 
-def gather_keys(all_ref, kv_ref, stale_refs, got_refs):
-    count = kv_ref.shape[0]
-    first_core = lax.axis_index("pipe") == 0
-    all_ref[:count] = kv_ref[...]
-
-    @pl.when(first_core)
-    def _():
-        join(stale_refs, all_ref.at[count:])
-
-    @pl.when(jnp.logical_not(first_core))
-    def _():
-        join(got_refs, all_ref.at[count:])
+def fresh_kernel(q_ref, kv_ref, sum_ref, state_ref):
+    def body(start, size):
+        rows = pl.ds(start, size)
+        sums, state = attend_begin(q_ref[rows], kv_ref)
+        sum_ref[rows] = sums
+        state_ref[rows] = state
+
+    each_block(q_ref.shape[0], body)
+
+
+def attend_fresh(q, kv):
+    count = q.shape[0]
+    return pl.pallas_call(
+        fresh_kernel,
+        out_shape=(jax.ShapeDtypeStruct((count, DP), F32), jax.ShapeDtypeStruct((count, LANES), F32)),
+        in_specs=[VMEM] * 2,
+        out_specs=(VMEM,) * 2,
+        compiler_params=params(count),
+        name="attention_over_own_keys",
+    )(q, kv)
 
 
 def block_kernel(n_pieces, n_got, *refs):
     stale_refs = refs[:n_pieces]
     got_refs = refs[n_pieces : n_pieces + n_got]
     (
-        x_ref, q_ref, kv_ref, idx_ref, vec_ref, w1_ref, wo_ref,
-        xt_ref, qt_ref, kv1_ref, send_ref, all_ref, pick_ref,
+        x_ref, q_ref, sum_ref, state_ref, idx_ref, vec_ref, w1_ref, wo_ref,
+        xt_ref, qt_ref, kv1_ref, send_ref, other_ref, pick_ref,
     ) = refs[n_pieces + n_got :]
     count = x_ref.shape[0]
     first_core = lax.axis_index("pipe") == 0
-    gather_keys(all_ref, kv_ref, stale_refs, got_refs)
     join(stale_refs, send_ref)
+
+    @pl.when(first_core)
+    def _():
+        join(stale_refs, other_ref)
+
+    @pl.when(jnp.logical_not(first_core))
+    def _():
+        join(got_refs, other_ref)
+
     pick_ref[...] = jnp.zeros_like(pick_ref)
     tile_rows = idx_ref.shape[0]
 
     def body(start, size):
         rows = pl.ds(start, size)
-        attended = attend(q_ref[rows], all_ref).astype(BF16)
+        attended = attend_end(q_ref[rows], other_ref, sum_ref[rows], state_ref[rows]).astype(BF16)
         branch = dot(attended, wo_ref[...])
         x1 = (x_ref[rows].astype(F32) + vec_ref[2:3] * branch).astype(BF16)
         modulated = normed(x1.astype(F32), vec_ref[4:5], vec_ref[3:4])
@@ -234,7 +294,7 @@
     qt_ref[...] = query_of(pick_ref[1].astype(BF16), w1_ref)
 
 
-def first_block(stale_pieces, got_pieces, x, q, kv, idx, vecs, w_next, wo_block):
+def first_block(stale_pieces, got_pieces, x, q, sums, state, idx, vecs, w_next, wo_block):
     count = x.shape[0]
     tile_rows = idx.shape[0]
     return pl.pallas_call(
@@ -245,15 +305,15 @@
             jax.ShapeDtypeStruct((count, 2 * DA), BF16),
             jax.ShapeDtypeStruct((count, 2 * DA), BF16),
         ),
-        in_specs=[VMEM] * (len(stale_pieces) + len(got_pieces) + 7),
+        in_specs=[VMEM] * (len(stale_pieces) + len(got_pieces) + 8),
         out_specs=(VMEM,) * 4,
         scratch_shapes=[
-            pltpu.VMEM((2 * count, 2 * DA), BF16),
+            pltpu.VMEM((count, 2 * DA), BF16),
             pltpu.VMEM((2, tile_rows, D), F32),
         ],
         compiler_params=params(count),
         name="attention_and_next_keys",
-    )(*stale_pieces, *got_pieces, x, q, kv, idx, vecs, w_next, wo_block)
+    )(*stale_pieces, *got_pieces, x, q, sums, state, idx, vecs, w_next, wo_block)
 
 
 def tile_kernel(x_ref, q_ref, kv_ref, got_ref, idx_ref, vec_ref, wf_ref, wo_ref, patch_ref, all_ref):
@@ -422,6 +482,8 @@
     w_qkv_other = lax.ppermute(w_qkv, "pipe", swap)
     tables = lax.all_gather(block_table[0], "pipe")
     x_column = [swapped(own_tokens, k, 0) for k in range(1, outer)]
+    own_stale = stale_kv[0, 1]
+    stale_line = [swapped(own_stale, 0, k) for k in range(1, inner)]
 
     time_row = lax.dynamic_index_in_dim(time_table, t_index[0], 0, keepdims=False)
     ones = jnp.asarray([[0.0], [1.0], [0.0]], F32)
@@ -445,23 +507,24 @@
     spot = (k_inner * outer + k_outer) * own_count + token % own_count
     idx = jnp.broadcast_to(jnp.where(inside, spot, -1)[:, None], (padded_rows, LANES)).astype(jnp.int32)
 
-    x_column, w_qkv_other, vecs, idx, own_stale, w_out = lax.optimization_barrier(
-        (x_column, w_qkv_other, vecs, idx, stale_kv[0, 1], w_out)
+    x_column, w_qkv_other, vecs, idx, own_stale, stale_line, w_out = lax.optimization_barrier(
+        (x_column, w_qkv_other, vecs, idx, own_stale, stale_line, w_out)
     )
     x_column = jnp.concatenate([own_tokens] + x_column, axis=0)
     x_column, own_stale, w_out = lax.optimization_barrier((x_column, own_stale, w_out))
     x_pieces = [x_column] + [swapped(x_column, 0, k) for k in range(1, inner)]
-    stale_column = [own_stale] + [swapped(own_stale, k, 0) for k in range(1, outer)]
+    stale_column = [swapped(own_stale, k, 0) for k in range(1, outer)]
     w_out_other = lax.ppermute(w_out, "pipe", swap)
     w_0, w_1, wo_0, wo_1 = weights_in_vmem(w_qkv, w_qkv_other, w_out, w_out_other)
     x_pieces, stale_column, w_0 = lax.optimization_barrier((x_pieces, stale_column, w_0))
     stale_column = jnp.concatenate(stale_column, axis=0)
     x_pieces, stale_column = lax.optimization_barrier((x_pieces, stale_column))
-    stale_pieces = [stale_column] + [swapped(stale_column, 0, k) for k in range(1, inner)]
+    stale_pieces = [own_stale, stale_column] + stale_line + [swapped(stale_column, 0, k) for k in range(1, inner)]
     x, query, fresh, *parts = project(x_pieces, vecs, w_0)
     got_pieces = [lax.ppermute(part, "pipe", swap) for part in parts]
+    sums, state = attend_fresh(query, fresh)
     x_tile, q_tile, fresh, send = first_block(
-        stale_pieces, got_pieces, x, query, fresh, idx, vecs, w_1, wo_0
+        stale_pieces, got_pieces, x, query, sums, state, idx, vecs, w_1, wo_0
     )
     send, w_in = lax.optimization_barrier((send, w_in))
     got = lax.ppermute(send, "pipe", swap)

time: 47.5 us -> 47.8 us (level)
  waiting for transfers between devices: 10.6 us -> 6.05 us
  Pallas kernels: 16.7 us -> 19.3 us
  starting transfers between devices: 13.1 us -> 15.4 us
    ppermute x8 -> x9, waiting for transfers between devices: 6.55 us -> 3.28 us  [swapped(): lax.ppermute(block, 'patch', [(i ^ k_outer * inner + k_inner, i) for i in...]
    ppermute x8 -> x9, starting transfers between devices: 11.7 us -> 13.3 us  [swapped(): lax.ppermute(block, 'patch', [(i ^ k_outer * inner + k_inner, i) for i in...]
    pallas_call x1, Pallas kernels: 4.96 us -> 6.61 us  [first_block(): pl.pallas_call(functools.partial(block_kernel, len(stale_pieces), len(got...]
    ppermute x3 -> x4, waiting for transfers between devices: 1.42 us -> 0.13 us  [local(): got_pieces = [lax.ppermute(part, 'pipe', swap) for part in parts]]
    pallas_call x0 -> x1, Pallas kernels: none -> 0.91 us  [attend_fresh(): pl.pallas_call(fresh_kernel, out_shape=(jax.ShapeDtypeStruct((count, DP),...]
    ppermute x3 -> x4, starting transfers between devices: 0.65 us -> 1.08 us  [local(): got_pieces = [lax.ppermute(part, 'pipe', swap) for part in parts]]
  transfers between devices with their start and end apart: 15 -> 17, of which waited for: 6 -> 5; matrix products, arithmetic and copies ran while one was open for 8% -> 8% of each run, Pallas kernels for 12% -> 14%
where the time goes in v14:
time: 47.8 us; the launch traced here: 47.5 us
  Pallas kernels  19.3 us (40%)
  starting transfers between devices  15.4 us (32%)
  waiting for transfers between devices  6.05 us (13%)
  local copies, waits for them, and re-layouts  2.86 us (6%)
  blocking collectives  1.82 us (4%)
  between operations  0.9 us (2%)
  other arithmetic  0.85 us (2%)
    ppermute x9, starting transfers between devices, swapped(): lax.ppermute(block, 'patch', [(i ^ k_outer * inner + k_inner, i) for i in...  13.3 us
    pallas_call x1, Pallas kernels, first_block(): pl.pallas_call(functools.partial(block_kernel, len(stale_pieces), len(got...  6.61 us
    pallas_call x1, Pallas kernels, weights_in_vmem(): pl.pallas_call(weights_kernel, out_shape=(jax.ShapeDtypeStruct((3 * DA, D...  3.7 us
    ppermute x9, waiting for transfers between devices, swapped(): lax.ppermute(block, 'patch', [(i ^ k_outer * inner + k_inner, i) for i in...  3.28 us
    pallas_call x1, Pallas kernels, decode(): pl.pallas_call(functools.partial(decode_kernel, rows, cols, pitch), out_s...  3.14 us
    pallas_call x1, Pallas kernels, tile_block(): pl.pallas_call(tile_kernel, out_shape=jax.ShapeDtypeStruct((x.shape[0], L...  3.05 us
    pallas_call x1, Pallas kernels, project(): pl.pallas_call(functools.partial(project_kernel, len(pieces)), out_shape=...  1.89 us
    all_gather x1, blocking collectives, local(): tables = lax.all_gather(block_table[0], 'pipe')  1.82 us
  transfers between devices with their start and end apart: 17, of which 5 were waited for; matrix products, arithmetic and copies ran while one was open for 8% of the time, Pallas kernels for 14%

profile of v14, /device:TPU:0, one launch (start us, length us, event | category | flops | bytes accessed | tf_op | source)
XLA Modules:
  0.0 47.5 jit_solution(9909561366894281909)
XLA Ops:
  0.5 1.1 %dynamic-slice_bitcast_fusion = bf16[32,1152]{1,0:T(8,128)(2,1)S(1)} fusion(bf16[2,32,1152]{2,1,0:T(8,128)(2,1)} %param.14, s32[]{:T(128)S(6)} %select_n.80), kind=kLoop, calls=%fused_computation.5 | loop fusion | bytes 147460 | tf_op jit(solution)/shard_map/jit(dynamic_index_in_dim)/squeeze | solution.py:480
  1.6 2.5 %collective-permute-start = (bf16[32,1152]{1,0:T(8,128)(2,1)S(1)}, bf16[32,1152]{1,0:T(8,128)(2,1)S(1)}, u32[]{:S(2)}, u32[]{:S(2)}) collective-permute-start(bf16[32,1152]{1,0:T(8,128)(2,1)S(1)} %dynamic-slice_bitcast_fusion), channel_id=1, source_target_pairs={{2,0},{3,1},{0,2},{1,3},{6,4},{7,5},{4,6},{5,7},{10,8},{11,9},{8,1... | collective-permute-start | bytes 221192 | tf_op jit(solution)/shard_map/ppermute | solution.py:451
  4.1 2.6 %collective-permute-start.1 = (bf16[32,1152]{1,0:T(8,128)(2,1)S(1)}, bf16[32,1152]{1,0:T(8,128)(2,1)S(1)}, u32[]{:S(2)}, u32[]{:S(2)}) collective-permute-start(bf16[32,1152]{1,0:T(8,128)(2,1)S(1)} %dynamic-slice_bitcast_fusion), channel_id=1, source_target_pairs={{4,0},{5,1},{6,2},{7,3},{0,4},{1,5},{2,6},{3,7},{12,8},{13,9},{14,... | collective-permute-start | bytes 221192 | tf_op jit(solution)/shard_map/ppermute | solution.py:451
  6.7 0.9 %slice_bitcast_fusion.refs_0_ = bf16[32,1152]{1,0:T(8,128)(2,1)S(1)} fusion(bf16[1,2,32,1152]{3,2,1,0:T(8,128)(2,1)} %param.15), kind=kLoop, calls=%fused_computation.4 | loop fusion | bytes 147456 | tf_op jit(solution)/shard_map/squeeze | solution.py:485
  7.6 1.7 %collective-permute-start.4 = (bf16[32,1152]{1,0:T(8,128)(2,1)S(1)}, bf16[32,1152]{1,0:T(8,128)(2,1)S(1)}, u32[]{:S(2)}, u32[]{:S(2)}) collective-permute-start(bf16[32,1152]{1,0:T(8,128)(2,1)S(1)} %slice_bitcast_fusion.refs_0_), channel_id=1, source_target_pairs={{1,0},{0,1},{3,2},{2,3},{5,4},{4,5},{7,6},{6,7},{9,8},{8,9},{11,10... | collective-permute-start | bytes 221192 | tf_op jit(solution)/shard_map/ppermute | solution.py:451
  10.0 0.7 %copy.19 = f32[1,3,1152]{2,1,0:T(4,128)S(1)} copy(f32[1,3,1152]{2,0,1:T(1,128)} %param.18) | data formatting | bytes 27648 | tf_op args[4]
  10.7 1.8 %all_gather.3 = f32[2,3,1152]{2,1,0:T(4,128)S(1)} all-gather(f32[1,3,1152]{2,1,0:T(4,128)S(1)} %copy.19), channel_id=1, replica_groups=mesh['grp'=2,'pipe'=2,'patch'=8] {'pipe'}, dimensions={0}, use_global_device_ids=true | all-gather | bytes 41472 | tf_op jit(solution)/shard_map/all_gather | solution.py:483
  12.6 0.7 %fusion.2 = (f32[3,1152]{1,0:T(4,128)S(1)}, f32[3,1152]{1,0:T(4,128)S(1)}) fusion(f32[1,3,1152]{2,0,1:T(1,128)S(1)} %constant_dynamic-slice_fusion, f32[2,3,1152]{2,1,0:T(4,128)S(1)} %all_gather.3, f32[3]{0:T(128)} %constant.120), kind=kLoop, calls=%fused_computation.10 | loop fusion | flops 13824 | bytes 69132 | tf_op jit(solution)/shard_map/add | solution.py:492
  13.8 1.1 %collective-permute-start.5 = (bf16[128,1152]{1,0:T(8,128)(2,1)S(1)}, bf16[128,1152]{1,0:T(8,128)(2,1)S(1)}, u32[]{:S(2)}, u32[]{:S(2)}) collective-permute-start(bf16[128,1152]{1,0:T(8,128)(2,1)S(1)} %pad_maximum_fusion.refs_0_), channel_id=1, source_target_pairs={{1,0},{0,1},{3,2},{2,3},{5,4},{4,5},{7,6},{6,7},{9,8},{8,9},{11,10... | collective-permute-start | bytes 884744 | tf_op jit(solution)/shard_map/ppermute | solution.py:451
  14.9 1.6 %collective-permute-start.6 = (bf16[32,1152]{1,0:T(8,128)(2,1)S(1)}, bf16[32,1152]{1,0:T(8,128)(2,1)S(1)}, u32[]{:S(2)}, u32[]{:S(2)}) collective-permute-start(bf16[32,1152]{1,0:T(8,128)(2,1)S(1)} %slice_bitcast_fusion.refs_0_), channel_id=1, source_target_pairs={{2,0},{3,1},{0,2},{1,3},{6,4},{7,5},{4,6},{5,7},{10,8},{11,9},{8,1... | collective-permute-start | bytes 221192 | tf_op jit(solution)/shard_map/ppermute | solution.py:451
  16.4 2.0 %collective-permute-start.7 = (bf16[32,1152]{1,0:T(8,128)(2,1)S(1)}, bf16[32,1152]{1,0:T(8,128)(2,1)S(1)}, u32[]{:S(2)}, u32[]{:S(2)}) collective-permute-start(bf16[32,1152]{1,0:T(8,128)(2,1)S(1)} %slice_bitcast_fusion.refs_0_), channel_id=1, source_target_pairs={{4,0},{5,1},{6,2},{7,3},{0,4},{1,5},{2,6},{3,7},{12,8},{13,9},{14,... | collective-permute-start | bytes 221192 | tf_op jit(solution)/shard_map/ppermute | solution.py:451
  18.4 0.8 %collective-permute-start.8 = (bf16[32,1152]{1,0:T(8,128)(2,1)S(1)}, bf16[32,1152]{1,0:T(8,128)(2,1)S(1)}, u32[]{:S(2)}, u32[]{:S(2)}) collective-permute-start(bf16[32,1152]{1,0:T(8,128)(2,1)S(1)} %slice_bitcast_fusion.refs_0_), channel_id=1, source_target_pairs={{6,0},{7,1},{4,2},{5,3},{2,4},{3,5},{0,6},{1,7},{14,8},{15,9},{12,... | collective-permute-start | bytes 221192 | tf_op jit(solution)/shard_map/ppermute | solution.py:451
  19.3 3.7 %weights_by_block.1 = (bf16[1728,1152]{1,0:T(8,128)(2,1)S(1)}, bf16[1728,1152]{1,0:T(8,128)(2,1)S(1)}, bf16[640,1152]{1,0:T(8,128)(2,1)S(1)}, bf16[640,1152]{1,0:T(8,128)(2,1)S(1)}) custom-call(bf16[1,1728,1152]{2,1,0:T(8,128)(2,1)} %bitcast.34, bf16[1,1728,1152]{2,1,0:T(8,128)(2,1)} %collective-permute-done.3.other_ref, bf16[1,576,1152]{2,1,0:T(8,128)(2,1)} %wo_own, ...), custom_call_target="tpu_custom_call" | custom-call | tf_op jit(solution)/shard_map/weights_by_block/pallas_call | solution.py:163
  23.0 2.3 %collective-permute-done.7 = bf16[32,1152]{1,0:T(8,128)(2,1)S(1)} collective-permute-done((bf16[32,1152]{1,0:T(8,128)(2,1)S(1)}, bf16[32,1152]{1,0:T(8,128)(2,1)S(1)}, u32[]{:S(2)}, u32[]{:S(2)}) %collective-permute-start.7) | collective-permute-done | bytes 73760 | tf_op jit(solution)/shard_map/ppermute | solution.py:451
  25.3 1.0 %collective-permute-start.10 = (bf16[96,1152]{1,0:T(8,128)(2,1)S(1)}, bf16[96,1152]{1,0:T(8,128)(2,1)S(1)}, u32[]{:S(2)}, u32[]{:S(2)}) collective-permute-start(bf16[96,1152]{1,0:T(8,128)(2,1)S(1)} %pad_maximum_fusion.1.refs_1_), channel_id=1, source_target_pairs={{1,0},{0,1},{3,2},{2,3},{5,4},{4,5},{7,6},{6,7},{9,8},{8,9},{11,10... | collective-permute-start | bytes 663560 | tf_op jit(solution)/shard_map/ppermute | solution.py:451
  26.3 1.9 %layer_norm_and_projections.1 = (bf16[256,1152]{1,0:T(8,128)(2,1)S(1)}, bf16[256,640]{1,0:T(8,128)(2,1)S(1)}, bf16[256,1152]{1,0:T(8,128)(2,1)S(1)}, bf16[64,115...) custom-call(bf16[128,1152]{1,0:T(8,128)(2,1)S(1)} %pad_maximum_fusio, ...), custom_call_target="tpu_custom_call" | custom-call | tf_op jit(solution)/shard_map/layer_norm_and_projections/pallas_call | solution.py:211
  28.3 0.5 %collective-permute-start.12 = (bf16[64,1152]{1,0:T(8,128)(2,1)S(1)}, bf16[64,1152]{1,0:T(8,128)(2,1)S(1)}, u32[]{:S(2)}, u32[]{:S(2)}) collective-permute-start(bf16[64,1152]{1,0:T(8,128)(2,1)S(1)} %get-tuple-element.69), channel_id=1, source_target_pairs={{0,8},{8,0},{1,9},{9,1},{2,10},{10,2},{3,11},{11,3},{4,12},{12,4},... | collective-permute-start | bytes 442376 | tf_op jit(solution)/shard_map/ppermute | solution.py:524
  29.3 0.9 %attention_over_own_keys.1 = (f32[256,640]{1,0:T(8,128)S(1)}, f32[256,128]{1,0:T(8,128)S(1)}) custom-call(bf16[256,640]{1,0:T(8,128)(2,1)S(1)} %get-tuple-element.73.q_ref.refs_9_, bf16[256,1152]{1,0:T(8,128)(2,1)S(1)} %get-tuple-element.74.kv_ref), custom_call_target="tpu_custom_call" | custom-call | tf_op jit(solution)/shard_map/attention_over_own_keys/pallas_call | solution.py:242
  30.4 0.9 %collective-permute-done.10.refs_3_ = bf16[96,1152]{1,0:T(8,128)(2,1)S(1)} collective-permute-done((bf16[96,1152]{1,0:T(8,128)(2,1)S(1)}, bf16[96,1152]{1,0:T(8,128)(2,1)S(1)}, u32[]{:S(2)}, u32[]{:S(2)}) %collective-permute-start.10) | collective-permute-done | bytes 221216 | tf_op jit(solution)/shard_map/ppermute | solution.py:451
  31.3 6.6 %attention_and_next_keys.1 = (bf16[48,1152]{1,0:T(8,128)(2,1)S(1)}, bf16[48,640]{1,0:T(8,128)(2,1)S(1)}, bf16[256,1152]{1,0:T(8,128)(2,1)S(1)}, bf16[256,1152]{1,0:T(8,128)(2,1)S(1)}) custom-call(bf16[32,1152]{1,0:T(8,128)(2,1)S(1)} %slice_bitcast_fusion.refs_0_, bf16[96,1152]{1,0:T(8,128)(2,1)S(1)} %pad_maximum_fusion.1.refs_1_, ...), custom_call_target="tpu_custom_call" | custom-call | tf_op jit(solution)/shard_map/attention_and_next_keys/pallas_call | solution.py:300
  38.5 1.6 %collective-permute-done.15.got_ref = bf16[256,1152]{1,0:T(8,128)(2,1)S(1)} collective-permute-done((bf16[256,1152]{1,0:T(8,128)(2,1)S(1)}, bf16[256,1152]{1,0:T(8,128)(2,1)S(1)}, u32[]{:S(2)}, u32[]{:S(2)}) %collective-permute-start.15) | collective-permute-done | bytes 589856 | tf_op jit(solution)/shard_map/ppermute | solution.py:530
  40.1 3.1 %tile_attention_and_patches.1.patch_ref = f32[48,128]{1,0:T(8,128)S(1)} custom-call(bf16[48,1152]{1,0:T(8,128)(2,1)S(1)} %get-tuple-element.80.x_ref, bf16[48,640]{1,0:T(8,128)(2,1)S(1)} %get-tuple-element.81.q_ref, bf16[256,1152]{1,0:T(8,128)(2,1)S(1)} %get-tuple-element.82.kv_ref, bf16[256,1152]{1,0:T(8,128)(2,1)S(1)} %collective-permute-done.15.got_ref, ...), custom_call_target="tpu_custom_call" | custom-call | tf_op jit(solution)/shard_map/tile_attention_and_patches/pallas_call | solution.py:334
  43.3 1.1 %collective-permute-done.16.got_ref = f32[48,128]{1,0:T(8,128)S(1)} collective-permute-done((f32[48,128]{1,0:T(8,128)S(1)}, f32[48,128]{1,0:T(8,128)S(1)}, u32[]{:S(2)}, u32[]{:S(2)}) %collective-permute-start.16) | collective-permute-done | bytes 24608 | tf_op jit(solution)/shard_map/ppermute | solution.py:537
  44.4 3.1 %decoder_convolutions.1 = bf16[4,128,512]{2,1,0:T(8,128)(2,1)} custom-call(f32[48,128]{1,0:T(8,128)S(1)} %tile_attention_and_patches.1.patch_ref, f32[48,128]{1,0:T(8,128)S(1)} %collective-permute-done.16.got_ref, s32[48,128]{1,0:T(8,128)S(1)} %broadcast_in_dim.14.refs_12_.idx_ref, bf16[1024,512]{1,0:T(8,128)(2,1)S(1)} %fusion.wp_ref, ...), custom_call_target="tpu_custom_call" | custom-call | tf_op jit(solution)/shard_map/decoder_convolutions/pallas_call | solution.py:416
  (47 shorter events, 2.3 us)
Async XLA Ops:
  0.0 12.5 %copy-start = (f32[100,5,1152]{2,0,1:T(8,128)S(1)}, f32[100,5,1152]{2,0,1:T(8,128)}, u32[]{:S(2)}) copy-start(f32[100,5,1152]{2,0,1:T(8,128)} %param.19) | copy-start | bytes 6912004
  0.0 13.4 %collective-permute-start.3 = (bf16[1,1728,1152]{2,1,0:T(8,128)(2,1)}, bf16[1,1728,1152]{2,1,0:T(8,128)(2,1)}, u32[]{:S(2)}, u32[]{:S(2)}) collective-permute-start(bf16[1,1728,1152]{2,1,0:T(8,128)(2,1)} %bitcast.33), channel_id=1, source_target_pairs={{0,8},{8,0},{1,9},{9,1},{2,10},{10,2},{3,11},{11,3},{4,12},{12,4},... | collective-permute-start | bytes 11943944 | tf_op jit(solution)/shard_map/ppermute | solution.py:482
  1.6 11.8 %collective-permute-start = (bf16[32,1152]{1,0:T(8,128)(2,1)S(1)}, bf16[32,1152]{1,0:T(8,128)(2,1)S(1)}, u32[]{:S(2)}, u32[]{:S(2)}) collective-permute-start(bf16[32,1152]{1,0:T(8,128)(2,1)S(1)} %dynamic-slice_bitcast_fusion), channel_id=1, source_target_pairs={{2,0},{3,1},{0,2},{1,3},{6,4},{7,5},{4,6},{5,7},{10,8},{11,9},{8,1... | collective-permute-start | bytes 221192 | tf_op jit(solution)/shard_map/ppermute | solution.py:451
  4.1 9.3 %collective-permute-start.1 = (bf16[32,1152]{1,0:T(8,128)(2,1)S(1)}, bf16[32,1152]{1,0:T(8,128)(2,1)S(1)}, u32[]{:S(2)}, u32[]{:S(2)}) collective-permute-start(bf16[32,1152]{1,0:T(8,128)(2,1)S(1)} %dynamic-slice_bitcast_fusion), channel_id=1, source_target_pairs={{4,0},{5,1},{6,2},{7,3},{0,4},{1,5},{2,6},{3,7},{12,8},{13,9},{14,... | collective-permute-start | bytes 221192 | tf_op jit(solution)/shard_map/ppermute | solution.py:451
  6.7 6.7 %collective-permute-start.2 = (bf16[32,1152]{1,0:T(8,128)(2,1)S(1)}, bf16[32,1152]{1,0:T(8,128)(2,1)S(1)}, u32[]{:S(2)}, u32[]{:S(2)}) collective-permute-start(bf16[32,1152]{1,0:T(8,128)(2,1)S(1)} %dynamic-slice_bitcast_fusion), channel_id=1, source_target_pairs={{6,0},{7,1},{4,2},{5,3},{2,4},{3,5},{0,6},{1,7},{14,8},{15,9},{12,... | collective-permute-start | bytes 221192 | tf_op jit(solution)/shard_map/ppermute | solution.py:451
  7.6 5.8 %collective-permute-start.4 = (bf16[32,1152]{1,0:T(8,128)(2,1)S(1)}, bf16[32,1152]{1,0:T(8,128)(2,1)S(1)}, u32[]{:S(2)}, u32[]{:S(2)}) collective-permute-start(bf16[32,1152]{1,0:T(8,128)(2,1)S(1)} %slice_bitcast_fusion.refs_0_), channel_id=1, source_target_pairs={{1,0},{0,1},{3,2},{2,3},{5,4},{4,5},{7,6},{6,7},{9,8},{8,9},{11,10... | collective-permute-start | bytes 221192 | tf_op jit(solution)/shard_map/ppermute | solution.py:451
  13.5 5.7 %collective-permute-start.9 = (bf16[1,576,1152]{2,1,0:T(8,128)(2,1)}, bf16[1,576,1152]{2,1,0:T(8,128)(2,1)S(1)}, u32[]{:S(2)}, u32[]{:S(2)}) collective-permute-start(bf16[1,576,1152]{2,1,0:T(8,128)(2,1)} %wo_own), channel_id=1, source_target_pairs={{0,8},{8,0},{1,9},{9,1},{2,10},{10,2},{3,11},{11,3},{4,12},{12,4},... | collective-permute-start | bytes 3981320 | tf_op jit(solution)/shard_map/ppermute | solution.py:517
  13.8 11.5 %collective-permute-start.5 = (bf16[128,1152]{1,0:T(8,128)(2,1)S(1)}, bf16[128,1152]{1,0:T(8,128)(2,1)S(1)}, u32[]{:S(2)}, u32[]{:S(2)}) collective-permute-start(bf16[128,1152]{1,0:T(8,128)(2,1)S(1)} %pad_maximum_fusion.refs_0_), channel_id=1, source_target_pairs={{1,0},{0,1},{3,2},{2,3},{5,4},{4,5},{7,6},{6,7},{9,8},{8,9},{11,10... | collective-permute-start | bytes 884744 | tf_op jit(solution)/shard_map/ppermute | solution.py:451
  14.9 8.1 %collective-permute-start.6 = (bf16[32,1152]{1,0:T(8,128)(2,1)S(1)}, bf16[32,1152]{1,0:T(8,128)(2,1)S(1)}, u32[]{:S(2)}, u32[]{:S(2)}) collective-permute-start(bf16[32,1152]{1,0:T(8,128)(2,1)S(1)} %slice_bitcast_fusion.refs_0_), channel_id=1, source_target_pairs={{2,0},{3,1},{0,2},{1,3},{6,4},{7,5},{4,6},{5,7},{10,8},{11,9},{8,1... | collective-permute-start | bytes 221192 | tf_op jit(solution)/shard_map/ppermute | solution.py:451
  16.4 8.9 %collective-permute-start.7 = (bf16[32,1152]{1,0:T(8,128)(2,1)S(1)}, bf16[32,1152]{1,0:T(8,128)(2,1)S(1)}, u32[]{:S(2)}, u32[]{:S(2)}) collective-permute-start(bf16[32,1152]{1,0:T(8,128)(2,1)S(1)} %slice_bitcast_fusion.refs_0_), channel_id=1, source_target_pairs={{4,0},{5,1},{6,2},{7,3},{0,4},{1,5},{2,6},{3,7},{12,8},{13,9},{14,... | collective-permute-start | bytes 221192 | tf_op jit(solution)/shard_map/ppermute | solution.py:451
  18.4 6.9 %collective-permute-start.8 = (bf16[32,1152]{1,0:T(8,128)(2,1)S(1)}, bf16[32,1152]{1,0:T(8,128)(2,1)S(1)}, u32[]{:S(2)}, u32[]{:S(2)}) collective-permute-start(bf16[32,1152]{1,0:T(8,128)(2,1)S(1)} %slice_bitcast_fusion.refs_0_), channel_id=1, source_target_pairs={{6,0},{7,1},{4,2},{5,3},{2,4},{3,5},{0,6},{1,7},{14,8},{15,9},{12,... | collective-permute-start | bytes 221192 | tf_op jit(solution)/shard_map/ppermute | solution.py:451
  25.3 6.0 %collective-permute-start.10 = (bf16[96,1152]{1,0:T(8,128)(2,1)S(1)}, bf16[96,1152]{1,0:T(8,128)(2,1)S(1)}, u32[]{:S(2)}, u32[]{:S(2)}) collective-permute-start(bf16[96,1152]{1,0:T(8,128)(2,1)S(1)} %pad_maximum_fusion.1.refs_1_), channel_id=1, source_target_pairs={{1,0},{0,1},{3,2},{2,3},{5,4},{4,5},{7,6},{6,7},{9,8},{8,9},{11,10... | collective-permute-start | bytes 663560 | tf_op jit(solution)/shard_map/ppermute | solution.py:451
  28.2 2.0 %collective-permute-start.11 = (bf16[64,1152]{1,0:T(8,128)(2,1)S(1)}, bf16[64,1152]{1,0:T(8,128)(2,1)S(1)}, u32[]{:S(2)}, u32[]{:S(2)}) collective-permute-start(bf16[64,1152]{1,0:T(8,128)(2,1)S(1)} %get-tuple-element.68), channel_id=1, source_target_pairs={{0,8},{8,0},{1,9},{9,1},{2,10},{10,2},{3,11},{11,3},{4,12},{12,4},... | collective-permute-start | bytes 442376 | tf_op jit(solution)/shard_map/ppermute | solution.py:524
  28.3 1.9 %collective-permute-start.12 = (bf16[64,1152]{1,0:T(8,128)(2,1)S(1)}, bf16[64,1152]{1,0:T(8,128)(2,1)S(1)}, u32[]{:S(2)}, u32[]{:S(2)}) collective-permute-start(bf16[64,1152]{1,0:T(8,128)(2,1)S(1)} %get-tuple-element.69), channel_id=1, source_target_pairs={{0,8},{8,0},{1,9},{9,1},{2,10},{10,2},{3,11},{11,3},{4,12},{12,4},... | collective-permute-start | bytes 442376 | tf_op jit(solution)/shard_map/ppermute | solution.py:524
  28.8 1.4 %collective-permute-start.13 = (bf16[64,1152]{1,0:T(8,128)(2,1)S(1)}, bf16[64,1152]{1,0:T(8,128)(2,1)S(1)}, u32[]{:S(2)}, u32[]{:S(2)}) collective-permute-start(bf16[64,1152]{1,0:T(8,128)(2,1)S(1)} %get-tuple-element.70), channel_id=1, source_target_pairs={{0,8},{8,0},{1,9},{9,1},{2,10},{10,2},{3,11},{11,3},{4,12},{12,4},... | collective-permute-start | bytes 442376 | tf_op jit(solution)/shard_map/ppermute | solution.py:524
  28.9 1.5 %collective-permute-start.14 = (bf16[64,1152]{1,0:T(8,128)(2,1)S(1)}, bf16[64,1152]{1,0:T(8,128)(2,1)S(1)}, u32[]{:S(2)}, u32[]{:S(2)}) collective-permute-start(bf16[64,1152]{1,0:T(8,128)(2,1)S(1)} %get-tuple-element.71), channel_id=1, source_target_pairs={{0,8},{8,0},{1,9},{9,1},{2,10},{10,2},{3,11},{11,3},{4,12},{12,4},... | collective-permute-start | bytes 442376 | tf_op jit(solution)/shard_map/ppermute | solution.py:524
  31.3 13.1 %slice-start = ((s8[4718592]{0:T(1024)(128)(4,1)}), s8[4194304]{0:T(1024)(128)(4,1)S(1)}, s32[]{:S(2)}) async-start(s8[4718592]{0:T(1024)(128)(4,1)} %bitcast.28), calls=%async_computation | async-start | bytes 8388608
  31.3 6.7 %copy-start.4 = (bf16[1024,36]{1,0:T(8,128)(2,1)S(1)}, bf16[1024,36]{1,0:T(8,128)(2,1)}, u32[]{:S(2)}) copy-start(bf16[1024,36]{1,0:T(8,128)(2,1)} %constant.114.clone) | copy-start | bytes 221188
  31.3 6.7 %copy-start.5 = (bf16[36,512]{1,0:T(8,128)(2,1)S(1)}, bf16[36,512]{1,0:T(8,128)(2,1)}, u32[]{:S(2)}) copy-start(bf16[36,512]{1,0:T(8,128)(2,1)} %param.22) | copy-start | bytes 110596
  31.3 8.7 %copy-start.1 = (bf16[1152,16]{0,1:T(8,128)(2,1)S(1)}, bf16[1152,16]{0,1:T(8,128)(2,1)}, u32[]{:S(2)}) copy-start(bf16[1152,16]{0,1:T(8,128)(2,1)} %param.21) | copy-start | bytes 110596
  31.3 13.0 %slice-start.1 = ((s8[4718592]{0:T(1024)(128)(4,1)}), s8[524288]{0:T(1024)(128)(4,1)S(1)}, s32[]{:S(2)}) async-start(s8[4718592]{0:T(1024)(128)(4,1)} %bitcast.28), calls=%async_computation.1 | async-start | bytes 1048576
  38.0 6.4 %copy-start.2 = (f32[512]{0:T(512)S(1)}, f32[512]{0:T(512)}, u32[]{:S(2)}) copy-start(f32[512]{0:T(512)} %param.23) | copy-start | bytes 6148
  38.0 2.1 %collective-permute-start.15 = (bf16[256,1152]{1,0:T(8,128)(2,1)S(1)}, bf16[256,1152]{1,0:T(8,128)(2,1)S(1)}, u32[]{:S(2)}, u32[]{:S(2)}) collective-permute-start(bf16[256,1152]{1,0:T(8,128)(2,1)S(1)} %get-tuple-element.84), channel_id=1, source_target_pairs={{0,8},{8,0},{1,9},{9,1},{2,10},{10,2},{3,11},{11,3},{4,12},{12,4},... | collective-permute-start | bytes 1769480 | tf_op jit(solution)/shard_map/ppermute | solution.py:530
  43.1 1.3 %collective-permute-start.16 = (f32[48,128]{1,0:T(8,128)S(1)}, f32[48,128]{1,0:T(8,128)S(1)}, u32[]{:S(2)}, u32[]{:S(2)}) collective-permute-start(f32[48,128]{1,0:T(8,128)S(1)} %tile_attention_and_patches.1.patch_ref), channel_id=1, source_target_pairs={{0,8},{8,0},{1,9},{9,1},{2,10},{10,2},{3,11},{11,3},{4,12},{12,4},... | collective-permute-start | bytes 73736 | tf_op jit(solution)/shard_map/ppermute | solution.py:537
  (1 other events, 6.4 us)

commit v15 on v14

--- a/solution.py
+++ b/solution.py
@@ -244,7 +244,7 @@
         out_shape=(jax.ShapeDtypeStruct((count, DP), F32), jax.ShapeDtypeStruct((count, LANES), F32)),
         in_specs=[VMEM] * 2,
         out_specs=(VMEM,) * 2,
-        compiler_params=params(count),
+        compiler_params=params(kv.shape[0]),
         name="attention_over_own_keys",
     )(q, kv)
 
@@ -253,27 +253,28 @@
     stale_refs = refs[:n_pieces]
     got_refs = refs[n_pieces : n_pieces + n_got]
     (
-        x_ref, q_ref, sum_ref, state_ref, idx_ref, vec_ref, w1_ref, wo_ref,
-        xt_ref, qt_ref, kv1_ref, send_ref, other_ref, pick_ref,
+        x_ref, q_ref, kv_ref, idx_ref, vec_ref, w1_ref, wo_ref,
+        xt_ref, qt_ref, kv1_ref, send_ref, all_ref, pick_ref,
     ) = refs[n_pieces + n_got :]
     count = x_ref.shape[0]
     first_core = lax.axis_index("pipe") == 0
     join(stale_refs, send_ref)
+    all_ref[:count] = kv_ref[...]
 
     @pl.when(first_core)
     def _():
-        join(stale_refs, other_ref)
+        join(stale_refs, all_ref.at[count:])
 
     @pl.when(jnp.logical_not(first_core))
     def _():
-        join(got_refs, other_ref)
+        join(got_refs, all_ref.at[count:])
 
     pick_ref[...] = jnp.zeros_like(pick_ref)
     tile_rows = idx_ref.shape[0]
 
     def body(start, size):
         rows = pl.ds(start, size)
-        attended = attend_end(q_ref[rows], other_ref, sum_ref[rows], state_ref[rows]).astype(BF16)
+        attended = attend(q_ref[rows], all_ref).astype(BF16)
         branch = dot(attended, wo_ref[...])
         x1 = (x_ref[rows].astype(F32) + vec_ref[2:3] * branch).astype(BF16)
         modulated = normed(x1.astype(F32), vec_ref[4:5], vec_ref[3:4])
@@ -294,7 +295,7 @@
     qt_ref[...] = query_of(pick_ref[1].astype(BF16), w1_ref)
 
 
-def first_block(stale_pieces, got_pieces, x, q, sums, state, idx, vecs, w_next, wo_block):
+def first_block(stale_pieces, got_pieces, x, q, kv, idx, vecs, w_next, wo_block):
     count = x.shape[0]
     tile_rows = idx.shape[0]
     return pl.pallas_call(
@@ -305,22 +306,19 @@
             jax.ShapeDtypeStruct((count, 2 * DA), BF16),
             jax.ShapeDtypeStruct((count, 2 * DA), BF16),
         ),
-        in_specs=[VMEM] * (len(stale_pieces) + len(got_pieces) + 8),
+        in_specs=[VMEM] * (len(stale_pieces) + len(got_pieces) + 7),
         out_specs=(VMEM,) * 4,
         scratch_shapes=[
-            pltpu.VMEM((count, 2 * DA), BF16),
+            pltpu.VMEM((2 * count, 2 * DA), BF16),
             pltpu.VMEM((2, tile_rows, D), F32),
         ],
         compiler_params=params(count),
         name="attention_and_next_keys",
-    )(*stale_pieces, *got_pieces, x, q, sums, state, idx, vecs, w_next, wo_block)
-
-
-def tile_kernel(x_ref, q_ref, kv_ref, got_ref, idx_ref, vec_ref, wf_ref, wo_ref, patch_ref, all_ref):
-    count = kv_ref.shape[0]
-    all_ref[:count] = kv_ref[...]
-    all_ref[count:] = got_ref[...]
-    attended = attend(q_ref[...], all_ref).astype(BF16)
+    )(*stale_pieces, *got_pieces, x, q, kv, idx, vecs, w_next, wo_block)
+
+
+def tile_kernel(x_ref, q_ref, sum_ref, state_ref, got_ref, idx_ref, vec_ref, wf_ref, wo_ref, patch_ref):
+    attended = attend_end(q_ref[...], got_ref, sum_ref[...], state_ref[...]).astype(BF16)
     branch = dot(attended, wo_ref[...])
     x2 = (x_ref[...].astype(F32) + vec_ref[5:6] * branch).astype(BF16)
     final = normed(x2.astype(F32), vec_ref[7:8], vec_ref[6:7])
@@ -329,17 +327,15 @@
     patch_ref[:, : 4 * LATC] = jnp.where(idx_ref[:, :1] >= 0, patches, 0.0)
 
 
-def tile_block(x, q, kv, got, idx, vecs, w_final, wo_block):
-    count = kv.shape[0]
+def tile_block(x, q, sums, state, got, idx, vecs, w_final, wo_block):
     return pl.pallas_call(
         tile_kernel,
         out_shape=jax.ShapeDtypeStruct((x.shape[0], LANES), F32),
-        in_specs=[VMEM] * 8,
+        in_specs=[VMEM] * 9,
         out_specs=VMEM,
-        scratch_shapes=[pltpu.VMEM((2 * count, 2 * DA), BF16)],
-        compiler_params=params(count),
+        compiler_params=params(got.shape[0]),
         name="tile_attention_and_patches",
-    )(x, q, kv, got, idx, vecs, w_final, wo_block)
+    )(x, q, sums, state, got, idx, vecs, w_final, wo_block)
 
 
 def decode_kernel(
@@ -522,15 +518,15 @@
     stale_pieces = [own_stale, stale_column] + stale_line + [swapped(stale_column, 0, k) for k in range(1, inner)]
     x, query, fresh, *parts = project(x_pieces, vecs, w_0)
     got_pieces = [lax.ppermute(part, "pipe", swap) for part in parts]
-    sums, state = attend_fresh(query, fresh)
     x_tile, q_tile, fresh, send = first_block(
-        stale_pieces, got_pieces, x, query, sums, state, idx, vecs, w_1, wo_0
+        stale_pieces, got_pieces, x, query, fresh, idx, vecs, w_1, wo_0
     )
     send, w_in = lax.optimization_barrier((send, w_in))
     got = lax.ppermute(send, "pipe", swap)
     w_patch = dot(jnp.asarray(patch_selector(), BF16), w_in).astype(BF16)
-    got, w_patch = lax.optimization_barrier((got, w_patch))
-    patches = tile_block(x_tile, q_tile, fresh, got, idx, vecs, w_final.T, wo_1)
+    sums, state = attend_fresh(q_tile, fresh)
+    got, w_patch, sums, state = lax.optimization_barrier((got, w_patch, sums, state))
+    patches = tile_block(x_tile, q_tile, sums, state, got, idx, vecs, w_final.T, wo_1)
     edge = patches
     if rows > 1:
         edge = jnp.where(first_core, patches[(rows - 1) * pitch : rows * pitch], patches[:pitch])

time: 47.8 us -> 45.6 us (0.954)
  Pallas kernels: 19.3 us -> 17.4 us
    pallas_call x1, Pallas kernels: 6.61 us -> 4.96 us  [first_block(): pl.pallas_call(functools.partial(block_kernel, len(stale_pieces), len(got...]
    ppermute x1, waiting for transfers between devices: 1.57 us -> 0.34 us  [local(): got = lax.ppermute(send, 'pipe', swap)]
    ppermute x4, waiting for transfers between devices: 0.13 us -> 1.07 us  [local(): got_pieces = [lax.ppermute(part, 'pipe', swap) for part in parts]]
    pallas_call x1, Pallas kernels: 3.05 us -> 2.54 us  [tile_block(): pl.pallas_call(tile_kernel, out_shape=jax.ShapeDtypeStruct((x.shape[0], L...]
  transfers between devices with their start and end apart: 17 -> 17, of which waited for: 5 -> 8; matrix products, arithmetic and copies ran while one was open for 8% -> 9% of each run, Pallas kernels for 14% -> 15%
where the time goes in v15:
time: 45.6 us; the launch traced here: 45.4 us
  Pallas kernels  17.4 us (38%)
  starting transfers between devices  15.4 us (34%)
  waiting for transfers between devices  5.72 us (13%)
  local copies, waits for them, and re-layouts  2.86 us (6%)
  blocking collectives  1.82 us (4%)
  between operations  0.88 us (2%)
  other arithmetic  0.85 us (2%)
    ppermute x9, starting transfers between devices, swapped(): lax.ppermute(block, 'patch', [(i ^ k_outer * inner + k_inner, i) for i in...  13.3 us
    pallas_call x1, Pallas kernels, first_block(): pl.pallas_call(functools.partial(block_kernel, len(stale_pieces), len(got...  4.96 us
    pallas_call x1, Pallas kernels, weights_in_vmem(): pl.pallas_call(weights_kernel, out_shape=(jax.ShapeDtypeStruct((3 * DA, D...  3.7 us
    ppermute x9, waiting for transfers between devices, swapped(): lax.ppermute(block, 'patch', [(i ^ k_outer * inner + k_inner, i) for i in...  3.28 us
    pallas_call x1, Pallas kernels, decode(): pl.pallas_call(functools.partial(decode_kernel, rows, cols, pitch), out_s...  3.14 us
    pallas_call x1, Pallas kernels, tile_block(): pl.pallas_call(tile_kernel, out_shape=jax.ShapeDtypeStruct((x.shape[0], L...  2.54 us
    pallas_call x1, Pallas kernels, project(): pl.pallas_call(functools.partial(project_kernel, len(pieces)), out_shape=...  1.89 us
    all_gather x1, blocking collectives, local(): tables = lax.all_gather(block_table[0], 'pipe')  1.82 us
  transfers between devices with their start and end apart: 17, of which 8 were waited for; matrix products, arithmetic and copies ran while one was open for 9% of the time, Pallas kernels for 15%

profile of v15, /device:TPU:0, one launch (start us, length us, event | category | flops | bytes accessed | tf_op | source)
XLA Modules:
  0.0 45.4 jit_solution(11094051410987370641)
XLA Ops:
  0.0 0.5 collective-permute-start.3
  0.5 1.1 %dynamic-slice_bitcast_fusion = bf16[32,1152]{1,0:T(8,128)(2,1)S(1)} fusion(bf16[2,32,1152]{2,1,0:T(8,128)(2,1)} %param.14, s32[]{:T(128)S(6)} %select_n.80), kind=kLoop, calls=%fused_computation.5 | loop fusion | bytes 147460 | tf_op jit(solution)/shard_map/jit(dynamic_index_in_dim)/squeeze | solution.py:476
  1.6 2.5 %collective-permute-start = (bf16[32,1152]{1,0:T(8,128)(2,1)S(1)}, bf16[32,1152]{1,0:T(8,128)(2,1)S(1)}, u32[]{:S(2)}, u32[]{:S(2)}) collective-permute-start(bf16[32,1152]{1,0:T(8,128)(2,1)S(1)} %dynamic-slice_bitcast_fusion), channel_id=1, source_target_pairs={{2,0},{3,1},{0,2},{1,3},{6,4},{7,5},{4,6},{5,7},{10,8},{11,9},{8,1... | collective-permute-start | bytes 221192 | tf_op jit(solution)/shard_map/ppermute | solution.py:447
  4.1 2.6 %collective-permute-start.1 = (bf16[32,1152]{1,0:T(8,128)(2,1)S(1)}, bf16[32,1152]{1,0:T(8,128)(2,1)S(1)}, u32[]{:S(2)}, u32[]{:S(2)}) collective-permute-start(bf16[32,1152]{1,0:T(8,128)(2,1)S(1)} %dynamic-slice_bitcast_fusion), channel_id=1, source_target_pairs={{4,0},{5,1},{6,2},{7,3},{0,4},{1,5},{2,6},{3,7},{12,8},{13,9},{14,... | collective-permute-start | bytes 221192 | tf_op jit(solution)/shard_map/ppermute | solution.py:447
  6.7 0.9 %slice_bitcast_fusion.refs_0_ = bf16[32,1152]{1,0:T(8,128)(2,1)S(1)} fusion(bf16[1,2,32,1152]{3,2,1,0:T(8,128)(2,1)} %param.15), kind=kLoop, calls=%fused_computation.4 | loop fusion | bytes 147456 | tf_op jit(solution)/shard_map/squeeze | solution.py:481
  7.6 1.7 %collective-permute-start.4 = (bf16[32,1152]{1,0:T(8,128)(2,1)S(1)}, bf16[32,1152]{1,0:T(8,128)(2,1)S(1)}, u32[]{:S(2)}, u32[]{:S(2)}) collective-permute-start(bf16[32,1152]{1,0:T(8,128)(2,1)S(1)} %slice_bitcast_fusion.refs_0_), channel_id=1, source_target_pairs={{1,0},{0,1},{3,2},{2,3},{5,4},{4,5},{7,6},{6,7},{9,8},{8,9},{11,10... | collective-permute-start | bytes 221192 | tf_op jit(solution)/shard_map/ppermute | solution.py:447
  10.0 0.7 %copy.19 = f32[1,3,1152]{2,1,0:T(4,128)S(1)} copy(f32[1,3,1152]{2,0,1:T(1,128)} %param.18) | data formatting | bytes 27648 | tf_op args[4]
  10.7 1.8 %all_gather.3 = f32[2,3,1152]{2,1,0:T(4,128)S(1)} all-gather(f32[1,3,1152]{2,1,0:T(4,128)S(1)} %copy.19), channel_id=1, replica_groups=mesh['grp'=2,'pipe'=2,'patch'=8] {'pipe'}, dimensions={0}, use_global_device_ids=true | all-gather | bytes 41472 | tf_op jit(solution)/shard_map/all_gather | solution.py:479
  12.6 0.7 %fusion.2 = (f32[3,1152]{1,0:T(4,128)S(1)}, f32[3,1152]{1,0:T(4,128)S(1)}) fusion(f32[1,3,1152]{2,0,1:T(1,128)S(1)} %constant_dynamic-slice_fusion, f32[2,3,1152]{2,1,0:T(4,128)S(1)} %all_gather.3, f32[3]{0:T(128)} %constant.120), kind=kLoop, calls=%fused_computation.10 | loop fusion | flops 13824 | bytes 69132 | tf_op jit(solution)/shard_map/add | solution.py:488
  13.8 1.1 %collective-permute-start.5 = (bf16[128,1152]{1,0:T(8,128)(2,1)S(1)}, bf16[128,1152]{1,0:T(8,128)(2,1)S(1)}, u32[]{:S(2)}, u32[]{:S(2)}) collective-permute-start(bf16[128,1152]{1,0:T(8,128)(2,1)S(1)} %pad_maximum_fusion.refs_0_), channel_id=1, source_target_pairs={{1,0},{0,1},{3,2},{2,3},{5,4},{4,5},{7,6},{6,7},{9,8},{8,9},{11,10... | collective-permute-start | bytes 884744 | tf_op jit(solution)/shard_map/ppermute | solution.py:447
  14.9 1.6 %collective-permute-start.6 = (bf16[32,1152]{1,0:T(8,128)(2,1)S(1)}, bf16[32,1152]{1,0:T(8,128)(2,1)S(1)}, u32[]{:S(2)}, u32[]{:S(2)}) collective-permute-start(bf16[32,1152]{1,0:T(8,128)(2,1)S(1)} %slice_bitcast_fusion.refs_0_), channel_id=1, source_target_pairs={{2,0},{3,1},{0,2},{1,3},{6,4},{7,5},{4,6},{5,7},{10,8},{11,9},{8,1... | collective-permute-start | bytes 221192 | tf_op jit(solution)/shard_map/ppermute | solution.py:447
  16.4 2.0 %collective-permute-start.7 = (bf16[32,1152]{1,0:T(8,128)(2,1)S(1)}, bf16[32,1152]{1,0:T(8,128)(2,1)S(1)}, u32[]{:S(2)}, u32[]{:S(2)}) collective-permute-start(bf16[32,1152]{1,0:T(8,128)(2,1)S(1)} %slice_bitcast_fusion.refs_0_), channel_id=1, source_target_pairs={{4,0},{5,1},{6,2},{7,3},{0,4},{1,5},{2,6},{3,7},{12,8},{13,9},{14,... | collective-permute-start | bytes 221192 | tf_op jit(solution)/shard_map/ppermute | solution.py:447
  18.4 0.8 %collective-permute-start.8 = (bf16[32,1152]{1,0:T(8,128)(2,1)S(1)}, bf16[32,1152]{1,0:T(8,128)(2,1)S(1)}, u32[]{:S(2)}, u32[]{:S(2)}) collective-permute-start(bf16[32,1152]{1,0:T(8,128)(2,1)S(1)} %slice_bitcast_fusion.refs_0_), channel_id=1, source_target_pairs={{6,0},{7,1},{4,2},{5,3},{2,4},{3,5},{0,6},{1,7},{14,8},{15,9},{12,... | collective-permute-start | bytes 221192 | tf_op jit(solution)/shard_map/ppermute | solution.py:447
  19.3 3.7 %weights_by_block.1 = (bf16[1728,1152]{1,0:T(8,128)(2,1)S(1)}, bf16[1728,1152]{1,0:T(8,128)(2,1)S(1)}, bf16[640,1152]{1,0:T(8,128)(2,1)S(1)}, bf16[640,1152]{1,0:T(8,128)(2,1)S(1)}) custom-call(bf16[1,1728,1152]{2,1,0:T(8,128)(2,1)} %bitcast.34, bf16[1,1728,1152]{2,1,0:T(8,128)(2,1)} %collective-permute-done.3.other_ref, bf16[1,576,1152]{2,1,0:T(8,128)(2,1)} %wo_own, ...), custom_call_target="tpu_custom_call" | custom-call | tf_op jit(solution)/shard_map/weights_by_block/pallas_call | solution.py:163
  23.0 2.3 %collective-permute-done.7 = bf16[32,1152]{1,0:T(8,128)(2,1)S(1)} collective-permute-done((bf16[32,1152]{1,0:T(8,128)(2,1)S(1)}, bf16[32,1152]{1,0:T(8,128)(2,1)S(1)}, u32[]{:S(2)}, u32[]{:S(2)}) %collective-permute-start.7) | collective-permute-done | bytes 73760 | tf_op jit(solution)/shard_map/ppermute | solution.py:447
  25.3 1.0 %collective-permute-start.10 = (bf16[96,1152]{1,0:T(8,128)(2,1)S(1)}, bf16[96,1152]{1,0:T(8,128)(2,1)S(1)}, u32[]{:S(2)}, u32[]{:S(2)}) collective-permute-start(bf16[96,1152]{1,0:T(8,128)(2,1)S(1)} %pad_maximum_fusion.1.refs_1_), channel_id=1, source_target_pairs={{1,0},{0,1},{3,2},{2,3},{5,4},{4,5},{7,6},{6,7},{9,8},{8,9},{11,10... | collective-permute-start | bytes 663560 | tf_op jit(solution)/shard_map/ppermute | solution.py:447
  26.3 1.9 %layer_norm_and_projections.1 = (bf16[256,1152]{1,0:T(8,128)(2,1)S(1)}, bf16[256,640]{1,0:T(8,128)(2,1)S(1)}, bf16[256,1152]{1,0:T(8,128)(2,1)S(1)}, bf16[64,115...) custom-call(bf16[128,1152]{1,0:T(8,128)(2,1)S(1)} %pad_maximum_fusio, ...), custom_call_target="tpu_custom_call" | custom-call | tf_op jit(solution)/shard_map/layer_norm_and_projections/pallas_call | solution.py:211
  28.3 0.5 %collective-permute-start.12 = (bf16[64,1152]{1,0:T(8,128)(2,1)S(1)}, bf16[64,1152]{1,0:T(8,128)(2,1)S(1)}, u32[]{:S(2)}, u32[]{:S(2)}) collective-permute-start(bf16[64,1152]{1,0:T(8,128)(2,1)S(1)} %get-tuple-element.71), channel_id=1, source_target_pairs={{0,8},{8,0},{1,9},{9,1},{2,10},{10,2},{3,11},{11,3},{4,12},{12,4},... | collective-permute-start | bytes 442376 | tf_op jit(solution)/shard_map/ppermute | solution.py:520
  30.4 0.9 %collective-permute-done.10.refs_3_ = bf16[96,1152]{1,0:T(8,128)(2,1)S(1)} collective-permute-done((bf16[96,1152]{1,0:T(8,128)(2,1)S(1)}, bf16[96,1152]{1,0:T(8,128)(2,1)S(1)}, u32[]{:S(2)}, u32[]{:S(2)}) %collective-permute-start.10) | collective-permute-done | bytes 221216 | tf_op jit(solution)/shard_map/ppermute | solution.py:447
  31.3 5.0 %attention_and_next_keys.1 = (bf16[48,1152]{1,0:T(8,128)(2,1)S(1)}, bf16[48,640]{1,0:T(8,128)(2,1)S(1)}, bf16[256,1152]{1,0:T(8,128)(2,1)S(1)}, bf16[256,1152]{1,0:T(8,128)(2,1)S(1)}) custom-call(bf16[32,1152]{1,0:T(8,128)(2,1)S(1)} %slice_bitcast_fusion.refs_0_, bf16[96,1152]{1,0:T(8,128)(2,1)S(1)} %pad_maximum_fusion.1.refs_1_, ...), custom_call_target="tpu_custom_call" | custom-call | tf_op jit(solution)/shard_map/attention_and_next_keys/pallas_call | solution.py:301
  36.4 1.2 %attention_over_own_keys.1 = (f32[48,640]{1,0:T(8,128)S(1)}, f32[48,128]{1,0:T(8,128)S(1)}) custom-call(bf16[48,640]{1,0:T(8,128)(2,1)S(1)} %get-tuple-element.81.q_ref, bf16[256,1152]{1,0:T(8,128)(2,1)S(1)} %get-tuple-element.85.kv_ref), custom_call_target="tpu_custom_call" | custom-call | tf_op jit(solution)/shard_map/attention_over_own_keys/pallas_call | solution.py:242
  38.4 2.5 %tile_attention_and_patches.1.patch_ref = f32[48,128]{1,0:T(8,128)S(1)} custom-call(bf16[48,1152]{1,0:T(8,128)(2,1)S(1)} %get-tuple-element.80.x_ref, bf16[48,640]{1,0:T(8,128)(2,1)S(1)} %get-tuple-element.81.q_ref, f32[48,640]{1,0:T(8,128)S(1)} %get-tuple-element.88.sum_ref, f32[48,128]{1,0:T(8,128)S(1)} %get-tuple-element.89.state_ref, ...), custom_call_target="tpu_custom_call" | custom-call | tf_op jit(solution)/shard_map/tile_attention_and_patches/pallas_call | solution.py:331
  41.2 1.0 %collective-permute-done.16.got_ref = f32[48,128]{1,0:T(8,128)S(1)} collective-permute-done((f32[48,128]{1,0:T(8,128)S(1)}, f32[48,128]{1,0:T(8,128)S(1)}, u32[]{:S(2)}, u32[]{:S(2)}) %collective-permute-start.16) | collective-permute-done | bytes 24608 | tf_op jit(solution)/shard_map/ppermute | solution.py:533
  42.2 3.1 %decoder_convolutions.1 = bf16[4,128,512]{2,1,0:T(8,128)(2,1)} custom-call(f32[48,128]{1,0:T(8,128)S(1)} %tile_attention_and_patches.1.patch_ref, f32[48,128]{1,0:T(8,128)S(1)} %collective-permute-done.16.got_ref, s32[48,128]{1,0:T(8,128)S(1)} %broadcast_in_dim.14.refs_11_.idx_ref, bf16[1024,512]{1,0:T(8,128)(2,1)S(1)} %fusion.wp_ref, ...), custom_call_target="tpu_custom_call" | custom-call | tf_op jit(solution)/shard_map/decoder_convolutions/pallas_call | solution.py:412
  (47 shorter events, 3.2 us)
Async XLA Ops:
  0.0 12.5 %copy-start = (f32[100,5,1152]{2,0,1:T(8,128)S(1)}, f32[100,5,1152]{2,0,1:T(8,128)}, u32[]{:S(2)}) copy-start(f32[100,5,1152]{2,0,1:T(8,128)} %param.19) | copy-start | bytes 6912004
  0.0 13.4 %collective-permute-start.3 = (bf16[1,1728,1152]{2,1,0:T(8,128)(2,1)}, bf16[1,1728,1152]{2,1,0:T(8,128)(2,1)}, u32[]{:S(2)}, u32[]{:S(2)}) collective-permute-start(bf16[1,1728,1152]{2,1,0:T(8,128)(2,1)} %bitcast.33), channel_id=1, source_target_pairs={{0,8},{8,0},{1,9},{9,1},{2,10},{10,2},{3,11},{11,3},{4,12},{12,4},... | collective-permute-start | bytes 11943944 | tf_op jit(solution)/shard_map/ppermute | solution.py:478
  1.6 11.8 %collective-permute-start = (bf16[32,1152]{1,0:T(8,128)(2,1)S(1)}, bf16[32,1152]{1,0:T(8,128)(2,1)S(1)}, u32[]{:S(2)}, u32[]{:S(2)}) collective-permute-start(bf16[32,1152]{1,0:T(8,128)(2,1)S(1)} %dynamic-slice_bitcast_fusion), channel_id=1, source_target_pairs={{2,0},{3,1},{0,2},{1,3},{6,4},{7,5},{4,6},{5,7},{10,8},{11,9},{8,1... | collective-permute-start | bytes 221192 | tf_op jit(solution)/shard_map/ppermute | solution.py:447
  4.1 9.3 %collective-permute-start.1 = (bf16[32,1152]{1,0:T(8,128)(2,1)S(1)}, bf16[32,1152]{1,0:T(8,128)(2,1)S(1)}, u32[]{:S(2)}, u32[]{:S(2)}) collective-permute-start(bf16[32,1152]{1,0:T(8,128)(2,1)S(1)} %dynamic-slice_bitcast_fusion), channel_id=1, source_target_pairs={{4,0},{5,1},{6,2},{7,3},{0,4},{1,5},{2,6},{3,7},{12,8},{13,9},{14,... | collective-permute-start | bytes 221192 | tf_op jit(solution)/shard_map/ppermute | solution.py:447
  6.7 6.7 %collective-permute-start.2 = (bf16[32,1152]{1,0:T(8,128)(2,1)S(1)}, bf16[32,1152]{1,0:T(8,128)(2,1)S(1)}, u32[]{:S(2)}, u32[]{:S(2)}) collective-permute-start(bf16[32,1152]{1,0:T(8,128)(2,1)S(1)} %dynamic-slice_bitcast_fusion), channel_id=1, source_target_pairs={{6,0},{7,1},{4,2},{5,3},{2,4},{3,5},{0,6},{1,7},{14,8},{15,9},{12,... | collective-permute-start | bytes 221192 | tf_op jit(solution)/shard_map/ppermute | solution.py:447
  7.6 5.8 %collective-permute-start.4 = (bf16[32,1152]{1,0:T(8,128)(2,1)S(1)}, bf16[32,1152]{1,0:T(8,128)(2,1)S(1)}, u32[]{:S(2)}, u32[]{:S(2)}) collective-permute-start(bf16[32,1152]{1,0:T(8,128)(2,1)S(1)} %slice_bitcast_fusion.refs_0_), channel_id=1, source_target_pairs={{1,0},{0,1},{3,2},{2,3},{5,4},{4,5},{7,6},{6,7},{9,8},{8,9},{11,10... | collective-permute-start | bytes 221192 | tf_op jit(solution)/shard_map/ppermute | solution.py:447
  13.5 5.7 %collective-permute-start.9 = (bf16[1,576,1152]{2,1,0:T(8,128)(2,1)}, bf16[1,576,1152]{2,1,0:T(8,128)(2,1)S(1)}, u32[]{:S(2)}, u32[]{:S(2)}) collective-permute-start(bf16[1,576,1152]{2,1,0:T(8,128)(2,1)} %wo_own), channel_id=1, source_target_pairs={{0,8},{8,0},{1,9},{9,1},{2,10},{10,2},{3,11},{11,3},{4,12},{12,4},... | collective-permute-start | bytes 3981320 | tf_op jit(solution)/shard_map/ppermute | solution.py:513
  13.8 11.5 %collective-permute-start.5 = (bf16[128,1152]{1,0:T(8,128)(2,1)S(1)}, bf16[128,1152]{1,0:T(8,128)(2,1)S(1)}, u32[]{:S(2)}, u32[]{:S(2)}) collective-permute-start(bf16[128,1152]{1,0:T(8,128)(2,1)S(1)} %pad_maximum_fusion.refs_0_), channel_id=1, source_target_pairs={{1,0},{0,1},{3,2},{2,3},{5,4},{4,5},{7,6},{6,7},{9,8},{8,9},{11,10... | collective-permute-start | bytes 884744 | tf_op jit(solution)/shard_map/ppermute | solution.py:447
  14.9 8.1 %collective-permute-start.6 = (bf16[32,1152]{1,0:T(8,128)(2,1)S(1)}, bf16[32,1152]{1,0:T(8,128)(2,1)S(1)}, u32[]{:S(2)}, u32[]{:S(2)}) collective-permute-start(bf16[32,1152]{1,0:T(8,128)(2,1)S(1)} %slice_bitcast_fusion.refs_0_), channel_id=1, source_target_pairs={{2,0},{3,1},{0,2},{1,3},{6,4},{7,5},{4,6},{5,7},{10,8},{11,9},{8,1... | collective-permute-start | bytes 221192 | tf_op jit(solution)/shard_map/ppermute | solution.py:447
  16.4 8.9 %collective-permute-start.7 = (bf16[32,1152]{1,0:T(8,128)(2,1)S(1)}, bf16[32,1152]{1,0:T(8,128)(2,1)S(1)}, u32[]{:S(2)}, u32[]{:S(2)}) collective-permute-start(bf16[32,1152]{1,0:T(8,128)(2,1)S(1)} %slice_bitcast_fusion.refs_0_), channel_id=1, source_target_pairs={{4,0},{5,1},{6,2},{7,3},{0,4},{1,5},{2,6},{3,7},{12,8},{13,9},{14,... | collective-permute-start | bytes 221192 | tf_op jit(solution)/shard_map/ppermute | solution.py:447
  18.4 6.9 %collective-permute-start.8 = (bf16[32,1152]{1,0:T(8,128)(2,1)S(1)}, bf16[32,1152]{1,0:T(8,128)(2,1)S(1)}, u32[]{:S(2)}, u32[]{:S(2)}) collective-permute-start(bf16[32,1152]{1,0:T(8,128)(2,1)S(1)} %slice_bitcast_fusion.refs_0_), channel_id=1, source_target_pairs={{6,0},{7,1},{4,2},{5,3},{2,4},{3,5},{0,6},{1,7},{14,8},{15,9},{12,... | collective-permute-start | bytes 221192 | tf_op jit(solution)/shard_map/ppermute | solution.py:447
  25.3 6.0 %collective-permute-start.10 = (bf16[96,1152]{1,0:T(8,128)(2,1)S(1)}, bf16[96,1152]{1,0:T(8,128)(2,1)S(1)}, u32[]{:S(2)}, u32[]{:S(2)}) collective-permute-start(bf16[96,1152]{1,0:T(8,128)(2,1)S(1)} %pad_maximum_fusion.1.refs_1_), channel_id=1, source_target_pairs={{1,0},{0,1},{3,2},{2,3},{5,4},{4,5},{7,6},{6,7},{9,8},{8,9},{11,10... | collective-permute-start | bytes 663560 | tf_op jit(solution)/shard_map/ppermute | solution.py:447
  28.2 1.4 %collective-permute-start.11 = (bf16[64,1152]{1,0:T(8,128)(2,1)S(1)}, bf16[64,1152]{1,0:T(8,128)(2,1)S(1)}, u32[]{:S(2)}, u32[]{:S(2)}) collective-permute-start(bf16[64,1152]{1,0:T(8,128)(2,1)S(1)} %get-tuple-element.70), channel_id=1, source_target_pairs={{0,8},{8,0},{1,9},{9,1},{2,10},{10,2},{3,11},{11,3},{4,12},{12,4},... | collective-permute-start | bytes 442376 | tf_op jit(solution)/shard_map/ppermute | solution.py:520
  28.3 1.6 %collective-permute-start.12 = (bf16[64,1152]{1,0:T(8,128)(2,1)S(1)}, bf16[64,1152]{1,0:T(8,128)(2,1)S(1)}, u32[]{:S(2)}, u32[]{:S(2)}) collective-permute-start(bf16[64,1152]{1,0:T(8,128)(2,1)S(1)} %get-tuple-element.71), channel_id=1, source_target_pairs={{0,8},{8,0},{1,9},{9,1},{2,10},{10,2},{3,11},{11,3},{4,12},{12,4},... | collective-permute-start | bytes 442376 | tf_op jit(solution)/shard_map/ppermute | solution.py:520
  28.8 1.4 %collective-permute-start.13 = (bf16[64,1152]{1,0:T(8,128)(2,1)S(1)}, bf16[64,1152]{1,0:T(8,128)(2,1)S(1)}, u32[]{:S(2)}, u32[]{:S(2)}) collective-permute-start(bf16[64,1152]{1,0:T(8,128)(2,1)S(1)} %get-tuple-element.72), channel_id=1, source_target_pairs={{0,8},{8,0},{1,9},{9,1},{2,10},{10,2},{3,11},{11,3},{4,12},{12,4},... | collective-permute-start | bytes 442376 | tf_op jit(solution)/shard_map/ppermute | solution.py:520
  28.9 1.5 %collective-permute-start.14 = (bf16[64,1152]{1,0:T(8,128)(2,1)S(1)}, bf16[64,1152]{1,0:T(8,128)(2,1)S(1)}, u32[]{:S(2)}, u32[]{:S(2)}) collective-permute-start(bf16[64,1152]{1,0:T(8,128)(2,1)S(1)} %get-tuple-element.73), channel_id=1, source_target_pairs={{0,8},{8,0},{1,9},{9,1},{2,10},{10,2},{3,11},{11,3},{4,12},{12,4},... | collective-permute-start | bytes 442376 | tf_op jit(solution)/shard_map/ppermute | solution.py:520
  31.3 10.9 %slice-start = ((s8[4718592]{0:T(1024)(128)(4,1)}), s8[4194304]{0:T(1024)(128)(4,1)S(1)}, s32[]{:S(2)}) async-start(s8[4718592]{0:T(1024)(128)(4,1)} %bitcast.28), calls=%async_computation | async-start | bytes 8388608
  31.3 6.3 %copy-start.4 = (bf16[1024,36]{1,0:T(8,128)(2,1)S(1)}, bf16[1024,36]{1,0:T(8,128)(2,1)}, u32[]{:S(2)}) copy-start(bf16[1024,36]{1,0:T(8,128)(2,1)} %constant.114.clone) | copy-start | bytes 221188
  31.3 6.3 %copy-start.5 = (bf16[36,512]{1,0:T(8,128)(2,1)S(1)}, bf16[36,512]{1,0:T(8,128)(2,1)}, u32[]{:S(2)}) copy-start(bf16[36,512]{1,0:T(8,128)(2,1)} %param.22) | copy-start | bytes 110596
  31.3 7.1 %copy-start.1 = (bf16[1152,16]{0,1:T(8,128)(2,1)S(1)}, bf16[1152,16]{0,1:T(8,128)(2,1)}, u32[]{:S(2)}) copy-start(bf16[1152,16]{0,1:T(8,128)(2,1)} %param.21) | copy-start | bytes 110596
  31.3 10.9 %slice-start.1 = ((s8[4718592]{0:T(1024)(128)(4,1)}), s8[524288]{0:T(1024)(128)(4,1)S(1)}, s32[]{:S(2)}) async-start(s8[4718592]{0:T(1024)(128)(4,1)} %bitcast.28), calls=%async_computation.1 | async-start | bytes 1048576
  36.3 5.9 %copy-start.2 = (f32[512]{0:T(512)S(1)}, f32[512]{0:T(512)}, u32[]{:S(2)}) copy-start(f32[512]{0:T(512)} %param.23) | copy-start | bytes 6148
  36.3 2.1 %collective-permute-start.15 = (bf16[256,1152]{1,0:T(8,128)(2,1)S(1)}, bf16[256,1152]{1,0:T(8,128)(2,1)S(1)}, u32[]{:S(2)}, u32[]{:S(2)}) collective-permute-start(bf16[256,1152]{1,0:T(8,128)(2,1)S(1)} %get-tuple-element.83), channel_id=1, source_target_pairs={{0,8},{8,0},{1,9},{9,1},{2,10},{10,2},{3,11},{11,3},{4,12},{12,4},... | collective-permute-start | bytes 1769480 | tf_op jit(solution)/shard_map/ppermute | solution.py:525
  41.0 1.3 %collective-permute-start.16 = (f32[48,128]{1,0:T(8,128)S(1)}, f32[48,128]{1,0:T(8,128)S(1)}, u32[]{:S(2)}, u32[]{:S(2)}) collective-permute-start(f32[48,128]{1,0:T(8,128)S(1)} %tile_attention_and_patches.1.patch_ref), channel_id=1, source_target_pairs={{0,8},{8,0},{1,9},{9,1},{2,10},{10,2},{3,11},{11,3},{4,12},{12,4},... | collective-permute-start | bytes 73736 | tf_op jit(solution)/shard_map/ppermute | solution.py:533
  (1 other events, 5.9 us)

commit v16 on v15

--- a/solution.py
+++ b/solution.py
@@ -227,34 +227,47 @@
     return pltpu.with_memory_space_constraint(array, pltpu.HBM)
 
 
-def fresh_kernel(q_ref, kv_ref, sum_ref, state_ref):
+def fresh_kernel(x_ref, mod_ref, kv_ref, idx_ref, w_ref, xt_ref, qt_ref, sum_ref, state_ref, pick_ref):
+    tile_rows = idx_ref.shape[0]
+    pick_ref[...] = jnp.zeros_like(pick_ref)
+
     def body(start, size):
         rows = pl.ds(start, size)
-        sums, state = attend_begin(q_ref[rows], kv_ref)
-        sum_ref[rows] = sums
-        state_ref[rows] = state
-
-    each_block(q_ref.shape[0], body)
-
-
-def attend_fresh(q, kv):
-    count = q.shape[0]
+        lane = lax.broadcasted_iota(jnp.int32, (tile_rows, size), 1) + start
+        chosen = (lane == idx_ref[:, :1]).astype(F32).astype(BF16)
+        pick_ref[0] += dot(chosen, mod_ref[rows])
+        pick_ref[1] += dot(chosen, x_ref[rows])
+
+    each_block(x_ref.shape[0], body)
+    query = query_of(pick_ref[0].astype(BF16), w_ref)
+    sum_ref[...], state_ref[...] = attend_begin(query, kv_ref)
+    qt_ref[...] = query
+    xt_ref[...] = pick_ref[1].astype(BF16)
+
+
+def attend_fresh(x, modulated, kv, idx, w_block):
+    rows = idx.shape[0]
     return pl.pallas_call(
         fresh_kernel,
-        out_shape=(jax.ShapeDtypeStruct((count, DP), F32), jax.ShapeDtypeStruct((count, LANES), F32)),
-        in_specs=[VMEM] * 2,
-        out_specs=(VMEM,) * 2,
+        out_shape=(
+            jax.ShapeDtypeStruct((rows, D), BF16),
+            jax.ShapeDtypeStruct((rows, DP), BF16),
+            jax.ShapeDtypeStruct((rows, DP), F32),
+            jax.ShapeDtypeStruct((rows, LANES), F32),
+        ),
+        in_specs=[VMEM] * 5,
+        out_specs=(VMEM,) * 4,
+        scratch_shapes=[pltpu.VMEM((2, rows, D), F32)],
         compiler_params=params(kv.shape[0]),
-        name="attention_over_own_keys",
-    )(q, kv)
+        name="tile_attention_over_own_keys",
+    )(x, modulated, kv, idx, w_block)
 
 
 def block_kernel(n_pieces, n_got, *refs):
     stale_refs = refs[:n_pieces]
     got_refs = refs[n_pieces : n_pieces + n_got]
     (
-        x_ref, q_ref, kv_ref, idx_ref, vec_ref, w1_ref, wo_ref,
-        xt_ref, qt_ref, kv1_ref, send_ref, all_ref, pick_ref,
+        x_ref, q_ref, kv_ref, vec_ref, w1_ref, wo_ref, x1_ref, mod_ref, kv1_ref, send_ref, all_ref,
     ) = refs[n_pieces + n_got :]
     count = x_ref.shape[0]
     first_core = lax.axis_index("pipe") == 0
@@ -269,8 +282,6 @@
     def _():
         join(got_refs, all_ref.at[count:])
 
-    pick_ref[...] = jnp.zeros_like(pick_ref)
-    tile_rows = idx_ref.shape[0]
 
     def body(start, size):
         rows = pl.ds(start, size)
@@ -285,36 +296,28 @@
         def _():
             send_ref[rows] = fresh
 
-        lane = lax.broadcasted_iota(jnp.int32, (tile_rows, size), 1) + start
-        chosen = (lane == idx_ref[:, :1]).astype(F32).astype(BF16)
-        pick_ref[0] += dot(chosen, x1)
-        pick_ref[1] += dot(chosen, modulated)
+        x1_ref[rows] = x1
+        mod_ref[rows] = modulated
 
     each_block(count, body)
-    xt_ref[...] = pick_ref[0].astype(BF16)
-    qt_ref[...] = query_of(pick_ref[1].astype(BF16), w1_ref)
-
-
-def first_block(stale_pieces, got_pieces, x, q, kv, idx, vecs, w_next, wo_block):
+
+
+def first_block(stale_pieces, got_pieces, x, q, kv, vecs, w_next, wo_block):
     count = x.shape[0]
-    tile_rows = idx.shape[0]
     return pl.pallas_call(
         functools.partial(block_kernel, len(stale_pieces), len(got_pieces)),
         out_shape=(
-            jax.ShapeDtypeStruct((tile_rows, D), BF16),
-            jax.ShapeDtypeStruct((tile_rows, DP), BF16),
+            jax.ShapeDtypeStruct((count, D), BF16),
+            jax.ShapeDtypeStruct((count, D), BF16),
             jax.ShapeDtypeStruct((count, 2 * DA), BF16),
             jax.ShapeDtypeStruct((count, 2 * DA), BF16),
         ),
-        in_specs=[VMEM] * (len(stale_pieces) + len(got_pieces) + 7),
+        in_specs=[VMEM] * (len(stale_pieces) + len(got_pieces) + 6),
         out_specs=(VMEM,) * 4,
-        scratch_shapes=[
-            pltpu.VMEM((2 * count, 2 * DA), BF16),
-            pltpu.VMEM((2, tile_rows, D), F32),
-        ],
+        scratch_shapes=[pltpu.VMEM((2 * count, 2 * DA), BF16)],
         compiler_params=params(count),
         name="attention_and_next_keys",
-    )(*stale_pieces, *got_pieces, x, q, kv, idx, vecs, w_next, wo_block)
+    )(*stale_pieces, *got_pieces, x, q, kv, vecs, w_next, wo_block)
 
 
 def tile_kernel(x_ref, q_ref, sum_ref, state_ref, got_ref, idx_ref, vec_ref, wf_ref, wo_ref, patch_ref):
@@ -348,6 +351,7 @@
     rim = [above] + [patch_ref[r * pitch : (r + 1) * pitch] for r in range(rows)] + [below]
     column_in = idx_ref[:pitch, :1] >= 0
     shifted = [[pltpu.roll(p, (-ds) % pitch, 0) if ds else p for ds in (-1, 0, 1)] for p in rim]
+    around = []
     for r in range(rows + 2):
         low, high = None, None
         for dr in (-1, 0, 1):
@@ -362,23 +366,24 @@
                     piece = pltpu.roll(piece, 4 * LATC * tap, 1) if tap else piece
                     low = piece if low is None else low + piece
         high = jnp.zeros_like(low) if high is None else high
-        around = jnp.concatenate([low, high], axis=1).astype(BF16)
-        for p in range(2):
-            y = 2 * (r - 1) + p + 1
-            if not 0 <= y < 2 * rows + 2:
-                continue
-            for q in range(2):
-                at = (2 * p + q) * 2 * LANES
-                act = dot(around, wp_ref[at : at + 2 * LANES]) + bin_ref[...]
-                feature = act / (1.0 + jnp.exp(-act))
+        around.append(jnp.concatenate([low, high], axis=1))
+    for p in range(2):
+        first = 1 - p
+        stacked = jnp.concatenate(around[first : first + rows + 1], axis=0).astype(BF16)
+        for q in range(2):
+            at = (2 * p + q) * 2 * LANES
+            act = dot(stacked, wp_ref[at : at + 2 * LANES]) + bin_ref[...]
+            feature = act / (1.0 + jnp.exp(-act))
+            for i in range(rows + 1):
+                y = 2 * (first + i - 1) + p + 1
                 keep = column_in
                 if y == 0:
                     keep = keep & jnp.logical_not(first_core)
                 if y == 2 * rows + 1:
                     keep = keep & first_core
-                feature = jnp.where(keep, feature, 0.0)
+                kept = jnp.where(keep, feature[i * pitch : (i + 1) * pitch], 0.0)
                 for c in range(CH // LANES):
-                    part = feature[:, c * LANES : (c + 1) * LANES]
+                    part = kept[:, c * LANES : (c + 1) * LANES]
                     u_ref[y, c, pl.ds(2 * q, pitch, stride=4), :] = part
                     u_ref[y, c, pl.ds(2 * q + 1, pitch, stride=4), :] = part
     wide = 4 * cols
@@ -479,7 +484,7 @@
     tables = lax.all_gather(block_table[0], "pipe")
     x_column = [swapped(own_tokens, k, 0) for k in range(1, outer)]
     own_stale = stale_kv[0, 1]
-    stale_line = [swapped(own_stale, 0, k) for k in range(1, inner)]
+    w_out_other = lax.ppermute(w_out, "pipe", swap)
 
     time_row = lax.dynamic_index_in_dim(time_table, t_index[0], 0, keepdims=False)
     ones = jnp.asarray([[0.0], [1.0], [0.0]], F32)
@@ -503,29 +508,27 @@
     spot = (k_inner * outer + k_outer) * own_count + token % own_count
     idx = jnp.broadcast_to(jnp.where(inside, spot, -1)[:, None], (padded_rows, LANES)).astype(jnp.int32)
 
-    x_column, w_qkv_other, vecs, idx, own_stale, stale_line, w_out = lax.optimization_barrier(
-        (x_column, w_qkv_other, vecs, idx, own_stale, stale_line, w_out)
+    x_column, w_qkv_other, w_out_other, vecs, idx, own_stale, w_in = lax.optimization_barrier(
+        (x_column, w_qkv_other, w_out_other, vecs, idx, own_stale, w_in)
     )
     x_column = jnp.concatenate([own_tokens] + x_column, axis=0)
-    x_column, own_stale, w_out = lax.optimization_barrier((x_column, own_stale, w_out))
+    x_column, own_stale = lax.optimization_barrier((x_column, own_stale))
     x_pieces = [x_column] + [swapped(x_column, 0, k) for k in range(1, inner)]
     stale_column = [swapped(own_stale, k, 0) for k in range(1, outer)]
-    w_out_other = lax.ppermute(w_out, "pipe", swap)
+    stale_line = [swapped(own_stale, 0, k) for k in range(1, inner)]
+    w_patch = dot(jnp.asarray(patch_selector(), BF16), w_in).astype(BF16)
     w_0, w_1, wo_0, wo_1 = weights_in_vmem(w_qkv, w_qkv_other, w_out, w_out_other)
-    x_pieces, stale_column, w_0 = lax.optimization_barrier((x_pieces, stale_column, w_0))
+    x_pieces, stale_column, stale_line, w_patch, w_0 = lax.optimization_barrier(
+        (x_pieces, stale_column, stale_line, w_patch, w_0)
+    )
     stale_column = jnp.concatenate(stale_column, axis=0)
     x_pieces, stale_column = lax.optimization_barrier((x_pieces, stale_column))
     stale_pieces = [own_stale, stale_column] + stale_line + [swapped(stale_column, 0, k) for k in range(1, inner)]
     x, query, fresh, *parts = project(x_pieces, vecs, w_0)
     got_pieces = [lax.ppermute(part, "pipe", swap) for part in parts]
-    x_tile, q_tile, fresh, send = first_block(
-        stale_pieces, got_pieces, x, query, fresh, idx, vecs, w_1, wo_0
-    )
-    send, w_in = lax.optimization_barrier((send, w_in))
+    x, modulated, fresh, send = first_block(stale_pieces, got_pieces, x, query, fresh, vecs, w_1, wo_0)
     got = lax.ppermute(send, "pipe", swap)
-    w_patch = dot(jnp.asarray(patch_selector(), BF16), w_in).astype(BF16)
-    sums, state = attend_fresh(q_tile, fresh)
-    got, w_patch, sums, state = lax.optimization_barrier((got, w_patch, sums, state))
+    x_tile, q_tile, sums, state = attend_fresh(x, modulated, fresh, idx, w_1)
     patches = tile_block(x_tile, q_tile, sums, state, got, idx, vecs, w_final.T, wo_1)
     edge = patches
     if rows > 1:

time: 45.6 us -> 45.1 us (0.989)
  waiting for transfers between devices: 5.72 us -> 3.53 us
  matrix products: 0.4 us -> 1.37 us
  Pallas kernels: 17.4 us -> 18 us
    ppermute x9, waiting for transfers between devices: 3.28 us -> 1.6 us  [swapped(): lax.ppermute(block, 'patch', [(i ^ k_outer * inner + k_inner, i) for i in...]
    dot_general x1, matrix products: 0.4 us -> 1.37 us  [dot(): return jnp.dot(a, b, preferred_element_type=F32)]
    pallas_call x1, Pallas kernels: 1.21 us -> 2.08 us  [attend_fresh(): pl.pallas_call(fresh_kernel, out_shape=(jax.ShapeDtypeStruct((rows, D), B...]
    pallas_call x1, Pallas kernels: 4.96 us -> 4.3 us  [first_block(): pl.pallas_call(functools.partial(block_kernel, len(stale_pieces), len(got...]
  transfers between devices with their start and end apart: 17 -> 17, of which waited for: 8 -> 7; matrix products, arithmetic and copies ran while one was open for 9% -> 11% of each run, Pallas kernels for 15% -> 18%
where the time goes in v16:
time: 45.1 us; the launch traced here: 44.9 us
  Pallas kernels  18 us (40%)
  starting transfers between devices  15.3 us (34%)
  waiting for transfers between devices  3.53 us (8%)
  local copies, waits for them, and re-layouts  2.87 us (6%)
  blocking collectives  1.99 us (4%)
  matrix products  1.37 us (3%)
  between operations  0.91 us (2%)
  other arithmetic  0.84 us (2%)
    ppermute x9, starting transfers between devices, swapped(): lax.ppermute(block, 'patch', [(i ^ k_outer * inner + k_inner, i) for i in...  13.2 us
    pallas_call x1, Pallas kernels, first_block(): pl.pallas_call(functools.partial(block_kernel, len(stale_pieces), len(got...  4.3 us
    pallas_call x1, Pallas kernels, weights_in_vmem(): pl.pallas_call(weights_kernel, out_shape=(jax.ShapeDtypeStruct((3 * DA, D...  4.08 us
    pallas_call x1, Pallas kernels, decode(): pl.pallas_call(functools.partial(decode_kernel, rows, cols, pitch), out_s...  3.14 us
    pallas_call x1, Pallas kernels, tile_block(): pl.pallas_call(tile_kernel, out_shape=jax.ShapeDtypeStruct((x.shape[0], L...  2.54 us
    pallas_call x1, Pallas kernels, attend_fresh(): pl.pallas_call(fresh_kernel, out_shape=(jax.ShapeDtypeStruct((rows, D), B...  2.08 us
    all_gather x1, blocking collectives, local(): tables = lax.all_gather(block_table[0], 'pipe')  1.99 us
    pallas_call x1, Pallas kernels, project(): pl.pallas_call(functools.partial(project_kernel, len(pieces)), out_shape=...  1.89 us
  transfers between devices with their start and end apart: 17, of which 7 were waited for; matrix products, arithmetic and copies ran while one was open for 11% of the time, Pallas kernels for 18%

profile of v16, /device:TPU:0, one launch (start us, length us, event | category | flops | bytes accessed | tf_op | source)
XLA Modules:
  0.0 44.9 jit_solution(12207555033319212441)
XLA Ops:
  0.5 1.1 %dynamic-slice_bitcast_fusion = bf16[32,1152]{1,0:T(8,128)(2,1)S(1)} fusion(bf16[2,32,1152]{2,1,0:T(8,128)(2,1)} %param.14, s32[]{:T(128)S(6)} %select_n.80), kind=kLoop, calls=%fused_computation.5 | loop fusion | bytes 147460 | tf_op jit(solution)/shard_map/jit(dynamic_index_in_dim)/squeeze | solution.py:481
  1.6 2.5 %collective-permute-start = (bf16[32,1152]{1,0:T(8,128)(2,1)S(1)}, bf16[32,1152]{1,0:T(8,128)(2,1)S(1)}, u32[]{:S(2)}, u32[]{:S(2)}) collective-permute-start(bf16[32,1152]{1,0:T(8,128)(2,1)S(1)} %dynamic-slice_bitcast_fusion), channel_id=1, source_target_pairs={{2,0},{3,1},{0,2},{1,3},{6,4},{7,5},{4,6},{5,7},{10,8},{11,9},{8,1... | collective-permute-start | bytes 221192 | tf_op jit(solution)/shard_map/ppermute | solution.py:452
  4.1 2.6 %collective-permute-start.1 = (bf16[32,1152]{1,0:T(8,128)(2,1)S(1)}, bf16[32,1152]{1,0:T(8,128)(2,1)S(1)}, u32[]{:S(2)}, u32[]{:S(2)}) collective-permute-start(bf16[32,1152]{1,0:T(8,128)(2,1)S(1)} %dynamic-slice_bitcast_fusion), channel_id=1, source_target_pairs={{4,0},{5,1},{6,2},{7,3},{0,4},{1,5},{2,6},{3,7},{12,8},{13,9},{14,... | collective-permute-start | bytes 221192 | tf_op jit(solution)/shard_map/ppermute | solution.py:452
  7.5 0.7 %copy.19 = f32[1,3,1152]{2,1,0:T(4,128)S(1)} copy(f32[1,3,1152]{2,0,1:T(1,128)} %param.18) | data formatting | bytes 27648 | tf_op args[4]
  8.2 2.0 %all_gather.3 = f32[2,3,1152]{2,1,0:T(4,128)S(1)} all-gather(f32[1,3,1152]{2,1,0:T(4,128)S(1)} %copy.19), channel_id=1, replica_groups=mesh['grp'=2,'pipe'=2,'patch'=8] {'pipe'}, dimensions={0}, use_global_device_ids=true | all-gather | bytes 41472 | tf_op jit(solution)/shard_map/all_gather | solution.py:484
  10.2 0.7 %fusion.2 = (f32[3,1152]{1,0:T(4,128)S(1)}, f32[3,1152]{1,0:T(4,128)S(1)}) fusion(f32[1,3,1152]{2,0,1:T(1,128)S(1)} %constant_dynamic-slice_fusion, f32[2,3,1152]{2,1,0:T(4,128)S(1)} %all_gather.3, f32[3]{0:T(128)} %constant.120), kind=kLoop, calls=%fused_computation.10 | loop fusion | flops 13824 | bytes 69132 | tf_op jit(solution)/shard_map/add | solution.py:493
  10.9 0.9 %slice_bitcast_fusion.refs_0_ = bf16[32,1152]{1,0:T(8,128)(2,1)S(1)} fusion(bf16[1,2,32,1152]{3,2,1,0:T(8,128)(2,1)} %param.15), kind=kLoop, calls=%fused_computation.4 | loop fusion | bytes 147456 | tf_op jit(solution)/shard_map/squeeze | solution.py:486
  11.9 1.2 %collective-permute-done.1 = bf16[32,1152]{1,0:T(8,128)(2,1)S(1)} collective-permute-done((bf16[32,1152]{1,0:T(8,128)(2,1)S(1)}, bf16[32,1152]{1,0:T(8,128)(2,1)S(1)}, u32[]{:S(2)}, u32[]{:S(2)}) %collective-permute-start.1) | collective-permute-done | bytes 73760 | tf_op jit(solution)/shard_map/ppermute | solution.py:452
  13.2 1.6 %collective-permute-start.5 = (bf16[128,1152]{1,0:T(8,128)(2,1)S(1)}, bf16[128,1152]{1,0:T(8,128)(2,1)S(1)}, u32[]{:S(2)}, u32[]{:S(2)}) collective-permute-start(bf16[128,1152]{1,0:T(8,128)(2,1)S(1)} %pad_maximum_fusion.refs_0_), channel_id=1, source_target_pairs={{1,0},{0,1},{3,2},{2,3},{5,4},{4,5},{7,6},{6,7},{9,8},{8,9},{11,10... | collective-permute-start | bytes 884744 | tf_op jit(solution)/shard_map/ppermute | solution.py:452
  14.8 1.6 %collective-permute-start.6 = (bf16[32,1152]{1,0:T(8,128)(2,1)S(1)}, bf16[32,1152]{1,0:T(8,128)(2,1)S(1)}, u32[]{:S(2)}, u32[]{:S(2)}) collective-permute-start(bf16[32,1152]{1,0:T(8,128)(2,1)S(1)} %slice_bitcast_fusion.refs_0_), channel_id=1, source_target_pairs={{2,0},{3,1},{0,2},{1,3},{6,4},{7,5},{4,6},{5,7},{10,8},{11,9},{8,1... | collective-permute-start | bytes 221192 | tf_op jit(solution)/shard_map/ppermute | solution.py:452
  16.3 1.6 %collective-permute-start.7 = (bf16[32,1152]{1,0:T(8,128)(2,1)S(1)}, bf16[32,1152]{1,0:T(8,128)(2,1)S(1)}, u32[]{:S(2)}, u32[]{:S(2)}) collective-permute-start(bf16[32,1152]{1,0:T(8,128)(2,1)S(1)} %slice_bitcast_fusion.refs_0_), channel_id=1, source_target_pairs={{4,0},{5,1},{6,2},{7,3},{0,4},{1,5},{2,6},{3,7},{12,8},{13,9},{14,... | collective-permute-start | bytes 221192 | tf_op jit(solution)/shard_map/ppermute | solution.py:452
  18.0 1.2 %collective-permute-start.8 = (bf16[32,1152]{1,0:T(8,128)(2,1)S(1)}, bf16[32,1152]{1,0:T(8,128)(2,1)S(1)}, u32[]{:S(2)}, u32[]{:S(2)}) collective-permute-start(bf16[32,1152]{1,0:T(8,128)(2,1)S(1)} %slice_bitcast_fusion.refs_0_), channel_id=1, source_target_pairs={{6,0},{7,1},{4,2},{5,3},{2,4},{3,5},{0,6},{1,7},{14,8},{15,9},{12,... | collective-permute-start | bytes 221192 | tf_op jit(solution)/shard_map/ppermute | solution.py:452
  19.2 0.5 %collective-permute-start.9 = (bf16[32,1152]{1,0:T(8,128)(2,1)S(1)}, bf16[32,1152]{1,0:T(8,128)(2,1)S(1)}, u32[]{:S(2)}, u32[]{:S(2)}) collective-permute-start(bf16[32,1152]{1,0:T(8,128)(2,1)S(1)} %slice_bitcast_fusion.refs_0_), channel_id=1, source_target_pairs={{1,0},{0,1},{3,2},{2,3},{5,4},{4,5},{7,6},{6,7},{9,8},{8,9},{11,10... | collective-permute-start | bytes 221192 | tf_op jit(solution)/shard_map/ppermute | solution.py:452
  19.7 1.4 %fusion.wp_ref = bf16[1024,512]{1,0:T(8,128)(2,1)S(1)} fusion(bf16[36,512]{1,0:T(8,128)(2,1)} %param.22, bf16[1024,36]{1,0:T(8,128)(2,1)} %constant.114.clone), kind=kOutput, calls=%fused_computation.1 | convolution fusion | flops 38273024 | bytes 1159168 | tf_op jit(solution)/shard_map/dot_general | solution.py:34
  21.1 4.1 %weights_by_block.1 = (bf16[1728,1152]{1,0:T(8,128)(2,1)S(1)}, bf16[1728,1152]{1,0:T(8,128)(2,1)S(1)}, bf16[640,1152]{1,0:T(8,128)(2,1)S(1)}, bf16[640,1152]{1,0:T(8,128)(2,1)S(1)}) custom-call(bf16[1,1728,1152]{2,1,0:T(8,128)(2,1)} %bitcast.34, bf16[1,1728,1152]{2,1,0:T(8,128)(2,1)} %collective-permute-done.3.other_ref, bf16[1,576,1152]{2,1,0:T(8,128)(2,1)} %wo_own.1, ...), custom_call_target="tpu_custom_call" | custom-call | tf_op jit(solution)/shard_map/weights_by_block/pallas_call | solution.py:163
  25.2 1.6 %collective-permute-start.10 = (bf16[96,1152]{1,0:T(8,128)(2,1)S(1)}, bf16[96,1152]{1,0:T(8,128)(2,1)S(1)}, u32[]{:S(2)}, u32[]{:S(2)}) collective-permute-start(bf16[96,1152]{1,0:T(8,128)(2,1)S(1)} %pad_maximum_fusion.1.refs_1_), channel_id=1, source_target_pairs={{1,0},{0,1},{3,2},{2,3},{5,4},{4,5},{7,6},{6,7},{9,8},{8,9},{11,10... | collective-permute-start | bytes 663560 | tf_op jit(solution)/shard_map/ppermute | solution.py:452
  26.8 1.9 %layer_norm_and_projections.1 = (bf16[256,1152]{1,0:T(8,128)(2,1)S(1)}, bf16[256,640]{1,0:T(8,128)(2,1)S(1)}, bf16[256,1152]{1,0:T(8,128)(2,1)S(1)}, bf16[64,115...) custom-call(bf16[128,1152]{1,0:T(8,128)(2,1)S(1)} %pad_maximum_fusio, ...), custom_call_target="tpu_custom_call" | custom-call | tf_op jit(solution)/shard_map/layer_norm_and_projections/pallas_call | solution.py:211
  28.8 0.5 %collective-permute-start.12 = (bf16[64,1152]{1,0:T(8,128)(2,1)S(1)}, bf16[64,1152]{1,0:T(8,128)(2,1)S(1)}, u32[]{:S(2)}, u32[]{:S(2)}) collective-permute-start(bf16[64,1152]{1,0:T(8,128)(2,1)S(1)} %get-tuple-element.68), channel_id=1, source_target_pairs={{0,8},{8,0},{1,9},{9,1},{2,10},{10,2},{3,11},{11,3},{4,12},{12,4},... | collective-permute-start | bytes 442376 | tf_op jit(solution)/shard_map/ppermute | solution.py:528
  31.2 4.3 %attention_and_next_keys.1 = (bf16[256,1152]{1,0:T(8,128)(2,1)S(1)}, bf16[256,1152]{1,0:T(8,128)(2,1)S(1)}, bf16[256,1152]{1,0:T(8,128)(2,1)S(1)}, bf16[256,1152]{1,0:T(8,128)(2,1)S(1)}) custom-call(bf16[32,1152]{1,0:T(8,128)(2,1)S(1)} %slice_bitcast_fusion.refs_0_, bf16[96,1152]{1,0:T(8,128)(2,1)S(1)} %pad_maximum_fusion.1.refs_1_, ...), custom_call_target="tpu_custom_call" | custom-call | tf_op jit(solution)/shard_map/attention_and_next_keys/pallas_call | solution.py:307
  35.6 2.1 %tile_attention_over_own_keys.1 = (bf16[48,1152]{1,0:T(8,128)(2,1)S(1)}, bf16[48,640]{1,0:T(8,128)(2,1)S(1)}, f32[48,640]{1,0:T(8,128)S(1)}, f32[48,128]{1,0:T(8,128)S(1)}) custom-call(bf16[256,1152]{1,0:T(8,128)(2,1)S(1)} %get-tuple-element.76.x_ref, bf16[256,1152]{1,0:T(8,128)(2,1)S(1)} %get-tuple-element.77.mod_ref, ...), custom_call_target="tpu_custom_call" | custom-call | tf_op jit(solution)/shard_map/tile_attention_over_own_keys/pallas_call | solution.py:250
  37.8 2.5 %tile_attention_and_patches.1.patch_ref = f32[48,128]{1,0:T(8,128)S(1)} custom-call(bf16[48,1152]{1,0:T(8,128)(2,1)S(1)} %get-tuple-element.80.x_ref, bf16[48,640]{1,0:T(8,128)(2,1)S(1)} %get-tuple-element.81.q_ref, f32[48,640]{1,0:T(8,128)S(1)} %get-tuple-element.82.sum_ref, f32[48,128]{1,0:T(8,128)S(1)} %get-tuple-element.83.state_ref, ...), custom_call_target="tpu_custom_call" | custom-call | tf_op jit(solution)/shard_map/tile_attention_and_patches/pallas_call | solution.py:334
  40.3 0.5 %collective-permute-start.16 = (f32[48,128]{1,0:T(8,128)S(1)}, f32[48,128]{1,0:T(8,128)S(1)}, u32[]{:S(2)}, u32[]{:S(2)}) collective-permute-start(f32[48,128]{1,0:T(8,128)S(1)} %tile_attention_and_patches.1.patch_ref), channel_id=1, source_target_pairs={{0,8},{8,0},{1,9},{9,1},{2,10},{10,2},{3,11},{11,3},{4,12},{12,4},... | collective-permute-start | bytes 73736 | tf_op jit(solution)/shard_map/ppermute | solution.py:536
  40.9 0.8 %collective-permute-done.16.got_ref = f32[48,128]{1,0:T(8,128)S(1)} collective-permute-done((f32[48,128]{1,0:T(8,128)S(1)}, f32[48,128]{1,0:T(8,128)S(1)}, u32[]{:S(2)}, u32[]{:S(2)}) %collective-permute-start.16) | collective-permute-done | bytes 24608 | tf_op jit(solution)/shard_map/ppermute | solution.py:536
  41.7 3.1 %decoder_convolutions.1 = bf16[4,128,512]{2,1,0:T(8,128)(2,1)} custom-call(f32[48,128]{1,0:T(8,128)S(1)} %tile_attention_and_patches.1.patch_ref, f32[48,128]{1,0:T(8,128)S(1)} %collective-permute-done.16.got_ref, s32[48,128]{1,0:T(8,128)S(1)} %broadcast_in_dim.14.idx_ref, bf16[1024,512]{1,0:T(8,128)(2,1)S(1)} %fusion.wp_ref, f32[1,512]{1,0:T(1,128)S(1)} %bitcast.31, ...), custom_call_target="tpu_custom_call" | custom-call | tf_op jit(solution)/shard_map/decoder_convolutions/pallas_call | solution.py:417
  (43 shorter events, 2.8 us)
Async XLA Ops:
  0.0 7.4 %copy-start = (f32[100,5,1152]{2,0,1:T(8,128)S(1)}, f32[100,5,1152]{2,0,1:T(8,128)}, u32[]{:S(2)}) copy-start(f32[100,5,1152]{2,0,1:T(8,128)} %param.19) | copy-start | bytes 6912004
  0.0 13.1 %collective-permute-start.3 = (bf16[1,1728,1152]{2,1,0:T(8,128)(2,1)}, bf16[1,1728,1152]{2,1,0:T(8,128)(2,1)}, u32[]{:S(2)}, u32[]{:S(2)}) collective-permute-start(bf16[1,1728,1152]{2,1,0:T(8,128)(2,1)} %bitcast.33), channel_id=1, source_target_pairs={{0,8},{8,0},{1,9},{9,1},{2,10},{10,2},{3,11},{11,3},{4,12},{12,4},... | collective-permute-start | bytes 11943944 | tf_op jit(solution)/shard_map/ppermute | solution.py:483
  1.6 10.3 %collective-permute-start = (bf16[32,1152]{1,0:T(8,128)(2,1)S(1)}, bf16[32,1152]{1,0:T(8,128)(2,1)S(1)}, u32[]{:S(2)}, u32[]{:S(2)}) collective-permute-start(bf16[32,1152]{1,0:T(8,128)(2,1)S(1)} %dynamic-slice_bitcast_fusion), channel_id=1, source_target_pairs={{2,0},{3,1},{0,2},{1,3},{6,4},{7,5},{4,6},{5,7},{10,8},{11,9},{8,1... | collective-permute-start | bytes 221192 | tf_op jit(solution)/shard_map/ppermute | solution.py:452
  4.1 9.0 %collective-permute-start.1 = (bf16[32,1152]{1,0:T(8,128)(2,1)S(1)}, bf16[32,1152]{1,0:T(8,128)(2,1)S(1)}, u32[]{:S(2)}, u32[]{:S(2)}) collective-permute-start(bf16[32,1152]{1,0:T(8,128)(2,1)S(1)} %dynamic-slice_bitcast_fusion), channel_id=1, source_target_pairs={{4,0},{5,1},{6,2},{7,3},{0,4},{1,5},{2,6},{3,7},{12,8},{13,9},{14,... | collective-permute-start | bytes 221192 | tf_op jit(solution)/shard_map/ppermute | solution.py:452
  6.7 6.4 %collective-permute-start.2 = (bf16[32,1152]{1,0:T(8,128)(2,1)S(1)}, bf16[32,1152]{1,0:T(8,128)(2,1)S(1)}, u32[]{:S(2)}, u32[]{:S(2)}) collective-permute-start(bf16[32,1152]{1,0:T(8,128)(2,1)S(1)} %dynamic-slice_bitcast_fusion), channel_id=1, source_target_pairs={{6,0},{7,1},{4,2},{5,3},{2,4},{3,5},{0,6},{1,7},{14,8},{15,9},{12,... | collective-permute-start | bytes 221192 | tf_op jit(solution)/shard_map/ppermute | solution.py:452
  6.7 6.4 %collective-permute-start.4 = (bf16[1,576,1152]{2,1,0:T(8,128)(2,1)}, bf16[1,576,1152]{2,1,0:T(8,128)(2,1)}, u32[]{:S(2)}, u32[]{:S(2)}) collective-permute-start(bf16[1,576,1152]{2,1,0:T(8,128)(2,1)} %wo_own.1), channel_id=1, source_target_pairs={{0,8},{8,0},{1,9},{9,1},{2,10},{10,2},{3,11},{11,3},{4,12},{12,4},... | collective-permute-start | bytes 3981320 | tf_op jit(solution)/shard_map/ppermute | solution.py:487
  13.2 12.0 %collective-permute-start.5 = (bf16[128,1152]{1,0:T(8,128)(2,1)S(1)}, bf16[128,1152]{1,0:T(8,128)(2,1)S(1)}, u32[]{:S(2)}, u32[]{:S(2)}) collective-permute-start(bf16[128,1152]{1,0:T(8,128)(2,1)S(1)} %pad_maximum_fusion.refs_0_), channel_id=1, source_target_pairs={{1,0},{0,1},{3,2},{2,3},{5,4},{4,5},{7,6},{6,7},{9,8},{8,9},{11,10... | collective-permute-start | bytes 884744 | tf_op jit(solution)/shard_map/ppermute | solution.py:452
  14.8 10.4 %collective-permute-start.6 = (bf16[32,1152]{1,0:T(8,128)(2,1)S(1)}, bf16[32,1152]{1,0:T(8,128)(2,1)S(1)}, u32[]{:S(2)}, u32[]{:S(2)}) collective-permute-start(bf16[32,1152]{1,0:T(8,128)(2,1)S(1)} %slice_bitcast_fusion.refs_0_), channel_id=1, source_target_pairs={{2,0},{3,1},{0,2},{1,3},{6,4},{7,5},{4,6},{5,7},{10,8},{11,9},{8,1... | collective-permute-start | bytes 221192 | tf_op jit(solution)/shard_map/ppermute | solution.py:452
  16.3 8.8 %collective-permute-start.7 = (bf16[32,1152]{1,0:T(8,128)(2,1)S(1)}, bf16[32,1152]{1,0:T(8,128)(2,1)S(1)}, u32[]{:S(2)}, u32[]{:S(2)}) collective-permute-start(bf16[32,1152]{1,0:T(8,128)(2,1)S(1)} %slice_bitcast_fusion.refs_0_), channel_id=1, source_target_pairs={{4,0},{5,1},{6,2},{7,3},{0,4},{1,5},{2,6},{3,7},{12,8},{13,9},{14,... | collective-permute-start | bytes 221192 | tf_op jit(solution)/shard_map/ppermute | solution.py:452
  18.0 7.2 %collective-permute-start.8 = (bf16[32,1152]{1,0:T(8,128)(2,1)S(1)}, bf16[32,1152]{1,0:T(8,128)(2,1)S(1)}, u32[]{:S(2)}, u32[]{:S(2)}) collective-permute-start(bf16[32,1152]{1,0:T(8,128)(2,1)S(1)} %slice_bitcast_fusion.refs_0_), channel_id=1, source_target_pairs={{6,0},{7,1},{4,2},{5,3},{2,4},{3,5},{0,6},{1,7},{14,8},{15,9},{12,... | collective-permute-start | bytes 221192 | tf_op jit(solution)/shard_map/ppermute | solution.py:452
  19.2 6.0 %collective-permute-start.9 = (bf16[32,1152]{1,0:T(8,128)(2,1)S(1)}, bf16[32,1152]{1,0:T(8,128)(2,1)S(1)}, u32[]{:S(2)}, u32[]{:S(2)}) collective-permute-start(bf16[32,1152]{1,0:T(8,128)(2,1)S(1)} %slice_bitcast_fusion.refs_0_), channel_id=1, source_target_pairs={{1,0},{0,1},{3,2},{2,3},{5,4},{4,5},{7,6},{6,7},{9,8},{8,9},{11,10... | collective-permute-start | bytes 221192 | tf_op jit(solution)/shard_map/ppermute | solution.py:452
  25.2 6.0 %collective-permute-start.10 = (bf16[96,1152]{1,0:T(8,128)(2,1)S(1)}, bf16[96,1152]{1,0:T(8,128)(2,1)S(1)}, u32[]{:S(2)}, u32[]{:S(2)}) collective-permute-start(bf16[96,1152]{1,0:T(8,128)(2,1)S(1)} %pad_maximum_fusion.1.refs_1_), channel_id=1, source_target_pairs={{1,0},{0,1},{3,2},{2,3},{5,4},{4,5},{7,6},{6,7},{9,8},{8,9},{11,10... | collective-permute-start | bytes 663560 | tf_op jit(solution)/shard_map/ppermute | solution.py:452
  28.7 1.4 %collective-permute-start.11 = (bf16[64,1152]{1,0:T(8,128)(2,1)S(1)}, bf16[64,1152]{1,0:T(8,128)(2,1)S(1)}, u32[]{:S(2)}, u32[]{:S(2)}) collective-permute-start(bf16[64,1152]{1,0:T(8,128)(2,1)S(1)} %get-tuple-element.67), channel_id=1, source_target_pairs={{0,8},{8,0},{1,9},{9,1},{2,10},{10,2},{3,11},{11,3},{4,12},{12,4},... | collective-permute-start | bytes 442376 | tf_op jit(solution)/shard_map/ppermute | solution.py:528
  28.8 1.6 %collective-permute-start.12 = (bf16[64,1152]{1,0:T(8,128)(2,1)S(1)}, bf16[64,1152]{1,0:T(8,128)(2,1)S(1)}, u32[]{:S(2)}, u32[]{:S(2)}) collective-permute-start(bf16[64,1152]{1,0:T(8,128)(2,1)S(1)} %get-tuple-element.68), channel_id=1, source_target_pairs={{0,8},{8,0},{1,9},{9,1},{2,10},{10,2},{3,11},{11,3},{4,12},{12,4},... | collective-permute-start | bytes 442376 | tf_op jit(solution)/shard_map/ppermute | solution.py:528
  29.3 1.4 %collective-permute-start.13 = (bf16[64,1152]{1,0:T(8,128)(2,1)S(1)}, bf16[64,1152]{1,0:T(8,128)(2,1)S(1)}, u32[]{:S(2)}, u32[]{:S(2)}) collective-permute-start(bf16[64,1152]{1,0:T(8,128)(2,1)S(1)} %get-tuple-element.69), channel_id=1, source_target_pairs={{0,8},{8,0},{1,9},{9,1},{2,10},{10,2},{3,11},{11,3},{4,12},{12,4},... | collective-permute-start | bytes 442376 | tf_op jit(solution)/shard_map/ppermute | solution.py:528
  29.4 1.5 %collective-permute-start.14 = (bf16[64,1152]{1,0:T(8,128)(2,1)S(1)}, bf16[64,1152]{1,0:T(8,128)(2,1)S(1)}, u32[]{:S(2)}, u32[]{:S(2)}) collective-permute-start(bf16[64,1152]{1,0:T(8,128)(2,1)S(1)} %get-tuple-element.70), channel_id=1, source_target_pairs={{0,8},{8,0},{1,9},{9,1},{2,10},{10,2},{3,11},{11,3},{4,12},{12,4},... | collective-permute-start | bytes 442376 | tf_op jit(solution)/shard_map/ppermute | solution.py:528
  31.2 10.5 %slice-start = ((s8[4718592]{0:T(1024)(128)(4,1)}), s8[524288]{0:T(1024)(128)(4,1)S(1)}, s32[]{:S(2)}) async-start(s8[4718592]{0:T(1024)(128)(4,1)} %bitcast.28), calls=%async_computation | async-start | bytes 1048576
  35.5 2.2 %collective-permute-start.15 = (bf16[256,1152]{1,0:T(8,128)(2,1)S(1)}, bf16[256,1152]{1,0:T(8,128)(2,1)S(1)}, u32[]{:S(2)}, u32[]{:S(2)}) collective-permute-start(bf16[256,1152]{1,0:T(8,128)(2,1)S(1)} %get-tuple-element.84), channel_id=1, source_target_pairs={{0,8},{8,0},{1,9},{9,1},{2,10},{10,2},{3,11},{11,3},{4,12},{12,4},... | collective-permute-start | bytes 1769480 | tf_op jit(solution)/shard_map/ppermute | solution.py:530
  35.6 2.2 %copy-start.1 = (bf16[1152,16]{0,1:T(8,128)(2,1)S(1)}, bf16[1152,16]{0,1:T(8,128)(2,1)}, u32[]{:S(2)}) copy-start(bf16[1152,16]{0,1:T(8,128)(2,1)} %param.21) | copy-start | bytes 110596
  35.6 6.1 %slice-start.1 = ((s8[4718592]{0:T(1024)(128)(4,1)}), s8[4194304]{0:T(1024)(128)(4,1)S(1)}, s32[]{:S(2)}) async-start(s8[4718592]{0:T(1024)(128)(4,1)} %bitcast.28), calls=%async_computation.1 | async-start | bytes 8388608
  37.7 4.0 %copy-start.2 = (f32[512]{0:T(512)S(1)}, f32[512]{0:T(512)}, u32[]{:S(2)}) copy-start(f32[512]{0:T(512)} %param.23) | copy-start | bytes 6148
  37.7 4.0 %copy-start.3 = (f32[512]{0:T(512)S(1)}, f32[512]{0:T(512)}, u32[]{:S(2)}) copy-start(f32[512]{0:T(512)} %param.25) | copy-start | bytes 6148
  40.3 1.4 %collective-permute-start.16 = (f32[48,128]{1,0:T(8,128)S(1)}, f32[48,128]{1,0:T(8,128)S(1)}, u32[]{:S(2)}, u32[]{:S(2)}) collective-permute-start(f32[48,128]{1,0:T(8,128)S(1)} %tile_attention_and_patches.1.patch_ref), channel_id=1, source_target_pairs={{0,8},{8,0},{1,9},{9,1},{2,10},{10,2},{3,11},{11,3},{4,12},{12,4},... | collective-permute-start | bytes 73736 | tf_op jit(solution)/shard_map/ppermute | solution.py:536

commit v17 on v16

--- a/solution.py
+++ b/solution.py
@@ -516,11 +516,8 @@
     x_pieces = [x_column] + [swapped(x_column, 0, k) for k in range(1, inner)]
     stale_column = [swapped(own_stale, k, 0) for k in range(1, outer)]
     stale_line = [swapped(own_stale, 0, k) for k in range(1, inner)]
-    w_patch = dot(jnp.asarray(patch_selector(), BF16), w_in).astype(BF16)
     w_0, w_1, wo_0, wo_1 = weights_in_vmem(w_qkv, w_qkv_other, w_out, w_out_other)
-    x_pieces, stale_column, stale_line, w_patch, w_0 = lax.optimization_barrier(
-        (x_pieces, stale_column, stale_line, w_patch, w_0)
-    )
+    x_pieces, stale_column, stale_line, w_0 = lax.optimization_barrier((x_pieces, stale_column, stale_line, w_0))
     stale_column = jnp.concatenate(stale_column, axis=0)
     x_pieces, stale_column = lax.optimization_barrier((x_pieces, stale_column))
     stale_pieces = [own_stale, stale_column] + stale_line + [swapped(stale_column, 0, k) for k in range(1, inner)]
@@ -530,6 +527,8 @@
     got = lax.ppermute(send, "pipe", swap)
     x_tile, q_tile, sums, state = attend_fresh(x, modulated, fresh, idx, w_1)
     patches = tile_block(x_tile, q_tile, sums, state, got, idx, vecs, w_final.T, wo_1)
+    patches, w_in = lax.optimization_barrier((patches, w_in))
+    w_patch = dot(jnp.asarray(patch_selector(), BF16), w_in).astype(BF16)
     edge = patches
     if rows > 1:
         edge = jnp.where(first_core, patches[(rows - 1) * pitch : rows * pitch], patches[:pitch])

time: 45.1 us -> 44.3 us (0.982)
  matrix products: 1.37 us -> 0.4 us
  waiting for transfers between devices: 3.53 us -> 4.2 us
  starting transfers between devices: 15.3 us -> 14.8 us
    ppermute x9, waiting for transfers between devices: 1.6 us -> 2.68 us  [swapped(): lax.ppermute(block, 'patch', [(i ^ k_outer * inner + k_inner, i) for i in...]
    dot_general x1, matrix products: 1.37 us -> 0.4 us  [dot(): return jnp.dot(a, b, preferred_element_type=F32)]
    ppermute x9, starting transfers between devices: 13.2 us -> 12.7 us  [swapped(): lax.ppermute(block, 'patch', [(i ^ k_outer * inner + k_inner, i) for i in...]
  transfers between devices with their start and end apart: 17 -> 17, of which waited for: 7 -> 8; matrix products, arithmetic and copies ran while one was open for 11% -> 9% of each run, Pallas kernels for 18% -> 18%
where the time goes in v17:
time: 44.3 us; the launch traced here: 44 us
  Pallas kernels  18 us (41%)
  starting transfers between devices  14.8 us (33%)
  waiting for transfers between devices  4.2 us (9%)
  local copies, waits for them, and re-layouts  2.89 us (7%)
  blocking collectives  1.99 us (4%)
  between operations  0.9 us (2%)
  other arithmetic  0.84 us (2%)
    ppermute x9, starting transfers between devices, swapped(): lax.ppermute(block, 'patch', [(i ^ k_outer * inner + k_inner, i) for i in...  12.7 us
    pallas_call x1, Pallas kernels, first_block(): pl.pallas_call(functools.partial(block_kernel, len(stale_pieces), len(got...  4.3 us
    pallas_call x1, Pallas kernels, weights_in_vmem(): pl.pallas_call(weights_kernel, out_shape=(jax.ShapeDtypeStruct((3 * DA, D...  4.08 us
    pallas_call x1, Pallas kernels, decode(): pl.pallas_call(functools.partial(decode_kernel, rows, cols, pitch), out_s...  3.13 us
    ppermute x9, waiting for transfers between devices, swapped(): lax.ppermute(block, 'patch', [(i ^ k_outer * inner + k_inner, i) for i in...  2.68 us
    pallas_call x1, Pallas kernels, tile_block(): pl.pallas_call(tile_kernel, out_shape=jax.ShapeDtypeStruct((x.shape[0], L...  2.54 us
    pallas_call x1, Pallas kernels, attend_fresh(): pl.pallas_call(fresh_kernel, out_shape=(jax.ShapeDtypeStruct((rows, D), B...  2.08 us
    all_gather x1, blocking collectives, local(): tables = lax.all_gather(block_table[0], 'pipe')  1.99 us
  transfers between devices with their start and end apart: 17, of which 8 were waited for; matrix products, arithmetic and copies ran while one was open for 9% of the time, Pallas kernels for 18%

profile of v17, /device:TPU:0, one launch (start us, length us, event | category | flops | bytes accessed | tf_op | source)
XLA Modules:
  0.0 44.0 jit_solution(8796885150903870879)
XLA Ops:
  0.5 1.1 %dynamic-slice_bitcast_fusion = bf16[32,1152]{1,0:T(8,128)(2,1)S(1)} fusion(bf16[2,32,1152]{2,1,0:T(8,128)(2,1)} %param.14, s32[]{:T(128)S(6)} %select_n.80), kind=kLoop, calls=%fused_computation.5 | loop fusion | bytes 147460 | tf_op jit(solution)/shard_map/jit(dynamic_index_in_dim)/squeeze | solution.py:481
  1.6 2.5 %collective-permute-start = (bf16[32,1152]{1,0:T(8,128)(2,1)S(1)}, bf16[32,1152]{1,0:T(8,128)(2,1)S(1)}, u32[]{:S(2)}, u32[]{:S(2)}) collective-permute-start(bf16[32,1152]{1,0:T(8,128)(2,1)S(1)} %dynamic-slice_bitcast_fusion), channel_id=1, source_target_pairs={{2,0},{3,1},{0,2},{1,3},{6,4},{7,5},{4,6},{5,7},{10,8},{11,9},{8,1... | collective-permute-start | bytes 221192 | tf_op jit(solution)/shard_map/ppermute | solution.py:452
  4.1 2.6 %collective-permute-start.1 = (bf16[32,1152]{1,0:T(8,128)(2,1)S(1)}, bf16[32,1152]{1,0:T(8,128)(2,1)S(1)}, u32[]{:S(2)}, u32[]{:S(2)}) collective-permute-start(bf16[32,1152]{1,0:T(8,128)(2,1)S(1)} %dynamic-slice_bitcast_fusion), channel_id=1, source_target_pairs={{4,0},{5,1},{6,2},{7,3},{0,4},{1,5},{2,6},{3,7},{12,8},{13,9},{14,... | collective-permute-start | bytes 221192 | tf_op jit(solution)/shard_map/ppermute | solution.py:452
  7.5 0.7 %copy.19 = f32[1,3,1152]{2,1,0:T(4,128)S(1)} copy(f32[1,3,1152]{2,0,1:T(1,128)} %param.18) | data formatting | bytes 27648 | tf_op args[4]
  8.2 2.0 %all_gather.3 = f32[2,3,1152]{2,1,0:T(4,128)S(1)} all-gather(f32[1,3,1152]{2,1,0:T(4,128)S(1)} %copy.19), channel_id=1, replica_groups=mesh['grp'=2,'pipe'=2,'patch'=8] {'pipe'}, dimensions={0}, use_global_device_ids=true | all-gather | bytes 41472 | tf_op jit(solution)/shard_map/all_gather | solution.py:484
  10.2 0.7 %fusion.2 = (f32[3,1152]{1,0:T(4,128)S(1)}, f32[3,1152]{1,0:T(4,128)S(1)}) fusion(f32[1,3,1152]{2,0,1:T(1,128)S(1)} %constant_dynamic-slice_fusion, f32[2,3,1152]{2,1,0:T(4,128)S(1)} %all_gather.3, f32[3]{0:T(128)} %constant.120), kind=kLoop, calls=%fused_computation.10 | loop fusion | flops 13824 | bytes 69132 | tf_op jit(solution)/shard_map/add | solution.py:493
  10.9 0.9 %slice_bitcast_fusion.refs_0_ = bf16[32,1152]{1,0:T(8,128)(2,1)S(1)} fusion(bf16[1,2,32,1152]{3,2,1,0:T(8,128)(2,1)} %param.15), kind=kLoop, calls=%fused_computation.4 | loop fusion | bytes 147456 | tf_op jit(solution)/shard_map/squeeze | solution.py:486
  11.9 1.2 %collective-permute-done.1 = bf16[32,1152]{1,0:T(8,128)(2,1)S(1)} collective-permute-done((bf16[32,1152]{1,0:T(8,128)(2,1)S(1)}, bf16[32,1152]{1,0:T(8,128)(2,1)S(1)}, u32[]{:S(2)}, u32[]{:S(2)}) %collective-permute-start.1) | collective-permute-done | bytes 73760 | tf_op jit(solution)/shard_map/ppermute | solution.py:452
  13.2 1.6 %collective-permute-start.5 = (bf16[128,1152]{1,0:T(8,128)(2,1)S(1)}, bf16[128,1152]{1,0:T(8,128)(2,1)S(1)}, u32[]{:S(2)}, u32[]{:S(2)}) collective-permute-start(bf16[128,1152]{1,0:T(8,128)(2,1)S(1)} %pad_maximum_fusion.refs_0_), channel_id=1, source_target_pairs={{1,0},{0,1},{3,2},{2,3},{5,4},{4,5},{7,6},{6,7},{9,8},{8,9},{11,10... | collective-permute-start | bytes 884744 | tf_op jit(solution)/shard_map/ppermute | solution.py:452
  14.8 1.6 %collective-permute-start.6 = (bf16[32,1152]{1,0:T(8,128)(2,1)S(1)}, bf16[32,1152]{1,0:T(8,128)(2,1)S(1)}, u32[]{:S(2)}, u32[]{:S(2)}) collective-permute-start(bf16[32,1152]{1,0:T(8,128)(2,1)S(1)} %slice_bitcast_fusion.refs_0_), channel_id=1, source_target_pairs={{2,0},{3,1},{0,2},{1,3},{6,4},{7,5},{4,6},{5,7},{10,8},{11,9},{8,1... | collective-permute-start | bytes 221192 | tf_op jit(solution)/shard_map/ppermute | solution.py:452
  16.3 1.6 %collective-permute-start.7 = (bf16[32,1152]{1,0:T(8,128)(2,1)S(1)}, bf16[32,1152]{1,0:T(8,128)(2,1)S(1)}, u32[]{:S(2)}, u32[]{:S(2)}) collective-permute-start(bf16[32,1152]{1,0:T(8,128)(2,1)S(1)} %slice_bitcast_fusion.refs_0_), channel_id=1, source_target_pairs={{4,0},{5,1},{6,2},{7,3},{0,4},{1,5},{2,6},{3,7},{12,8},{13,9},{14,... | collective-permute-start | bytes 221192 | tf_op jit(solution)/shard_map/ppermute | solution.py:452
  18.0 1.2 %collective-permute-start.8 = (bf16[32,1152]{1,0:T(8,128)(2,1)S(1)}, bf16[32,1152]{1,0:T(8,128)(2,1)S(1)}, u32[]{:S(2)}, u32[]{:S(2)}) collective-permute-start(bf16[32,1152]{1,0:T(8,128)(2,1)S(1)} %slice_bitcast_fusion.refs_0_), channel_id=1, source_target_pairs={{6,0},{7,1},{4,2},{5,3},{2,4},{3,5},{0,6},{1,7},{14,8},{15,9},{12,... | collective-permute-start | bytes 221192 | tf_op jit(solution)/shard_map/ppermute | solution.py:452
  19.2 0.5 %collective-permute-start.9 = (bf16[32,1152]{1,0:T(8,128)(2,1)S(1)}, bf16[32,1152]{1,0:T(8,128)(2,1)S(1)}, u32[]{:S(2)}, u32[]{:S(2)}) collective-permute-start(bf16[32,1152]{1,0:T(8,128)(2,1)S(1)} %slice_bitcast_fusion.refs_0_), channel_id=1, source_target_pairs={{1,0},{0,1},{3,2},{2,3},{5,4},{4,5},{7,6},{6,7},{9,8},{8,9},{11,10... | collective-permute-start | bytes 221192 | tf_op jit(solution)/shard_map/ppermute | solution.py:452
  19.7 4.1 %weights_by_block.1 = (bf16[1728,1152]{1,0:T(8,128)(2,1)S(1)}, bf16[1728,1152]{1,0:T(8,128)(2,1)S(1)}, bf16[640,1152]{1,0:T(8,128)(2,1)S(1)}, bf16[640,1152]{1,0:T(8,128)(2,1)S(1)}) custom-call(bf16[1,1728,1152]{2,1,0:T(8,128)(2,1)} %bitcast.34, bf16[1,1728,1152]{2,1,0:T(8,128)(2,1)} %collective-permute-done.3.other_ref, bf16[1,576,1152]{2,1,0:T(8,128)(2,1)} %wo_own.1, ...), custom_call_target="tpu_custom_call" | custom-call | tf_op jit(solution)/shard_map/weights_by_block/pallas_call | solution.py:163
  23.8 0.6 %collective-permute-done.7 = bf16[32,1152]{1,0:T(8,128)(2,1)S(1)} collective-permute-done((bf16[32,1152]{1,0:T(8,128)(2,1)S(1)}, bf16[32,1152]{1,0:T(8,128)(2,1)S(1)}, u32[]{:S(2)}, u32[]{:S(2)}) %collective-permute-start.7) | collective-permute-done | bytes 73760 | tf_op jit(solution)/shard_map/ppermute | solution.py:452
  24.4 1.1 %collective-permute-start.10 = (bf16[96,1152]{1,0:T(8,128)(2,1)S(1)}, bf16[96,1152]{1,0:T(8,128)(2,1)S(1)}, u32[]{:S(2)}, u32[]{:S(2)}) collective-permute-start(bf16[96,1152]{1,0:T(8,128)(2,1)S(1)} %pad_maximum_fusion.1.refs_1_), channel_id=1, source_target_pairs={{1,0},{0,1},{3,2},{2,3},{5,4},{4,5},{7,6},{6,7},{9,8},{8,9},{11,10... | collective-permute-start | bytes 663560 | tf_op jit(solution)/shard_map/ppermute | solution.py:452
  25.4 1.9 %layer_norm_and_projections.1 = (bf16[256,1152]{1,0:T(8,128)(2,1)S(1)}, bf16[256,640]{1,0:T(8,128)(2,1)S(1)}, bf16[256,1152]{1,0:T(8,128)(2,1)S(1)}, bf16[64,115...) custom-call(bf16[128,1152]{1,0:T(8,128)(2,1)S(1)} %pad_maximum_fusio, ...), custom_call_target="tpu_custom_call" | custom-call | tf_op jit(solution)/shard_map/layer_norm_and_projections/pallas_call | solution.py:211
  27.4 0.5 %collective-permute-start.12 = (bf16[64,1152]{1,0:T(8,128)(2,1)S(1)}, bf16[64,1152]{1,0:T(8,128)(2,1)S(1)}, u32[]{:S(2)}, u32[]{:S(2)}) collective-permute-start(bf16[64,1152]{1,0:T(8,128)(2,1)S(1)} %get-tuple-element.68), channel_id=1, source_target_pairs={{0,8},{8,0},{1,9},{9,1},{2,10},{10,2},{3,11},{11,3},{4,12},{12,4},... | collective-permute-start | bytes 442376 | tf_op jit(solution)/shard_map/ppermute | solution.py:525
  29.5 0.9 %collective-permute-done.10.refs_3_ = bf16[96,1152]{1,0:T(8,128)(2,1)S(1)} collective-permute-done((bf16[96,1152]{1,0:T(8,128)(2,1)S(1)}, bf16[96,1152]{1,0:T(8,128)(2,1)S(1)}, u32[]{:S(2)}, u32[]{:S(2)}) %collective-permute-start.10) | collective-permute-done | bytes 221216 | tf_op jit(solution)/shard_map/ppermute | solution.py:452
  30.4 4.3 %attention_and_next_keys.1 = (bf16[256,1152]{1,0:T(8,128)(2,1)S(1)}, bf16[256,1152]{1,0:T(8,128)(2,1)S(1)}, bf16[256,1152]{1,0:T(8,128)(2,1)S(1)}, bf16[256,1152]{1,0:T(8,128)(2,1)S(1)}) custom-call(bf16[32,1152]{1,0:T(8,128)(2,1)S(1)} %slice_bitcast_fusion.refs_0_, bf16[96,1152]{1,0:T(8,128)(2,1)S(1)} %pad_maximum_fusion.1.refs_1_, ...), custom_call_target="tpu_custom_call" | custom-call | tf_op jit(solution)/shard_map/attention_and_next_keys/pallas_call | solution.py:307
  34.8 2.1 %tile_attention_over_own_keys.1 = (bf16[48,1152]{1,0:T(8,128)(2,1)S(1)}, bf16[48,640]{1,0:T(8,128)(2,1)S(1)}, f32[48,640]{1,0:T(8,128)S(1)}, f32[48,128]{1,0:T(8,128)S(1)}) custom-call(bf16[256,1152]{1,0:T(8,128)(2,1)S(1)} %get-tuple-element.76.x_ref, bf16[256,1152]{1,0:T(8,128)(2,1)S(1)} %get-tuple-element.77.mod_ref, ...), custom_call_target="tpu_custom_call" | custom-call | tf_op jit(solution)/shard_map/tile_attention_over_own_keys/pallas_call | solution.py:250
  37.0 2.5 %tile_attention_and_patches.1.patch_ref = f32[48,128]{1,0:T(8,128)S(1)} custom-call(bf16[48,1152]{1,0:T(8,128)(2,1)S(1)} %get-tuple-element.80.x_ref, bf16[48,640]{1,0:T(8,128)(2,1)S(1)} %get-tuple-element.81.q_ref, f32[48,640]{1,0:T(8,128)S(1)} %get-tuple-element.82.sum_ref, f32[48,128]{1,0:T(8,128)S(1)} %get-tuple-element.83.state_ref, ...), custom_call_target="tpu_custom_call" | custom-call | tf_op jit(solution)/shard_map/tile_attention_and_patches/pallas_call | solution.py:334
  39.5 0.5 %collective-permute-start.16 = (f32[48,128]{1,0:T(8,128)S(1)}, f32[48,128]{1,0:T(8,128)S(1)}, u32[]{:S(2)}, u32[]{:S(2)}) collective-permute-start(f32[48,128]{1,0:T(8,128)S(1)} %tile_attention_and_patches.1.patch_ref), channel_id=1, source_target_pairs={{0,8},{8,0},{1,9},{9,1},{2,10},{10,2},{3,11},{11,3},{4,12},{12,4},... | collective-permute-start | bytes 73736 | tf_op jit(solution)/shard_map/ppermute | solution.py:535
  40.9 3.1 %decoder_convolutions.1 = bf16[4,128,512]{2,1,0:T(8,128)(2,1)} custom-call(f32[48,128]{1,0:T(8,128)S(1)} %tile_attention_and_patches.1.patch_ref, f32[48,128]{1,0:T(8,128)S(1)} %collective-permute-done.16.got_ref, s32[48,128]{1,0:T(8,128)S(1)} %broadcast_in_dim.14.idx_ref, bf16[1024,512]{1,0:T(8,128)(2,1)S(1)} %fusion.wp_ref, f32[1,512]{1,0:T(1,128)S(1)} %bitcast.31, ...), custom_call_target="tpu_custom_call" | custom-call | tf_op jit(solution)/shard_map/decoder_convolutions/pallas_call | solution.py:417
  (47 shorter events, 3.3 us)
Async XLA Ops:
  0.0 7.4 %copy-start = (f32[100,5,1152]{2,0,1:T(8,128)S(1)}, f32[100,5,1152]{2,0,1:T(8,128)}, u32[]{:S(2)}) copy-start(f32[100,5,1152]{2,0,1:T(8,128)} %param.19) | copy-start | bytes 6912004
  0.0 13.1 %collective-permute-start.3 = (bf16[1,1728,1152]{2,1,0:T(8,128)(2,1)}, bf16[1,1728,1152]{2,1,0:T(8,128)(2,1)}, u32[]{:S(2)}, u32[]{:S(2)}) collective-permute-start(bf16[1,1728,1152]{2,1,0:T(8,128)(2,1)} %bitcast.33), channel_id=1, source_target_pairs={{0,8},{8,0},{1,9},{9,1},{2,10},{10,2},{3,11},{11,3},{4,12},{12,4},... | collective-permute-start | bytes 11943944 | tf_op jit(solution)/shard_map/ppermute | solution.py:483
  1.6 10.3 %collective-permute-start = (bf16[32,1152]{1,0:T(8,128)(2,1)S(1)}, bf16[32,1152]{1,0:T(8,128)(2,1)S(1)}, u32[]{:S(2)}, u32[]{:S(2)}) collective-permute-start(bf16[32,1152]{1,0:T(8,128)(2,1)S(1)} %dynamic-slice_bitcast_fusion), channel_id=1, source_target_pairs={{2,0},{3,1},{0,2},{1,3},{6,4},{7,5},{4,6},{5,7},{10,8},{11,9},{8,1... | collective-permute-start | bytes 221192 | tf_op jit(solution)/shard_map/ppermute | solution.py:452
  4.1 9.0 %collective-permute-start.1 = (bf16[32,1152]{1,0:T(8,128)(2,1)S(1)}, bf16[32,1152]{1,0:T(8,128)(2,1)S(1)}, u32[]{:S(2)}, u32[]{:S(2)}) collective-permute-start(bf16[32,1152]{1,0:T(8,128)(2,1)S(1)} %dynamic-slice_bitcast_fusion), channel_id=1, source_target_pairs={{4,0},{5,1},{6,2},{7,3},{0,4},{1,5},{2,6},{3,7},{12,8},{13,9},{14,... | collective-permute-start | bytes 221192 | tf_op jit(solution)/shard_map/ppermute | solution.py:452
  6.7 6.4 %collective-permute-start.2 = (bf16[32,1152]{1,0:T(8,128)(2,1)S(1)}, bf16[32,1152]{1,0:T(8,128)(2,1)S(1)}, u32[]{:S(2)}, u32[]{:S(2)}) collective-permute-start(bf16[32,1152]{1,0:T(8,128)(2,1)S(1)} %dynamic-slice_bitcast_fusion), channel_id=1, source_target_pairs={{6,0},{7,1},{4,2},{5,3},{2,4},{3,5},{0,6},{1,7},{14,8},{15,9},{12,... | collective-permute-start | bytes 221192 | tf_op jit(solution)/shard_map/ppermute | solution.py:452
  6.7 6.4 %collective-permute-start.4 = (bf16[1,576,1152]{2,1,0:T(8,128)(2,1)}, bf16[1,576,1152]{2,1,0:T(8,128)(2,1)}, u32[]{:S(2)}, u32[]{:S(2)}) collective-permute-start(bf16[1,576,1152]{2,1,0:T(8,128)(2,1)} %wo_own.1), channel_id=1, source_target_pairs={{0,8},{8,0},{1,9},{9,1},{2,10},{10,2},{3,11},{11,3},{4,12},{12,4},... | collective-permute-start | bytes 3981320 | tf_op jit(solution)/shard_map/ppermute | solution.py:487
  13.2 11.1 %collective-permute-start.5 = (bf16[128,1152]{1,0:T(8,128)(2,1)S(1)}, bf16[128,1152]{1,0:T(8,128)(2,1)S(1)}, u32[]{:S(2)}, u32[]{:S(2)}) collective-permute-start(bf16[128,1152]{1,0:T(8,128)(2,1)S(1)} %pad_maximum_fusion.refs_0_), channel_id=1, source_target_pairs={{1,0},{0,1},{3,2},{2,3},{5,4},{4,5},{7,6},{6,7},{9,8},{8,9},{11,10... | collective-permute-start | bytes 884744 | tf_op jit(solution)/shard_map/ppermute | solution.py:452
  14.8 9.0 %collective-permute-start.6 = (bf16[32,1152]{1,0:T(8,128)(2,1)S(1)}, bf16[32,1152]{1,0:T(8,128)(2,1)S(1)}, u32[]{:S(2)}, u32[]{:S(2)}) collective-permute-start(bf16[32,1152]{1,0:T(8,128)(2,1)S(1)} %slice_bitcast_fusion.refs_0_), channel_id=1, source_target_pairs={{2,0},{3,1},{0,2},{1,3},{6,4},{7,5},{4,6},{5,7},{10,8},{11,9},{8,1... | collective-permute-start | bytes 221192 | tf_op jit(solution)/shard_map/ppermute | solution.py:452
  16.3 8.0 %collective-permute-start.7 = (bf16[32,1152]{1,0:T(8,128)(2,1)S(1)}, bf16[32,1152]{1,0:T(8,128)(2,1)S(1)}, u32[]{:S(2)}, u32[]{:S(2)}) collective-permute-start(bf16[32,1152]{1,0:T(8,128)(2,1)S(1)} %slice_bitcast_fusion.refs_0_), channel_id=1, source_target_pairs={{4,0},{5,1},{6,2},{7,3},{0,4},{1,5},{2,6},{3,7},{12,8},{13,9},{14,... | collective-permute-start | bytes 221192 | tf_op jit(solution)/shard_map/ppermute | solution.py:452
  18.0 6.4 %collective-permute-start.8 = (bf16[32,1152]{1,0:T(8,128)(2,1)S(1)}, bf16[32,1152]{1,0:T(8,128)(2,1)S(1)}, u32[]{:S(2)}, u32[]{:S(2)}) collective-permute-start(bf16[32,1152]{1,0:T(8,128)(2,1)S(1)} %slice_bitcast_fusion.refs_0_), channel_id=1, source_target_pairs={{6,0},{7,1},{4,2},{5,3},{2,4},{3,5},{0,6},{1,7},{14,8},{15,9},{12,... | collective-permute-start | bytes 221192 | tf_op jit(solution)/shard_map/ppermute | solution.py:452
  19.2 5.2 %collective-permute-start.9 = (bf16[32,1152]{1,0:T(8,128)(2,1)S(1)}, bf16[32,1152]{1,0:T(8,128)(2,1)S(1)}, u32[]{:S(2)}, u32[]{:S(2)}) collective-permute-start(bf16[32,1152]{1,0:T(8,128)(2,1)S(1)} %slice_bitcast_fusion.refs_0_), channel_id=1, source_target_pairs={{1,0},{0,1},{3,2},{2,3},{5,4},{4,5},{7,6},{6,7},{9,8},{8,9},{11,10... | collective-permute-start | bytes 221192 | tf_op jit(solution)/shard_map/ppermute | solution.py:452
  24.4 6.0 %collective-permute-start.10 = (bf16[96,1152]{1,0:T(8,128)(2,1)S(1)}, bf16[96,1152]{1,0:T(8,128)(2,1)S(1)}, u32[]{:S(2)}, u32[]{:S(2)}) collective-permute-start(bf16[96,1152]{1,0:T(8,128)(2,1)S(1)} %pad_maximum_fusion.1.refs_1_), channel_id=1, source_target_pairs={{1,0},{0,1},{3,2},{2,3},{5,4},{4,5},{7,6},{6,7},{9,8},{8,9},{11,10... | collective-permute-start | bytes 663560 | tf_op jit(solution)/shard_map/ppermute | solution.py:452
  27.3 1.4 %collective-permute-start.11 = (bf16[64,1152]{1,0:T(8,128)(2,1)S(1)}, bf16[64,1152]{1,0:T(8,128)(2,1)S(1)}, u32[]{:S(2)}, u32[]{:S(2)}) collective-permute-start(bf16[64,1152]{1,0:T(8,128)(2,1)S(1)} %get-tuple-element.67), channel_id=1, source_target_pairs={{0,8},{8,0},{1,9},{9,1},{2,10},{10,2},{3,11},{11,3},{4,12},{12,4},... | collective-permute-start | bytes 442376 | tf_op jit(solution)/shard_map/ppermute | solution.py:525
  27.4 1.6 %collective-permute-start.12 = (bf16[64,1152]{1,0:T(8,128)(2,1)S(1)}, bf16[64,1152]{1,0:T(8,128)(2,1)S(1)}, u32[]{:S(2)}, u32[]{:S(2)}) collective-permute-start(bf16[64,1152]{1,0:T(8,128)(2,1)S(1)} %get-tuple-element.68), channel_id=1, source_target_pairs={{0,8},{8,0},{1,9},{9,1},{2,10},{10,2},{3,11},{11,3},{4,12},{12,4},... | collective-permute-start | bytes 442376 | tf_op jit(solution)/shard_map/ppermute | solution.py:525
  27.9 1.4 %collective-permute-start.13 = (bf16[64,1152]{1,0:T(8,128)(2,1)S(1)}, bf16[64,1152]{1,0:T(8,128)(2,1)S(1)}, u32[]{:S(2)}, u32[]{:S(2)}) collective-permute-start(bf16[64,1152]{1,0:T(8,128)(2,1)S(1)} %get-tuple-element.69), channel_id=1, source_target_pairs={{0,8},{8,0},{1,9},{9,1},{2,10},{10,2},{3,11},{11,3},{4,12},{12,4},... | collective-permute-start | bytes 442376 | tf_op jit(solution)/shard_map/ppermute | solution.py:525
  28.0 1.5 %collective-permute-start.14 = (bf16[64,1152]{1,0:T(8,128)(2,1)S(1)}, bf16[64,1152]{1,0:T(8,128)(2,1)S(1)}, u32[]{:S(2)}, u32[]{:S(2)}) collective-permute-start(bf16[64,1152]{1,0:T(8,128)(2,1)S(1)} %get-tuple-element.70), channel_id=1, source_target_pairs={{0,8},{8,0},{1,9},{9,1},{2,10},{10,2},{3,11},{11,3},{4,12},{12,4},... | collective-permute-start | bytes 442376 | tf_op jit(solution)/shard_map/ppermute | solution.py:525
  34.7 2.3 %collective-permute-start.15 = (bf16[256,1152]{1,0:T(8,128)(2,1)S(1)}, bf16[256,1152]{1,0:T(8,128)(2,1)S(1)}, u32[]{:S(2)}, u32[]{:S(2)}) collective-permute-start(bf16[256,1152]{1,0:T(8,128)(2,1)S(1)} %get-tuple-element.84), channel_id=1, source_target_pairs={{0,8},{8,0},{1,9},{9,1},{2,10},{10,2},{3,11},{11,3},{4,12},{12,4},... | collective-permute-start | bytes 1769480 | tf_op jit(solution)/shard_map/ppermute | solution.py:527
  34.8 6.1 %slice-start = ((s8[4718592]{0:T(1024)(128)(4,1)}), s8[4194304]{0:T(1024)(128)(4,1)S(1)}, s32[]{:S(2)}) async-start(s8[4718592]{0:T(1024)(128)(4,1)} %bitcast.28), calls=%async_computation | async-start | bytes 8388608
  34.8 6.1 %slice-start.1 = ((s8[4718592]{0:T(1024)(128)(4,1)}), s8[524288]{0:T(1024)(128)(4,1)S(1)}, s32[]{:S(2)}) async-start(s8[4718592]{0:T(1024)(128)(4,1)} %bitcast.28), calls=%async_computation.1 | async-start | bytes 1048576
  36.9 3.2 %copy-start.4 = (bf16[1024,36]{1,0:T(8,128)(2,1)S(1)}, bf16[1024,36]{1,0:T(8,128)(2,1)}, u32[]{:S(2)}) copy-start(bf16[1024,36]{1,0:T(8,128)(2,1)} %constant.114.clone) | copy-start | bytes 221188
  36.9 3.1 %copy-start.5 = (bf16[36,512]{1,0:T(8,128)(2,1)S(1)}, bf16[36,512]{1,0:T(8,128)(2,1)}, u32[]{:S(2)}) copy-start(bf16[36,512]{1,0:T(8,128)(2,1)} %param.22) | copy-start | bytes 110596
  36.9 4.0 %copy-start.2 = (f32[512]{0:T(512)S(1)}, f32[512]{0:T(512)}, u32[]{:S(2)}) copy-start(f32[512]{0:T(512)} %param.23) | copy-start | bytes 6148
  36.9 4.0 %copy-start.3 = (f32[512]{0:T(512)S(1)}, f32[512]{0:T(512)}, u32[]{:S(2)}) copy-start(f32[512]{0:T(512)} %param.25) | copy-start | bytes 6148
  39.5 1.4 %collective-permute-start.16 = (f32[48,128]{1,0:T(8,128)S(1)}, f32[48,128]{1,0:T(8,128)S(1)}, u32[]{:S(2)}, u32[]{:S(2)}) collective-permute-start(f32[48,128]{1,0:T(8,128)S(1)} %tile_attention_and_patches.1.patch_ref), channel_id=1, source_target_pairs={{0,8},{8,0},{1,9},{9,1},{2,10},{10,2},{3,11},{11,3},{4,12},{12,4},... | collective-permute-start | bytes 73736 | tf_op jit(solution)/shard_map/ppermute | solution.py:535
  (1 other events, 2.2 us)

commit v18 on v17

--- a/solution.py
+++ b/solution.py
@@ -342,7 +342,7 @@
 
 
 def decode_kernel(
-    rows, cols, pitch, patch_ref, got_ref, idx_ref, wp_ref, bin_ref, bup_ref, w_ref, out_ref, u_ref, ub_ref
+    rows, cols, pitch, patch_ref, got_ref, idx_ref, wp_ref, bin_ref, bup_ref, w_ref, out_ref, f_ref, fb_ref, o_ref
 ):
     first_core = lax.axis_index("pipe") == 0
     got = got_ref[:pitch]
@@ -384,33 +384,49 @@
                 kept = jnp.where(keep, feature[i * pitch : (i + 1) * pitch], 0.0)
                 for c in range(CH // LANES):
                     part = kept[:, c * LANES : (c + 1) * LANES]
-                    u_ref[y, c, pl.ds(2 * q, pitch, stride=4), :] = part
-                    u_ref[y, c, pl.ds(2 * q + 1, pitch, stride=4), :] = part
-    wide = 4 * cols
+                    f_ref[y, c, pl.ds(RIM - 2 + q, pitch, stride=2), :] = part
+    across = 2 * cols
+    wide = feature_pitch(cols)
     for y in range(2 * rows + 2):
-        for dx in range(3):
-            for c in range(CH // LANES):
-                ub_ref[dx, y * wide : (y + 1) * wide, c * LANES : (c + 1) * LANES] = u_ref[
-                    y, c, 3 + dx : 3 + dx + wide, :
-                ].astype(BF16)
-
-    def tap_row(dy, y_first, y_count):
-        total = None
-        for dx in range(3):
-            part = dot(ub_ref[dx, y_first * wide : (y_first + y_count) * wide], w_ref[3 * dy + dx])
-            total = part if total is None else total + part
-        return total
-
-    def rows_of(total, y):
-        return total[y * wide : (y + 1) * wide]
-
-    middle = tap_row(1, 1, 2 * rows) + bup_ref[...]
-    before = tap_row(0, 0, 2 * rows + 1)
-    after = tap_row(2, 1, 2 * rows + 1)
-    for y in range(2 * rows):
-        own = rows_of(middle, y)
-        out_ref[2 * y] = (own + rows_of(before, y) + rows_of(after, y)).astype(BF16)
-        out_ref[2 * y + 1] = (own + rows_of(before, y + 1) + rows_of(after, y + 1)).astype(BF16)
+        for c in range(CH // LANES):
+            fb_ref[y * wide : (y + 1) * wide, c * LANES : (c + 1) * LANES] = f_ref[y, c, :wide, :].astype(BF16)
+
+    def product(dy, dx, first, count):
+        return dot(fb_ref[first * wide : (first + count) * wide], w_ref[3 * dy + dx])
+
+    sums = []
+    for dx in range(3):
+        before = product(0, dx, 0, 2 * rows + 1)
+        middle = product(1, dx, 1, 2 * rows)
+        after = product(2, dx, 1, 2 * rows + 1)
+
+        def rows_of(total, y):
+            return total[y * wide : (y + 1) * wide]
+
+        sums.append(
+            [
+                rows_of(middle, y) + rows_of(before, y + odd) + rows_of(after, y + odd)
+                for y in range(2 * rows)
+                for odd in range(2)
+            ]
+        )
+    for row in range(4 * rows):
+        left, centre, right = (sums[dx][row] for dx in range(3))
+        here = slice(RIM, RIM + across)
+        even = (centre + right)[here] + left[RIM - 1 : RIM - 1 + across] + bup_ref[...]
+        odd = (centre + left)[here] + right[RIM + 1 : RIM + 1 + across] + bup_ref[...]
+        for c in range(CH // LANES):
+            lanes = slice(c * LANES, (c + 1) * LANES)
+            o_ref[row, c, pl.ds(0, across, stride=2), :] = even[:, lanes]
+            o_ref[row, c, pl.ds(1, across, stride=2), :] = odd[:, lanes]
+            out_ref[row, :, lanes] = o_ref[row, c].astype(BF16)
+
+
+RIM = 8
+
+
+def feature_pitch(cols):
+    return -(-(2 * cols + 2 * RIM) // 16) * 16
 
 
 def decode(rows, cols, pitch, patches, got, idx, w_patch, b_in, b_up, w_up):
@@ -420,8 +436,9 @@
         in_specs=[VMEM] * 7,
         out_specs=VMEM,
         scratch_shapes=[
-            pltpu.VMEM((2 * rows + 2, CH // LANES, 4 * pitch, LANES), F32),
-            pltpu.VMEM((3, (2 * rows + 2) * 4 * cols, CH), BF16),
+            pltpu.VMEM((2 * rows + 2, CH // LANES, max(2 * pitch + RIM, feature_pitch(cols)), LANES), F32),
+            pltpu.VMEM(((2 * rows + 2) * feature_pitch(cols), CH), BF16),
+            pltpu.VMEM((4 * rows, CH // LANES, 4 * cols, LANES), F32),
         ],
         compiler_params=params(0),
         name="decoder_convolutions",

time: 44.3 us -> 43.9 us (level)
  no operation moved by 1% of the time
where the time goes in v18:
time: 43.9 us; the launch traced here: 43.6 us
  Pallas kernels  17.6 us (40%)
  starting transfers between devices  14.8 us (34%)
  waiting for transfers between devices  4.2 us (10%)
  local copies, waits for them, and re-layouts  2.89 us (7%)
  blocking collectives  1.99 us (5%)
  between operations  0.9 us (2%)
  other arithmetic  0.84 us (2%)
    ppermute x9, starting transfers between devices, swapped(): lax.ppermute(block, 'patch', [(i ^ k_outer * inner + k_inner, i) for i in...  12.7 us
    pallas_call x1, Pallas kernels, first_block(): pl.pallas_call(functools.partial(block_kernel, len(stale_pieces), len(got...  4.3 us
    pallas_call x1, Pallas kernels, weights_in_vmem(): pl.pallas_call(weights_kernel, out_shape=(jax.ShapeDtypeStruct((3 * DA, D...  4.08 us
    pallas_call x1, Pallas kernels, decode(): pl.pallas_call(functools.partial(decode_kernel, rows, cols, pitch), out_s...  2.7 us
    ppermute x9, waiting for transfers between devices, swapped(): lax.ppermute(block, 'patch', [(i ^ k_outer * inner + k_inner, i) for i in...  2.68 us
    pallas_call x1, Pallas kernels, tile_block(): pl.pallas_call(tile_kernel, out_shape=jax.ShapeDtypeStruct((x.shape[0], L...  2.54 us
    pallas_call x1, Pallas kernels, attend_fresh(): pl.pallas_call(fresh_kernel, out_shape=(jax.ShapeDtypeStruct((rows, D), B...  2.08 us
    all_gather x1, blocking collectives, local(): tables = lax.all_gather(block_table[0], 'pipe')  1.99 us
  transfers between devices with their start and end apart: 17, of which 8 were waited for; matrix products, arithmetic and copies ran while one was open for 9% of the time, Pallas kernels for 18%

profile of v18, /device:TPU:0, one launch (start us, length us, event | category | flops | bytes accessed | tf_op | source)
XLA Modules:
  0.0 43.6 jit_solution(6735780284745325670)
XLA Ops:
  0.5 1.1 %dynamic-slice_bitcast_fusion = bf16[32,1152]{1,0:T(8,128)(2,1)S(1)} fusion(bf16[2,32,1152]{2,1,0:T(8,128)(2,1)} %param.14, s32[]{:T(128)S(6)} %select_n.80), kind=kLoop, calls=%fused_computation.5 | loop fusion | bytes 147460 | tf_op jit(solution)/shard_map/jit(dynamic_index_in_dim)/squeeze | solution.py:498
  1.6 2.5 %collective-permute-start = (bf16[32,1152]{1,0:T(8,128)(2,1)S(1)}, bf16[32,1152]{1,0:T(8,128)(2,1)S(1)}, u32[]{:S(2)}, u32[]{:S(2)}) collective-permute-start(bf16[32,1152]{1,0:T(8,128)(2,1)S(1)} %dynamic-slice_bitcast_fusion), channel_id=1, source_target_pairs={{2,0},{3,1},{0,2},{1,3},{6,4},{7,5},{4,6},{5,7},{10,8},{11,9},{8,1... | collective-permute-start | bytes 221192 | tf_op jit(solution)/shard_map/ppermute | solution.py:469
  4.1 2.6 %collective-permute-start.1 = (bf16[32,1152]{1,0:T(8,128)(2,1)S(1)}, bf16[32,1152]{1,0:T(8,128)(2,1)S(1)}, u32[]{:S(2)}, u32[]{:S(2)}) collective-permute-start(bf16[32,1152]{1,0:T(8,128)(2,1)S(1)} %dynamic-slice_bitcast_fusion), channel_id=1, source_target_pairs={{4,0},{5,1},{6,2},{7,3},{0,4},{1,5},{2,6},{3,7},{12,8},{13,9},{14,... | collective-permute-start | bytes 221192 | tf_op jit(solution)/shard_map/ppermute | solution.py:469
  7.5 0.7 %copy.19 = f32[1,3,1152]{2,1,0:T(4,128)S(1)} copy(f32[1,3,1152]{2,0,1:T(1,128)} %param.18) | data formatting | bytes 27648 | tf_op args[4]
  8.2 2.0 %all_gather.3 = f32[2,3,1152]{2,1,0:T(4,128)S(1)} all-gather(f32[1,3,1152]{2,1,0:T(4,128)S(1)} %copy.19), channel_id=1, replica_groups=mesh['grp'=2,'pipe'=2,'patch'=8] {'pipe'}, dimensions={0}, use_global_device_ids=true | all-gather | bytes 41472 | tf_op jit(solution)/shard_map/all_gather | solution.py:501
  10.2 0.7 %fusion.2 = (f32[3,1152]{1,0:T(4,128)S(1)}, f32[3,1152]{1,0:T(4,128)S(1)}) fusion(f32[1,3,1152]{2,0,1:T(1,128)S(1)} %constant_dynamic-slice_fusion, f32[2,3,1152]{2,1,0:T(4,128)S(1)} %all_gather.3, f32[3]{0:T(128)} %constant.120), kind=kLoop, calls=%fused_computation.10 | loop fusion | flops 13824 | bytes 69132 | tf_op jit(solution)/shard_map/add | solution.py:510
  10.9 0.9 %slice_bitcast_fusion.refs_0_ = bf16[32,1152]{1,0:T(8,128)(2,1)S(1)} fusion(bf16[1,2,32,1152]{3,2,1,0:T(8,128)(2,1)} %param.15), kind=kLoop, calls=%fused_computation.4 | loop fusion | bytes 147456 | tf_op jit(solution)/shard_map/squeeze | solution.py:503
  11.9 1.2 %collective-permute-done.1 = bf16[32,1152]{1,0:T(8,128)(2,1)S(1)} collective-permute-done((bf16[32,1152]{1,0:T(8,128)(2,1)S(1)}, bf16[32,1152]{1,0:T(8,128)(2,1)S(1)}, u32[]{:S(2)}, u32[]{:S(2)}) %collective-permute-start.1) | collective-permute-done | bytes 73760 | tf_op jit(solution)/shard_map/ppermute | solution.py:469
  13.2 1.6 %collective-permute-start.5 = (bf16[128,1152]{1,0:T(8,128)(2,1)S(1)}, bf16[128,1152]{1,0:T(8,128)(2,1)S(1)}, u32[]{:S(2)}, u32[]{:S(2)}) collective-permute-start(bf16[128,1152]{1,0:T(8,128)(2,1)S(1)} %pad_maximum_fusion.refs_0_), channel_id=1, source_target_pairs={{1,0},{0,1},{3,2},{2,3},{5,4},{4,5},{7,6},{6,7},{9,8},{8,9},{11,10... | collective-permute-start | bytes 884744 | tf_op jit(solution)/shard_map/ppermute | solution.py:469
  14.8 1.6 %collective-permute-start.6 = (bf16[32,1152]{1,0:T(8,128)(2,1)S(1)}, bf16[32,1152]{1,0:T(8,128)(2,1)S(1)}, u32[]{:S(2)}, u32[]{:S(2)}) collective-permute-start(bf16[32,1152]{1,0:T(8,128)(2,1)S(1)} %slice_bitcast_fusion.refs_0_), channel_id=1, source_target_pairs={{2,0},{3,1},{0,2},{1,3},{6,4},{7,5},{4,6},{5,7},{10,8},{11,9},{8,1... | collective-permute-start | bytes 221192 | tf_op jit(solution)/shard_map/ppermute | solution.py:469
  16.3 1.6 %collective-permute-start.7 = (bf16[32,1152]{1,0:T(8,128)(2,1)S(1)}, bf16[32,1152]{1,0:T(8,128)(2,1)S(1)}, u32[]{:S(2)}, u32[]{:S(2)}) collective-permute-start(bf16[32,1152]{1,0:T(8,128)(2,1)S(1)} %slice_bitcast_fusion.refs_0_), channel_id=1, source_target_pairs={{4,0},{5,1},{6,2},{7,3},{0,4},{1,5},{2,6},{3,7},{12,8},{13,9},{14,... | collective-permute-start | bytes 221192 | tf_op jit(solution)/shard_map/ppermute | solution.py:469
  18.0 1.2 %collective-permute-start.8 = (bf16[32,1152]{1,0:T(8,128)(2,1)S(1)}, bf16[32,1152]{1,0:T(8,128)(2,1)S(1)}, u32[]{:S(2)}, u32[]{:S(2)}) collective-permute-start(bf16[32,1152]{1,0:T(8,128)(2,1)S(1)} %slice_bitcast_fusion.refs_0_), channel_id=1, source_target_pairs={{6,0},{7,1},{4,2},{5,3},{2,4},{3,5},{0,6},{1,7},{14,8},{15,9},{12,... | collective-permute-start | bytes 221192 | tf_op jit(solution)/shard_map/ppermute | solution.py:469
  19.2 0.5 %collective-permute-start.9 = (bf16[32,1152]{1,0:T(8,128)(2,1)S(1)}, bf16[32,1152]{1,0:T(8,128)(2,1)S(1)}, u32[]{:S(2)}, u32[]{:S(2)}) collective-permute-start(bf16[32,1152]{1,0:T(8,128)(2,1)S(1)} %slice_bitcast_fusion.refs_0_), channel_id=1, source_target_pairs={{1,0},{0,1},{3,2},{2,3},{5,4},{4,5},{7,6},{6,7},{9,8},{8,9},{11,10... | collective-permute-start | bytes 221192 | tf_op jit(solution)/shard_map/ppermute | solution.py:469
  19.7 4.1 %weights_by_block.1 = (bf16[1728,1152]{1,0:T(8,128)(2,1)S(1)}, bf16[1728,1152]{1,0:T(8,128)(2,1)S(1)}, bf16[640,1152]{1,0:T(8,128)(2,1)S(1)}, bf16[640,1152]{1,0:T(8,128)(2,1)S(1)}) custom-call(bf16[1,1728,1152]{2,1,0:T(8,128)(2,1)} %bitcast.34, bf16[1,1728,1152]{2,1,0:T(8,128)(2,1)} %collective-permute-done.3.other_ref, bf16[1,576,1152]{2,1,0:T(8,128)(2,1)} %wo_own.1, ...), custom_call_target="tpu_custom_call" | custom-call | tf_op jit(solution)/shard_map/weights_by_block/pallas_call | solution.py:163
  23.8 0.6 %collective-permute-done.7 = bf16[32,1152]{1,0:T(8,128)(2,1)S(1)} collective-permute-done((bf16[32,1152]{1,0:T(8,128)(2,1)S(1)}, bf16[32,1152]{1,0:T(8,128)(2,1)S(1)}, u32[]{:S(2)}, u32[]{:S(2)}) %collective-permute-start.7) | collective-permute-done | bytes 73760 | tf_op jit(solution)/shard_map/ppermute | solution.py:469
  24.4 1.1 %collective-permute-start.10 = (bf16[96,1152]{1,0:T(8,128)(2,1)S(1)}, bf16[96,1152]{1,0:T(8,128)(2,1)S(1)}, u32[]{:S(2)}, u32[]{:S(2)}) collective-permute-start(bf16[96,1152]{1,0:T(8,128)(2,1)S(1)} %pad_maximum_fusion.1.refs_1_), channel_id=1, source_target_pairs={{1,0},{0,1},{3,2},{2,3},{5,4},{4,5},{7,6},{6,7},{9,8},{8,9},{11,10... | collective-permute-start | bytes 663560 | tf_op jit(solution)/shard_map/ppermute | solution.py:469
  25.4 1.9 %layer_norm_and_projections.1 = (bf16[256,1152]{1,0:T(8,128)(2,1)S(1)}, bf16[256,640]{1,0:T(8,128)(2,1)S(1)}, bf16[256,1152]{1,0:T(8,128)(2,1)S(1)}, bf16[64,115...) custom-call(bf16[128,1152]{1,0:T(8,128)(2,1)S(1)} %pad_maximum_fusio, ...), custom_call_target="tpu_custom_call" | custom-call | tf_op jit(solution)/shard_map/layer_norm_and_projections/pallas_call | solution.py:211
  27.4 0.5 %collective-permute-start.12 = (bf16[64,1152]{1,0:T(8,128)(2,1)S(1)}, bf16[64,1152]{1,0:T(8,128)(2,1)S(1)}, u32[]{:S(2)}, u32[]{:S(2)}) collective-permute-start(bf16[64,1152]{1,0:T(8,128)(2,1)S(1)} %get-tuple-element.68), channel_id=1, source_target_pairs={{0,8},{8,0},{1,9},{9,1},{2,10},{10,2},{3,11},{11,3},{4,12},{12,4},... | collective-permute-start | bytes 442376 | tf_op jit(solution)/shard_map/ppermute | solution.py:542
  29.5 0.9 %collective-permute-done.10.refs_3_ = bf16[96,1152]{1,0:T(8,128)(2,1)S(1)} collective-permute-done((bf16[96,1152]{1,0:T(8,128)(2,1)S(1)}, bf16[96,1152]{1,0:T(8,128)(2,1)S(1)}, u32[]{:S(2)}, u32[]{:S(2)}) %collective-permute-start.10) | collective-permute-done | bytes 221216 | tf_op jit(solution)/shard_map/ppermute | solution.py:469
  30.4 4.3 %attention_and_next_keys.1 = (bf16[256,1152]{1,0:T(8,128)(2,1)S(1)}, bf16[256,1152]{1,0:T(8,128)(2,1)S(1)}, bf16[256,1152]{1,0:T(8,128)(2,1)S(1)}, bf16[256,1152]{1,0:T(8,128)(2,1)S(1)}) custom-call(bf16[32,1152]{1,0:T(8,128)(2,1)S(1)} %slice_bitcast_fusion.refs_0_, bf16[96,1152]{1,0:T(8,128)(2,1)S(1)} %pad_maximum_fusion.1.refs_1_, ...), custom_call_target="tpu_custom_call" | custom-call | tf_op jit(solution)/shard_map/attention_and_next_keys/pallas_call | solution.py:307
  34.8 2.1 %tile_attention_over_own_keys.1 = (bf16[48,1152]{1,0:T(8,128)(2,1)S(1)}, bf16[48,640]{1,0:T(8,128)(2,1)S(1)}, f32[48,640]{1,0:T(8,128)S(1)}, f32[48,128]{1,0:T(8,128)S(1)}) custom-call(bf16[256,1152]{1,0:T(8,128)(2,1)S(1)} %get-tuple-element.76.x_ref, bf16[256,1152]{1,0:T(8,128)(2,1)S(1)} %get-tuple-element.77.mod_ref, ...), custom_call_target="tpu_custom_call" | custom-call | tf_op jit(solution)/shard_map/tile_attention_over_own_keys/pallas_call | solution.py:250
  37.0 2.5 %tile_attention_and_patches.1.patch_ref = f32[48,128]{1,0:T(8,128)S(1)} custom-call(bf16[48,1152]{1,0:T(8,128)(2,1)S(1)} %get-tuple-element.80.x_ref, bf16[48,640]{1,0:T(8,128)(2,1)S(1)} %get-tuple-element.81.q_ref, f32[48,640]{1,0:T(8,128)S(1)} %get-tuple-element.82.sum_ref, f32[48,128]{1,0:T(8,128)S(1)} %get-tuple-element.83.state_ref, ...), custom_call_target="tpu_custom_call" | custom-call | tf_op jit(solution)/shard_map/tile_attention_and_patches/pallas_call | solution.py:334
  39.5 0.5 %collective-permute-start.16 = (f32[48,128]{1,0:T(8,128)S(1)}, f32[48,128]{1,0:T(8,128)S(1)}, u32[]{:S(2)}, u32[]{:S(2)}) collective-permute-start(f32[48,128]{1,0:T(8,128)S(1)} %tile_attention_and_patches.1.patch_ref), channel_id=1, source_target_pairs={{0,8},{8,0},{1,9},{9,1},{2,10},{10,2},{3,11},{11,3},{4,12},{12,4},... | collective-permute-start | bytes 73736 | tf_op jit(solution)/shard_map/ppermute | solution.py:552
  40.9 2.7 %decoder_convolutions.1 = bf16[4,128,512]{2,1,0:T(8,128)(2,1)} custom-call(f32[48,128]{1,0:T(8,128)S(1)} %tile_attention_and_patches.1.patch_ref, f32[48,128]{1,0:T(8,128)S(1)} %collective-permute-done.16.got_ref, s32[48,128]{1,0:T(8,128)S(1)} %broadcast_in_dim.14.idx_ref, bf16[1024,512]{1,0:T(8,128)(2,1)S(1)} %fusion.wp_ref, f32[1,512]{1,0:T(1,128)S(1)} %bitcast.31, ...), custom_call_target="tpu_custom_call" | custom-call | tf_op jit(solution)/shard_map/decoder_convolutions/pallas_call | solution.py:433
  (47 shorter events, 3.3 us)
Async XLA Ops:
  0.0 7.4 %copy-start = (f32[100,5,1152]{2,0,1:T(8,128)S(1)}, f32[100,5,1152]{2,0,1:T(8,128)}, u32[]{:S(2)}) copy-start(f32[100,5,1152]{2,0,1:T(8,128)} %param.19) | copy-start | bytes 6912004
  0.0 13.1 %collective-permute-start.3 = (bf16[1,1728,1152]{2,1,0:T(8,128)(2,1)}, bf16[1,1728,1152]{2,1,0:T(8,128)(2,1)}, u32[]{:S(2)}, u32[]{:S(2)}) collective-permute-start(bf16[1,1728,1152]{2,1,0:T(8,128)(2,1)} %bitcast.33), channel_id=1, source_target_pairs={{0,8},{8,0},{1,9},{9,1},{2,10},{10,2},{3,11},{11,3},{4,12},{12,4},... | collective-permute-start | bytes 11943944 | tf_op jit(solution)/shard_map/ppermute | solution.py:500
  1.6 10.3 %collective-permute-start = (bf16[32,1152]{1,0:T(8,128)(2,1)S(1)}, bf16[32,1152]{1,0:T(8,128)(2,1)S(1)}, u32[]{:S(2)}, u32[]{:S(2)}) collective-permute-start(bf16[32,1152]{1,0:T(8,128)(2,1)S(1)} %dynamic-slice_bitcast_fusion), channel_id=1, source_target_pairs={{2,0},{3,1},{0,2},{1,3},{6,4},{7,5},{4,6},{5,7},{10,8},{11,9},{8,1... | collective-permute-start | bytes 221192 | tf_op jit(solution)/shard_map/ppermute | solution.py:469
  4.1 9.0 %collective-permute-start.1 = (bf16[32,1152]{1,0:T(8,128)(2,1)S(1)}, bf16[32,1152]{1,0:T(8,128)(2,1)S(1)}, u32[]{:S(2)}, u32[]{:S(2)}) collective-permute-start(bf16[32,1152]{1,0:T(8,128)(2,1)S(1)} %dynamic-slice_bitcast_fusion), channel_id=1, source_target_pairs={{4,0},{5,1},{6,2},{7,3},{0,4},{1,5},{2,6},{3,7},{12,8},{13,9},{14,... | collective-permute-start | bytes 221192 | tf_op jit(solution)/shard_map/ppermute | solution.py:469
  6.7 6.4 %collective-permute-start.2 = (bf16[32,1152]{1,0:T(8,128)(2,1)S(1)}, bf16[32,1152]{1,0:T(8,128)(2,1)S(1)}, u32[]{:S(2)}, u32[]{:S(2)}) collective-permute-start(bf16[32,1152]{1,0:T(8,128)(2,1)S(1)} %dynamic-slice_bitcast_fusion), channel_id=1, source_target_pairs={{6,0},{7,1},{4,2},{5,3},{2,4},{3,5},{0,6},{1,7},{14,8},{15,9},{12,... | collective-permute-start | bytes 221192 | tf_op jit(solution)/shard_map/ppermute | solution.py:469
  6.7 6.4 %collective-permute-start.4 = (bf16[1,576,1152]{2,1,0:T(8,128)(2,1)}, bf16[1,576,1152]{2,1,0:T(8,128)(2,1)}, u32[]{:S(2)}, u32[]{:S(2)}) collective-permute-start(bf16[1,576,1152]{2,1,0:T(8,128)(2,1)} %wo_own.1), channel_id=1, source_target_pairs={{0,8},{8,0},{1,9},{9,1},{2,10},{10,2},{3,11},{11,3},{4,12},{12,4},... | collective-permute-start | bytes 3981320 | tf_op jit(solution)/shard_map/ppermute | solution.py:504
  13.2 11.1 %collective-permute-start.5 = (bf16[128,1152]{1,0:T(8,128)(2,1)S(1)}, bf16[128,1152]{1,0:T(8,128)(2,1)S(1)}, u32[]{:S(2)}, u32[]{:S(2)}) collective-permute-start(bf16[128,1152]{1,0:T(8,128)(2,1)S(1)} %pad_maximum_fusion.refs_0_), channel_id=1, source_target_pairs={{1,0},{0,1},{3,2},{2,3},{5,4},{4,5},{7,6},{6,7},{9,8},{8,9},{11,10... | collective-permute-start | bytes 884744 | tf_op jit(solution)/shard_map/ppermute | solution.py:469
  14.8 9.0 %collective-permute-start.6 = (bf16[32,1152]{1,0:T(8,128)(2,1)S(1)}, bf16[32,1152]{1,0:T(8,128)(2,1)S(1)}, u32[]{:S(2)}, u32[]{:S(2)}) collective-permute-start(bf16[32,1152]{1,0:T(8,128)(2,1)S(1)} %slice_bitcast_fusion.refs_0_), channel_id=1, source_target_pairs={{2,0},{3,1},{0,2},{1,3},{6,4},{7,5},{4,6},{5,7},{10,8},{11,9},{8,1... | collective-permute-start | bytes 221192 | tf_op jit(solution)/shard_map/ppermute | solution.py:469
  16.3 8.0 %collective-permute-start.7 = (bf16[32,1152]{1,0:T(8,128)(2,1)S(1)}, bf16[32,1152]{1,0:T(8,128)(2,1)S(1)}, u32[]{:S(2)}, u32[]{:S(2)}) collective-permute-start(bf16[32,1152]{1,0:T(8,128)(2,1)S(1)} %slice_bitcast_fusion.refs_0_), channel_id=1, source_target_pairs={{4,0},{5,1},{6,2},{7,3},{0,4},{1,5},{2,6},{3,7},{12,8},{13,9},{14,... | collective-permute-start | bytes 221192 | tf_op jit(solution)/shard_map/ppermute | solution.py:469
  18.0 6.4 %collective-permute-start.8 = (bf16[32,1152]{1,0:T(8,128)(2,1)S(1)}, bf16[32,1152]{1,0:T(8,128)(2,1)S(1)}, u32[]{:S(2)}, u32[]{:S(2)}) collective-permute-start(bf16[32,1152]{1,0:T(8,128)(2,1)S(1)} %slice_bitcast_fusion.refs_0_), channel_id=1, source_target_pairs={{6,0},{7,1},{4,2},{5,3},{2,4},{3,5},{0,6},{1,7},{14,8},{15,9},{12,... | collective-permute-start | bytes 221192 | tf_op jit(solution)/shard_map/ppermute | solution.py:469
  19.2 5.2 %collective-permute-start.9 = (bf16[32,1152]{1,0:T(8,128)(2,1)S(1)}, bf16[32,1152]{1,0:T(8,128)(2,1)S(1)}, u32[]{:S(2)}, u32[]{:S(2)}) collective-permute-start(bf16[32,1152]{1,0:T(8,128)(2,1)S(1)} %slice_bitcast_fusion.refs_0_), channel_id=1, source_target_pairs={{1,0},{0,1},{3,2},{2,3},{5,4},{4,5},{7,6},{6,7},{9,8},{8,9},{11,10... | collective-permute-start | bytes 221192 | tf_op jit(solution)/shard_map/ppermute | solution.py:469
  24.4 6.0 %collective-permute-start.10 = (bf16[96,1152]{1,0:T(8,128)(2,1)S(1)}, bf16[96,1152]{1,0:T(8,128)(2,1)S(1)}, u32[]{:S(2)}, u32[]{:S(2)}) collective-permute-start(bf16[96,1152]{1,0:T(8,128)(2,1)S(1)} %pad_maximum_fusion.1.refs_1_), channel_id=1, source_target_pairs={{1,0},{0,1},{3,2},{2,3},{5,4},{4,5},{7,6},{6,7},{9,8},{8,9},{11,10... | collective-permute-start | bytes 663560 | tf_op jit(solution)/shard_map/ppermute | solution.py:469
  27.3 1.4 %collective-permute-start.11 = (bf16[64,1152]{1,0:T(8,128)(2,1)S(1)}, bf16[64,1152]{1,0:T(8,128)(2,1)S(1)}, u32[]{:S(2)}, u32[]{:S(2)}) collective-permute-start(bf16[64,1152]{1,0:T(8,128)(2,1)S(1)} %get-tuple-element.67), channel_id=1, source_target_pairs={{0,8},{8,0},{1,9},{9,1},{2,10},{10,2},{3,11},{11,3},{4,12},{12,4},... | collective-permute-start | bytes 442376 | tf_op jit(solution)/shard_map/ppermute | solution.py:542
  27.4 1.6 %collective-permute-start.12 = (bf16[64,1152]{1,0:T(8,128)(2,1)S(1)}, bf16[64,1152]{1,0:T(8,128)(2,1)S(1)}, u32[]{:S(2)}, u32[]{:S(2)}) collective-permute-start(bf16[64,1152]{1,0:T(8,128)(2,1)S(1)} %get-tuple-element.68), channel_id=1, source_target_pairs={{0,8},{8,0},{1,9},{9,1},{2,10},{10,2},{3,11},{11,3},{4,12},{12,4},... | collective-permute-start | bytes 442376 | tf_op jit(solution)/shard_map/ppermute | solution.py:542
  27.9 1.4 %collective-permute-start.13 = (bf16[64,1152]{1,0:T(8,128)(2,1)S(1)}, bf16[64,1152]{1,0:T(8,128)(2,1)S(1)}, u32[]{:S(2)}, u32[]{:S(2)}) collective-permute-start(bf16[64,1152]{1,0:T(8,128)(2,1)S(1)} %get-tuple-element.69), channel_id=1, source_target_pairs={{0,8},{8,0},{1,9},{9,1},{2,10},{10,2},{3,11},{11,3},{4,12},{12,4},... | collective-permute-start | bytes 442376 | tf_op jit(solution)/shard_map/ppermute | solution.py:542
  28.0 1.5 %collective-permute-start.14 = (bf16[64,1152]{1,0:T(8,128)(2,1)S(1)}, bf16[64,1152]{1,0:T(8,128)(2,1)S(1)}, u32[]{:S(2)}, u32[]{:S(2)}) collective-permute-start(bf16[64,1152]{1,0:T(8,128)(2,1)S(1)} %get-tuple-element.70), channel_id=1, source_target_pairs={{0,8},{8,0},{1,9},{9,1},{2,10},{10,2},{3,11},{11,3},{4,12},{12,4},... | collective-permute-start | bytes 442376 | tf_op jit(solution)/shard_map/ppermute | solution.py:542
  34.7 2.3 %collective-permute-start.15 = (bf16[256,1152]{1,0:T(8,128)(2,1)S(1)}, bf16[256,1152]{1,0:T(8,128)(2,1)S(1)}, u32[]{:S(2)}, u32[]{:S(2)}) collective-permute-start(bf16[256,1152]{1,0:T(8,128)(2,1)S(1)} %get-tuple-element.84), channel_id=1, source_target_pairs={{0,8},{8,0},{1,9},{9,1},{2,10},{10,2},{3,11},{11,3},{4,12},{12,4},... | collective-permute-start | bytes 1769480 | tf_op jit(solution)/shard_map/ppermute | solution.py:544
  34.8 6.1 %slice-start = ((s8[4718592]{0:T(1024)(128)(4,1)}), s8[4194304]{0:T(1024)(128)(4,1)S(1)}, s32[]{:S(2)}) async-start(s8[4718592]{0:T(1024)(128)(4,1)} %bitcast.28), calls=%async_computation | async-start | bytes 8388608
  34.8 6.1 %slice-start.1 = ((s8[4718592]{0:T(1024)(128)(4,1)}), s8[524288]{0:T(1024)(128)(4,1)S(1)}, s32[]{:S(2)}) async-start(s8[4718592]{0:T(1024)(128)(4,1)} %bitcast.28), calls=%async_computation.1 | async-start | bytes 1048576
  36.9 3.2 %copy-start.4 = (bf16[1024,36]{1,0:T(8,128)(2,1)S(1)}, bf16[1024,36]{1,0:T(8,128)(2,1)}, u32[]{:S(2)}) copy-start(bf16[1024,36]{1,0:T(8,128)(2,1)} %constant.114.clone) | copy-start | bytes 221188
  36.9 3.1 %copy-start.5 = (bf16[36,512]{1,0:T(8,128)(2,1)S(1)}, bf16[36,512]{1,0:T(8,128)(2,1)}, u32[]{:S(2)}) copy-start(bf16[36,512]{1,0:T(8,128)(2,1)} %param.22) | copy-start | bytes 110596
  36.9 4.0 %copy-start.2 = (f32[512]{0:T(512)S(1)}, f32[512]{0:T(512)}, u32[]{:S(2)}) copy-start(f32[512]{0:T(512)} %param.23) | copy-start | bytes 6148
  36.9 4.0 %copy-start.3 = (f32[512]{0:T(512)S(1)}, f32[512]{0:T(512)}, u32[]{:S(2)}) copy-start(f32[512]{0:T(512)} %param.25) | copy-start | bytes 6148
  39.5 1.4 %collective-permute-start.16 = (f32[48,128]{1,0:T(8,128)S(1)}, f32[48,128]{1,0:T(8,128)S(1)}, u32[]{:S(2)}, u32[]{:S(2)}) collective-permute-start(f32[48,128]{1,0:T(8,128)S(1)} %tile_attention_and_patches.1.patch_ref), channel_id=1, source_target_pairs={{0,8},{8,0},{1,9},{9,1},{2,10},{10,2},{3,11},{11,3},{4,12},{12,4},... | collective-permute-start | bytes 73736 | tf_op jit(solution)/shard_map/ppermute | solution.py:552
  (1 other events, 2.2 us)

commit v19 on v18

--- a/solution.py
+++ b/solution.py
@@ -497,11 +497,11 @@
 
     own_tokens = lax.dynamic_index_in_dim(tokens, section, 0, keepdims=False)
     w_qkv = jnp.swapaxes(w_qkv, 1, 2)
-    w_qkv_other = lax.ppermute(w_qkv, "pipe", swap)
     tables = lax.all_gather(block_table[0], "pipe")
     x_column = [swapped(own_tokens, k, 0) for k in range(1, outer)]
     own_stale = stale_kv[0, 1]
     w_out_other = lax.ppermute(w_out, "pipe", swap)
+    stale_line = [swapped(own_stale, 0, k) for k in range(1, inner)]
 
     time_row = lax.dynamic_index_in_dim(time_table, t_index[0], 0, keepdims=False)
     ones = jnp.asarray([[0.0], [1.0], [0.0]], F32)
@@ -525,16 +525,16 @@
     spot = (k_inner * outer + k_outer) * own_count + token % own_count
     idx = jnp.broadcast_to(jnp.where(inside, spot, -1)[:, None], (padded_rows, LANES)).astype(jnp.int32)
 
-    x_column, w_qkv_other, w_out_other, vecs, idx, own_stale, w_in = lax.optimization_barrier(
-        (x_column, w_qkv_other, w_out_other, vecs, idx, own_stale, w_in)
+    x_column, stale_line, w_out_other, vecs, idx, own_stale, w_send = lax.optimization_barrier(
+        (x_column, stale_line, w_out_other, vecs, idx, own_stale, w_qkv)
     )
     x_column = jnp.concatenate([own_tokens] + x_column, axis=0)
     x_column, own_stale = lax.optimization_barrier((x_column, own_stale))
+    w_qkv_other = lax.ppermute(w_send, "pipe", swap)
     x_pieces = [x_column] + [swapped(x_column, 0, k) for k in range(1, inner)]
     stale_column = [swapped(own_stale, k, 0) for k in range(1, outer)]
-    stale_line = [swapped(own_stale, 0, k) for k in range(1, inner)]
     w_0, w_1, wo_0, wo_1 = weights_in_vmem(w_qkv, w_qkv_other, w_out, w_out_other)
-    x_pieces, stale_column, stale_line, w_0 = lax.optimization_barrier((x_pieces, stale_column, stale_line, w_0))
+    x_pieces, stale_column, w_0 = lax.optimization_barrier((x_pieces, stale_column, w_0))
     stale_column = jnp.concatenate(stale_column, axis=0)
     x_pieces, stale_column = lax.optimization_barrier((x_pieces, stale_column))
     stale_pieces = [own_stale, stale_column] + stale_line + [swapped(stale_column, 0, k) for k in range(1, inner)]

time: 43.9 us -> 45.3 us (1.032)
  waiting for transfers between devices: 4.2 us -> 5.63 us
  starting transfers between devices: 14.8 us -> 15.9 us
  Pallas kernels: 17.6 us -> 16.6 us
    ppermute x1, waiting for transfers between devices: 0.01 us -> 1.72 us  [local(): w_qkv_other = lax.ppermute(w_send, 'pipe', swap)]
    ppermute x9, starting transfers between devices: 12.7 us -> 13.9 us  [swapped(): lax.ppermute(block, 'patch', [(i ^ k_outer * inner + k_inner, i) for i in...]
    pallas_call x1, Pallas kernels: 4.08 us -> 3.05 us  [weights_in_vmem(): pl.pallas_call(weights_kernel, out_shape=(jax.ShapeDtypeStruct((3 * DA, D...]
  transfers between devices with their start and end apart: 17 -> 17, of which waited for: 8 -> 9; matrix products, arithmetic and copies ran while one was open for 9% -> 6% of each run, Pallas kernels for 18% -> 16%
where the time goes in v19:
time: 45.3 us; the launch traced here: 45.1 us
  Pallas kernels  16.6 us (37%)
  starting transfers between devices  15.9 us (35%)
  waiting for transfers between devices  5.63 us (12%)
  local copies, waits for them, and re-layouts  2.81 us (6%)
  blocking collectives  1.99 us (4%)
  between operations  0.92 us (2%)
  other arithmetic  0.85 us (2%)
    ppermute x9, starting transfers between devices, swapped(): lax.ppermute(block, 'patch', [(i ^ k_outer * inner + k_inner, i) for i in...  13.9 us
    pallas_call x1, Pallas kernels, first_block(): pl.pallas_call(functools.partial(block_kernel, len(stale_pieces), len(got...  4.29 us
    pallas_call x1, Pallas kernels, weights_in_vmem(): pl.pallas_call(weights_kernel, out_shape=(jax.ShapeDtypeStruct((3 * DA, D...  3.05 us
    pallas_call x1, Pallas kernels, decode(): pl.pallas_call(functools.partial(decode_kernel, rows, cols, pitch), out_s...  2.71 us
    pallas_call x1, Pallas kernels, tile_block(): pl.pallas_call(tile_kernel, out_shape=jax.ShapeDtypeStruct((x.shape[0], L...  2.54 us
    ppermute x9, waiting for transfers between devices, swapped(): lax.ppermute(block, 'patch', [(i ^ k_outer * inner + k_inner, i) for i in...  2.4 us
    pallas_call x1, Pallas kernels, attend_fresh(): pl.pallas_call(fresh_kernel, out_shape=(jax.ShapeDtypeStruct((rows, D), B...  2.08 us
    all_gather x1, blocking collectives, local(): tables = lax.all_gather(block_table[0], 'pipe')  1.99 us
  transfers between devices with their start and end apart: 17, of which 9 were waited for; matrix products, arithmetic and copies ran while one was open for 6% of the time, Pallas kernels for 16%

profile of v19, /device:TPU:0, one launch (start us, length us, event | category | flops | bytes accessed | tf_op | source)
XLA Modules:
  0.0 45.1 jit_solution(2347071373636853770)
XLA Ops:
  0.0 1.0 %dynamic-slice_bitcast_fusion = bf16[32,1152]{1,0:T(8,128)(2,1)S(1)} fusion(bf16[2,32,1152]{2,1,0:T(8,128)(2,1)} %param.14, s32[]{:T(128)S(6)} %select_n.80), kind=kLoop, calls=%fused_computation.5 | loop fusion | bytes 147460 | tf_op jit(solution)/shard_map/jit(dynamic_index_in_dim)/squeeze | solution.py:498
  1.0 3.0 %collective-permute-start = (bf16[32,1152]{1,0:T(8,128)(2,1)S(1)}, bf16[32,1152]{1,0:T(8,128)(2,1)S(1)}, u32[]{:S(2)}, u32[]{:S(2)}) collective-permute-start(bf16[32,1152]{1,0:T(8,128)(2,1)S(1)} %dynamic-slice_bitcast_fusion), channel_id=1, source_target_pairs={{2,0},{3,1},{0,2},{1,3},{6,4},{7,5},{4,6},{5,7},{10,8},{11,9},{8,1... | collective-permute-start | bytes 221192 | tf_op jit(solution)/shard_map/ppermute | solution.py:469
  4.1 2.6 %collective-permute-start.1 = (bf16[32,1152]{1,0:T(8,128)(2,1)S(1)}, bf16[32,1152]{1,0:T(8,128)(2,1)S(1)}, u32[]{:S(2)}, u32[]{:S(2)}) collective-permute-start(bf16[32,1152]{1,0:T(8,128)(2,1)S(1)} %dynamic-slice_bitcast_fusion), channel_id=1, source_target_pairs={{4,0},{5,1},{6,2},{7,3},{0,4},{1,5},{2,6},{3,7},{12,8},{13,9},{14,... | collective-permute-start | bytes 221192 | tf_op jit(solution)/shard_map/ppermute | solution.py:469
  6.7 0.9 %slice_bitcast_fusion.refs_0_ = bf16[32,1152]{1,0:T(8,128)(2,1)S(1)} fusion(bf16[1,2,32,1152]{3,2,1,0:T(8,128)(2,1)} %param.15), kind=kLoop, calls=%fused_computation.4 | loop fusion | bytes 147456 | tf_op jit(solution)/shard_map/squeeze | solution.py:502
  7.6 1.7 %collective-permute-start.3 = (bf16[32,1152]{1,0:T(8,128)(2,1)S(1)}, bf16[32,1152]{1,0:T(8,128)(2,1)S(1)}, u32[]{:S(2)}, u32[]{:S(2)}) collective-permute-start(bf16[32,1152]{1,0:T(8,128)(2,1)S(1)} %slice_bitcast_fusion.refs_0_), channel_id=1, source_target_pairs={{1,0},{0,1},{3,2},{2,3},{5,4},{4,5},{7,6},{6,7},{9,8},{8,9},{11,10... | collective-permute-start | bytes 221192 | tf_op jit(solution)/shard_map/ppermute | solution.py:469
  10.0 0.7 %copy.19 = f32[1,3,1152]{2,1,0:T(4,128)S(1)} copy(f32[1,3,1152]{2,0,1:T(1,128)} %param.18) | data formatting | bytes 27648 | tf_op args[4]
  10.7 2.0 %all_gather.3 = f32[2,3,1152]{2,1,0:T(4,128)S(1)} all-gather(f32[1,3,1152]{2,1,0:T(4,128)S(1)} %copy.19), channel_id=1, replica_groups=mesh['grp'=2,'pipe'=2,'patch'=8] {'pipe'}, dimensions={0}, use_global_device_ids=true | all-gather | bytes 41472 | tf_op jit(solution)/shard_map/all_gather | solution.py:500
  12.7 0.7 %fusion.2 = (f32[3,1152]{1,0:T(4,128)S(1)}, f32[3,1152]{1,0:T(4,128)S(1)}) fusion(f32[1,3,1152]{2,0,1:T(1,128)S(1)} %constant_dynamic-slice_fusion, f32[2,3,1152]{2,1,0:T(4,128)S(1)} %all_gather.3, f32[3]{0:T(128)} %constant.120), kind=kLoop, calls=%fused_computation.10 | loop fusion | flops 13824 | bytes 69132 | tf_op jit(solution)/shard_map/add | solution.py:510
  14.0 0.6 %collective-permute-start.5 = (bf16[128,1152]{1,0:T(8,128)(2,1)S(1)}, bf16[128,1152]{1,0:T(8,128)(2,1)S(1)}, u32[]{:S(2)}, u32[]{:S(2)}) collective-permute-start(bf16[128,1152]{1,0:T(8,128)(2,1)S(1)} %pad_maximum_fusion.refs_0_), channel_id=1, source_target_pairs={{1,0},{0,1},{3,2},{2,3},{5,4},{4,5},{7,6},{6,7},{9,8},{8,9},{11,10... | collective-permute-start | bytes 884744 | tf_op jit(solution)/shard_map/ppermute | solution.py:469
  14.6 1.1 %collective-permute-start.6 = (bf16[32,1152]{1,0:T(8,128)(2,1)S(1)}, bf16[32,1152]{1,0:T(8,128)(2,1)S(1)}, u32[]{:S(2)}, u32[]{:S(2)}) collective-permute-start(bf16[32,1152]{1,0:T(8,128)(2,1)S(1)} %slice_bitcast_fusion.refs_0_), channel_id=1, source_target_pairs={{2,0},{3,1},{0,2},{1,3},{6,4},{7,5},{4,6},{5,7},{10,8},{11,9},{8,1... | collective-permute-start | bytes 221192 | tf_op jit(solution)/shard_map/ppermute | solution.py:469
  15.7 3.1 %collective-permute-start.7 = (bf16[32,1152]{1,0:T(8,128)(2,1)S(1)}, bf16[32,1152]{1,0:T(8,128)(2,1)S(1)}, u32[]{:S(2)}, u32[]{:S(2)}) collective-permute-start(bf16[32,1152]{1,0:T(8,128)(2,1)S(1)} %slice_bitcast_fusion.refs_0_), channel_id=1, source_target_pairs={{4,0},{5,1},{6,2},{7,3},{0,4},{1,5},{2,6},{3,7},{12,8},{13,9},{14,... | collective-permute-start | bytes 221192 | tf_op jit(solution)/shard_map/ppermute | solution.py:469
  19.0 1.7 %collective-permute-done.9.other_ref = bf16[1,1728,1152]{2,1,0:T(8,128)(2,1)S(1)} collective-permute-done((bf16[1,1728,1152]{2,1,0:T(8,128)(2,1)}, bf16[1,1728,1152]{2,1,0:T(8,128)(2,1)S(1)}, u32[]{:S(2)}, u32[]{:S(2)}) %collective-permute-start.9) | collective-permute-done | bytes 3981344 | tf_op jit(solution)/shard_map/ppermute | solution.py:533
  20.7 3.0 %weights_by_block.1 = (bf16[1728,1152]{1,0:T(8,128)(2,1)S(1)}, bf16[1728,1152]{1,0:T(8,128)(2,1)S(1)}, bf16[640,1152]{1,0:T(8,128)(2,1)S(1)}, bf16[640,1152]{1,0:T(8,128)(2,1)S(1)}) custom-call(bf16[1,1728,1152]{2,1,0:T(8,128)(2,1)} %bitcast.34, bf16[1,1728,1152]{2,1,0:T(8,128)(2,1)S(1)} %collective-permute-done.9.other_ref, bf16[1,576,1152]{2,1,0:T(8,128)(2,1)} %wo_own.1, ...), custom_call_target="tpu_custom_call" | custom-call | tf_op jit(solution)/shard_map/weights_by_block/pallas_call | solution.py:163
  23.9 1.1 %collective-permute-done.8 = bf16[32,1152]{1,0:T(8,128)(2,1)S(1)} collective-permute-done((bf16[32,1152]{1,0:T(8,128)(2,1)S(1)}, bf16[32,1152]{1,0:T(8,128)(2,1)S(1)}, u32[]{:S(2)}, u32[]{:S(2)}) %collective-permute-start.8) | collective-permute-done | bytes 73760 | tf_op jit(solution)/shard_map/ppermute | solution.py:469
  25.1 1.6 %collective-permute-start.10 = (bf16[96,1152]{1,0:T(8,128)(2,1)S(1)}, bf16[96,1152]{1,0:T(8,128)(2,1)S(1)}, u32[]{:S(2)}, u32[]{:S(2)}) collective-permute-start(bf16[96,1152]{1,0:T(8,128)(2,1)S(1)} %pad_maximum_fusion.1.refs_1_), channel_id=1, source_target_pairs={{1,0},{0,1},{3,2},{2,3},{5,4},{4,5},{7,6},{6,7},{9,8},{8,9},{11,10... | collective-permute-start | bytes 663560 | tf_op jit(solution)/shard_map/ppermute | solution.py:469
  26.6 1.9 %layer_norm_and_projections.1 = (bf16[256,1152]{1,0:T(8,128)(2,1)S(1)}, bf16[256,640]{1,0:T(8,128)(2,1)S(1)}, bf16[256,1152]{1,0:T(8,128)(2,1)S(1)}, bf16[64,115...) custom-call(bf16[128,1152]{1,0:T(8,128)(2,1)S(1)} %pad_maximum_fusio, ...), custom_call_target="tpu_custom_call" | custom-call | tf_op jit(solution)/shard_map/layer_norm_and_projections/pallas_call | solution.py:211
  28.6 0.5 %collective-permute-start.12 = (bf16[64,1152]{1,0:T(8,128)(2,1)S(1)}, bf16[64,1152]{1,0:T(8,128)(2,1)S(1)}, u32[]{:S(2)}, u32[]{:S(2)}) collective-permute-start(bf16[64,1152]{1,0:T(8,128)(2,1)S(1)} %get-tuple-element.67), channel_id=1, source_target_pairs={{0,8},{8,0},{1,9},{9,1},{2,10},{10,2},{3,11},{11,3},{4,12},{12,4},... | collective-permute-start | bytes 442376 | tf_op jit(solution)/shard_map/ppermute | solution.py:542
  30.7 1.1 %collective-permute-done.10.refs_3_ = bf16[96,1152]{1,0:T(8,128)(2,1)S(1)} collective-permute-done((bf16[96,1152]{1,0:T(8,128)(2,1)S(1)}, bf16[96,1152]{1,0:T(8,128)(2,1)S(1)}, u32[]{:S(2)}, u32[]{:S(2)}) %collective-permute-start.10) | collective-permute-done | bytes 221216 | tf_op jit(solution)/shard_map/ppermute | solution.py:469
  31.9 4.3 %attention_and_next_keys.1 = (bf16[256,1152]{1,0:T(8,128)(2,1)S(1)}, bf16[256,1152]{1,0:T(8,128)(2,1)S(1)}, bf16[256,1152]{1,0:T(8,128)(2,1)S(1)}, bf16[256,1152]{1,0:T(8,128)(2,1)S(1)}) custom-call(bf16[32,1152]{1,0:T(8,128)(2,1)S(1)} %slice_bitcast_fusion.refs_0_, bf16[96,1152]{1,0:T(8,128)(2,1)S(1)} %pad_maximum_fusion.1.refs_1_, ...), custom_call_target="tpu_custom_call" | custom-call | tf_op jit(solution)/shard_map/attention_and_next_keys/pallas_call | solution.py:307
  36.3 2.1 %tile_attention_over_own_keys.1 = (bf16[48,1152]{1,0:T(8,128)(2,1)S(1)}, bf16[48,640]{1,0:T(8,128)(2,1)S(1)}, f32[48,640]{1,0:T(8,128)S(1)}, f32[48,128]{1,0:T(8,128)S(1)}) custom-call(bf16[256,1152]{1,0:T(8,128)(2,1)S(1)} %get-tuple-element.75.x_ref, bf16[256,1152]{1,0:T(8,128)(2,1)S(1)} %get-tuple-element.76.mod_ref, ...), custom_call_target="tpu_custom_call" | custom-call | tf_op jit(solution)/shard_map/tile_attention_over_own_keys/pallas_call | solution.py:250
  38.4 2.5 %tile_attention_and_patches.1.patch_ref = f32[48,128]{1,0:T(8,128)S(1)} custom-call(bf16[48,1152]{1,0:T(8,128)(2,1)S(1)} %get-tuple-element.79.x_ref, bf16[48,640]{1,0:T(8,128)(2,1)S(1)} %get-tuple-element.80.q_ref, f32[48,640]{1,0:T(8,128)S(1)} %get-tuple-element.81.sum_ref, f32[48,128]{1,0:T(8,128)S(1)} %get-tuple-element.82.state_ref, ...), custom_call_target="tpu_custom_call" | custom-call | tf_op jit(solution)/shard_map/tile_attention_and_patches/pallas_call | solution.py:334
  41.0 0.5 %collective-permute-start.16 = (f32[48,128]{1,0:T(8,128)S(1)}, f32[48,128]{1,0:T(8,128)S(1)}, u32[]{:S(2)}, u32[]{:S(2)}) collective-permute-start(f32[48,128]{1,0:T(8,128)S(1)} %tile_attention_and_patches.1.patch_ref), channel_id=1, source_target_pairs={{0,8},{8,0},{1,9},{9,1},{2,10},{10,2},{3,11},{11,3},{4,12},{12,4},... | collective-permute-start | bytes 73736 | tf_op jit(solution)/shard_map/ppermute | solution.py:552
  41.9 0.4 collective-permute-done.16.got_ref
  42.4 2.7 %decoder_convolutions.1 = bf16[4,128,512]{2,1,0:T(8,128)(2,1)} custom-call(f32[48,128]{1,0:T(8,128)S(1)} %tile_attention_and_patches.1.patch_ref, f32[48,128]{1,0:T(8,128)S(1)} %collective-permute-done.16.got_ref, s32[48,128]{1,0:T(8,128)S(1)} %broadcast_in_dim.14.idx_ref, bf16[1024,512]{1,0:T(8,128)(2,1)S(1)} %fusion.wp_ref, f32[1,512]{1,0:T(1,128)S(1)} %bitcast.31, ...), custom_call_target="tpu_custom_call" | custom-call | tf_op jit(solution)/shard_map/decoder_convolutions/pallas_call | solution.py:433
  (47 shorter events, 3.1 us)
Async XLA Ops:
  0.0 10.0 %copy-start = (f32[100,5,1152]{2,0,1:T(8,128)S(1)}, f32[100,5,1152]{2,0,1:T(8,128)}, u32[]{:S(2)}) copy-start(f32[100,5,1152]{2,0,1:T(8,128)} %param.19) | copy-start | bytes 6912004
  1.0 12.5 %collective-permute-start = (bf16[32,1152]{1,0:T(8,128)(2,1)S(1)}, bf16[32,1152]{1,0:T(8,128)(2,1)S(1)}, u32[]{:S(2)}, u32[]{:S(2)}) collective-permute-start(bf16[32,1152]{1,0:T(8,128)(2,1)S(1)} %dynamic-slice_bitcast_fusion), channel_id=1, source_target_pairs={{2,0},{3,1},{0,2},{1,3},{6,4},{7,5},{4,6},{5,7},{10,8},{11,9},{8,1... | collective-permute-start | bytes 221192 | tf_op jit(solution)/shard_map/ppermute | solution.py:469
  4.1 9.5 %collective-permute-start.1 = (bf16[32,1152]{1,0:T(8,128)(2,1)S(1)}, bf16[32,1152]{1,0:T(8,128)(2,1)S(1)}, u32[]{:S(2)}, u32[]{:S(2)}) collective-permute-start(bf16[32,1152]{1,0:T(8,128)(2,1)S(1)} %dynamic-slice_bitcast_fusion), channel_id=1, source_target_pairs={{4,0},{5,1},{6,2},{7,3},{0,4},{1,5},{2,6},{3,7},{12,8},{13,9},{14,... | collective-permute-start | bytes 221192 | tf_op jit(solution)/shard_map/ppermute | solution.py:469
  6.7 6.9 %collective-permute-start.2 = (bf16[32,1152]{1,0:T(8,128)(2,1)S(1)}, bf16[32,1152]{1,0:T(8,128)(2,1)S(1)}, u32[]{:S(2)}, u32[]{:S(2)}) collective-permute-start(bf16[32,1152]{1,0:T(8,128)(2,1)S(1)} %dynamic-slice_bitcast_fusion), channel_id=1, source_target_pairs={{6,0},{7,1},{4,2},{5,3},{2,4},{3,5},{0,6},{1,7},{14,8},{15,9},{12,... | collective-permute-start | bytes 221192 | tf_op jit(solution)/shard_map/ppermute | solution.py:469
  7.6 6.0 %collective-permute-start.3 = (bf16[32,1152]{1,0:T(8,128)(2,1)S(1)}, bf16[32,1152]{1,0:T(8,128)(2,1)S(1)}, u32[]{:S(2)}, u32[]{:S(2)}) collective-permute-start(bf16[32,1152]{1,0:T(8,128)(2,1)S(1)} %slice_bitcast_fusion.refs_0_), channel_id=1, source_target_pairs={{1,0},{0,1},{3,2},{2,3},{5,4},{4,5},{7,6},{6,7},{9,8},{8,9},{11,10... | collective-permute-start | bytes 221192 | tf_op jit(solution)/shard_map/ppermute | solution.py:469
  9.3 4.3 %collective-permute-start.4 = (bf16[1,576,1152]{2,1,0:T(8,128)(2,1)}, bf16[1,576,1152]{2,1,0:T(8,128)(2,1)}, u32[]{:S(2)}, u32[]{:S(2)}) collective-permute-start(bf16[1,576,1152]{2,1,0:T(8,128)(2,1)} %wo_own.1), channel_id=1, source_target_pairs={{0,8},{8,0},{1,9},{9,1},{2,10},{10,2},{3,11},{11,3},{4,12},{12,4},... | collective-permute-start | bytes 3981320 | tf_op jit(solution)/shard_map/ppermute | solution.py:503
  13.7 7.1 %collective-permute-start.9 = (bf16[1,1728,1152]{2,1,0:T(8,128)(2,1)}, bf16[1,1728,1152]{2,1,0:T(8,128)(2,1)S(1)}, u32[]{:S(2)}, u32[]{:S(2)}) collective-permute-start(bf16[1,1728,1152]{2,1,0:T(8,128)(2,1)} %bitcast.33), channel_id=1, source_target_pairs={{0,8},{8,0},{1,9},{9,1},{2,10},{10,2},{3,11},{11,3},{4,12},{12,4},... | collective-permute-start | bytes 11943944 | tf_op jit(solution)/shard_map/ppermute | solution.py:533
  14.0 11.0 %collective-permute-start.5 = (bf16[128,1152]{1,0:T(8,128)(2,1)S(1)}, bf16[128,1152]{1,0:T(8,128)(2,1)S(1)}, u32[]{:S(2)}, u32[]{:S(2)}) collective-permute-start(bf16[128,1152]{1,0:T(8,128)(2,1)S(1)} %pad_maximum_fusion.refs_0_), channel_id=1, source_target_pairs={{1,0},{0,1},{3,2},{2,3},{5,4},{4,5},{7,6},{6,7},{9,8},{8,9},{11,10... | collective-permute-start | bytes 884744 | tf_op jit(solution)/shard_map/ppermute | solution.py:469
  14.6 9.2 %collective-permute-start.6 = (bf16[32,1152]{1,0:T(8,128)(2,1)S(1)}, bf16[32,1152]{1,0:T(8,128)(2,1)S(1)}, u32[]{:S(2)}, u32[]{:S(2)}) collective-permute-start(bf16[32,1152]{1,0:T(8,128)(2,1)S(1)} %slice_bitcast_fusion.refs_0_), channel_id=1, source_target_pairs={{2,0},{3,1},{0,2},{1,3},{6,4},{7,5},{4,6},{5,7},{10,8},{11,9},{8,1... | collective-permute-start | bytes 221192 | tf_op jit(solution)/shard_map/ppermute | solution.py:469
  15.7 8.2 %collective-permute-start.7 = (bf16[32,1152]{1,0:T(8,128)(2,1)S(1)}, bf16[32,1152]{1,0:T(8,128)(2,1)S(1)}, u32[]{:S(2)}, u32[]{:S(2)}) collective-permute-start(bf16[32,1152]{1,0:T(8,128)(2,1)S(1)} %slice_bitcast_fusion.refs_0_), channel_id=1, source_target_pairs={{4,0},{5,1},{6,2},{7,3},{0,4},{1,5},{2,6},{3,7},{12,8},{13,9},{14,... | collective-permute-start | bytes 221192 | tf_op jit(solution)/shard_map/ppermute | solution.py:469
  18.8 6.3 %collective-permute-start.8 = (bf16[32,1152]{1,0:T(8,128)(2,1)S(1)}, bf16[32,1152]{1,0:T(8,128)(2,1)S(1)}, u32[]{:S(2)}, u32[]{:S(2)}) collective-permute-start(bf16[32,1152]{1,0:T(8,128)(2,1)S(1)} %slice_bitcast_fusion.refs_0_), channel_id=1, source_target_pairs={{6,0},{7,1},{4,2},{5,3},{2,4},{3,5},{0,6},{1,7},{14,8},{15,9},{12,... | collective-permute-start | bytes 221192 | tf_op jit(solution)/shard_map/ppermute | solution.py:469
  25.1 6.8 %collective-permute-start.10 = (bf16[96,1152]{1,0:T(8,128)(2,1)S(1)}, bf16[96,1152]{1,0:T(8,128)(2,1)S(1)}, u32[]{:S(2)}, u32[]{:S(2)}) collective-permute-start(bf16[96,1152]{1,0:T(8,128)(2,1)S(1)} %pad_maximum_fusion.1.refs_1_), channel_id=1, source_target_pairs={{1,0},{0,1},{3,2},{2,3},{5,4},{4,5},{7,6},{6,7},{9,8},{8,9},{11,10... | collective-permute-start | bytes 663560 | tf_op jit(solution)/shard_map/ppermute | solution.py:469
  28.5 1.4 %collective-permute-start.11 = (bf16[64,1152]{1,0:T(8,128)(2,1)S(1)}, bf16[64,1152]{1,0:T(8,128)(2,1)S(1)}, u32[]{:S(2)}, u32[]{:S(2)}) collective-permute-start(bf16[64,1152]{1,0:T(8,128)(2,1)S(1)} %get-tuple-element.66), channel_id=1, source_target_pairs={{0,8},{8,0},{1,9},{9,1},{2,10},{10,2},{3,11},{11,3},{4,12},{12,4},... | collective-permute-start | bytes 442376 | tf_op jit(solution)/shard_map/ppermute | solution.py:542
  28.6 1.6 %collective-permute-start.12 = (bf16[64,1152]{1,0:T(8,128)(2,1)S(1)}, bf16[64,1152]{1,0:T(8,128)(2,1)S(1)}, u32[]{:S(2)}, u32[]{:S(2)}) collective-permute-start(bf16[64,1152]{1,0:T(8,128)(2,1)S(1)} %get-tuple-element.67), channel_id=1, source_target_pairs={{0,8},{8,0},{1,9},{9,1},{2,10},{10,2},{3,11},{11,3},{4,12},{12,4},... | collective-permute-start | bytes 442376 | tf_op jit(solution)/shard_map/ppermute | solution.py:542
  29.1 1.4 %collective-permute-start.13 = (bf16[64,1152]{1,0:T(8,128)(2,1)S(1)}, bf16[64,1152]{1,0:T(8,128)(2,1)S(1)}, u32[]{:S(2)}, u32[]{:S(2)}) collective-permute-start(bf16[64,1152]{1,0:T(8,128)(2,1)S(1)} %get-tuple-element.68), channel_id=1, source_target_pairs={{0,8},{8,0},{1,9},{9,1},{2,10},{10,2},{3,11},{11,3},{4,12},{12,4},... | collective-permute-start | bytes 442376 | tf_op jit(solution)/shard_map/ppermute | solution.py:542
  29.2 1.5 %collective-permute-start.14 = (bf16[64,1152]{1,0:T(8,128)(2,1)S(1)}, bf16[64,1152]{1,0:T(8,128)(2,1)S(1)}, u32[]{:S(2)}, u32[]{:S(2)}) collective-permute-start(bf16[64,1152]{1,0:T(8,128)(2,1)S(1)} %get-tuple-element.69), channel_id=1, source_target_pairs={{0,8},{8,0},{1,9},{9,1},{2,10},{10,2},{3,11},{11,3},{4,12},{12,4},... | collective-permute-start | bytes 442376 | tf_op jit(solution)/shard_map/ppermute | solution.py:542
  36.2 2.3 %collective-permute-start.15 = (bf16[256,1152]{1,0:T(8,128)(2,1)S(1)}, bf16[256,1152]{1,0:T(8,128)(2,1)S(1)}, u32[]{:S(2)}, u32[]{:S(2)}) collective-permute-start(bf16[256,1152]{1,0:T(8,128)(2,1)S(1)} %get-tuple-element.83), channel_id=1, source_target_pairs={{0,8},{8,0},{1,9},{9,1},{2,10},{10,2},{3,11},{11,3},{4,12},{12,4},... | collective-permute-start | bytes 1769480 | tf_op jit(solution)/shard_map/ppermute | solution.py:544
  36.2 6.1 %slice-start = ((s8[4718592]{0:T(1024)(128)(4,1)}), s8[4194304]{0:T(1024)(128)(4,1)S(1)}, s32[]{:S(2)}) async-start(s8[4718592]{0:T(1024)(128)(4,1)} %bitcast.28), calls=%async_computation | async-start | bytes 8388608
  36.3 6.1 %slice-start.1 = ((s8[4718592]{0:T(1024)(128)(4,1)}), s8[524288]{0:T(1024)(128)(4,1)S(1)}, s32[]{:S(2)}) async-start(s8[4718592]{0:T(1024)(128)(4,1)} %bitcast.28), calls=%async_computation.1 | async-start | bytes 1048576
  38.4 3.2 %copy-start.4 = (bf16[1024,36]{1,0:T(8,128)(2,1)S(1)}, bf16[1024,36]{1,0:T(8,128)(2,1)}, u32[]{:S(2)}) copy-start(bf16[1024,36]{1,0:T(8,128)(2,1)} %constant.114.clone) | copy-start | bytes 221188
  38.4 3.1 %copy-start.5 = (bf16[36,512]{1,0:T(8,128)(2,1)S(1)}, bf16[36,512]{1,0:T(8,128)(2,1)}, u32[]{:S(2)}) copy-start(bf16[36,512]{1,0:T(8,128)(2,1)} %param.22) | copy-start | bytes 110596
  38.4 4.0 %copy-start.2 = (f32[512]{0:T(512)S(1)}, f32[512]{0:T(512)}, u32[]{:S(2)}) copy-start(f32[512]{0:T(512)} %param.23) | copy-start | bytes 6148
  38.4 4.0 %copy-start.3 = (f32[512]{0:T(512)S(1)}, f32[512]{0:T(512)}, u32[]{:S(2)}) copy-start(f32[512]{0:T(512)} %param.25) | copy-start | bytes 6148
  41.0 1.4 %collective-permute-start.16 = (f32[48,128]{1,0:T(8,128)S(1)}, f32[48,128]{1,0:T(8,128)S(1)}, u32[]{:S(2)}, u32[]{:S(2)}) collective-permute-start(f32[48,128]{1,0:T(8,128)S(1)} %tile_attention_and_patches.1.patch_ref), channel_id=1, source_target_pairs={{0,8},{8,0},{1,9},{9,1},{2,10},{10,2},{3,11},{11,3},{4,12},{12,4},... | collective-permute-start | bytes 73736 | tf_op jit(solution)/shard_map/ppermute | solution.py:552
  (1 other events, 2.2 us)

commit v20 on v18

--- a/solution.py
+++ b/solution.py
@@ -469,6 +469,10 @@
     return lax.ppermute(block, "patch", [(i ^ (k_outer * inner + k_inner), i) for i in range(n)])
 
 
+def across_outer(block, outer):
+    return [swapped(block, k, 0) for k in range(outer - 1, 0, -1)]
+
+
 def local(
     tokens,
     stale_kv,
@@ -499,7 +503,7 @@
     w_qkv = jnp.swapaxes(w_qkv, 1, 2)
     w_qkv_other = lax.ppermute(w_qkv, "pipe", swap)
     tables = lax.all_gather(block_table[0], "pipe")
-    x_column = [swapped(own_tokens, k, 0) for k in range(1, outer)]
+    x_column = across_outer(own_tokens, outer)
     own_stale = stale_kv[0, 1]
     w_out_other = lax.ppermute(w_out, "pipe", swap)
 
@@ -522,7 +526,7 @@
     source = token // own_count
     k_outer = (source // inner) ^ (tile // inner)
     k_inner = (source % inner) ^ (tile % inner)
-    spot = (k_inner * outer + k_outer) * own_count + token % own_count
+    spot = (k_inner * outer + -k_outer % outer) * own_count + token % own_count
     idx = jnp.broadcast_to(jnp.where(inside, spot, -1)[:, None], (padded_rows, LANES)).astype(jnp.int32)
 
     x_column, w_qkv_other, w_out_other, vecs, idx, own_stale, w_in = lax.optimization_barrier(
@@ -531,7 +535,7 @@
     x_column = jnp.concatenate([own_tokens] + x_column, axis=0)
     x_column, own_stale = lax.optimization_barrier((x_column, own_stale))
     x_pieces = [x_column] + [swapped(x_column, 0, k) for k in range(1, inner)]
-    stale_column = [swapped(own_stale, k, 0) for k in range(1, outer)]
+    stale_column = across_outer(own_stale, outer)
     stale_line = [swapped(own_stale, 0, k) for k in range(1, inner)]
     w_0, w_1, wo_0, wo_1 = weights_in_vmem(w_qkv, w_qkv_other, w_out, w_out_other)
     x_pieces, stale_column, stale_line, w_0 = lax.optimization_barrier((x_pieces, stale_column, stale_line, w_0))

time: 43.9 us -> 44.4 us (1.011)
  no operation moved by 1% of the time
where the time goes in v20:
time: 44.4 us; the launch traced here: 44.1 us
  Pallas kernels  17.6 us (40%)
  starting transfers between devices  15.1 us (34%)
  waiting for transfers between devices  4.4 us (10%)
  local copies, waits for them, and re-layouts  2.89 us (7%)
  blocking collectives  1.99 us (4%)
  between operations  0.9 us (2%)
  other arithmetic  0.84 us (2%)
    ppermute x9, starting transfers between devices, swapped(): lax.ppermute(block, 'patch', [(i ^ k_outer * inner + k_inner, i) for i in...  13 us
    pallas_call x1, Pallas kernels, first_block(): pl.pallas_call(functools.partial(block_kernel, len(stale_pieces), len(got...  4.3 us
    pallas_call x1, Pallas kernels, weights_in_vmem(): pl.pallas_call(weights_kernel, out_shape=(jax.ShapeDtypeStruct((3 * DA, D...  4.08 us
    ppermute x9, waiting for transfers between devices, swapped(): lax.ppermute(block, 'patch', [(i ^ k_outer * inner + k_inner, i) for i in...  2.89 us
    pallas_call x1, Pallas kernels, decode(): pl.pallas_call(functools.partial(decode_kernel, rows, cols, pitch), out_s...  2.7 us
    pallas_call x1, Pallas kernels, tile_block(): pl.pallas_call(tile_kernel, out_shape=jax.ShapeDtypeStruct((x.shape[0], L...  2.54 us
    pallas_call x1, Pallas kernels, attend_fresh(): pl.pallas_call(fresh_kernel, out_shape=(jax.ShapeDtypeStruct((rows, D), B...  2.08 us
    all_gather x1, blocking collectives, local(): tables = lax.all_gather(block_table[0], 'pipe')  1.99 us
  transfers between devices with their start and end apart: 17, of which 8 were waited for; matrix products, arithmetic and copies ran while one was open for 9% of the time, Pallas kernels for 18%

profile of v20, /device:TPU:0, one launch (start us, length us, event | category | flops | bytes accessed | tf_op | source)
XLA Modules:
  0.0 44.1 jit_solution(6346829838660318993)
XLA Ops:
  0.0 0.5 %collective-permute-start.3 = (bf16[1,1728,1152]{2,1,0:T(8,128)(2,1)}, bf16[1,1728,1152]{2,1,0:T(8,128)(2,1)}, u32[]{:S(2)}, u32[]{:S(2)}) collective-permute-start(bf16[1,1728,1152]{2,1,0:T(8,128)(2,1)} %bitcast.33), channel_id=1, source_target_pairs={{0,8},{8,0},{1,9},{9,1},{2,10},{10,2},{3,11},{11,3},{4,12},{12,4},... | collective-permute-start | bytes 11943944 | tf_op jit(solution)/shard_map/ppermute | solution.py:504
  0.5 1.1 %dynamic-slice_bitcast_fusion = bf16[32,1152]{1,0:T(8,128)(2,1)S(1)} fusion(bf16[2,32,1152]{2,1,0:T(8,128)(2,1)} %param.14, s32[]{:T(128)S(6)} %select_n.88), kind=kLoop, calls=%fused_computation.5 | loop fusion | bytes 147460 | tf_op jit(solution)/shard_map/jit(dynamic_index_in_dim)/squeeze | solution.py:502
  1.6 4.6 %collective-permute-start = (bf16[32,1152]{1,0:T(8,128)(2,1)S(1)}, bf16[32,1152]{1,0:T(8,128)(2,1)S(1)}, u32[]{:S(2)}, u32[]{:S(2)}) collective-permute-start(bf16[32,1152]{1,0:T(8,128)(2,1)S(1)} %dynamic-slice_bitcast_fusion), channel_id=1, source_target_pairs={{6,0},{7,1},{4,2},{5,3},{2,4},{3,5},{0,6},{1,7},{14,8},{15,9},{12,... | collective-permute-start | bytes 221192 | tf_op jit(solution)/shard_map/ppermute | solution.py:469
  6.1 0.6 %collective-permute-start.2 = (bf16[32,1152]{1,0:T(8,128)(2,1)S(1)}, bf16[32,1152]{1,0:T(8,128)(2,1)S(1)}, u32[]{:S(2)}, u32[]{:S(2)}) collective-permute-start(bf16[32,1152]{1,0:T(8,128)(2,1)S(1)} %dynamic-slice_bitcast_fusion), channel_id=1, source_target_pairs={{2,0},{3,1},{0,2},{1,3},{6,4},{7,5},{4,6},{5,7},{10,8},{11,9},{8,1... | collective-permute-start | bytes 221192 | tf_op jit(solution)/shard_map/ppermute | solution.py:469
  7.5 0.7 %copy.19 = f32[1,3,1152]{2,1,0:T(4,128)S(1)} copy(f32[1,3,1152]{2,0,1:T(1,128)} %param.18) | data formatting | bytes 27648 | tf_op args[4]
  8.2 2.0 %all_gather.3 = f32[2,3,1152]{2,1,0:T(4,128)S(1)} all-gather(f32[1,3,1152]{2,1,0:T(4,128)S(1)} %copy.19), channel_id=1, replica_groups=mesh['grp'=2,'pipe'=2,'patch'=8] {'pipe'}, dimensions={0}, use_global_device_ids=true | all-gather | bytes 41472 | tf_op jit(solution)/shard_map/all_gather | solution.py:505
  10.2 0.7 %fusion.2 = (f32[3,1152]{1,0:T(4,128)S(1)}, f32[3,1152]{1,0:T(4,128)S(1)}) fusion(f32[1,3,1152]{2,0,1:T(1,128)S(1)} %constant_dynamic-slice_fusion, f32[2,3,1152]{2,1,0:T(4,128)S(1)} %all_gather.3, f32[3]{0:T(128)} %constant.130), kind=kLoop, calls=%fused_computation.10 | loop fusion | flops 13824 | bytes 69132 | tf_op jit(solution)/shard_map/add | solution.py:514
  11.0 0.9 %slice_bitcast_fusion.refs_0_ = bf16[32,1152]{1,0:T(8,128)(2,1)S(1)} fusion(bf16[1,2,32,1152]{3,2,1,0:T(8,128)(2,1)} %param.15), kind=kLoop, calls=%fused_computation.4 | loop fusion | bytes 147456 | tf_op jit(solution)/shard_map/squeeze | solution.py:507
  11.9 0.9 %collective-permute-done.1 = bf16[32,1152]{1,0:T(8,128)(2,1)S(1)} collective-permute-done((bf16[32,1152]{1,0:T(8,128)(2,1)S(1)}, bf16[32,1152]{1,0:T(8,128)(2,1)S(1)}, u32[]{:S(2)}, u32[]{:S(2)}) %collective-permute-start.1) | collective-permute-done | bytes 73760 | tf_op jit(solution)/shard_map/ppermute | solution.py:469
  12.9 1.6 %collective-permute-start.5 = (bf16[128,1152]{1,0:T(8,128)(2,1)S(1)}, bf16[128,1152]{1,0:T(8,128)(2,1)S(1)}, u32[]{:S(2)}, u32[]{:S(2)}) collective-permute-start(bf16[128,1152]{1,0:T(8,128)(2,1)S(1)} %pad_maximum_fusion.refs_0_), channel_id=1, source_target_pairs={{1,0},{0,1},{3,2},{2,3},{5,4},{4,5},{7,6},{6,7},{9,8},{8,9},{11,10... | collective-permute-start | bytes 884744 | tf_op jit(solution)/shard_map/ppermute | solution.py:469
  14.5 2.9 %collective-permute-start.6 = (bf16[32,1152]{1,0:T(8,128)(2,1)S(1)}, bf16[32,1152]{1,0:T(8,128)(2,1)S(1)}, u32[]{:S(2)}, u32[]{:S(2)}) collective-permute-start(bf16[32,1152]{1,0:T(8,128)(2,1)S(1)} %slice_bitcast_fusion.refs_0_), channel_id=1, source_target_pairs={{6,0},{7,1},{4,2},{5,3},{2,4},{3,5},{0,6},{1,7},{14,8},{15,9},{12,... | collective-permute-start | bytes 221192 | tf_op jit(solution)/shard_map/ppermute | solution.py:469
  17.4 1.5 %collective-permute-start.8 = (bf16[32,1152]{1,0:T(8,128)(2,1)S(1)}, bf16[32,1152]{1,0:T(8,128)(2,1)S(1)}, u32[]{:S(2)}, u32[]{:S(2)}) collective-permute-start(bf16[32,1152]{1,0:T(8,128)(2,1)S(1)} %slice_bitcast_fusion.refs_0_), channel_id=1, source_target_pairs={{2,0},{3,1},{0,2},{1,3},{6,4},{7,5},{4,6},{5,7},{10,8},{11,9},{8,1... | collective-permute-start | bytes 221192 | tf_op jit(solution)/shard_map/ppermute | solution.py:469
  18.9 0.5 %collective-permute-start.9 = (bf16[32,1152]{1,0:T(8,128)(2,1)S(1)}, bf16[32,1152]{1,0:T(8,128)(2,1)S(1)}, u32[]{:S(2)}, u32[]{:S(2)}) collective-permute-start(bf16[32,1152]{1,0:T(8,128)(2,1)S(1)} %slice_bitcast_fusion.refs_0_), channel_id=1, source_target_pairs={{1,0},{0,1},{3,2},{2,3},{5,4},{4,5},{7,6},{6,7},{9,8},{8,9},{11,10... | collective-permute-start | bytes 221192 | tf_op jit(solution)/shard_map/ppermute | solution.py:469
  19.4 4.1 %weights_by_block.1 = (bf16[1728,1152]{1,0:T(8,128)(2,1)S(1)}, bf16[1728,1152]{1,0:T(8,128)(2,1)S(1)}, bf16[640,1152]{1,0:T(8,128)(2,1)S(1)}, bf16[640,1152]{1,0:T(8,128)(2,1)S(1)}) custom-call(bf16[1,1728,1152]{2,1,0:T(8,128)(2,1)} %bitcast.34, bf16[1,1728,1152]{2,1,0:T(8,128)(2,1)} %collective-permute-done.3.other_ref, bf16[1,576,1152]{2,1,0:T(8,128)(2,1)} %wo_own.1, ...), custom_call_target="tpu_custom_call" | custom-call | tf_op jit(solution)/shard_map/weights_by_block/pallas_call | solution.py:163
  23.9 1.3 %collective-permute-start.10 = (bf16[96,1152]{1,0:T(8,128)(2,1)S(1)}, bf16[96,1152]{1,0:T(8,128)(2,1)S(1)}, u32[]{:S(2)}, u32[]{:S(2)}) collective-permute-start(bf16[96,1152]{1,0:T(8,128)(2,1)S(1)} %pad_maximum_fusion.1.refs_1_), channel_id=1, source_target_pairs={{1,0},{0,1},{3,2},{2,3},{5,4},{4,5},{7,6},{6,7},{9,8},{8,9},{11,10... | collective-permute-start | bytes 663560 | tf_op jit(solution)/shard_map/ppermute | solution.py:469
  25.2 1.9 %layer_norm_and_projections.1 = (bf16[256,1152]{1,0:T(8,128)(2,1)S(1)}, bf16[256,640]{1,0:T(8,128)(2,1)S(1)}, bf16[256,1152]{1,0:T(8,128)(2,1)S(1)}, bf16[64,115...) custom-call(bf16[128,1152]{1,0:T(8,128)(2,1)S(1)} %pad_maximum_fusio, ...), custom_call_target="tpu_custom_call" | custom-call | tf_op jit(solution)/shard_map/layer_norm_and_projections/pallas_call | solution.py:211
  27.1 0.5 %collective-permute-start.12 = (bf16[64,1152]{1,0:T(8,128)(2,1)S(1)}, bf16[64,1152]{1,0:T(8,128)(2,1)S(1)}, u32[]{:S(2)}, u32[]{:S(2)}) collective-permute-start(bf16[64,1152]{1,0:T(8,128)(2,1)S(1)} %get-tuple-element.68), channel_id=1, source_target_pairs={{0,8},{8,0},{1,9},{9,1},{2,10},{10,2},{3,11},{11,3},{4,12},{12,4},... | collective-permute-start | bytes 442376 | tf_op jit(solution)/shard_map/ppermute | solution.py:546
  29.2 1.6 %collective-permute-done.10.refs_3_ = bf16[96,1152]{1,0:T(8,128)(2,1)S(1)} collective-permute-done((bf16[96,1152]{1,0:T(8,128)(2,1)S(1)}, bf16[96,1152]{1,0:T(8,128)(2,1)S(1)}, u32[]{:S(2)}, u32[]{:S(2)}) %collective-permute-start.10) | collective-permute-done | bytes 221216 | tf_op jit(solution)/shard_map/ppermute | solution.py:469
  30.9 4.3 %attention_and_next_keys.1 = (bf16[256,1152]{1,0:T(8,128)(2,1)S(1)}, bf16[256,1152]{1,0:T(8,128)(2,1)S(1)}, bf16[256,1152]{1,0:T(8,128)(2,1)S(1)}, bf16[256,1152]{1,0:T(8,128)(2,1)S(1)}) custom-call(bf16[32,1152]{1,0:T(8,128)(2,1)S(1)} %slice_bitcast_fusion.refs_0_, bf16[96,1152]{1,0:T(8,128)(2,1)S(1)} %pad_maximum_fusion.1.refs_1_, ...), custom_call_target="tpu_custom_call" | custom-call | tf_op jit(solution)/shard_map/attention_and_next_keys/pallas_call | solution.py:307
  35.3 2.1 %tile_attention_over_own_keys.1 = (bf16[48,1152]{1,0:T(8,128)(2,1)S(1)}, bf16[48,640]{1,0:T(8,128)(2,1)S(1)}, f32[48,640]{1,0:T(8,128)S(1)}, f32[48,128]{1,0:T(8,128)S(1)}) custom-call(bf16[256,1152]{1,0:T(8,128)(2,1)S(1)} %get-tuple-element.76.x_ref, bf16[256,1152]{1,0:T(8,128)(2,1)S(1)} %get-tuple-element.77.mod_ref, ...), custom_call_target="tpu_custom_call" | custom-call | tf_op jit(solution)/shard_map/tile_attention_over_own_keys/pallas_call | solution.py:250
  37.5 2.5 %tile_attention_and_patches.1.patch_ref = f32[48,128]{1,0:T(8,128)S(1)} custom-call(bf16[48,1152]{1,0:T(8,128)(2,1)S(1)} %get-tuple-element.80.x_ref, bf16[48,640]{1,0:T(8,128)(2,1)S(1)} %get-tuple-element.81.q_ref, f32[48,640]{1,0:T(8,128)S(1)} %get-tuple-element.82.sum_ref, f32[48,128]{1,0:T(8,128)S(1)} %get-tuple-element.83.state_ref, ...), custom_call_target="tpu_custom_call" | custom-call | tf_op jit(solution)/shard_map/tile_attention_and_patches/pallas_call | solution.py:334
  40.0 0.5 %collective-permute-start.16 = (f32[48,128]{1,0:T(8,128)S(1)}, f32[48,128]{1,0:T(8,128)S(1)}, u32[]{:S(2)}, u32[]{:S(2)}) collective-permute-start(f32[48,128]{1,0:T(8,128)S(1)} %tile_attention_and_patches.1.patch_ref), channel_id=1, source_target_pairs={{0,8},{8,0},{1,9},{9,1},{2,10},{10,2},{3,11},{11,3},{4,12},{12,4},... | collective-permute-start | bytes 73736 | tf_op jit(solution)/shard_map/ppermute | solution.py:556
  40.9 0.4 collective-permute-done.16.got_ref
  41.4 2.7 %decoder_convolutions.1 = bf16[4,128,512]{2,1,0:T(8,128)(2,1)} custom-call(f32[48,128]{1,0:T(8,128)S(1)} %tile_attention_and_patches.1.patch_ref, f32[48,128]{1,0:T(8,128)S(1)} %collective-permute-done.16.got_ref, s32[48,128]{1,0:T(8,128)S(1)} %broadcast_in_dim.14.idx_ref, bf16[1024,512]{1,0:T(8,128)(2,1)S(1)} %fusion.wp_ref, f32[1,512]{1,0:T(1,128)S(1)} %bitcast.31, ...), custom_call_target="tpu_custom_call" | custom-call | tf_op jit(solution)/shard_map/decoder_convolutions/pallas_call | solution.py:433
  (47 shorter events, 2.8 us)
Async XLA Ops:
  0.0 7.4 %copy-start = (f32[100,5,1152]{2,0,1:T(8,128)S(1)}, f32[100,5,1152]{2,0,1:T(8,128)}, u32[]{:S(2)}) copy-start(f32[100,5,1152]{2,0,1:T(8,128)} %param.19) | copy-start | bytes 6912004
  0.0 12.8 %collective-permute-start.3 = (bf16[1,1728,1152]{2,1,0:T(8,128)(2,1)}, bf16[1,1728,1152]{2,1,0:T(8,128)(2,1)}, u32[]{:S(2)}, u32[]{:S(2)}) collective-permute-start(bf16[1,1728,1152]{2,1,0:T(8,128)(2,1)} %bitcast.33), channel_id=1, source_target_pairs={{0,8},{8,0},{1,9},{9,1},{2,10},{10,2},{3,11},{11,3},{4,12},{12,4},... | collective-permute-start | bytes 11943944 | tf_op jit(solution)/shard_map/ppermute | solution.py:504
  1.6 10.3 %collective-permute-start = (bf16[32,1152]{1,0:T(8,128)(2,1)S(1)}, bf16[32,1152]{1,0:T(8,128)(2,1)S(1)}, u32[]{:S(2)}, u32[]{:S(2)}) collective-permute-start(bf16[32,1152]{1,0:T(8,128)(2,1)S(1)} %dynamic-slice_bitcast_fusion), channel_id=1, source_target_pairs={{6,0},{7,1},{4,2},{5,3},{2,4},{3,5},{0,6},{1,7},{14,8},{15,9},{12,... | collective-permute-start | bytes 221192 | tf_op jit(solution)/shard_map/ppermute | solution.py:469
  6.1 6.7 %collective-permute-start.1 = (bf16[32,1152]{1,0:T(8,128)(2,1)S(1)}, bf16[32,1152]{1,0:T(8,128)(2,1)S(1)}, u32[]{:S(2)}, u32[]{:S(2)}) collective-permute-start(bf16[32,1152]{1,0:T(8,128)(2,1)S(1)} %dynamic-slice_bitcast_fusion), channel_id=1, source_target_pairs={{4,0},{5,1},{6,2},{7,3},{0,4},{1,5},{2,6},{3,7},{12,8},{13,9},{14,... | collective-permute-start | bytes 221192 | tf_op jit(solution)/shard_map/ppermute | solution.py:469
  6.1 6.7 %collective-permute-start.2 = (bf16[32,1152]{1,0:T(8,128)(2,1)S(1)}, bf16[32,1152]{1,0:T(8,128)(2,1)S(1)}, u32[]{:S(2)}, u32[]{:S(2)}) collective-permute-start(bf16[32,1152]{1,0:T(8,128)(2,1)S(1)} %dynamic-slice_bitcast_fusion), channel_id=1, source_target_pairs={{2,0},{3,1},{0,2},{1,3},{6,4},{7,5},{4,6},{5,7},{10,8},{11,9},{8,1... | collective-permute-start | bytes 221192 | tf_op jit(solution)/shard_map/ppermute | solution.py:469
  6.8 6.1 %collective-permute-start.4 = (bf16[1,576,1152]{2,1,0:T(8,128)(2,1)}, bf16[1,576,1152]{2,1,0:T(8,128)(2,1)}, u32[]{:S(2)}, u32[]{:S(2)}) collective-permute-start(bf16[1,576,1152]{2,1,0:T(8,128)(2,1)} %wo_own.1), channel_id=1, source_target_pairs={{0,8},{8,0},{1,9},{9,1},{2,10},{10,2},{3,11},{11,3},{4,12},{12,4},... | collective-permute-start | bytes 3981320 | tf_op jit(solution)/shard_map/ppermute | solution.py:508
  12.9 10.9 %collective-permute-start.5 = (bf16[128,1152]{1,0:T(8,128)(2,1)S(1)}, bf16[128,1152]{1,0:T(8,128)(2,1)S(1)}, u32[]{:S(2)}, u32[]{:S(2)}) collective-permute-start(bf16[128,1152]{1,0:T(8,128)(2,1)S(1)} %pad_maximum_fusion.refs_0_), channel_id=1, source_target_pairs={{1,0},{0,1},{3,2},{2,3},{5,4},{4,5},{7,6},{6,7},{9,8},{8,9},{11,10... | collective-permute-start | bytes 884744 | tf_op jit(solution)/shard_map/ppermute | solution.py:469
  14.5 9.0 %collective-permute-start.6 = (bf16[32,1152]{1,0:T(8,128)(2,1)S(1)}, bf16[32,1152]{1,0:T(8,128)(2,1)S(1)}, u32[]{:S(2)}, u32[]{:S(2)}) collective-permute-start(bf16[32,1152]{1,0:T(8,128)(2,1)S(1)} %slice_bitcast_fusion.refs_0_), channel_id=1, source_target_pairs={{6,0},{7,1},{4,2},{5,3},{2,4},{3,5},{0,6},{1,7},{14,8},{15,9},{12,... | collective-permute-start | bytes 221192 | tf_op jit(solution)/shard_map/ppermute | solution.py:469
  17.4 6.4 %collective-permute-start.7 = (bf16[32,1152]{1,0:T(8,128)(2,1)S(1)}, bf16[32,1152]{1,0:T(8,128)(2,1)S(1)}, u32[]{:S(2)}, u32[]{:S(2)}) collective-permute-start(bf16[32,1152]{1,0:T(8,128)(2,1)S(1)} %slice_bitcast_fusion.refs_0_), channel_id=1, source_target_pairs={{4,0},{5,1},{6,2},{7,3},{0,4},{1,5},{2,6},{3,7},{12,8},{13,9},{14,... | collective-permute-start | bytes 221192 | tf_op jit(solution)/shard_map/ppermute | solution.py:469
  17.4 6.4 %collective-permute-start.8 = (bf16[32,1152]{1,0:T(8,128)(2,1)S(1)}, bf16[32,1152]{1,0:T(8,128)(2,1)S(1)}, u32[]{:S(2)}, u32[]{:S(2)}) collective-permute-start(bf16[32,1152]{1,0:T(8,128)(2,1)S(1)} %slice_bitcast_fusion.refs_0_), channel_id=1, source_target_pairs={{2,0},{3,1},{0,2},{1,3},{6,4},{7,5},{4,6},{5,7},{10,8},{11,9},{8,1... | collective-permute-start | bytes 221192 | tf_op jit(solution)/shard_map/ppermute | solution.py:469
  18.9 4.9 %collective-permute-start.9 = (bf16[32,1152]{1,0:T(8,128)(2,1)S(1)}, bf16[32,1152]{1,0:T(8,128)(2,1)S(1)}, u32[]{:S(2)}, u32[]{:S(2)}) collective-permute-start(bf16[32,1152]{1,0:T(8,128)(2,1)S(1)} %slice_bitcast_fusion.refs_0_), channel_id=1, source_target_pairs={{1,0},{0,1},{3,2},{2,3},{5,4},{4,5},{7,6},{6,7},{9,8},{8,9},{11,10... | collective-permute-start | bytes 221192 | tf_op jit(solution)/shard_map/ppermute | solution.py:469
  23.9 7.0 %collective-permute-start.10 = (bf16[96,1152]{1,0:T(8,128)(2,1)S(1)}, bf16[96,1152]{1,0:T(8,128)(2,1)S(1)}, u32[]{:S(2)}, u32[]{:S(2)}) collective-permute-start(bf16[96,1152]{1,0:T(8,128)(2,1)S(1)} %pad_maximum_fusion.1.refs_1_), channel_id=1, source_target_pairs={{1,0},{0,1},{3,2},{2,3},{5,4},{4,5},{7,6},{6,7},{9,8},{8,9},{11,10... | collective-permute-start | bytes 663560 | tf_op jit(solution)/shard_map/ppermute | solution.py:469
  27.1 1.4 %collective-permute-start.11 = (bf16[64,1152]{1,0:T(8,128)(2,1)S(1)}, bf16[64,1152]{1,0:T(8,128)(2,1)S(1)}, u32[]{:S(2)}, u32[]{:S(2)}) collective-permute-start(bf16[64,1152]{1,0:T(8,128)(2,1)S(1)} %get-tuple-element.67), channel_id=1, source_target_pairs={{0,8},{8,0},{1,9},{9,1},{2,10},{10,2},{3,11},{11,3},{4,12},{12,4},... | collective-permute-start | bytes 442376 | tf_op jit(solution)/shard_map/ppermute | solution.py:546
  27.1 1.6 %collective-permute-start.12 = (bf16[64,1152]{1,0:T(8,128)(2,1)S(1)}, bf16[64,1152]{1,0:T(8,128)(2,1)S(1)}, u32[]{:S(2)}, u32[]{:S(2)}) collective-permute-start(bf16[64,1152]{1,0:T(8,128)(2,1)S(1)} %get-tuple-element.68), channel_id=1, source_target_pairs={{0,8},{8,0},{1,9},{9,1},{2,10},{10,2},{3,11},{11,3},{4,12},{12,4},... | collective-permute-start | bytes 442376 | tf_op jit(solution)/shard_map/ppermute | solution.py:546
  27.6 1.4 %collective-permute-start.13 = (bf16[64,1152]{1,0:T(8,128)(2,1)S(1)}, bf16[64,1152]{1,0:T(8,128)(2,1)S(1)}, u32[]{:S(2)}, u32[]{:S(2)}) collective-permute-start(bf16[64,1152]{1,0:T(8,128)(2,1)S(1)} %get-tuple-element.69), channel_id=1, source_target_pairs={{0,8},{8,0},{1,9},{9,1},{2,10},{10,2},{3,11},{11,3},{4,12},{12,4},... | collective-permute-start | bytes 442376 | tf_op jit(solution)/shard_map/ppermute | solution.py:546
  27.7 1.5 %collective-permute-start.14 = (bf16[64,1152]{1,0:T(8,128)(2,1)S(1)}, bf16[64,1152]{1,0:T(8,128)(2,1)S(1)}, u32[]{:S(2)}, u32[]{:S(2)}) collective-permute-start(bf16[64,1152]{1,0:T(8,128)(2,1)S(1)} %get-tuple-element.70), channel_id=1, source_target_pairs={{0,8},{8,0},{1,9},{9,1},{2,10},{10,2},{3,11},{11,3},{4,12},{12,4},... | collective-permute-start | bytes 442376 | tf_op jit(solution)/shard_map/ppermute | solution.py:546
  35.2 2.3 %collective-permute-start.15 = (bf16[256,1152]{1,0:T(8,128)(2,1)S(1)}, bf16[256,1152]{1,0:T(8,128)(2,1)S(1)}, u32[]{:S(2)}, u32[]{:S(2)}) collective-permute-start(bf16[256,1152]{1,0:T(8,128)(2,1)S(1)} %get-tuple-element.84), channel_id=1, source_target_pairs={{0,8},{8,0},{1,9},{9,1},{2,10},{10,2},{3,11},{11,3},{4,12},{12,4},... | collective-permute-start | bytes 1769480 | tf_op jit(solution)/shard_map/ppermute | solution.py:548
  35.3 6.1 %slice-start = ((s8[4718592]{0:T(1024)(128)(4,1)}), s8[4194304]{0:T(1024)(128)(4,1)S(1)}, s32[]{:S(2)}) async-start(s8[4718592]{0:T(1024)(128)(4,1)} %bitcast.28), calls=%async_computation | async-start | bytes 8388608
  35.3 6.1 %slice-start.1 = ((s8[4718592]{0:T(1024)(128)(4,1)}), s8[524288]{0:T(1024)(128)(4,1)S(1)}, s32[]{:S(2)}) async-start(s8[4718592]{0:T(1024)(128)(4,1)} %bitcast.28), calls=%async_computation.1 | async-start | bytes 1048576
  37.4 3.2 %copy-start.4 = (bf16[1024,36]{1,0:T(8,128)(2,1)S(1)}, bf16[1024,36]{1,0:T(8,128)(2,1)}, u32[]{:S(2)}) copy-start(bf16[1024,36]{1,0:T(8,128)(2,1)} %constant.124.clone) | copy-start | bytes 221188
  37.4 3.1 %copy-start.5 = (bf16[36,512]{1,0:T(8,128)(2,1)S(1)}, bf16[36,512]{1,0:T(8,128)(2,1)}, u32[]{:S(2)}) copy-start(bf16[36,512]{1,0:T(8,128)(2,1)} %param.22) | copy-start | bytes 110596
  37.4 4.0 %copy-start.2 = (f32[512]{0:T(512)S(1)}, f32[512]{0:T(512)}, u32[]{:S(2)}) copy-start(f32[512]{0:T(512)} %param.23) | copy-start | bytes 6148
  37.4 4.0 %copy-start.3 = (f32[512]{0:T(512)S(1)}, f32[512]{0:T(512)}, u32[]{:S(2)}) copy-start(f32[512]{0:T(512)} %param.25) | copy-start | bytes 6148
  40.0 1.4 %collective-permute-start.16 = (f32[48,128]{1,0:T(8,128)S(1)}, f32[48,128]{1,0:T(8,128)S(1)}, u32[]{:S(2)}, u32[]{:S(2)}) collective-permute-start(f32[48,128]{1,0:T(8,128)S(1)} %tile_attention_and_patches.1.patch_ref), channel_id=1, source_target_pairs={{0,8},{8,0},{1,9},{9,1},{2,10},{10,2},{3,11},{11,3},{4,12},{12,4},... | collective-permute-start | bytes 73736 | tf_op jit(solution)/shard_map/ppermute | solution.py:556
  (1 other events, 2.2 us)

commit v21 on v18

--- a/solution.py
+++ b/solution.py
@@ -419,7 +419,7 @@
             lanes = slice(c * LANES, (c + 1) * LANES)
             o_ref[row, c, pl.ds(0, across, stride=2), :] = even[:, lanes]
             o_ref[row, c, pl.ds(1, across, stride=2), :] = odd[:, lanes]
-            out_ref[row, :, lanes] = o_ref[row, c].astype(BF16)
+            out_ref[row, :, lanes] = o_ref[row, c, : 2 * across].astype(BF16)
 
 
 RIM = 8
@@ -438,7 +438,7 @@
         scratch_shapes=[
             pltpu.VMEM((2 * rows + 2, CH // LANES, max(2 * pitch + RIM, feature_pitch(cols)), LANES), F32),
             pltpu.VMEM(((2 * rows + 2) * feature_pitch(cols), CH), BF16),
-            pltpu.VMEM((4 * rows, CH // LANES, 4 * cols, LANES), F32),
+            pltpu.VMEM((4 * rows, CH // LANES, 4 * cols + RIM, LANES), F32),
         ],
         compiler_params=params(0),
         name="decoder_convolutions",

time: 43.9 us -> 43.9 us (level)
  no operation moved by 1% of the time
where the time goes in v21:
time: 43.9 us; the launch traced here: 43.6 us
  Pallas kernels  17.6 us (40%)
  starting transfers between devices  14.8 us (34%)
  waiting for transfers between devices  4.2 us (10%)
  local copies, waits for them, and re-layouts  2.89 us (7%)
  blocking collectives  1.99 us (5%)
  between operations  0.9 us (2%)
  other arithmetic  0.84 us (2%)
    ppermute x9, starting transfers between devices, swapped(): lax.ppermute(block, 'patch', [(i ^ k_outer * inner + k_inner, i) for i in...  12.7 us
    pallas_call x1, Pallas kernels, first_block(): pl.pallas_call(functools.partial(block_kernel, len(stale_pieces), len(got...  4.3 us
    pallas_call x1, Pallas kernels, weights_in_vmem(): pl.pallas_call(weights_kernel, out_shape=(jax.ShapeDtypeStruct((3 * DA, D...  4.08 us
    pallas_call x1, Pallas kernels, decode(): pl.pallas_call(functools.partial(decode_kernel, rows, cols, pitch), out_s...  2.7 us
    ppermute x9, waiting for transfers between devices, swapped(): lax.ppermute(block, 'patch', [(i ^ k_outer * inner + k_inner, i) for i in...  2.68 us
    pallas_call x1, Pallas kernels, tile_block(): pl.pallas_call(tile_kernel, out_shape=jax.ShapeDtypeStruct((x.shape[0], L...  2.54 us
    pallas_call x1, Pallas kernels, attend_fresh(): pl.pallas_call(fresh_kernel, out_shape=(jax.ShapeDtypeStruct((rows, D), B...  2.08 us
    all_gather x1, blocking collectives, local(): tables = lax.all_gather(block_table[0], 'pipe')  1.99 us
  transfers between devices with their start and end apart: 17, of which 8 were waited for; matrix products, arithmetic and copies ran while one was open for 9% of the time, Pallas kernels for 18%

profile of v21, /device:TPU:0, one launch (start us, length us, event | category | flops | bytes accessed | tf_op | source)
XLA Modules:
  0.0 43.6 jit_solution(4548606228845700910)
XLA Ops:
  0.5 1.1 %dynamic-slice_bitcast_fusion = bf16[32,1152]{1,0:T(8,128)(2,1)S(1)} fusion(bf16[2,32,1152]{2,1,0:T(8,128)(2,1)} %param.14, s32[]{:T(128)S(6)} %select_n.80), kind=kLoop, calls=%fused_computation.5 | loop fusion | bytes 147460 | tf_op jit(solution)/shard_map/jit(dynamic_index_in_dim)/squeeze | solution.py:498
  1.6 2.5 %collective-permute-start = (bf16[32,1152]{1,0:T(8,128)(2,1)S(1)}, bf16[32,1152]{1,0:T(8,128)(2,1)S(1)}, u32[]{:S(2)}, u32[]{:S(2)}) collective-permute-start(bf16[32,1152]{1,0:T(8,128)(2,1)S(1)} %dynamic-slice_bitcast_fusion), channel_id=1, source_target_pairs={{2,0},{3,1},{0,2},{1,3},{6,4},{7,5},{4,6},{5,7},{10,8},{11,9},{8,1... | collective-permute-start | bytes 221192 | tf_op jit(solution)/shard_map/ppermute | solution.py:469
  4.1 2.6 %collective-permute-start.1 = (bf16[32,1152]{1,0:T(8,128)(2,1)S(1)}, bf16[32,1152]{1,0:T(8,128)(2,1)S(1)}, u32[]{:S(2)}, u32[]{:S(2)}) collective-permute-start(bf16[32,1152]{1,0:T(8,128)(2,1)S(1)} %dynamic-slice_bitcast_fusion), channel_id=1, source_target_pairs={{4,0},{5,1},{6,2},{7,3},{0,4},{1,5},{2,6},{3,7},{12,8},{13,9},{14,... | collective-permute-start | bytes 221192 | tf_op jit(solution)/shard_map/ppermute | solution.py:469
  7.5 0.7 %copy.19 = f32[1,3,1152]{2,1,0:T(4,128)S(1)} copy(f32[1,3,1152]{2,0,1:T(1,128)} %param.18) | data formatting | bytes 27648 | tf_op args[4]
  8.2 2.0 %all_gather.3 = f32[2,3,1152]{2,1,0:T(4,128)S(1)} all-gather(f32[1,3,1152]{2,1,0:T(4,128)S(1)} %copy.19), channel_id=1, replica_groups=mesh['grp'=2,'pipe'=2,'patch'=8] {'pipe'}, dimensions={0}, use_global_device_ids=true | all-gather | bytes 41472 | tf_op jit(solution)/shard_map/all_gather | solution.py:501
  10.2 0.7 %fusion.2 = (f32[3,1152]{1,0:T(4,128)S(1)}, f32[3,1152]{1,0:T(4,128)S(1)}) fusion(f32[1,3,1152]{2,0,1:T(1,128)S(1)} %constant_dynamic-slice_fusion, f32[2,3,1152]{2,1,0:T(4,128)S(1)} %all_gather.3, f32[3]{0:T(128)} %constant.120), kind=kLoop, calls=%fused_computation.10 | loop fusion | flops 13824 | bytes 69132 | tf_op jit(solution)/shard_map/add | solution.py:510
  10.9 0.9 %slice_bitcast_fusion.refs_0_ = bf16[32,1152]{1,0:T(8,128)(2,1)S(1)} fusion(bf16[1,2,32,1152]{3,2,1,0:T(8,128)(2,1)} %param.15), kind=kLoop, calls=%fused_computation.4 | loop fusion | bytes 147456 | tf_op jit(solution)/shard_map/squeeze | solution.py:503
  11.9 1.2 %collective-permute-done.1 = bf16[32,1152]{1,0:T(8,128)(2,1)S(1)} collective-permute-done((bf16[32,1152]{1,0:T(8,128)(2,1)S(1)}, bf16[32,1152]{1,0:T(8,128)(2,1)S(1)}, u32[]{:S(2)}, u32[]{:S(2)}) %collective-permute-start.1) | collective-permute-done | bytes 73760 | tf_op jit(solution)/shard_map/ppermute | solution.py:469
  13.2 1.6 %collective-permute-start.5 = (bf16[128,1152]{1,0:T(8,128)(2,1)S(1)}, bf16[128,1152]{1,0:T(8,128)(2,1)S(1)}, u32[]{:S(2)}, u32[]{:S(2)}) collective-permute-start(bf16[128,1152]{1,0:T(8,128)(2,1)S(1)} %pad_maximum_fusion.refs_0_), channel_id=1, source_target_pairs={{1,0},{0,1},{3,2},{2,3},{5,4},{4,5},{7,6},{6,7},{9,8},{8,9},{11,10... | collective-permute-start | bytes 884744 | tf_op jit(solution)/shard_map/ppermute | solution.py:469
  14.8 1.6 %collective-permute-start.6 = (bf16[32,1152]{1,0:T(8,128)(2,1)S(1)}, bf16[32,1152]{1,0:T(8,128)(2,1)S(1)}, u32[]{:S(2)}, u32[]{:S(2)}) collective-permute-start(bf16[32,1152]{1,0:T(8,128)(2,1)S(1)} %slice_bitcast_fusion.refs_0_), channel_id=1, source_target_pairs={{2,0},{3,1},{0,2},{1,3},{6,4},{7,5},{4,6},{5,7},{10,8},{11,9},{8,1... | collective-permute-start | bytes 221192 | tf_op jit(solution)/shard_map/ppermute | solution.py:469
  16.3 1.6 %collective-permute-start.7 = (bf16[32,1152]{1,0:T(8,128)(2,1)S(1)}, bf16[32,1152]{1,0:T(8,128)(2,1)S(1)}, u32[]{:S(2)}, u32[]{:S(2)}) collective-permute-start(bf16[32,1152]{1,0:T(8,128)(2,1)S(1)} %slice_bitcast_fusion.refs_0_), channel_id=1, source_target_pairs={{4,0},{5,1},{6,2},{7,3},{0,4},{1,5},{2,6},{3,7},{12,8},{13,9},{14,... | collective-permute-start | bytes 221192 | tf_op jit(solution)/shard_map/ppermute | solution.py:469
  18.0 1.2 %collective-permute-start.8 = (bf16[32,1152]{1,0:T(8,128)(2,1)S(1)}, bf16[32,1152]{1,0:T(8,128)(2,1)S(1)}, u32[]{:S(2)}, u32[]{:S(2)}) collective-permute-start(bf16[32,1152]{1,0:T(8,128)(2,1)S(1)} %slice_bitcast_fusion.refs_0_), channel_id=1, source_target_pairs={{6,0},{7,1},{4,2},{5,3},{2,4},{3,5},{0,6},{1,7},{14,8},{15,9},{12,... | collective-permute-start | bytes 221192 | tf_op jit(solution)/shard_map/ppermute | solution.py:469
  19.2 0.5 %collective-permute-start.9 = (bf16[32,1152]{1,0:T(8,128)(2,1)S(1)}, bf16[32,1152]{1,0:T(8,128)(2,1)S(1)}, u32[]{:S(2)}, u32[]{:S(2)}) collective-permute-start(bf16[32,1152]{1,0:T(8,128)(2,1)S(1)} %slice_bitcast_fusion.refs_0_), channel_id=1, source_target_pairs={{1,0},{0,1},{3,2},{2,3},{5,4},{4,5},{7,6},{6,7},{9,8},{8,9},{11,10... | collective-permute-start | bytes 221192 | tf_op jit(solution)/shard_map/ppermute | solution.py:469
  19.7 4.1 %weights_by_block.1 = (bf16[1728,1152]{1,0:T(8,128)(2,1)S(1)}, bf16[1728,1152]{1,0:T(8,128)(2,1)S(1)}, bf16[640,1152]{1,0:T(8,128)(2,1)S(1)}, bf16[640,1152]{1,0:T(8,128)(2,1)S(1)}) custom-call(bf16[1,1728,1152]{2,1,0:T(8,128)(2,1)} %bitcast.34, bf16[1,1728,1152]{2,1,0:T(8,128)(2,1)} %collective-permute-done.3.other_ref, bf16[1,576,1152]{2,1,0:T(8,128)(2,1)} %wo_own.1, ...), custom_call_target="tpu_custom_call" | custom-call | tf_op jit(solution)/shard_map/weights_by_block/pallas_call | solution.py:163
  23.8 0.6 %collective-permute-done.7 = bf16[32,1152]{1,0:T(8,128)(2,1)S(1)} collective-permute-done((bf16[32,1152]{1,0:T(8,128)(2,1)S(1)}, bf16[32,1152]{1,0:T(8,128)(2,1)S(1)}, u32[]{:S(2)}, u32[]{:S(2)}) %collective-permute-start.7) | collective-permute-done | bytes 73760 | tf_op jit(solution)/shard_map/ppermute | solution.py:469
  24.4 1.1 %collective-permute-start.10 = (bf16[96,1152]{1,0:T(8,128)(2,1)S(1)}, bf16[96,1152]{1,0:T(8,128)(2,1)S(1)}, u32[]{:S(2)}, u32[]{:S(2)}) collective-permute-start(bf16[96,1152]{1,0:T(8,128)(2,1)S(1)} %pad_maximum_fusion.1.refs_1_), channel_id=1, source_target_pairs={{1,0},{0,1},{3,2},{2,3},{5,4},{4,5},{7,6},{6,7},{9,8},{8,9},{11,10... | collective-permute-start | bytes 663560 | tf_op jit(solution)/shard_map/ppermute | solution.py:469
  25.4 1.9 %layer_norm_and_projections.1 = (bf16[256,1152]{1,0:T(8,128)(2,1)S(1)}, bf16[256,640]{1,0:T(8,128)(2,1)S(1)}, bf16[256,1152]{1,0:T(8,128)(2,1)S(1)}, bf16[64,115...) custom-call(bf16[128,1152]{1,0:T(8,128)(2,1)S(1)} %pad_maximum_fusio, ...), custom_call_target="tpu_custom_call" | custom-call | tf_op jit(solution)/shard_map/layer_norm_and_projections/pallas_call | solution.py:211
  27.4 0.5 %collective-permute-start.12 = (bf16[64,1152]{1,0:T(8,128)(2,1)S(1)}, bf16[64,1152]{1,0:T(8,128)(2,1)S(1)}, u32[]{:S(2)}, u32[]{:S(2)}) collective-permute-start(bf16[64,1152]{1,0:T(8,128)(2,1)S(1)} %get-tuple-element.68), channel_id=1, source_target_pairs={{0,8},{8,0},{1,9},{9,1},{2,10},{10,2},{3,11},{11,3},{4,12},{12,4},... | collective-permute-start | bytes 442376 | tf_op jit(solution)/shard_map/ppermute | solution.py:542
  29.5 0.9 %collective-permute-done.10.refs_3_ = bf16[96,1152]{1,0:T(8,128)(2,1)S(1)} collective-permute-done((bf16[96,1152]{1,0:T(8,128)(2,1)S(1)}, bf16[96,1152]{1,0:T(8,128)(2,1)S(1)}, u32[]{:S(2)}, u32[]{:S(2)}) %collective-permute-start.10) | collective-permute-done | bytes 221216 | tf_op jit(solution)/shard_map/ppermute | solution.py:469
  30.4 4.3 %attention_and_next_keys.1 = (bf16[256,1152]{1,0:T(8,128)(2,1)S(1)}, bf16[256,1152]{1,0:T(8,128)(2,1)S(1)}, bf16[256,1152]{1,0:T(8,128)(2,1)S(1)}, bf16[256,1152]{1,0:T(8,128)(2,1)S(1)}) custom-call(bf16[32,1152]{1,0:T(8,128)(2,1)S(1)} %slice_bitcast_fusion.refs_0_, bf16[96,1152]{1,0:T(8,128)(2,1)S(1)} %pad_maximum_fusion.1.refs_1_, ...), custom_call_target="tpu_custom_call" | custom-call | tf_op jit(solution)/shard_map/attention_and_next_keys/pallas_call | solution.py:307
  34.8 2.1 %tile_attention_over_own_keys.1 = (bf16[48,1152]{1,0:T(8,128)(2,1)S(1)}, bf16[48,640]{1,0:T(8,128)(2,1)S(1)}, f32[48,640]{1,0:T(8,128)S(1)}, f32[48,128]{1,0:T(8,128)S(1)}) custom-call(bf16[256,1152]{1,0:T(8,128)(2,1)S(1)} %get-tuple-element.76.x_ref, bf16[256,1152]{1,0:T(8,128)(2,1)S(1)} %get-tuple-element.77.mod_ref, ...), custom_call_target="tpu_custom_call" | custom-call | tf_op jit(solution)/shard_map/tile_attention_over_own_keys/pallas_call | solution.py:250
  37.0 2.5 %tile_attention_and_patches.1.patch_ref = f32[48,128]{1,0:T(8,128)S(1)} custom-call(bf16[48,1152]{1,0:T(8,128)(2,1)S(1)} %get-tuple-element.80.x_ref, bf16[48,640]{1,0:T(8,128)(2,1)S(1)} %get-tuple-element.81.q_ref, f32[48,640]{1,0:T(8,128)S(1)} %get-tuple-element.82.sum_ref, f32[48,128]{1,0:T(8,128)S(1)} %get-tuple-element.83.state_ref, ...), custom_call_target="tpu_custom_call" | custom-call | tf_op jit(solution)/shard_map/tile_attention_and_patches/pallas_call | solution.py:334
  39.5 0.5 %collective-permute-start.16 = (f32[48,128]{1,0:T(8,128)S(1)}, f32[48,128]{1,0:T(8,128)S(1)}, u32[]{:S(2)}, u32[]{:S(2)}) collective-permute-start(f32[48,128]{1,0:T(8,128)S(1)} %tile_attention_and_patches.1.patch_ref), channel_id=1, source_target_pairs={{0,8},{8,0},{1,9},{9,1},{2,10},{10,2},{3,11},{11,3},{4,12},{12,4},... | collective-permute-start | bytes 73736 | tf_op jit(solution)/shard_map/ppermute | solution.py:552
  40.9 2.7 %decoder_convolutions.1 = bf16[4,128,512]{2,1,0:T(8,128)(2,1)} custom-call(f32[48,128]{1,0:T(8,128)S(1)} %tile_attention_and_patches.1.patch_ref, f32[48,128]{1,0:T(8,128)S(1)} %collective-permute-done.16.got_ref, s32[48,128]{1,0:T(8,128)S(1)} %broadcast_in_dim.14.idx_ref, bf16[1024,512]{1,0:T(8,128)(2,1)S(1)} %fusion.wp_ref, f32[1,512]{1,0:T(1,128)S(1)} %bitcast.31, ...), custom_call_target="tpu_custom_call" | custom-call | tf_op jit(solution)/shard_map/decoder_convolutions/pallas_call | solution.py:433
  (47 shorter events, 3.3 us)
Async XLA Ops:
  0.0 7.4 %copy-start = (f32[100,5,1152]{2,0,1:T(8,128)S(1)}, f32[100,5,1152]{2,0,1:T(8,128)}, u32[]{:S(2)}) copy-start(f32[100,5,1152]{2,0,1:T(8,128)} %param.19) | copy-start | bytes 6912004
  0.0 13.1 %collective-permute-start.3 = (bf16[1,1728,1152]{2,1,0:T(8,128)(2,1)}, bf16[1,1728,1152]{2,1,0:T(8,128)(2,1)}, u32[]{:S(2)}, u32[]{:S(2)}) collective-permute-start(bf16[1,1728,1152]{2,1,0:T(8,128)(2,1)} %bitcast.33), channel_id=1, source_target_pairs={{0,8},{8,0},{1,9},{9,1},{2,10},{10,2},{3,11},{11,3},{4,12},{12,4},... | collective-permute-start | bytes 11943944 | tf_op jit(solution)/shard_map/ppermute | solution.py:500
  1.6 10.3 %collective-permute-start = (bf16[32,1152]{1,0:T(8,128)(2,1)S(1)}, bf16[32,1152]{1,0:T(8,128)(2,1)S(1)}, u32[]{:S(2)}, u32[]{:S(2)}) collective-permute-start(bf16[32,1152]{1,0:T(8,128)(2,1)S(1)} %dynamic-slice_bitcast_fusion), channel_id=1, source_target_pairs={{2,0},{3,1},{0,2},{1,3},{6,4},{7,5},{4,6},{5,7},{10,8},{11,9},{8,1... | collective-permute-start | bytes 221192 | tf_op jit(solution)/shard_map/ppermute | solution.py:469
  4.1 9.0 %collective-permute-start.1 = (bf16[32,1152]{1,0:T(8,128)(2,1)S(1)}, bf16[32,1152]{1,0:T(8,128)(2,1)S(1)}, u32[]{:S(2)}, u32[]{:S(2)}) collective-permute-start(bf16[32,1152]{1,0:T(8,128)(2,1)S(1)} %dynamic-slice_bitcast_fusion), channel_id=1, source_target_pairs={{4,0},{5,1},{6,2},{7,3},{0,4},{1,5},{2,6},{3,7},{12,8},{13,9},{14,... | collective-permute-start | bytes 221192 | tf_op jit(solution)/shard_map/ppermute | solution.py:469
  6.7 6.4 %collective-permute-start.2 = (bf16[32,1152]{1,0:T(8,128)(2,1)S(1)}, bf16[32,1152]{1,0:T(8,128)(2,1)S(1)}, u32[]{:S(2)}, u32[]{:S(2)}) collective-permute-start(bf16[32,1152]{1,0:T(8,128)(2,1)S(1)} %dynamic-slice_bitcast_fusion), channel_id=1, source_target_pairs={{6,0},{7,1},{4,2},{5,3},{2,4},{3,5},{0,6},{1,7},{14,8},{15,9},{12,... | collective-permute-start | bytes 221192 | tf_op jit(solution)/shard_map/ppermute | solution.py:469
  6.7 6.4 %collective-permute-start.4 = (bf16[1,576,1152]{2,1,0:T(8,128)(2,1)}, bf16[1,576,1152]{2,1,0:T(8,128)(2,1)}, u32[]{:S(2)}, u32[]{:S(2)}) collective-permute-start(bf16[1,576,1152]{2,1,0:T(8,128)(2,1)} %wo_own.1), channel_id=1, source_target_pairs={{0,8},{8,0},{1,9},{9,1},{2,10},{10,2},{3,11},{11,3},{4,12},{12,4},... | collective-permute-start | bytes 3981320 | tf_op jit(solution)/shard_map/ppermute | solution.py:504
  13.2 11.1 %collective-permute-start.5 = (bf16[128,1152]{1,0:T(8,128)(2,1)S(1)}, bf16[128,1152]{1,0:T(8,128)(2,1)S(1)}, u32[]{:S(2)}, u32[]{:S(2)}) collective-permute-start(bf16[128,1152]{1,0:T(8,128)(2,1)S(1)} %pad_maximum_fusion.refs_0_), channel_id=1, source_target_pairs={{1,0},{0,1},{3,2},{2,3},{5,4},{4,5},{7,6},{6,7},{9,8},{8,9},{11,10... | collective-permute-start | bytes 884744 | tf_op jit(solution)/shard_map/ppermute | solution.py:469
  14.8 9.0 %collective-permute-start.6 = (bf16[32,1152]{1,0:T(8,128)(2,1)S(1)}, bf16[32,1152]{1,0:T(8,128)(2,1)S(1)}, u32[]{:S(2)}, u32[]{:S(2)}) collective-permute-start(bf16[32,1152]{1,0:T(8,128)(2,1)S(1)} %slice_bitcast_fusion.refs_0_), channel_id=1, source_target_pairs={{2,0},{3,1},{0,2},{1,3},{6,4},{7,5},{4,6},{5,7},{10,8},{11,9},{8,1... | collective-permute-start | bytes 221192 | tf_op jit(solution)/shard_map/ppermute | solution.py:469
  16.3 8.0 %collective-permute-start.7 = (bf16[32,1152]{1,0:T(8,128)(2,1)S(1)}, bf16[32,1152]{1,0:T(8,128)(2,1)S(1)}, u32[]{:S(2)}, u32[]{:S(2)}) collective-permute-start(bf16[32,1152]{1,0:T(8,128)(2,1)S(1)} %slice_bitcast_fusion.refs_0_), channel_id=1, source_target_pairs={{4,0},{5,1},{6,2},{7,3},{0,4},{1,5},{2,6},{3,7},{12,8},{13,9},{14,... | collective-permute-start | bytes 221192 | tf_op jit(solution)/shard_map/ppermute | solution.py:469
  18.0 6.4 %collective-permute-start.8 = (bf16[32,1152]{1,0:T(8,128)(2,1)S(1)}, bf16[32,1152]{1,0:T(8,128)(2,1)S(1)}, u32[]{:S(2)}, u32[]{:S(2)}) collective-permute-start(bf16[32,1152]{1,0:T(8,128)(2,1)S(1)} %slice_bitcast_fusion.refs_0_), channel_id=1, source_target_pairs={{6,0},{7,1},{4,2},{5,3},{2,4},{3,5},{0,6},{1,7},{14,8},{15,9},{12,... | collective-permute-start | bytes 221192 | tf_op jit(solution)/shard_map/ppermute | solution.py:469
  19.2 5.2 %collective-permute-start.9 = (bf16[32,1152]{1,0:T(8,128)(2,1)S(1)}, bf16[32,1152]{1,0:T(8,128)(2,1)S(1)}, u32[]{:S(2)}, u32[]{:S(2)}) collective-permute-start(bf16[32,1152]{1,0:T(8,128)(2,1)S(1)} %slice_bitcast_fusion.refs_0_), channel_id=1, source_target_pairs={{1,0},{0,1},{3,2},{2,3},{5,4},{4,5},{7,6},{6,7},{9,8},{8,9},{11,10... | collective-permute-start | bytes 221192 | tf_op jit(solution)/shard_map/ppermute | solution.py:469
  24.4 6.0 %collective-permute-start.10 = (bf16[96,1152]{1,0:T(8,128)(2,1)S(1)}, bf16[96,1152]{1,0:T(8,128)(2,1)S(1)}, u32[]{:S(2)}, u32[]{:S(2)}) collective-permute-start(bf16[96,1152]{1,0:T(8,128)(2,1)S(1)} %pad_maximum_fusion.1.refs_1_), channel_id=1, source_target_pairs={{1,0},{0,1},{3,2},{2,3},{5,4},{4,5},{7,6},{6,7},{9,8},{8,9},{11,10... | collective-permute-start | bytes 663560 | tf_op jit(solution)/shard_map/ppermute | solution.py:469
  27.3 1.4 %collective-permute-start.11 = (bf16[64,1152]{1,0:T(8,128)(2,1)S(1)}, bf16[64,1152]{1,0:T(8,128)(2,1)S(1)}, u32[]{:S(2)}, u32[]{:S(2)}) collective-permute-start(bf16[64,1152]{1,0:T(8,128)(2,1)S(1)} %get-tuple-element.67), channel_id=1, source_target_pairs={{0,8},{8,0},{1,9},{9,1},{2,10},{10,2},{3,11},{11,3},{4,12},{12,4},... | collective-permute-start | bytes 442376 | tf_op jit(solution)/shard_map/ppermute | solution.py:542
  27.4 1.6 %collective-permute-start.12 = (bf16[64,1152]{1,0:T(8,128)(2,1)S(1)}, bf16[64,1152]{1,0:T(8,128)(2,1)S(1)}, u32[]{:S(2)}, u32[]{:S(2)}) collective-permute-start(bf16[64,1152]{1,0:T(8,128)(2,1)S(1)} %get-tuple-element.68), channel_id=1, source_target_pairs={{0,8},{8,0},{1,9},{9,1},{2,10},{10,2},{3,11},{11,3},{4,12},{12,4},... | collective-permute-start | bytes 442376 | tf_op jit(solution)/shard_map/ppermute | solution.py:542
  27.9 1.4 %collective-permute-start.13 = (bf16[64,1152]{1,0:T(8,128)(2,1)S(1)}, bf16[64,1152]{1,0:T(8,128)(2,1)S(1)}, u32[]{:S(2)}, u32[]{:S(2)}) collective-permute-start(bf16[64,1152]{1,0:T(8,128)(2,1)S(1)} %get-tuple-element.69), channel_id=1, source_target_pairs={{0,8},{8,0},{1,9},{9,1},{2,10},{10,2},{3,11},{11,3},{4,12},{12,4},... | collective-permute-start | bytes 442376 | tf_op jit(solution)/shard_map/ppermute | solution.py:542
  28.0 1.5 %collective-permute-start.14 = (bf16[64,1152]{1,0:T(8,128)(2,1)S(1)}, bf16[64,1152]{1,0:T(8,128)(2,1)S(1)}, u32[]{:S(2)}, u32[]{:S(2)}) collective-permute-start(bf16[64,1152]{1,0:T(8,128)(2,1)S(1)} %get-tuple-element.70), channel_id=1, source_target_pairs={{0,8},{8,0},{1,9},{9,1},{2,10},{10,2},{3,11},{11,3},{4,12},{12,4},... | collective-permute-start | bytes 442376 | tf_op jit(solution)/shard_map/ppermute | solution.py:542
  34.7 2.3 %collective-permute-start.15 = (bf16[256,1152]{1,0:T(8,128)(2,1)S(1)}, bf16[256,1152]{1,0:T(8,128)(2,1)S(1)}, u32[]{:S(2)}, u32[]{:S(2)}) collective-permute-start(bf16[256,1152]{1,0:T(8,128)(2,1)S(1)} %get-tuple-element.84), channel_id=1, source_target_pairs={{0,8},{8,0},{1,9},{9,1},{2,10},{10,2},{3,11},{11,3},{4,12},{12,4},... | collective-permute-start | bytes 1769480 | tf_op jit(solution)/shard_map/ppermute | solution.py:544
  34.8 6.1 %slice-start = ((s8[4718592]{0:T(1024)(128)(4,1)}), s8[4194304]{0:T(1024)(128)(4,1)S(1)}, s32[]{:S(2)}) async-start(s8[4718592]{0:T(1024)(128)(4,1)} %bitcast.28), calls=%async_computation | async-start | bytes 8388608
  34.8 6.1 %slice-start.1 = ((s8[4718592]{0:T(1024)(128)(4,1)}), s8[524288]{0:T(1024)(128)(4,1)S(1)}, s32[]{:S(2)}) async-start(s8[4718592]{0:T(1024)(128)(4,1)} %bitcast.28), calls=%async_computation.1 | async-start | bytes 1048576
  36.9 3.2 %copy-start.4 = (bf16[1024,36]{1,0:T(8,128)(2,1)S(1)}, bf16[1024,36]{1,0:T(8,128)(2,1)}, u32[]{:S(2)}) copy-start(bf16[1024,36]{1,0:T(8,128)(2,1)} %constant.114.clone) | copy-start | bytes 221188
  36.9 3.1 %copy-start.5 = (bf16[36,512]{1,0:T(8,128)(2,1)S(1)}, bf16[36,512]{1,0:T(8,128)(2,1)}, u32[]{:S(2)}) copy-start(bf16[36,512]{1,0:T(8,128)(2,1)} %param.22) | copy-start | bytes 110596
  36.9 4.0 %copy-start.2 = (f32[512]{0:T(512)S(1)}, f32[512]{0:T(512)}, u32[]{:S(2)}) copy-start(f32[512]{0:T(512)} %param.23) | copy-start | bytes 6148
  36.9 4.0 %copy-start.3 = (f32[512]{0:T(512)S(1)}, f32[512]{0:T(512)}, u32[]{:S(2)}) copy-start(f32[512]{0:T(512)} %param.25) | copy-start | bytes 6148
  39.5 1.4 %collective-permute-start.16 = (f32[48,128]{1,0:T(8,128)S(1)}, f32[48,128]{1,0:T(8,128)S(1)}, u32[]{:S(2)}, u32[]{:S(2)}) collective-permute-start(f32[48,128]{1,0:T(8,128)S(1)} %tile_attention_and_patches.1.patch_ref), channel_id=1, source_target_pairs={{0,8},{8,0},{1,9},{9,1},{2,10},{10,2},{3,11},{11,3},{4,12},{12,4},... | collective-permute-start | bytes 73736 | tf_op jit(solution)/shard_map/ppermute | solution.py:552
  (1 other events, 2.2 us)

commit v22 on v21

--- a/solution.py
+++ b/solution.py
@@ -271,7 +271,6 @@
     ) = refs[n_pieces + n_got :]
     count = x_ref.shape[0]
     first_core = lax.axis_index("pipe") == 0
-    join(stale_refs, send_ref)
     all_ref[:count] = kv_ref[...]
 
     @pl.when(first_core)
@@ -281,6 +280,7 @@
     @pl.when(jnp.logical_not(first_core))
     def _():
         join(got_refs, all_ref.at[count:])
+        join(stale_refs, send_ref)
 
 
     def body(start, size):

time: 43.9 us -> 43.8 us (level)
  no operation moved by 1% of the time
where the time goes in v22:
time: 43.8 us; the launch traced here: 43.6 us
  Pallas kernels  17.5 us (40%)
  starting transfers between devices  14.8 us (34%)
  waiting for transfers between devices  4.19 us (10%)
  local copies, waits for them, and re-layouts  2.89 us (7%)
  blocking collectives  1.99 us (5%)
  between operations  0.91 us (2%)
  other arithmetic  0.84 us (2%)
    ppermute x9, starting transfers between devices, swapped(): lax.ppermute(block, 'patch', [(i ^ k_outer * inner + k_inner, i) for i in...  12.7 us
    pallas_call x1, Pallas kernels, first_block(): pl.pallas_call(functools.partial(block_kernel, len(stale_pieces), len(got...  4.26 us
    pallas_call x1, Pallas kernels, weights_in_vmem(): pl.pallas_call(weights_kernel, out_shape=(jax.ShapeDtypeStruct((3 * DA, D...  4.08 us
    pallas_call x1, Pallas kernels, decode(): pl.pallas_call(functools.partial(decode_kernel, rows, cols, pitch), out_s...  2.69 us
    ppermute x9, waiting for transfers between devices, swapped(): lax.ppermute(block, 'patch', [(i ^ k_outer * inner + k_inner, i) for i in...  2.68 us
    pallas_call x1, Pallas kernels, tile_block(): pl.pallas_call(tile_kernel, out_shape=jax.ShapeDtypeStruct((x.shape[0], L...  2.54 us
    pallas_call x1, Pallas kernels, attend_fresh(): pl.pallas_call(fresh_kernel, out_shape=(jax.ShapeDtypeStruct((rows, D), B...  2.08 us
    all_gather x1, blocking collectives, local(): tables = lax.all_gather(block_table[0], 'pipe')  1.99 us
  transfers between devices with their start and end apart: 17, of which 8 were waited for; matrix products, arithmetic and copies ran while one was open for 9% of the time, Pallas kernels for 18%

profile of v22, /device:TPU:0, one launch (start us, length us, event | category | flops | bytes accessed | tf_op | source)
XLA Modules:
  0.0 43.6 jit_solution(5225458233919907234)
XLA Ops:
  0.5 1.1 %dynamic-slice_bitcast_fusion = bf16[32,1152]{1,0:T(8,128)(2,1)S(1)} fusion(bf16[2,32,1152]{2,1,0:T(8,128)(2,1)} %param.14, s32[]{:T(128)S(6)} %select_n.80), kind=kLoop, calls=%fused_computation.5 | loop fusion | bytes 147460 | tf_op jit(solution)/shard_map/jit(dynamic_index_in_dim)/squeeze | solution.py:498
  1.6 2.5 %collective-permute-start = (bf16[32,1152]{1,0:T(8,128)(2,1)S(1)}, bf16[32,1152]{1,0:T(8,128)(2,1)S(1)}, u32[]{:S(2)}, u32[]{:S(2)}) collective-permute-start(bf16[32,1152]{1,0:T(8,128)(2,1)S(1)} %dynamic-slice_bitcast_fusion), channel_id=1, source_target_pairs={{2,0},{3,1},{0,2},{1,3},{6,4},{7,5},{4,6},{5,7},{10,8},{11,9},{8,1... | collective-permute-start | bytes 221192 | tf_op jit(solution)/shard_map/ppermute | solution.py:469
  4.1 2.6 %collective-permute-start.1 = (bf16[32,1152]{1,0:T(8,128)(2,1)S(1)}, bf16[32,1152]{1,0:T(8,128)(2,1)S(1)}, u32[]{:S(2)}, u32[]{:S(2)}) collective-permute-start(bf16[32,1152]{1,0:T(8,128)(2,1)S(1)} %dynamic-slice_bitcast_fusion), channel_id=1, source_target_pairs={{4,0},{5,1},{6,2},{7,3},{0,4},{1,5},{2,6},{3,7},{12,8},{13,9},{14,... | collective-permute-start | bytes 221192 | tf_op jit(solution)/shard_map/ppermute | solution.py:469
  7.5 0.7 %copy.19 = f32[1,3,1152]{2,1,0:T(4,128)S(1)} copy(f32[1,3,1152]{2,0,1:T(1,128)} %param.18) | data formatting | bytes 27648 | tf_op args[4]
  8.2 2.0 %all_gather.3 = f32[2,3,1152]{2,1,0:T(4,128)S(1)} all-gather(f32[1,3,1152]{2,1,0:T(4,128)S(1)} %copy.19), channel_id=1, replica_groups=mesh['grp'=2,'pipe'=2,'patch'=8] {'pipe'}, dimensions={0}, use_global_device_ids=true | all-gather | bytes 41472 | tf_op jit(solution)/shard_map/all_gather | solution.py:501
  10.2 0.7 %fusion.2 = (f32[3,1152]{1,0:T(4,128)S(1)}, f32[3,1152]{1,0:T(4,128)S(1)}) fusion(f32[1,3,1152]{2,0,1:T(1,128)S(1)} %constant_dynamic-slice_fusion, f32[2,3,1152]{2,1,0:T(4,128)S(1)} %all_gather.3, f32[3]{0:T(128)} %constant.120), kind=kLoop, calls=%fused_computation.10 | loop fusion | flops 13824 | bytes 69132 | tf_op jit(solution)/shard_map/add | solution.py:510
  10.9 0.9 %slice_bitcast_fusion.refs_0_ = bf16[32,1152]{1,0:T(8,128)(2,1)S(1)} fusion(bf16[1,2,32,1152]{3,2,1,0:T(8,128)(2,1)} %param.15), kind=kLoop, calls=%fused_computation.4 | loop fusion | bytes 147456 | tf_op jit(solution)/shard_map/squeeze | solution.py:503
  11.9 1.2 %collective-permute-done.1 = bf16[32,1152]{1,0:T(8,128)(2,1)S(1)} collective-permute-done((bf16[32,1152]{1,0:T(8,128)(2,1)S(1)}, bf16[32,1152]{1,0:T(8,128)(2,1)S(1)}, u32[]{:S(2)}, u32[]{:S(2)}) %collective-permute-start.1) | collective-permute-done | bytes 73760 | tf_op jit(solution)/shard_map/ppermute | solution.py:469
  13.2 1.6 %collective-permute-start.5 = (bf16[128,1152]{1,0:T(8,128)(2,1)S(1)}, bf16[128,1152]{1,0:T(8,128)(2,1)S(1)}, u32[]{:S(2)}, u32[]{:S(2)}) collective-permute-start(bf16[128,1152]{1,0:T(8,128)(2,1)S(1)} %pad_maximum_fusion.refs_0_), channel_id=1, source_target_pairs={{1,0},{0,1},{3,2},{2,3},{5,4},{4,5},{7,6},{6,7},{9,8},{8,9},{11,10... | collective-permute-start | bytes 884744 | tf_op jit(solution)/shard_map/ppermute | solution.py:469
  14.8 1.6 %collective-permute-start.6 = (bf16[32,1152]{1,0:T(8,128)(2,1)S(1)}, bf16[32,1152]{1,0:T(8,128)(2,1)S(1)}, u32[]{:S(2)}, u32[]{:S(2)}) collective-permute-start(bf16[32,1152]{1,0:T(8,128)(2,1)S(1)} %slice_bitcast_fusion.refs_0_), channel_id=1, source_target_pairs={{2,0},{3,1},{0,2},{1,3},{6,4},{7,5},{4,6},{5,7},{10,8},{11,9},{8,1... | collective-permute-start | bytes 221192 | tf_op jit(solution)/shard_map/ppermute | solution.py:469
  16.3 1.6 %collective-permute-start.7 = (bf16[32,1152]{1,0:T(8,128)(2,1)S(1)}, bf16[32,1152]{1,0:T(8,128)(2,1)S(1)}, u32[]{:S(2)}, u32[]{:S(2)}) collective-permute-start(bf16[32,1152]{1,0:T(8,128)(2,1)S(1)} %slice_bitcast_fusion.refs_0_), channel_id=1, source_target_pairs={{4,0},{5,1},{6,2},{7,3},{0,4},{1,5},{2,6},{3,7},{12,8},{13,9},{14,... | collective-permute-start | bytes 221192 | tf_op jit(solution)/shard_map/ppermute | solution.py:469
  18.0 1.2 %collective-permute-start.8 = (bf16[32,1152]{1,0:T(8,128)(2,1)S(1)}, bf16[32,1152]{1,0:T(8,128)(2,1)S(1)}, u32[]{:S(2)}, u32[]{:S(2)}) collective-permute-start(bf16[32,1152]{1,0:T(8,128)(2,1)S(1)} %slice_bitcast_fusion.refs_0_), channel_id=1, source_target_pairs={{6,0},{7,1},{4,2},{5,3},{2,4},{3,5},{0,6},{1,7},{14,8},{15,9},{12,... | collective-permute-start | bytes 221192 | tf_op jit(solution)/shard_map/ppermute | solution.py:469
  19.2 0.5 %collective-permute-start.9 = (bf16[32,1152]{1,0:T(8,128)(2,1)S(1)}, bf16[32,1152]{1,0:T(8,128)(2,1)S(1)}, u32[]{:S(2)}, u32[]{:S(2)}) collective-permute-start(bf16[32,1152]{1,0:T(8,128)(2,1)S(1)} %slice_bitcast_fusion.refs_0_), channel_id=1, source_target_pairs={{1,0},{0,1},{3,2},{2,3},{5,4},{4,5},{7,6},{6,7},{9,8},{8,9},{11,10... | collective-permute-start | bytes 221192 | tf_op jit(solution)/shard_map/ppermute | solution.py:469
  19.7 4.1 %weights_by_block.1 = (bf16[1728,1152]{1,0:T(8,128)(2,1)S(1)}, bf16[1728,1152]{1,0:T(8,128)(2,1)S(1)}, bf16[640,1152]{1,0:T(8,128)(2,1)S(1)}, bf16[640,1152]{1,0:T(8,128)(2,1)S(1)}) custom-call(bf16[1,1728,1152]{2,1,0:T(8,128)(2,1)} %bitcast.34, bf16[1,1728,1152]{2,1,0:T(8,128)(2,1)} %collective-permute-done.3.other_ref, bf16[1,576,1152]{2,1,0:T(8,128)(2,1)} %wo_own.1, ...), custom_call_target="tpu_custom_call" | custom-call | tf_op jit(solution)/shard_map/weights_by_block/pallas_call | solution.py:163
  23.8 0.6 %collective-permute-done.7 = bf16[32,1152]{1,0:T(8,128)(2,1)S(1)} collective-permute-done((bf16[32,1152]{1,0:T(8,128)(2,1)S(1)}, bf16[32,1152]{1,0:T(8,128)(2,1)S(1)}, u32[]{:S(2)}, u32[]{:S(2)}) %collective-permute-start.7) | collective-permute-done | bytes 73760 | tf_op jit(solution)/shard_map/ppermute | solution.py:469
  24.4 1.1 %collective-permute-start.10 = (bf16[96,1152]{1,0:T(8,128)(2,1)S(1)}, bf16[96,1152]{1,0:T(8,128)(2,1)S(1)}, u32[]{:S(2)}, u32[]{:S(2)}) collective-permute-start(bf16[96,1152]{1,0:T(8,128)(2,1)S(1)} %pad_maximum_fusion.1.refs_1_), channel_id=1, source_target_pairs={{1,0},{0,1},{3,2},{2,3},{5,4},{4,5},{7,6},{6,7},{9,8},{8,9},{11,10... | collective-permute-start | bytes 663560 | tf_op jit(solution)/shard_map/ppermute | solution.py:469
  25.4 1.9 %layer_norm_and_projections.1 = (bf16[256,1152]{1,0:T(8,128)(2,1)S(1)}, bf16[256,640]{1,0:T(8,128)(2,1)S(1)}, bf16[256,1152]{1,0:T(8,128)(2,1)S(1)}, bf16[64,115...) custom-call(bf16[128,1152]{1,0:T(8,128)(2,1)S(1)} %pad_maximum_fusio, ...), custom_call_target="tpu_custom_call" | custom-call | tf_op jit(solution)/shard_map/layer_norm_and_projections/pallas_call | solution.py:211
  27.4 0.5 %collective-permute-start.12 = (bf16[64,1152]{1,0:T(8,128)(2,1)S(1)}, bf16[64,1152]{1,0:T(8,128)(2,1)S(1)}, u32[]{:S(2)}, u32[]{:S(2)}) collective-permute-start(bf16[64,1152]{1,0:T(8,128)(2,1)S(1)} %get-tuple-element.68), channel_id=1, source_target_pairs={{0,8},{8,0},{1,9},{9,1},{2,10},{10,2},{3,11},{11,3},{4,12},{12,4},... | collective-permute-start | bytes 442376 | tf_op jit(solution)/shard_map/ppermute | solution.py:542
  29.5 0.9 %collective-permute-done.10.refs_3_ = bf16[96,1152]{1,0:T(8,128)(2,1)S(1)} collective-permute-done((bf16[96,1152]{1,0:T(8,128)(2,1)S(1)}, bf16[96,1152]{1,0:T(8,128)(2,1)S(1)}, u32[]{:S(2)}, u32[]{:S(2)}) %collective-permute-start.10) | collective-permute-done | bytes 221216 | tf_op jit(solution)/shard_map/ppermute | solution.py:469
  30.4 4.3 %attention_and_next_keys.1 = (bf16[256,1152]{1,0:T(8,128)(2,1)S(1)}, bf16[256,1152]{1,0:T(8,128)(2,1)S(1)}, bf16[256,1152]{1,0:T(8,128)(2,1)S(1)}, bf16[256,1152]{1,0:T(8,128)(2,1)S(1)}) custom-call(bf16[32,1152]{1,0:T(8,128)(2,1)S(1)} %slice_bitcast_fusion.refs_0_, bf16[96,1152]{1,0:T(8,128)(2,1)S(1)} %pad_maximum_fusion.1.refs_1_, ...), custom_call_target="tpu_custom_call" | custom-call | tf_op jit(solution)/shard_map/attention_and_next_keys/pallas_call | solution.py:307
  34.8 2.1 %tile_attention_over_own_keys.1 = (bf16[48,1152]{1,0:T(8,128)(2,1)S(1)}, bf16[48,640]{1,0:T(8,128)(2,1)S(1)}, f32[48,640]{1,0:T(8,128)S(1)}, f32[48,128]{1,0:T(8,128)S(1)}) custom-call(bf16[256,1152]{1,0:T(8,128)(2,1)S(1)} %get-tuple-element.76.x_ref, bf16[256,1152]{1,0:T(8,128)(2,1)S(1)} %get-tuple-element.77.mod_ref, ...), custom_call_target="tpu_custom_call" | custom-call | tf_op jit(solution)/shard_map/tile_attention_over_own_keys/pallas_call | solution.py:250
  36.9 2.5 %tile_attention_and_patches.1.patch_ref = f32[48,128]{1,0:T(8,128)S(1)} custom-call(bf16[48,1152]{1,0:T(8,128)(2,1)S(1)} %get-tuple-element.80.x_ref, bf16[48,640]{1,0:T(8,128)(2,1)S(1)} %get-tuple-element.81.q_ref, f32[48,640]{1,0:T(8,128)S(1)} %get-tuple-element.82.sum_ref, f32[48,128]{1,0:T(8,128)S(1)} %get-tuple-element.83.state_ref, ...), custom_call_target="tpu_custom_call" | custom-call | tf_op jit(solution)/shard_map/tile_attention_and_patches/pallas_call | solution.py:334
  39.5 0.5 %collective-permute-start.16 = (f32[48,128]{1,0:T(8,128)S(1)}, f32[48,128]{1,0:T(8,128)S(1)}, u32[]{:S(2)}, u32[]{:S(2)}) collective-permute-start(f32[48,128]{1,0:T(8,128)S(1)} %tile_attention_and_patches.1.patch_ref), channel_id=1, source_target_pairs={{0,8},{8,0},{1,9},{9,1},{2,10},{10,2},{3,11},{11,3},{4,12},{12,4},... | collective-permute-start | bytes 73736 | tf_op jit(solution)/shard_map/ppermute | solution.py:552
  40.9 2.7 %decoder_convolutions.1 = bf16[4,128,512]{2,1,0:T(8,128)(2,1)} custom-call(f32[48,128]{1,0:T(8,128)S(1)} %tile_attention_and_patches.1.patch_ref, f32[48,128]{1,0:T(8,128)S(1)} %collective-permute-done.16.got_ref, s32[48,128]{1,0:T(8,128)S(1)} %broadcast_in_dim.14.idx_ref, bf16[1024,512]{1,0:T(8,128)(2,1)S(1)} %fusion.wp_ref, f32[1,512]{1,0:T(1,128)S(1)} %bitcast.31, ...), custom_call_target="tpu_custom_call" | custom-call | tf_op jit(solution)/shard_map/decoder_convolutions/pallas_call | solution.py:433
  (47 shorter events, 3.3 us)
Async XLA Ops:
  0.0 7.4 %copy-start = (f32[100,5,1152]{2,0,1:T(8,128)S(1)}, f32[100,5,1152]{2,0,1:T(8,128)}, u32[]{:S(2)}) copy-start(f32[100,5,1152]{2,0,1:T(8,128)} %param.19) | copy-start | bytes 6912004
  0.0 13.1 %collective-permute-start.3 = (bf16[1,1728,1152]{2,1,0:T(8,128)(2,1)}, bf16[1,1728,1152]{2,1,0:T(8,128)(2,1)}, u32[]{:S(2)}, u32[]{:S(2)}) collective-permute-start(bf16[1,1728,1152]{2,1,0:T(8,128)(2,1)} %bitcast.33), channel_id=1, source_target_pairs={{0,8},{8,0},{1,9},{9,1},{2,10},{10,2},{3,11},{11,3},{4,12},{12,4},... | collective-permute-start | bytes 11943944 | tf_op jit(solution)/shard_map/ppermute | solution.py:500
  1.6 10.3 %collective-permute-start = (bf16[32,1152]{1,0:T(8,128)(2,1)S(1)}, bf16[32,1152]{1,0:T(8,128)(2,1)S(1)}, u32[]{:S(2)}, u32[]{:S(2)}) collective-permute-start(bf16[32,1152]{1,0:T(8,128)(2,1)S(1)} %dynamic-slice_bitcast_fusion), channel_id=1, source_target_pairs={{2,0},{3,1},{0,2},{1,3},{6,4},{7,5},{4,6},{5,7},{10,8},{11,9},{8,1... | collective-permute-start | bytes 221192 | tf_op jit(solution)/shard_map/ppermute | solution.py:469
  4.1 9.0 %collective-permute-start.1 = (bf16[32,1152]{1,0:T(8,128)(2,1)S(1)}, bf16[32,1152]{1,0:T(8,128)(2,1)S(1)}, u32[]{:S(2)}, u32[]{:S(2)}) collective-permute-start(bf16[32,1152]{1,0:T(8,128)(2,1)S(1)} %dynamic-slice_bitcast_fusion), channel_id=1, source_target_pairs={{4,0},{5,1},{6,2},{7,3},{0,4},{1,5},{2,6},{3,7},{12,8},{13,9},{14,... | collective-permute-start | bytes 221192 | tf_op jit(solution)/shard_map/ppermute | solution.py:469
  6.7 6.4 %collective-permute-start.2 = (bf16[32,1152]{1,0:T(8,128)(2,1)S(1)}, bf16[32,1152]{1,0:T(8,128)(2,1)S(1)}, u32[]{:S(2)}, u32[]{:S(2)}) collective-permute-start(bf16[32,1152]{1,0:T(8,128)(2,1)S(1)} %dynamic-slice_bitcast_fusion), channel_id=1, source_target_pairs={{6,0},{7,1},{4,2},{5,3},{2,4},{3,5},{0,6},{1,7},{14,8},{15,9},{12,... | collective-permute-start | bytes 221192 | tf_op jit(solution)/shard_map/ppermute | solution.py:469
  6.7 6.4 %collective-permute-start.4 = (bf16[1,576,1152]{2,1,0:T(8,128)(2,1)}, bf16[1,576,1152]{2,1,0:T(8,128)(2,1)}, u32[]{:S(2)}, u32[]{:S(2)}) collective-permute-start(bf16[1,576,1152]{2,1,0:T(8,128)(2,1)} %wo_own.1), channel_id=1, source_target_pairs={{0,8},{8,0},{1,9},{9,1},{2,10},{10,2},{3,11},{11,3},{4,12},{12,4},... | collective-permute-start | bytes 3981320 | tf_op jit(solution)/shard_map/ppermute | solution.py:504
  13.2 11.1 %collective-permute-start.5 = (bf16[128,1152]{1,0:T(8,128)(2,1)S(1)}, bf16[128,1152]{1,0:T(8,128)(2,1)S(1)}, u32[]{:S(2)}, u32[]{:S(2)}) collective-permute-start(bf16[128,1152]{1,0:T(8,128)(2,1)S(1)} %pad_maximum_fusion.refs_0_), channel_id=1, source_target_pairs={{1,0},{0,1},{3,2},{2,3},{5,4},{4,5},{7,6},{6,7},{9,8},{8,9},{11,10... | collective-permute-start | bytes 884744 | tf_op jit(solution)/shard_map/ppermute | solution.py:469
  14.8 9.0 %collective-permute-start.6 = (bf16[32,1152]{1,0:T(8,128)(2,1)S(1)}, bf16[32,1152]{1,0:T(8,128)(2,1)S(1)}, u32[]{:S(2)}, u32[]{:S(2)}) collective-permute-start(bf16[32,1152]{1,0:T(8,128)(2,1)S(1)} %slice_bitcast_fusion.refs_0_), channel_id=1, source_target_pairs={{2,0},{3,1},{0,2},{1,3},{6,4},{7,5},{4,6},{5,7},{10,8},{11,9},{8,1... | collective-permute-start | bytes 221192 | tf_op jit(solution)/shard_map/ppermute | solution.py:469
  16.3 8.0 %collective-permute-start.7 = (bf16[32,1152]{1,0:T(8,128)(2,1)S(1)}, bf16[32,1152]{1,0:T(8,128)(2,1)S(1)}, u32[]{:S(2)}, u32[]{:S(2)}) collective-permute-start(bf16[32,1152]{1,0:T(8,128)(2,1)S(1)} %slice_bitcast_fusion.refs_0_), channel_id=1, source_target_pairs={{4,0},{5,1},{6,2},{7,3},{0,4},{1,5},{2,6},{3,7},{12,8},{13,9},{14,... | collective-permute-start | bytes 221192 | tf_op jit(solution)/shard_map/ppermute | solution.py:469
  18.0 6.4 %collective-permute-start.8 = (bf16[32,1152]{1,0:T(8,128)(2,1)S(1)}, bf16[32,1152]{1,0:T(8,128)(2,1)S(1)}, u32[]{:S(2)}, u32[]{:S(2)}) collective-permute-start(bf16[32,1152]{1,0:T(8,128)(2,1)S(1)} %slice_bitcast_fusion.refs_0_), channel_id=1, source_target_pairs={{6,0},{7,1},{4,2},{5,3},{2,4},{3,5},{0,6},{1,7},{14,8},{15,9},{12,... | collective-permute-start | bytes 221192 | tf_op jit(solution)/shard_map/ppermute | solution.py:469
  19.2 5.2 %collective-permute-start.9 = (bf16[32,1152]{1,0:T(8,128)(2,1)S(1)}, bf16[32,1152]{1,0:T(8,128)(2,1)S(1)}, u32[]{:S(2)}, u32[]{:S(2)}) collective-permute-start(bf16[32,1152]{1,0:T(8,128)(2,1)S(1)} %slice_bitcast_fusion.refs_0_), channel_id=1, source_target_pairs={{1,0},{0,1},{3,2},{2,3},{5,4},{4,5},{7,6},{6,7},{9,8},{8,9},{11,10... | collective-permute-start | bytes 221192 | tf_op jit(solution)/shard_map/ppermute | solution.py:469
  24.4 6.0 %collective-permute-start.10 = (bf16[96,1152]{1,0:T(8,128)(2,1)S(1)}, bf16[96,1152]{1,0:T(8,128)(2,1)S(1)}, u32[]{:S(2)}, u32[]{:S(2)}) collective-permute-start(bf16[96,1152]{1,0:T(8,128)(2,1)S(1)} %pad_maximum_fusion.1.refs_1_), channel_id=1, source_target_pairs={{1,0},{0,1},{3,2},{2,3},{5,4},{4,5},{7,6},{6,7},{9,8},{8,9},{11,10... | collective-permute-start | bytes 663560 | tf_op jit(solution)/shard_map/ppermute | solution.py:469
  27.3 1.4 %collective-permute-start.11 = (bf16[64,1152]{1,0:T(8,128)(2,1)S(1)}, bf16[64,1152]{1,0:T(8,128)(2,1)S(1)}, u32[]{:S(2)}, u32[]{:S(2)}) collective-permute-start(bf16[64,1152]{1,0:T(8,128)(2,1)S(1)} %get-tuple-element.67), channel_id=1, source_target_pairs={{0,8},{8,0},{1,9},{9,1},{2,10},{10,2},{3,11},{11,3},{4,12},{12,4},... | collective-permute-start | bytes 442376 | tf_op jit(solution)/shard_map/ppermute | solution.py:542
  27.4 1.6 %collective-permute-start.12 = (bf16[64,1152]{1,0:T(8,128)(2,1)S(1)}, bf16[64,1152]{1,0:T(8,128)(2,1)S(1)}, u32[]{:S(2)}, u32[]{:S(2)}) collective-permute-start(bf16[64,1152]{1,0:T(8,128)(2,1)S(1)} %get-tuple-element.68), channel_id=1, source_target_pairs={{0,8},{8,0},{1,9},{9,1},{2,10},{10,2},{3,11},{11,3},{4,12},{12,4},... | collective-permute-start | bytes 442376 | tf_op jit(solution)/shard_map/ppermute | solution.py:542
  27.9 1.4 %collective-permute-start.13 = (bf16[64,1152]{1,0:T(8,128)(2,1)S(1)}, bf16[64,1152]{1,0:T(8,128)(2,1)S(1)}, u32[]{:S(2)}, u32[]{:S(2)}) collective-permute-start(bf16[64,1152]{1,0:T(8,128)(2,1)S(1)} %get-tuple-element.69), channel_id=1, source_target_pairs={{0,8},{8,0},{1,9},{9,1},{2,10},{10,2},{3,11},{11,3},{4,12},{12,4},... | collective-permute-start | bytes 442376 | tf_op jit(solution)/shard_map/ppermute | solution.py:542
  28.0 1.5 %collective-permute-start.14 = (bf16[64,1152]{1,0:T(8,128)(2,1)S(1)}, bf16[64,1152]{1,0:T(8,128)(2,1)S(1)}, u32[]{:S(2)}, u32[]{:S(2)}) collective-permute-start(bf16[64,1152]{1,0:T(8,128)(2,1)S(1)} %get-tuple-element.70), channel_id=1, source_target_pairs={{0,8},{8,0},{1,9},{9,1},{2,10},{10,2},{3,11},{11,3},{4,12},{12,4},... | collective-permute-start | bytes 442376 | tf_op jit(solution)/shard_map/ppermute | solution.py:542
  34.6 2.3 %collective-permute-start.15 = (bf16[256,1152]{1,0:T(8,128)(2,1)S(1)}, bf16[256,1152]{1,0:T(8,128)(2,1)S(1)}, u32[]{:S(2)}, u32[]{:S(2)}) collective-permute-start(bf16[256,1152]{1,0:T(8,128)(2,1)S(1)} %get-tuple-element.84), channel_id=1, source_target_pairs={{0,8},{8,0},{1,9},{9,1},{2,10},{10,2},{3,11},{11,3},{4,12},{12,4},... | collective-permute-start | bytes 1769480 | tf_op jit(solution)/shard_map/ppermute | solution.py:544
  34.7 6.1 %slice-start = ((s8[4718592]{0:T(1024)(128)(4,1)}), s8[4194304]{0:T(1024)(128)(4,1)S(1)}, s32[]{:S(2)}) async-start(s8[4718592]{0:T(1024)(128)(4,1)} %bitcast.28), calls=%async_computation | async-start | bytes 8388608
  34.7 6.1 %slice-start.1 = ((s8[4718592]{0:T(1024)(128)(4,1)}), s8[524288]{0:T(1024)(128)(4,1)S(1)}, s32[]{:S(2)}) async-start(s8[4718592]{0:T(1024)(128)(4,1)} %bitcast.28), calls=%async_computation.1 | async-start | bytes 1048576
  36.8 3.2 %copy-start.4 = (bf16[1024,36]{1,0:T(8,128)(2,1)S(1)}, bf16[1024,36]{1,0:T(8,128)(2,1)}, u32[]{:S(2)}) copy-start(bf16[1024,36]{1,0:T(8,128)(2,1)} %constant.114.clone) | copy-start | bytes 221188
  36.9 3.1 %copy-start.5 = (bf16[36,512]{1,0:T(8,128)(2,1)S(1)}, bf16[36,512]{1,0:T(8,128)(2,1)}, u32[]{:S(2)}) copy-start(bf16[36,512]{1,0:T(8,128)(2,1)} %param.22) | copy-start | bytes 110596
  36.9 4.0 %copy-start.2 = (f32[512]{0:T(512)S(1)}, f32[512]{0:T(512)}, u32[]{:S(2)}) copy-start(f32[512]{0:T(512)} %param.23) | copy-start | bytes 6148
  36.9 4.0 %copy-start.3 = (f32[512]{0:T(512)S(1)}, f32[512]{0:T(512)}, u32[]{:S(2)}) copy-start(f32[512]{0:T(512)} %param.25) | copy-start | bytes 6148
  39.5 1.4 %collective-permute-start.16 = (f32[48,128]{1,0:T(8,128)S(1)}, f32[48,128]{1,0:T(8,128)S(1)}, u32[]{:S(2)}, u32[]{:S(2)}) collective-permute-start(f32[48,128]{1,0:T(8,128)S(1)} %tile_attention_and_patches.1.patch_ref), channel_id=1, source_target_pairs={{0,8},{8,0},{1,9},{9,1},{2,10},{10,2},{3,11},{11,3},{4,12},{12,4},... | collective-permute-start | bytes 73736 | tf_op jit(solution)/shard_map/ppermute | solution.py:552
  (1 other events, 2.2 us)
